TPU v7x, 32 devices: a whole 2x2x4 slice. The times are simulated.
32 devices in a mesh: groups: 2 (over y), ep: 4 (over z), sub: 4 (over x, core).
Axes of the slice: x: 2, y: 2, z: 4, core: 2. Of those that a mesh axis runs over, the one named last changes fastest.
Arguments:
- grad_out: bfloat16 [1024, 2048], P(('groups', 'ep'), 'sub'), parts along dimension 0, may hold values from -6 to 6
- route_weight: bfloat16 [1024, 8], P(('groups', 'ep')), parts along dimension 0, may hold values from 0.049804688 to 0.59765625
- routes: int32 [1024, 8], P(('groups', 'ep')), parts along dimension 0, may hold values from 0 to 15, as said below
- replica: int32 [1024, 8], P(('groups', 'ep')), parts along dimension 0, may hold values from 0 to 3, as said below
- replica_slot: int32 [32, 4], P('groups'), parts along dimension 0, may hold values from 0 to 31, as said below
- token_count: int32 [8], P(('groups', 'ep')), parts along dimension 0, may hold values from 64 to 128, as said below
- saved_input: bfloat16 [64, 4, 32, 2048], P(('groups', 'ep'), None, None, 'sub'), parts along dimension 0, may hold values from -6 to 6
- saved_gate_up: bfloat16 [64, 128, 1536], P(('groups', 'ep')), parts along dimension 0, may hold values from -6 to 6
- weight_in: bfloat16 [64, 1536, 2048], P(('groups', 'ep'), None, 'sub'), parts along dimension 0
- weight_down: bfloat16 [64, 768, 2048], P(('groups', 'ep'), None, 'sub'), parts along dimension 0
Outputs:
- grad_tokens: bfloat16 [1024, 2048], P(('groups', 'ep'), 'sub'), parts along dimension 0
- grad_route_weight: bfloat16 [1024, 8], P(('groups', 'ep')), parts along dimension 0
- grad_weight_in: bfloat16 [32, 1536, 2048], P('groups', 'ep', 'sub'), parts along dimension 0
- grad_weight_down: bfloat16 [32, 768, 2048], P('groups', 'ep', 'sub'), parts along dimension 0
There are 2 independent parts, one for each index of `groups`. A program takes and returns all parts, laid end to end along the dimension named above; each array names one. Nothing has to cross between parts.
Inputs may be any that keep to these rules, and one draw needn't show every extreme that they name: A token's 8 experts differ. Counting padding tokens too, each index of ep names expert e on c * 32 of its routes, c being the number of slots of e. A route's replica is below the number of slots of its expert. Counting padding tokens too, each index of ep sends exactly 32 of its routes to each slot. `replica_slot`: every slot appears in exactly one row. Expert e has 1 to 4 slots, listed first in its row; the rest of the row repeats the first of them. `token_count`: some index of ep has all 128 tokens valid.
All inputs are finite; a program needn't handle non-finite values.
Results may differ from a plain program's by a relative error of at most 0.018.
Values may be sent and summed in bfloat16 or wider, within the bound.
No kernel may reach another device: no remote copies, remote signals or barrier semaphores. Data moves between devices by JAX's collectives and lax.ppermute only.
A program may use at most 192 MiB of HBM per device.

v0:
```python
import jax
import jax.numpy as jnp
from jax import lax
from jax.sharding import PartitionSpec as P


def silu_grads(gate_pre, up_pre, grad_hidden, scale_rows):
    sigmoid_gate = jax.nn.sigmoid(gate_pre)
    hidden = gate_pre * sigmoid_gate * up_pre
    scaled_grad = scale_rows[..., None] * grad_hidden
    grad_gate = scaled_grad * up_pre * sigmoid_gate * (1.0 + gate_pre * (1.0 - sigmoid_gate))
    grad_up = scaled_grad * gate_pre * sigmoid_gate
    pre_grad = jnp.concatenate([grad_gate, grad_up], axis=-1).astype(jnp.bfloat16)
    route_rows = jnp.sum(hidden * grad_hidden, axis=-1).astype(jnp.bfloat16)
    return (pre_grad, route_rows)


def expert_totals(members, pieces):
    return jnp.einsum("es,sapd->eapd", members, pieces, precision=lax.Precision.HIGHEST)[:, 0]


def body(
    grad_out,
    route_weight,
    routes,
    replica,
    replica_slot,
    token_count,
    saved_input,
    saved_gate_up,
    weight_in,
    weight_down,
):
    ep_size = lax.axis_size("ep")
    local_slots = weight_in.shape[0]
    all_slots = ep_size * local_slots
    token_rows, top_count = routes.shape
    capacity = saved_input.shape[2]
    hidden_width = weight_down.shape[1]
    pair_width = weight_in.shape[1]
    slot_rows = ep_size * capacity
    experts, replica_max = replica_slot.shape
    total_rows = all_slots * capacity
    table_keys = routes * replica_max + replica
    table_ids = jnp.arange(experts * replica_max, dtype=jnp.int32)
    route_slot = jnp.sum(
        jnp.where(table_keys[..., None] == table_ids, replica_slot.reshape(-1), 0), axis=-1
    ).reshape(-1)
    live_token = jnp.arange(token_rows, dtype=jnp.int32) < token_count[0]
    live = jnp.broadcast_to(live_token[:, None], routes.shape).reshape(-1)
    slot_ids = jnp.arange(all_slots, dtype=jnp.int32)
    hits = ((route_slot[:, None] == slot_ids[None, :]) & live[:, None]).astype(jnp.int32)
    earlier = jnp.cumsum(hits, axis=0) - hits
    position = jnp.sum(earlier * hits, axis=1)
    place = (route_slot % local_slots * ep_size + route_slot // local_slots) * capacity + position
    target = jnp.where(live, place, total_rows)
    token_of_route = jnp.arange(token_rows * top_count, dtype=jnp.int32) // top_count
    source = jnp.zeros((total_rows,), jnp.int32).at[target].set(token_of_route, mode="drop")
    filled = jnp.zeros((total_rows,), jnp.bool_).at[target].set(True, mode="drop")
    weight_rows = (
        jnp.zeros((total_rows,), jnp.bfloat16).at[target].set(route_weight.reshape(-1), mode="drop")
    )
    send_rows = jnp.where(filled[:, None], grad_out[source], jnp.zeros((), jnp.bfloat16))
    arrived, arrived_scale = (
        lax.all_to_all(
            send_rows.reshape(local_slots, ep_size, capacity, -1),
            "ep",
            split_axis=1,
            concat_axis=1,
            tiled=True,
        ),
        lax.all_to_all(
            weight_rows.reshape(local_slots, ep_size, capacity),
            "ep",
            split_axis=1,
            concat_axis=1,
            tiled=True,
        ),
    )
    grad_rows = arrived.reshape(local_slots, slot_rows, -1)
    scale_rows = arrived_scale.reshape(local_slots, slot_rows).astype(jnp.float32)
    input_rows = saved_input.reshape(local_slots, slot_rows, -1)
    gate_pre = saved_gate_up[..., :hidden_width].astype(jnp.float32)
    up_pre = saved_gate_up[..., hidden_width:].astype(jnp.float32)
    hidden_bf = (gate_pre * jax.nn.sigmoid(gate_pre) * up_pre).astype(jnp.bfloat16)
    scaled = (scale_rows[..., None] * grad_rows.astype(jnp.float32)).astype(jnp.bfloat16)
    grad_down = jnp.einsum("srf,srd->sfd", hidden_bf, scaled, preferred_element_type=jnp.float32)
    down_parts = grad_down.reshape(local_slots, ep_size, hidden_width // ep_size, -1)
    members = jnp.any(replica_slot[:, :, None] == slot_ids[None, None, :], axis=1).astype(
        jnp.float32
    )
    partial_term = jnp.einsum(
        "srd,sfd->srf", grad_rows, weight_down, preferred_element_type=jnp.float32
    )
    grad_hidden = lax.psum(partial_term.astype(jnp.bfloat16), "sub").astype(jnp.float32)
    pre_grad, route_rows = silu_grads(gate_pre, up_pre, grad_hidden, scale_rows)
    grad_in = jnp.einsum("srf,srd->sfd", pre_grad, input_rows, preferred_element_type=jnp.float32)
    row_grads = jnp.einsum(
        "srf,sfd->srd", pre_grad, weight_in, preferred_element_type=jnp.float32
    ).astype(jnp.bfloat16)
    returned, returned_route = (
        lax.all_to_all(
            row_grads.reshape(local_slots, ep_size, capacity, -1),
            "ep",
            split_axis=1,
            concat_axis=1,
            tiled=True,
        ),
        lax.all_to_all(
            route_rows.reshape(local_slots, ep_size, capacity),
            "ep",
            split_axis=1,
            concat_axis=1,
            tiled=True,
        ),
    )
    in_parts = grad_in.reshape(local_slots, ep_size, pair_width // ep_size, -1)
    stacked = jnp.concatenate([in_parts, down_parts], axis=2)
    pieces = lax.all_to_all(
        stacked.astype(jnp.bfloat16), "ep", split_axis=1, concat_axis=0, tiled=True
    ).astype(stacked.dtype)
    totals = expert_totals(members, pieces)
    in_total = totals[:, : pair_width // ep_size]
    down_total = totals[:, pair_width // ep_size :]
    safe = jnp.where(live, place, 0)
    routed = jnp.where(
        live[:, None], returned.reshape(total_rows, -1)[safe], jnp.zeros((), jnp.bfloat16)
    )
    grad_tokens = jnp.sum(
        routed.reshape(token_rows, top_count, -1).astype(jnp.float32), axis=1
    ).astype(jnp.bfloat16)
    route_grad = jnp.where(
        live, returned_route.reshape(total_rows)[safe], jnp.zeros((), jnp.bfloat16)
    ).reshape(token_rows, top_count)
    return (grad_tokens, route_grad, in_total.astype(jnp.bfloat16), down_total.astype(jnp.bfloat16))


def solution(mesh):
    return jax.shard_map(
        body,
        mesh=mesh,
        in_specs=(
            P(("groups", "ep"), "sub"),
            P(("groups", "ep"), None),
            P(("groups", "ep"), None),
            P(("groups", "ep"), None),
            P("groups", None),
            P(("groups", "ep")),
            P(("groups", "ep"), None, None, "sub"),
            P(("groups", "ep"), None, None),
            P(("groups", "ep"), None, "sub"),
            P(("groups", "ep"), None, "sub"),
        ),
        out_specs=(
            P(("groups", "ep"), "sub"),
            P(("groups", "ep"), None),
            P("groups", "ep", "sub"),
            P("groups", "ep", "sub"),
        ),
        check_vma=False,
    )
```

profile of v0, /device:TPU:0, one launch (start us, length us, event | category | flops | bytes accessed | tf_op | source)
XLA Modules:
  0.0 627.4 jit_solution(11830197518051876557)
XLA Ops:
  7.2 0.9 copy.75
  8.2 0.7 multiply_add_fusion.1
  8.9 0.1 select_reduce_fusion
  9.0 0.1 copy.76
  9.1 0.1 eq.60
  9.2 0.1 eq.56
  10.0 0.1 reshape.281
  10.1 0.1 broadcast_in_dim.81
  10.2 0.1 reshape.283
  10.5 0.1 broadcast_in_dim.83
  10.6 9.0 %reduce-window.6 = s32[32,8,128]{2,1,0:T(8,128)S(1)} reduce-window(s32[32,8,128]{2,1,0:T(8,128)S(1)} %fusion.26, s32[]{:T(128)} %constant.54.clone.1), window={size=1x1x128 pad=0_0x0_0x127_0}, to_apply=%region_1.2 | reduce-window | flops 4161536 | bytes 262148 | tf_op jit(solution)/shard_map/reduce-window
  19.6 0.1 slice.32
  19.7 0.1 copy.79
  19.9 0.1 broadcast_add_fusion
  20.2 4.3 scatter_custom_fusion.2
  24.5 4.3 scatter_custom_fusion.1
  29.0 4.0 gather_fusion
  32.9 0.2 copy_select_fusion
  33.2 31.8 %all_to_all.35 = bf16[8,4,32,512]{3,2,0,1:T(8,128)(2,1)S(1)} all-to-all(bf16[8,4,32,512]{3,2,0,1:T(8,128)(2,1)S(1)} %copy_select_fusion), channel_id=1, replica_groups=mesh['groups'=2,'ep'=4,'sub'=4] {'ep'}, dimensions={1} | all-to-all | bytes 2097152 | tf_op jit(solution)/shard_map/all_to_all | solution.py:65
  65.1 1.0 copy-done.3
  66.0 6.1 convolution_convert_fusion.2
  72.2 0.1 copy.81
  72.3 0.1 reshape.324
  72.4 7.8 %scatter_custom_fusion = bf16[1024]{0:T(1024)(128)(2,1)S(1)} fusion(s32[1024]{0:T(1024)S(1)} %bitcast.76, bf16[1024]{0:T(1024)(128)(2,1)S(1)} %reshape.324, bf16[]{:T(256)} %constant.52.clone.1), kind=kCustom, calls=%fused_computation.83 | custom fusion | bytes 2050 | tf_op jit(solution)/shard_map/scatter | solution.py:61
  80.3 8.1 %all_to_all.36 = bf16[4,2,128]{2,1,0:T(2,128)(2,1)S(1)} all-to-all(bf16[4,2,128]{2,1,0:T(2,128)(2,1)S(1)} %reshape.352), channel_id=1, replica_groups=mesh['groups'=2,'ep'=4,'sub'=4] {'ep'}, dimensions={0} | all-to-all | bytes 4096 | tf_op jit(solution)/shard_map/all_to_all | solution.py:72
  88.6 25.7 %all-reduce.2.cloned.1.call-done = bf16[8,128,768]{2,1,0:T(8,128)(2,1)} async-done(((bf16[8,128,768]{2,1,0:T(8,128)(2,1)}), bf16[8,128,768]{2,1,0:T(8,128)(2,1)}) %all-reduce.2.cloned.1.call-update) | async-done | bytes 1572880 | tf_op jit(solution)/shard_map/psum | solution.py:95
  114.3 5.3 fusion.9
  119.6 0.7 reshape.354
  120.3 4.6 all-to-all-start.3
  124.9 6.9 %fusion.18 = bf16[8,128,512]{2,1,0:T(8,128)(2,1)S(1)} fusion(bf16[8,1536,512]{2,1,0:T(8,128)(2,1)} %param.18, bf16[8,128,768]{2,1,0:T(8,128)(2,1)} %get-tuple-element.27, bf16[8,128,768]{2,1,0:T(8,128)(2,1)S(1)} %get-tuple-element.26), kind=kOutput, calls=%fused_computation.36 | convolution fusion | flops 1617428480 | bytes 16777216 | tf_op jit(solution)/shard_map/srf,sfd->srd/dot_general | solution.py:98
  131.8 1.1 copy.87
  132.9 5.1 all-to-all-start.2
  138.0 6.8 %convolution_convert_fusion.1 = bf16[8,768,512]{2,1,0:T(8,128)(2,1)} fusion(bf16[8,128,512]{2,1,0:T(8,128)(2,1)} %bitcast.63, f32[8,128]{1,0:T(8,128)S(1)} %reshape.295, bf16[8,128,1536]{2,1,0:T(8,128)(2,1)} %param.17), kind=kOutput, calls=%fused_computation.20 | convolution fusion | flops 816316416 | bytes 10489856 | tf_op jit(solution)/shard_map/srf,srd->sfd/dot_general | solution.py:87
  144.8 7.8 %convolution_convert_fusion = bf16[8,1536,512]{2,1,0:T(8,128)(2,1)} fusion(bf16[8,128,512]{2,1,0:T(8,128)(2,1)S(1)} %bitcast.58, bf16[8,128,768]{2,1,0:T(8,128)(2,1)} %get-tuple-element.27, bf16[8,128,768]{2,1,0:T(8,128)(2,1)S(1)} %get-tuple-element.26), kind=kOutput, calls=%fused_computation.10 | convolution fusion | flops 1623195648 | bytes 16777216 | tf_op jit(solution)/shard_map/srf,srd->sfd/dot_general | solution.py:97
  152.6 12.9 %pad_maximum_fusion = bf16[8,4,576,512]{3,2,1,0:T(8,128)(2,1)S(1)} fusion(bf16[8,4,192,512]{3,2,1,0:T(8,128)(2,1)} %bitcast.61, bf16[8,4,384,512]{3,2,1,0:T(8,128)(2,1)} %bitcast.60), kind=kLoop, calls=%fused_computation.6 | loop fusion | flops 37748736 | bytes 37748736 | tf_op jit(solution)/shard_map/concatenate | solution.py:118
  165.6 6.7 %copy.101 = bf16[8,4,576,512]{3,2,0,1:T(8,128)(2,1)} copy(bf16[8,4,576,512]{3,2,1,0:T(8,128)(2,1)S(1)} %pad_maximum_fusion) | data formatting | bytes 37748736 | tf_op jit(solution)/shard_map/concatenate | solution.py:118
  172.2 7.7 %all-to-all-start.4 = ((bf16[8,4,576,512]{3,2,0,1:T(8,128)(2,1)}), bf16[8,4,576,512]{3,2,0,1:T(8,128)(2,1)}, u32[]{:S(2)}, u32[]{:S(2)}) async-start(bf16[8,4,576,512]{3,2,0,1:T(8,128)(2,1)} %copy.101), calls=%async_computation.4 | async-start | bytes 37748736 | tf_op jit(solution)/shard_map/all_to_all | solution.py:119
  180.2 6.8 %gather_fusion.2 = bf16[1024]{0:T(1024)(128)(2,1)S(1)} fusion(bf16[1024]{0:T(1024)(128)(2,1)S(1)} %reshape.290, s32[1024]{0:T(1024)S(1)} %broadcast_clamp_fusion), kind=kCustom, calls=%fused_computation.2 | custom fusion | bytes 8192 | tf_op jit(solution)/shard_map/gather | solution.py:133
  187.0 0.1 gather.20
  187.2 0.7 copy.96
  187.9 1.3 copy.88
  189.2 4.0 gather_fusion.1
  193.2 1.2 fusion.19
  194.4 392.7 %all-to-all-done.4 = bf16[8,4,576,512]{3,2,0,1:T(8,128)(2,1)} async-done(((bf16[8,4,576,512]{3,2,0,1:T(8,128)(2,1)}), bf16[8,4,576,512]{3,2,0,1:T(8,128)(2,1)}, u32[]{:S(2)}, u32[]{:S(2)}) %all-to-all-start.4) | async-done | bytes 18874400 | tf_op jit(solution)/shard_map/all_to_all | solution.py:119
  587.2 20.8 %fusion.3 = bf16[16,576,512]{2,0,1:T(8,128)(2,1)} fusion(bf16[4,8,1,576,512]{4,3,1,0,2:T(8,128)(2,1)} %bitcast.16, pred[16,32]{1,0:T(8,128)(4,1)S(1)} %fusion.27), kind=kOutput, calls=%fused_computation.11 | convolution fusion | flops 306708480 | bytes 28312064 | tf_op jit(solution)/shard_map/es,sapd->eapd/dot_general | solution.py:19
  607.9 2.8 slice-done
  610.7 6.4 %copy.97 = bf16[16,384,512]{2,1,0:T(8,128)(2,1)} copy(bf16[16,384,512]{2,0,1:T(8,128)(2,1)S(1)} %slice-done) | data formatting | bytes 12582912
  617.1 3.4 copy.98
  (50 shorter events, 1.5 us)
Async XLA Ops:
  7.2 137.6 %copy-start = (bf16[8,4,32,512]{3,2,1,0:T(8,128)(2,1)S(1)}, bf16[8,4,32,512]{3,2,1,0:T(8,128)(2,1)}, u32[]{:S(2)}) copy-start(bf16[8,4,32,512]{3,2,1,0:T(8,128)(2,1)} %param.16) | copy-start | bytes 3145732
  7.2 21.8 %copy-start.2 = (bf16[128,512]{1,0:T(8,128)(2,1)S(1)}, bf16[128,512]{1,0:T(8,128)(2,1)}, u32[]{:S(2)}) copy-start(bf16[128,512]{1,0:T(8,128)(2,1)} %param.10) | copy-start | bytes 393220
  7.2 107.1 %all-reduce.2.cloned.1.call-start = ((), (), s32[]{:S(2)}) async-start(), calls=%async_computation.5 | async-start | bytes 3145728 | tf_op jit(solution)/shard_map/psum | solution.py:95
  65.1 1.0 copy-start.3
  66.0 6.1 copy-start.5
  120.3 12.6 %all-to-all-start.3 = ((bf16[4,2,128]{2,1,0:T(2,128)(2,1)}), bf16[4,2,128]{2,1,0:T(2,128)(2,1)S(1)}, u32[]{:S(2)}, u32[]{:S(2)}) async-start(bf16[4,2,128]{2,1,0:T(2,128)(2,1)} %reshape.354), calls=%async_computation.3 | async-start | bytes 4096 | tf_op jit(solution)/shard_map/all_to_all | solution.py:109
  132.9 39.4 %all-to-all-start.2 = ((bf16[8,4,32,512]{3,2,0,1:T(8,128)(2,1)}), bf16[8,4,32,512]{3,2,0,1:T(8,128)(2,1)}, u32[]{:S(2)}, u32[]{:S(2)}) async-start(bf16[8,4,32,512]{3,2,0,1:T(8,128)(2,1)} %copy.87), calls=%async_computation.2 | async-start | bytes 2097152 | tf_op jit(solution)/shard_map/all_to_all | solution.py:102
  172.2 7.7 %copy-start.4 = (s32[16,4]{0,1:T(4,128)S(1)}, s32[16,4]{0,1:T(4,128)}, u32[]{:S(2)}) copy-start(s32[16,4]{0,1:T(4,128)} %param.14) | copy-start | bytes 772
  172.2 414.9 %all-to-all-start.4 = ((bf16[8,4,576,512]{3,2,0,1:T(8,128)(2,1)}), bf16[8,4,576,512]{3,2,0,1:T(8,128)(2,1)}, u32[]{:S(2)}, u32[]{:S(2)}) async-start(bf16[8,4,576,512]{3,2,0,1:T(8,128)(2,1)} %copy.101), calls=%async_computation.4 | async-start | bytes 37748736 | tf_op jit(solution)/shard_map/all_to_all | solution.py:119
  607.9 2.8 slice-start
  610.7 6.4 %slice-start.1 = ((bf16[16,576,512]{2,0,1:T(8,128)(2,1)}), bf16[16,192,512]{2,0,1:T(8,128)(2,1)S(1)}, s32[]{:S(2)}) async-start(bf16[16,576,512]{2,0,1:T(8,128)(2,1)} %fusion.3), calls=%async_computation.7 | async-start | bytes 6291456 | tf_op jit(solution)/shard_map/slice | solution.py:124
  610.7 9.8 %copy-start.1 = (bf16[8,4,32,512]{3,2,1,0:T(8,128)(2,1)S(1)}, bf16[8,4,32,512]{3,2,1,0:T(8,128)(2,1)}, u32[]{:S(2)}) copy-start(bf16[8,4,32,512]{3,2,1,0:T(8,128)(2,1)} %param.16) | copy-start | bytes 3145732
Sparse Core Ops, SparseCore 0:
  72.3 41.9 all-reduce.1
where the time goes:
time: 628 us; the launch traced here: 627 us
  waiting for transfers between devices  418 us (67%)
  local copies, waits for them, and re-layouts  58.3 us (9%)
  matrix products  48.4 us (8%)
  blocking collectives  39.9 us (6%)
  other arithmetic  29.9 us (5%)
  starting transfers between devices  17.4 us (3%)
  between operations  15 us (2%)
    all_to_all x1, waiting for transfers between devices, body(): lax.all_to_all(stacked.astype(jnp.bfloat16), 'ep', split_axis=1, concat_a...  393 us
    all_to_all x1, blocking collectives, body(): lax.all_to_all(send_rows.reshape(local_slots, ep_size, capacity, -1), 'ep...  31.8 us
    psum x1, waiting for transfers between devices, body(): lax.psum(partial_term.astype(jnp.bfloat16), 'sub').astype(jnp.float32)  25.7 us
    dot_general x1, matrix products, expert_totals(): jnp.einsum('es,sapd->eapd', members, pieces, precision=lax.Precision.HIGH...  20.8 us
    another operation x4, other arithmetic  14.4 us
    unnamed x21, local copies, waits for them, and re-layouts  13.3 us
    concatenate x1, other arithmetic, body(): stacked = jnp.concatenate([in_parts, down_parts], axis=2)  12.9 us
  transfers between devices with their start and end apart: 4, of which 2 were waited for; matrix products, arithmetic and copies ran while one was open for 10% of the time, Pallas kernels for 0%

commit v1 on v0

v1 whole, which is shorter than its diff:
```python
import functools
import math

import jax
import jax.numpy as jnp
from jax import lax
from jax.experimental import pallas as pl
from jax.experimental.pallas import tpu as pltpu
from jax.sharding import PartitionSpec as P

BF = jnp.bfloat16
F32 = jnp.float32
VMEM_BYTES = 48 * 1024 * 1024


def nt(a, b):
    return lax.dot_general(a, b, (((1,), (1,)), ((), ())), preferred_element_type=F32)


def tn(a, b):
    return lax.dot_general(a, b, (((0,), (0,)), ((), ())), preferred_element_type=F32)


def nn(a, b):
    return jnp.dot(a, b, preferred_element_type=F32)


def whole(shape):
    zeros = (0,) * len(shape)
    return pl.BlockSpec(shape, lambda *_: zeros)


def smem():
    return pl.BlockSpec(memory_space=pltpu.SMEM)


def params(axes=1):
    return pltpu.CompilerParams(
        vmem_limit_bytes=VMEM_BYTES, dimension_semantics=("arbitrary",) * axes
    )


class Sizes:
    def __init__(self, grad_out, routes, replica_slot, saved_input, weight_in, weight_down):
        self.ep = lax.axis_size("ep")
        self.sub = lax.axis_size("sub")
        self.tokens, self.width = grad_out.shape
        self.top = routes.shape[1]
        self.experts, self.reps = replica_slot.shape
        self.local = weight_in.shape[0]
        self.slots = self.ep * self.local
        self.cap = saved_input.shape[2]
        self.rows = self.ep * self.cap
        self.hidden = weight_down.shape[1]
        self.pair = weight_in.shape[1]
        self.all_rows = self.local * self.rows
        self.part = self.all_rows // self.sub
        self.block = math.gcd(self.rows, self.part)
        self.sources = self.block // self.cap
        self.blocks = self.all_rows // self.block
        self.part_blocks = self.part // self.block
        self.slot_blocks = self.rows // self.block
        self.in_cols = self.pair // self.ep
        self.down_cols = self.hidden // self.ep
        self.cols = self.in_cols + self.down_cols
        self.folds = self.width // self.tokens
        self.tail = 2 * self.slots // self.folds


def key_columns(z, routes_ref, replica_ref):
    return routes_ref[...] * z.reps + replica_ref[...]


def slot_table(z, table_ref):
    ids = lax.broadcasted_iota(jnp.int32, (z.slots, z.experts * z.reps), 0)
    return (table_ref[...] == ids).astype(F32).astype(BF)


def route_kernel(z, count_ref, grad_ref, weight_ref, routes_ref, replica_ref, table_ref, out_ref):
    keys = key_columns(z, routes_ref, replica_ref)
    weights = weight_ref[...].astype(F32)
    width = z.experts * z.reps
    ids = lax.broadcasted_iota(jnp.int32, (z.tokens, width), 1)
    live = lax.broadcasted_iota(jnp.int32, (z.tokens, width), 0) < count_ref[0]
    hit = jnp.zeros((z.tokens, width), F32)
    load = jnp.zeros((z.tokens, width), F32)
    for k in range(z.top):
        same = (keys[:, k : k + 1] == ids) & live
        hit = jnp.where(same, 1.0, hit)
        load = jnp.where(same, weights[:, k : k + 1], load)
    table = slot_table(z, table_ref)
    hits = nt(table, hit.astype(BF))
    loads = nt(table, load.astype(BF))
    before = lax.broadcasted_iota(jnp.int32, (z.tokens, z.tokens), 0)
    after = lax.broadcasted_iota(jnp.int32, (z.tokens, z.tokens), 1)
    earlier = nn(hits.astype(BF), (before < after).astype(F32).astype(BF))
    code = jnp.where(hits > 0.5, earlier, -1.0)
    both = jnp.concatenate([code, loads], axis=0).astype(BF)
    out_ref[: z.tokens, :] = grad_ref[...]
    for b in range(z.folds):
        out_ref[z.tokens :, b * z.tokens : (b + 1) * z.tokens] = both[
            b * z.tail : (b + 1) * z.tail, :
        ]


def block_place(z, block):
    slot = block // z.slot_blocks
    first = (block % z.slot_blocks) * z.sources
    return slot, first


def block_picks(z, codes_ref, slot, first):
    rows = lax.broadcasted_iota(jnp.int32, (z.cap, z.tokens), 0).astype(F32)
    for a in range(z.sources):
        code = codes_ref[first + a, pl.ds(slot, 1), :]
        yield a, rows == code


def block_scale(z, codes_ref, slot, first):
    parts = []
    for a, pick in block_picks(z, codes_ref, slot, first):
        load = codes_ref[first + a, pl.ds(z.slots + slot, 1), :]
        parts.append(jnp.sum(jnp.where(pick, load, 0.0), axis=1, keepdims=True))
    return jnp.concatenate(parts, axis=0)


def block_rows(z, codes_ref, grads_ref, slot, first):
    parts = []
    for a, pick in block_picks(z, codes_ref, slot, first):
        parts.append(nn(pick.astype(F32).astype(BF), grads_ref[first + a]))
    return jnp.concatenate(parts, axis=0)


def down_kernel(z, ids_ref, *refs):
    bufs = refs[: z.ep]
    weight_ref = refs[z.ep]
    parts = refs[z.ep + 1 : z.ep + 1 + z.sub]
    grads_ref, codes_ref = refs[z.ep + 1 + z.sub :]
    me, mine = ids_ref[0], ids_ref[1]
    step = pl.program_id(0)

    @pl.when(step == 0)
    def _():
        for k in range(z.ep):
            source = me ^ k
            grads_ref[source] = bufs[k][: z.tokens, :]
            for b in range(z.folds):
                codes_ref[source, b * z.tail : (b + 1) * z.tail, :] = bufs[k][
                    z.tokens :, b * z.tokens : (b + 1) * z.tokens
                ].astype(F32)

    place = step // z.part_blocks
    block = (place ^ mine) * z.part_blocks + step % z.part_blocks
    slot, first = block_place(z, block)
    rows = block_rows(z, codes_ref, grads_ref, me * z.local + slot, first).astype(BF)
    partial = nt(rows, weight_ref[0]).astype(BF)
    spot = pl.multiple_of((step % z.part_blocks) * z.block, z.block)
    for k in range(z.sub):

        @pl.when(place == k)
        def _():
            parts[k][pl.ds(spot, z.block), :] = partial


def gate_terms(z, pair, grad, scale):
    gate = pair[:, : z.hidden].astype(F32)
    up = pair[:, z.hidden :].astype(F32)
    sig = 1.0 / (1.0 + jnp.exp(-gate))
    act = gate * sig
    hidden = act * up
    scaled = scale * grad
    grad_gate = scaled * up * sig * (1.0 + gate * (1.0 - sig))
    grad_up = scaled * act
    return hidden, grad_gate.astype(BF), grad_up.astype(BF)


def pre_kernel(z, ids_ref, *refs):
    parts = refs[: z.sub]
    pair_ref, codes_ref, out_ref, grad_ref = refs[z.sub :]
    block = ids_ref[1] * z.part_blocks + pl.program_id(0)
    slot, first = block_place(z, block)
    scale = block_scale(z, codes_ref, ids_ref[0] * z.local + slot, first)
    grad = parts[0][...].astype(F32)
    for k in range(1, z.sub):
        grad = grad + parts[k][...].astype(F32)
    grad_ref[...] = grad.astype(BF)
    hidden, grad_gate, grad_up = gate_terms(z, pair_ref[...], grad, scale)
    hidden = hidden.astype(BF)
    pre = jnp.concatenate([grad_gate, grad_up], axis=1)
    for q in range(z.ep):
        out_ref[q, :, : z.in_cols] = pre[:, q * z.in_cols : (q + 1) * z.in_cols]
        out_ref[q, :, z.in_cols :] = hidden[:, q * z.down_cols : (q + 1) * z.down_cols]


def row_kernel(z, ids_ref, *refs):
    grads = refs[: z.sub]
    pair_ref, weight_ref, codes_ref, out_ref, sums, marks, held = refs[z.sub :]
    me, mine = ids_ref[0], ids_ref[1]
    step = pl.program_id(0)
    place = step // z.part_blocks
    block = (place ^ mine) * z.part_blocks + step % z.part_blocks
    slot, first = block_place(z, block)

    @pl.when(step == 0)
    def _():
        sums[...] = jnp.zeros_like(sums)
        marks[...] = jnp.zeros_like(marks)

    spot = pl.multiple_of((step % z.part_blocks) * z.block, z.block)
    for k in range(z.sub):

        @pl.when(place == k)
        def _():
            held[...] = grads[k][pl.ds(spot, z.block), :]

    grad = held[...].astype(F32)
    scale = block_scale(z, codes_ref, me * z.local + slot, first)
    hidden, grad_gate, grad_up = gate_terms(z, pair_ref[...], grad, scale)
    route = jnp.sum(hidden * grad, axis=1, keepdims=True).astype(BF).astype(F32)
    rows = nn(grad_gate, weight_ref[0, : z.hidden, :]) + nn(grad_up, weight_ref[0, z.hidden :, :])
    rows = rows.astype(BF)
    for a, pick in block_picks(z, codes_ref, me * z.local + slot, first):
        lo, hi = a * z.cap, (a + 1) * z.cap
        sums[first + a] += tn(pick.astype(F32).astype(BF), rows[lo:hi, :])
        marks[first + a, pl.ds(slot, 1), :] = jnp.sum(
            jnp.where(pick, route[lo:hi, :], 0.0), axis=0, keepdims=True
        )

    @pl.when(step == z.blocks - 1)
    def _():
        for p in range(z.ep):
            out_ref[p ^ me, : z.tokens, :] = sums[p].astype(BF)
            tail = jnp.concatenate(
                [
                    marks[p],
                    jnp.zeros((marks.shape[1], z.width - z.tokens), F32),
                ],
                axis=1,
            )
            out_ref[p ^ me, z.tokens :, :] = tail.astype(BF)


def token_kernel(z, ids_ref, count_ref, *refs):
    got = refs[: z.ep]
    routes_ref, replica_ref, table_ref, tokens_ref, route_ref, marks = refs[z.ep :]
    me = ids_ref[0]
    total = got[0][: z.tokens, :].astype(F32)
    for k in range(1, z.ep):
        total = total + got[k][: z.tokens, :].astype(F32)
    tokens_ref[...] = total.astype(BF)
    for k in range(z.ep):
        marks[me ^ k] = got[k][z.tokens :, : z.tokens].astype(F32)
    rows = jnp.concatenate([marks[p][: z.local, :] for p in range(z.ep)], axis=0)
    spread = tn(rows.astype(BF), slot_table(z, table_ref))
    keys = key_columns(z, routes_ref, replica_ref)
    width = z.experts * z.reps
    ids = lax.broadcasted_iota(jnp.int32, (z.tokens, width), 1)
    live = lax.broadcasted_iota(jnp.int32, (z.tokens, width), 0) < count_ref[0]
    columns = []
    for k in range(z.top):
        same = (keys[:, k : k + 1] == ids) & live
        columns.append(jnp.sum(jnp.where(same, spread, 0.0), axis=1, keepdims=True))
    route_ref[...] = jnp.concatenate(columns, axis=1).astype(BF)


def total_kernel(z, ids_ref, table_ref, *refs):
    sides = refs[: z.sub]
    inputs_ref, grads_ref, codes_ref, in_ref, down_ref = refs[z.sub : z.sub + 5]
    held, in_sum, down_sum, sems = refs[z.sub + 5 :]
    mine = ids_ref[1]
    expert = pl.program_id(0)

    @pl.when(expert == 0)
    def _():
        copies = [
            pltpu.make_async_copy(sides[k], held.at[k], sems.at[k]) for k in range(z.sub)
        ]
        for copy in copies:
            copy.start()
        for copy in copies:
            copy.wait()

    first_slot = table_ref[expert, 0]

    def add(slot_id, fresh):
        source = slot_id // z.local
        for b in range(z.slot_blocks):
            block = (slot_id % z.local) * z.slot_blocks + b
            part = (block // z.part_blocks) ^ mine
            spot = pl.multiple_of((block % z.part_blocks) * z.block, z.block)
            left = held[part, source, pl.ds(spot, z.block), :]
            start = pl.multiple_of(block * z.block, z.block)
            right = inputs_ref[source, pl.ds(start, z.block), :]
            first = b * z.sources
            scale = block_scale(z, codes_ref, slot_id, first)
            rows = (block_rows(z, codes_ref, grads_ref, slot_id, first) * scale).astype(BF)
            grad_in = tn(left[:, : z.in_cols], right)
            grad_down = tn(left[:, z.in_cols :], rows)
            if fresh and b == 0:
                in_sum[...] = grad_in
                down_sum[...] = grad_down
            else:
                in_sum[...] += grad_in
                down_sum[...] += grad_down

    add(first_slot, True)
    for r in range(1, z.reps):
        slot_id = table_ref[expert, r]

        @pl.when(slot_id != first_slot)
        def _():
            add(slot_id, False)

    in_ref[0] = in_sum[...].astype(BF)
    down_ref[0] = down_sum[...].astype(BF)


def swap(x, axis, size, bit):
    return lax.ppermute(x, axis, [(i, i ^ bit) for i in range(size)])


def spread_over(x, axis, size):
    have = {0: x}
    bit = size // 2
    while bit:
        for k in list(have):
            have[k | bit] = swap(have[k], axis, size, bit)
        bit //= 2
    return [have[k] for k in range(size)]


def body(
    grad_out,
    route_weight,
    routes,
    replica,
    replica_slot,
    token_count,
    saved_input,
    saved_gate_up,
    weight_in,
    weight_down,
):
    z = Sizes(grad_out, routes, replica_slot, saved_input, weight_in, weight_down)
    n, m = z.ep, z.sub
    ids = jnp.stack([lax.axis_index("ep"), lax.axis_index("sub")]).astype(jnp.int32)
    table_row = replica_slot.reshape(1, -1)
    pair_rows = saved_gate_up.reshape(z.all_rows, z.pair)
    grad_shape = (z.tokens + z.tail, z.width)
    code_shape = (n, 2 * z.slots, z.tokens)

    inputs_all = lax.all_gather(saved_input.reshape(z.all_rows, z.width), "ep")

    buf = pl.pallas_call(
        functools.partial(route_kernel, z),
        out_shape=jax.ShapeDtypeStruct(grad_shape, BF),
        in_specs=[smem()]
        + [
            whole(a.shape) for a in (grad_out, route_weight, routes, replica, table_row)
        ],
        out_specs=whole(grad_shape),
        grid=(1,),
        compiler_params=params(),
        name="route",
    )(token_count, grad_out, route_weight, routes, replica, table_row)
    bufs = [buf] + [swap(buf, "ep", n, k) for k in range(1, n)]

    def down_slot(i, ids_ref):
        place = i // z.part_blocks
        block = (place ^ ids_ref[1]) * z.part_blocks + i % z.part_blocks
        return block // z.slot_blocks

    outs = pl.pallas_call(
        functools.partial(down_kernel, z),
        grid_spec=pltpu.PrefetchScalarGridSpec(
            num_scalar_prefetch=1,
            grid=(z.blocks,),
            in_specs=[whole(grad_shape)] * n
            + [pl.BlockSpec((1, z.hidden, z.width), lambda i, r: (down_slot(i, r), 0, 0))],
            out_specs=[whole((z.part, z.hidden))] * m
            + [whole((n, z.tokens, z.width)), whole(code_shape)],
        ),
        out_shape=[jax.ShapeDtypeStruct((z.part, z.hidden), BF)] * m
        + [
            jax.ShapeDtypeStruct((n, z.tokens, z.width), BF),
            jax.ShapeDtypeStruct(code_shape, F32),
        ],
        compiler_params=params(),
        name="hidden_partials",
    )(ids, *bufs, weight_down)
    parts, (grads_all, codes) = outs[:m], outs[m:]
    parts = [parts[0]] + [swap(parts[k], "sub", m, k) for k in range(1, m)]

    pre, grad_part = pl.pallas_call(
        functools.partial(pre_kernel, z),
        grid_spec=pltpu.PrefetchScalarGridSpec(
            num_scalar_prefetch=1,
            grid=(z.part_blocks,),
            in_specs=[pl.BlockSpec((z.block, z.hidden), lambda i, r: (i, 0))] * m
            + [
                pl.BlockSpec((z.block, z.pair), lambda i, r: (r[1] * z.part_blocks + i, 0)),
                whole(code_shape),
            ],
            out_specs=[
                pl.BlockSpec((n, z.block, z.cols), lambda i, r: (0, i, 0)),
                pl.BlockSpec((z.block, z.hidden), lambda i, r: (i, 0)),
            ],
        ),
        out_shape=[
            jax.ShapeDtypeStruct((n, z.part, z.cols), BF),
            jax.ShapeDtypeStruct((z.part, z.hidden), BF),
        ],
        compiler_params=params(),
        name="pre_grads",
    )(ids, *parts, pair_rows, codes)

    columns = lax.all_to_all(pre, "ep", split_axis=0, concat_axis=0, tiled=True)
    grad_parts = spread_over(grad_part, "sub", m)
    sides = spread_over(columns, "sub", m)

    def row_block(i, ids_ref):
        place = i // z.part_blocks
        return (place ^ ids_ref[1]) * z.part_blocks + i % z.part_blocks

    mark_rows = -(-z.local // 16) * 16
    back_shape = (n, z.tokens + mark_rows, z.width)
    back = pl.pallas_call(
        functools.partial(row_kernel, z),
        grid_spec=pltpu.PrefetchScalarGridSpec(
            num_scalar_prefetch=1,
            grid=(z.blocks,),
            in_specs=[whole((z.part, z.hidden))] * m
            + [
                pl.BlockSpec((z.block, z.pair), lambda i, r: (row_block(i, r), 0)),
                pl.BlockSpec((1, z.pair, z.width), lambda i, r: (down_slot(i, r), 0, 0)),
                whole(code_shape),
            ],
            out_specs=whole(back_shape),
            scratch_shapes=[
                pltpu.VMEM((n, z.tokens, z.width), F32),
                pltpu.VMEM((n, mark_rows, z.tokens), F32),
                pltpu.VMEM((z.block, z.hidden), BF),
            ],
        ),
        out_shape=jax.ShapeDtypeStruct(back_shape, BF),
        compiler_params=params(),
        name="row_grads",
    )(ids, *grad_parts, pair_rows, weight_in, codes)
    got = [back[0]] + [swap(back[k], "ep", n, k) for k in range(1, n)]

    grad_tokens, grad_routes = pl.pallas_call(
        functools.partial(token_kernel, z),
        out_shape=[
            jax.ShapeDtypeStruct((z.tokens, z.width), BF),
            jax.ShapeDtypeStruct((z.tokens, z.top), BF),
        ],
        in_specs=[smem(), smem()]
        + [whole(back_shape[1:])] * n
        + [whole(a.shape) for a in (routes, replica, table_row)],
        out_specs=[whole((z.tokens, z.width)), whole((z.tokens, z.top))],
        grid=(1,),
        scratch_shapes=[pltpu.VMEM((n, mark_rows, z.tokens), F32)],
        compiler_params=params(),
        name="token_grads",
    )(ids, token_count, *got, routes, replica, table_row)

    side_shape = (n, z.part, z.cols)
    grad_in, grad_down = pl.pallas_call(
        functools.partial(total_kernel, z),
        grid_spec=pltpu.PrefetchScalarGridSpec(
            num_scalar_prefetch=2,
            grid=(z.experts,),
            in_specs=[pl.BlockSpec(memory_space=pl.ANY)] * m
            + [
                whole((n, z.all_rows, z.width)),
                whole((n, z.tokens, z.width)),
                whole(code_shape),
            ],
            out_specs=[
                pl.BlockSpec((1, z.in_cols, z.width), lambda e, r, t: (e, 0, 0)),
                pl.BlockSpec((1, z.down_cols, z.width), lambda e, r, t: (e, 0, 0)),
            ],
            scratch_shapes=[
                pltpu.VMEM((m,) + side_shape, BF),
                pltpu.VMEM((z.in_cols, z.width), F32),
                pltpu.VMEM((z.down_cols, z.width), F32),
                pltpu.SemaphoreType.DMA((m,)),
            ],
        ),
        out_shape=[
            jax.ShapeDtypeStruct((z.experts, z.in_cols, z.width), BF),
            jax.ShapeDtypeStruct((z.experts, z.down_cols, z.width), BF),
        ],
        compiler_params=params(),
        name="weight_grads",
    )(ids, replica_slot, *sides, inputs_all, grads_all, codes)
    return grad_tokens, grad_routes, grad_in, grad_down


def solution(mesh):
    return jax.shard_map(
        body,
        mesh=mesh,
        in_specs=(
            P(("groups", "ep"), "sub"),
            P(("groups", "ep"), None),
            P(("groups", "ep"), None),
            P(("groups", "ep"), None),
            P("groups", None),
            P(("groups", "ep")),
            P(("groups", "ep"), None, None, "sub"),
            P(("groups", "ep"), None, None),
            P(("groups", "ep"), None, "sub"),
            P(("groups", "ep"), None, "sub"),
        ),
        out_specs=(
            P(("groups", "ep"), "sub"),
            P(("groups", "ep"), None),
            P("groups", "ep", "sub"),
            P("groups", "ep", "sub"),
        ),
        check_vma=False,
    )
```

time: 628 us -> 232 us (0.37)
  waiting for transfers between devices: 418 us -> 93.1 us
  matrix products: 48.4 us -> 0 us
  Pallas kernels: 0 us -> 44.2 us
  local copies, waits for them, and re-layouts: 58.3 us -> 19.9 us
  other arithmetic: 29.9 us -> 0.07 us
    all_to_all x3 -> x0, waiting for transfers between devices: 393 us -> none  [the longest x1 393 us: body(): lax.all_to_all(stacked.astype(jnp.bfloat16), 'ep', split_axis=1, concat_a...]
    ppermute x0 -> x15, waiting for transfers between devices: none -> 92.4 us  [swap(): return lax.ppermute(x, axis, [(i, i ^ bit) for i in range(size)])]
    dot_general x5 -> x0, matrix products: 48.4 us -> none  [the longest x1 20.8 us: expert_totals(): jnp.einsum('es,sapd->eapd', members, pieces, precision=lax.Precision.HIGH...]
    pallas_call x0 -> x6, Pallas kernels: none -> 44.2 us  [the longest x1 20.4 us: body(): pl.pallas_call(functools.partial(total_kernel, z), grid_spec=pltpu.Prefet...]
    psum x1 -> x0, waiting for transfers between devices: 25.7 us -> none  [body(): lax.psum(partial_term.astype(jnp.bfloat16), 'sub').astype(jnp.float32)]
    all_to_all x3 -> x0, starting transfers between devices: 17.4 us -> none  [the longest x1 7.69 us: body(): lax.all_to_all(stacked.astype(jnp.bfloat16), 'ep', split_axis=1, concat_a...]
    scatter x3 -> x0, local copies, waits for them, and re-layouts: 16.4 us -> none  [the longest x1 7.75 us: body(): jnp.zeros((total_rows,), jnp.bfloat16).at[target]]
    ppermute x0 -> x15, starting transfers between devices: none -> 15.1 us  [swap(): return lax.ppermute(x, axis, [(i, i ^ bit) for i in range(size)])]
  transfers between devices with their start and end apart: 4 -> 16, of which waited for: 2 -> 9; matrix products, arithmetic and copies ran while one was open for 10% -> 6% of each run, Pallas kernels for 0% -> 10%
where the time goes in v1:
time: 232 us; the launch traced here: 231 us
  waiting for transfers between devices  93.1 us (40%)
  Pallas kernels  44.2 us (19%)
  blocking collectives  43.7 us (19%)
  local copies, waits for them, and re-layouts  19.9 us (9%)
  starting transfers between devices  15.2 us (7%)
  between operations  14.8 us (6%)
    ppermute x15, waiting for transfers between devices, swap(): return lax.ppermute(x, axis, [(i, i ^ bit) for i in range(size)])  92.4 us
    all_to_all x1, blocking collectives, body(): columns = lax.all_to_all(pre, 'ep', split_axis=0, concat_axis=0, tiled=True)  43.7 us
    pallas_call x1, Pallas kernels, body(): pl.pallas_call(functools.partial(total_kernel, z), grid_spec=pltpu.Prefet...  20.4 us
    ppermute x15, starting transfers between devices, swap(): return lax.ppermute(x, axis, [(i, i ^ bit) for i in range(size)])  15.1 us
    pallas_call x1, Pallas kernels, body(): pl.pallas_call(functools.partial(row_kernel, z), grid_spec=pltpu.Prefetch...  10.8 us
    unnamed x23, local copies, waits for them, and re-layouts  9.02 us
    pallas_call x1, Pallas kernels, body(): pl.pallas_call(functools.partial(down_kernel, z), grid_spec=pltpu.Prefetc...  7.95 us
    ppermute x3, local copies, waits for them, and re-layouts, swap(): return lax.ppermute(x, axis, [(i, i ^ bit) for i in range(size)])  6.54 us
  transfers between devices with their start and end apart: 16, of which 9 were waited for; matrix products, arithmetic and copies ran while one was open for 6% of the time, Pallas kernels for 10%

profile of v1, /device:TPU:0, one launch (start us, length us, event | category | flops | bytes accessed | tf_op | source)
XLA Modules:
  0.0 230.9 jit_solution(12599610638646029228)
XLA Ops:
  7.2 0.0 all-gather.2.cloned.1.call-start
  7.2 0.7 all-gather.2.cloned.1.call-update
  8.6 0.8 copy.30.table_ref
  9.3 0.1 reshape.14.table_ref.refs_6_
  9.4 0.8 copy.31.weight_ref
  10.2 0.8 copy.32.routes_ref.refs_4_
  11.0 0.8 copy.33.replica_ref.refs_5_
  11.8 0.5 route.1.refs_0_
  12.3 5.1 %collective-permute-start.2 = (bf16[144,512]{1,0:T(8,128)(2,1)S(1)}, bf16[144,512]{1,0:T(8,128)(2,1)S(1)}, u32[]{:S(2)}, u32[]{:S(2)}) collective-permute-start(bf16[144,512]{1,0:T(8,128)(2,1)S(1)} %route.1.refs_0_), channel_id=1, source_target_pairs={{0,12},{4,8},{8,4},{12,0},{1,13},{5,9},{9,5},{13,1},{2,14},{6,10},... | collective-permute-start | bytes 442376 | tf_op jit(solution)/shard_map/ppermute | solution.py:319
  17.4 0.0 collective-permute-start.1
  17.4 0.6 collective-permute-start
  18.0 0.1 pad_add_fusion.ids_ref
  18.0 4.1 %collective-permute-done.2.refs_3_ = bf16[144,512]{1,0:T(8,128)(2,1)S(1)} collective-permute-done((bf16[144,512]{1,0:T(8,128)(2,1)S(1)}, bf16[144,512]{1,0:T(8,128)(2,1)S(1)}, u32[]{:S(2)}, u32[]{:S(2)}) %collective-permute-start.2) | collective-permute-done | bytes 147488 | tf_op jit(solution)/shard_map/ppermute | solution.py:319
  22.1 22.0 %collective-permute-done.1.refs_2_ = bf16[144,512]{1,0:T(8,128)(2,1)S(1)} collective-permute-done((bf16[144,512]{1,0:T(8,128)(2,1)S(1)}, bf16[144,512]{1,0:T(8,128)(2,1)S(1)}, u32[]{:S(2)}, u32[]{:S(2)}) %collective-permute-start.1) | collective-permute-done | bytes 147488 | tf_op jit(solution)/shard_map/ppermute | solution.py:319
  44.2 8.0 %hidden_partials.1 = (bf16[256,768]{1,0:T(8,128)(2,1)S(1)}, bf16[256,768]{1,0:T(8,128)(2,1)S(1)}, bf16[256,768]{1,0:T(8,128)(2,1)S(1)}, bf16[256,768]{1,0:T(8,12...) custom-call(s32[2]{0:T(128)S(1)} %pad_add_fusion.ids_ref, bf16[144,512]{1,0:T(8,128)(2,1)S(1)} %route.1.refs_0_, ...), custom_call_target="tpu_custom_call" | custom-call | tf_op jit(solution)/shard_map/hidden_partials/pallas_call | solution.py:373
  52.1 0.8 copy-done.4
  52.9 1.4 collective-permute-start.4
  54.3 0.5 collective-permute-start.5
  54.8 10.0 %collective-permute-done.4.refs_2_ = bf16[256,768]{1,0:T(8,128)(2,1)S(1)} collective-permute-done((bf16[256,768]{1,0:T(8,128)(2,1)S(1)}, bf16[256,768]{1,0:T(8,128)(2,1)S(1)}, u32[]{:S(2)}, u32[]{:S(2)}) %collective-permute-start.4) | collective-permute-done | bytes 393248 | tf_op jit(solution)/shard_map/ppermute | solution.py:319
  64.8 7.7 %collective-permute-done.5.refs_3_ = bf16[256,768]{1,0:T(8,128)(2,1)S(1)} collective-permute-done((bf16[256,768]{1,0:T(8,128)(2,1)S(1)}, bf16[256,768]{1,0:T(8,128)(2,1)S(1)}, u32[]{:S(2)}, u32[]{:S(2)}) %collective-permute-start.5) | collective-permute-done | bytes 393248 | tf_op jit(solution)/shard_map/ppermute | solution.py:319
  72.5 2.5 %pre_grads.1 = (bf16[4,256,576]{2,1,0:T(8,128)(2,1)S(1)}, bf16[256,768]{1,0:T(8,128)(2,1)S(1)}) custom-call(s32[2]{0:T(128)S(1)} %pad_add_fusion.ids_ref, bf16[256,768]{1,0:T(8,128)(2,1)S(1)} %get-tuple-element.16.refs_0_, bf16[256,768]{1,0:T(8,128)(2,1)S(1)} %collective-permute-done.3.refs_1_, bf16[256,768]{1,0:T(8,128)(2,1)S(1)} %collective-permute-done.4.refs_2_, ...), custom_call_target="tpu_custom_call" | custom-call | tf_op jit(solution)/shard_map/pre_grads/pallas_call | solution.py:394
  75.0 0.0 copy-start.3
  75.0 1.0 copy-done.3
  76.0 0.7 copy-done.6
  76.8 2.5 %copy.36 = bf16[4,256,576]{1,2,0:T(8,128)(2,1)} copy(bf16[4,256,576]{2,1,0:T(8,128)(2,1)} %copy-done.3) | data formatting | bytes 2359296 | tf_op jit(solution)/shard_map/pre_grads/pallas_call | solution.py:394
  79.3 43.7 %all_to_all.5 = bf16[4,256,576]{1,2,0:T(8,128)(2,1)} all-to-all(bf16[4,256,576]{1,2,0:T(8,128)(2,1)} %copy.36), channel_id=1, replica_groups=mesh['groups'=2,'ep'=4,'sub'=4] {'ep'}, dimensions={0} | all-to-all | bytes 2359296 | tf_op jit(solution)/shard_map/all_to_all | solution.py:417
  123.1 1.5 collective-permute-start.13
  124.5 0.0 collective-permute-start.12
  124.5 26.7 %collective-permute-done.13 = bf16[4,256,576]{1,2,0:T(8,128)(2,1)} collective-permute-done((bf16[4,256,576]{1,2,0:T(8,128)(2,1)}, bf16[4,256,576]{1,2,0:T(8,128)(2,1)}, u32[]{:S(2)}, u32[]{:S(2)}) %collective-permute-start.13) | collective-permute-done | bytes 1179680 | tf_op jit(solution)/shard_map/ppermute | solution.py:319
  151.2 0.0 collective-permute-start.14
  151.2 1.5 collective-permute-start.7
  152.7 0.2 collective-permute-start.6
  152.9 9.8 %collective-permute-done.7.refs_2_ = bf16[256,768]{1,0:T(8,128)(2,1)S(1)} collective-permute-done((bf16[256,768]{1,0:T(8,128)(2,1)S(1)}, bf16[256,768]{1,0:T(8,128)(2,1)S(1)}, u32[]{:S(2)}, u32[]{:S(2)}) %collective-permute-start.7) | collective-permute-done | bytes 393248 | tf_op jit(solution)/shard_map/ppermute | solution.py:319
  162.8 1.7 collective-permute-done.8.refs_3_
  164.5 10.8 %row_grads.1 = bf16[4,144,512]{2,1,0:T(8,128)(2,1)S(1)} custom-call(s32[2]{0:T(128)S(1)} %pad_add_fusion.ids_ref, bf16[256,768]{1,0:T(8,128)(2,1)S(1)} %copy-done.7, bf16[256,768]{1,0:T(8,128)(2,1)S(1)} %collective-permute-done.6.refs_1_, bf16[256,768]{1,0:T(8,128)(2,1)S(1)} %collective-permute-done.7.refs_2_, ...), custom_call_target="tpu_custom_call" | custom-call | tf_op jit(solution)/shard_map/row_grads/pallas_call | solution.py:427
  175.3 2.6 %collective-permute-start.11 = (bf16[144,512]{1,0:T(8,128)(2,1)S(1)}, bf16[144,512]{1,0:T(8,128)(2,1)S(1)}, u32[]{:S(2)}, u32[]{:S(2)}) collective-permute-start(bf16[144,512]{1,0:T(8,128)(2,1)S(1)} %get-tuple-element.40), channel_id=1, source_target_pairs={{0,12},{4,8},{8,4},{12,0},{1,13},{5,9},{9,5},{13,1},{2,14},{6,10},... | collective-permute-start | bytes 442376 | tf_op jit(solution)/shard_map/ppermute | solution.py:319
  177.9 1.8 collective-permute-start.9
  179.8 4.2 %collective-permute-done.11.refs_3_ = bf16[144,512]{1,0:T(8,128)(2,1)S(1)} collective-permute-done((bf16[144,512]{1,0:T(8,128)(2,1)S(1)}, bf16[144,512]{1,0:T(8,128)(2,1)S(1)}, u32[]{:S(2)}, u32[]{:S(2)}) %collective-permute-start.11) | collective-permute-done | bytes 147488 | tf_op jit(solution)/shard_map/ppermute | solution.py:319
  184.0 6.0 %collective-permute-done.10.refs_2_ = bf16[144,512]{1,0:T(8,128)(2,1)S(1)} collective-permute-done((bf16[144,512]{1,0:T(8,128)(2,1)S(1)}, bf16[144,512]{1,0:T(8,128)(2,1)S(1)}, u32[]{:S(2)}, u32[]{:S(2)}) %collective-permute-start.10) | collective-permute-done | bytes 147488 | tf_op jit(solution)/shard_map/ppermute | solution.py:319
  190.1 2.0 token_grads.1
  192.1 0.7 copy.42
  192.7 1.7 copy.38.refs_0_
  194.4 1.7 copy.40.refs_2_
  196.1 2.4 %copy.39.refs_1_ = bf16[4,256,576]{2,1,0:T(8,128)(2,1)} copy(bf16[4,256,576]{1,2,0:T(8,128)(2,1)} %collective-permute-done.12) | data formatting | bytes 2359296 | tf_op jit(solution)/shard_map/ppermute | solution.py:319
  198.5 2.5 %copy.41.refs_3_ = bf16[4,256,576]{2,1,0:T(8,128)(2,1)} copy(bf16[4,256,576]{1,2,0:T(8,128)(2,1)} %collective-permute-done.14) | data formatting | bytes 2359296 | tf_op jit(solution)/shard_map/ppermute | solution.py:319
  201.0 1.3 copy-done.1
  202.3 1.3 copy-done.2
  203.6 20.4 %weight_grads.1 = (bf16[16,384,512]{2,1,0:T(8,128)(2,1)}, bf16[16,192,512]{2,1,0:T(8,128)(2,1)}) custom-call(s32[2]{0:T(128)S(1)} %pad_add_fusion.ids_ref, s32[16,4]{1,0:T(8,128)S(1)} %copy.30.table_ref, bf16[4,256,576]{2,1,0:T(8,128)(2,1)S(1)} %copy.38.refs_0_, bf16[4,256,576]{2,1,0:T(8,128)(2,1)S(1)} %copy-done.1, bf16[4,256,576]{2,1,0:T(8,128)(2,1)S(1)} %copy.40.refs_2_, ...), custom_call_target="tpu_custom_call" | custom-call | tf_op jit(solution)/shard_map/weight_grads/pallas_call | solution.py:468
  (23 shorter events, 0.1 us)
Async XLA Ops:
  7.2 4.6 %copy-start.8 = (bf16[128,512]{1,0:T(8,128)(2,1)S(1)}, bf16[128,512]{1,0:T(8,128)(2,1)}, u32[]{:S(2)}) copy-start(bf16[128,512]{1,0:T(8,128)(2,1)} %grad_ref.1) | copy-start | bytes 393220
  7.2 193.8 %all-gather.2.cloned.1.call-start = ((), (), s32[]{:S(2)}) async-start(), calls=%async_computation.1 | async-start | bytes 5242880 | tf_op jit(solution)/shard_map/all_gather | solution.py:352
  12.3 9.8 %collective-permute-start.2 = (bf16[144,512]{1,0:T(8,128)(2,1)S(1)}, bf16[144,512]{1,0:T(8,128)(2,1)S(1)}, u32[]{:S(2)}, u32[]{:S(2)}) collective-permute-start(bf16[144,512]{1,0:T(8,128)(2,1)S(1)} %route.1.refs_0_), channel_id=1, source_target_pairs={{0,12},{4,8},{8,4},{12,0},{1,13},{5,9},{9,5},{13,1},{2,14},{6,10},... | collective-permute-start | bytes 442376 | tf_op jit(solution)/shard_map/ppermute | solution.py:319
  17.4 26.8 %collective-permute-start.1 = (bf16[144,512]{1,0:T(8,128)(2,1)S(1)}, bf16[144,512]{1,0:T(8,128)(2,1)S(1)}, u32[]{:S(2)}, u32[]{:S(2)}) collective-permute-start(bf16[144,512]{1,0:T(8,128)(2,1)S(1)} %route.1.refs_0_), channel_id=1, source_target_pairs={{0,8},{4,12},{8,0},{12,4},{1,9},{5,13},{9,1},{13,5},{2,10},{6,14},... | collective-permute-start | bytes 442376 | tf_op jit(solution)/shard_map/ppermute | solution.py:319
  17.4 26.8 %collective-permute-start = (bf16[144,512]{1,0:T(8,128)(2,1)S(1)}, bf16[144,512]{1,0:T(8,128)(2,1)S(1)}, u32[]{:S(2)}, u32[]{:S(2)}) collective-permute-start(bf16[144,512]{1,0:T(8,128)(2,1)S(1)} %route.1.refs_0_), channel_id=1, source_target_pairs={{0,4},{4,0},{8,12},{12,8},{1,5},{5,1},{9,13},{13,9},{2,6},{6,2},{1... | collective-permute-start | bytes 442376 | tf_op jit(solution)/shard_map/ppermute | solution.py:319
  52.1 0.8 copy-start.4
  52.9 1.9 collective-permute-start.3
  52.9 11.9 %collective-permute-start.4 = (bf16[256,768]{1,0:T(8,128)(2,1)S(1)}, bf16[256,768]{1,0:T(8,128)(2,1)S(1)}, u32[]{:S(2)}, u32[]{:S(2)}) collective-permute-start(bf16[256,768]{1,0:T(8,128)(2,1)S(1)} %get-tuple-element.18), channel_id=1, source_target_pairs={{0,2},{1,3},{2,0},{3,1},{4,6},{5,7},{6,4},{7,5},{8,10},{9,11},{10,... | collective-permute-start | bytes 1179656 | tf_op jit(solution)/shard_map/ppermute | solution.py:319
  54.3 18.2 %collective-permute-start.5 = (bf16[256,768]{1,0:T(8,128)(2,1)S(1)}, bf16[256,768]{1,0:T(8,128)(2,1)S(1)}, u32[]{:S(2)}, u32[]{:S(2)}) collective-permute-start(bf16[256,768]{1,0:T(8,128)(2,1)S(1)} %get-tuple-element.19), channel_id=1, source_target_pairs={{0,3},{1,2},{2,1},{3,0},{4,7},{5,6},{6,5},{7,4},{8,11},{9,10},{10,... | collective-permute-start | bytes 1179656 | tf_op jit(solution)/shard_map/ppermute | solution.py:319
  75.0 1.1 copy-start.3
  76.0 0.8 copy-start.6
  76.8 87.7 %copy-start = (bf16[8,128,1536]{2,1,0:T(8,128)(2,1)S(1)}, bf16[8,128,1536]{2,1,0:T(8,128)(2,1)}, u32[]{:S(2)}) copy-start(bf16[8,128,1536]{2,1,0:T(8,128)(2,1)} %param.17) | copy-start | bytes 9437188
  79.3 71.9 %copy-start.7 = (bf16[256,768]{1,0:T(8,128)(2,1)S(1)}, bf16[256,768]{1,0:T(8,128)(2,1)}, u32[]{:S(2)}) copy-start(bf16[256,768]{1,0:T(8,128)(2,1)} %copy-done.6) | copy-start | bytes 1179652
  123.1 28.2 %collective-permute-start.13 = (bf16[4,256,576]{1,2,0:T(8,128)(2,1)}, bf16[4,256,576]{1,2,0:T(8,128)(2,1)}, u32[]{:S(2)}, u32[]{:S(2)}) collective-permute-start(bf16[4,256,576]{1,2,0:T(8,128)(2,1)} %all_to_all.5), channel_id=1, source_target_pairs={{0,2},{1,3},{2,0},{3,1},{4,6},{5,7},{6,4},{7,5},{8,10},{9,11},{10,... | collective-permute-start | bytes 3538952 | tf_op jit(solution)/shard_map/ppermute | solution.py:319
  124.5 71.6 %collective-permute-start.12 = (bf16[4,256,576]{1,2,0:T(8,128)(2,1)}, bf16[4,256,576]{1,2,0:T(8,128)(2,1)}, u32[]{:S(2)}, u32[]{:S(2)}) collective-permute-start(bf16[4,256,576]{1,2,0:T(8,128)(2,1)} %all_to_all.5), channel_id=1, source_target_pairs={{0,1},{1,0},{2,3},{3,2},{4,5},{5,4},{6,7},{7,6},{8,9},{9,8},{10,11... | collective-permute-start | bytes 3538952 | tf_op jit(solution)/shard_map/ppermute | solution.py:319
  151.2 47.3 %collective-permute-start.14 = (bf16[4,256,576]{1,2,0:T(8,128)(2,1)}, bf16[4,256,576]{1,2,0:T(8,128)(2,1)}, u32[]{:S(2)}, u32[]{:S(2)}) collective-permute-start(bf16[4,256,576]{1,2,0:T(8,128)(2,1)} %collective-permute-done.13), channel_id=1, source_target_pairs={{0,1},{1,0},{2,3},{3,2},{4,5},{5,4},{6,7},{7,6},{8,9},{9,8},{10,11... | collective-permute-start | bytes 3538952 | tf_op jit(solution)/shard_map/ppermute | solution.py:319
  151.2 11.5 %collective-permute-start.7 = (bf16[256,768]{1,0:T(8,128)(2,1)S(1)}, bf16[256,768]{1,0:T(8,128)(2,1)S(1)}, u32[]{:S(2)}, u32[]{:S(2)}) collective-permute-start(bf16[256,768]{1,0:T(8,128)(2,1)S(1)} %copy-done.7), channel_id=1, source_target_pairs={{0,2},{1,3},{2,0},{3,1},{4,6},{5,7},{6,4},{7,5},{8,10},{9,11},{10,... | collective-permute-start | bytes 1179656 | tf_op jit(solution)/shard_map/ppermute | solution.py:319
  152.7 10.1 %collective-permute-start.6 = (bf16[256,768]{1,0:T(8,128)(2,1)S(1)}, bf16[256,768]{1,0:T(8,128)(2,1)S(1)}, u32[]{:S(2)}, u32[]{:S(2)}) collective-permute-start(bf16[256,768]{1,0:T(8,128)(2,1)S(1)} %copy-done.7), channel_id=1, source_target_pairs={{0,1},{1,0},{2,3},{3,2},{4,5},{5,4},{6,7},{7,6},{8,9},{9,8},{10,11... | collective-permute-start | bytes 1179656 | tf_op jit(solution)/shard_map/ppermute | solution.py:319
  162.8 1.7 collective-permute-start.8
  175.3 8.7 %collective-permute-start.11 = (bf16[144,512]{1,0:T(8,128)(2,1)S(1)}, bf16[144,512]{1,0:T(8,128)(2,1)S(1)}, u32[]{:S(2)}, u32[]{:S(2)}) collective-permute-start(bf16[144,512]{1,0:T(8,128)(2,1)S(1)} %get-tuple-element.40), channel_id=1, source_target_pairs={{0,12},{4,8},{8,4},{12,0},{1,13},{5,9},{9,5},{13,1},{2,14},{6,10},... | collective-permute-start | bytes 442376 | tf_op jit(solution)/shard_map/ppermute | solution.py:319
  177.9 12.1 %collective-permute-start.10 = (bf16[144,512]{1,0:T(8,128)(2,1)S(1)}, bf16[144,512]{1,0:T(8,128)(2,1)S(1)}, u32[]{:S(2)}, u32[]{:S(2)}) collective-permute-start(bf16[144,512]{1,0:T(8,128)(2,1)S(1)} %get-tuple-element.41), channel_id=1, source_target_pairs={{0,8},{4,12},{8,0},{12,4},{1,9},{5,13},{9,1},{13,5},{2,10},{6,14},... | collective-permute-start | bytes 442376 | tf_op jit(solution)/shard_map/ppermute | solution.py:319
  177.9 12.1 %collective-permute-start.9 = (bf16[144,512]{1,0:T(8,128)(2,1)S(1)}, bf16[144,512]{1,0:T(8,128)(2,1)S(1)}, u32[]{:S(2)}, u32[]{:S(2)}) collective-permute-start(bf16[144,512]{1,0:T(8,128)(2,1)S(1)} %get-tuple-element.42), channel_id=1, source_target_pairs={{0,4},{4,0},{8,12},{12,8},{1,5},{5,1},{9,13},{13,9},{2,6},{6,2},{1... | collective-permute-start | bytes 442376 | tf_op jit(solution)/shard_map/ppermute | solution.py:319
  198.5 2.5 %copy-start.5 = (bf16[4,128,512]{2,1,0:T(8,128)(2,1)S(1)}, bf16[4,128,512]{2,1,0:T(8,128)(2,1)}, u32[]{:S(2)}) copy-start(bf16[4,128,512]{2,1,0:T(8,128)(2,1)} %copy-done.4) | copy-start | bytes 1572868
  201.0 1.3 copy-start.1
  202.3 1.3 copy-start.2
Sparse Core Ops, SparseCore 0:
  9.6 107.8 all-gather.1

commit v2 on v1

v2 whole, which is shorter than its diff:
```python
import functools
import math

import jax
import jax.numpy as jnp
from jax import lax
from jax.experimental import pallas as pl
from jax.experimental.pallas import tpu as pltpu
from jax.sharding import PartitionSpec as P

BF = jnp.bfloat16
F32 = jnp.float32
CUTS = 2


def nt(a, b):
    return lax.dot_general(a, b, (((1,), (1,)), ((), ())), preferred_element_type=F32)


def tn(a, b):
    return lax.dot_general(a, b, (((0,), (0,)), ((), ())), preferred_element_type=F32)


def nn(a, b):
    return jnp.dot(a, b, preferred_element_type=F32)


def whole(shape):
    zeros = (0,) * len(shape)
    return pl.BlockSpec(shape, lambda *_: zeros)


def smem():
    return pl.BlockSpec(memory_space=pltpu.SMEM)


def params(mib):
    return pltpu.CompilerParams(
        vmem_limit_bytes=mib * 1024 * 1024, dimension_semantics=("arbitrary",)
    )


class Sizes:
    def __init__(self, grad_out, routes, replica_slot, saved_input, weight_in, weight_down):
        self.ep = lax.axis_size("ep")
        self.sub = lax.axis_size("sub")
        self.tokens, self.width = grad_out.shape
        self.top = routes.shape[1]
        self.experts, self.reps = replica_slot.shape
        self.local = weight_in.shape[0]
        self.slots = self.ep * self.local
        self.cap = saved_input.shape[2]
        self.rows = self.ep * self.cap
        self.hidden = weight_down.shape[1]
        self.pair = weight_in.shape[1]
        self.all_rows = self.local * self.rows
        self.part = self.all_rows // self.sub
        self.block = math.gcd(self.rows, self.part)
        self.sources = self.block // self.cap
        self.blocks = self.all_rows // self.block
        self.part_blocks = self.part // self.block
        self.slot_blocks = self.rows // self.block
        self.in_cols = self.pair // self.ep
        self.down_cols = self.hidden // self.ep
        self.cols = self.in_cols + self.down_cols
        self.folds = self.width // self.tokens
        self.tail = 2 * self.slots // self.folds


def slot_table(z, table_ref, r):
    ids = lax.broadcasted_iota(jnp.int32, (z.slots, z.experts), 0)
    return (table_ref[r : r + 1, :] == ids).astype(F32).astype(BF)


def key_hits(z, count_ref, routes_ref, replica_ref, r, k):
    ids = lax.broadcasted_iota(jnp.int32, (z.experts, z.tokens), 0)
    live = lax.broadcasted_iota(jnp.int32, (1, z.tokens), 1) < count_ref[0]
    key = jnp.where(live & (replica_ref[k : k + 1, :] == r), routes_ref[k : k + 1, :], -1)
    return key == ids


def route_kernel(z, count_ref, grad_ref, weight_ref, routes_ref, replica_ref, table_ref, out_ref):
    weights = weight_ref[...].astype(F32)
    hits = jnp.zeros((z.slots, z.tokens), F32)
    loads = jnp.zeros((z.slots, z.tokens), F32)
    for r in range(z.reps):
        hit = jnp.zeros((z.experts, z.tokens), F32)
        load = jnp.zeros((z.experts, z.tokens), F32)
        for k in range(z.top):
            same = key_hits(z, count_ref, routes_ref, replica_ref, r, k)
            hit = jnp.where(same, 1.0, hit)
            load = jnp.where(same, weights[k : k + 1, :], load)
        table = slot_table(z, table_ref, r)
        hits = hits + nn(table, hit.astype(BF))
        loads = loads + nn(table, load.astype(BF))
    before = lax.broadcasted_iota(jnp.int32, (z.tokens, z.tokens), 0)
    after = lax.broadcasted_iota(jnp.int32, (z.tokens, z.tokens), 1)
    earlier = nn(hits.astype(BF), (before < after).astype(F32).astype(BF))
    code = jnp.where(hits > 0.5, earlier, -1.0)
    both = jnp.concatenate([code, loads], axis=0).astype(BF)
    out_ref[: z.tokens, :] = grad_ref[...]
    for b in range(z.folds):
        out_ref[z.tokens :, b * z.tokens : (b + 1) * z.tokens] = both[
            b * z.tail : (b + 1) * z.tail, :
        ]


def block_place(z, block):
    slot = block // z.slot_blocks
    first = (block % z.slot_blocks) * z.sources
    return slot, first


def block_picks(z, codes_ref, slot, first):
    rows = lax.broadcasted_iota(jnp.int32, (z.cap, z.tokens), 0).astype(F32)
    for a in range(z.sources):
        code = codes_ref[first + a, pl.ds(slot, 1), :]
        yield a, rows == code


def block_scale(z, codes_ref, slot, first):
    parts = []
    for a, pick in block_picks(z, codes_ref, slot, first):
        load = codes_ref[first + a, pl.ds(z.slots + slot, 1), :]
        parts.append(jnp.sum(jnp.where(pick, load, 0.0), axis=1, keepdims=True))
    return jnp.concatenate(parts, axis=0)


def scaled_rows(z, codes_ref, grads_ref, slot, first):
    parts = []
    for a, pick in block_picks(z, codes_ref, slot, first):
        load = codes_ref[first + a, pl.ds(z.slots + slot, 1), :]
        parts.append(nn(jnp.where(pick, load, 0.0).astype(BF), grads_ref[first + a]))
    return jnp.concatenate(parts, axis=0).astype(BF)


def local_picks(z, codes_ref, source, me):
    code = codes_ref[source, pl.ds(pl.multiple_of(me * z.local, z.local), z.local), :]
    rows = lax.broadcasted_iota(jnp.int32, (z.local, z.cap, z.tokens), 1).astype(F32)
    pick = (code[:, None, :] == rows).astype(F32)
    return pick.reshape(z.local * z.cap, z.tokens).astype(BF)


def down_kernel(z, ids_ref, *refs):
    bufs = refs[: z.ep]
    weight_ref = refs[z.ep]
    parts = refs[z.ep + 1 : z.ep + 1 + z.sub]
    grads_ref, codes_ref, rows_ref = refs[z.ep + 1 + z.sub :]
    me, mine = ids_ref[0], ids_ref[1]
    step = pl.program_id(0)

    @pl.when(step == 0)
    def _():
        for k in range(z.ep):
            source = me ^ k
            grads_ref[source] = bufs[k][: z.tokens, :]
            for b in range(z.folds):
                codes_ref[source, b * z.tail : (b + 1) * z.tail, :] = bufs[k][
                    z.tokens :, b * z.tokens : (b + 1) * z.tokens
                ].astype(F32)
        for p in range(z.ep):
            rows = nn(local_picks(z, codes_ref, p, me), grads_ref[p]).astype(BF)
            rows_ref[:, p * z.cap : (p + 1) * z.cap, :] = rows.reshape(z.local, z.cap, z.width)

    place = step // z.part_blocks
    block = (place ^ mine) * z.part_blocks + step % z.part_blocks
    slot, first = block_place(z, block)
    start = pl.multiple_of(first * z.cap, z.block)
    partial = nt(rows_ref[slot, pl.ds(start, z.block), :], weight_ref[0]).astype(BF)
    spot = pl.multiple_of((step % z.part_blocks) * z.block, z.block)
    for k in range(z.sub):

        @pl.when(place == k)
        def _():
            parts[k][pl.ds(spot, z.block), :] = partial


def gate_terms(z, pair, grad, scale):
    gate = pair[:, : z.hidden].astype(F32)
    up = pair[:, z.hidden :].astype(F32)
    sig = 1.0 / (1.0 + jnp.exp(-gate))
    act = gate * sig
    hidden = act * up
    scaled = scale * grad
    grad_gate = scaled * up * sig * (1.0 + gate * (1.0 - sig))
    grad_up = scaled * act
    return hidden, grad_gate.astype(BF), grad_up.astype(BF)


def pre_kernel(z, ids_ref, *refs):
    parts = refs[: z.sub]
    pair_ref, codes_ref, out_ref, grad_ref = refs[z.sub :]
    block = ids_ref[1] * z.part_blocks + pl.program_id(0)
    slot, first = block_place(z, block)
    scale = block_scale(z, codes_ref, ids_ref[0] * z.local + slot, first)
    grad = parts[0][...].astype(F32)
    for k in range(1, z.sub):
        grad = grad + parts[k][...].astype(F32)
    grad_ref[...] = grad.astype(BF)
    hidden, grad_gate, grad_up = gate_terms(z, pair_ref[...], grad, scale)
    hidden = hidden.astype(BF).T
    pre = jnp.concatenate([grad_gate.T, grad_up.T], axis=0)
    for q in range(z.ep):
        out_ref[q, : z.in_cols, :] = pre[q * z.in_cols : (q + 1) * z.in_cols, :]
        out_ref[q, z.in_cols :, :] = hidden[q * z.down_cols : (q + 1) * z.down_cols, :]


def row_kernel(z, ids_ref, *refs):
    grads = refs[: z.sub]
    pair_ref, weight_ref, codes_ref, out_ref, rows_ref, marks, held = refs[z.sub :]
    me, mine = ids_ref[0], ids_ref[1]
    step = pl.program_id(0)
    place = step // z.part_blocks
    block = (place ^ mine) * z.part_blocks + step % z.part_blocks
    slot, first = block_place(z, block)

    @pl.when(step == 0)
    def _():
        marks[...] = jnp.zeros_like(marks)

    spot = pl.multiple_of((step % z.part_blocks) * z.block, z.block)
    for k in range(z.sub):

        @pl.when(place == k)
        def _():
            held[...] = grads[k][pl.ds(spot, z.block), :]

    grad = held[...].astype(F32)
    scale = block_scale(z, codes_ref, me * z.local + slot, first)
    hidden, grad_gate, grad_up = gate_terms(z, pair_ref[...], grad, scale)
    route = jnp.sum(hidden * grad, axis=1, keepdims=True).astype(BF).astype(F32)
    rows = nn(grad_gate, weight_ref[0, : z.hidden, :]) + nn(grad_up, weight_ref[0, z.hidden :, :])
    start = pl.multiple_of(first * z.cap, z.block)
    rows_ref[slot, pl.ds(start, z.block), :] = rows.astype(BF)
    for a, pick in block_picks(z, codes_ref, me * z.local + slot, first):
        marks[first + a, pl.ds(slot, 1), :] = jnp.sum(
            jnp.where(pick, route[a * z.cap : (a + 1) * z.cap, :], 0.0), axis=0, keepdims=True
        )

    @pl.when(step == z.blocks - 1)
    def _():
        for p in range(z.ep):
            rows = rows_ref[:, p * z.cap : (p + 1) * z.cap, :].reshape(z.local * z.cap, z.width)
            out_ref[p ^ me, : z.tokens, :] = tn(local_picks(z, codes_ref, p, me), rows).astype(BF)
            out_ref[p ^ me, z.tokens :, : z.tokens] = marks[p].astype(BF)
            out_ref[p ^ me, z.tokens :, z.tokens :] = jnp.zeros(
                (marks.shape[1], z.width - z.tokens), BF
            )


def token_kernel(z, ids_ref, count_ref, *refs):
    got = refs[: z.ep]
    routes_ref, replica_ref, table_ref, tokens_ref, route_ref, marks = refs[z.ep :]
    me = ids_ref[0]
    total = got[0][: z.tokens, :].astype(F32)
    for k in range(1, z.ep):
        total = total + got[k][: z.tokens, :].astype(F32)
    tokens_ref[...] = total.astype(BF)
    for k in range(z.ep):
        marks[me ^ k] = got[k][z.tokens :, : z.tokens].astype(F32)
    rows = jnp.concatenate([marks[p][: z.local, :] for p in range(z.ep)], axis=0).astype(BF)
    totals = [jnp.zeros((1, z.tokens), F32)] * z.top
    for r in range(z.reps):
        spread = tn(slot_table(z, table_ref, r), rows)
        for k in range(z.top):
            same = key_hits(z, count_ref, routes_ref, replica_ref, r, k)
            totals[k] += jnp.sum(jnp.where(same, spread, 0.0), axis=0, keepdims=True)
    route_ref[...] = jnp.concatenate(totals, axis=0).astype(BF)


def total_kernel(z, down, ids_ref, table_ref, *refs):
    sides = refs[: z.sub]
    inputs_ref, grads_ref, codes_ref = refs[z.sub : z.sub + 3]
    if down:
        in_ref, down_ref, held, sems = refs[z.sub + 3 :]
    else:
        in_ref, held, sems = refs[z.sub + 4 :]
    mine = ids_ref[1]
    expert = pl.program_id(0)

    @pl.when(expert == 0)
    def _():
        copies = [
            pltpu.make_async_copy(sides[k], held.at[k], sems.at[k]) for k in range(z.sub)
        ]
        for copy in copies:
            copy.start()
        for copy in copies:
            copy.wait()

    slot_ids = [table_ref[r, expert] for r in range(z.reps)]
    count = 1
    for r in range(1, z.reps):
        count = count + (slot_ids[r] != slot_ids[0]).astype(jnp.int32)

    def add(used):
        lefts, rights, rows = [], [], []
        for slot_id in used:
            source = slot_id // z.local
            for b in range(z.slot_blocks):
                block = (slot_id % z.local) * z.slot_blocks + b
                part = (block // z.part_blocks) ^ mine
                spot = pl.multiple_of((block % z.part_blocks) * z.block, z.block)
                lefts.append(held[part, source, :, pl.ds(spot, z.block)])
                start = pl.multiple_of(block * z.block, z.block)
                rights.append(inputs_ref[source, pl.ds(start, z.block), :])
                if down:
                    rows.append(scaled_rows(z, codes_ref, grads_ref, slot_id, b * z.sources))
        left = jnp.concatenate(lefts, axis=1)
        in_ref[0] = nn(left[: z.in_cols, :], jnp.concatenate(rights, axis=0)).astype(BF)
        if down:
            down_ref[0] = nn(left[z.in_cols :, :], jnp.concatenate(rows, axis=0)).astype(BF)

    for c in range(1, z.reps + 1):

        @pl.when(count == c)
        def _():
            add(slot_ids[:c])


def swap(x, axis, size, bit):
    return lax.ppermute(x, axis, [(i, i ^ bit) for i in range(size)])


def spread_over(x, axis, size):
    have = {0: x}
    bit = size // 2
    while bit:
        for k in list(have):
            have[k | bit] = swap(have[k], axis, size, bit)
        bit //= 2
    return [have[k] for k in range(size)]


def body(
    grad_out,
    route_weight,
    routes,
    replica,
    replica_slot,
    token_count,
    saved_input,
    saved_gate_up,
    weight_in,
    weight_down,
):
    z = Sizes(grad_out, routes, replica_slot, saved_input, weight_in, weight_down)
    n, m = z.ep, z.sub
    ids = jnp.stack([lax.axis_index("ep"), lax.axis_index("sub")]).astype(jnp.int32)
    routes, replica, table = routes.T, replica.T, replica_slot.T
    route_weight = route_weight.T
    pair_rows = saved_gate_up.reshape(z.all_rows, z.pair)
    grad_shape = (z.tokens + z.tail, z.width)
    code_shape = (n, 2 * z.slots, z.tokens)
    chunk = z.width // CUTS
    inputs = saved_input.reshape(z.all_rows, z.width)
    inputs = [inputs[:, c * chunk : (c + 1) * chunk] for c in range(CUTS)]

    buf = pl.pallas_call(
        functools.partial(route_kernel, z),
        out_shape=jax.ShapeDtypeStruct(grad_shape, BF),
        in_specs=[smem()]
        + [whole(a.shape) for a in (grad_out, route_weight, routes, replica, table)],
        out_specs=whole(grad_shape),
        grid=(1,),
        compiler_params=params(4),
        name="route",
    )(token_count, grad_out, route_weight, routes, replica, table)
    bufs = [buf] + [swap(buf, "ep", n, k) for k in range(1, n)]
    bufs, inputs[0] = lax.optimization_barrier((bufs, inputs[0]))
    gathered = [lax.all_gather(inputs[0], "ep")]

    def row_block(i, ids_ref):
        place = i // z.part_blocks
        return (place ^ ids_ref[1]) * z.part_blocks + i % z.part_blocks

    def row_slot(i, ids_ref):
        return row_block(i, ids_ref) // z.slot_blocks

    outs = pl.pallas_call(
        functools.partial(down_kernel, z),
        grid_spec=pltpu.PrefetchScalarGridSpec(
            num_scalar_prefetch=1,
            grid=(z.blocks,),
            in_specs=[whole(grad_shape)] * n
            + [pl.BlockSpec((1, z.hidden, z.width), lambda i, r: (row_slot(i, r), 0, 0))],
            out_specs=[whole((z.part, z.hidden))] * m
            + [whole((n, z.tokens, z.width)), whole(code_shape)],
            scratch_shapes=[pltpu.VMEM((z.local, z.rows, z.width), BF)],
        ),
        out_shape=[jax.ShapeDtypeStruct((z.part, z.hidden), BF)] * m
        + [
            jax.ShapeDtypeStruct((n, z.tokens, z.width), BF),
            jax.ShapeDtypeStruct(code_shape, F32),
        ],
        compiler_params=params(16),
        name="hidden_partials",
    )(ids, *bufs, weight_down)
    parts, (grads_all, codes) = outs[:m], outs[m:]
    parts = [parts[0]] + [swap(parts[k], "sub", m, k) for k in range(1, m)]

    pre, grad_part = pl.pallas_call(
        functools.partial(pre_kernel, z),
        grid_spec=pltpu.PrefetchScalarGridSpec(
            num_scalar_prefetch=1,
            grid=(z.part_blocks,),
            in_specs=[pl.BlockSpec((z.block, z.hidden), lambda i, r: (i, 0))] * m
            + [
                pl.BlockSpec((z.block, z.pair), lambda i, r: (r[1] * z.part_blocks + i, 0)),
                whole(code_shape),
            ],
            out_specs=[
                pl.BlockSpec((n, z.cols, z.block), lambda i, r: (0, 0, i)),
                pl.BlockSpec((z.block, z.hidden), lambda i, r: (i, 0)),
            ],
        ),
        out_shape=[
            jax.ShapeDtypeStruct((n, z.cols, z.part), BF),
            jax.ShapeDtypeStruct((z.part, z.hidden), BF),
        ],
        compiler_params=params(16),
        name="pre_grads",
    )(ids, *parts, pair_rows, codes)

    grad_parts = spread_over(grad_part, "sub", m)
    columns = lax.all_to_all(pre, "ep", split_axis=0, concat_axis=0, tiled=True)
    columns, *inputs[1:] = lax.optimization_barrier((columns, *inputs[1:]))
    gathered += [lax.all_gather(a, "ep") for a in inputs[1:]]
    sides = spread_over(columns, "sub", m)

    mark_rows = -(-z.local // 16) * 16
    back_shape = (n, z.tokens + mark_rows, z.width)
    back = pl.pallas_call(
        functools.partial(row_kernel, z),
        grid_spec=pltpu.PrefetchScalarGridSpec(
            num_scalar_prefetch=1,
            grid=(z.blocks,),
            in_specs=[whole((z.part, z.hidden))] * m
            + [
                pl.BlockSpec((z.block, z.pair), lambda i, r: (row_block(i, r), 0)),
                pl.BlockSpec((1, z.pair, z.width), lambda i, r: (row_slot(i, r), 0, 0)),
                whole(code_shape),
            ],
            out_specs=whole(back_shape),
            scratch_shapes=[
                pltpu.VMEM((z.local, z.rows, z.width), BF),
                pltpu.VMEM((n, mark_rows, z.tokens), F32),
                pltpu.VMEM((z.block, z.hidden), BF),
            ],
        ),
        out_shape=jax.ShapeDtypeStruct(back_shape, BF),
        compiler_params=params(24),
        name="row_grads",
    )(ids, *grad_parts, pair_rows, weight_in, codes)
    got = [back[0]] + [swap(back[k], "ep", n, k) for k in range(1, n)]

    grad_tokens, grad_routes = pl.pallas_call(
        functools.partial(token_kernel, z),
        out_shape=[
            jax.ShapeDtypeStruct((z.tokens, z.width), BF),
            jax.ShapeDtypeStruct((z.top, z.tokens), BF),
        ],
        in_specs=[smem(), smem()]
        + [whole(back_shape[1:])] * n
        + [whole(a.shape) for a in (routes, replica, table)],
        out_specs=[whole((z.tokens, z.width)), whole((z.top, z.tokens))],
        grid=(1,),
        scratch_shapes=[pltpu.VMEM((n, mark_rows, z.tokens), F32)],
        compiler_params=params(8),
        name="token_grads",
    )(ids, token_count, *got, routes, replica, table)

    in_shape = jax.ShapeDtypeStruct((z.experts, z.in_cols, z.width), BF)
    down_shape = jax.ShapeDtypeStruct((z.experts, z.down_cols, z.width), BF)
    grad_in, grad_down = None, None
    for c in range(CUTS):
        first = c == 0
        in_spec = pl.BlockSpec((1, z.in_cols, chunk), lambda e, r, t, c=c: (e, 0, c))
        down_spec = pl.BlockSpec((1, z.down_cols, z.width), lambda e, r, t: (e, 0, 0))
        out = pl.pallas_call(
            functools.partial(total_kernel, z, first),
            grid_spec=pltpu.PrefetchScalarGridSpec(
                num_scalar_prefetch=2,
                grid=(z.experts,),
                in_specs=[pl.BlockSpec(memory_space=pl.ANY)] * m
                + [
                    whole((n, z.all_rows, chunk)),
                    whole((n, z.tokens, z.width)),
                    whole(code_shape),
                ]
                + ([] if first else [pl.BlockSpec(memory_space=pl.ANY)]),
                out_specs=[in_spec, down_spec] if first else [in_spec],
                scratch_shapes=[
                    pltpu.VMEM((m, n, z.cols, z.part), BF),
                    pltpu.SemaphoreType.DMA((m,)),
                ],
            ),
            out_shape=[in_shape, down_shape] if first else [in_shape],
            input_output_aliases={} if first else {2 + m + 3: 0},
            compiler_params=params(24),
            name="weight_grads",
        )(
            ids,
            table,
            *sides,
            gathered[c],
            grads_all,
            codes,
            *([] if first else [grad_in]),
        )
        grad_in = out[0]
        if first:
            grad_down = out[1]
    return grad_tokens, grad_routes.T, grad_in, grad_down


def solution(mesh):
    return jax.shard_map(
        body,
        mesh=mesh,
        in_specs=(
            P(("groups", "ep"), "sub"),
            P(("groups", "ep"), None),
            P(("groups", "ep"), None),
            P(("groups", "ep"), None),
            P("groups", None),
            P(("groups", "ep")),
            P(("groups", "ep"), None, None, "sub"),
            P(("groups", "ep"), None, None),
            P(("groups", "ep"), None, "sub"),
            P(("groups", "ep"), None, "sub"),
        ),
        out_specs=(
            P(("groups", "ep"), "sub"),
            P(("groups", "ep"), None),
            P("groups", "ep", "sub"),
            P("groups", "ep", "sub"),
        ),
        check_vma=False,
    )
```

time: 232 us -> 206 us (0.89)
  waiting for transfers between devices: 93.1 us -> 75.4 us
  Pallas kernels: 44.2 us -> 37.8 us
  blocking collectives: 43.7 us -> 39.8 us
    ppermute x15, waiting for transfers between devices: 92.4 us -> 75.3 us  [swap(): return lax.ppermute(x, axis, [(i, i ^ bit) for i in range(size)])]
    unnamed x23 -> x48, local copies, waits for them, and re-layouts: 9.02 us -> 19.9 us
    ppermute x3 -> x0, local copies, waits for them, and re-layouts: 6.54 us -> none  [swap(): return lax.ppermute(x, axis, [(i, i ^ bit) for i in range(size)])]
    pallas_call x1, Pallas kernels: 10.8 us -> 5.69 us  [body(): pl.pallas_call(functools.partial(row_kernel, z), grid_spec=pltpu.Prefetch...]
    all_to_all x1, blocking collectives: 43.7 us -> 39.8 us  [body(): columns = lax.all_to_all(pre, 'ep', split_axis=0, concat_axis=0, tiled=True)]
    pallas_call x1 -> x2, Pallas kernels: 20.4 us -> 24.3 us  [body(): pl.pallas_call(functools.partial(total_kernel, z, first), grid_spec=pltpu...]
    pallas_call x1, Pallas kernels: 7.95 us -> 4.42 us  [body(): pl.pallas_call(functools.partial(down_kernel, z), grid_spec=pltpu.Prefetc...]
    pallas_call x1 -> x0, local copies, waits for them, and re-layouts: 2.54 us -> none  [body(): pl.pallas_call(functools.partial(pre_kernel, z), grid_spec=pltpu.Prefetch...]
  transfers between devices with their start and end apart: 16 -> 17, of which waited for: 9 -> 9; matrix products, arithmetic and copies ran while one was open for 6% -> 1% of each run, Pallas kernels for 10% -> 13%
where the time goes in v2:
time: 206 us
  waiting for transfers between devices  75.4 us (37%)
  blocking collectives  39.8 us (19%)
  Pallas kernels  37.8 us (18%)
  local copies, waits for them, and re-layouts  22.2 us (11%)
  starting transfers between devices  15.5 us (8%)
  between operations  14.9 us (7%)
    ppermute x15, waiting for transfers between devices, swap(): return lax.ppermute(x, axis, [(i, i ^ bit) for i in range(size)])  75.3 us
    all_to_all x1, blocking collectives, body(): columns = lax.all_to_all(pre, 'ep', split_axis=0, concat_axis=0, tiled=True)  39.8 us
    pallas_call x2, Pallas kernels, body(): pl.pallas_call(functools.partial(total_kernel, z, first), grid_spec=pltpu...  24.3 us
    unnamed x48, local copies, waits for them, and re-layouts  19.9 us
    ppermute x15, starting transfers between devices, swap(): return lax.ppermute(x, axis, [(i, i ^ bit) for i in range(size)])  15.4 us
    pallas_call x1, Pallas kernels, body(): pl.pallas_call(functools.partial(row_kernel, z), grid_spec=pltpu.Prefetch...  5.69 us
    pallas_call x1, Pallas kernels, body(): pl.pallas_call(functools.partial(down_kernel, z), grid_spec=pltpu.Prefetc...  4.42 us
  transfers between devices with their start and end apart: 17, of which 9 were waited for; matrix products, arithmetic and copies ran while one was open for 1% of the time, Pallas kernels for 13%

profile of v2, /device:TPU:0, one launch (start us, length us, event | category | flops | bytes accessed | tf_op | source)
XLA Modules:
  0.0 205.6 jit_solution(1803021760395423185)
XLA Ops:
  7.2 0.0 all-gather.7.cloned.1.call-start
  7.9 0.9 copy-done.16
  8.8 0.7 copy-done.17
  9.4 0.7 copy-done.19
  10.1 0.7 copy-done.21
  10.8 0.7 copy-done.23
  11.5 0.3 route.1.refs_0_
  11.8 5.1 %collective-permute-start.2 = (bf16[144,512]{1,0:T(8,128)(2,1)S(1)}, bf16[144,512]{1,0:T(8,128)(2,1)S(1)}, u32[]{:S(2)}, u32[]{:S(2)}) collective-permute-start(bf16[144,512]{1,0:T(8,128)(2,1)S(1)} %route.1.refs_0_), channel_id=1, source_target_pairs={{0,12},{4,8},{8,4},{12,0},{1,13},{5,9},{9,5},{13,1},{2,14},{6,10},... | collective-permute-start | bytes 442376 | tf_op jit(solution)/shard_map/ppermute | solution.py:322
  16.8 0.6 collective-permute-start
  17.4 2.2 %fusion = (bf16[1024,256]{1,0:T(8,128)(2,1)}, bf16[1024,256]{1,0:T(8,128)(2,1)}) fusion(bf16[1024,512]{1,0:T(8,128)(2,1)} %bitcast.32), kind=kLoop, calls=%fused_computation.5 | loop fusion | bytes 2097152 | tf_op jit(solution)/shard_map/slice | solution.py:357
  19.7 1.9 collective-permute-done.2.refs_3_
  21.6 0.7 copy-done.10
  22.3 7.0 %collective-permute-done.1.refs_2_ = bf16[144,512]{1,0:T(8,128)(2,1)S(1)} collective-permute-done((bf16[144,512]{1,0:T(8,128)(2,1)S(1)}, bf16[144,512]{1,0:T(8,128)(2,1)S(1)}, u32[]{:S(2)}, u32[]{:S(2)}) %collective-permute-start.1) | collective-permute-done | bytes 147488 | tf_op jit(solution)/shard_map/ppermute | solution.py:322
  29.3 0.7 copy-done.12
  30.0 0.7 copy-done.14
  30.7 0.0 all-gather.5.cloned.1.call-start
  30.7 0.1 pad_add_fusion.ids_ref
  30.8 2.8 %copy-done.3 = bf16[8,768,512]{2,1,0:T(8,128)(2,1)S(1)} copy-done((bf16[8,768,512]{2,1,0:T(8,128)(2,1)S(1)}, bf16[8,768,512]{2,1,0:T(8,128)(2,1)}, u32[]{:S(2)}) %copy-start.3) | copy-done | bytes 6291480
  33.6 0.9 copy-done.11
  34.5 0.9 copy-done.13
  35.4 0.9 copy-done.15
  36.3 4.4 %hidden_partials.1 = (bf16[256,768]{1,0:T(8,128)(2,1)S(1)}, bf16[256,768]{1,0:T(8,128)(2,1)S(1)}, bf16[256,768]{1,0:T(8,128)(2,1)S(1)}, bf16[256,768]{1,0:T(8,12...) custom-call(s32[2]{0:T(128)S(1)} %pad_add_fusion.ids_ref, bf16[144,512]{1,0:T(8,128)(2,1)S(1)} %route.1.refs_0_, ...), custom_call_target="tpu_custom_call" | custom-call | tf_op jit(solution)/shard_map/hidden_partials/pallas_call | solution.py:380
  40.8 0.1 collective-permute-start.3
  40.8 1.6 collective-permute-start.4
  42.4 0.3 collective-permute-start.5
  42.7 10.1 %collective-permute-done.4.refs_2_ = bf16[256,768]{1,0:T(8,128)(2,1)S(1)} collective-permute-done((bf16[256,768]{1,0:T(8,128)(2,1)S(1)}, bf16[256,768]{1,0:T(8,128)(2,1)S(1)}, u32[]{:S(2)}, u32[]{:S(2)}) %collective-permute-start.4) | collective-permute-done | bytes 393248 | tf_op jit(solution)/shard_map/ppermute | solution.py:322
  52.8 7.5 %collective-permute-done.5.refs_3_ = bf16[256,768]{1,0:T(8,128)(2,1)S(1)} collective-permute-done((bf16[256,768]{1,0:T(8,128)(2,1)S(1)}, bf16[256,768]{1,0:T(8,128)(2,1)S(1)}, u32[]{:S(2)}, u32[]{:S(2)}) %collective-permute-start.5) | collective-permute-done | bytes 393248 | tf_op jit(solution)/shard_map/ppermute | solution.py:322
  60.3 1.7 pre_grads.1
  62.1 39.8 %all_to_all.5.refs_0_ = bf16[4,576,256]{2,1,0:T(8,128)(2,1)} all-to-all(bf16[4,576,256]{2,1,0:T(8,128)(2,1)S(1)} %get-tuple-element.35), channel_id=1, replica_groups=mesh['groups'=2,'ep'=4,'sub'=4] {'ep'}, dimensions={0} | all-to-all | bytes 2359296 | tf_op jit(solution)/shard_map/all_to_all | solution.py:426
  101.9 1.6 collective-permute-start.13
  103.5 26.7 %collective-permute-done.13.refs_2_ = bf16[4,576,256]{2,1,0:T(8,128)(2,1)} collective-permute-done((bf16[4,576,256]{2,1,0:T(8,128)(2,1)}, bf16[4,576,256]{2,1,0:T(8,128)(2,1)}, u32[]{:S(2)}, u32[]{:S(2)}) %collective-permute-start.13) | collective-permute-done | bytes 1179680 | tf_op jit(solution)/shard_map/ppermute | solution.py:322
  130.2 1.5 collective-permute-start.7
  131.7 0.2 collective-permute-start.6
  131.9 10.0 %collective-permute-done.7.refs_2_ = bf16[256,768]{1,0:T(8,128)(2,1)S(1)} collective-permute-done((bf16[256,768]{1,0:T(8,128)(2,1)}, bf16[256,768]{1,0:T(8,128)(2,1)S(1)}, u32[]{:S(2)}, u32[]{:S(2)}) %collective-permute-start.7) | collective-permute-done | bytes 393248 | tf_op jit(solution)/shard_map/ppermute | solution.py:322
  141.9 1.7 collective-permute-done.8.refs_3_
  143.6 4.6 %copy-done = bf16[8,1536,512]{2,1,0:T(8,128)(2,1)S(1)} copy-done((bf16[8,1536,512]{2,1,0:T(8,128)(2,1)S(1)}, bf16[8,1536,512]{2,1,0:T(8,128)(2,1)}, u32[]{:S(2)}) %copy-start) | copy-done | bytes 12582936
  148.2 1.0 copy-done.9
  149.2 5.7 %row_grads.1 = bf16[4,144,512]{2,1,0:T(8,128)(2,1)S(1)} custom-call(s32[2]{0:T(128)S(1)} %pad_add_fusion.ids_ref, bf16[256,768]{1,0:T(8,128)(2,1)S(1)} %copy-done.9, bf16[256,768]{1,0:T(8,128)(2,1)S(1)} %collective-permute-done.6.refs_1_, bf16[256,768]{1,0:T(8,128)(2,1)S(1)} %collective-permute-done.7.refs_2_, ...), custom_call_target="tpu_custom_call" | custom-call | tf_op jit(solution)/shard_map/row_grads/pallas_call | solution.py:433
  155.0 1.1 collective-permute-start.11
  156.1 0.3 collective-permute-start.10
  156.4 3.1 %collective-permute-start.9 = (bf16[144,512]{1,0:T(8,128)(2,1)S(1)}, bf16[144,512]{1,0:T(8,128)(2,1)S(1)}, u32[]{:S(2)}, u32[]{:S(2)}) collective-permute-start(bf16[144,512]{1,0:T(8,128)(2,1)S(1)} %get-tuple-element.46), channel_id=1, source_target_pairs={{0,4},{4,0},{8,12},{12,8},{1,5},{5,1},{9,13},{13,9},{2,6},{6,2},{1... | collective-permute-start | bytes 442376 | tf_op jit(solution)/shard_map/ppermute | solution.py:322
  159.4 4.2 %collective-permute-done.11.refs_3_ = bf16[144,512]{1,0:T(8,128)(2,1)S(1)} collective-permute-done((bf16[144,512]{1,0:T(8,128)(2,1)S(1)}, bf16[144,512]{1,0:T(8,128)(2,1)S(1)}, u32[]{:S(2)}, u32[]{:S(2)}) %collective-permute-start.11) | collective-permute-done | bytes 147488 | tf_op jit(solution)/shard_map/ppermute | solution.py:322
  163.7 6.1 %collective-permute-done.10.refs_2_ = bf16[144,512]{1,0:T(8,128)(2,1)S(1)} collective-permute-done((bf16[144,512]{1,0:T(8,128)(2,1)S(1)}, bf16[144,512]{1,0:T(8,128)(2,1)S(1)}, u32[]{:S(2)}, u32[]{:S(2)}) %collective-permute-start.10) | collective-permute-done | bytes 147488 | tf_op jit(solution)/shard_map/ppermute | solution.py:322
  169.8 1.4 token_grads.1
  171.2 1.6 copy-done.7
  172.8 13.8 %weight_grads.2 = (bf16[16,384,512]{2,1,0:T(8,128)(2,1)}, bf16[16,192,512]{2,1,0:T(8,128)(2,1)}) custom-call(s32[2]{0:T(128)S(1)} %pad_add_fusion.ids_ref, s32[4,16]{1,0:T(4,128)S(1)} %bitcast.25, bf16[4,576,256]{2,1,0:T(8,128)(2,1)S(1)} %copy-done.2, bf16[4,576,256]{2,1,0:T(8,128)(2,1)} %collective-permute-done.12.refs_1_, ...), custom_call_target="tpu_custom_call" | custom-call | tf_op jit(solution)/shard_map/weight_grads/pallas_call | solution.py:480
  186.6 1.6 copy-done.4
  188.2 10.5 %weight_grads.3 = bf16[16,384,512]{2,1,0:T(8,128)(2,1)} custom-call(s32[2]{0:T(128)S(1)} %pad_add_fusion.ids_ref, s32[4,16]{1,0:T(4,128)S(1)} %bitcast.26, bf16[4,576,256]{2,1,0:T(8,128)(2,1)S(1)} %copy-done.2, bf16[4,576,256]{2,1,0:T(8,128)(2,1)} %collective-permute-done.12.refs_1_, ...), custom_call_target="tpu_custom_call", output_to_operand_aliasing={{}: (9, {})} | custom-call | tf_op jit(solution)/shard_map/weight_grads/pallas_call | solution.py:480
  (47 shorter events, 0.2 us)
Async XLA Ops:
  7.2 164.0 %all-gather.7.cloned.1.call-start = ((), (), s32[]{:S(2)}) async-start(), calls=%async_computation.2 | async-start | bytes 2621440 | tf_op jit(solution)/shard_map/all_gather | solution.py:371
  7.9 0.9 copy-start.16
  8.8 0.7 copy-start.17
  9.4 0.7 copy-start.19
  10.1 0.7 copy-start.21
  10.8 0.7 copy-start.23
  11.8 9.8 %collective-permute-start.2 = (bf16[144,512]{1,0:T(8,128)(2,1)S(1)}, bf16[144,512]{1,0:T(8,128)(2,1)S(1)}, u32[]{:S(2)}, u32[]{:S(2)}) collective-permute-start(bf16[144,512]{1,0:T(8,128)(2,1)S(1)} %route.1.refs_0_), channel_id=1, source_target_pairs={{0,12},{4,8},{8,4},{12,0},{1,13},{5,9},{9,5},{13,1},{2,14},{6,10},... | collective-permute-start | bytes 442376 | tf_op jit(solution)/shard_map/ppermute | solution.py:322
  16.8 12.5 %collective-permute-start.1 = (bf16[144,512]{1,0:T(8,128)(2,1)S(1)}, bf16[144,512]{1,0:T(8,128)(2,1)S(1)}, u32[]{:S(2)}, u32[]{:S(2)}) collective-permute-start(bf16[144,512]{1,0:T(8,128)(2,1)S(1)} %route.1.refs_0_), channel_id=1, source_target_pairs={{0,8},{4,12},{8,0},{12,4},{1,9},{5,13},{9,1},{13,5},{2,10},{6,14},... | collective-permute-start | bytes 442376 | tf_op jit(solution)/shard_map/ppermute | solution.py:322
  16.8 13.1 %collective-permute-start = (bf16[144,512]{1,0:T(8,128)(2,1)S(1)}, bf16[144,512]{1,0:T(8,128)(2,1)S(1)}, u32[]{:S(2)}, u32[]{:S(2)}) collective-permute-start(bf16[144,512]{1,0:T(8,128)(2,1)S(1)} %route.1.refs_0_), channel_id=1, source_target_pairs={{0,4},{4,0},{8,12},{12,8},{1,5},{5,1},{9,13},{13,9},{2,6},{6,2},{1... | collective-permute-start | bytes 442376 | tf_op jit(solution)/shard_map/ppermute | solution.py:322
  21.6 0.7 copy-start.10
  29.3 0.7 copy-start.12
  30.0 0.7 copy-start.14
  30.7 155.9 %all-gather.5.cloned.1.call-start = ((), (), s32[]{:S(2)}) async-start(), calls=%async_computation.1 | async-start | bytes 2621440 | tf_op jit(solution)/shard_map/all_gather | solution.py:428
  30.8 2.8 %copy-start.3 = (bf16[8,768,512]{2,1,0:T(8,128)(2,1)S(1)}, bf16[8,768,512]{2,1,0:T(8,128)(2,1)}, u32[]{:S(2)}) copy-start(bf16[8,768,512]{2,1,0:T(8,128)(2,1)} %refs_4_.1) | copy-start | bytes 18874372
  33.6 0.9 copy-start.11
  34.5 0.9 copy-start.13
  35.4 0.9 copy-start.15
  36.3 24.0 %copy-start.1 = (bf16[8,128,1536]{2,1,0:T(8,128)(2,1)S(1)}, bf16[8,128,1536]{2,1,0:T(8,128)(2,1)}, u32[]{:S(2)}) copy-start(bf16[8,128,1536]{2,1,0:T(8,128)(2,1)} %param.17) | copy-start | bytes 9437188
  40.8 21.3 %copy-start.5 = (bf16[4,128,512]{2,1,0:T(8,128)(2,1)}, bf16[4,128,512]{2,1,0:T(8,128)(2,1)S(1)}, u32[]{:S(2)}) copy-start(bf16[4,128,512]{2,1,0:T(8,128)(2,1)S(1)} %get-tuple-element.38.refs_5_) | copy-start | bytes 1572868
  40.8 1.9 collective-permute-start.3
  40.8 12.0 %collective-permute-start.4 = (bf16[256,768]{1,0:T(8,128)(2,1)S(1)}, bf16[256,768]{1,0:T(8,128)(2,1)S(1)}, u32[]{:S(2)}, u32[]{:S(2)}) collective-permute-start(bf16[256,768]{1,0:T(8,128)(2,1)S(1)} %get-tuple-element.29), channel_id=1, source_target_pairs={{0,2},{1,3},{2,0},{3,1},{4,6},{5,7},{6,4},{7,5},{8,10},{9,11},{10,... | collective-permute-start | bytes 1179656 | tf_op jit(solution)/shard_map/ppermute | solution.py:322
  42.4 17.9 %collective-permute-start.5 = (bf16[256,768]{1,0:T(8,128)(2,1)S(1)}, bf16[256,768]{1,0:T(8,128)(2,1)S(1)}, u32[]{:S(2)}, u32[]{:S(2)}) collective-permute-start(bf16[256,768]{1,0:T(8,128)(2,1)S(1)} %get-tuple-element.30), channel_id=1, source_target_pairs={{0,3},{1,2},{2,1},{3,0},{4,7},{5,6},{6,5},{7,4},{8,11},{9,10},{10,... | collective-permute-start | bytes 1179656 | tf_op jit(solution)/shard_map/ppermute | solution.py:322
  62.1 39.8 %copy-start.8 = (bf16[256,768]{1,0:T(8,128)(2,1)}, bf16[256,768]{1,0:T(8,128)(2,1)S(1)}, u32[]{:S(2)}) copy-start(bf16[256,768]{1,0:T(8,128)(2,1)S(1)} %get-tuple-element.32.refs_0_) | copy-start | bytes 1179652
  101.9 28.3 %collective-permute-start.13 = (bf16[4,576,256]{2,1,0:T(8,128)(2,1)}, bf16[4,576,256]{2,1,0:T(8,128)(2,1)}, u32[]{:S(2)}, u32[]{:S(2)}) collective-permute-start(bf16[4,576,256]{2,1,0:T(8,128)(2,1)} %all_to_all.5.refs_0_), channel_id=1, source_target_pairs={{0,2},{1,3},{2,0},{3,1},{4,6},{5,7},{6,4},{7,5},{8,10},{9,11},{10,... | collective-permute-start | bytes 3538952 | tf_op jit(solution)/shard_map/ppermute | solution.py:322
  103.5 67.7 %collective-permute-start.12 = (bf16[4,576,256]{2,1,0:T(8,128)(2,1)}, bf16[4,576,256]{2,1,0:T(8,128)(2,1)}, u32[]{:S(2)}, u32[]{:S(2)}) collective-permute-start(bf16[4,576,256]{2,1,0:T(8,128)(2,1)} %all_to_all.5.refs_0_), channel_id=1, source_target_pairs={{0,1},{1,0},{2,3},{3,2},{4,5},{5,4},{6,7},{7,6},{8,9},{9,8},{10,11... | collective-permute-start | bytes 3538952 | tf_op jit(solution)/shard_map/ppermute | solution.py:322
  130.2 41.0 %collective-permute-start.14 = (bf16[4,576,256]{2,1,0:T(8,128)(2,1)}, bf16[4,576,256]{2,1,0:T(8,128)(2,1)}, u32[]{:S(2)}, u32[]{:S(2)}) collective-permute-start(bf16[4,576,256]{2,1,0:T(8,128)(2,1)} %collective-permute-done.13.refs_2_), channel_id=1, source_target_pairs={{0,1},{1,0},{2,3},{3,2},{4,5},{5,4},{6,7},{7,6},{8,9},{9,8},{10,11... | collective-permute-start | bytes 3538952 | tf_op jit(solution)/shard_map/ppermute | solution.py:322
  130.2 11.7 %collective-permute-start.7 = (bf16[256,768]{1,0:T(8,128)(2,1)}, bf16[256,768]{1,0:T(8,128)(2,1)S(1)}, u32[]{:S(2)}, u32[]{:S(2)}) collective-permute-start(bf16[256,768]{1,0:T(8,128)(2,1)} %copy-done.8), channel_id=1, source_target_pairs={{0,2},{1,3},{2,0},{3,1},{4,6},{5,7},{6,4},{7,5},{8,10},{9,11},{10,... | collective-permute-start | bytes 1179656 | tf_op jit(solution)/shard_map/ppermute | solution.py:322
  131.7 10.2 %collective-permute-start.6 = (bf16[256,768]{1,0:T(8,128)(2,1)}, bf16[256,768]{1,0:T(8,128)(2,1)S(1)}, u32[]{:S(2)}, u32[]{:S(2)}) collective-permute-start(bf16[256,768]{1,0:T(8,128)(2,1)} %copy-done.8), channel_id=1, source_target_pairs={{0,1},{1,0},{2,3},{3,2},{4,5},{5,4},{6,7},{7,6},{8,9},{9,8},{10,11... | collective-permute-start | bytes 1179656 | tf_op jit(solution)/shard_map/ppermute | solution.py:322
  141.9 1.7 collective-permute-start.8
  143.6 4.6 %copy-start = (bf16[8,1536,512]{2,1,0:T(8,128)(2,1)S(1)}, bf16[8,1536,512]{2,1,0:T(8,128)(2,1)}, u32[]{:S(2)}) copy-start(bf16[8,1536,512]{2,1,0:T(8,128)(2,1)} %refs_5_.1) | copy-start | bytes 37748740
  148.2 1.0 copy-start.9
  149.2 20.6 %copy-start.18 = (s32[16,4]{0,1:T(4,128)S(1)}, s32[16,4]{0,1:T(4,128)}, u32[]{:S(2)}) copy-start(s32[16,4]{0,1:T(4,128)} %param.14) | copy-start | bytes 772
  149.2 20.6 %copy-start.20 = (s32[128,8]{0,1:T(8,128)S(1)}, s32[128,8]{0,1:T(8,128)}, u32[]{:S(2)}) copy-start(s32[128,8]{0,1:T(8,128)} %param.12) | copy-start | bytes 12292
  149.2 20.6 %copy-start.22 = (s32[128,8]{0,1:T(8,128)S(1)}, s32[128,8]{0,1:T(8,128)}, u32[]{:S(2)}) copy-start(s32[128,8]{0,1:T(8,128)} %param.13) | copy-start | bytes 12292
  154.9 16.3 %copy-start.2 = (bf16[4,576,256]{2,1,0:T(8,128)(2,1)S(1)}, bf16[4,576,256]{2,1,0:T(8,128)(2,1)}, u32[]{:S(2)}) copy-start(bf16[4,576,256]{2,1,0:T(8,128)(2,1)} %all_to_all.5.refs_0_) | copy-start | bytes 3538948
  154.9 16.3 %copy-start.6 = (bf16[4,128,512]{2,1,0:T(8,128)(2,1)S(1)}, bf16[4,128,512]{2,1,0:T(8,128)(2,1)}, u32[]{:S(2)}) copy-start(bf16[4,128,512]{2,1,0:T(8,128)(2,1)} %copy-done.5) | copy-start | bytes 1572868
  155.0 8.7 %collective-permute-start.11 = (bf16[144,512]{1,0:T(8,128)(2,1)S(1)}, bf16[144,512]{1,0:T(8,128)(2,1)S(1)}, u32[]{:S(2)}, u32[]{:S(2)}) collective-permute-start(bf16[144,512]{1,0:T(8,128)(2,1)S(1)} %get-tuple-element.44), channel_id=1, source_target_pairs={{0,12},{4,8},{8,4},{12,0},{1,13},{5,9},{9,5},{13,1},{2,14},{6,10},... | collective-permute-start | bytes 442376 | tf_op jit(solution)/shard_map/ppermute | solution.py:322
  156.1 13.7 %collective-permute-start.10 = (bf16[144,512]{1,0:T(8,128)(2,1)S(1)}, bf16[144,512]{1,0:T(8,128)(2,1)S(1)}, u32[]{:S(2)}, u32[]{:S(2)}) collective-permute-start(bf16[144,512]{1,0:T(8,128)(2,1)S(1)} %get-tuple-element.45), channel_id=1, source_target_pairs={{0,8},{4,12},{8,0},{12,4},{1,9},{5,13},{9,1},{13,5},{2,10},{6,14},... | collective-permute-start | bytes 442376 | tf_op jit(solution)/shard_map/ppermute | solution.py:322
  156.4 13.4 %collective-permute-start.9 = (bf16[144,512]{1,0:T(8,128)(2,1)S(1)}, bf16[144,512]{1,0:T(8,128)(2,1)S(1)}, u32[]{:S(2)}, u32[]{:S(2)}) collective-permute-start(bf16[144,512]{1,0:T(8,128)(2,1)S(1)} %get-tuple-element.46), channel_id=1, source_target_pairs={{0,4},{4,0},{8,12},{12,8},{1,5},{5,1},{9,13},{13,9},{2,6},{6,2},{1... | collective-permute-start | bytes 442376 | tf_op jit(solution)/shard_map/ppermute | solution.py:322
  171.2 1.6 copy-start.7
  186.6 1.6 copy-start.4
Sparse Core Ops, SparseCore 0:
  30.8 56.1 all-gather.6
  102.0 44.6 all-gather.4

commit v3 on v2

--- a/solution.py
+++ b/solution.py
@@ -11,6 +11,7 @@
 BF = jnp.bfloat16
 F32 = jnp.float32
 CUTS = 2
+GROUPS = 2
 
 
 def nt(a, b):
@@ -37,6 +38,12 @@
 def params(mib):
     return pltpu.CompilerParams(
         vmem_limit_bytes=mib * 1024 * 1024, dimension_semantics=("arbitrary",)
+    )
+
+
+def cost(micros):
+    return pl.CostEstimate(
+        flops=int(micros * 1.1e9), bytes_accessed=int(micros * 3.6e6), transcendentals=0
     )
 
 
@@ -189,10 +196,13 @@
 
 def pre_kernel(z, ids_ref, *refs):
     parts = refs[: z.sub]
-    pair_ref, codes_ref, out_ref, grad_ref = refs[z.sub :]
+    pair_ref, codes_ref = refs[z.sub : z.sub + 2]
+    outs = refs[z.sub + 2 : z.sub + 2 + z.ep]
+    grad_ref, sides = refs[z.sub + 2 + z.ep :]
+    me = ids_ref[0]
     block = ids_ref[1] * z.part_blocks + pl.program_id(0)
     slot, first = block_place(z, block)
-    scale = block_scale(z, codes_ref, ids_ref[0] * z.local + slot, first)
+    scale = block_scale(z, codes_ref, me * z.local + slot, first)
     grad = parts[0][...].astype(F32)
     for k in range(1, z.sub):
         grad = grad + parts[k][...].astype(F32)
@@ -201,8 +211,18 @@
     hidden = hidden.astype(BF).T
     pre = jnp.concatenate([grad_gate.T, grad_up.T], axis=0)
     for q in range(z.ep):
-        out_ref[q, : z.in_cols, :] = pre[q * z.in_cols : (q + 1) * z.in_cols, :]
-        out_ref[q, z.in_cols :, :] = hidden[q * z.down_cols : (q + 1) * z.down_cols, :]
+        sides[q, : z.in_cols, :] = pre[q * z.in_cols : (q + 1) * z.in_cols, :]
+        sides[q, z.in_cols :, :] = hidden[q * z.down_cols : (q + 1) * z.down_cols, :]
+    for k in range(z.ep):
+        outs[k][...] = sides[me ^ k]
+
+
+def stack_kernel(count, extra, *refs):
+    ins, outs = refs[: count + extra], refs[count + extra :]
+    for i in range(count):
+        outs[0][i] = ins[i][...]
+    for i, out in enumerate(outs[1:]):
+        out[...] = ins[count + i][...]
 
 
 def row_kernel(z, ids_ref, *refs):
@@ -268,25 +288,52 @@
     route_ref[...] = jnp.concatenate(totals, axis=0).astype(BF)
 
 
-def total_kernel(z, down, ids_ref, table_ref, *refs):
-    sides = refs[: z.sub]
-    inputs_ref, grads_ref, codes_ref = refs[z.sub : z.sub + 3]
+def total_kernel(z, down, groups, ids_ref, table_ref, *refs):
+    sides, refs = refs[: groups * z.sub], refs[groups * z.sub :]
+    own_ref, rights, lefts = refs[0], refs[1 : z.ep], refs[z.ep : 2 * z.ep - 1]
+    grads_ref, codes_ref = refs[2 * z.ep - 1 : 2 * z.ep + 1]
+    refs = refs[2 * z.ep + 1 :]
     if down:
-        in_ref, down_ref, held, sems = refs[z.sub + 3 :]
+        in_ref, down_ref, held, inputs_ref, sems, own_sem, right_sems, left_sems = refs
     else:
-        in_ref, held, sems = refs[z.sub + 4 :]
-    mine = ids_ref[1]
+        in_ref, held, inputs_ref, sems, own_sem, right_sems, left_sems = refs[1:]
+    me, mine = ids_ref[0], ids_ref[1]
     expert = pl.program_id(0)
+    size = z.ep // groups
+
+    def moves(act):
+        for g in range(groups):
+            for k in range(z.sub):
+                act(
+                    pltpu.make_async_copy(
+                        sides[g * z.sub + k],
+                        held.at[k, pl.ds(g * size, size)],
+                        sems.at[g * z.sub + k],
+                    )
+                )
+        act(pltpu.make_async_copy(own_ref, inputs_ref.at[me], own_sem))
+        for d in range(1, z.ep):
+
+            @pl.when(me >= d)
+            def _():
+                act(
+                    pltpu.make_async_copy(
+                        rights[d - 1], inputs_ref.at[me - d], right_sems.at[d - 1]
+                    )
+                )
+
+            @pl.when(me + d < z.ep)
+            def _():
+                act(
+                    pltpu.make_async_copy(
+                        lefts[d - 1], inputs_ref.at[me + d], left_sems.at[d - 1]
+                    )
+                )
 
     @pl.when(expert == 0)
     def _():
-        copies = [
-            pltpu.make_async_copy(sides[k], held.at[k], sems.at[k]) for k in range(z.sub)
-        ]
-        for copy in copies:
-            copy.start()
-        for copy in copies:
-            copy.wait()
+        moves(lambda copy: copy.start())
+        moves(lambda copy: copy.wait())
 
     slot_ids = [table_ref[r, expert] for r in range(z.reps)]
     count = 1
@@ -294,20 +341,20 @@
         count = count + (slot_ids[r] != slot_ids[0]).astype(jnp.int32)
 
     def add(used):
-        lefts, rights, rows = [], [], []
+        left_parts, right_parts, rows = [], [], []
         for slot_id in used:
             source = slot_id // z.local
             for b in range(z.slot_blocks):
                 block = (slot_id % z.local) * z.slot_blocks + b
                 part = (block // z.part_blocks) ^ mine
                 spot = pl.multiple_of((block % z.part_blocks) * z.block, z.block)
-                lefts.append(held[part, source, :, pl.ds(spot, z.block)])
+                left_parts.append(held[part, source ^ me, :, pl.ds(spot, z.block)])
                 start = pl.multiple_of(block * z.block, z.block)
-                rights.append(inputs_ref[source, pl.ds(start, z.block), :])
+                right_parts.append(inputs_ref[source, pl.ds(start, z.block), :])
                 if down:
                     rows.append(scaled_rows(z, codes_ref, grads_ref, slot_id, b * z.sources))
-        left = jnp.concatenate(lefts, axis=1)
-        in_ref[0] = nn(left[: z.in_cols, :], jnp.concatenate(rights, axis=0)).astype(BF)
+        left = jnp.concatenate(left_parts, axis=1)
+        in_ref[0] = nn(left[: z.in_cols, :], jnp.concatenate(right_parts, axis=0)).astype(BF)
         if down:
             down_ref[0] = nn(left[z.in_cols :, :], jnp.concatenate(rows, axis=0)).astype(BF)
 
@@ -330,6 +377,17 @@
             have[k | bit] = swap(have[k], axis, size, bit)
         bit //= 2
     return [have[k] for k in range(size)]
+
+
+def chain_gather(x, axis, size):
+    rights, lefts = [], []
+    go, back = x, x
+    for d in range(1, size):
+        go = lax.ppermute(go, axis, [(i, i + 1) for i in range(d - 1, size - 1)])
+        back = lax.ppermute(back, axis, [(i, i - 1) for i in range(size - d, 0, -1)])
+        rights.append(go)
+        lefts.append(back)
+    return [x] + rights + lefts
 
 
 def body(
@@ -354,7 +412,7 @@
     code_shape = (n, 2 * z.slots, z.tokens)
     chunk = z.width // CUTS
     inputs = saved_input.reshape(z.all_rows, z.width)
-    inputs = [inputs[:, c * chunk : (c + 1) * chunk] for c in range(CUTS)]
+    gathered = [chain_gather(inputs[:, :chunk], "ep", n)]
 
     buf = pl.pallas_call(
         functools.partial(route_kernel, z),
@@ -363,12 +421,11 @@
         + [whole(a.shape) for a in (grad_out, route_weight, routes, replica, table)],
         out_specs=whole(grad_shape),
         grid=(1,),
-        compiler_params=params(4),
+        compiler_params=params(60),
+        cost_estimate=cost(1),
         name="route",
     )(token_count, grad_out, route_weight, routes, replica, table)
     bufs = [buf] + [swap(buf, "ep", n, k) for k in range(1, n)]
-    bufs, inputs[0] = lax.optimization_barrier((bufs, inputs[0]))
-    gathered = [lax.all_gather(inputs[0], "ep")]
 
     def row_block(i, ids_ref):
         place = i // z.part_blocks
@@ -393,13 +450,14 @@
             jax.ShapeDtypeStruct((n, z.tokens, z.width), BF),
             jax.ShapeDtypeStruct(code_shape, F32),
         ],
-        compiler_params=params(16),
+        compiler_params=params(56),
+        cost_estimate=cost(6),
         name="hidden_partials",
     )(ids, *bufs, weight_down)
     parts, (grads_all, codes) = outs[:m], outs[m:]
     parts = [parts[0]] + [swap(parts[k], "sub", m, k) for k in range(1, m)]
 
-    pre, grad_part = pl.pallas_call(
+    outs = pl.pallas_call(
         functools.partial(pre_kernel, z),
         grid_spec=pltpu.PrefetchScalarGridSpec(
             num_scalar_prefetch=1,
@@ -410,23 +468,43 @@
                 whole(code_shape),
             ],
             out_specs=[
-                pl.BlockSpec((n, z.cols, z.block), lambda i, r: (0, 0, i)),
-                pl.BlockSpec((z.block, z.hidden), lambda i, r: (i, 0)),
-            ],
+                pl.BlockSpec((z.cols, z.block), lambda i, r: (0, i))
+            ]
+            * n
+            + [pl.BlockSpec((z.block, z.hidden), lambda i, r: (i, 0))],
+            scratch_shapes=[pltpu.VMEM((n, z.cols, z.block), BF)],
         ),
-        out_shape=[
-            jax.ShapeDtypeStruct((n, z.cols, z.part), BF),
-            jax.ShapeDtypeStruct((z.part, z.hidden), BF),
-        ],
+        out_shape=[jax.ShapeDtypeStruct((z.cols, z.part), BF)] * n
+        + [jax.ShapeDtypeStruct((z.part, z.hidden), BF)],
         compiler_params=params(16),
+        cost_estimate=cost(2),
         name="pre_grads",
     )(ids, *parts, pair_rows, codes)
 
+    pieces, grad_part = outs[:n], outs[n]
+    pieces = [pieces[0]] + [swap(pieces[k], "ep", n, k) for k in range(1, n)]
     grad_parts = spread_over(grad_part, "sub", m)
-    columns = lax.all_to_all(pre, "ep", split_axis=0, concat_axis=0, tiled=True)
-    columns, *inputs[1:] = lax.optimization_barrier((columns, *inputs[1:]))
-    gathered += [lax.all_gather(a, "ep") for a in inputs[1:]]
-    sides = spread_over(columns, "sub", m)
+    size = n // GROUPS
+    sides = []
+    for g in range(GROUPS):
+        extra = CUTS - 1 if g == GROUPS - 1 else 0
+        outs = pl.pallas_call(
+            functools.partial(stack_kernel, size, extra),
+            in_specs=[whole((z.cols, z.part))] * size
+            + [
+                pl.BlockSpec((z.all_rows, chunk), lambda i, c=c: (0, c + 1))
+                for c in range(extra)
+            ],
+            out_specs=[whole((size, z.cols, z.part))] + [whole((z.all_rows, chunk))] * extra,
+            out_shape=[jax.ShapeDtypeStruct((size, z.cols, z.part), BF)]
+            + [jax.ShapeDtypeStruct((z.all_rows, chunk), BF)] * extra,
+            grid=(1,),
+            compiler_params=params(16),
+            cost_estimate=cost(1),
+            name="stack_columns",
+        )(*pieces[g * size : (g + 1) * size], *[inputs] * extra)
+        sides += spread_over(outs[0], "sub", m)
+        gathered += [chain_gather(a, "ep", n) for a in outs[1:]]
 
     mark_rows = -(-z.local // 16) * 16
     back_shape = (n, z.tokens + mark_rows, z.width)
@@ -449,7 +527,8 @@
             ],
         ),
         out_shape=jax.ShapeDtypeStruct(back_shape, BF),
-        compiler_params=params(24),
+        compiler_params=params(54),
+        cost_estimate=cost(7),
         name="row_grads",
     )(ids, *grad_parts, pair_rows, weight_in, codes)
     got = [back[0]] + [swap(back[k], "ep", n, k) for k in range(1, n)]
@@ -466,7 +545,8 @@
         out_specs=[whole((z.tokens, z.width)), whole((z.top, z.tokens))],
         grid=(1,),
         scratch_shapes=[pltpu.VMEM((n, mark_rows, z.tokens), F32)],
-        compiler_params=params(8),
+        compiler_params=params(60),
+        cost_estimate=cost(2),
         name="token_grads",
     )(ids, token_count, *got, routes, replica, table)
 
@@ -478,32 +558,33 @@
         in_spec = pl.BlockSpec((1, z.in_cols, chunk), lambda e, r, t, c=c: (e, 0, c))
         down_spec = pl.BlockSpec((1, z.down_cols, z.width), lambda e, r, t: (e, 0, 0))
         out = pl.pallas_call(
-            functools.partial(total_kernel, z, first),
+            functools.partial(total_kernel, z, first, GROUPS),
             grid_spec=pltpu.PrefetchScalarGridSpec(
                 num_scalar_prefetch=2,
                 grid=(z.experts,),
-                in_specs=[pl.BlockSpec(memory_space=pl.ANY)] * m
-                + [
-                    whole((n, z.all_rows, chunk)),
-                    whole((n, z.tokens, z.width)),
-                    whole(code_shape),
-                ]
+                in_specs=[pl.BlockSpec(memory_space=pl.ANY)] * (GROUPS * m + 2 * n - 1)
+                + [whole((n, z.tokens, z.width)), whole(code_shape)]
                 + ([] if first else [pl.BlockSpec(memory_space=pl.ANY)]),
                 out_specs=[in_spec, down_spec] if first else [in_spec],
                 scratch_shapes=[
                     pltpu.VMEM((m, n, z.cols, z.part), BF),
-                    pltpu.SemaphoreType.DMA((m,)),
+                    pltpu.VMEM((n, z.all_rows, chunk), BF),
+                    pltpu.SemaphoreType.DMA((GROUPS * m,)),
+                    pltpu.SemaphoreType.DMA,
+                    pltpu.SemaphoreType.DMA((n - 1,)),
+                    pltpu.SemaphoreType.DMA((n - 1,)),
                 ],
             ),
             out_shape=[in_shape, down_shape] if first else [in_shape],
-            input_output_aliases={} if first else {2 + m + 3: 0},
-            compiler_params=params(24),
+            input_output_aliases={} if first else {2 + GROUPS * m + 2 * n + 1: 0},
+            compiler_params=params(32),
+            cost_estimate=cost(12 if first else 8),
             name="weight_grads",
         )(
             ids,
             table,
             *sides,
-            gathered[c],
+            *gathered[c],
             grads_all,
             codes,
             *([] if first else [grad_in]),

time: 206 us -> 198 us (0.961)
  the two profiles are of different devices: /device:TPU:0 before, /device:TPU:24 now
where the time goes in v3:
time: 198 us; the launch traced here: 197 us
  waiting for transfers between devices  90.4 us (46%)
  Pallas kernels  51.9 us (26%)
  starting transfers between devices  40.5 us (20%)
  local copies, waits for them, and re-layouts  12 us (6%)
    ppermute x21, waiting for transfers between devices, swap(): return lax.ppermute(x, axis, [(i, i ^ bit) for i in range(size)])  53.7 us
    ppermute x6, waiting for transfers between devices, chain_gather(): go = lax.ppermute(go, axis, [(i, i + 1) for i in range(d - 1, size - 1)])  36.7 us
    pallas_call x2, Pallas kernels, body(): pl.pallas_call(functools.partial(total_kernel, z, first, GROUPS), grid_sp...  24.5 us
    ppermute x21, starting transfers between devices, swap(): return lax.ppermute(x, axis, [(i, i ^ bit) for i in range(size)])  19.1 us
    ppermute x6, starting transfers between devices, chain_gather(): lax.ppermute(back, axis, [(i, i - 1) for i in range(size - d, 0, -1)])  13.7 us
    pallas_call x1, Pallas kernels, body(): pl.pallas_call(functools.partial(row_kernel, z), grid_spec=pltpu.Prefetch...  11.9 us
    unnamed x58, local copies, waits for them, and re-layouts  10.2 us
    pallas_call x1, Pallas kernels, body(): pl.pallas_call(functools.partial(down_kernel, z), grid_spec=pltpu.Prefetc...  9.57 us
  transfers between devices with their start and end apart: 33, of which 12 were waited for; matrix products, arithmetic and copies ran while one was open for 1% of the time, Pallas kernels for 15%

profile of v3, /device:TPU:24, one launch (start us, length us, event | category | flops | bytes accessed | tf_op | source)
XLA Modules:
  0.0 197.0 jit_solution(13141881181518021715)
XLA Ops:
  1.3 1.9 route.1.refs_0_
  3.2 1.9 collective-permute-start.1
  5.1 2.5 %collective-permute-start = (bf16[144,512]{1,0:T(8,128)(2,1)}, bf16[144,512]{1,0:T(8,128)(2,1)S(1)}, u32[]{:S(2)}, u32[]{:S(2)}) collective-permute-start(bf16[144,512]{1,0:T(8,128)(2,1)} %route.1.refs_0_), channel_id=1, source_target_pairs={{0,4},{4,0},{8,12},{12,8},{1,5},{5,1},{9,13},{13,9},{2,6},{6,2},{1... | collective-permute-start | bytes 442376 | tf_op jit(solution)/shard_map/ppermute | solution.py:369
  8.1 3.9 %collective-permute-done.2.refs_3_ = bf16[144,512]{1,0:T(8,128)(2,1)S(1)} collective-permute-done((bf16[144,512]{1,0:T(8,128)(2,1)}, bf16[144,512]{1,0:T(8,128)(2,1)S(1)}, u32[]{:S(2)}, u32[]{:S(2)}) %collective-permute-start.2) | collective-permute-done | bytes 147488 | tf_op jit(solution)/shard_map/ppermute | solution.py:369
  12.0 6.4 %collective-permute-done.1.refs_2_ = bf16[144,512]{1,0:T(8,128)(2,1)S(1)} collective-permute-done((bf16[144,512]{1,0:T(8,128)(2,1)}, bf16[144,512]{1,0:T(8,128)(2,1)S(1)}, u32[]{:S(2)}, u32[]{:S(2)}) %collective-permute-start.1) | collective-permute-done | bytes 147488 | tf_op jit(solution)/shard_map/ppermute | solution.py:369
  19.7 9.6 %hidden_partials.1 = (bf16[256,768]{1,0:T(8,128)(2,1)}, bf16[256,768]{1,0:T(8,128)(2,1)}, bf16[256,768]{1,0:T(8,128)(2,1)}, bf16[256,768]{1,0:T(8,128)(2,1)}, bf...) custom-call(s32[2]{0:T(128)} %pad_add_fusion.ids_ref, bf16[144,512]{1,0:T(8,128)(2,1)} %route.1.refs_0_, ...), custom_call_target="tpu_custom_call" | custom-call | flops 6600000000 | bytes 21600000 | tf_op jit(solution)/shard_map/hidden_partials/pallas_call | solution.py:437
  29.2 1.6 collective-permute-start.4
  31.1 1.3 collective-permute-start.30
  32.5 1.3 collective-permute-start.27
  33.8 7.6 %collective-permute-done.4.refs_2_ = bf16[256,768]{1,0:T(8,128)(2,1)S(1)} collective-permute-done((bf16[256,768]{1,0:T(8,128)(2,1)}, bf16[256,768]{1,0:T(8,128)(2,1)S(1)}, u32[]{:S(2)}, u32[]{:S(2)}) %collective-permute-start.4) | collective-permute-done | bytes 393248 | tf_op jit(solution)/shard_map/ppermute | solution.py:369
  41.4 7.5 %collective-permute-done.5.refs_3_ = bf16[256,768]{1,0:T(8,128)(2,1)S(1)} collective-permute-done((bf16[256,768]{1,0:T(8,128)(2,1)}, bf16[256,768]{1,0:T(8,128)(2,1)S(1)}, u32[]{:S(2)}, u32[]{:S(2)}) %collective-permute-start.5) | collective-permute-done | bytes 393248 | tf_op jit(solution)/shard_map/ppermute | solution.py:369
  49.0 1.0 copy-done.16
  50.0 0.9 copy-done.17
  50.9 1.8 pre_grads.1
  52.8 1.4 collective-permute-start.17
  54.2 1.5 collective-permute-start.7
  55.7 2.1 %collective-permute-start.12 = (bf16[576,256]{1,0:T(8,128)(2,1)S(1)}, bf16[576,256]{1,0:T(8,128)(2,1)S(1)}, u32[]{:S(2)}, u32[]{:S(2)}) collective-permute-start(bf16[576,256]{1,0:T(8,128)(2,1)S(1)} %get-tuple-element.30), channel_id=1, source_target_pairs={{0,4},{4,0},{8,12},{12,8},{1,5},{5,1},{9,13},{13,9},{2,6},{6,2},{1... | collective-permute-start | bytes 884744 | tf_op jit(solution)/shard_map/ppermute | solution.py:369
  57.8 16.5 %collective-permute-done.16.refs_0_ = bf16[576,256]{1,0:T(8,128)(2,1)S(1)} collective-permute-done((bf16[576,256]{1,0:T(8,128)(2,1)S(1)}, bf16[576,256]{1,0:T(8,128)(2,1)S(1)}, u32[]{:S(2)}, u32[]{:S(2)}) %collective-permute-start.16) | collective-permute-done | bytes 294944 | tf_op jit(solution)/shard_map/ppermute | solution.py:369
  75.0 1.3 collective-permute-start.28
  76.9 8.9 %collective-permute-start.24 = (bf16[1024,256]{1,0:T(8,128)(2,1)S(1)}, bf16[1024,256]{1,0:T(8,128)(2,1)}, u32[]{:S(2)}, u32[]{:S(2)}) collective-permute-start(bf16[1024,256]{1,0:T(8,128)(2,1)S(1)} %get-tuple-element.34.refs_8_), channel_id=1, source_target_pairs={{12,8},{8,4},{4,0},{13,9},{9,5},{5,1},{14,10},{10,6},{6,2},{15,11}... | collective-permute-start | bytes 1572872 | tf_op jit(solution)/shard_map/ppermute | solution.py:387
  85.8 1.3 collective-permute-start.21
  87.3 1.6 collective-permute-start.19
  88.9 7.0 %collective-permute-done.28.refs_10_ = bf16[1024,256]{1,0:T(8,128)(2,1)} collective-permute-done((bf16[1024,256]{1,0:T(8,128)(2,1)S(1)}, bf16[1024,256]{1,0:T(8,128)(2,1)}, u32[]{:S(2)}, u32[]{:S(2)}) %collective-permute-start.28) | collective-permute-done | bytes 524320 | tf_op jit(solution)/shard_map/ppermute | solution.py:386
  95.8 1.6 collective-permute-start.14
  97.6 8.8 %collective-permute-done.21.refs_9_ = bf16[1024,256]{1,0:T(8,128)(2,1)} collective-permute-done((bf16[1024,256]{1,0:T(8,128)(2,1)S(1)}, bf16[1024,256]{1,0:T(8,128)(2,1)}, u32[]{:S(2)}, u32[]{:S(2)}) %collective-permute-start.21) | collective-permute-done | bytes 524320 | tf_op jit(solution)/shard_map/ppermute | solution.py:386
  107.2 11.9 %row_grads.1 = bf16[4,144,512]{2,1,0:T(8,128)(2,1)} custom-call(s32[2]{0:T(128)} %pad_add_fusion.ids_ref, bf16[256,768]{1,0:T(8,128)(2,1)} %copy-done.12, bf16[256,768]{1,0:T(8,128)(2,1)} %copy-done.21, bf16[256,768]{1,0:T(8,128)(2,1)} %copy-done.20, bf16[256,768]{1,0:T(8,128)(2,1)} %copy-done.22, bf16[1024,1536]{1,0:T(8,128)(2,1)} %bitcast.19, ...), custom_call_target="tpu_custom_call" | custom-call | flops 7699999744 | bytes 25200000 | tf_op jit(solution)/shard_map/row_grads/pallas_call | solution.py:511
  119.1 1.8 slice_bitcast_fusion
  120.9 3.2 %collective-permute-start.10 = (bf16[144,512]{1,0:T(8,128)(2,1)S(1)}, bf16[144,512]{1,0:T(8,128)(2,1)S(1)}, u32[]{:S(2)}, u32[]{:S(2)}) collective-permute-start(bf16[144,512]{1,0:T(8,128)(2,1)S(1)} %get-tuple-element.39), channel_id=1, source_target_pairs={{0,8},{4,12},{8,0},{12,4},{1,9},{5,13},{9,1},{13,5},{2,10},{6,14},... | collective-permute-start | bytes 442376 | tf_op jit(solution)/shard_map/ppermute | solution.py:369
  124.1 1.2 collective-permute-start.9
  125.3 4.2 %collective-permute-done.11.refs_3_ = bf16[144,512]{1,0:T(8,128)(2,1)S(1)} collective-permute-done((bf16[144,512]{1,0:T(8,128)(2,1)S(1)}, bf16[144,512]{1,0:T(8,128)(2,1)S(1)}, u32[]{:S(2)}, u32[]{:S(2)}) %collective-permute-start.11) | collective-permute-done | bytes 147488 | tf_op jit(solution)/shard_map/ppermute | solution.py:369
  129.6 7.0 %collective-permute-done.10.refs_2_ = bf16[144,512]{1,0:T(8,128)(2,1)S(1)} collective-permute-done((bf16[144,512]{1,0:T(8,128)(2,1)S(1)}, bf16[144,512]{1,0:T(8,128)(2,1)S(1)}, u32[]{:S(2)}, u32[]{:S(2)}) %collective-permute-start.10) | collective-permute-done | bytes 147488 | tf_op jit(solution)/shard_map/ppermute | solution.py:369
  136.6 1.4 collective-permute-start.25
  138.0 1.3 collective-permute-start.22
  139.3 0.8 copy-done.10
  140.1 1.3 collective-permute-start.29
  141.4 2.0 %token_grads.1 = (bf16[128,512]{1,0:T(8,128)(2,1)}, bf16[8,128]{1,0:T(8,128)(2,1)}) custom-call(s32[2]{0:T(128)} %pad_add_fusion.ids_ref, s32[1]{0:T(128)S(6)} %copy.16.count_ref, bf16[144,512]{1,0:T(8,128)(2,1)} %get-tuple-element.41.refs_0_, bf16[144,512]{1,0:T(8,128)(2,1)} %copy-done.25, bf16[144,512]{1,0:T(8,128)(2,1)} %copy-done.24, ...), custom_call_target="tpu_custom_call" | custom-call | flops 2200000000 | bytes 7200000 | tf_op jit(solution)/shard_map/token_grads/pallas_call | solution.py:536
  143.5 0.7 collective-permute-start.26
  144.1 10.9 %collective-permute-done.22.refs_10_ = bf16[1024,256]{1,0:T(8,128)(2,1)} collective-permute-done((bf16[1024,256]{1,0:T(8,128)(2,1)}, bf16[1024,256]{1,0:T(8,128)(2,1)}, u32[]{:S(2)}, u32[]{:S(2)}) %collective-permute-start.22) | collective-permute-done | bytes 524320 | tf_op jit(solution)/shard_map/ppermute | solution.py:386
  155.1 1.3 collective-permute-start.23
  156.4 9.9 %collective-permute-done.29.refs_11_ = bf16[1024,256]{1,0:T(8,128)(2,1)} collective-permute-done((bf16[1024,256]{1,0:T(8,128)(2,1)}, bf16[1024,256]{1,0:T(8,128)(2,1)}, u32[]{:S(2)}, u32[]{:S(2)}) %collective-permute-start.29) | collective-permute-done | bytes 524320 | tf_op jit(solution)/shard_map/ppermute | solution.py:386
  166.3 1.0 copy-done.3
  167.4 1.0 copy-done.5
  168.4 1.0 copy-done.9
  169.4 1.0 copy-done.11
  170.5 0.9 copy-done.18
  171.4 1.0 copy-done.19
  172.4 14.0 %weight_grads.2 = (bf16[16,384,512]{2,1,0:T(8,128)(2,1)}, bf16[16,192,512]{2,1,0:T(8,128)(2,1)}) custom-call(s32[2]{0:T(128)S(1)} %copy-done.15, s32[4,16]{1,0:T(4,128)S(1)} %bitcast.23, bf16[2,576,256]{2,1,0:T(8,128)(2,1)S(1)} %stack_columns.2.refs_0_, bf16[2,576,256]{2,1,0:T(8,128)(2,1)S(1)} %collective-permute-done.13.refs_1_, ...), custom_call_target="tpu_custom_call" | custom-call | flops 13200000000 | bytes 43200000 | tf_op jit(solution)/shard_map/weight_grads/pallas_call | solution.py:560
  186.4 10.6 %weight_grads.3 = bf16[16,384,512]{2,1,0:T(8,128)(2,1)} custom-call(s32[2]{0:T(128)S(1)} %copy-done.15, s32[4,16]{1,0:T(4,128)S(1)} %bitcast.24, bf16[2,576,256]{2,1,0:T(8,128)(2,1)S(1)} %stack_columns.2.refs_0_, bf16[2,576,256]{2,1,0:T(8,128)(2,1)S(1)} %collective-permute-done.13.refs_1_, ...), custom_call_target="tpu_custom_call", output_to_operand_aliasing={{}: (19, {})} | custom-call | flops 8800000000 | bytes 28800000 | tf_op jit(solution)/shard_map/weight_grads/pallas_call | solution.py:560
  (88 shorter events, 4.7 us)
Async XLA Ops:
  3.2 8.8 %collective-permute-start.2 = (bf16[144,512]{1,0:T(8,128)(2,1)}, bf16[144,512]{1,0:T(8,128)(2,1)S(1)}, u32[]{:S(2)}, u32[]{:S(2)}) collective-permute-start(bf16[144,512]{1,0:T(8,128)(2,1)} %route.1.refs_0_), channel_id=1, source_target_pairs={{0,12},{4,8},{8,4},{12,0},{1,13},{5,9},{9,5},{13,1},{2,14},{6,10},... | collective-permute-start | bytes 442376 | tf_op jit(solution)/shard_map/ppermute | solution.py:369
  3.2 15.2 %collective-permute-start.1 = (bf16[144,512]{1,0:T(8,128)(2,1)}, bf16[144,512]{1,0:T(8,128)(2,1)S(1)}, u32[]{:S(2)}, u32[]{:S(2)}) collective-permute-start(bf16[144,512]{1,0:T(8,128)(2,1)} %route.1.refs_0_), channel_id=1, source_target_pairs={{0,8},{4,12},{8,0},{12,4},{1,9},{5,13},{9,1},{13,5},{2,10},{6,14},... | collective-permute-start | bytes 442376 | tf_op jit(solution)/shard_map/ppermute | solution.py:369
  5.1 13.3 %collective-permute-start = (bf16[144,512]{1,0:T(8,128)(2,1)}, bf16[144,512]{1,0:T(8,128)(2,1)S(1)}, u32[]{:S(2)}, u32[]{:S(2)}) collective-permute-start(bf16[144,512]{1,0:T(8,128)(2,1)} %route.1.refs_0_), channel_id=1, source_target_pairs={{0,4},{4,0},{8,12},{12,8},{1,5},{5,1},{9,13},{13,9},{2,6},{6,2},{1... | collective-permute-start | bytes 442376 | tf_op jit(solution)/shard_map/ppermute | solution.py:369
  8.1 23.0 %copy-start = (bf16[8,4,32,512]{3,2,1,0:T(8,128)(2,1)S(1)}, bf16[8,4,32,512]{3,2,1,0:T(8,128)(2,1)}, u32[]{:S(2)}) copy-start(bf16[8,4,32,512]{3,2,1,0:T(8,128)(2,1)} %param.16) | copy-start | bytes 3145732
  8.1 40.8 %copy-start.1 = (bf16[8,128,1536]{2,1,0:T(8,128)(2,1)S(1)}, bf16[8,128,1536]{2,1,0:T(8,128)(2,1)}, u32[]{:S(2)}) copy-start(bf16[8,128,1536]{2,1,0:T(8,128)(2,1)} %param.17) | copy-start | bytes 9437188
  8.1 40.8 %copy-start.14 = (s32[2]{0:T(128)S(1)}, s32[2]{0:T(128)}, u32[]{:S(2)}) copy-start(s32[2]{0:T(128)} %pad_add_fusion.ids_ref) | copy-start | bytes 28
  29.2 4.5 %collective-permute-start.3 = (bf16[256,768]{1,0:T(8,128)(2,1)}, bf16[256,768]{1,0:T(8,128)(2,1)S(1)}, u32[]{:S(2)}, u32[]{:S(2)}) collective-permute-start(bf16[256,768]{1,0:T(8,128)(2,1)} %get-tuple-element.22), channel_id=1, source_target_pairs={{0,1},{1,0},{2,3},{3,2},{4,5},{5,4},{6,7},{7,6},{8,9},{9,8},{10,11... | collective-permute-start | bytes 1179656 | tf_op jit(solution)/shard_map/ppermute | solution.py:369
  29.2 12.2 %collective-permute-start.4 = (bf16[256,768]{1,0:T(8,128)(2,1)}, bf16[256,768]{1,0:T(8,128)(2,1)S(1)}, u32[]{:S(2)}, u32[]{:S(2)}) collective-permute-start(bf16[256,768]{1,0:T(8,128)(2,1)} %get-tuple-element.23), channel_id=1, source_target_pairs={{0,2},{1,3},{2,0},{3,1},{4,6},{5,7},{6,4},{7,5},{8,10},{9,11},{10,... | collective-permute-start | bytes 1179656 | tf_op jit(solution)/shard_map/ppermute | solution.py:369
  30.8 18.2 %collective-permute-start.5 = (bf16[256,768]{1,0:T(8,128)(2,1)}, bf16[256,768]{1,0:T(8,128)(2,1)S(1)}, u32[]{:S(2)}, u32[]{:S(2)}) collective-permute-start(bf16[256,768]{1,0:T(8,128)(2,1)} %get-tuple-element.24), channel_id=1, source_target_pairs={{0,3},{1,2},{2,1},{3,0},{4,7},{5,6},{6,5},{7,4},{8,11},{9,10},{10,... | collective-permute-start | bytes 1179656 | tf_op jit(solution)/shard_map/ppermute | solution.py:369
  31.1 24.5 %collective-permute-start.30 = (bf16[1024,256]{1,0:T(8,128)(2,1)S(1)}, bf16[1024,256]{1,0:T(8,128)(2,1)S(1)}, u32[]{:S(2)}, u32[]{:S(2)}) collective-permute-start(bf16[1024,256]{1,0:T(8,128)(2,1)S(1)} %slice.24.refs_8_), channel_id=1, source_target_pairs={{12,8},{8,4},{4,0},{13,9},{9,5},{5,1},{14,10},{10,6},{6,2},{15,11}... | collective-permute-start | bytes 1572872 | tf_op jit(solution)/shard_map/ppermute | solution.py:387
  32.5 25.3 %collective-permute-start.27 = (bf16[1024,256]{1,0:T(8,128)(2,1)S(1)}, bf16[1024,256]{1,0:T(8,128)(2,1)S(1)}, u32[]{:S(2)}, u32[]{:S(2)}) collective-permute-start(bf16[1024,256]{1,0:T(8,128)(2,1)S(1)} %slice.24.refs_8_), channel_id=1, source_target_pairs={{0,4},{4,8},{8,12},{1,5},{5,9},{9,13},{2,6},{6,10},{10,14},{3,7},{... | collective-permute-start | bytes 1572872 | tf_op jit(solution)/shard_map/ppermute | solution.py:386
  52.7 54.5 %copy-start.12 = (bf16[256,768]{1,0:T(8,128)(2,1)}, bf16[256,768]{1,0:T(8,128)(2,1)S(1)}, u32[]{:S(2)}) copy-start(bf16[256,768]{1,0:T(8,128)(2,1)S(1)} %get-tuple-element.26.refs_0_) | copy-start | bytes 1179652
  52.7 21.6 %collective-permute-start.16 = (bf16[576,256]{1,0:T(8,128)(2,1)S(1)}, bf16[576,256]{1,0:T(8,128)(2,1)S(1)}, u32[]{:S(2)}, u32[]{:S(2)}) collective-permute-start(bf16[576,256]{1,0:T(8,128)(2,1)S(1)} %get-tuple-element.31), channel_id=1, source_target_pairs={{0,8},{4,12},{8,0},{12,4},{1,9},{5,13},{9,1},{13,5},{2,10},{6,14},... | collective-permute-start | bytes 884744 | tf_op jit(solution)/shard_map/ppermute | solution.py:369
  52.8 22.2 %collective-permute-start.17 = (bf16[576,256]{1,0:T(8,128)(2,1)S(1)}, bf16[576,256]{1,0:T(8,128)(2,1)S(1)}, u32[]{:S(2)}, u32[]{:S(2)}) collective-permute-start(bf16[576,256]{1,0:T(8,128)(2,1)S(1)} %get-tuple-element.32), channel_id=1, source_target_pairs={{0,12},{4,8},{8,4},{12,0},{1,13},{5,9},{9,5},{13,1},{2,14},{6,10},... | collective-permute-start | bytes 884744 | tf_op jit(solution)/shard_map/ppermute | solution.py:369
  54.2 31.7 %collective-permute-start.7 = (bf16[256,768]{1,0:T(8,128)(2,1)S(1)}, bf16[256,768]{1,0:T(8,128)(2,1)S(1)}, u32[]{:S(2)}, u32[]{:S(2)}) collective-permute-start(bf16[256,768]{1,0:T(8,128)(2,1)S(1)} %get-tuple-element.26.refs_0_), channel_id=1, source_target_pairs={{0,2},{1,3},{2,0},{3,1},{4,6},{5,7},{6,4},{7,5},{8,10},{9,11},{10,... | collective-permute-start | bytes 1179656 | tf_op jit(solution)/shard_map/ppermute | solution.py:369
  55.7 41.7 %copy-start.2 = (bf16[1024,256]{1,0:T(8,128)(2,1)}, bf16[1024,256]{1,0:T(8,128)(2,1)S(1)}, u32[]{:S(2)}) copy-start(bf16[1024,256]{1,0:T(8,128)(2,1)S(1)} %collective-permute-done.30.refs_12_) | copy-start | bytes 1572868
  55.7 21.3 %collective-permute-start.12 = (bf16[576,256]{1,0:T(8,128)(2,1)S(1)}, bf16[576,256]{1,0:T(8,128)(2,1)S(1)}, u32[]{:S(2)}, u32[]{:S(2)}) collective-permute-start(bf16[576,256]{1,0:T(8,128)(2,1)S(1)} %get-tuple-element.30), channel_id=1, source_target_pairs={{0,4},{4,0},{8,12},{12,8},{1,5},{5,1},{9,13},{13,9},{2,6},{6,2},{1... | collective-permute-start | bytes 884744 | tf_op jit(solution)/shard_map/ppermute | solution.py:369
  57.8 39.6 %copy-start.4 = (bf16[1024,256]{1,0:T(8,128)(2,1)}, bf16[1024,256]{1,0:T(8,128)(2,1)S(1)}, u32[]{:S(2)}) copy-start(bf16[1024,256]{1,0:T(8,128)(2,1)S(1)} %collective-permute-done.27.refs_9_) | copy-start | bytes 1572868
  57.8 29.4 %collective-permute-start.6 = (bf16[256,768]{1,0:T(8,128)(2,1)S(1)}, bf16[256,768]{1,0:T(8,128)(2,1)S(1)}, u32[]{:S(2)}, u32[]{:S(2)}) collective-permute-start(bf16[256,768]{1,0:T(8,128)(2,1)S(1)} %get-tuple-element.26.refs_0_), channel_id=1, source_target_pairs={{0,1},{1,0},{2,3},{3,2},{4,5},{5,4},{6,7},{7,6},{8,9},{9,8},{10,11... | collective-permute-start | bytes 1179656 | tf_op jit(solution)/shard_map/ppermute | solution.py:369
  74.3 13.0 %collective-permute-start.31 = (bf16[1024,256]{1,0:T(8,128)(2,1)S(1)}, bf16[1024,256]{1,0:T(8,128)(2,1)S(1)}, u32[]{:S(2)}, u32[]{:S(2)}) collective-permute-start(bf16[1024,256]{1,0:T(8,128)(2,1)S(1)} %collective-permute-done.30.refs_12_), channel_id=1, source_target_pairs={{8,4},{4,0},{9,5},{5,1},{10,6},{6,2},{11,7},{7,3},{24,20},{20,16},... | collective-permute-start | bytes 1572872 | tf_op jit(solution)/shard_map/ppermute | solution.py:387
  75.0 20.8 %collective-permute-start.28 = (bf16[1024,256]{1,0:T(8,128)(2,1)S(1)}, bf16[1024,256]{1,0:T(8,128)(2,1)}, u32[]{:S(2)}, u32[]{:S(2)}) collective-permute-start(bf16[1024,256]{1,0:T(8,128)(2,1)S(1)} %collective-permute-done.27.refs_9_), channel_id=1, source_target_pairs={{4,8},{8,12},{5,9},{9,13},{6,10},{10,14},{7,11},{11,15},{20,24},{2... | collective-permute-start | bytes 1572872 | tf_op jit(solution)/shard_map/ppermute | solution.py:386
  76.4 21.3 %copy-start.6 = (bf16[1024,256]{1,0:T(8,128)(2,1)}, bf16[1024,256]{1,0:T(8,128)(2,1)S(1)}, u32[]{:S(2)}) copy-start(bf16[1024,256]{1,0:T(8,128)(2,1)S(1)} %get-tuple-element.34.refs_8_) | copy-start | bytes 1572868
  76.9 20.5 %collective-permute-start.24 = (bf16[1024,256]{1,0:T(8,128)(2,1)S(1)}, bf16[1024,256]{1,0:T(8,128)(2,1)}, u32[]{:S(2)}, u32[]{:S(2)}) collective-permute-start(bf16[1024,256]{1,0:T(8,128)(2,1)S(1)} %get-tuple-element.34.refs_8_), channel_id=1, source_target_pairs={{12,8},{8,4},{4,0},{13,9},{9,5},{5,1},{14,10},{10,6},{6,2},{15,11}... | collective-permute-start | bytes 1572872 | tf_op jit(solution)/shard_map/ppermute | solution.py:387
  85.8 21.3 %copy-start.20 = (bf16[256,768]{1,0:T(8,128)(2,1)}, bf16[256,768]{1,0:T(8,128)(2,1)S(1)}, u32[]{:S(2)}) copy-start(bf16[256,768]{1,0:T(8,128)(2,1)S(1)} %collective-permute-done.7.refs_2_) | copy-start | bytes 1179652
  85.8 20.6 %collective-permute-start.21 = (bf16[1024,256]{1,0:T(8,128)(2,1)S(1)}, bf16[1024,256]{1,0:T(8,128)(2,1)}, u32[]{:S(2)}, u32[]{:S(2)}) collective-permute-start(bf16[1024,256]{1,0:T(8,128)(2,1)S(1)} %get-tuple-element.34.refs_8_), channel_id=1, source_target_pairs={{0,4},{4,8},{8,12},{1,5},{5,9},{9,13},{2,6},{6,10},{10,14},{3,7},{... | collective-permute-start | bytes 1572872 | tf_op jit(solution)/shard_map/ppermute | solution.py:386
  87.1 20.0 %copy-start.21 = (bf16[256,768]{1,0:T(8,128)(2,1)}, bf16[256,768]{1,0:T(8,128)(2,1)S(1)}, u32[]{:S(2)}) copy-start(bf16[256,768]{1,0:T(8,128)(2,1)S(1)} %collective-permute-done.6.refs_1_) | copy-start | bytes 1179652
  87.2 8.7 %collective-permute-start.8 = (bf16[256,768]{1,0:T(8,128)(2,1)S(1)}, bf16[256,768]{1,0:T(8,128)(2,1)S(1)}, u32[]{:S(2)}, u32[]{:S(2)}) collective-permute-start(bf16[256,768]{1,0:T(8,128)(2,1)S(1)} %collective-permute-done.7.refs_2_), channel_id=1, source_target_pairs={{0,1},{1,0},{2,3},{3,2},{4,5},{5,4},{6,7},{7,6},{8,9},{9,8},{10,11... | collective-permute-start | bytes 1179656 | tf_op jit(solution)/shard_map/ppermute | solution.py:369
  87.3 31.8 %copy-start.8 = (bf16[1024,256]{1,0:T(8,128)(2,1)}, bf16[1024,256]{1,0:T(8,128)(2,1)S(1)}, u32[]{:S(2)}) copy-start(bf16[1024,256]{1,0:T(8,128)(2,1)S(1)} %collective-permute-done.31.refs_13_) | copy-start | bytes 1572868
  87.3 33.6 %collective-permute-start.19 = (bf16[2,576,256]{2,1,0:T(8,128)(2,1)S(1)}, bf16[2,576,256]{2,1,0:T(8,128)(2,1)S(1)}, u32[]{:S(2)}, u32[]{:S(2)}) collective-permute-start(bf16[2,576,256]{2,1,0:T(8,128)(2,1)S(1)} %get-tuple-element.33.refs_4_), channel_id=1, source_target_pairs={{0,2},{1,3},{2,0},{3,1},{4,6},{5,7},{6,4},{7,5},{8,10},{9,11},{10,... | collective-permute-start | bytes 1769480 | tf_op jit(solution)/shard_map/ppermute | solution.py:369
  95.8 25.1 %collective-permute-start.18 = (bf16[2,576,256]{2,1,0:T(8,128)(2,1)S(1)}, bf16[2,576,256]{2,1,0:T(8,128)(2,1)S(1)}, u32[]{:S(2)}, u32[]{:S(2)}) collective-permute-start(bf16[2,576,256]{2,1,0:T(8,128)(2,1)S(1)} %get-tuple-element.33.refs_4_), channel_id=1, source_target_pairs={{0,1},{1,0},{2,3},{3,2},{4,5},{5,4},{6,7},{7,6},{8,9},{9,8},{10,11... | collective-permute-start | bytes 1769480 | tf_op jit(solution)/shard_map/ppermute | solution.py:369
  95.8 11.4 %copy-start.22 = (bf16[256,768]{1,0:T(8,128)(2,1)}, bf16[256,768]{1,0:T(8,128)(2,1)S(1)}, u32[]{:S(2)}) copy-start(bf16[256,768]{1,0:T(8,128)(2,1)S(1)} %collective-permute-done.8.refs_3_) | copy-start | bytes 1179652
  95.8 28.3 %collective-permute-start.14 = (bf16[2,576,256]{2,1,0:T(8,128)(2,1)S(1)}, bf16[2,576,256]{2,1,0:T(8,128)(2,1)S(1)}, u32[]{:S(2)}, u32[]{:S(2)}) collective-permute-start(bf16[2,576,256]{2,1,0:T(8,128)(2,1)S(1)} %stack_columns.2.refs_0_), channel_id=1, source_target_pairs={{0,2},{1,3},{2,0},{3,1},{4,6},{5,7},{6,4},{7,5},{8,10},{9,11},{10,... | collective-permute-start | bytes 1769480 | tf_op jit(solution)/shard_map/ppermute | solution.py:369
  97.4 27.9 %collective-permute-start.13 = (bf16[2,576,256]{2,1,0:T(8,128)(2,1)S(1)}, bf16[2,576,256]{2,1,0:T(8,128)(2,1)S(1)}, u32[]{:S(2)}, u32[]{:S(2)}) collective-permute-start(bf16[2,576,256]{2,1,0:T(8,128)(2,1)S(1)} %stack_columns.2.refs_0_), channel_id=1, source_target_pairs={{0,1},{1,0},{2,3},{3,2},{4,5},{5,4},{6,7},{7,6},{8,9},{9,8},{10,11... | collective-permute-start | bytes 1769480 | tf_op jit(solution)/shard_map/ppermute | solution.py:369
  106.5 32.8 %collective-permute-start.32 = (bf16[1024,256]{1,0:T(8,128)(2,1)S(1)}, bf16[1024,256]{1,0:T(8,128)(2,1)S(1)}, u32[]{:S(2)}, u32[]{:S(2)}) collective-permute-start(bf16[1024,256]{1,0:T(8,128)(2,1)S(1)} %collective-permute-done.31.refs_13_), channel_id=1, source_target_pairs={{4,0},{5,1},{6,2},{7,3},{20,16},{21,17},{22,18},{23,19}} | collective-permute-start | bytes 1572872 | tf_op jit(solution)/shard_map/ppermute | solution.py:387
  119.1 47.2 %copy-start.13 = (s32[16,4]{0,1:T(4,128)S(1)}, s32[16,4]{0,1:T(4,128)}, u32[]{:S(2)}) copy-start(s32[16,4]{0,1:T(4,128)} %param.14) | copy-start | bytes 772
  119.1 47.2 %copy-start.15 = (s32[2]{0:T(128)S(1)}, s32[2]{0:T(128)}, u32[]{:S(2)}) copy-start(s32[2]{0:T(128)} %pad_add_fusion.ids_ref) | copy-start | bytes 28
  120.9 8.6 %collective-permute-start.11 = (bf16[144,512]{1,0:T(8,128)(2,1)S(1)}, bf16[144,512]{1,0:T(8,128)(2,1)S(1)}, u32[]{:S(2)}, u32[]{:S(2)}) collective-permute-start(bf16[144,512]{1,0:T(8,128)(2,1)S(1)} %get-tuple-element.38), channel_id=1, source_target_pairs={{0,12},{4,8},{8,4},{12,0},{1,13},{5,9},{9,5},{13,1},{2,14},{6,10},... | collective-permute-start | bytes 442376 | tf_op jit(solution)/shard_map/ppermute | solution.py:369
  120.9 15.6 %collective-permute-start.10 = (bf16[144,512]{1,0:T(8,128)(2,1)S(1)}, bf16[144,512]{1,0:T(8,128)(2,1)S(1)}, u32[]{:S(2)}, u32[]{:S(2)}) collective-permute-start(bf16[144,512]{1,0:T(8,128)(2,1)S(1)} %get-tuple-element.39), channel_id=1, source_target_pairs={{0,8},{4,12},{8,0},{12,4},{1,9},{5,13},{9,1},{13,5},{2,10},{6,14},... | collective-permute-start | bytes 442376 | tf_op jit(solution)/shard_map/ppermute | solution.py:369
  124.1 13.9 %collective-permute-start.9 = (bf16[144,512]{1,0:T(8,128)(2,1)S(1)}, bf16[144,512]{1,0:T(8,128)(2,1)S(1)}, u32[]{:S(2)}, u32[]{:S(2)}) collective-permute-start(bf16[144,512]{1,0:T(8,128)(2,1)S(1)} %get-tuple-element.40), channel_id=1, source_target_pairs={{0,4},{4,0},{8,12},{12,8},{1,5},{5,1},{9,13},{13,9},{2,6},{6,2},{1... | collective-permute-start | bytes 442376 | tf_op jit(solution)/shard_map/ppermute | solution.py:369
  125.3 41.0 %collective-permute-start.20 = (bf16[2,576,256]{2,1,0:T(8,128)(2,1)S(1)}, bf16[2,576,256]{2,1,0:T(8,128)(2,1)}, u32[]{:S(2)}, u32[]{:S(2)}) collective-permute-start(bf16[2,576,256]{2,1,0:T(8,128)(2,1)S(1)} %collective-permute-done.19.refs_6_), channel_id=1, source_target_pairs={{0,1},{1,0},{2,3},{3,2},{4,5},{5,4},{6,7},{7,6},{8,9},{9,8},{10,11... | collective-permute-start | bytes 1769480 | tf_op jit(solution)/shard_map/ppermute | solution.py:369
  129.6 9.7 %copy-start.23 = (bf16[144,512]{1,0:T(8,128)(2,1)}, bf16[144,512]{1,0:T(8,128)(2,1)S(1)}, u32[]{:S(2)}) copy-start(bf16[144,512]{1,0:T(8,128)(2,1)S(1)} %collective-permute-done.11.refs_3_) | copy-start | bytes 442372
  129.6 36.7 %collective-permute-start.15 = (bf16[2,576,256]{2,1,0:T(8,128)(2,1)S(1)}, bf16[2,576,256]{2,1,0:T(8,128)(2,1)}, u32[]{:S(2)}, u32[]{:S(2)}) collective-permute-start(bf16[2,576,256]{2,1,0:T(8,128)(2,1)S(1)} %collective-permute-done.14.refs_2_), channel_id=1, source_target_pairs={{0,1},{1,0},{2,3},{3,2},{4,5},{5,4},{6,7},{7,6},{8,9},{9,8},{10,11... | collective-permute-start | bytes 1769480 | tf_op jit(solution)/shard_map/ppermute | solution.py:369
  136.6 6.9 %collective-permute-start.25 = (bf16[1024,256]{1,0:T(8,128)(2,1)}, bf16[1024,256]{1,0:T(8,128)(2,1)}, u32[]{:S(2)}, u32[]{:S(2)}) collective-permute-start(bf16[1024,256]{1,0:T(8,128)(2,1)} %collective-permute-done.24.refs_12_), channel_id=1, source_target_pairs={{8,4},{4,0},{9,5},{5,1},{10,6},{6,2},{11,7},{7,3},{24,20},{20,16},... | collective-permute-start | bytes 1572872 | tf_op jit(solution)/shard_map/ppermute | solution.py:387
  138.0 17.1 %collective-permute-start.22 = (bf16[1024,256]{1,0:T(8,128)(2,1)}, bf16[1024,256]{1,0:T(8,128)(2,1)}, u32[]{:S(2)}, u32[]{:S(2)}) collective-permute-start(bf16[1024,256]{1,0:T(8,128)(2,1)} %collective-permute-done.21.refs_9_), channel_id=1, source_target_pairs={{4,8},{8,12},{5,9},{9,13},{6,10},{10,14},{7,11},{11,15},{20,24},{2... | collective-permute-start | bytes 1572872 | tf_op jit(solution)/shard_map/ppermute | solution.py:386
  140.1 26.2 %collective-permute-start.29 = (bf16[1024,256]{1,0:T(8,128)(2,1)}, bf16[1024,256]{1,0:T(8,128)(2,1)}, u32[]{:S(2)}, u32[]{:S(2)}) collective-permute-start(bf16[1024,256]{1,0:T(8,128)(2,1)} %collective-permute-done.28.refs_10_), channel_id=1, source_target_pairs={{8,12},{9,13},{10,14},{11,15},{24,28},{25,29},{26,30},{27,31}} | collective-permute-start | bytes 1572872 | tf_op jit(solution)/shard_map/ppermute | solution.py:386
  143.5 43.0 %collective-permute-start.26 = (bf16[1024,256]{1,0:T(8,128)(2,1)}, bf16[1024,256]{1,0:T(8,128)(2,1)S(1)}, u32[]{:S(2)}, u32[]{:S(2)}) collective-permute-start(bf16[1024,256]{1,0:T(8,128)(2,1)} %collective-permute-done.25.refs_13_), channel_id=1, source_target_pairs={{4,0},{5,1},{6,2},{7,3},{20,16},{21,17},{22,18},{23,19}} | collective-permute-start | bytes 1572872 | tf_op jit(solution)/shard_map/ppermute | solution.py:387
  155.1 31.4 %collective-permute-start.23 = (bf16[1024,256]{1,0:T(8,128)(2,1)}, bf16[1024,256]{1,0:T(8,128)(2,1)S(1)}, u32[]{:S(2)}, u32[]{:S(2)}) collective-permute-start(bf16[1024,256]{1,0:T(8,128)(2,1)} %collective-permute-done.22.refs_10_), channel_id=1, source_target_pairs={{8,12},{9,13},{10,14},{11,15},{24,28},{25,29},{26,30},{27,31}} | collective-permute-start | bytes 1572872 | tf_op jit(solution)/shard_map/ppermute | solution.py:386
  172.4 14.0 %copy-start.7 = (bf16[1024,256]{1,0:T(8,128)(2,1)S(1)}, bf16[1024,256]{1,0:T(8,128)(2,1)}, u32[]{:S(2)}) copy-start(bf16[1024,256]{1,0:T(8,128)(2,1)} %copy-done.6) | copy-start | bytes 1572868
  (14 other events, 24.7 us)

commit v4 on v2

--- a/solution.py
+++ b/solution.py
@@ -10,7 +10,8 @@
 
 BF = jnp.bfloat16
 F32 = jnp.float32
-CUTS = 2
+GROUPS = 2
+PER = 2
 
 
 def nt(a, b):
@@ -65,6 +66,9 @@
         self.cols = self.in_cols + self.down_cols
         self.folds = self.width // self.tokens
         self.tail = 2 * self.slots // self.folds
+        self.side_folds = self.width // self.part
+        self.side_rows = self.down_cols // self.side_folds
+        self.side_start = self.tokens + self.tail
 
 
 def slot_table(z, table_ref, r):
@@ -79,7 +83,9 @@
     return key == ids
 
 
-def route_kernel(z, count_ref, grad_ref, weight_ref, routes_ref, replica_ref, table_ref, out_ref):
+def route_kernel(z, ids_ref, count_ref, *refs):
+    grad_ref, weight_ref, routes_ref, replica_ref, table_ref, pair_ref = refs[:6]
+    outs, sides = refs[6:-1], refs[-1]
     weights = weight_ref[...].astype(F32)
     hits = jnp.zeros((z.slots, z.tokens), F32)
     loads = jnp.zeros((z.slots, z.tokens), F32)
@@ -98,11 +104,21 @@
     earlier = nn(hits.astype(BF), (before < after).astype(F32).astype(BF))
     code = jnp.where(hits > 0.5, earlier, -1.0)
     both = jnp.concatenate([code, loads], axis=0).astype(BF)
-    out_ref[: z.tokens, :] = grad_ref[...]
-    for b in range(z.folds):
-        out_ref[z.tokens :, b * z.tokens : (b + 1) * z.tokens] = both[
-            b * z.tail : (b + 1) * z.tail, :
-        ]
+    pair = pair_ref[...]
+    gate = pair[:, : z.hidden].astype(F32)
+    up = pair[:, z.hidden :].astype(F32)
+    hidden = (gate * (1.0 / (1.0 + jnp.exp(-gate))) * up).astype(BF).T
+    for q in range(z.ep):
+        for f in range(z.side_folds):
+            lo = q * z.down_cols + f * z.side_rows
+            sides[q, :, f * z.part : (f + 1) * z.part] = hidden[lo : lo + z.side_rows, :]
+    for k in range(z.ep):
+        outs[k][: z.tokens, :] = grad_ref[...]
+        for b in range(z.folds):
+            outs[k][z.tokens : z.side_start, b * z.tokens : (b + 1) * z.tokens] = both[
+                b * z.tail : (b + 1) * z.tail, :
+            ]
+        outs[k][z.side_start :, :] = sides[ids_ref[0] ^ k]
 
 
 def block_place(z, block):
@@ -141,22 +157,33 @@
     return pick.reshape(z.local * z.cap, z.tokens).astype(BF)
 
 
+def block_slot(z, mine, step):
+    place = step // z.part_blocks
+    return ((place ^ mine) * z.part_blocks + step % z.part_blocks) // z.slot_blocks
+
+
+def weight_copy(weight_ref, held, sems, slot):
+    return pltpu.make_async_copy(weight_ref.at[slot], held.at[slot], sems.at[slot])
+
+
 def down_kernel(z, ids_ref, *refs):
     bufs = refs[: z.ep]
     weight_ref = refs[z.ep]
     parts = refs[z.ep + 1 : z.ep + 1 + z.sub]
-    grads_ref, codes_ref, rows_ref = refs[z.ep + 1 + z.sub :]
+    grads_ref, codes_ref, rows_ref, held, sems = refs[z.ep + 1 + z.sub :]
     me, mine = ids_ref[0], ids_ref[1]
     step = pl.program_id(0)
 
     @pl.when(step == 0)
     def _():
+        for s in range(z.local):
+            weight_copy(weight_ref, held, sems, s).start()
         for k in range(z.ep):
             source = me ^ k
             grads_ref[source] = bufs[k][: z.tokens, :]
             for b in range(z.folds):
                 codes_ref[source, b * z.tail : (b + 1) * z.tail, :] = bufs[k][
-                    z.tokens :, b * z.tokens : (b + 1) * z.tokens
+                    z.tokens : z.side_start, b * z.tokens : (b + 1) * z.tokens
                 ].astype(F32)
         for p in range(z.ep):
             rows = nn(local_picks(z, codes_ref, p, me), grads_ref[p]).astype(BF)
@@ -166,7 +193,12 @@
     block = (place ^ mine) * z.part_blocks + step % z.part_blocks
     slot, first = block_place(z, block)
     start = pl.multiple_of(first * z.cap, z.block)
-    partial = nt(rows_ref[slot, pl.ds(start, z.block), :], weight_ref[0]).astype(BF)
+
+    @pl.when((step == 0) | (slot != block_slot(z, mine, step - 1)))
+    def _():
+        weight_copy(weight_ref, held, sems, slot).wait()
+
+    partial = nt(rows_ref[slot, pl.ds(start, z.block), :], held[slot]).astype(BF)
     spot = pl.multiple_of((step % z.part_blocks) * z.block, z.block)
     for k in range(z.sub):
 
@@ -189,25 +221,43 @@
 
 def pre_kernel(z, ids_ref, *refs):
     parts = refs[: z.sub]
-    pair_ref, codes_ref, out_ref, grad_ref = refs[z.sub :]
+    pair_ref, codes_ref = refs[z.sub : z.sub + 2]
+    bufs, refs = refs[z.sub + 2 : z.sub + 2 + z.ep], refs[z.sub + 2 + z.ep :]
+    outs = refs[: z.ep]
+    grad_ref, down_ref, sides = refs[z.ep :]
+
+    @pl.when(pl.program_id(0) == 0)
+    def _():
+        for k in range(z.ep):
+            for f in range(z.side_folds):
+                down_ref[k, f * z.side_rows : (f + 1) * z.side_rows, :] = bufs[k][
+                    z.side_start :, f * z.part : (f + 1) * z.part
+                ]
+
+    me = ids_ref[0]
     block = ids_ref[1] * z.part_blocks + pl.program_id(0)
     slot, first = block_place(z, block)
-    scale = block_scale(z, codes_ref, ids_ref[0] * z.local + slot, first)
+    scale = block_scale(z, codes_ref, me * z.local + slot, first)
     grad = parts[0][...].astype(F32)
     for k in range(1, z.sub):
         grad = grad + parts[k][...].astype(F32)
     grad_ref[...] = grad.astype(BF)
-    hidden, grad_gate, grad_up = gate_terms(z, pair_ref[...], grad, scale)
-    hidden = hidden.astype(BF).T
+    _, grad_gate, grad_up = gate_terms(z, pair_ref[...], grad, scale)
     pre = jnp.concatenate([grad_gate.T, grad_up.T], axis=0)
     for q in range(z.ep):
-        out_ref[q, : z.in_cols, :] = pre[q * z.in_cols : (q + 1) * z.in_cols, :]
-        out_ref[q, z.in_cols :, :] = hidden[q * z.down_cols : (q + 1) * z.down_cols, :]
+        sides[q] = pre[q * z.in_cols : (q + 1) * z.in_cols, :]
+    for k in range(z.ep):
+        outs[k][...] = sides[me ^ k]
+
+
+def stack_kernel(*refs):
+    for i, ref in enumerate(refs[:-1]):
+        refs[-1][i] = ref[...]
 
 
 def row_kernel(z, ids_ref, *refs):
     grads = refs[: z.sub]
-    pair_ref, weight_ref, codes_ref, out_ref, rows_ref, marks, held = refs[z.sub :]
+    pair_ref, weight_ref, codes_ref, out_ref, rows_ref, marks, held, weights, sems = refs[z.sub :]
     me, mine = ids_ref[0], ids_ref[1]
     step = pl.program_id(0)
     place = step // z.part_blocks
@@ -216,6 +266,8 @@
 
     @pl.when(step == 0)
     def _():
+        for s in range(z.local):
+            weight_copy(weight_ref, weights, sems, s).start()
         marks[...] = jnp.zeros_like(marks)
 
     spot = pl.multiple_of((step % z.part_blocks) * z.block, z.block)
@@ -229,7 +281,12 @@
     scale = block_scale(z, codes_ref, me * z.local + slot, first)
     hidden, grad_gate, grad_up = gate_terms(z, pair_ref[...], grad, scale)
     route = jnp.sum(hidden * grad, axis=1, keepdims=True).astype(BF).astype(F32)
-    rows = nn(grad_gate, weight_ref[0, : z.hidden, :]) + nn(grad_up, weight_ref[0, z.hidden :, :])
+
+    @pl.when((step == 0) | (slot != block_slot(z, mine, step - 1)))
+    def _():
+        weight_copy(weight_ref, weights, sems, slot).wait()
+
+    rows = nn(grad_gate, weights[slot, : z.hidden, :]) + nn(grad_up, weights[slot, z.hidden :, :])
     start = pl.multiple_of(first * z.cap, z.block)
     rows_ref[slot, pl.ds(start, z.block), :] = rows.astype(BF)
     for a, pick in block_picks(z, codes_ref, me * z.local + slot, first):
@@ -268,54 +325,100 @@
     route_ref[...] = jnp.concatenate(totals, axis=0).astype(BF)
 
 
-def total_kernel(z, down, ids_ref, table_ref, *refs):
+def side_moves(z, groups, sides, held, sems, act):
+    size = z.ep // groups
+    for g in range(groups):
+        for k in range(z.sub):
+            i = g * z.sub + k
+            act(pltpu.make_async_copy(sides[i], held.at[k, pl.ds(g * size, size)], sems.at[i]))
+
+
+def input_moves(z, me, own_ref, rights, lefts, inputs_ref, own_sem, right_sems, left_sems, act):
+    act(pltpu.make_async_copy(own_ref, inputs_ref.at[me], own_sem))
+    for d in range(1, z.ep):
+
+        @pl.when(me >= d)
+        def _():
+            act(
+                pltpu.make_async_copy(
+                    rights[d - 1], inputs_ref.at[me - d], right_sems.at[d - 1]
+                )
+            )
+
+        @pl.when(me + d < z.ep)
+        def _():
+            act(
+                pltpu.make_async_copy(
+                    lefts[d - 1], inputs_ref.at[me + d], left_sems.at[d - 1]
+                )
+            )
+
+
+def expert_products(z, ids_ref, table_ref, held, right_rows, out_ref):
+    me, mine = ids_ref[0], ids_ref[1]
+
+    def one(i, carry):
+        expert = pl.program_id(0) * PER + i
+        slot_ids = [table_ref[r, expert] for r in range(z.reps)]
+        count = 1
+        for r in range(1, z.reps):
+            count = count + (slot_ids[r] != slot_ids[0]).astype(jnp.int32)
+        for c in range(1, z.reps + 1):
+
+            @pl.when(count == c)
+            def _():
+                left, right = [], []
+                for slot_id in slot_ids[:c]:
+                    source = slot_id // z.local
+                    for b in range(z.slot_blocks):
+                        block = (slot_id % z.local) * z.slot_blocks + b
+                        part = (block // z.part_blocks) ^ mine
+                        spot = pl.multiple_of((block % z.part_blocks) * z.block, z.block)
+                        left.append(held[part, source ^ me, :, pl.ds(spot, z.block)])
+                        right.append(right_rows(slot_id, b))
+                left = jnp.concatenate(left, axis=1)
+                out_ref[i] = nn(left, jnp.concatenate(right, axis=0)).astype(BF)
+
+        return carry
+
+    lax.fori_loop(0, PER, one, 0)
+
+
+def total_down_kernel(z, ids_ref, table_ref, *refs):
     sides = refs[: z.sub]
-    inputs_ref, grads_ref, codes_ref = refs[z.sub : z.sub + 3]
-    if down:
-        in_ref, down_ref, held, sems = refs[z.sub + 3 :]
-    else:
-        in_ref, held, sems = refs[z.sub + 4 :]
-    mine = ids_ref[1]
-    expert = pl.program_id(0)
-
-    @pl.when(expert == 0)
-    def _():
-        copies = [
-            pltpu.make_async_copy(sides[k], held.at[k], sems.at[k]) for k in range(z.sub)
-        ]
-        for copy in copies:
-            copy.start()
-        for copy in copies:
-            copy.wait()
-
-    slot_ids = [table_ref[r, expert] for r in range(z.reps)]
-    count = 1
-    for r in range(1, z.reps):
-        count = count + (slot_ids[r] != slot_ids[0]).astype(jnp.int32)
-
-    def add(used):
-        lefts, rights, rows = [], [], []
-        for slot_id in used:
-            source = slot_id // z.local
-            for b in range(z.slot_blocks):
-                block = (slot_id % z.local) * z.slot_blocks + b
-                part = (block // z.part_blocks) ^ mine
-                spot = pl.multiple_of((block % z.part_blocks) * z.block, z.block)
-                lefts.append(held[part, source, :, pl.ds(spot, z.block)])
-                start = pl.multiple_of(block * z.block, z.block)
-                rights.append(inputs_ref[source, pl.ds(start, z.block), :])
-                if down:
-                    rows.append(scaled_rows(z, codes_ref, grads_ref, slot_id, b * z.sources))
-        left = jnp.concatenate(lefts, axis=1)
-        in_ref[0] = nn(left[: z.in_cols, :], jnp.concatenate(rights, axis=0)).astype(BF)
-        if down:
-            down_ref[0] = nn(left[z.in_cols :, :], jnp.concatenate(rows, axis=0)).astype(BF)
-
-    for c in range(1, z.reps + 1):
-
-        @pl.when(count == c)
-        def _():
-            add(slot_ids[:c])
+    grads_ref, codes_ref, out_ref, held, sems = refs[z.sub :]
+
+    @pl.when(pl.program_id(0) == 0)
+    def _():
+        side_moves(z, 1, sides, held, sems, lambda copy: copy.start())
+        side_moves(z, 1, sides, held, sems, lambda copy: copy.wait())
+
+    def right_rows(slot_id, b):
+        return scaled_rows(z, codes_ref, grads_ref, slot_id, b * z.sources)
+
+    expert_products(z, ids_ref, table_ref, held, right_rows, out_ref)
+
+
+def total_in_kernel(z, ids_ref, table_ref, *refs):
+    sides, refs = refs[: GROUPS * z.sub], refs[GROUPS * z.sub :]
+    own_ref, rights, lefts = refs[0], refs[1 : z.ep], refs[z.ep : 2 * z.ep - 1]
+    out_ref, held, inputs_ref, sems, *other_sems = refs[2 * z.ep - 1 :]
+
+    @pl.when(pl.program_id(0) == 0)
+    def _():
+        def moves(act):
+            side_moves(z, GROUPS, sides, held, sems, act)
+            input_moves(z, ids_ref[0], own_ref, rights, lefts, inputs_ref, *other_sems, act)
+
+        moves(lambda copy: copy.start())
+        moves(lambda copy: copy.wait())
+
+    def right_rows(slot_id, b):
+        block = (slot_id % z.local) * z.slot_blocks + b
+        start = pl.multiple_of(block * z.block, z.block)
+        return inputs_ref[slot_id // z.local, pl.ds(start, z.block), :]
+
+    expert_products(z, ids_ref, table_ref, held, right_rows, out_ref)
 
 
 def swap(x, axis, size, bit):
@@ -330,6 +433,17 @@
             have[k | bit] = swap(have[k], axis, size, bit)
         bit //= 2
     return [have[k] for k in range(size)]
+
+
+def chain_gather(x, axis, size):
+    rights, lefts = [], []
+    go, back = x, x
+    for d in range(1, size):
+        go = lax.ppermute(go, axis, [(i, i + 1) for i in range(d - 1, size - 1)])
+        back = lax.ppermute(back, axis, [(i, i - 1) for i in range(size - d, 0, -1)])
+        rights.append(go)
+        lefts.append(back)
+    return [x] + rights + lefts
 
 
 def body(
@@ -350,56 +464,71 @@
     routes, replica, table = routes.T, replica.T, replica_slot.T
     route_weight = route_weight.T
     pair_rows = saved_gate_up.reshape(z.all_rows, z.pair)
-    grad_shape = (z.tokens + z.tail, z.width)
+    grad_shape = (z.side_start + z.side_rows, z.width)
     code_shape = (n, 2 * z.slots, z.tokens)
-    chunk = z.width // CUTS
     inputs = saved_input.reshape(z.all_rows, z.width)
-    inputs = [inputs[:, c * chunk : (c + 1) * chunk] for c in range(CUTS)]
-
-    buf = pl.pallas_call(
+    gathered = chain_gather(inputs, "ep", n)
+
+    routing = (grad_out, route_weight, routes, replica, table)
+    bufs = pl.pallas_call(
         functools.partial(route_kernel, z),
-        out_shape=jax.ShapeDtypeStruct(grad_shape, BF),
-        in_specs=[smem()]
-        + [whole(a.shape) for a in (grad_out, route_weight, routes, replica, table)],
-        out_specs=whole(grad_shape),
-        grid=(1,),
-        compiler_params=params(4),
+        grid_spec=pltpu.PrefetchScalarGridSpec(
+            num_scalar_prefetch=1,
+            grid=(1,),
+            in_specs=[smem()]
+            + [whole(a.shape) for a in routing]
+            + [pl.BlockSpec((z.part, z.pair), lambda i, r: (r[1], 0))],
+            out_specs=[whole(grad_shape)] * n,
+            scratch_shapes=[pltpu.VMEM((n, z.side_rows, z.width), BF)],
+        ),
+        out_shape=[jax.ShapeDtypeStruct(grad_shape, BF)] * n,
+        compiler_params=params(60),
         name="route",
-    )(token_count, grad_out, route_weight, routes, replica, table)
-    bufs = [buf] + [swap(buf, "ep", n, k) for k in range(1, n)]
-    bufs, inputs[0] = lax.optimization_barrier((bufs, inputs[0]))
-    gathered = [lax.all_gather(inputs[0], "ep")]
+    )(ids, token_count, *routing, pair_rows)
+    bufs = [bufs[0]] + [swap(bufs[k], "ep", n, k) for k in range(1, n)]
+
+    def stack(pieces):
+        shape = pieces[0].shape
+        return pl.pallas_call(
+            stack_kernel,
+            in_specs=[whole(shape)] * len(pieces),
+            out_specs=whole((len(pieces),) + shape),
+            out_shape=jax.ShapeDtypeStruct((len(pieces),) + shape, BF),
+            grid=(1,),
+            compiler_params=params(8),
+            name="stack_columns",
+        )(*pieces)
 
     def row_block(i, ids_ref):
         place = i // z.part_blocks
         return (place ^ ids_ref[1]) * z.part_blocks + i % z.part_blocks
-
-    def row_slot(i, ids_ref):
-        return row_block(i, ids_ref) // z.slot_blocks
 
     outs = pl.pallas_call(
         functools.partial(down_kernel, z),
         grid_spec=pltpu.PrefetchScalarGridSpec(
             num_scalar_prefetch=1,
             grid=(z.blocks,),
-            in_specs=[whole(grad_shape)] * n
-            + [pl.BlockSpec((1, z.hidden, z.width), lambda i, r: (row_slot(i, r), 0, 0))],
+            in_specs=[whole(grad_shape)] * n + [pl.BlockSpec(memory_space=pltpu.HBM)],
             out_specs=[whole((z.part, z.hidden))] * m
             + [whole((n, z.tokens, z.width)), whole(code_shape)],
-            scratch_shapes=[pltpu.VMEM((z.local, z.rows, z.width), BF)],
+            scratch_shapes=[
+                pltpu.VMEM((z.local, z.rows, z.width), BF),
+                pltpu.VMEM((z.local, z.hidden, z.width), BF),
+                pltpu.SemaphoreType.DMA((z.local,)),
+            ],
         ),
         out_shape=[jax.ShapeDtypeStruct((z.part, z.hidden), BF)] * m
         + [
             jax.ShapeDtypeStruct((n, z.tokens, z.width), BF),
             jax.ShapeDtypeStruct(code_shape, F32),
         ],
-        compiler_params=params(16),
+        compiler_params=params(52),
         name="hidden_partials",
     )(ids, *bufs, weight_down)
     parts, (grads_all, codes) = outs[:m], outs[m:]
     parts = [parts[0]] + [swap(parts[k], "sub", m, k) for k in range(1, m)]
 
-    pre, grad_part = pl.pallas_call(
+    outs = pl.pallas_call(
         functools.partial(pre_kernel, z),
         grid_spec=pltpu.PrefetchScalarGridSpec(
             num_scalar_prefetch=1,
@@ -408,25 +537,31 @@
             + [
                 pl.BlockSpec((z.block, z.pair), lambda i, r: (r[1] * z.part_blocks + i, 0)),
                 whole(code_shape),
+            ]
+            + [whole(grad_shape)] * n,
+            out_specs=[pl.BlockSpec((z.in_cols, z.block), lambda i, r: (0, i))] * n
+            + [
+                pl.BlockSpec((z.block, z.hidden), lambda i, r: (i, 0)),
+                whole((n, z.down_cols, z.part)),
             ],
-            out_specs=[
-                pl.BlockSpec((n, z.cols, z.block), lambda i, r: (0, 0, i)),
-                pl.BlockSpec((z.block, z.hidden), lambda i, r: (i, 0)),
-            ],
+            scratch_shapes=[pltpu.VMEM((n, z.in_cols, z.block), BF)],
         ),
-        out_shape=[
-            jax.ShapeDtypeStruct((n, z.cols, z.part), BF),
+        out_shape=[jax.ShapeDtypeStruct((z.in_cols, z.part), BF)] * n
+        + [
             jax.ShapeDtypeStruct((z.part, z.hidden), BF),
+            jax.ShapeDtypeStruct((n, z.down_cols, z.part), BF),
         ],
         compiler_params=params(16),
         name="pre_grads",
-    )(ids, *parts, pair_rows, codes)
-
+    )(ids, *parts, pair_rows, codes, *bufs)
+    pieces, grad_part = outs[:n], outs[n]
+    pieces = [pieces[0]] + [swap(pieces[k], "ep", n, k) for k in range(1, n)]
     grad_parts = spread_over(grad_part, "sub", m)
-    columns = lax.all_to_all(pre, "ep", split_axis=0, concat_axis=0, tiled=True)
-    columns, *inputs[1:] = lax.optimization_barrier((columns, *inputs[1:]))
-    gathered += [lax.all_gather(a, "ep") for a in inputs[1:]]
-    sides = spread_over(columns, "sub", m)
+    down_sides = spread_over(outs[n + 1], "sub", m)
+    size = n // GROUPS
+    sides = []
+    for g in range(GROUPS):
+        sides += spread_over(stack(pieces[g * size : (g + 1) * size]), "sub", m)
 
     mark_rows = -(-z.local // 16) * 16
     back_shape = (n, z.tokens + mark_rows, z.width)
@@ -438,7 +573,7 @@
             in_specs=[whole((z.part, z.hidden))] * m
             + [
                 pl.BlockSpec((z.block, z.pair), lambda i, r: (row_block(i, r), 0)),
-                pl.BlockSpec((1, z.pair, z.width), lambda i, r: (row_slot(i, r), 0, 0)),
+                pl.BlockSpec(memory_space=pltpu.HBM),
                 whole(code_shape),
             ],
             out_specs=whole(back_shape),
@@ -446,10 +581,12 @@
                 pltpu.VMEM((z.local, z.rows, z.width), BF),
                 pltpu.VMEM((n, mark_rows, z.tokens), F32),
                 pltpu.VMEM((z.block, z.hidden), BF),
+                pltpu.VMEM((z.local, z.pair, z.width), BF),
+                pltpu.SemaphoreType.DMA((z.local,)),
             ],
         ),
         out_shape=jax.ShapeDtypeStruct(back_shape, BF),
-        compiler_params=params(24),
+        compiler_params=params(32),
         name="row_grads",
     )(ids, *grad_parts, pair_rows, weight_in, codes)
     got = [back[0]] + [swap(back[k], "ep", n, k) for k in range(1, n)]
@@ -466,51 +603,49 @@
         out_specs=[whole((z.tokens, z.width)), whole((z.top, z.tokens))],
         grid=(1,),
         scratch_shapes=[pltpu.VMEM((n, mark_rows, z.tokens), F32)],
-        compiler_params=params(8),
+        compiler_params=params(16),
         name="token_grads",
     )(ids, token_count, *got, routes, replica, table)
 
-    in_shape = jax.ShapeDtypeStruct((z.experts, z.in_cols, z.width), BF)
-    down_shape = jax.ShapeDtypeStruct((z.experts, z.down_cols, z.width), BF)
-    grad_in, grad_down = None, None
-    for c in range(CUTS):
-        first = c == 0
-        in_spec = pl.BlockSpec((1, z.in_cols, chunk), lambda e, r, t, c=c: (e, 0, c))
-        down_spec = pl.BlockSpec((1, z.down_cols, z.width), lambda e, r, t: (e, 0, 0))
-        out = pl.pallas_call(
-            functools.partial(total_kernel, z, first),
+    def total_call(kernel, operands, specs, cols, scratch, name):
+        return pl.pallas_call(
+            functools.partial(kernel, z),
             grid_spec=pltpu.PrefetchScalarGridSpec(
                 num_scalar_prefetch=2,
-                grid=(z.experts,),
-                in_specs=[pl.BlockSpec(memory_space=pl.ANY)] * m
-                + [
-                    whole((n, z.all_rows, chunk)),
-                    whole((n, z.tokens, z.width)),
-                    whole(code_shape),
-                ]
-                + ([] if first else [pl.BlockSpec(memory_space=pl.ANY)]),
-                out_specs=[in_spec, down_spec] if first else [in_spec],
-                scratch_shapes=[
-                    pltpu.VMEM((m, n, z.cols, z.part), BF),
-                    pltpu.SemaphoreType.DMA((m,)),
-                ],
+                grid=(z.experts // PER,),
+                in_specs=specs,
+                out_specs=pl.BlockSpec((PER, cols, z.width), lambda e, r, t: (e, 0, 0)),
+                scratch_shapes=[pltpu.VMEM((m, n, cols, z.part), BF)] + scratch,
             ),
-            out_shape=[in_shape, down_shape] if first else [in_shape],
-            input_output_aliases={} if first else {2 + m + 3: 0},
-            compiler_params=params(24),
-            name="weight_grads",
-        )(
-            ids,
-            table,
-            *sides,
-            gathered[c],
-            grads_all,
-            codes,
-            *([] if first else [grad_in]),
-        )
-        grad_in = out[0]
-        if first:
-            grad_down = out[1]
+            out_shape=jax.ShapeDtypeStruct((z.experts, cols, z.width), BF),
+            compiler_params=params(32),
+            name=name,
+        )(ids, table, *operands)
+
+    anywhere = pl.BlockSpec(memory_space=pl.ANY)
+    pinned = pl.BlockSpec(memory_space=pltpu.HBM)
+    grad_down = total_call(
+        total_down_kernel,
+        [*down_sides, grads_all, codes],
+        [anywhere] * m + [whole((n, z.tokens, z.width)), whole(code_shape)],
+        z.down_cols,
+        [pltpu.SemaphoreType.DMA((m,))],
+        "down_grads",
+    )
+    grad_in = total_call(
+        total_in_kernel,
+        [*sides, *gathered],
+        [anywhere] * (GROUPS * m) + [pinned] * (2 * n - 1),
+        z.in_cols,
+        [
+            pltpu.VMEM((n, z.all_rows, z.width), BF),
+            pltpu.SemaphoreType.DMA((GROUPS * m,)),
+            pltpu.SemaphoreType.DMA,
+            pltpu.SemaphoreType.DMA((n - 1,)),
+            pltpu.SemaphoreType.DMA((n - 1,)),
+        ],
+        "in_grads",
+    )
     return grad_tokens, grad_routes.T, grad_in, grad_down
 
 

time: 206 us -> 181 us (0.88)
  blocking collectives: 39.8 us -> 0 us
  starting transfers between devices: 15.5 us -> 35.9 us
  waiting for transfers between devices: 75.4 us -> 94.3 us
  local copies, waits for them, and re-layouts: 22.2 us -> 6.19 us
  between operations: 14.9 us -> 1.55 us
  Pallas kernels: 37.8 us -> 41.6 us
    all_to_all x1 -> x0, blocking collectives: 39.8 us -> none  [body(): columns = lax.all_to_all(pre, 'ep', split_axis=0, concat_axis=0, tiled=True)]
    ppermute x15 -> x24, waiting for transfers between devices: 75.3 us -> 94.3 us  [swap(): return lax.ppermute(x, axis, [(i, i ^ bit) for i in range(size)])]
    unnamed x48 -> x20, local copies, waits for them, and re-layouts: 19.9 us -> 6.15 us
    ppermute x0 -> x6, starting transfers between devices: none -> 11.5 us  [the longest x3 7.62 us: chain_gather(): go = lax.ppermute(go, axis, [(i, i + 1) for i in range(d - 1, size - 1)])]
    ppermute x15 -> x24, starting transfers between devices: 15.4 us -> 24.4 us  [swap(): return lax.ppermute(x, axis, [(i, i ^ bit) for i in range(size)])]
    pallas_call x1, Pallas kernels: 5.69 us -> 8.07 us  [body(): pl.pallas_call(functools.partial(row_kernel, z), grid_spec=pltpu.Prefetch...]
    slice x1 -> x0, local copies, waits for them, and re-layouts: 2.23 us -> none  [body(): inputs = [inputs[:, c * chunk:(c + 1) * chunk] for c in range(CUTS)]]
    pallas_call x3 -> x5, Pallas kernels: 24.5 us -> 24 us  [the longest x2 20.6 us: total_call(): pl.pallas_call(functools.partial(kernel, z), grid_spec=pltpu.PrefetchScal...]
  transfers between devices with their start and end apart: 17 -> 30, of which waited for: 9 -> 10; matrix products, arithmetic and copies ran while one was open for 1% -> 0% of each run, Pallas kernels for 13% -> 17%
where the time goes in v4:
time: 181 us; the launch traced here: 180 us
  waiting for transfers between devices  94.3 us (52%)
  Pallas kernels  41.6 us (23%)
  starting transfers between devices  35.9 us (20%)
  local copies, waits for them, and re-layouts  6.19 us (3%)
    ppermute x24, waiting for transfers between devices, swap(): return lax.ppermute(x, axis, [(i, i ^ bit) for i in range(size)])  94.3 us
    ppermute x24, starting transfers between devices, swap(): return lax.ppermute(x, axis, [(i, i ^ bit) for i in range(size)])  24.4 us
    pallas_call x2, Pallas kernels, total_call(): pl.pallas_call(functools.partial(kernel, z), grid_spec=pltpu.PrefetchScal...  20.6 us
    pallas_call x1, Pallas kernels, body(): pl.pallas_call(functools.partial(row_kernel, z), grid_spec=pltpu.Prefetch...  8.07 us
    ppermute x3, starting transfers between devices, chain_gather(): go = lax.ppermute(go, axis, [(i, i + 1) for i in range(d - 1, size - 1)])  7.62 us
    pallas_call x1, Pallas kernels, body(): pl.pallas_call(functools.partial(down_kernel, z), grid_spec=pltpu.Prefetc...  6.38 us
    unnamed x20, local copies, waits for them, and re-layouts  6.15 us
    ppermute x3, starting transfers between devices, chain_gather(): lax.ppermute(back, axis, [(i, i - 1) for i in range(size - d, 0, -1)])  3.86 us
  transfers between devices with their start and end apart: 30, of which 10 were waited for; matrix products, arithmetic and copies ran while one was open for 0% of the time, Pallas kernels for 17%

profile of v4, /device:TPU:0, one launch (start us, length us, event | category | flops | bytes accessed | tf_op | source)
XLA Modules:
  0.0 180.2 jit_solution(6215277848366158000)
XLA Ops:
  0.6 0.0 copy-start
  0.6 6.2 %collective-permute-start.21 = (bf16[1024,512]{1,0:T(8,128)(2,1)}, bf16[1024,512]{1,0:T(8,128)(2,1)}, u32[]{:S(2)}, u32[]{:S(2)}) collective-permute-start(bf16[1024,512]{1,0:T(8,128)(2,1)} %bitcast.20), channel_id=1, source_target_pairs={{0,4},{4,8},{8,12},{1,5},{5,9},{9,13},{2,6},{6,10},{10,14},{3,7},{... | collective-permute-start | bytes 3145736 | tf_op jit(solution)/shard_map/ppermute | solution.py:442
  6.8 1.3 collective-permute-start.24
  8.8 0.6 pad_add_fusion.ids_ref
  9.3 3.3 %route.1 = (bf16[240,512]{1,0:T(8,128)(2,1)}, bf16[240,512]{1,0:T(8,128)(2,1)}, bf16[240,512]{1,0:T(8,128)(2,1)}, bf16[240,512]{1,0:T(8,128)(2,1)}) custom-call(s32[2]{0:T(128)} %pad_add_fusion.ids_ref, s32[1]{0:T(128)S(6)} %copy.14.count_ref, bf16[128,512]{1,0:T(8,128)(2,1)} %refs_0_.1, bf16[8,128]{1,0:T(8,128)(2,1)} %bitcast.31, s32[8,128]{1,0:T(8,128)} %bitcast.27, ...), custom_call_target="tpu_custom_call" | custom-call | tf_op jit(solution)/shard_map/route/pallas_call | solution.py:473
  12.7 2.6 %collective-permute-start = (bf16[240,512]{1,0:T(8,128)(2,1)}, bf16[240,512]{1,0:T(8,128)(2,1)S(1)}, u32[]{:S(2)}, u32[]{:S(2)}) collective-permute-start(bf16[240,512]{1,0:T(8,128)(2,1)} %get-tuple-element.23), channel_id=1, source_target_pairs={{0,4},{4,0},{8,12},{12,8},{1,5},{5,1},{9,13},{13,9},{2,6},{6,2},{1... | collective-permute-start | bytes 737288 | tf_op jit(solution)/shard_map/ppermute | solution.py:425
  15.3 2.6 %collective-permute-start.1 = (bf16[240,512]{1,0:T(8,128)(2,1)}, bf16[240,512]{1,0:T(8,128)(2,1)S(1)}, u32[]{:S(2)}, u32[]{:S(2)}) collective-permute-start(bf16[240,512]{1,0:T(8,128)(2,1)} %get-tuple-element.24), channel_id=1, source_target_pairs={{0,8},{4,12},{8,0},{12,4},{1,9},{5,13},{9,1},{13,5},{2,10},{6,14},... | collective-permute-start | bytes 737288 | tf_op jit(solution)/shard_map/ppermute | solution.py:425
  17.9 26.1 %collective-permute-done.refs_1_.refs_7_ = bf16[240,512]{1,0:T(8,128)(2,1)S(1)} collective-permute-done((bf16[240,512]{1,0:T(8,128)(2,1)}, bf16[240,512]{1,0:T(8,128)(2,1)S(1)}, u32[]{:S(2)}, u32[]{:S(2)}) %collective-permute-start) | collective-permute-done | bytes 245792 | tf_op jit(solution)/shard_map/ppermute | solution.py:425
  44.0 6.9 %collective-permute-done.1.refs_2_.refs_8_ = bf16[240,512]{1,0:T(8,128)(2,1)S(1)} collective-permute-done((bf16[240,512]{1,0:T(8,128)(2,1)}, bf16[240,512]{1,0:T(8,128)(2,1)S(1)}, u32[]{:S(2)}, u32[]{:S(2)}) %collective-permute-start.1) | collective-permute-done | bytes 245792 | tf_op jit(solution)/shard_map/ppermute | solution.py:425
  50.9 0.9 copy-done.3
  51.8 0.6 copy-done.6
  52.4 6.4 %hidden_partials.1 = (bf16[256,768]{1,0:T(8,128)(2,1)S(1)}, bf16[256,768]{1,0:T(8,128)(2,1)S(1)}, bf16[256,768]{1,0:T(8,128)(2,1)}, bf16[256,768]{1,0:T(8,128)(2...) custom-call(s32[2]{0:T(128)S(1)} %copy-done.6, bf16[240,512]{1,0:T(8,128)(2,1)S(1)} %copy-done.3, ...), custom_call_target="tpu_custom_call" | custom-call | tf_op jit(solution)/shard_map/hidden_partials/pallas_call | solution.py:506
  58.8 0.1 collective-permute-start.3
  58.9 2.5 %collective-permute-start.4 = (bf16[256,768]{1,0:T(8,128)(2,1)}, bf16[256,768]{1,0:T(8,128)(2,1)S(1)}, u32[]{:S(2)}, u32[]{:S(2)}) collective-permute-start(bf16[256,768]{1,0:T(8,128)(2,1)} %get-tuple-element.28), channel_id=1, source_target_pairs={{0,2},{1,3},{2,0},{3,1},{4,6},{5,7},{6,4},{7,5},{8,10},{9,11},{10,... | collective-permute-start | bytes 1179656 | tf_op jit(solution)/shard_map/ppermute | solution.py:425
  61.5 0.1 collective-permute-start.5
  61.5 0.7 collective-permute-start.22
  62.3 1.3 collective-permute-start.25
  63.6 8.1 %collective-permute-done.4.refs_2_ = bf16[256,768]{1,0:T(8,128)(2,1)S(1)} collective-permute-done((bf16[256,768]{1,0:T(8,128)(2,1)}, bf16[256,768]{1,0:T(8,128)(2,1)S(1)}, u32[]{:S(2)}, u32[]{:S(2)}) %collective-permute-start.4) | collective-permute-done | bytes 393248 | tf_op jit(solution)/shard_map/ppermute | solution.py:425
  71.6 7.9 %collective-permute-done.5.refs_3_ = bf16[256,768]{1,0:T(8,128)(2,1)S(1)} collective-permute-done((bf16[256,768]{1,0:T(8,128)(2,1)}, bf16[256,768]{1,0:T(8,128)(2,1)S(1)}, u32[]{:S(2)}, u32[]{:S(2)}) %collective-permute-start.5) | collective-permute-done | bytes 393248 | tf_op jit(solution)/shard_map/ppermute | solution.py:425
  79.5 1.8 pre_grads.1
  81.3 4.4 %collective-permute-start.12 = (bf16[384,256]{1,0:T(8,128)(2,1)S(1)}, bf16[384,256]{1,0:T(8,128)(2,1)S(1)}, u32[]{:S(2)}, u32[]{:S(2)}) collective-permute-start(bf16[384,256]{1,0:T(8,128)(2,1)S(1)} %get-tuple-element.35), channel_id=1, source_target_pairs={{0,4},{4,0},{8,12},{12,8},{1,5},{5,1},{9,13},{13,9},{2,6},{6,2},{1... | collective-permute-start | bytes 589832 | tf_op jit(solution)/shard_map/ppermute | solution.py:425
  85.8 2.4 %collective-permute-start.17 = (bf16[384,256]{1,0:T(8,128)(2,1)S(1)}, bf16[384,256]{1,0:T(8,128)(2,1)S(1)}, u32[]{:S(2)}, u32[]{:S(2)}) collective-permute-start(bf16[384,256]{1,0:T(8,128)(2,1)S(1)} %get-tuple-element.37), channel_id=1, source_target_pairs={{0,12},{4,8},{8,4},{12,0},{1,13},{5,9},{9,5},{13,1},{2,14},{6,10},... | collective-permute-start | bytes 589832 | tf_op jit(solution)/shard_map/ppermute | solution.py:425
  88.2 13.0 %collective-permute-done.12.refs_1_ = bf16[384,256]{1,0:T(8,128)(2,1)S(1)} collective-permute-done((bf16[384,256]{1,0:T(8,128)(2,1)S(1)}, bf16[384,256]{1,0:T(8,128)(2,1)S(1)}, u32[]{:S(2)}, u32[]{:S(2)}) %collective-permute-start.12) | collective-permute-done | bytes 196640 | tf_op jit(solution)/shard_map/ppermute | solution.py:425
  101.3 6.5 %collective-permute-done.16.refs_0_ = bf16[384,256]{1,0:T(8,128)(2,1)S(1)} collective-permute-done((bf16[384,256]{1,0:T(8,128)(2,1)S(1)}, bf16[384,256]{1,0:T(8,128)(2,1)S(1)}, u32[]{:S(2)}, u32[]{:S(2)}) %collective-permute-start.16) | collective-permute-done | bytes 196640 | tf_op jit(solution)/shard_map/ppermute | solution.py:425
  107.7 1.7 collective-permute-start.7
  109.5 0.4 collective-permute-start.28
  109.9 9.9 %collective-permute-done.7.refs_2_ = bf16[256,768]{1,0:T(8,128)(2,1)S(1)} collective-permute-done((bf16[256,768]{1,0:T(8,128)(2,1)S(1)}, bf16[256,768]{1,0:T(8,128)(2,1)S(1)}, u32[]{:S(2)}, u32[]{:S(2)}) %collective-permute-start.7) | collective-permute-done | bytes 393248 | tf_op jit(solution)/shard_map/ppermute | solution.py:425
  119.8 0.5 collective-permute-start.8
  120.3 0.7 collective-permute-start.23
  121.1 1.3 collective-permute-start.26
  122.4 3.2 %collective-permute-done.28.refs_2_ = bf16[4,192,256]{2,1,0:T(8,128)(2,1)S(1)} collective-permute-done((bf16[4,192,256]{2,1,0:T(8,128)(2,1)S(1)}, bf16[4,192,256]{2,1,0:T(8,128)(2,1)S(1)}, u32[]{:S(2)}, u32[]{:S(2)}) %collective-permute-start.28) | collective-permute-done | bytes 393248 | tf_op jit(solution)/shard_map/ppermute | solution.py:425
  125.5 1.7 collective-permute-start.14
  127.3 0.3 collective-permute-start.19
  127.7 0.0 copy-start.1
  127.7 4.6 %copy-done.1 = bf16[8,1536,512]{2,1,0:T(8,128)(2,1)S(1)} copy-done((bf16[8,1536,512]{2,1,0:T(8,128)(2,1)S(1)}, bf16[8,1536,512]{2,1,0:T(8,128)(2,1)}, u32[]{:S(2)}) %copy-start.1) | copy-done | bytes 12582936
  132.2 8.1 %row_grads.1 = bf16[4,144,512]{2,1,0:T(8,128)(2,1)S(1)} custom-call(s32[2]{0:T(128)S(1)} %copy-done.7, bf16[256,768]{1,0:T(8,128)(2,1)S(1)} %get-tuple-element.31.refs_0_, bf16[256,768]{1,0:T(8,128)(2,1)S(1)} %collective-permute-done.6.refs_1_, bf16[256,768]{1,0:T(8,128)(2,1)S(1)} %collective-permute-done.7.refs_2_, ...), custom_call_target="tpu_custom_call" | custom-call | tf_op jit(solution)/shard_map/row_grads/pallas_call | solution.py:568
  140.3 0.0 copy-start.8
  140.3 0.0 copy-start.9
  140.3 0.0 copy-start.2
  140.4 0.1 collective-permute-start.9
  140.5 1.9 %collective-permute-done.19.refs_6_ = bf16[2,384,256]{2,1,0:T(8,128)(2,1)S(1)} collective-permute-done((bf16[2,384,256]{2,1,0:T(8,128)(2,1)S(1)}, bf16[2,384,256]{2,1,0:T(8,128)(2,1)S(1)}, u32[]{:S(2)}, u32[]{:S(2)}) %collective-permute-start.19) | collective-permute-done | bytes 393248 | tf_op jit(solution)/shard_map/ppermute | solution.py:425
  142.4 4.3 %collective-permute-start.11 = (bf16[144,512]{1,0:T(8,128)(2,1)S(1)}, bf16[144,512]{1,0:T(8,128)(2,1)S(1)}, u32[]{:S(2)}, u32[]{:S(2)}) collective-permute-start(bf16[144,512]{1,0:T(8,128)(2,1)S(1)} %get-tuple-element.40), channel_id=1, source_target_pairs={{0,12},{4,8},{8,4},{12,0},{1,13},{5,9},{9,5},{13,1},{2,14},{6,10},... | collective-permute-start | bytes 442376 | tf_op jit(solution)/shard_map/ppermute | solution.py:425
  146.7 10.8 %collective-permute-done.9.refs_1_ = bf16[144,512]{1,0:T(8,128)(2,1)S(1)} collective-permute-done((bf16[144,512]{1,0:T(8,128)(2,1)S(1)}, bf16[144,512]{1,0:T(8,128)(2,1)S(1)}, u32[]{:S(2)}, u32[]{:S(2)}) %collective-permute-start.9) | collective-permute-done | bytes 147488 | tf_op jit(solution)/shard_map/ppermute | solution.py:425
  157.5 0.5 collective-permute-start.15
  158.0 0.1 collective-permute-start.20
  158.1 10.1 %down_grads.1 = bf16[16,192,512]{2,1,0:T(8,128)(2,1)} custom-call(s32[2]{0:T(128)S(1)} %copy-done.7, s32[4,16]{1,0:T(4,128)S(1)} %bitcast.24, bf16[4,192,256]{2,1,0:T(8,128)(2,1)S(1)} %get-tuple-element.38.refs_0_, bf16[4,192,256]{2,1,0:T(8,128)(2,1)S(1)} %collective-permute-done.27.refs_1_, bf16[4,192,256]{2,1,0:T(8,128)(2,1)S(1)} %collective-permute-done.28.refs_2_, ...), custom_call_target="tpu_custom_call" | custom-call | tf_op jit(solution)/shard_map/down_grads/pallas_call | solution.py:611
  168.2 1.4 token_grads.1
  169.7 10.5 %in_grads.1 = bf16[16,384,512]{2,1,0:T(8,128)(2,1)} custom-call(s32[2]{0:T(128)S(1)} %copy-done.7, s32[4,16]{1,0:T(4,128)S(1)} %bitcast.26, bf16[2,384,256]{2,1,0:T(8,128)(2,1)S(1)} %stack_columns.2.refs_0_, bf16[2,384,256]{2,1,0:T(8,128)(2,1)S(1)} %collective-permute-done.13.refs_1_, bf16[2,384,256]{2,1,0:T(8,128)(2,1)S(1)} %collective-permute-done.14.refs_2_, ...), custom_call_target="tpu_custom_call" | custom-call | tf_op jit(solution)/shard_map/in_grads/pallas_call | solution.py:611
  (43 shorter events, 0.2 us)
Async XLA Ops:
  0.6 78.9 %copy-start = (bf16[8,128,1536]{2,1,0:T(8,128)(2,1)S(1)}, bf16[8,128,1536]{2,1,0:T(8,128)(2,1)}, u32[]{:S(2)}) copy-start(bf16[8,128,1536]{2,1,0:T(8,128)(2,1)} %param.17) | copy-start | bytes 9437188
  0.6 60.9 %collective-permute-start.21 = (bf16[1024,512]{1,0:T(8,128)(2,1)}, bf16[1024,512]{1,0:T(8,128)(2,1)}, u32[]{:S(2)}, u32[]{:S(2)}) collective-permute-start(bf16[1024,512]{1,0:T(8,128)(2,1)} %bitcast.20), channel_id=1, source_target_pairs={{0,4},{4,8},{8,12},{1,5},{5,9},{9,13},{2,6},{6,10},{10,14},{3,7},{... | collective-permute-start | bytes 3145736 | tf_op jit(solution)/shard_map/ppermute | solution.py:442
  6.8 55.4 %collective-permute-start.24 = (bf16[1024,512]{1,0:T(8,128)(2,1)}, bf16[1024,512]{1,0:T(8,128)(2,1)}, u32[]{:S(2)}, u32[]{:S(2)}) collective-permute-start(bf16[1024,512]{1,0:T(8,128)(2,1)} %bitcast.21), channel_id=1, source_target_pairs={{12,8},{8,4},{4,0},{13,9},{9,5},{5,1},{14,10},{10,6},{6,2},{15,11}... | collective-permute-start | bytes 3145736 | tf_op jit(solution)/shard_map/ppermute | solution.py:443
  12.7 31.3 %collective-permute-start = (bf16[240,512]{1,0:T(8,128)(2,1)}, bf16[240,512]{1,0:T(8,128)(2,1)S(1)}, u32[]{:S(2)}, u32[]{:S(2)}) collective-permute-start(bf16[240,512]{1,0:T(8,128)(2,1)} %get-tuple-element.23), channel_id=1, source_target_pairs={{0,4},{4,0},{8,12},{12,8},{1,5},{5,1},{9,13},{13,9},{2,6},{6,2},{1... | collective-permute-start | bytes 737288 | tf_op jit(solution)/shard_map/ppermute | solution.py:425
  15.3 35.6 %collective-permute-start.1 = (bf16[240,512]{1,0:T(8,128)(2,1)}, bf16[240,512]{1,0:T(8,128)(2,1)S(1)}, u32[]{:S(2)}, u32[]{:S(2)}) collective-permute-start(bf16[240,512]{1,0:T(8,128)(2,1)} %get-tuple-element.24), channel_id=1, source_target_pairs={{0,8},{4,12},{8,0},{12,4},{1,9},{5,13},{9,1},{13,5},{2,10},{6,14},... | collective-permute-start | bytes 737288 | tf_op jit(solution)/shard_map/ppermute | solution.py:425
  17.9 33.0 %collective-permute-start.2 = (bf16[240,512]{1,0:T(8,128)(2,1)}, bf16[240,512]{1,0:T(8,128)(2,1)S(1)}, u32[]{:S(2)}, u32[]{:S(2)}) collective-permute-start(bf16[240,512]{1,0:T(8,128)(2,1)} %get-tuple-element.25), channel_id=1, source_target_pairs={{0,12},{4,8},{8,4},{12,0},{1,13},{5,9},{9,5},{13,1},{2,14},{6,10},... | collective-permute-start | bytes 737288 | tf_op jit(solution)/shard_map/ppermute | solution.py:425
  50.9 0.9 copy-start.3
  51.8 0.6 copy-start.6
  52.4 75.2 %copy-start.7 = (s32[2]{0:T(128)S(1)}, s32[2]{0:T(128)}, u32[]{:S(2)}) copy-start(s32[2]{0:T(128)} %pad_add_fusion.ids_ref) | copy-start | bytes 28
  58.8 4.7 %collective-permute-start.3 = (bf16[256,768]{1,0:T(8,128)(2,1)S(1)}, bf16[256,768]{1,0:T(8,128)(2,1)S(1)}, u32[]{:S(2)}, u32[]{:S(2)}) collective-permute-start(bf16[256,768]{1,0:T(8,128)(2,1)S(1)} %get-tuple-element.27), channel_id=1, source_target_pairs={{0,1},{1,0},{2,3},{3,2},{4,5},{5,4},{6,7},{7,6},{8,9},{9,8},{10,11... | collective-permute-start | bytes 1179656 | tf_op jit(solution)/shard_map/ppermute | solution.py:425
  58.9 12.7 %collective-permute-start.4 = (bf16[256,768]{1,0:T(8,128)(2,1)}, bf16[256,768]{1,0:T(8,128)(2,1)S(1)}, u32[]{:S(2)}, u32[]{:S(2)}) collective-permute-start(bf16[256,768]{1,0:T(8,128)(2,1)} %get-tuple-element.28), channel_id=1, source_target_pairs={{0,2},{1,3},{2,0},{3,1},{4,6},{5,7},{6,4},{7,5},{8,10},{9,11},{10,... | collective-permute-start | bytes 1179656 | tf_op jit(solution)/shard_map/ppermute | solution.py:425
  61.5 18.1 %collective-permute-start.5 = (bf16[256,768]{1,0:T(8,128)(2,1)}, bf16[256,768]{1,0:T(8,128)(2,1)S(1)}, u32[]{:S(2)}, u32[]{:S(2)}) collective-permute-start(bf16[256,768]{1,0:T(8,128)(2,1)} %get-tuple-element.29), channel_id=1, source_target_pairs={{0,3},{1,2},{2,1},{3,0},{4,7},{5,6},{6,5},{7,4},{8,11},{9,10},{10,... | collective-permute-start | bytes 1179656 | tf_op jit(solution)/shard_map/ppermute | solution.py:425
  61.5 58.8 %collective-permute-start.22 = (bf16[1024,512]{1,0:T(8,128)(2,1)}, bf16[1024,512]{1,0:T(8,128)(2,1)S(1)}, u32[]{:S(2)}, u32[]{:S(2)}) collective-permute-start(bf16[1024,512]{1,0:T(8,128)(2,1)} %collective-permute-done.21.refs_9_), channel_id=1, source_target_pairs={{4,8},{8,12},{5,9},{9,13},{6,10},{10,14},{7,11},{11,15},{20,24},{2... | collective-permute-start | bytes 3145736 | tf_op jit(solution)/shard_map/ppermute | solution.py:442
  62.3 58.8 %collective-permute-start.25 = (bf16[1024,512]{1,0:T(8,128)(2,1)}, bf16[1024,512]{1,0:T(8,128)(2,1)S(1)}, u32[]{:S(2)}, u32[]{:S(2)}) collective-permute-start(bf16[1024,512]{1,0:T(8,128)(2,1)} %collective-permute-done.24.refs_12_), channel_id=1, source_target_pairs={{8,4},{4,0},{9,5},{5,1},{10,6},{6,2},{11,7},{7,3},{24,20},{20,16},... | collective-permute-start | bytes 3145736 | tf_op jit(solution)/shard_map/ppermute | solution.py:443
  81.3 19.9 %collective-permute-start.12 = (bf16[384,256]{1,0:T(8,128)(2,1)S(1)}, bf16[384,256]{1,0:T(8,128)(2,1)S(1)}, u32[]{:S(2)}, u32[]{:S(2)}) collective-permute-start(bf16[384,256]{1,0:T(8,128)(2,1)S(1)} %get-tuple-element.35), channel_id=1, source_target_pairs={{0,4},{4,0},{8,12},{12,8},{1,5},{5,1},{9,13},{13,9},{2,6},{6,2},{1... | collective-permute-start | bytes 589832 | tf_op jit(solution)/shard_map/ppermute | solution.py:425
  85.8 22.0 %collective-permute-start.16 = (bf16[384,256]{1,0:T(8,128)(2,1)S(1)}, bf16[384,256]{1,0:T(8,128)(2,1)S(1)}, u32[]{:S(2)}, u32[]{:S(2)}) collective-permute-start(bf16[384,256]{1,0:T(8,128)(2,1)S(1)} %get-tuple-element.36), channel_id=1, source_target_pairs={{0,8},{4,12},{8,0},{12,4},{1,9},{5,13},{9,1},{13,5},{2,10},{6,14},... | collective-permute-start | bytes 589832 | tf_op jit(solution)/shard_map/ppermute | solution.py:425
  85.8 23.7 %collective-permute-start.17 = (bf16[384,256]{1,0:T(8,128)(2,1)S(1)}, bf16[384,256]{1,0:T(8,128)(2,1)S(1)}, u32[]{:S(2)}, u32[]{:S(2)}) collective-permute-start(bf16[384,256]{1,0:T(8,128)(2,1)S(1)} %get-tuple-element.37), channel_id=1, source_target_pairs={{0,12},{4,8},{8,4},{12,0},{1,13},{5,9},{9,5},{13,1},{2,14},{6,10},... | collective-permute-start | bytes 589832 | tf_op jit(solution)/shard_map/ppermute | solution.py:425
  101.3 8.2 %collective-permute-start.6 = (bf16[256,768]{1,0:T(8,128)(2,1)S(1)}, bf16[256,768]{1,0:T(8,128)(2,1)S(1)}, u32[]{:S(2)}, u32[]{:S(2)}) collective-permute-start(bf16[256,768]{1,0:T(8,128)(2,1)S(1)} %get-tuple-element.31.refs_0_), channel_id=1, source_target_pairs={{0,1},{1,0},{2,3},{3,2},{4,5},{5,4},{6,7},{7,6},{8,9},{9,8},{10,11... | collective-permute-start | bytes 1179656 | tf_op jit(solution)/shard_map/ppermute | solution.py:425
  107.7 12.1 %collective-permute-start.7 = (bf16[256,768]{1,0:T(8,128)(2,1)S(1)}, bf16[256,768]{1,0:T(8,128)(2,1)S(1)}, u32[]{:S(2)}, u32[]{:S(2)}) collective-permute-start(bf16[256,768]{1,0:T(8,128)(2,1)S(1)} %get-tuple-element.31.refs_0_), channel_id=1, source_target_pairs={{0,2},{1,3},{2,0},{3,1},{4,6},{5,7},{6,4},{7,5},{8,10},{9,11},{10,... | collective-permute-start | bytes 1179656 | tf_op jit(solution)/shard_map/ppermute | solution.py:425
  109.4 10.4 %collective-permute-start.27 = (bf16[4,192,256]{2,1,0:T(8,128)(2,1)S(1)}, bf16[4,192,256]{2,1,0:T(8,128)(2,1)S(1)}, u32[]{:S(2)}, u32[]{:S(2)}) collective-permute-start(bf16[4,192,256]{2,1,0:T(8,128)(2,1)S(1)} %get-tuple-element.38.refs_0_), channel_id=1, source_target_pairs={{0,1},{1,0},{2,3},{3,2},{4,5},{5,4},{6,7},{7,6},{8,9},{9,8},{10,11... | collective-permute-start | bytes 1179656 | tf_op jit(solution)/shard_map/ppermute | solution.py:425
  109.5 16.1 %collective-permute-start.28 = (bf16[4,192,256]{2,1,0:T(8,128)(2,1)S(1)}, bf16[4,192,256]{2,1,0:T(8,128)(2,1)S(1)}, u32[]{:S(2)}, u32[]{:S(2)}) collective-permute-start(bf16[4,192,256]{2,1,0:T(8,128)(2,1)S(1)} %get-tuple-element.38.refs_0_), channel_id=1, source_target_pairs={{0,2},{1,3},{2,0},{3,1},{4,6},{5,7},{6,4},{7,5},{8,10},{9,11},{10,... | collective-permute-start | bytes 1179656 | tf_op jit(solution)/shard_map/ppermute | solution.py:425
  119.8 7.5 %collective-permute-start.13 = (bf16[2,384,256]{2,1,0:T(8,128)(2,1)S(1)}, bf16[2,384,256]{2,1,0:T(8,128)(2,1)S(1)}, u32[]{:S(2)}, u32[]{:S(2)}) collective-permute-start(bf16[2,384,256]{2,1,0:T(8,128)(2,1)S(1)} %stack_columns.2.refs_0_), channel_id=1, source_target_pairs={{0,1},{1,0},{2,3},{3,2},{4,5},{5,4},{6,7},{7,6},{8,9},{9,8},{10,11... | collective-permute-start | bytes 1179656 | tf_op jit(solution)/shard_map/ppermute | solution.py:425
  119.8 7.9 %collective-permute-start.8 = (bf16[256,768]{1,0:T(8,128)(2,1)S(1)}, bf16[256,768]{1,0:T(8,128)(2,1)S(1)}, u32[]{:S(2)}, u32[]{:S(2)}) collective-permute-start(bf16[256,768]{1,0:T(8,128)(2,1)S(1)} %collective-permute-done.7.refs_2_), channel_id=1, source_target_pairs={{0,1},{1,0},{2,3},{3,2},{4,5},{5,4},{6,7},{7,6},{8,9},{9,8},{10,11... | collective-permute-start | bytes 1179656 | tf_op jit(solution)/shard_map/ppermute | solution.py:425
  120.3 49.4 %collective-permute-start.23 = (bf16[1024,512]{1,0:T(8,128)(2,1)S(1)}, bf16[1024,512]{1,0:T(8,128)(2,1)S(1)}, u32[]{:S(2)}, u32[]{:S(2)}) collective-permute-start(bf16[1024,512]{1,0:T(8,128)(2,1)S(1)} %collective-permute-done.22.refs_10_), channel_id=1, source_target_pairs={{8,12},{9,13},{10,14},{11,15},{24,28},{25,29},{26,30},{27,31}} | collective-permute-start | bytes 3145736 | tf_op jit(solution)/shard_map/ppermute | solution.py:442
  121.1 48.6 %collective-permute-start.26 = (bf16[1024,512]{1,0:T(8,128)(2,1)S(1)}, bf16[1024,512]{1,0:T(8,128)(2,1)S(1)}, u32[]{:S(2)}, u32[]{:S(2)}) collective-permute-start(bf16[1024,512]{1,0:T(8,128)(2,1)S(1)} %collective-permute-done.25.refs_13_), channel_id=1, source_target_pairs={{4,0},{5,1},{6,2},{7,3},{20,16},{21,17},{22,18},{23,19}} | collective-permute-start | bytes 3145736 | tf_op jit(solution)/shard_map/ppermute | solution.py:443
  125.5 14.9 %collective-permute-start.14 = (bf16[2,384,256]{2,1,0:T(8,128)(2,1)S(1)}, bf16[2,384,256]{2,1,0:T(8,128)(2,1)S(1)}, u32[]{:S(2)}, u32[]{:S(2)}) collective-permute-start(bf16[2,384,256]{2,1,0:T(8,128)(2,1)S(1)} %stack_columns.2.refs_0_), channel_id=1, source_target_pairs={{0,2},{1,3},{2,0},{3,1},{4,6},{5,7},{6,4},{7,5},{8,10},{9,11},{10,... | collective-permute-start | bytes 1179656 | tf_op jit(solution)/shard_map/ppermute | solution.py:425
  127.3 30.8 %copy-start.4 = (bf16[4,128,512]{2,1,0:T(8,128)(2,1)S(1)}, bf16[4,128,512]{2,1,0:T(8,128)(2,1)}, u32[]{:S(2)}) copy-start(bf16[4,128,512]{2,1,0:T(8,128)(2,1)} %get-tuple-element.39.refs_4_) | copy-start | bytes 1572868
  127.3 30.8 %copy-start.5 = (s32[16,4]{0,1:T(4,128)S(1)}, s32[16,4]{0,1:T(4,128)}, u32[]{:S(2)}) copy-start(s32[16,4]{0,1:T(4,128)} %param.14) | copy-start | bytes 772
  127.3 15.1 %collective-permute-start.19 = (bf16[2,384,256]{2,1,0:T(8,128)(2,1)S(1)}, bf16[2,384,256]{2,1,0:T(8,128)(2,1)S(1)}, u32[]{:S(2)}, u32[]{:S(2)}) collective-permute-start(bf16[2,384,256]{2,1,0:T(8,128)(2,1)S(1)} %stack_columns.3.refs_4_), channel_id=1, source_target_pairs={{0,2},{1,3},{2,0},{3,1},{4,6},{5,7},{6,4},{7,5},{8,10},{9,11},{10,... | collective-permute-start | bytes 1179656 | tf_op jit(solution)/shard_map/ppermute | solution.py:425
  127.7 14.8 %collective-permute-start.29 = (bf16[4,192,256]{2,1,0:T(8,128)(2,1)S(1)}, bf16[4,192,256]{2,1,0:T(8,128)(2,1)S(1)}, u32[]{:S(2)}, u32[]{:S(2)}) collective-permute-start(bf16[4,192,256]{2,1,0:T(8,128)(2,1)S(1)} %collective-permute-done.28.refs_2_), channel_id=1, source_target_pairs={{0,1},{1,0},{2,3},{3,2},{4,5},{5,4},{6,7},{7,6},{8,9},{9,8},{10,11... | collective-permute-start | bytes 1179656 | tf_op jit(solution)/shard_map/ppermute | solution.py:425
  127.7 4.6 %copy-start.1 = (bf16[8,1536,512]{2,1,0:T(8,128)(2,1)S(1)}, bf16[8,1536,512]{2,1,0:T(8,128)(2,1)}, u32[]{:S(2)}) copy-start(bf16[8,1536,512]{2,1,0:T(8,128)(2,1)} %refs_5_.1) | copy-start | bytes 37748740
  140.3 27.9 %copy-start.8 = (s32[128,8]{0,1:T(8,128)S(1)}, s32[128,8]{0,1:T(8,128)}, u32[]{:S(2)}) copy-start(s32[128,8]{0,1:T(8,128)} %param.12) | copy-start | bytes 12292
  140.3 27.9 %copy-start.9 = (s32[128,8]{0,1:T(8,128)S(1)}, s32[128,8]{0,1:T(8,128)}, u32[]{:S(2)}) copy-start(s32[128,8]{0,1:T(8,128)} %param.13) | copy-start | bytes 12292
  140.3 29.4 %copy-start.2 = (bf16[8,4,32,512]{3,2,1,0:T(8,128)(2,1)S(1)}, bf16[8,4,32,512]{3,2,1,0:T(8,128)(2,1)}, u32[]{:S(2)}) copy-start(bf16[8,4,32,512]{3,2,1,0:T(8,128)(2,1)} %param.16) | copy-start | bytes 3145732
  140.4 17.1 %collective-permute-start.9 = (bf16[144,512]{1,0:T(8,128)(2,1)S(1)}, bf16[144,512]{1,0:T(8,128)(2,1)S(1)}, u32[]{:S(2)}, u32[]{:S(2)}) collective-permute-start(bf16[144,512]{1,0:T(8,128)(2,1)S(1)} %get-tuple-element.42), channel_id=1, source_target_pairs={{0,4},{4,0},{8,12},{12,8},{1,5},{5,1},{9,13},{13,9},{2,6},{6,2},{1... | collective-permute-start | bytes 442376 | tf_op jit(solution)/shard_map/ppermute | solution.py:425
  142.4 15.1 %collective-permute-start.10 = (bf16[144,512]{1,0:T(8,128)(2,1)S(1)}, bf16[144,512]{1,0:T(8,128)(2,1)S(1)}, u32[]{:S(2)}, u32[]{:S(2)}) collective-permute-start(bf16[144,512]{1,0:T(8,128)(2,1)S(1)} %get-tuple-element.41), channel_id=1, source_target_pairs={{0,8},{4,12},{8,0},{12,4},{1,9},{5,13},{9,1},{13,5},{2,10},{6,14},... | collective-permute-start | bytes 442376 | tf_op jit(solution)/shard_map/ppermute | solution.py:425
  142.4 15.6 %collective-permute-start.11 = (bf16[144,512]{1,0:T(8,128)(2,1)S(1)}, bf16[144,512]{1,0:T(8,128)(2,1)S(1)}, u32[]{:S(2)}, u32[]{:S(2)}) collective-permute-start(bf16[144,512]{1,0:T(8,128)(2,1)S(1)} %get-tuple-element.40), channel_id=1, source_target_pairs={{0,12},{4,8},{8,4},{12,0},{1,13},{5,9},{9,5},{13,1},{2,14},{6,10},... | collective-permute-start | bytes 442376 | tf_op jit(solution)/shard_map/ppermute | solution.py:425
  157.5 12.2 %collective-permute-start.18 = (bf16[2,384,256]{2,1,0:T(8,128)(2,1)S(1)}, bf16[2,384,256]{2,1,0:T(8,128)(2,1)S(1)}, u32[]{:S(2)}, u32[]{:S(2)}) collective-permute-start(bf16[2,384,256]{2,1,0:T(8,128)(2,1)S(1)} %stack_columns.3.refs_4_), channel_id=1, source_target_pairs={{0,1},{1,0},{2,3},{3,2},{4,5},{5,4},{6,7},{7,6},{8,9},{9,8},{10,11... | collective-permute-start | bytes 1179656 | tf_op jit(solution)/shard_map/ppermute | solution.py:425
  157.5 12.2 %collective-permute-start.15 = (bf16[2,384,256]{2,1,0:T(8,128)(2,1)S(1)}, bf16[2,384,256]{2,1,0:T(8,128)(2,1)S(1)}, u32[]{:S(2)}, u32[]{:S(2)}) collective-permute-start(bf16[2,384,256]{2,1,0:T(8,128)(2,1)S(1)} %collective-permute-done.14.refs_2_), channel_id=1, source_target_pairs={{0,1},{1,0},{2,3},{3,2},{4,5},{5,4},{6,7},{7,6},{8,9},{9,8},{10,11... | collective-permute-start | bytes 1179656 | tf_op jit(solution)/shard_map/ppermute | solution.py:425
  158.0 11.6 %collective-permute-start.20 = (bf16[2,384,256]{2,1,0:T(8,128)(2,1)S(1)}, bf16[2,384,256]{2,1,0:T(8,128)(2,1)S(1)}, u32[]{:S(2)}, u32[]{:S(2)}) collective-permute-start(bf16[2,384,256]{2,1,0:T(8,128)(2,1)S(1)} %collective-permute-done.19.refs_6_), channel_id=1, source_target_pairs={{0,1},{1,0},{2,3},{3,2},{4,5},{5,4},{6,7},{7,6},{8,9},{9,8},{10,11... | collective-permute-start | bytes 1179656 | tf_op jit(solution)/shard_map/ppermute | solution.py:425

commit v5 on v4

--- a/solution.py
+++ b/solution.py
@@ -66,9 +66,6 @@
         self.cols = self.in_cols + self.down_cols
         self.folds = self.width // self.tokens
         self.tail = 2 * self.slots // self.folds
-        self.side_folds = self.width // self.part
-        self.side_rows = self.down_cols // self.side_folds
-        self.side_start = self.tokens + self.tail
 
 
 def slot_table(z, table_ref, r):
@@ -83,9 +80,7 @@
     return key == ids
 
 
-def route_kernel(z, ids_ref, count_ref, *refs):
-    grad_ref, weight_ref, routes_ref, replica_ref, table_ref, pair_ref = refs[:6]
-    outs, sides = refs[6:-1], refs[-1]
+def route_kernel(z, count_ref, grad_ref, weight_ref, routes_ref, replica_ref, table_ref, out_ref):
     weights = weight_ref[...].astype(F32)
     hits = jnp.zeros((z.slots, z.tokens), F32)
     loads = jnp.zeros((z.slots, z.tokens), F32)
@@ -104,21 +99,23 @@
     earlier = nn(hits.astype(BF), (before < after).astype(F32).astype(BF))
     code = jnp.where(hits > 0.5, earlier, -1.0)
     both = jnp.concatenate([code, loads], axis=0).astype(BF)
+    out_ref[: z.tokens, :] = grad_ref[...]
+    for b in range(z.folds):
+        out_ref[z.tokens :, b * z.tokens : (b + 1) * z.tokens] = both[
+            b * z.tail : (b + 1) * z.tail, :
+        ]
+
+
+def hidden_kernel(z, ids_ref, pair_ref, after_ref, *refs):
+    outs, sides = refs[:-1], refs[-1]
     pair = pair_ref[...]
-    gate = pair[:, : z.hidden].astype(F32)
+    gate_pre = pair[:, : z.hidden].astype(F32)
     up = pair[:, z.hidden :].astype(F32)
-    hidden = (gate * (1.0 / (1.0 + jnp.exp(-gate))) * up).astype(BF).T
+    hidden = (gate_pre * (1.0 / (1.0 + jnp.exp(-gate_pre))) * up).astype(BF).T
     for q in range(z.ep):
-        for f in range(z.side_folds):
-            lo = q * z.down_cols + f * z.side_rows
-            sides[q, :, f * z.part : (f + 1) * z.part] = hidden[lo : lo + z.side_rows, :]
+        sides[q] = hidden[q * z.down_cols : (q + 1) * z.down_cols, :]
     for k in range(z.ep):
-        outs[k][: z.tokens, :] = grad_ref[...]
-        for b in range(z.folds):
-            outs[k][z.tokens : z.side_start, b * z.tokens : (b + 1) * z.tokens] = both[
-                b * z.tail : (b + 1) * z.tail, :
-            ]
-        outs[k][z.side_start :, :] = sides[ids_ref[0] ^ k]
+        outs[k][...] = sides[ids_ref[0] ^ k]
 
 
 def block_place(z, block):
@@ -140,14 +137,6 @@
         load = codes_ref[first + a, pl.ds(z.slots + slot, 1), :]
         parts.append(jnp.sum(jnp.where(pick, load, 0.0), axis=1, keepdims=True))
     return jnp.concatenate(parts, axis=0)
-
-
-def scaled_rows(z, codes_ref, grads_ref, slot, first):
-    parts = []
-    for a, pick in block_picks(z, codes_ref, slot, first):
-        load = codes_ref[first + a, pl.ds(z.slots + slot, 1), :]
-        parts.append(nn(jnp.where(pick, load, 0.0).astype(BF), grads_ref[first + a]))
-    return jnp.concatenate(parts, axis=0).astype(BF)
 
 
 def local_picks(z, codes_ref, source, me):
@@ -183,7 +172,7 @@
             grads_ref[source] = bufs[k][: z.tokens, :]
             for b in range(z.folds):
                 codes_ref[source, b * z.tail : (b + 1) * z.tail, :] = bufs[k][
-                    z.tokens : z.side_start, b * z.tokens : (b + 1) * z.tokens
+                    z.tokens :, b * z.tokens : (b + 1) * z.tokens
                 ].astype(F32)
         for p in range(z.ep):
             rows = nn(local_picks(z, codes_ref, p, me), grads_ref[p]).astype(BF)
@@ -222,17 +211,14 @@
 def pre_kernel(z, ids_ref, *refs):
     parts = refs[: z.sub]
     pair_ref, codes_ref = refs[z.sub : z.sub + 2]
-    bufs, refs = refs[z.sub + 2 : z.sub + 2 + z.ep], refs[z.sub + 2 + z.ep :]
+    downs, refs = refs[z.sub + 2 : z.sub + 2 + z.ep], refs[z.sub + 2 + z.ep :]
     outs = refs[: z.ep]
     grad_ref, down_ref, sides = refs[z.ep :]
 
     @pl.when(pl.program_id(0) == 0)
     def _():
         for k in range(z.ep):
-            for f in range(z.side_folds):
-                down_ref[k, f * z.side_rows : (f + 1) * z.side_rows, :] = bufs[k][
-                    z.side_start :, f * z.part : (f + 1) * z.part
-                ]
+            down_ref[k] = downs[k][...]
 
     me = ids_ref[0]
     block = ids_ref[1] * z.part_blocks + pl.program_id(0)
@@ -257,7 +243,8 @@
 
 def row_kernel(z, ids_ref, *refs):
     grads = refs[: z.sub]
-    pair_ref, weight_ref, codes_ref, out_ref, rows_ref, marks, held, weights, sems = refs[z.sub :]
+    pair_ref, weight_ref, codes_ref = refs[z.sub : z.sub + 3]
+    out_ref, rows_ref, marks, held, weights, sems = refs[-6:]
     me, mine = ids_ref[0], ids_ref[1]
     step = pl.program_id(0)
     place = step // z.part_blocks
@@ -356,45 +343,43 @@
 
 def expert_products(z, ids_ref, table_ref, held, right_rows, out_ref):
     me, mine = ids_ref[0], ids_ref[1]
-
-    def one(i, carry):
+    for i in range(PER):
         expert = pl.program_id(0) * PER + i
-        slot_ids = [table_ref[r, expert] for r in range(z.reps)]
-        count = 1
-        for r in range(1, z.reps):
-            count = count + (slot_ids[r] != slot_ids[0]).astype(jnp.int32)
-        for c in range(1, z.reps + 1):
-
-            @pl.when(count == c)
-            def _():
-                left, right = [], []
-                for slot_id in slot_ids[:c]:
-                    source = slot_id // z.local
-                    for b in range(z.slot_blocks):
-                        block = (slot_id % z.local) * z.slot_blocks + b
-                        part = (block // z.part_blocks) ^ mine
-                        spot = pl.multiple_of((block % z.part_blocks) * z.block, z.block)
-                        left.append(held[part, source ^ me, :, pl.ds(spot, z.block)])
-                        right.append(right_rows(slot_id, b))
-                left = jnp.concatenate(left, axis=1)
-                out_ref[i] = nn(left, jnp.concatenate(right, axis=0)).astype(BF)
-
-        return carry
-
-    lax.fori_loop(0, PER, one, 0)
+        first = table_ref[0, expert]
+        left, right = [], []
+        for r in range(z.reps):
+            slot_id = table_ref[r, expert]
+            source = slot_id // z.local
+            for b in range(z.slot_blocks):
+                block = (slot_id % z.local) * z.slot_blocks + b
+                part = (block // z.part_blocks) ^ mine
+                spot = pl.multiple_of((block % z.part_blocks) * z.block, z.block)
+                side = jnp.where(slot_id == first, z.ep, source ^ me) if r else source ^ me
+                left.append(held[part, side, :, pl.ds(spot, z.block)])
+                right.append(right_rows(slot_id, block, b))
+        left = jnp.concatenate(left, axis=1)
+        out_ref[i] = nn(left, jnp.concatenate(right, axis=0)).astype(BF)
 
 
 def total_down_kernel(z, ids_ref, table_ref, *refs):
     sides = refs[: z.sub]
-    grads_ref, codes_ref, out_ref, held, sems = refs[z.sub :]
+    grads_ref, codes_ref, out_ref, held, scaled, sems = refs[z.sub :]
 
     @pl.when(pl.program_id(0) == 0)
     def _():
         side_moves(z, 1, sides, held, sems, lambda copy: copy.start())
+        held[:, z.ep] = jnp.zeros_like(held[:, z.ep])
+        rows = lax.broadcasted_iota(jnp.int32, (z.slots, z.cap, z.tokens), 1).astype(F32)
+        for p in range(z.ep):
+            code = codes_ref[p, : z.slots, :][:, None, :]
+            load = codes_ref[p, z.slots :, :][:, None, :]
+            pick = jnp.where(rows == code, load, 0.0).reshape(z.slots * z.cap, z.tokens)
+            made = nn(pick.astype(BF), grads_ref[p]).astype(BF)
+            scaled[:, p * z.cap : (p + 1) * z.cap, :] = made.reshape(z.slots, z.cap, z.width)
         side_moves(z, 1, sides, held, sems, lambda copy: copy.wait())
 
-    def right_rows(slot_id, b):
-        return scaled_rows(z, codes_ref, grads_ref, slot_id, b * z.sources)
+    def right_rows(slot_id, block, b):
+        return scaled[slot_id, b * z.block : (b + 1) * z.block, :]
 
     expert_products(z, ids_ref, table_ref, held, right_rows, out_ref)
 
@@ -411,10 +396,10 @@
             input_moves(z, ids_ref[0], own_ref, rights, lefts, inputs_ref, *other_sems, act)
 
         moves(lambda copy: copy.start())
+        held[:, z.ep] = jnp.zeros_like(held[:, z.ep])
         moves(lambda copy: copy.wait())
 
-    def right_rows(slot_id, b):
-        block = (slot_id % z.local) * z.slot_blocks + b
+    def right_rows(slot_id, block, b):
         start = pl.multiple_of(block * z.block, z.block)
         return inputs_ref[slot_id // z.local, pl.ds(start, z.block), :]
 
@@ -435,15 +420,26 @@
     return [have[k] for k in range(size)]
 
 
-def chain_gather(x, axis, size):
-    rights, lefts = [], []
-    go, back = x, x
-    for d in range(1, size):
-        go = lax.ppermute(go, axis, [(i, i + 1) for i in range(d - 1, size - 1)])
-        back = lax.ppermute(back, axis, [(i, i - 1) for i in range(size - d, 0, -1)])
-        rights.append(go)
-        lefts.append(back)
-    return [x] + rights + lefts
+def nothing(*refs):
+    pass
+
+
+def gate(values, after):
+    anywhere = pl.BlockSpec(memory_space=pl.ANY)
+    return pl.pallas_call(
+        nothing,
+        in_specs=[anywhere] * (len(values) + len(after)),
+        out_specs=[anywhere] * len(values),
+        out_shape=[jax.ShapeDtypeStruct(v.shape, v.dtype) for v in values],
+        input_output_aliases={i: i for i in range(len(values))},
+        name="gate",
+    )(*values, *after)
+
+
+def chain_step(go, back, axis, size, d):
+    go = lax.ppermute(go, axis, [(i, i + 1) for i in range(d - 1, size - 1)])
+    back = lax.ppermute(back, axis, [(i, i - 1) for i in range(size - d, 0, -1)])
+    return go, back
 
 
 def body(
@@ -464,28 +460,39 @@
     routes, replica, table = routes.T, replica.T, replica_slot.T
     route_weight = route_weight.T
     pair_rows = saved_gate_up.reshape(z.all_rows, z.pair)
-    grad_shape = (z.side_start + z.side_rows, z.width)
+    grad_shape = (z.tokens + z.tail, z.width)
     code_shape = (n, 2 * z.slots, z.tokens)
     inputs = saved_input.reshape(z.all_rows, z.width)
-    gathered = chain_gather(inputs, "ep", n)
 
     routing = (grad_out, route_weight, routes, replica, table)
-    bufs = pl.pallas_call(
+    buf = pl.pallas_call(
         functools.partial(route_kernel, z),
+        out_shape=jax.ShapeDtypeStruct(grad_shape, BF),
+        in_specs=[smem()] + [whole(a.shape) for a in routing],
+        out_specs=whole(grad_shape),
+        grid=(1,),
+        compiler_params=params(60),
+        name="route",
+    )(token_count, *routing)
+    bufs = [buf] + [swap(buf, "ep", n, k) for k in range(1, n)]
+
+    downs = pl.pallas_call(
+        functools.partial(hidden_kernel, z),
         grid_spec=pltpu.PrefetchScalarGridSpec(
             num_scalar_prefetch=1,
-            grid=(1,),
-            in_specs=[smem()]
-            + [whole(a.shape) for a in routing]
-            + [pl.BlockSpec((z.part, z.pair), lambda i, r: (r[1], 0))],
-            out_specs=[whole(grad_shape)] * n,
-            scratch_shapes=[pltpu.VMEM((n, z.side_rows, z.width), BF)],
+            grid=(z.part_blocks,),
+            in_specs=[
+                pl.BlockSpec((z.block, z.pair), lambda i, r: (r[1] * z.part_blocks + i, 0)),
+                pl.BlockSpec(memory_space=pl.ANY),
+            ],
+            out_specs=[pl.BlockSpec((z.down_cols, z.block), lambda i, r: (0, i))] * n,
+            scratch_shapes=[pltpu.VMEM((n, z.down_cols, z.block), BF)],
         ),
-        out_shape=[jax.ShapeDtypeStruct(grad_shape, BF)] * n,
-        compiler_params=params(60),
-        name="route",
-    )(ids, token_count, *routing, pair_rows)
-    bufs = [bufs[0]] + [swap(bufs[k], "ep", n, k) for k in range(1, n)]
+        out_shape=[jax.ShapeDtypeStruct((z.down_cols, z.part), BF)] * n,
+        compiler_params=params(16),
+        name="hidden_columns",
+    )(ids, pair_rows, bufs[1])
+    downs = [downs[0]] + [swap(downs[k], "ep", n, k) for k in range(1, n)]
 
     def stack(pieces):
         shape = pieces[0].shape
@@ -522,10 +529,12 @@
             jax.ShapeDtypeStruct((n, z.tokens, z.width), BF),
             jax.ShapeDtypeStruct(code_shape, F32),
         ],
-        compiler_params=params(52),
+        compiler_params=params(48),
         name="hidden_partials",
     )(ids, *bufs, weight_down)
     parts, (grads_all, codes) = outs[:m], outs[m:]
+    chain = gate([inputs], downs[1:] + [codes])
+    steps = [chain_step(chain[0], chain[0], "ep", n, 1)]
     parts = [parts[0]] + [swap(parts[k], "sub", m, k) for k in range(1, m)]
 
     outs = pl.pallas_call(
@@ -538,7 +547,7 @@
                 pl.BlockSpec((z.block, z.pair), lambda i, r: (r[1] * z.part_blocks + i, 0)),
                 whole(code_shape),
             ]
-            + [whole(grad_shape)] * n,
+            + [whole((z.down_cols, z.part))] * n,
             out_specs=[pl.BlockSpec((z.in_cols, z.block), lambda i, r: (0, i))] * n
             + [
                 pl.BlockSpec((z.block, z.hidden), lambda i, r: (i, 0)),
@@ -553,10 +562,14 @@
         ],
         compiler_params=params(16),
         name="pre_grads",
-    )(ids, *parts, pair_rows, codes, *bufs)
+    )(ids, *parts, pair_rows, codes, *downs)
     pieces, grad_part = outs[:n], outs[n]
     pieces = [pieces[0]] + [swap(pieces[k], "ep", n, k) for k in range(1, n)]
     grad_parts = spread_over(grad_part, "sub", m)
+    steps[0] = gate(steps[0], pieces[1:])
+    for d in range(2, n):
+        steps.append(chain_step(*steps[-1], "ep", n, d))
+    gathered = [inputs] + [go for go, _ in steps] + [back for _, back in steps]
     down_sides = spread_over(outs[n + 1], "sub", m)
     size = n // GROUPS
     sides = []
@@ -575,7 +588,8 @@
                 pl.BlockSpec((z.block, z.pair), lambda i, r: (row_block(i, r), 0)),
                 pl.BlockSpec(memory_space=pltpu.HBM),
                 whole(code_shape),
-            ],
+            ]
+            + [pl.BlockSpec(memory_space=pl.ANY)] * (m - 1),
             out_specs=whole(back_shape),
             scratch_shapes=[
                 pltpu.VMEM((z.local, z.rows, z.width), BF),
@@ -586,9 +600,9 @@
             ],
         ),
         out_shape=jax.ShapeDtypeStruct(back_shape, BF),
-        compiler_params=params(32),
+        compiler_params=params(46),
         name="row_grads",
-    )(ids, *grad_parts, pair_rows, weight_in, codes)
+    )(ids, *grad_parts, pair_rows, weight_in, codes, *sides[1 - m :])
     got = [back[0]] + [swap(back[k], "ep", n, k) for k in range(1, n)]
 
     grad_tokens, grad_routes = pl.pallas_call(
@@ -615,7 +629,7 @@
                 grid=(z.experts // PER,),
                 in_specs=specs,
                 out_specs=pl.BlockSpec((PER, cols, z.width), lambda e, r, t: (e, 0, 0)),
-                scratch_shapes=[pltpu.VMEM((m, n, cols, z.part), BF)] + scratch,
+                scratch_shapes=[pltpu.VMEM((m, n + 1, cols, z.part), BF)] + scratch,
             ),
             out_shape=jax.ShapeDtypeStruct((z.experts, cols, z.width), BF),
             compiler_params=params(32),
@@ -629,7 +643,7 @@
         [*down_sides, grads_all, codes],
         [anywhere] * m + [whole((n, z.tokens, z.width)), whole(code_shape)],
         z.down_cols,
-        [pltpu.SemaphoreType.DMA((m,))],
+        [pltpu.VMEM((z.slots, z.rows, z.width), BF), pltpu.SemaphoreType.DMA((m,))],
         "down_grads",
     )
     grad_in = total_call(

time: 181 us -> 190 us (1.050)
  waiting for transfers between devices: 94.3 us -> 78.3 us
  local copies, waits for them, and re-layouts: 6.19 us -> 20.8 us
  starting transfers between devices: 35.9 us -> 49 us
    ppermute x24 -> x27, waiting for transfers between devices: 94.3 us -> 78.2 us  [swap(): return lax.ppermute(x, axis, [(i, i ^ bit) for i in range(size)])]
    unnamed x20 -> x71, local copies, waits for them, and re-layouts: 6.15 us -> 20.8 us
    ppermute x24 -> x27, starting transfers between devices: 24.4 us -> 34.2 us  [swap(): return lax.ppermute(x, axis, [(i, i ^ bit) for i in range(size)])]
    ppermute x6, starting transfers between devices: 11.5 us -> 14.7 us  [the longest x3 10.9 us: chain_step(): go = lax.ppermute(go, axis, [(i, i + 1) for i in range(d - 1, size - 1)])]
    pallas_call x2, Pallas kernels: 20.6 us -> 17.9 us  [total_call(): pl.pallas_call(functools.partial(kernel, z), grid_spec=pltpu.PrefetchScal...]
  transfers between devices with their start and end apart: 30 -> 33, of which waited for: 10 -> 11; matrix products, arithmetic and copies ran while one was open for 0% -> 1% of each run, Pallas kernels for 17% -> 15%
where the time goes in v5:
time: 190 us
  waiting for transfers between devices  78.3 us (41%)
  starting transfers between devices  49 us (26%)
  Pallas kernels  39.8 us (21%)
  local copies, waits for them, and re-layouts  20.8 us (11%)
    ppermute x27, waiting for transfers between devices, swap(): return lax.ppermute(x, axis, [(i, i ^ bit) for i in range(size)])  78.2 us
    ppermute x27, starting transfers between devices, swap(): return lax.ppermute(x, axis, [(i, i ^ bit) for i in range(size)])  34.2 us
    unnamed x71, local copies, waits for them, and re-layouts  20.8 us
    pallas_call x2, Pallas kernels, total_call(): pl.pallas_call(functools.partial(kernel, z), grid_spec=pltpu.PrefetchScal...  17.9 us
    ppermute x3, starting transfers between devices, chain_step(): go = lax.ppermute(go, axis, [(i, i + 1) for i in range(d - 1, size - 1)])  10.9 us
    pallas_call x1, Pallas kernels, body(): pl.pallas_call(functools.partial(row_kernel, z), grid_spec=pltpu.Prefetch...  8.24 us
    pallas_call x1, Pallas kernels, body(): pl.pallas_call(functools.partial(down_kernel, z), grid_spec=pltpu.Prefetc...  6.47 us
    ppermute x3, starting transfers between devices, chain_step(): lax.ppermute(back, axis, [(i, i - 1) for i in range(size - d, 0, -1)])  3.85 us
  transfers between devices with their start and end apart: 33, of which 11 were waited for; matrix products, arithmetic and copies ran while one was open for 1% of the time, Pallas kernels for 15%

profile of v5, /device:TPU:0, one launch (start us, length us, event | category | flops | bytes accessed | tf_op | source)
XLA Modules:
  0.0 189.6 jit_solution(11148042396561951816)
XLA Ops:
  1.3 1.9 route.1.refs_0_
  3.2 3.0 %collective-permute-start = (bf16[144,512]{1,0:T(8,128)(2,1)}, bf16[144,512]{1,0:T(8,128)(2,1)S(1)}, u32[]{:S(2)}, u32[]{:S(2)}) collective-permute-start(bf16[144,512]{1,0:T(8,128)(2,1)} %route.1.refs_0_), channel_id=1, source_target_pairs={{0,4},{4,0},{8,12},{12,8},{1,5},{5,1},{9,13},{13,9},{2,6},{6,2},{1... | collective-permute-start | bytes 442376 | tf_op jit(solution)/shard_map/ppermute | solution.py:410
  6.2 2.6 %collective-permute-start.1 = (bf16[144,512]{1,0:T(8,128)(2,1)}, bf16[144,512]{1,0:T(8,128)(2,1)}, u32[]{:S(2)}, u32[]{:S(2)}) collective-permute-start(bf16[144,512]{1,0:T(8,128)(2,1)} %route.1.refs_0_), channel_id=1, source_target_pairs={{0,8},{4,12},{8,0},{12,4},{1,9},{5,13},{9,1},{13,5},{2,10},{6,14},... | collective-permute-start | bytes 442376 | tf_op jit(solution)/shard_map/ppermute | solution.py:410
  8.9 3.4 %collective-permute-done.refs_1_.after_ref = bf16[144,512]{1,0:T(8,128)(2,1)S(1)} collective-permute-done((bf16[144,512]{1,0:T(8,128)(2,1)}, bf16[144,512]{1,0:T(8,128)(2,1)S(1)}, u32[]{:S(2)}, u32[]{:S(2)}) %collective-permute-start) | collective-permute-done | bytes 147488 | tf_op jit(solution)/shard_map/ppermute | solution.py:410
  12.3 1.9 copy-done
  14.1 1.1 hidden_columns.1
  15.9 3.7 %collective-permute-start.7 = (bf16[192,256]{1,0:T(8,128)(2,1)S(1)}, bf16[192,256]{1,0:T(8,128)(2,1)S(1)}, u32[]{:S(2)}, u32[]{:S(2)}) collective-permute-start(bf16[192,256]{1,0:T(8,128)(2,1)S(1)} %get-tuple-element.31), channel_id=1, source_target_pairs={{0,8},{4,12},{8,0},{12,4},{1,9},{5,13},{9,1},{13,5},{2,10},{6,14},... | collective-permute-start | bytes 294920 | tf_op jit(solution)/shard_map/ppermute | solution.py:410
  19.7 2.3 %copy.17.refs_0_ = bf16[1024,512]{1,0:T(8,128)(2,1)} copy(bf16[1024,512]{1,0:T(8,128)(2,1)} %bitcast.20) | data formatting | bytes 2097152
  22.0 0.9 copy-done.12
  22.9 6.5 %hidden_partials.1 = (bf16[256,768]{1,0:T(8,128)(2,1)S(1)}, bf16[256,768]{1,0:T(8,128)(2,1)S(1)}, bf16[256,768]{1,0:T(8,128)(2,1)S(1)}, bf16[256,768]{1,0:T(8,12...) custom-call(s32[2]{0:T(128)S(1)} %pad_add_fusion.ids_ref, bf16[144,512]{1,0:T(8,128)(2,1)S(1)} %copy-done.12, ...), custom_call_target="tpu_custom_call" | custom-call | tf_op jit(solution)/shard_map/hidden_partials/pallas_call | solution.py:513
  30.0 0.8 copy-done.13
  34.5 9.4 %collective-permute-start.24 = (bf16[1024,512]{1,0:T(8,128)(2,1)}, bf16[1024,512]{1,0:T(8,128)(2,1)}, u32[]{:S(2)}, u32[]{:S(2)}) collective-permute-start(bf16[1024,512]{1,0:T(8,128)(2,1)} %gate.2), channel_id=1, source_target_pairs={{0,4},{4,8},{8,12},{1,5},{5,9},{9,13},{2,6},{6,10},{10,14},{3,7},{... | collective-permute-start | bytes 3145736 | tf_op jit(solution)/shard_map/ppermute | solution.py:440
  43.9 1.3 collective-permute-start.25
  45.3 2.5 %collective-permute-start.4 = (bf16[256,768]{1,0:T(8,128)(2,1)}, bf16[256,768]{1,0:T(8,128)(2,1)S(1)}, u32[]{:S(2)}, u32[]{:S(2)}) collective-permute-start(bf16[256,768]{1,0:T(8,128)(2,1)} %copy-done.33), channel_id=1, source_target_pairs={{0,2},{1,3},{2,0},{3,1},{4,6},{5,7},{6,4},{7,5},{8,10},{9,11},{10,... | collective-permute-start | bytes 1179656 | tf_op jit(solution)/shard_map/ppermute | solution.py:410
  47.9 10.1 %collective-permute-done.4.refs_2_ = bf16[256,768]{1,0:T(8,128)(2,1)S(1)} collective-permute-done((bf16[256,768]{1,0:T(8,128)(2,1)}, bf16[256,768]{1,0:T(8,128)(2,1)S(1)}, u32[]{:S(2)}, u32[]{:S(2)}) %collective-permute-start.4) | collective-permute-done | bytes 393248 | tf_op jit(solution)/shard_map/ppermute | solution.py:410
  58.0 7.9 %collective-permute-done.5.refs_3_ = bf16[256,768]{1,0:T(8,128)(2,1)S(1)} collective-permute-done((bf16[256,768]{1,0:T(8,128)(2,1)}, bf16[256,768]{1,0:T(8,128)(2,1)S(1)}, u32[]{:S(2)}, u32[]{:S(2)}) %collective-permute-start.5) | collective-permute-done | bytes 393248 | tf_op jit(solution)/shard_map/ppermute | solution.py:410
  65.9 0.9 copy-done.4
  66.8 0.9 copy-done.18
  67.7 0.9 copy-done.20
  68.6 1.0 copy-done.24
  69.6 0.9 copy-done.28
  70.4 2.7 %pre_grads.1 = (bf16[384,256]{1,0:T(8,128)(2,1)S(1)}, bf16[384,256]{1,0:T(8,128)(2,1)S(1)}, bf16[384,256]{1,0:T(8,128)(2,1)S(1)}, bf16[384,256]{1,0:T(8,128)(2,1...) custom-call(s32[2]{0:T(128)S(1)} %pad_add_fusion.ids_ref, bf16[256,768]{1,0:T(8,128)(2,1)S(1)} %copy-done.24, ...), custom_call_target="tpu_custom_call" | custom-call | tf_op jit(solution)/shard_map/pre_grads/pallas_call | solution.py:540
  73.8 2.4 %collective-permute-start.12 = (bf16[384,256]{1,0:T(8,128)(2,1)S(1)}, bf16[384,256]{1,0:T(8,128)(2,1)S(1)}, u32[]{:S(2)}, u32[]{:S(2)}) collective-permute-start(bf16[384,256]{1,0:T(8,128)(2,1)S(1)} %get-tuple-element.34), channel_id=1, source_target_pairs={{0,8},{4,12},{8,0},{12,4},{1,9},{5,13},{9,1},{13,5},{2,10},{6,14},... | collective-permute-start | bytes 589832 | tf_op jit(solution)/shard_map/ppermute | solution.py:410
  76.2 2.6 %collective-permute-start.13 = (bf16[384,256]{1,0:T(8,128)(2,1)S(1)}, bf16[384,256]{1,0:T(8,128)(2,1)S(1)}, u32[]{:S(2)}, u32[]{:S(2)}) collective-permute-start(bf16[384,256]{1,0:T(8,128)(2,1)S(1)} %get-tuple-element.35), channel_id=1, source_target_pairs={{0,12},{4,8},{8,4},{12,0},{1,13},{5,9},{9,5},{13,1},{2,14},{6,10},... | collective-permute-start | bytes 589832 | tf_op jit(solution)/shard_map/ppermute | solution.py:410
  78.8 12.1 %collective-permute-done.12.refs_0_.refs_3_ = bf16[384,256]{1,0:T(8,128)(2,1)S(1)} collective-permute-done((bf16[384,256]{1,0:T(8,128)(2,1)S(1)}, bf16[384,256]{1,0:T(8,128)(2,1)S(1)}, u32[]{:S(2)}, u32[]{:S(2)}) %collective-permute-start.12) | collective-permute-done | bytes 196640 | tf_op jit(solution)/shard_map/ppermute | solution.py:410
  90.9 0.9 collective-permute-done.20.refs_1_.refs_2_
  93.2 1.3 collective-permute-start.28
  94.6 1.9 collective-permute-start.10
  96.7 0.9 copy-done.9
  97.6 0.9 copy-done.11
  98.6 1.9 collective-permute-start.15
  100.4 6.3 %collective-permute-done.10.refs_2_ = bf16[256,768]{1,0:T(8,128)(2,1)S(1)} collective-permute-done((bf16[256,768]{1,0:T(8,128)(2,1)}, bf16[256,768]{1,0:T(8,128)(2,1)S(1)}, u32[]{:S(2)}, u32[]{:S(2)}) %collective-permute-start.10) | collective-permute-done | bytes 393248 | tf_op jit(solution)/shard_map/ppermute | solution.py:410
  106.8 8.4 %collective-permute-done.31.refs_2_ = bf16[4,192,256]{2,1,0:T(8,128)(2,1)S(1)} collective-permute-done((bf16[4,192,256]{2,1,0:T(8,128)(2,1)}, bf16[4,192,256]{2,1,0:T(8,128)(2,1)S(1)}, u32[]{:S(2)}, u32[]{:S(2)}) %collective-permute-start.31) | collective-permute-done | bytes 393248 | tf_op jit(solution)/shard_map/ppermute | solution.py:410
  115.2 8.0 %collective-permute-done.15.refs_8_.refs_6_ = bf16[2,384,256]{2,1,0:T(8,128)(2,1)S(1)} collective-permute-done((bf16[2,384,256]{2,1,0:T(8,128)(2,1)S(1)}, bf16[2,384,256]{2,1,0:T(8,128)(2,1)S(1)}, u32[]{:S(2)}, u32[]{:S(2)}) %collective-permute-start.15) | collective-permute-done | bytes 393248 | tf_op jit(solution)/shard_map/ppermute | solution.py:410
  124.0 1.3 collective-permute-start.29
  125.8 0.9 copy-done.7
  126.8 0.9 copy-done.26
  127.8 1.8 collective-permute-start.22
  129.6 1.0 copy-done.22
  130.6 8.2 %row_grads.1 = bf16[4,144,512]{2,1,0:T(8,128)(2,1)S(1)} custom-call(s32[2]{0:T(128)S(1)} %pad_add_fusion.ids_ref, bf16[256,768]{1,0:T(8,128)(2,1)S(1)} %copy-done.22, bf16[256,768]{1,0:T(8,128)(2,1)S(1)} %collective-permute-done.9.refs_1_, bf16[256,768]{1,0:T(8,128)(2,1)S(1)} %collective-permute-done.10.refs_2_, ...), custom_call_target="tpu_custom_call" | custom-call | tf_op jit(solution)/shard_map/row_grads/pallas_call | solution.py:581
  138.9 7.0 %collective-permute-start.17 = (bf16[144,512]{1,0:T(8,128)(2,1)S(1)}, bf16[144,512]{1,0:T(8,128)(2,1)S(1)}, u32[]{:S(2)}, u32[]{:S(2)}) collective-permute-start(bf16[144,512]{1,0:T(8,128)(2,1)S(1)} %get-tuple-element.46), channel_id=1, source_target_pairs={{0,4},{4,0},{8,12},{12,8},{1,5},{5,1},{9,13},{13,9},{2,6},{6,2},{1... | collective-permute-start | bytes 442376 | tf_op jit(solution)/shard_map/ppermute | solution.py:410
  145.9 1.2 collective-permute-start.21
  147.2 12.0 %collective-permute-done.17.refs_1_ = bf16[144,512]{1,0:T(8,128)(2,1)S(1)} collective-permute-done((bf16[144,512]{1,0:T(8,128)(2,1)S(1)}, bf16[144,512]{1,0:T(8,128)(2,1)S(1)}, u32[]{:S(2)}, u32[]{:S(2)}) %collective-permute-start.17) | collective-permute-done | bytes 147488 | tf_op jit(solution)/shard_map/ppermute | solution.py:410
  159.5 9.0 %collective-permute-done.18.refs_2_ = bf16[144,512]{1,0:T(8,128)(2,1)S(1)} collective-permute-done((bf16[144,512]{1,0:T(8,128)(2,1)S(1)}, bf16[144,512]{1,0:T(8,128)(2,1)S(1)}, u32[]{:S(2)}, u32[]{:S(2)}) %collective-permute-start.18) | collective-permute-done | bytes 147488 | tf_op jit(solution)/shard_map/ppermute | solution.py:410
  168.5 1.6 collective-permute-start.19
  170.1 7.7 %down_grads.1 = bf16[16,192,512]{2,1,0:T(8,128)(2,1)} custom-call(s32[2]{0:T(128)S(1)} %pad_add_fusion.ids_ref, s32[4,16]{1,0:T(4,128)S(1)} %bitcast.23, bf16[4,192,256]{2,1,0:T(8,128)(2,1)S(1)} %copy-done.16, bf16[4,192,256]{2,1,0:T(8,128)(2,1)S(1)} %collective-permute-done.30.refs_1_, bf16[4,192,256]{2,1,0:T(8,128)(2,1)S(1)} %collective-permute-done.31.refs_2_, ...), custom_call_target="tpu_custom_call" | custom-call | tf_op jit(solution)/shard_map/down_grads/pallas_call | solution.py:625
  177.9 1.4 token_grads.1
  179.3 10.2 %in_grads.1 = bf16[16,384,512]{2,1,0:T(8,128)(2,1)} custom-call(s32[2]{0:T(128)S(1)} %pad_add_fusion.ids_ref, s32[4,16]{1,0:T(4,128)S(1)} %bitcast.25, bf16[2,384,256]{2,1,0:T(8,128)(2,1)S(1)} %stack_columns.3.refs_0_, bf16[2,384,256]{2,1,0:T(8,128)(2,1)S(1)} %collective-permute-done.21.refs_1_, bf16[2,384,256]{2,1,0:T(8,128)(2,1)S(1)} %collective-permute-done.22.refs_2_, ...), custom_call_target="tpu_custom_call" | custom-call | tf_op jit(solution)/shard_map/in_grads/pallas_call | solution.py:625
  (103 shorter events, 9.5 us)
Async XLA Ops:
  3.2 9.1 %collective-permute-start = (bf16[144,512]{1,0:T(8,128)(2,1)}, bf16[144,512]{1,0:T(8,128)(2,1)S(1)}, u32[]{:S(2)}, u32[]{:S(2)}) collective-permute-start(bf16[144,512]{1,0:T(8,128)(2,1)} %route.1.refs_0_), channel_id=1, source_target_pairs={{0,4},{4,0},{8,12},{12,8},{1,5},{5,1},{9,13},{13,9},{2,6},{6,2},{1... | collective-permute-start | bytes 442376 | tf_op jit(solution)/shard_map/ppermute | solution.py:410
  6.2 15.8 %collective-permute-start.1 = (bf16[144,512]{1,0:T(8,128)(2,1)}, bf16[144,512]{1,0:T(8,128)(2,1)}, u32[]{:S(2)}, u32[]{:S(2)}) collective-permute-start(bf16[144,512]{1,0:T(8,128)(2,1)} %route.1.refs_0_), channel_id=1, source_target_pairs={{0,8},{4,12},{8,0},{12,4},{1,9},{5,13},{9,1},{13,5},{2,10},{6,14},... | collective-permute-start | bytes 442376 | tf_op jit(solution)/shard_map/ppermute | solution.py:410
  8.8 13.2 %collective-permute-start.2 = (bf16[144,512]{1,0:T(8,128)(2,1)}, bf16[144,512]{1,0:T(8,128)(2,1)}, u32[]{:S(2)}, u32[]{:S(2)}) collective-permute-start(bf16[144,512]{1,0:T(8,128)(2,1)} %route.1.refs_0_), channel_id=1, source_target_pairs={{0,12},{4,8},{8,4},{12,0},{1,13},{5,9},{9,5},{13,1},{2,14},{6,10},... | collective-permute-start | bytes 442376 | tf_op jit(solution)/shard_map/ppermute | solution.py:410
  12.3 1.9 copy-start
  15.2 6.7 %copy-start.27 = (bf16[192,256]{1,0:T(8,128)(2,1)}, bf16[192,256]{1,0:T(8,128)(2,1)S(1)}, u32[]{:S(2)}) copy-start(bf16[192,256]{1,0:T(8,128)(2,1)S(1)} %get-tuple-element.29.refs_6_) | copy-start | bytes 294916
  15.2 50.6 %copy-start.1 = (bf16[8,128,1536]{2,1,0:T(8,128)(2,1)S(1)}, bf16[8,128,1536]{2,1,0:T(8,128)(2,1)}, u32[]{:S(2)}) copy-start(bf16[8,128,1536]{2,1,0:T(8,128)(2,1)} %param.17) | copy-start | bytes 9437188
  15.2 18.6 %collective-permute-start.6 = (bf16[192,256]{1,0:T(8,128)(2,1)S(1)}, bf16[192,256]{1,0:T(8,128)(2,1)S(1)}, u32[]{:S(2)}, u32[]{:S(2)}) collective-permute-start(bf16[192,256]{1,0:T(8,128)(2,1)S(1)} %get-tuple-element.30), channel_id=1, source_target_pairs={{0,4},{4,0},{8,12},{12,8},{1,5},{5,1},{9,13},{13,9},{2,6},{6,2},{1... | collective-permute-start | bytes 294920 | tf_op jit(solution)/shard_map/ppermute | solution.py:410
  15.9 17.9 %collective-permute-start.7 = (bf16[192,256]{1,0:T(8,128)(2,1)S(1)}, bf16[192,256]{1,0:T(8,128)(2,1)S(1)}, u32[]{:S(2)}, u32[]{:S(2)}) collective-permute-start(bf16[192,256]{1,0:T(8,128)(2,1)S(1)} %get-tuple-element.31), channel_id=1, source_target_pairs={{0,8},{4,12},{8,0},{12,4},{1,9},{5,13},{9,1},{13,5},{2,10},{6,14},... | collective-permute-start | bytes 294920 | tf_op jit(solution)/shard_map/ppermute | solution.py:410
  19.6 14.3 %collective-permute-start.8 = (bf16[192,256]{1,0:T(8,128)(2,1)S(1)}, bf16[192,256]{1,0:T(8,128)(2,1)}, u32[]{:S(2)}, u32[]{:S(2)}) collective-permute-start(bf16[192,256]{1,0:T(8,128)(2,1)S(1)} %get-tuple-element.32), channel_id=1, source_target_pairs={{0,12},{4,8},{8,4},{12,0},{1,13},{5,9},{9,5},{13,1},{2,14},{6,10},... | collective-permute-start | bytes 294920 | tf_op jit(solution)/shard_map/ppermute | solution.py:410
  33.8 95.8 %copy-start.5 = (f32[4,64,128]{2,1,0:T(8,128)S(1)}, f32[4,64,128]{2,1,0:T(8,128)}, u32[]{:S(2)}) copy-start(f32[4,64,128]{2,1,0:T(8,128)} %copy-done.3) | copy-start | bytes 393220
  34.5 57.3 %collective-permute-start.24 = (bf16[1024,512]{1,0:T(8,128)(2,1)}, bf16[1024,512]{1,0:T(8,128)(2,1)}, u32[]{:S(2)}, u32[]{:S(2)}) collective-permute-start(bf16[1024,512]{1,0:T(8,128)(2,1)} %gate.2), channel_id=1, source_target_pairs={{0,4},{4,8},{8,12},{1,5},{5,9},{9,13},{2,6},{6,10},{10,14},{3,7},{... | collective-permute-start | bytes 3145736 | tf_op jit(solution)/shard_map/ppermute | solution.py:440
  43.9 47.9 %collective-permute-start.25 = (bf16[1024,512]{1,0:T(8,128)(2,1)}, bf16[1024,512]{1,0:T(8,128)(2,1)}, u32[]{:S(2)}, u32[]{:S(2)}) collective-permute-start(bf16[1024,512]{1,0:T(8,128)(2,1)} %gate.2), channel_id=1, source_target_pairs={{12,8},{8,4},{4,0},{13,9},{9,5},{5,1},{14,10},{10,6},{6,2},{15,11}... | collective-permute-start | bytes 3145736 | tf_op jit(solution)/shard_map/ppermute | solution.py:441
  45.2 2.6 %collective-permute-start.3 = (bf16[256,768]{1,0:T(8,128)(2,1)}, bf16[256,768]{1,0:T(8,128)(2,1)S(1)}, u32[]{:S(2)}, u32[]{:S(2)}) collective-permute-start(bf16[256,768]{1,0:T(8,128)(2,1)} %copy-done.34), channel_id=1, source_target_pairs={{0,1},{1,0},{2,3},{3,2},{4,5},{5,4},{6,7},{7,6},{8,9},{9,8},{10,11... | collective-permute-start | bytes 1179656 | tf_op jit(solution)/shard_map/ppermute | solution.py:410
  45.3 12.7 %collective-permute-start.4 = (bf16[256,768]{1,0:T(8,128)(2,1)}, bf16[256,768]{1,0:T(8,128)(2,1)S(1)}, u32[]{:S(2)}, u32[]{:S(2)}) collective-permute-start(bf16[256,768]{1,0:T(8,128)(2,1)} %copy-done.33), channel_id=1, source_target_pairs={{0,2},{1,3},{2,0},{3,1},{4,6},{5,7},{6,4},{7,5},{8,10},{9,11},{10,... | collective-permute-start | bytes 1179656 | tf_op jit(solution)/shard_map/ppermute | solution.py:410
  47.8 18.1 %collective-permute-start.5 = (bf16[256,768]{1,0:T(8,128)(2,1)}, bf16[256,768]{1,0:T(8,128)(2,1)S(1)}, u32[]{:S(2)}, u32[]{:S(2)}) collective-permute-start(bf16[256,768]{1,0:T(8,128)(2,1)} %copy-done.32), channel_id=1, source_target_pairs={{0,3},{1,2},{2,1},{3,0},{4,7},{5,6},{6,5},{7,4},{8,11},{9,10},{10,... | collective-permute-start | bytes 1179656 | tf_op jit(solution)/shard_map/ppermute | solution.py:410
  68.6 1.0 copy-start.24
  73.8 18.0 %copy-start.15 = (bf16[4,192,256]{2,1,0:T(8,128)(2,1)}, bf16[4,192,256]{2,1,0:T(8,128)(2,1)S(1)}, u32[]{:S(2)}) copy-start(bf16[4,192,256]{2,1,0:T(8,128)(2,1)S(1)} %get-tuple-element.42.refs_0_) | copy-start | bytes 1179652
  73.8 18.0 %copy-start.21 = (bf16[256,768]{1,0:T(8,128)(2,1)}, bf16[256,768]{1,0:T(8,128)(2,1)S(1)}, u32[]{:S(2)}) copy-start(bf16[256,768]{1,0:T(8,128)(2,1)S(1)} %get-tuple-element.33.refs_0_) | copy-start | bytes 1179652
  73.8 17.1 %collective-permute-start.12 = (bf16[384,256]{1,0:T(8,128)(2,1)S(1)}, bf16[384,256]{1,0:T(8,128)(2,1)S(1)}, u32[]{:S(2)}, u32[]{:S(2)}) collective-permute-start(bf16[384,256]{1,0:T(8,128)(2,1)S(1)} %get-tuple-element.34), channel_id=1, source_target_pairs={{0,8},{4,12},{8,0},{12,4},{1,9},{5,13},{9,1},{13,5},{2,10},{6,14},... | collective-permute-start | bytes 589832 | tf_op jit(solution)/shard_map/ppermute | solution.py:410
  76.2 14.7 %collective-permute-start.13 = (bf16[384,256]{1,0:T(8,128)(2,1)S(1)}, bf16[384,256]{1,0:T(8,128)(2,1)S(1)}, u32[]{:S(2)}, u32[]{:S(2)}) collective-permute-start(bf16[384,256]{1,0:T(8,128)(2,1)S(1)} %get-tuple-element.35), channel_id=1, source_target_pairs={{0,12},{4,8},{8,4},{12,0},{1,13},{5,9},{9,5},{13,1},{2,14},{6,10},... | collective-permute-start | bytes 589832 | tf_op jit(solution)/shard_map/ppermute | solution.py:410
  78.8 13.0 %collective-permute-start.20 = (bf16[384,256]{1,0:T(8,128)(2,1)S(1)}, bf16[384,256]{1,0:T(8,128)(2,1)S(1)}, u32[]{:S(2)}, u32[]{:S(2)}) collective-permute-start(bf16[384,256]{1,0:T(8,128)(2,1)S(1)} %get-tuple-element.39), channel_id=1, source_target_pairs={{0,4},{4,0},{8,12},{12,8},{1,5},{5,1},{9,13},{13,9},{2,6},{6,2},{1... | collective-permute-start | bytes 589832 | tf_op jit(solution)/shard_map/ppermute | solution.py:410
  90.9 0.9 copy-start.10
  92.5 30.7 %collective-permute-start.26 = (bf16[1024,512]{1,0:T(8,128)(2,1)}, bf16[1024,512]{1,0:T(8,128)(2,1)S(1)}, u32[]{:S(2)}, u32[]{:S(2)}) collective-permute-start(bf16[1024,512]{1,0:T(8,128)(2,1)} %get-tuple-element.40.refs_9_), channel_id=1, source_target_pairs={{4,8},{8,12},{5,9},{9,13},{6,10},{10,14},{7,11},{11,15},{20,24},{2... | collective-permute-start | bytes 3145736 | tf_op jit(solution)/shard_map/ppermute | solution.py:440
  93.2 30.8 %collective-permute-start.28 = (bf16[1024,512]{1,0:T(8,128)(2,1)}, bf16[1024,512]{1,0:T(8,128)(2,1)S(1)}, u32[]{:S(2)}, u32[]{:S(2)}) collective-permute-start(bf16[1024,512]{1,0:T(8,128)(2,1)} %get-tuple-element.41.refs_12_), channel_id=1, source_target_pairs={{8,4},{4,0},{9,5},{5,1},{10,6},{6,2},{11,7},{7,3},{24,20},{20,16},... | collective-permute-start | bytes 3145736 | tf_op jit(solution)/shard_map/ppermute | solution.py:441
  94.5 4.1 %collective-permute-start.9 = (bf16[256,768]{1,0:T(8,128)(2,1)}, bf16[256,768]{1,0:T(8,128)(2,1)S(1)}, u32[]{:S(2)}, u32[]{:S(2)}) collective-permute-start(bf16[256,768]{1,0:T(8,128)(2,1)} %copy-done.21), channel_id=1, source_target_pairs={{0,1},{1,0},{2,3},{3,2},{4,5},{5,4},{6,7},{7,6},{8,9},{9,8},{10,11... | collective-permute-start | bytes 1179656 | tf_op jit(solution)/shard_map/ppermute | solution.py:410
  94.6 12.2 %collective-permute-start.10 = (bf16[256,768]{1,0:T(8,128)(2,1)}, bf16[256,768]{1,0:T(8,128)(2,1)S(1)}, u32[]{:S(2)}, u32[]{:S(2)}) collective-permute-start(bf16[256,768]{1,0:T(8,128)(2,1)} %copy-done.21), channel_id=1, source_target_pairs={{0,2},{1,3},{2,0},{3,1},{4,6},{5,7},{6,4},{7,5},{8,10},{9,11},{10,... | collective-permute-start | bytes 1179656 | tf_op jit(solution)/shard_map/ppermute | solution.py:410
  96.4 18.8 %collective-permute-start.31 = (bf16[4,192,256]{2,1,0:T(8,128)(2,1)}, bf16[4,192,256]{2,1,0:T(8,128)(2,1)S(1)}, u32[]{:S(2)}, u32[]{:S(2)}) collective-permute-start(bf16[4,192,256]{2,1,0:T(8,128)(2,1)} %copy-done.15), channel_id=1, source_target_pairs={{0,2},{1,3},{2,0},{3,1},{4,6},{5,7},{6,4},{7,5},{8,10},{9,11},{10,... | collective-permute-start | bytes 1179656 | tf_op jit(solution)/shard_map/ppermute | solution.py:410
  98.6 24.6 %collective-permute-start.15 = (bf16[2,384,256]{2,1,0:T(8,128)(2,1)S(1)}, bf16[2,384,256]{2,1,0:T(8,128)(2,1)S(1)}, u32[]{:S(2)}, u32[]{:S(2)}) collective-permute-start(bf16[2,384,256]{2,1,0:T(8,128)(2,1)S(1)} %stack_columns.2.refs_4_), channel_id=1, source_target_pairs={{0,2},{1,3},{2,0},{3,1},{4,6},{5,7},{6,4},{7,5},{8,10},{9,11},{10,... | collective-permute-start | bytes 1179656 | tf_op jit(solution)/shard_map/ppermute | solution.py:410
  106.8 18.5 %collective-permute-start.14 = (bf16[2,384,256]{2,1,0:T(8,128)(2,1)S(1)}, bf16[2,384,256]{2,1,0:T(8,128)(2,1)S(1)}, u32[]{:S(2)}, u32[]{:S(2)}) collective-permute-start(bf16[2,384,256]{2,1,0:T(8,128)(2,1)S(1)} %stack_columns.2.refs_4_), channel_id=1, source_target_pairs={{0,1},{1,0},{2,3},{3,2},{4,5},{5,4},{6,7},{7,6},{8,9},{9,8},{10,11... | collective-permute-start | bytes 1179656 | tf_op jit(solution)/shard_map/ppermute | solution.py:410
  115.2 12.5 %collective-permute-start.11 = (bf16[256,768]{1,0:T(8,128)(2,1)S(1)}, bf16[256,768]{1,0:T(8,128)(2,1)S(1)}, u32[]{:S(2)}, u32[]{:S(2)}) collective-permute-start(bf16[256,768]{1,0:T(8,128)(2,1)S(1)} %collective-permute-done.10.refs_2_), channel_id=1, source_target_pairs={{0,1},{1,0},{2,3},{3,2},{4,5},{5,4},{6,7},{7,6},{8,9},{9,8},{10,11... | collective-permute-start | bytes 1179656 | tf_op jit(solution)/shard_map/ppermute | solution.py:410
  123.2 6.4 %collective-permute-start.16 = (bf16[2,384,256]{2,1,0:T(8,128)(2,1)S(1)}, bf16[2,384,256]{2,1,0:T(8,128)(2,1)S(1)}, u32[]{:S(2)}, u32[]{:S(2)}) collective-permute-start(bf16[2,384,256]{2,1,0:T(8,128)(2,1)S(1)} %collective-permute-done.15.refs_8_.refs_6_), channel_id=1, source_target_pairs={{0,1},{1,0},{2,3},{3,2},{4,5},{5,4},{6,7},{7,6},{8,9},{9,8},{10,11... | collective-permute-start | bytes 1179656 | tf_op jit(solution)/shard_map/ppermute | solution.py:410
  123.2 56.1 %collective-permute-start.27 = (bf16[1024,512]{1,0:T(8,128)(2,1)S(1)}, bf16[1024,512]{1,0:T(8,128)(2,1)S(1)}, u32[]{:S(2)}, u32[]{:S(2)}) collective-permute-start(bf16[1024,512]{1,0:T(8,128)(2,1)S(1)} %collective-permute-done.26.refs_10_), channel_id=1, source_target_pairs={{8,12},{9,13},{10,14},{11,15},{24,28},{25,29},{26,30},{27,31}} | collective-permute-start | bytes 3145736 | tf_op jit(solution)/shard_map/ppermute | solution.py:440
  124.0 55.3 %collective-permute-start.29 = (bf16[1024,512]{1,0:T(8,128)(2,1)S(1)}, bf16[1024,512]{1,0:T(8,128)(2,1)S(1)}, u32[]{:S(2)}, u32[]{:S(2)}) collective-permute-start(bf16[1024,512]{1,0:T(8,128)(2,1)S(1)} %collective-permute-done.28.refs_13_), channel_id=1, source_target_pairs={{4,0},{5,1},{6,2},{7,3},{20,16},{21,17},{22,18},{23,19}} | collective-permute-start | bytes 3145736 | tf_op jit(solution)/shard_map/ppermute | solution.py:441
  125.3 13.6 %collective-permute-start.30 = (bf16[4,192,256]{2,1,0:T(8,128)(2,1)}, bf16[4,192,256]{2,1,0:T(8,128)(2,1)S(1)}, u32[]{:S(2)}, u32[]{:S(2)}) collective-permute-start(bf16[4,192,256]{2,1,0:T(8,128)(2,1)} %copy-done.15), channel_id=1, source_target_pairs={{0,1},{1,0},{2,3},{3,2},{4,5},{5,4},{6,7},{7,6},{8,9},{9,8},{10,11... | collective-permute-start | bytes 1179656 | tf_op jit(solution)/shard_map/ppermute | solution.py:410
  127.7 42.4 %copy-start.29 = (s32[16,4]{0,1:T(4,128)S(1)}, s32[16,4]{0,1:T(4,128)}, u32[]{:S(2)}) copy-start(s32[16,4]{0,1:T(4,128)} %param.14) | copy-start | bytes 772
  127.7 42.4 %copy-start.14 = (bf16[4,128,512]{2,1,0:T(8,128)(2,1)S(1)}, bf16[4,128,512]{2,1,0:T(8,128)(2,1)}, u32[]{:S(2)}) copy-start(bf16[4,128,512]{2,1,0:T(8,128)(2,1)} %copy-done.13) | copy-start | bytes 1572868
  127.7 42.4 %copy-start.16 = (bf16[4,192,256]{2,1,0:T(8,128)(2,1)S(1)}, bf16[4,192,256]{2,1,0:T(8,128)(2,1)}, u32[]{:S(2)}) copy-start(bf16[4,192,256]{2,1,0:T(8,128)(2,1)} %copy-done.15) | copy-start | bytes 1179652
  127.8 18.1 %collective-permute-start.22 = (bf16[2,384,256]{2,1,0:T(8,128)(2,1)S(1)}, bf16[2,384,256]{2,1,0:T(8,128)(2,1)S(1)}, u32[]{:S(2)}, u32[]{:S(2)}) collective-permute-start(bf16[2,384,256]{2,1,0:T(8,128)(2,1)S(1)} %stack_columns.3.refs_0_), channel_id=1, source_target_pairs={{0,2},{1,3},{2,0},{3,1},{4,6},{5,7},{6,4},{7,5},{8,10},{9,11},{10,... | collective-permute-start | bytes 1179656 | tf_op jit(solution)/shard_map/ppermute | solution.py:410
  129.6 17.5 %collective-permute-start.32 = (bf16[4,192,256]{2,1,0:T(8,128)(2,1)S(1)}, bf16[4,192,256]{2,1,0:T(8,128)(2,1)S(1)}, u32[]{:S(2)}, u32[]{:S(2)}) collective-permute-start(bf16[4,192,256]{2,1,0:T(8,128)(2,1)S(1)} %collective-permute-done.31.refs_2_), channel_id=1, source_target_pairs={{0,1},{1,0},{2,3},{3,2},{4,5},{5,4},{6,7},{7,6},{8,9},{9,8},{10,11... | collective-permute-start | bytes 1179656 | tf_op jit(solution)/shard_map/ppermute | solution.py:410
  129.6 1.0 copy-start.22
  138.8 39.0 %copy-start.30 = (s32[128,8]{0,1:T(8,128)S(1)}, s32[128,8]{0,1:T(8,128)}, u32[]{:S(2)}) copy-start(s32[128,8]{0,1:T(8,128)} %param.12) | copy-start | bytes 12292
  138.9 39.0 %copy-start.31 = (s32[128,8]{0,1:T(8,128)S(1)}, s32[128,8]{0,1:T(8,128)}, u32[]{:S(2)}) copy-start(s32[128,8]{0,1:T(8,128)} %param.13) | copy-start | bytes 12292
  138.9 40.5 %copy-start.2 = (bf16[8,4,32,512]{3,2,1,0:T(8,128)(2,1)S(1)}, bf16[8,4,32,512]{3,2,1,0:T(8,128)(2,1)}, u32[]{:S(2)}) copy-start(bf16[8,4,32,512]{3,2,1,0:T(8,128)(2,1)} %param.16) | copy-start | bytes 3145732
  138.9 20.2 %collective-permute-start.17 = (bf16[144,512]{1,0:T(8,128)(2,1)S(1)}, bf16[144,512]{1,0:T(8,128)(2,1)S(1)}, u32[]{:S(2)}, u32[]{:S(2)}) collective-permute-start(bf16[144,512]{1,0:T(8,128)(2,1)S(1)} %get-tuple-element.46), channel_id=1, source_target_pairs={{0,4},{4,0},{8,12},{12,8},{1,5},{5,1},{9,13},{13,9},{2,6},{6,2},{1... | collective-permute-start | bytes 442376 | tf_op jit(solution)/shard_map/ppermute | solution.py:410
  145.9 33.4 %collective-permute-start.21 = (bf16[2,384,256]{2,1,0:T(8,128)(2,1)S(1)}, bf16[2,384,256]{2,1,0:T(8,128)(2,1)S(1)}, u32[]{:S(2)}, u32[]{:S(2)}) collective-permute-start(bf16[2,384,256]{2,1,0:T(8,128)(2,1)S(1)} %stack_columns.3.refs_0_), channel_id=1, source_target_pairs={{0,1},{1,0},{2,3},{3,2},{4,5},{5,4},{6,7},{7,6},{8,9},{9,8},{10,11... | collective-permute-start | bytes 1179656 | tf_op jit(solution)/shard_map/ppermute | solution.py:410
  147.1 32.2 %collective-permute-start.23 = (bf16[2,384,256]{2,1,0:T(8,128)(2,1)S(1)}, bf16[2,384,256]{2,1,0:T(8,128)(2,1)S(1)}, u32[]{:S(2)}, u32[]{:S(2)}) collective-permute-start(bf16[2,384,256]{2,1,0:T(8,128)(2,1)S(1)} %collective-permute-done.22.refs_2_), channel_id=1, source_target_pairs={{0,1},{1,0},{2,3},{3,2},{4,5},{5,4},{6,7},{7,6},{8,9},{9,8},{10,11... | collective-permute-start | bytes 1179656 | tf_op jit(solution)/shard_map/ppermute | solution.py:410
  159.2 9.3 %collective-permute-start.18 = (bf16[144,512]{1,0:T(8,128)(2,1)S(1)}, bf16[144,512]{1,0:T(8,128)(2,1)S(1)}, u32[]{:S(2)}, u32[]{:S(2)}) collective-permute-start(bf16[144,512]{1,0:T(8,128)(2,1)S(1)} %get-tuple-element.45), channel_id=1, source_target_pairs={{0,8},{4,12},{8,0},{12,4},{1,9},{5,13},{9,1},{13,5},{2,10},{6,14},... | collective-permute-start | bytes 442376 | tf_op jit(solution)/shard_map/ppermute | solution.py:410
  168.5 9.3 %collective-permute-start.19 = (bf16[144,512]{1,0:T(8,128)(2,1)S(1)}, bf16[144,512]{1,0:T(8,128)(2,1)S(1)}, u32[]{:S(2)}, u32[]{:S(2)}) collective-permute-start(bf16[144,512]{1,0:T(8,128)(2,1)S(1)} %get-tuple-element.44), channel_id=1, source_target_pairs={{0,12},{4,8},{8,4},{12,0},{1,13},{5,9},{9,5},{13,1},{2,14},{6,10},... | collective-permute-start | bytes 442376 | tf_op jit(solution)/shard_map/ppermute | solution.py:410
  (20 other events, 16.2 us)

commit v6 on v5

--- a/solution.py
+++ b/solution.py
@@ -10,7 +10,6 @@
 
 BF = jnp.bfloat16
 F32 = jnp.float32
-GROUPS = 2
 PER = 2
 
 
@@ -158,8 +157,8 @@
 def down_kernel(z, ids_ref, *refs):
     bufs = refs[: z.ep]
     weight_ref = refs[z.ep]
-    parts = refs[z.ep + 1 : z.ep + 1 + z.sub]
-    grads_ref, codes_ref, rows_ref, held, sems = refs[z.ep + 1 + z.sub :]
+    parts = refs[z.ep + 2 : z.ep + 4]
+    grads_ref, codes_ref, rows_ref, held, sems = refs[z.ep + 4 :]
     me, mine = ids_ref[0], ids_ref[1]
     step = pl.program_id(0)
 
@@ -193,7 +192,7 @@
 
         @pl.when(place == k)
         def _():
-            parts[k][pl.ds(spot, z.block), :] = partial
+            parts[k % 2][k // 2, pl.ds(spot, z.block), :] = partial
 
 
 def gate_terms(z, pair, grad, scale):
@@ -208,43 +207,36 @@
     return hidden, grad_gate.astype(BF), grad_up.astype(BF)
 
 
-def pre_kernel(z, ids_ref, *refs):
-    parts = refs[: z.sub]
-    pair_ref, codes_ref = refs[z.sub : z.sub + 2]
-    downs, refs = refs[z.sub + 2 : z.sub + 2 + z.ep], refs[z.sub + 2 + z.ep :]
-    outs = refs[: z.ep]
-    grad_ref, down_ref, sides = refs[z.ep :]
+def pre_kernel(z, ids_ref, keep_ref, got_ref, pair_ref, codes_ref, *refs):
+    downs = refs[: z.ep]
+    out_ref, bundle_ref = refs[-2:]
 
     @pl.when(pl.program_id(0) == 0)
     def _():
         for k in range(z.ep):
-            down_ref[k] = downs[k][...]
+            bundle_ref[k] = downs[k][...]
 
     me = ids_ref[0]
     block = ids_ref[1] * z.part_blocks + pl.program_id(0)
     slot, first = block_place(z, block)
     scale = block_scale(z, codes_ref, me * z.local + slot, first)
-    grad = parts[0][...].astype(F32)
-    for k in range(1, z.sub):
-        grad = grad + parts[k][...].astype(F32)
-    grad_ref[...] = grad.astype(BF)
+    grad = keep_ref[0].astype(F32) + got_ref[0].astype(F32)
+    turned = grad.astype(BF).T
+    spot = pl.multiple_of(pl.program_id(0) * z.block, z.block)
+    for q in range(z.ep):
+        bundle_ref[z.ep + q, :, pl.ds(spot, z.block)] = turned[
+            q * z.down_cols : (q + 1) * z.down_cols, :
+        ]
     _, grad_gate, grad_up = gate_terms(z, pair_ref[...], grad, scale)
     pre = jnp.concatenate([grad_gate.T, grad_up.T], axis=0)
     for q in range(z.ep):
-        sides[q] = pre[q * z.in_cols : (q + 1) * z.in_cols, :]
-    for k in range(z.ep):
-        outs[k][...] = sides[me ^ k]
-
-
-def stack_kernel(*refs):
-    for i, ref in enumerate(refs[:-1]):
-        refs[-1][i] = ref[...]
+        out_ref[q] = pre[q * z.in_cols : (q + 1) * z.in_cols, :]
 
 
 def row_kernel(z, ids_ref, *refs):
     grads = refs[: z.sub]
-    pair_ref, weight_ref, codes_ref = refs[z.sub : z.sub + 3]
-    out_ref, rows_ref, marks, held, weights, sems = refs[-6:]
+    pair_ref, weight_ref, codes_ref, keep_ref, send_ref = refs[z.sub : z.sub + 5]
+    rows_ref, marks, held, weights, sems = refs[z.sub + 5 :]
     me, mine = ids_ref[0], ids_ref[1]
     step = pl.program_id(0)
     place = step // z.part_blocks
@@ -262,7 +254,8 @@
 
         @pl.when(place == k)
         def _():
-            held[...] = grads[k][pl.ds(spot, z.block), :]
+            turned = [grads[k][z.ep + q, :, pl.ds(spot, z.block)] for q in range(z.ep)]
+            held[...] = jnp.concatenate(turned, axis=0).T
 
     grad = held[...].astype(F32)
     scale = block_scale(z, codes_ref, me * z.local + slot, first)
@@ -277,32 +270,36 @@
     start = pl.multiple_of(first * z.cap, z.block)
     rows_ref[slot, pl.ds(start, z.block), :] = rows.astype(BF)
     for a, pick in block_picks(z, codes_ref, me * z.local + slot, first):
-        marks[first + a, pl.ds(slot, 1), :] = jnp.sum(
+        marks[first + a, pl.ds(me * z.local + slot, 1), :] = jnp.sum(
             jnp.where(pick, route[a * z.cap : (a + 1) * z.cap, :], 0.0), axis=0, keepdims=True
         )
 
     @pl.when(step == z.blocks - 1)
     def _():
-        for p in range(z.ep):
-            rows = rows_ref[:, p * z.cap : (p + 1) * z.cap, :].reshape(z.local * z.cap, z.width)
-            out_ref[p ^ me, : z.tokens, :] = tn(local_picks(z, codes_ref, p, me), rows).astype(BF)
-            out_ref[p ^ me, z.tokens :, : z.tokens] = marks[p].astype(BF)
-            out_ref[p ^ me, z.tokens :, z.tokens :] = jnp.zeros(
-                (marks.shape[1], z.width - z.tokens), BF
-            )
-
-
-def token_kernel(z, ids_ref, count_ref, *refs):
-    got = refs[: z.ep]
-    routes_ref, replica_ref, table_ref, tokens_ref, route_ref, marks = refs[z.ep :]
-    me = ids_ref[0]
-    total = got[0][: z.tokens, :].astype(F32)
-    for k in range(1, z.ep):
-        total = total + got[k][: z.tokens, :].astype(F32)
-    tokens_ref[...] = total.astype(BF)
-    for k in range(z.ep):
-        marks[me ^ k] = got[k][z.tokens :, : z.tokens].astype(F32)
-    rows = jnp.concatenate([marks[p][: z.local, :] for p in range(z.ep)], axis=0).astype(BF)
+        blank = jnp.zeros((z.slots, z.width - z.tokens), BF)
+        for k in range(z.ep):
+            source = me ^ k
+            start = pl.multiple_of(source * z.cap, z.cap)
+            rows = rows_ref[:, pl.ds(start, z.cap), :].reshape(z.local * z.cap, z.width)
+            out_ref = send_ref if k % 2 else keep_ref
+            picks = local_picks(z, codes_ref, source, me)
+            out_ref[k // 2, : z.tokens, :] = tn(picks, rows).astype(BF)
+            out_ref[k // 2, z.tokens :, : z.tokens] = marks[source].astype(BF)
+            out_ref[k // 2, z.tokens :, z.tokens :] = blank
+
+
+def halve_kernel(keep_ref, got_ref, out_keep, out_send):
+    for i in range(out_keep.shape[0]):
+        for j, out in enumerate((out_keep, out_send)):
+            total = keep_ref[2 * i + j].astype(F32) + got_ref[2 * i + j].astype(F32)
+            out[i] = total.astype(BF)
+
+
+def token_kernel(z, count_ref, *refs):
+    keep_ref, got_ref, routes_ref, replica_ref, table_ref, tokens_ref, route_ref = refs
+    total = keep_ref[0].astype(F32) + got_ref[0].astype(F32)
+    tokens_ref[...] = total[: z.tokens, :].astype(BF)
+    rows = total[z.tokens :, : z.tokens].astype(BF)
     totals = [jnp.zeros((1, z.tokens), F32)] * z.top
     for r in range(z.reps):
         spread = tn(slot_table(z, table_ref, r), rows)
@@ -312,14 +309,6 @@
     route_ref[...] = jnp.concatenate(totals, axis=0).astype(BF)
 
 
-def side_moves(z, groups, sides, held, sems, act):
-    size = z.ep // groups
-    for g in range(groups):
-        for k in range(z.sub):
-            i = g * z.sub + k
-            act(pltpu.make_async_copy(sides[i], held.at[k, pl.ds(g * size, size)], sems.at[i]))
-
-
 def input_moves(z, me, own_ref, rights, lefts, inputs_ref, own_sem, right_sems, left_sems, act):
     act(pltpu.make_async_copy(own_ref, inputs_ref.at[me], own_sem))
     for d in range(1, z.ep):
@@ -341,81 +330,99 @@
             )
 
 
-def expert_products(z, ids_ref, table_ref, held, right_rows, out_ref):
-    me, mine = ids_ref[0], ids_ref[1]
-    for i in range(PER):
-        expert = pl.program_id(0) * PER + i
-        first = table_ref[0, expert]
-        left, right = [], []
-        for r in range(z.reps):
-            slot_id = table_ref[r, expert]
-            source = slot_id // z.local
-            for b in range(z.slot_blocks):
-                block = (slot_id % z.local) * z.slot_blocks + b
-                part = (block // z.part_blocks) ^ mine
-                spot = pl.multiple_of((block % z.part_blocks) * z.block, z.block)
-                side = jnp.where(slot_id == first, z.ep, source ^ me) if r else source ^ me
-                left.append(held[part, side, :, pl.ds(spot, z.block)])
-                right.append(right_rows(slot_id, block, b))
-        left = jnp.concatenate(left, axis=1)
-        out_ref[i] = nn(left, jnp.concatenate(right, axis=0)).astype(BF)
+def expert_products(z, ids_ref, table_ref, turn, held, right_rows, out_ref, made, out_sems):
+    mine = ids_ref[1]
+
+    def out_copy(expert):
+        return pltpu.make_async_copy(made.at[expert], out_ref.at[expert], out_sems.at[expert])
+
+    def some(step, carry):
+        for i in range(PER):
+            expert = step * PER + i
+            first = table_ref[0, expert]
+            left, right = [], []
+            for r in range(z.reps):
+                slot_id = table_ref[r, expert]
+                source = slot_id // z.local
+                for b in range(z.slot_blocks):
+                    block = (slot_id % z.local) * z.slot_blocks + b
+                    part = (block // z.part_blocks) ^ mine
+                    spot = pl.multiple_of((block % z.part_blocks) * z.block, z.block)
+                    side = source ^ turn
+                    if r:
+                        side = jnp.where(slot_id == first, z.ep, side)
+                    left.append(held[part, side, :, pl.ds(spot, z.block)])
+                    right.append(right_rows(slot_id, block, b))
+            left = jnp.concatenate(left, axis=1)
+            made[expert] = nn(left, jnp.concatenate(right, axis=0)).astype(BF)
+            out_copy(expert).start()
+        return carry
+
+    lax.fori_loop(0, z.experts // PER, some, 0)
+    for expert in range(z.experts):
+        out_copy(expert).wait()
 
 
 def total_down_kernel(z, ids_ref, table_ref, *refs):
     sides = refs[: z.sub]
-    grads_ref, codes_ref, out_ref, held, scaled, sems = refs[z.sub :]
-
-    @pl.when(pl.program_id(0) == 0)
-    def _():
-        side_moves(z, 1, sides, held, sems, lambda copy: copy.start())
-        held[:, z.ep] = jnp.zeros_like(held[:, z.ep])
-        rows = lax.broadcasted_iota(jnp.int32, (z.slots, z.cap, z.tokens), 1).astype(F32)
-        for p in range(z.ep):
-            code = codes_ref[p, : z.slots, :][:, None, :]
-            load = codes_ref[p, z.slots :, :][:, None, :]
-            pick = jnp.where(rows == code, load, 0.0).reshape(z.slots * z.cap, z.tokens)
-            made = nn(pick.astype(BF), grads_ref[p]).astype(BF)
-            scaled[:, p * z.cap : (p + 1) * z.cap, :] = made.reshape(z.slots, z.cap, z.width)
-        side_moves(z, 1, sides, held, sems, lambda copy: copy.wait())
+    grads_ref, codes_ref, out_ref, held, made, out_sems, scaled, sems = refs[z.sub :]
+
+    def moves(act):
+        for k in range(z.sub):
+            act(
+                pltpu.make_async_copy(
+                    sides[k].at[pl.ds(0, z.ep)], held.at[k, pl.ds(0, z.ep)], sems.at[k]
+                )
+            )
+
+    moves(lambda copy: copy.start())
+    held[:, z.ep] = jnp.zeros_like(held[:, z.ep])
+    rows = lax.broadcasted_iota(jnp.int32, (z.slots, z.cap, z.tokens), 1).astype(F32)
+    for p in range(z.ep):
+        code = codes_ref[p, : z.slots, :][:, None, :]
+        load = codes_ref[p, z.slots :, :][:, None, :]
+        pick = jnp.where(rows == code, load, 0.0).reshape(z.slots * z.cap, z.tokens)
+        result = nn(pick.astype(BF), grads_ref[p]).astype(BF)
+        scaled[:, p * z.cap : (p + 1) * z.cap, :] = result.reshape(z.slots, z.cap, z.width)
+    moves(lambda copy: copy.wait())
 
     def right_rows(slot_id, block, b):
         return scaled[slot_id, b * z.block : (b + 1) * z.block, :]
 
-    expert_products(z, ids_ref, table_ref, held, right_rows, out_ref)
+    expert_products(z, ids_ref, table_ref, ids_ref[0], held, right_rows, out_ref, made, out_sems)
 
 
 def total_in_kernel(z, ids_ref, table_ref, *refs):
-    sides, refs = refs[: GROUPS * z.sub], refs[GROUPS * z.sub :]
+    sides, refs = refs[: z.sub], refs[z.sub :]
     own_ref, rights, lefts = refs[0], refs[1 : z.ep], refs[z.ep : 2 * z.ep - 1]
-    out_ref, held, inputs_ref, sems, *other_sems = refs[2 * z.ep - 1 :]
-
-    @pl.when(pl.program_id(0) == 0)
-    def _():
-        def moves(act):
-            side_moves(z, GROUPS, sides, held, sems, act)
-            input_moves(z, ids_ref[0], own_ref, rights, lefts, inputs_ref, *other_sems, act)
-
-        moves(lambda copy: copy.start())
-        held[:, z.ep] = jnp.zeros_like(held[:, z.ep])
-        moves(lambda copy: copy.wait())
+    out_ref, held, made, out_sems, inputs_ref, sems, *other_sems = refs[2 * z.ep - 1 :]
+
+    def moves(act):
+        for k in range(z.sub):
+            act(pltpu.make_async_copy(sides[k], held.at[k, pl.ds(0, z.ep)], sems.at[k]))
+        input_moves(z, ids_ref[0], own_ref, rights, lefts, inputs_ref, *other_sems, act)
+
+    moves(lambda copy: copy.start())
+    held[:, z.ep] = jnp.zeros_like(held[:, z.ep])
+    moves(lambda copy: copy.wait())
 
     def right_rows(slot_id, block, b):
         start = pl.multiple_of(block * z.block, z.block)
         return inputs_ref[slot_id // z.local, pl.ds(start, z.block), :]
 
-    expert_products(z, ids_ref, table_ref, held, right_rows, out_ref)
+    expert_products(z, ids_ref, table_ref, 0, held, right_rows, out_ref, made, out_sems)
 
 
 def swap(x, axis, size, bit):
     return lax.ppermute(x, axis, [(i, i ^ bit) for i in range(size)])
 
 
-def spread_over(x, axis, size):
-    have = {0: x}
-    bit = size // 2
+def spread_over(have, axis, size, bit):
+    have = dict(have)
     while bit:
         for k in list(have):
-            have[k | bit] = swap(have[k], axis, size, bit)
+            if k | bit not in have:
+                have[k | bit] = swap(have[k], axis, size, bit)
         bit //= 2
     return [have[k] for k in range(size)]
 
@@ -432,6 +439,7 @@
         out_specs=[anywhere] * len(values),
         out_shape=[jax.ShapeDtypeStruct(v.shape, v.dtype) for v in values],
         input_output_aliases={i: i for i in range(len(values))},
+        compiler_params=pltpu.CompilerParams(vmem_limit_bytes=1024 * 1024),
         name="gate",
     )(*values, *after)
 
@@ -494,29 +502,34 @@
     )(ids, pair_rows, bufs[1])
     downs = [downs[0]] + [swap(downs[k], "ep", n, k) for k in range(1, n)]
 
-    def stack(pieces):
-        shape = pieces[0].shape
+    def halve(keep, got):
+        half = (keep.shape[0] // 2,) + keep.shape[1:]
         return pl.pallas_call(
-            stack_kernel,
-            in_specs=[whole(shape)] * len(pieces),
-            out_specs=whole((len(pieces),) + shape),
-            out_shape=jax.ShapeDtypeStruct((len(pieces),) + shape, BF),
+            halve_kernel,
+            in_specs=[whole(keep.shape)] * 2,
+            out_specs=[whole(half)] * 2,
+            out_shape=[jax.ShapeDtypeStruct(half, BF)] * 2,
             grid=(1,),
-            compiler_params=params(8),
-            name="stack_columns",
-        )(*pieces)
+            compiler_params=params(16),
+            name="halve",
+        )(keep, got)
 
     def row_block(i, ids_ref):
         place = i // z.part_blocks
         return (place ^ ids_ref[1]) * z.part_blocks + i % z.part_blocks
 
+    chain = gate([inputs], bufs[1:] + downs[1:])
+    steps = [chain_step(chain[0], chain[0], "ep", n, 1)]
+
+    part_shape = (m // 2, z.part, z.hidden)
     outs = pl.pallas_call(
         functools.partial(down_kernel, z),
         grid_spec=pltpu.PrefetchScalarGridSpec(
             num_scalar_prefetch=1,
             grid=(z.blocks,),
-            in_specs=[whole(grad_shape)] * n + [pl.BlockSpec(memory_space=pltpu.HBM)],
-            out_specs=[whole((z.part, z.hidden))] * m
+            in_specs=[whole(grad_shape)] * n
+            + [pl.BlockSpec(memory_space=pltpu.HBM), pl.BlockSpec(memory_space=pl.ANY)],
+            out_specs=[whole(part_shape)] * 2
             + [whole((n, z.tokens, z.width)), whole(code_shape)],
             scratch_shapes=[
                 pltpu.VMEM((z.local, z.rows, z.width), BF),
@@ -524,86 +537,87 @@
                 pltpu.SemaphoreType.DMA((z.local,)),
             ],
         ),
-        out_shape=[jax.ShapeDtypeStruct((z.part, z.hidden), BF)] * m
+        out_shape=[jax.ShapeDtypeStruct(part_shape, BF)] * 2
         + [
             jax.ShapeDtypeStruct((n, z.tokens, z.width), BF),
             jax.ShapeDtypeStruct(code_shape, F32),
         ],
         compiler_params=params(48),
         name="hidden_partials",
-    )(ids, *bufs, weight_down)
-    parts, (grads_all, codes) = outs[:m], outs[m:]
-    chain = gate([inputs], downs[1:] + [codes])
-    steps = [chain_step(chain[0], chain[0], "ep", n, 1)]
-    parts = [parts[0]] + [swap(parts[k], "sub", m, k) for k in range(1, m)]
-
-    outs = pl.pallas_call(
+    )(ids, *bufs, weight_down, chain[0])
+    keep, send, grads_all, codes = outs
+    got = swap(send, "sub", m, 1)
+    bit = 2
+    while bit < m:
+        keep, send = halve(keep, got)
+        got = swap(send, "sub", m, bit)
+        bit *= 2
+    pre, bundle = pl.pallas_call(
         functools.partial(pre_kernel, z),
         grid_spec=pltpu.PrefetchScalarGridSpec(
             num_scalar_prefetch=1,
             grid=(z.part_blocks,),
-            in_specs=[pl.BlockSpec((z.block, z.hidden), lambda i, r: (i, 0))] * m
+            in_specs=[pl.BlockSpec((1, z.block, z.hidden), lambda i, r: (0, i, 0))] * 2
             + [
                 pl.BlockSpec((z.block, z.pair), lambda i, r: (r[1] * z.part_blocks + i, 0)),
                 whole(code_shape),
             ]
-            + [whole((z.down_cols, z.part))] * n,
-            out_specs=[pl.BlockSpec((z.in_cols, z.block), lambda i, r: (0, i))] * n
-            + [
-                pl.BlockSpec((z.block, z.hidden), lambda i, r: (i, 0)),
-                whole((n, z.down_cols, z.part)),
+            + [whole((z.down_cols, z.part))] * n
+            + [pl.BlockSpec(memory_space=pl.ANY)] * 2,
+            out_specs=[
+                pl.BlockSpec((n, z.in_cols, z.block), lambda i, r: (0, 0, i)),
+                whole((2 * n, z.down_cols, z.part)),
             ],
-            scratch_shapes=[pltpu.VMEM((n, z.in_cols, z.block), BF)],
         ),
-        out_shape=[jax.ShapeDtypeStruct((z.in_cols, z.part), BF)] * n
-        + [
-            jax.ShapeDtypeStruct((z.part, z.hidden), BF),
-            jax.ShapeDtypeStruct((n, z.down_cols, z.part), BF),
+        out_shape=[
+            jax.ShapeDtypeStruct((n, z.in_cols, z.part), BF),
+            jax.ShapeDtypeStruct((2 * n, z.down_cols, z.part), BF),
         ],
         compiler_params=params(16),
         name="pre_grads",
-    )(ids, *parts, pair_rows, codes, *downs)
-    pieces, grad_part = outs[:n], outs[n]
-    pieces = [pieces[0]] + [swap(pieces[k], "ep", n, k) for k in range(1, n)]
-    grad_parts = spread_over(grad_part, "sub", m)
-    steps[0] = gate(steps[0], pieces[1:])
+    )(ids, keep, got, pair_rows, codes, *downs, *steps[0])
+    columns = lax.all_to_all(pre, "ep", split_axis=0, concat_axis=0, tiled=True)
+    steps[0] = gate(steps[0], [columns])
     for d in range(2, n):
         steps.append(chain_step(*steps[-1], "ep", n, d))
+    bundles = spread_over({0: bundle}, "sub", m, m // 2)
+    sides = {0: gate([columns], [bundles[m // 2]])[0]}
+    sides[m // 2] = swap(sides[0], "sub", m, m // 2)
     gathered = [inputs] + [go for go, _ in steps] + [back for _, back in steps]
-    down_sides = spread_over(outs[n + 1], "sub", m)
-    size = n // GROUPS
-    sides = []
-    for g in range(GROUPS):
-        sides += spread_over(stack(pieces[g * size : (g + 1) * size]), "sub", m)
-
-    mark_rows = -(-z.local // 16) * 16
-    back_shape = (n, z.tokens + mark_rows, z.width)
-    back = pl.pallas_call(
+
+    back_shape = (n // 2, z.tokens + z.slots, z.width)
+    keep, send = pl.pallas_call(
         functools.partial(row_kernel, z),
         grid_spec=pltpu.PrefetchScalarGridSpec(
             num_scalar_prefetch=1,
             grid=(z.blocks,),
-            in_specs=[whole((z.part, z.hidden))] * m
+            in_specs=[whole(bundle.shape)] * m
             + [
                 pl.BlockSpec((z.block, z.pair), lambda i, r: (row_block(i, r), 0)),
                 pl.BlockSpec(memory_space=pltpu.HBM),
                 whole(code_shape),
-            ]
-            + [pl.BlockSpec(memory_space=pl.ANY)] * (m - 1),
-            out_specs=whole(back_shape),
+            ],
+            out_specs=[whole(back_shape)] * 2,
             scratch_shapes=[
                 pltpu.VMEM((z.local, z.rows, z.width), BF),
-                pltpu.VMEM((n, mark_rows, z.tokens), F32),
+                pltpu.VMEM((n, z.slots, z.tokens), F32),
                 pltpu.VMEM((z.block, z.hidden), BF),
                 pltpu.VMEM((z.local, z.pair, z.width), BF),
                 pltpu.SemaphoreType.DMA((z.local,)),
             ],
         ),
-        out_shape=jax.ShapeDtypeStruct(back_shape, BF),
+        out_shape=[jax.ShapeDtypeStruct(back_shape, BF)] * 2,
         compiler_params=params(46),
         name="row_grads",
-    )(ids, *grad_parts, pair_rows, weight_in, codes, *sides[1 - m :])
-    got = [back[0]] + [swap(back[k], "ep", n, k) for k in range(1, n)]
+    )(ids, *bundles, pair_rows, weight_in, codes)
+    sides[m // 2] = gate([sides[m // 2]], [keep])[0]
+    sides = spread_over(sides, "sub", m, m // 4)
+    got = swap(send, "ep", n, 1)
+    bit = 2
+    while bit < n:
+        keep, send = halve(keep, got)
+        got = swap(send, "ep", n, bit)
+        bit *= 2
 
     grad_tokens, grad_routes = pl.pallas_call(
         functools.partial(token_kernel, z),
@@ -611,25 +625,27 @@
             jax.ShapeDtypeStruct((z.tokens, z.width), BF),
             jax.ShapeDtypeStruct((z.top, z.tokens), BF),
         ],
-        in_specs=[smem(), smem()]
-        + [whole(back_shape[1:])] * n
-        + [whole(a.shape) for a in (routes, replica, table)],
+        in_specs=[smem()] + [whole(a.shape) for a in (keep, got, routes, replica, table)],
         out_specs=[whole((z.tokens, z.width)), whole((z.top, z.tokens))],
         grid=(1,),
-        scratch_shapes=[pltpu.VMEM((n, mark_rows, z.tokens), F32)],
         compiler_params=params(16),
         name="token_grads",
-    )(ids, token_count, *got, routes, replica, table)
+    )(token_count, keep, got, routes, replica, table)
 
     def total_call(kernel, operands, specs, cols, scratch, name):
         return pl.pallas_call(
             functools.partial(kernel, z),
             grid_spec=pltpu.PrefetchScalarGridSpec(
                 num_scalar_prefetch=2,
-                grid=(z.experts // PER,),
+                grid=(1,),
                 in_specs=specs,
-                out_specs=pl.BlockSpec((PER, cols, z.width), lambda e, r, t: (e, 0, 0)),
-                scratch_shapes=[pltpu.VMEM((m, n + 1, cols, z.part), BF)] + scratch,
+                out_specs=pl.BlockSpec(memory_space=pl.ANY),
+                scratch_shapes=[
+                    pltpu.VMEM((m, n + 1, cols, z.part), BF),
+                    pltpu.VMEM((z.experts, cols, z.width), BF),
+                    pltpu.SemaphoreType.DMA((z.experts,)),
+                ]
+                + scratch,
             ),
             out_shape=jax.ShapeDtypeStruct((z.experts, cols, z.width), BF),
             compiler_params=params(32),
@@ -637,10 +653,9 @@
         )(ids, table, *operands)
 
     anywhere = pl.BlockSpec(memory_space=pl.ANY)
-    pinned = pl.BlockSpec(memory_space=pltpu.HBM)
     grad_down = total_call(
         total_down_kernel,
-        [*down_sides, grads_all, codes],
+        [*bundles, grads_all, codes],
         [anywhere] * m + [whole((n, z.tokens, z.width)), whole(code_shape)],
         z.down_cols,
         [pltpu.VMEM((z.slots, z.rows, z.width), BF), pltpu.SemaphoreType.DMA((m,))],
@@ -649,11 +664,11 @@
     grad_in = total_call(
         total_in_kernel,
         [*sides, *gathered],
-        [anywhere] * (GROUPS * m) + [pinned] * (2 * n - 1),
+        [anywhere] * (m + 2 * n - 1),
         z.in_cols,
         [
             pltpu.VMEM((n, z.all_rows, z.width), BF),
-            pltpu.SemaphoreType.DMA((GROUPS * m,)),
+            pltpu.SemaphoreType.DMA((m,)),
             pltpu.SemaphoreType.DMA,
             pltpu.SemaphoreType.DMA((n - 1,)),
             pltpu.SemaphoreType.DMA((n - 1,)),

time: 190 us -> 171 us (0.900)
  local copies, waits for them, and re-layouts: 20.8 us -> 6.82 us
  starting transfers between devices: 49 us -> 42.2 us
  waiting for transfers between devices: 78.3 us -> 83.5 us
  Pallas kernels: 39.8 us -> 36.3 us
    ppermute x27 -> x16, waiting for transfers between devices: 78.2 us -> 25.8 us  [swap(): return lax.ppermute(x, axis, [(i, i ^ bit) for i in range(size)])]
    ppermute x3, waiting for transfers between devices: 0.07 us -> 39.2 us  [chain_step(): lax.ppermute(back, axis, [(i, i - 1) for i in range(size - d, 0, -1)])]
    all_to_all x0 -> x1, waiting for transfers between devices: none -> 17.4 us  [body(): columns = lax.all_to_all(pre, 'ep', split_axis=0, concat_axis=0, tiled=True)]
    unnamed x71 -> x25, local copies, waits for them, and re-layouts: 20.8 us -> 6.82 us
    ppermute x27 -> x16, starting transfers between devices: 34.2 us -> 24.3 us  [swap(): return lax.ppermute(x, axis, [(i, i ^ bit) for i in range(size)])]
    all_to_all x0 -> x1, starting transfers between devices: none -> 7.01 us  [body(): columns = lax.all_to_all(pre, 'ep', split_axis=0, concat_axis=0, tiled=True)]
    ppermute x3, starting transfers between devices: 10.9 us -> 6.98 us  [chain_step(): go = lax.ppermute(go, axis, [(i, i + 1) for i in range(d - 1, size - 1)])]
    pallas_call x2, Pallas kernels: 17.9 us -> 14.1 us  [total_call(): pl.pallas_call(functools.partial(kernel, z), grid_spec=pltpu.PrefetchScal...]
  transfers between devices with their start and end apart: 33 -> 23, of which waited for: 11 -> 9; matrix products, arithmetic and copies ran while one was open for 1% -> 1% of each run, Pallas kernels for 15% -> 11%
where the time goes in v6:
time: 171 us; the launch traced here: 170 us
  waiting for transfers between devices  83.5 us (49%)
  starting transfers between devices  42.2 us (25%)
  Pallas kernels  36.3 us (21%)
  local copies, waits for them, and re-layouts  6.82 us (4%)
    ppermute x3, waiting for transfers between devices, chain_step(): lax.ppermute(back, axis, [(i, i - 1) for i in range(size - d, 0, -1)])  39.2 us
    ppermute x16, waiting for transfers between devices, swap(): return lax.ppermute(x, axis, [(i, i ^ bit) for i in range(size)])  25.8 us
    ppermute x16, starting transfers between devices, swap(): return lax.ppermute(x, axis, [(i, i ^ bit) for i in range(size)])  24.3 us
    all_to_all x1, waiting for transfers between devices, body(): columns = lax.all_to_all(pre, 'ep', split_axis=0, concat_axis=0, tiled=True)  17.4 us
    pallas_call x2, Pallas kernels, total_call(): pl.pallas_call(functools.partial(kernel, z), grid_spec=pltpu.PrefetchScal...  14.1 us
    pallas_call x1, Pallas kernels, body(): pl.pallas_call(functools.partial(row_kernel, z), grid_spec=pltpu.Prefetch...  10 us
    all_to_all x1, starting transfers between devices, body(): columns = lax.all_to_all(pre, 'ep', split_axis=0, concat_axis=0, tiled=True)  7.01 us
    ppermute x3, starting transfers between devices, chain_step(): go = lax.ppermute(go, axis, [(i, i + 1) for i in range(d - 1, size - 1)])  6.98 us
  transfers between devices with their start and end apart: 23, of which 9 were waited for; matrix products, arithmetic and copies ran while one was open for 1% of the time, Pallas kernels for 11%

profile of v6, /device:TPU:0, one launch (start us, length us, event | category | flops | bytes accessed | tf_op | source)
XLA Modules:
  0.0 170.3 jit_solution(12117795964259780590)
XLA Ops:
  1.3 1.9 %route.1.refs_0_ = bf16[144,512]{1,0:T(8,128)(2,1)} custom-call(s32[1]{0:T(128)S(6)} %copy.24.count_ref, bf16[128,512]{1,0:T(8,128)(2,1)} %grad_ref.1, bf16[8,128]{1,0:T(8,128)(2,1)} %bitcast.22, s32[8,128]{1,0:T(8,128)} %bitcast.18, s32[8,128]{1,0:T(8,128)} %bitcast.20, s32[4,16]{1,0:T(4,128)} %bitcast.14), custom_call_target="tpu_custom_call" | custom-call | tf_op jit(solution)/shard_map/route/pallas_call | solution.py:476
  3.2 3.0 %collective-permute-start = (bf16[144,512]{1,0:T(8,128)(2,1)}, bf16[144,512]{1,0:T(8,128)(2,1)S(1)}, u32[]{:S(2)}, u32[]{:S(2)}) collective-permute-start(bf16[144,512]{1,0:T(8,128)(2,1)} %route.1.refs_0_), channel_id=1, source_target_pairs={{0,4},{4,0},{8,12},{12,8},{1,5},{5,1},{9,13},{13,9},{2,6},{6,2},{1... | collective-permute-start | bytes 442376 | tf_op jit(solution)/shard_map/ppermute | solution.py:417
  6.2 2.5 %collective-permute-start.2 = (bf16[144,512]{1,0:T(8,128)(2,1)}, bf16[144,512]{1,0:T(8,128)(2,1)}, u32[]{:S(2)}, u32[]{:S(2)}) collective-permute-start(bf16[144,512]{1,0:T(8,128)(2,1)} %route.1.refs_0_), channel_id=1, source_target_pairs={{0,12},{4,8},{8,4},{12,0},{1,13},{5,9},{9,5},{13,1},{2,14},{6,10},... | collective-permute-start | bytes 442376 | tf_op jit(solution)/shard_map/ppermute | solution.py:417
  8.7 0.1 collective-permute-start.1
  8.8 0.1 pad_add_fusion.ids_ref
  8.9 1.7 %collective-permute-done.after_ref.refs_1_ = bf16[144,512]{1,0:T(8,128)(2,1)S(1)} collective-permute-done((bf16[144,512]{1,0:T(8,128)(2,1)}, bf16[144,512]{1,0:T(8,128)(2,1)S(1)}, u32[]{:S(2)}, u32[]{:S(2)}) %collective-permute-start) | collective-permute-done | bytes 147488 | tf_op jit(solution)/shard_map/ppermute | solution.py:417
  10.6 1.9 %copy-done = bf16[8,128,1536]{2,1,0:T(8,128)(2,1)S(1)} copy-done((bf16[8,128,1536]{2,1,0:T(8,128)(2,1)S(1)}, bf16[8,128,1536]{2,1,0:T(8,128)(2,1)}, u32[]{:S(2)}) %copy-start) | copy-done | bytes 3145752
  12.5 1.1 hidden_columns.1
  13.5 2.4 %collective-permute-start.3 = (bf16[192,256]{1,0:T(8,128)(2,1)S(1)}, bf16[192,256]{1,0:T(8,128)(2,1)S(1)}, u32[]{:S(2)}, u32[]{:S(2)}) collective-permute-start(bf16[192,256]{1,0:T(8,128)(2,1)S(1)} %get-tuple-element.24), channel_id=1, source_target_pairs={{0,4},{4,0},{8,12},{12,8},{1,5},{5,1},{9,13},{13,9},{2,6},{6,2},{1... | collective-permute-start | bytes 294920 | tf_op jit(solution)/shard_map/ppermute | solution.py:417
  16.0 4.0 %collective-permute-start.4 = (bf16[192,256]{1,0:T(8,128)(2,1)S(1)}, bf16[192,256]{1,0:T(8,128)(2,1)S(1)}, u32[]{:S(2)}, u32[]{:S(2)}) collective-permute-start(bf16[192,256]{1,0:T(8,128)(2,1)S(1)} %get-tuple-element.25), channel_id=1, source_target_pairs={{0,8},{4,12},{8,0},{12,4},{1,9},{5,13},{9,1},{13,5},{2,10},{6,14},... | collective-permute-start | bytes 294920 | tf_op jit(solution)/shard_map/ppermute | solution.py:417
  20.0 1.2 copy.19.refs_0_
  21.2 6.3 %collective-permute-done.1.refs_2_ = bf16[144,512]{1,0:T(8,128)(2,1)} collective-permute-done((bf16[144,512]{1,0:T(8,128)(2,1)}, bf16[144,512]{1,0:T(8,128)(2,1)}, u32[]{:S(2)}, u32[]{:S(2)}) %collective-permute-start.1) | collective-permute-done | bytes 147488 | tf_op jit(solution)/shard_map/ppermute | solution.py:417
  27.5 1.9 %collective-permute-done.4.refs_5_.refs_2_ = bf16[192,256]{1,0:T(8,128)(2,1)S(1)} collective-permute-done((bf16[192,256]{1,0:T(8,128)(2,1)S(1)}, bf16[192,256]{1,0:T(8,128)(2,1)S(1)}, u32[]{:S(2)}, u32[]{:S(2)}) %collective-permute-start.4) | collective-permute-done | bytes 98336 | tf_op jit(solution)/shard_map/ppermute | solution.py:417
  29.4 6.5 %hidden_partials.1 = (bf16[2,256,768]{2,1,0:T(8,128)(2,1)S(1)}, bf16[2,256,768]{2,1,0:T(8,128)(2,1)S(1)}, bf16[4,128,512]{2,1,0:T(8,128)(2,1)S(1)}, f32[4,64,128]{2,1,0:T(8,128)S(1)}) custom-call(s32[2]{0:T(128)S(1)} %pad_add_fusion.ids_ref, bf16[144,512]{1,0:T(8,128)(2,1)S(1)} %copy-done.6, bf16[144,512]{1,0:T(8,128)(2,1)S(1)} %collective-permute-done.after_ref.refs_1_, ...), custom_call_target="tpu_custom_call" | custom-call | tf_op jit(solution)/shard_map/hidden_partials/pallas_call | solution.py:525
  35.9 0.8 copy-done.7
  36.7 1.3 collective-permute-start.9
  38.0 5.5 %collective-permute-start.8 = (bf16[1024,512]{1,0:T(8,128)(2,1)S(1)}, bf16[1024,512]{1,0:T(8,128)(2,1)}, u32[]{:S(2)}, u32[]{:S(2)}) collective-permute-start(bf16[1024,512]{1,0:T(8,128)(2,1)S(1)} %gate.4.refs_5_), channel_id=1, source_target_pairs={{0,4},{4,8},{8,12},{1,5},{5,9},{9,13},{2,6},{6,10},{10,14},{3,7},{... | collective-permute-start | bytes 3145736 | tf_op jit(solution)/shard_map/ppermute | solution.py:448
  43.6 0.2 halve.2
  43.8 2.5 %collective-permute-start.7 = (bf16[1,256,768]{2,1,0:T(8,128)(2,1)S(1)}, bf16[1,256,768]{2,1,0:T(8,128)(2,1)S(1)}, u32[]{:S(2)}, u32[]{:S(2)}) collective-permute-start(bf16[1,256,768]{2,1,0:T(8,128)(2,1)S(1)} %get-tuple-element.30), channel_id=1, source_target_pairs={{0,2},{1,3},{2,0},{3,1},{4,6},{5,7},{6,4},{7,5},{8,10},{9,11},{10,... | collective-permute-start | bytes 1179656 | tf_op jit(solution)/shard_map/ppermute | solution.py:417
  46.3 18.0 %collective-permute-done.9.refs_5_.refs_1_ = bf16[1024,512]{1,0:T(8,128)(2,1)} collective-permute-done((bf16[1024,512]{1,0:T(8,128)(2,1)S(1)}, bf16[1024,512]{1,0:T(8,128)(2,1)}, u32[]{:S(2)}, u32[]{:S(2)}) %collective-permute-start.9) | collective-permute-done | bytes 1048608 | tf_op jit(solution)/shard_map/ppermute | solution.py:449
  64.3 1.1 collective-permute-done.8.refs_4_.refs_0_
  65.4 1.6 pre_grads.1
  67.0 0.9 copy-done.3
  67.9 0.9 copy-done.5
  68.8 7.0 %all-to-all-start = ((bf16[4,384,256]{2,1,0:T(8,128)(2,1)}), bf16[4,384,256]{2,1,0:T(8,128)(2,1)}, u32[]{:S(2)}, u32[]{:S(2)}) async-start(bf16[4,384,256]{2,1,0:T(8,128)(2,1)} %copy-done.5), calls=%async_computation | async-start | bytes 1572864 | tf_op jit(solution)/shard_map/all_to_all | solution.py:579
  75.8 2.4 %collective-permute-start.11 = (bf16[8,192,256]{2,1,0:T(8,128)(2,1)}, bf16[8,192,256]{2,1,0:T(8,128)(2,1)}, u32[]{:S(2)}, u32[]{:S(2)}) collective-permute-start(bf16[8,192,256]{2,1,0:T(8,128)(2,1)} %copy-done.3), channel_id=1, source_target_pairs={{0,2},{1,3},{2,0},{3,1},{4,6},{5,7},{6,4},{7,5},{8,10},{9,11},{10,... | collective-permute-start | bytes 2359304 | tf_op jit(solution)/shard_map/ppermute | solution.py:417
  78.2 17.4 %all-to-all-done.refs_0_.refs_2_ = bf16[4,384,256]{2,1,0:T(8,128)(2,1)} async-done(((bf16[4,384,256]{2,1,0:T(8,128)(2,1)}), bf16[4,384,256]{2,1,0:T(8,128)(2,1)}, u32[]{:S(2)}, u32[]{:S(2)}) %all-to-all-start) | async-done | bytes 786464 | tf_op jit(solution)/shard_map/all_to_all | solution.py:579
  95.6 0.7 collective-permute-start.18
  96.3 1.3 collective-permute-start.20
  97.6 0.1 collective-permute-start.10
  97.7 0.5 collective-permute-start.12
  98.2 2.4 %collective-permute-start.16 = (bf16[4,384,256]{2,1,0:T(8,128)(2,1)}, bf16[4,384,256]{2,1,0:T(8,128)(2,1)S(1)}, u32[]{:S(2)}, u32[]{:S(2)}) collective-permute-start(bf16[4,384,256]{2,1,0:T(8,128)(2,1)} %gate.5.refs_0_), channel_id=1, source_target_pairs={{0,2},{1,3},{2,0},{3,1},{4,6},{5,7},{6,4},{7,5},{8,10},{9,11},{10,... | collective-permute-start | bytes 2359304 | tf_op jit(solution)/shard_map/ppermute | solution.py:417
  100.6 0.7 collective-permute-start.19
  101.3 21.2 %collective-permute-done.20.refs_9_ = bf16[1024,512]{1,0:T(8,128)(2,1)S(1)} collective-permute-done((bf16[1024,512]{1,0:T(8,128)(2,1)}, bf16[1024,512]{1,0:T(8,128)(2,1)S(1)}, u32[]{:S(2)}, u32[]{:S(2)}) %collective-permute-start.20) | collective-permute-done | bytes 1048608 | tf_op jit(solution)/shard_map/ppermute | solution.py:449
  122.5 1.3 collective-permute-start.21
  123.8 0.1 collective-permute-start.15
  123.9 0.0 copy-start.4
  123.9 1.1 copy-done.4
  125.0 10.0 %row_grads.1 = (bf16[2,160,512]{2,1,0:T(8,128)(2,1)S(1)}, bf16[2,160,512]{2,1,0:T(8,128)(2,1)S(1)}) custom-call(s32[2]{0:T(128)S(1)} %pad_add_fusion.ids_ref, bf16[8,192,256]{2,1,0:T(8,128)(2,1)S(1)} %copy-done.4, bf16[8,192,256]{2,1,0:T(8,128)(2,1)S(1)} %collective-permute-done.10.refs_1_, bf16[8,192,256]{2,1,0:T(8,128)(2,1)} %collective-permute-done.11.refs_2_.refs_1_, ...), custom_call_target="tpu_custom_call" | custom-call | tf_op jit(solution)/shard_map/row_grads/pallas_call | solution.py:589
  135.1 1.5 collective-permute-start.17
  136.6 2.7 %collective-permute-start.13 = (bf16[2,160,512]{2,1,0:T(8,128)(2,1)S(1)}, bf16[2,160,512]{2,1,0:T(8,128)(2,1)S(1)}, u32[]{:S(2)}, u32[]{:S(2)}) collective-permute-start(bf16[2,160,512]{2,1,0:T(8,128)(2,1)S(1)} %get-tuple-element.35), channel_id=1, source_target_pairs={{0,4},{4,0},{8,12},{12,8},{1,5},{5,1},{9,13},{13,9},{2,6},{6,2},{1... | collective-permute-start | bytes 983048 | tf_op jit(solution)/shard_map/ppermute | solution.py:417
  139.3 15.3 %collective-permute-done.13.got_ref = bf16[2,160,512]{2,1,0:T(8,128)(2,1)S(1)} collective-permute-done((bf16[2,160,512]{2,1,0:T(8,128)(2,1)S(1)}, bf16[2,160,512]{2,1,0:T(8,128)(2,1)S(1)}, u32[]{:S(2)}, u32[]{:S(2)}) %collective-permute-start.13) | collective-permute-done | bytes 327712 | tf_op jit(solution)/shard_map/ppermute | solution.py:417
  154.6 0.1 halve.3
  154.7 0.1 collective-permute-start.14
  154.8 6.4 %down_grads.1 = bf16[16,192,512]{2,1,0:T(8,128)(2,1)} custom-call(s32[2]{0:T(128)S(1)} %pad_add_fusion.ids_ref, s32[4,16]{1,0:T(4,128)S(1)} %bitcast.15, bf16[8,192,256]{2,1,0:T(8,128)(2,1)S(1)} %copy-done.4, bf16[8,192,256]{2,1,0:T(8,128)(2,1)S(1)} %collective-permute-done.10.refs_1_, bf16[8,192,256]{2,1,0:T(8,128)(2,1)} %collective-permute-done.11.refs_2_.refs_1_, ...), custom_call_target="tpu_custom_call" | custom-call | tf_op jit(solution)/shard_map/down_grads/pallas_call | solution.py:636
  161.1 0.6 collective-permute-done.14.refs_1_
  161.7 0.8 token_grads.1
  162.6 7.8 %in_grads.1 = bf16[16,384,512]{2,1,0:T(8,128)(2,1)} custom-call(s32[2]{0:T(128)S(1)} %pad_add_fusion.ids_ref, s32[4,16]{1,0:T(4,128)S(1)} %bitcast.17, bf16[4,384,256]{2,1,0:T(8,128)(2,1)} %gate.5.refs_0_, bf16[4,384,256]{2,1,0:T(8,128)(2,1)S(1)} %collective-permute-done.15.refs_1_, bf16[4,384,256]{2,1,0:T(8,128)(2,1)S(1)} %gate.6.refs_2_, ...), custom_call_target="tpu_custom_call" | custom-call | tf_op jit(solution)/shard_map/in_grads/pallas_call | solution.py:636
  (38 shorter events, 0.1 us)
Async XLA Ops:
  3.2 7.4 %collective-permute-start = (bf16[144,512]{1,0:T(8,128)(2,1)}, bf16[144,512]{1,0:T(8,128)(2,1)S(1)}, u32[]{:S(2)}, u32[]{:S(2)}) collective-permute-start(bf16[144,512]{1,0:T(8,128)(2,1)} %route.1.refs_0_), channel_id=1, source_target_pairs={{0,4},{4,0},{8,12},{12,8},{1,5},{5,1},{9,13},{13,9},{2,6},{6,2},{1... | collective-permute-start | bytes 442376 | tf_op jit(solution)/shard_map/ppermute | solution.py:417
  6.2 15.0 %collective-permute-start.2 = (bf16[144,512]{1,0:T(8,128)(2,1)}, bf16[144,512]{1,0:T(8,128)(2,1)}, u32[]{:S(2)}, u32[]{:S(2)}) collective-permute-start(bf16[144,512]{1,0:T(8,128)(2,1)} %route.1.refs_0_), channel_id=1, source_target_pairs={{0,12},{4,8},{8,4},{12,0},{1,13},{5,9},{9,5},{13,1},{2,14},{6,10},... | collective-permute-start | bytes 442376 | tf_op jit(solution)/shard_map/ppermute | solution.py:417
  8.7 18.8 %collective-permute-start.1 = (bf16[144,512]{1,0:T(8,128)(2,1)}, bf16[144,512]{1,0:T(8,128)(2,1)}, u32[]{:S(2)}, u32[]{:S(2)}) collective-permute-start(bf16[144,512]{1,0:T(8,128)(2,1)} %route.1.refs_0_), channel_id=1, source_target_pairs={{0,8},{4,12},{8,0},{12,4},{1,9},{5,13},{9,1},{13,5},{2,10},{6,14},... | collective-permute-start | bytes 442376 | tf_op jit(solution)/shard_map/ppermute | solution.py:417
  10.6 1.9 %copy-start = (bf16[8,128,1536]{2,1,0:T(8,128)(2,1)S(1)}, bf16[8,128,1536]{2,1,0:T(8,128)(2,1)}, u32[]{:S(2)}) copy-start(bf16[8,128,1536]{2,1,0:T(8,128)(2,1)} %param.17) | copy-start | bytes 9437188
  12.5 17.0 %copy-start.6 = (bf16[144,512]{1,0:T(8,128)(2,1)S(1)}, bf16[144,512]{1,0:T(8,128)(2,1)}, u32[]{:S(2)}) copy-start(bf16[144,512]{1,0:T(8,128)(2,1)} %route.1.refs_0_) | copy-start | bytes 442372
  13.5 14.0 %collective-permute-start.3 = (bf16[192,256]{1,0:T(8,128)(2,1)S(1)}, bf16[192,256]{1,0:T(8,128)(2,1)S(1)}, u32[]{:S(2)}, u32[]{:S(2)}) collective-permute-start(bf16[192,256]{1,0:T(8,128)(2,1)S(1)} %get-tuple-element.24), channel_id=1, source_target_pairs={{0,4},{4,0},{8,12},{12,8},{1,5},{5,1},{9,13},{13,9},{2,6},{6,2},{1... | collective-permute-start | bytes 294920 | tf_op jit(solution)/shard_map/ppermute | solution.py:417
  16.0 13.5 %collective-permute-start.4 = (bf16[192,256]{1,0:T(8,128)(2,1)S(1)}, bf16[192,256]{1,0:T(8,128)(2,1)S(1)}, u32[]{:S(2)}, u32[]{:S(2)}) collective-permute-start(bf16[192,256]{1,0:T(8,128)(2,1)S(1)} %get-tuple-element.25), channel_id=1, source_target_pairs={{0,8},{4,12},{8,0},{12,4},{1,9},{5,13},{9,1},{13,5},{2,10},{6,14},... | collective-permute-start | bytes 294920 | tf_op jit(solution)/shard_map/ppermute | solution.py:417
  19.9 9.5 %collective-permute-start.5 = (bf16[192,256]{1,0:T(8,128)(2,1)S(1)}, bf16[192,256]{1,0:T(8,128)(2,1)S(1)}, u32[]{:S(2)}, u32[]{:S(2)}) collective-permute-start(bf16[192,256]{1,0:T(8,128)(2,1)S(1)} %get-tuple-element.26), channel_id=1, source_target_pairs={{0,12},{4,8},{8,4},{12,0},{1,13},{5,9},{9,5},{13,1},{2,14},{6,10},... | collective-permute-start | bytes 294920 | tf_op jit(solution)/shard_map/ppermute | solution.py:417
  21.2 44.2 %copy-start.1 = (bf16[8,128,1536]{2,1,0:T(8,128)(2,1)S(1)}, bf16[8,128,1536]{2,1,0:T(8,128)(2,1)}, u32[]{:S(2)}) copy-start(bf16[8,128,1536]{2,1,0:T(8,128)(2,1)} %param.17) | copy-start | bytes 9437188
  35.9 0.8 copy-start.7
  36.7 6.8 %collective-permute-start.6 = (bf16[2,256,768]{2,1,0:T(8,128)(2,1)S(1)}, bf16[2,256,768]{2,1,0:T(8,128)(2,1)S(1)}, u32[]{:S(2)}, u32[]{:S(2)}) collective-permute-start(bf16[2,256,768]{2,1,0:T(8,128)(2,1)S(1)} %get-tuple-element.28), channel_id=1, source_target_pairs={{0,1},{1,0},{2,3},{3,2},{4,5},{5,4},{6,7},{7,6},{8,9},{9,8},{10,11... | collective-permute-start | bytes 2359304 | tf_op jit(solution)/shard_map/ppermute | solution.py:417
  36.7 27.6 %collective-permute-start.9 = (bf16[1024,512]{1,0:T(8,128)(2,1)S(1)}, bf16[1024,512]{1,0:T(8,128)(2,1)}, u32[]{:S(2)}, u32[]{:S(2)}) collective-permute-start(bf16[1024,512]{1,0:T(8,128)(2,1)S(1)} %gate.4.refs_5_), channel_id=1, source_target_pairs={{12,8},{8,4},{4,0},{13,9},{9,5},{5,1},{14,10},{10,6},{6,2},{15,11}... | collective-permute-start | bytes 3145736 | tf_op jit(solution)/shard_map/ppermute | solution.py:449
  38.0 27.3 %collective-permute-start.8 = (bf16[1024,512]{1,0:T(8,128)(2,1)S(1)}, bf16[1024,512]{1,0:T(8,128)(2,1)}, u32[]{:S(2)}, u32[]{:S(2)}) collective-permute-start(bf16[1024,512]{1,0:T(8,128)(2,1)S(1)} %gate.4.refs_5_), channel_id=1, source_target_pairs={{0,4},{4,8},{8,12},{1,5},{5,9},{9,13},{2,6},{6,10},{10,14},{3,7},{... | collective-permute-start | bytes 3145736 | tf_op jit(solution)/shard_map/ppermute | solution.py:448
  43.8 21.6 %collective-permute-start.7 = (bf16[1,256,768]{2,1,0:T(8,128)(2,1)S(1)}, bf16[1,256,768]{2,1,0:T(8,128)(2,1)S(1)}, u32[]{:S(2)}, u32[]{:S(2)}) collective-permute-start(bf16[1,256,768]{2,1,0:T(8,128)(2,1)S(1)} %get-tuple-element.30), channel_id=1, source_target_pairs={{0,2},{1,3},{2,0},{3,1},{4,6},{5,7},{6,4},{7,5},{8,10},{9,11},{10,... | collective-permute-start | bytes 1179656 | tf_op jit(solution)/shard_map/ppermute | solution.py:417
  67.0 0.9 copy-start.3
  67.9 0.9 copy-start.5
  68.8 26.8 %all-to-all-start = ((bf16[4,384,256]{2,1,0:T(8,128)(2,1)}), bf16[4,384,256]{2,1,0:T(8,128)(2,1)}, u32[]{:S(2)}, u32[]{:S(2)}) async-start(bf16[4,384,256]{2,1,0:T(8,128)(2,1)} %copy-done.5), calls=%async_computation | async-start | bytes 1572864 | tf_op jit(solution)/shard_map/all_to_all | solution.py:579
  75.8 21.9 %collective-permute-start.11 = (bf16[8,192,256]{2,1,0:T(8,128)(2,1)}, bf16[8,192,256]{2,1,0:T(8,128)(2,1)}, u32[]{:S(2)}, u32[]{:S(2)}) collective-permute-start(bf16[8,192,256]{2,1,0:T(8,128)(2,1)} %copy-done.3), channel_id=1, source_target_pairs={{0,2},{1,3},{2,0},{3,1},{4,6},{5,7},{6,4},{7,5},{8,10},{9,11},{10,... | collective-permute-start | bytes 2359304 | tf_op jit(solution)/shard_map/ppermute | solution.py:417
  95.6 5.0 %collective-permute-start.18 = (bf16[1024,512]{1,0:T(8,128)(2,1)}, bf16[1024,512]{1,0:T(8,128)(2,1)S(1)}, u32[]{:S(2)}, u32[]{:S(2)}) collective-permute-start(bf16[1024,512]{1,0:T(8,128)(2,1)} %get-tuple-element.41.refs_5_), channel_id=1, source_target_pairs={{4,8},{8,12},{5,9},{9,13},{6,10},{10,14},{7,11},{11,15},{20,24},{2... | collective-permute-start | bytes 3145736 | tf_op jit(solution)/shard_map/ppermute | solution.py:448
  96.3 26.2 %collective-permute-start.20 = (bf16[1024,512]{1,0:T(8,128)(2,1)}, bf16[1024,512]{1,0:T(8,128)(2,1)S(1)}, u32[]{:S(2)}, u32[]{:S(2)}) collective-permute-start(bf16[1024,512]{1,0:T(8,128)(2,1)} %get-tuple-element.42.refs_8_), channel_id=1, source_target_pairs={{8,4},{4,0},{9,5},{5,1},{10,6},{6,2},{11,7},{7,3},{24,20},{20,16},... | collective-permute-start | bytes 3145736 | tf_op jit(solution)/shard_map/ppermute | solution.py:449
  97.6 26.2 %collective-permute-start.10 = (bf16[8,192,256]{2,1,0:T(8,128)(2,1)}, bf16[8,192,256]{2,1,0:T(8,128)(2,1)S(1)}, u32[]{:S(2)}, u32[]{:S(2)}) collective-permute-start(bf16[8,192,256]{2,1,0:T(8,128)(2,1)} %copy-done.3), channel_id=1, source_target_pairs={{0,1},{1,0},{2,3},{3,2},{4,5},{5,4},{6,7},{7,6},{8,9},{9,8},{10,11... | collective-permute-start | bytes 2359304 | tf_op jit(solution)/shard_map/ppermute | solution.py:417
  97.7 26.2 %collective-permute-start.12 = (bf16[8,192,256]{2,1,0:T(8,128)(2,1)}, bf16[8,192,256]{2,1,0:T(8,128)(2,1)S(1)}, u32[]{:S(2)}, u32[]{:S(2)}) collective-permute-start(bf16[8,192,256]{2,1,0:T(8,128)(2,1)} %collective-permute-done.11.refs_2_.refs_1_), channel_id=1, source_target_pairs={{0,1},{1,0},{2,3},{3,2},{4,5},{5,4},{6,7},{7,6},{8,9},{9,8},{10,11... | collective-permute-start | bytes 2359304 | tf_op jit(solution)/shard_map/ppermute | solution.py:417
  98.2 56.6 %copy-start.8 = (bf16[4,128,512]{2,1,0:T(8,128)(2,1)S(1)}, bf16[4,128,512]{2,1,0:T(8,128)(2,1)}, u32[]{:S(2)}) copy-start(bf16[4,128,512]{2,1,0:T(8,128)(2,1)} %copy-done.7) | copy-start | bytes 1572868
  98.2 56.6 %copy-start.9 = (s32[16,4]{0,1:T(4,128)S(1)}, s32[16,4]{0,1:T(4,128)}, u32[]{:S(2)}) copy-start(s32[16,4]{0,1:T(4,128)} %param.14) | copy-start | bytes 772
  98.2 36.9 %collective-permute-start.16 = (bf16[4,384,256]{2,1,0:T(8,128)(2,1)}, bf16[4,384,256]{2,1,0:T(8,128)(2,1)S(1)}, u32[]{:S(2)}, u32[]{:S(2)}) collective-permute-start(bf16[4,384,256]{2,1,0:T(8,128)(2,1)} %gate.5.refs_0_), channel_id=1, source_target_pairs={{0,2},{1,3},{2,0},{3,1},{4,6},{5,7},{6,4},{7,5},{8,10},{9,11},{10,... | collective-permute-start | bytes 2359304 | tf_op jit(solution)/shard_map/ppermute | solution.py:417
  100.6 61.9 %collective-permute-start.19 = (bf16[1024,512]{1,0:T(8,128)(2,1)S(1)}, bf16[1024,512]{1,0:T(8,128)(2,1)S(1)}, u32[]{:S(2)}, u32[]{:S(2)}) collective-permute-start(bf16[1024,512]{1,0:T(8,128)(2,1)S(1)} %collective-permute-done.18.refs_6_), channel_id=1, source_target_pairs={{8,12},{9,13},{10,14},{11,15},{24,28},{25,29},{26,30},{27,31}} | collective-permute-start | bytes 3145736 | tf_op jit(solution)/shard_map/ppermute | solution.py:448
  122.5 40.0 %collective-permute-start.21 = (bf16[1024,512]{1,0:T(8,128)(2,1)S(1)}, bf16[1024,512]{1,0:T(8,128)(2,1)S(1)}, u32[]{:S(2)}, u32[]{:S(2)}) collective-permute-start(bf16[1024,512]{1,0:T(8,128)(2,1)S(1)} %collective-permute-done.20.refs_9_), channel_id=1, source_target_pairs={{4,0},{5,1},{6,2},{7,3},{20,16},{21,17},{22,18},{23,19}} | collective-permute-start | bytes 3145736 | tf_op jit(solution)/shard_map/ppermute | solution.py:449
  123.8 38.7 %collective-permute-start.15 = (bf16[4,384,256]{2,1,0:T(8,128)(2,1)}, bf16[4,384,256]{2,1,0:T(8,128)(2,1)S(1)}, u32[]{:S(2)}, u32[]{:S(2)}) collective-permute-start(bf16[4,384,256]{2,1,0:T(8,128)(2,1)} %gate.5.refs_0_), channel_id=1, source_target_pairs={{0,1},{1,0},{2,3},{3,2},{4,5},{5,4},{6,7},{7,6},{8,9},{9,8},{10,11... | collective-permute-start | bytes 2359304 | tf_op jit(solution)/shard_map/ppermute | solution.py:417
  123.9 1.1 copy-start.4
  135.1 26.7 %copy-start.10 = (s32[128,8]{0,1:T(8,128)S(1)}, s32[128,8]{0,1:T(8,128)}, u32[]{:S(2)}) copy-start(s32[128,8]{0,1:T(8,128)} %param.12) | copy-start | bytes 12292
  135.1 26.6 %copy-start.11 = (s32[128,8]{0,1:T(8,128)S(1)}, s32[128,8]{0,1:T(8,128)}, u32[]{:S(2)}) copy-start(s32[128,8]{0,1:T(8,128)} %param.13) | copy-start | bytes 12292
  135.1 27.5 %copy-start.2 = (bf16[8,4,32,512]{3,2,1,0:T(8,128)(2,1)S(1)}, bf16[8,4,32,512]{3,2,1,0:T(8,128)(2,1)}, u32[]{:S(2)}) copy-start(bf16[8,4,32,512]{3,2,1,0:T(8,128)(2,1)} %param.16) | copy-start | bytes 3145732
  135.1 27.4 %collective-permute-start.17 = (bf16[4,384,256]{2,1,0:T(8,128)(2,1)S(1)}, bf16[4,384,256]{2,1,0:T(8,128)(2,1)S(1)}, u32[]{:S(2)}, u32[]{:S(2)}) collective-permute-start(bf16[4,384,256]{2,1,0:T(8,128)(2,1)S(1)} %gate.6.refs_2_), channel_id=1, source_target_pairs={{0,1},{1,0},{2,3},{3,2},{4,5},{5,4},{6,7},{7,6},{8,9},{9,8},{10,11... | collective-permute-start | bytes 2359304 | tf_op jit(solution)/shard_map/ppermute | solution.py:417
  136.6 18.0 %collective-permute-start.13 = (bf16[2,160,512]{2,1,0:T(8,128)(2,1)S(1)}, bf16[2,160,512]{2,1,0:T(8,128)(2,1)S(1)}, u32[]{:S(2)}, u32[]{:S(2)}) collective-permute-start(bf16[2,160,512]{2,1,0:T(8,128)(2,1)S(1)} %get-tuple-element.35), channel_id=1, source_target_pairs={{0,4},{4,0},{8,12},{12,8},{1,5},{5,1},{9,13},{13,9},{2,6},{6,2},{1... | collective-permute-start | bytes 983048 | tf_op jit(solution)/shard_map/ppermute | solution.py:417
  154.7 7.0 %collective-permute-start.14 = (bf16[1,160,512]{2,1,0:T(8,128)(2,1)S(1)}, bf16[1,160,512]{2,1,0:T(8,128)(2,1)S(1)}, u32[]{:S(2)}, u32[]{:S(2)}) collective-permute-start(bf16[1,160,512]{2,1,0:T(8,128)(2,1)S(1)} %get-tuple-element.37), channel_id=1, source_target_pairs={{0,8},{4,12},{8,0},{12,4},{1,9},{5,13},{9,1},{13,5},{2,10},{6,14},... | collective-permute-start | bytes 491528 | tf_op jit(solution)/shard_map/ppermute | solution.py:417

commit v7 on v6

--- a/solution.py
+++ b/solution.py
@@ -105,7 +105,7 @@
         ]
 
 
-def hidden_kernel(z, ids_ref, pair_ref, after_ref, *refs):
+def hidden_kernel(z, ids_ref, pair_ref, after_ref, other_ref, *refs):
     outs, sides = refs[:-1], refs[-1]
     pair = pair_ref[...]
     gate_pre = pair[:, : z.hidden].astype(F32)
@@ -157,8 +157,8 @@
 def down_kernel(z, ids_ref, *refs):
     bufs = refs[: z.ep]
     weight_ref = refs[z.ep]
-    parts = refs[z.ep + 2 : z.ep + 4]
-    grads_ref, codes_ref, rows_ref, held, sems = refs[z.ep + 4 :]
+    parts = refs[2 * z.ep : 2 * z.ep + 2]
+    grads_ref, codes_ref, rows_ref, held, sems = refs[2 * z.ep + 2 :]
     me, mine = ids_ref[0], ids_ref[1]
     step = pl.program_id(0)
 
@@ -208,8 +208,8 @@
 
 
 def pre_kernel(z, ids_ref, keep_ref, got_ref, pair_ref, codes_ref, *refs):
-    downs = refs[: z.ep]
-    out_ref, bundle_ref = refs[-2:]
+    downs, outs = refs[: z.ep], refs[z.ep : 2 * z.ep]
+    bundle_ref, sides = refs[2 * z.ep :]
 
     @pl.when(pl.program_id(0) == 0)
     def _():
@@ -230,7 +230,14 @@
     _, grad_gate, grad_up = gate_terms(z, pair_ref[...], grad, scale)
     pre = jnp.concatenate([grad_gate.T, grad_up.T], axis=0)
     for q in range(z.ep):
-        out_ref[q] = pre[q * z.in_cols : (q + 1) * z.in_cols, :]
+        sides[q] = pre[q * z.in_cols : (q + 1) * z.in_cols, :]
+    for k in range(z.ep):
+        outs[k][...] = sides[me ^ k]
+
+
+def stack_kernel(*refs):
+    for i, ref in enumerate(refs[:-1]):
+        refs[-1][i] = ref[...]
 
 
 def row_kernel(z, ids_ref, *refs):
@@ -410,7 +417,7 @@
         start = pl.multiple_of(block * z.block, z.block)
         return inputs_ref[slot_id // z.local, pl.ds(start, z.block), :]
 
-    expert_products(z, ids_ref, table_ref, 0, held, right_rows, out_ref, made, out_sems)
+    expert_products(z, ids_ref, table_ref, ids_ref[0], held, right_rows, out_ref, made, out_sems)
 
 
 def swap(x, axis, size, bit):
@@ -484,6 +491,7 @@
     )(token_count, *routing)
     bufs = [buf] + [swap(buf, "ep", n, k) for k in range(1, n)]
 
+    chain = gate([inputs], [buf])
     downs = pl.pallas_call(
         functools.partial(hidden_kernel, z),
         grid_spec=pltpu.PrefetchScalarGridSpec(
@@ -492,6 +500,7 @@
             in_specs=[
                 pl.BlockSpec((z.block, z.pair), lambda i, r: (r[1] * z.part_blocks + i, 0)),
                 pl.BlockSpec(memory_space=pl.ANY),
+                pl.BlockSpec(memory_space=pl.ANY),
             ],
             out_specs=[pl.BlockSpec((z.down_cols, z.block), lambda i, r: (0, i))] * n,
             scratch_shapes=[pltpu.VMEM((n, z.down_cols, z.block), BF)],
@@ -499,8 +508,20 @@
         out_shape=[jax.ShapeDtypeStruct((z.down_cols, z.part), BF)] * n,
         compiler_params=params(16),
         name="hidden_columns",
-    )(ids, pair_rows, bufs[1])
+    )(ids, pair_rows, bufs[1], chain[0])
     downs = [downs[0]] + [swap(downs[k], "ep", n, k) for k in range(1, n)]
+
+    def stack(pieces):
+        shape = pieces[0].shape
+        return pl.pallas_call(
+            stack_kernel,
+            in_specs=[whole(shape)] * n,
+            out_specs=whole((n,) + shape),
+            out_shape=jax.ShapeDtypeStruct((n,) + shape, BF),
+            grid=(1,),
+            compiler_params=params(8),
+            name="stack_columns",
+        )(*pieces)
 
     def halve(keep, got):
         half = (keep.shape[0] // 2,) + keep.shape[1:]
@@ -518,9 +539,6 @@
         place = i // z.part_blocks
         return (place ^ ids_ref[1]) * z.part_blocks + i % z.part_blocks
 
-    chain = gate([inputs], bufs[1:] + downs[1:])
-    steps = [chain_step(chain[0], chain[0], "ep", n, 1)]
-
     part_shape = (m // 2, z.part, z.hidden)
     outs = pl.pallas_call(
         functools.partial(down_kernel, z),
@@ -528,7 +546,8 @@
             num_scalar_prefetch=1,
             grid=(z.blocks,),
             in_specs=[whole(grad_shape)] * n
-            + [pl.BlockSpec(memory_space=pltpu.HBM), pl.BlockSpec(memory_space=pl.ANY)],
+            + [pl.BlockSpec(memory_space=pltpu.HBM)]
+            + [pl.BlockSpec(memory_space=pl.ANY)] * (n - 1),
             out_specs=[whole(part_shape)] * 2
             + [whole((n, z.tokens, z.width)), whole(code_shape)],
             scratch_shapes=[
@@ -544,15 +563,17 @@
         ],
         compiler_params=params(48),
         name="hidden_partials",
-    )(ids, *bufs, weight_down, chain[0])
+    )(ids, *bufs, weight_down, *downs[1:])
     keep, send, grads_all, codes = outs
+    chain = gate(chain, downs[1:])
+    steps = [chain_step(chain[0], chain[0], "ep", n, 1)]
     got = swap(send, "sub", m, 1)
     bit = 2
     while bit < m:
         keep, send = halve(keep, got)
         got = swap(send, "sub", m, bit)
         bit *= 2
-    pre, bundle = pl.pallas_call(
+    *pieces, bundle = pl.pallas_call(
         functools.partial(pre_kernel, z),
         grid_spec=pltpu.PrefetchScalarGridSpec(
             num_scalar_prefetch=1,
@@ -562,28 +583,24 @@
                 pl.BlockSpec((z.block, z.pair), lambda i, r: (r[1] * z.part_blocks + i, 0)),
                 whole(code_shape),
             ]
-            + [whole((z.down_cols, z.part))] * n
-            + [pl.BlockSpec(memory_space=pl.ANY)] * 2,
-            out_specs=[
-                pl.BlockSpec((n, z.in_cols, z.block), lambda i, r: (0, 0, i)),
-                whole((2 * n, z.down_cols, z.part)),
-            ],
+            + [whole((z.down_cols, z.part))] * n,
+            out_specs=[pl.BlockSpec((z.in_cols, z.block), lambda i, r: (0, i))] * n
+            + [whole((2 * n, z.down_cols, z.part))],
+            scratch_shapes=[pltpu.VMEM((n, z.in_cols, z.block), BF)],
         ),
-        out_shape=[
-            jax.ShapeDtypeStruct((n, z.in_cols, z.part), BF),
-            jax.ShapeDtypeStruct((2 * n, z.down_cols, z.part), BF),
-        ],
+        out_shape=[jax.ShapeDtypeStruct((z.in_cols, z.part), BF)] * n
+        + [jax.ShapeDtypeStruct((2 * n, z.down_cols, z.part), BF)],
         compiler_params=params(16),
         name="pre_grads",
-    )(ids, keep, got, pair_rows, codes, *downs, *steps[0])
-    columns = lax.all_to_all(pre, "ep", split_axis=0, concat_axis=0, tiled=True)
-    steps[0] = gate(steps[0], [columns])
-    for d in range(2, n):
-        steps.append(chain_step(*steps[-1], "ep", n, d))
+    )(ids, keep, got, pair_rows, codes, *downs)
+    pieces = [pieces[0]] + [swap(pieces[k], "ep", n, k) for k in range(1, n)]
+    columns = stack(pieces)
+    bundle = gate([bundle], pieces[1:2])[0]
+    steps[0] = gate(steps[0], pieces[1:])
+    steps.append(chain_step(*steps[0], "ep", n, 2))
     bundles = spread_over({0: bundle}, "sub", m, m // 2)
     sides = {0: gate([columns], [bundles[m // 2]])[0]}
     sides[m // 2] = swap(sides[0], "sub", m, m // 2)
-    gathered = [inputs] + [go for go, _ in steps] + [back for _, back in steps]
 
     back_shape = (n // 2, z.tokens + z.slots, z.width)
     keep, send = pl.pallas_call(
@@ -610,6 +627,10 @@
         compiler_params=params(46),
         name="row_grads",
     )(ids, *bundles, pair_rows, weight_in, codes)
+    steps[1] = gate(steps[1], [keep])
+    for d in range(3, n):
+        steps.append(chain_step(*steps[-1], "ep", n, d))
+    gathered = [inputs] + [go for go, _ in steps] + [back for _, back in steps]
     sides[m // 2] = gate([sides[m // 2]], [keep])[0]
     sides = spread_over(sides, "sub", m, m // 4)
     got = swap(send, "ep", n, 1)

time: 171 us -> 173 us (1.012)
  waiting for transfers between devices: 83.5 us -> 97.7 us
  starting transfers between devices: 42.2 us -> 36.2 us
  local copies, waits for them, and re-layouts: 6.82 us -> 2.17 us
    ppermute x16 -> x19, waiting for transfers between devices: 25.8 us -> 79.9 us  [swap(): return lax.ppermute(x, axis, [(i, i ^ bit) for i in range(size)])]
    ppermute x3, waiting for transfers between devices: 39.2 us -> 17.8 us  [chain_step(): lax.ppermute(back, axis, [(i, i - 1) for i in range(size - d, 0, -1)])]
    all_to_all x1 -> x0, waiting for transfers between devices: 17.4 us -> none  [body(): columns = lax.all_to_all(pre, 'ep', split_axis=0, concat_axis=0, tiled=True)]
    all_to_all x1 -> x0, starting transfers between devices: 7.01 us -> none  [body(): columns = lax.all_to_all(pre, 'ep', split_axis=0, concat_axis=0, tiled=True)]
    unnamed x25 -> x15, local copies, waits for them, and re-layouts: 6.82 us -> 2.17 us
    ppermute x16 -> x19, starting transfers between devices: 24.3 us -> 26.3 us  [swap(): return lax.ppermute(x, axis, [(i, i ^ bit) for i in range(size)])]
  transfers between devices with their start and end apart: 23 -> 25, of which waited for: 9 -> 11; matrix products, arithmetic and copies ran while one was open for 1% -> 1% of each run, Pallas kernels for 11% -> 11%
where the time goes in v7:
time: 173 us
  waiting for transfers between devices  97.7 us (56%)
  starting transfers between devices  36.2 us (21%)
  Pallas kernels  34.6 us (20%)
  local copies, waits for them, and re-layouts  2.17 us (1%)
    ppermute x19, waiting for transfers between devices, swap(): return lax.ppermute(x, axis, [(i, i ^ bit) for i in range(size)])  79.9 us
    ppermute x19, starting transfers between devices, swap(): return lax.ppermute(x, axis, [(i, i ^ bit) for i in range(size)])  26.3 us
    ppermute x3, waiting for transfers between devices, chain_step(): lax.ppermute(back, axis, [(i, i - 1) for i in range(size - d, 0, -1)])  17.8 us
    pallas_call x2, Pallas kernels, total_call(): pl.pallas_call(functools.partial(kernel, z), grid_spec=pltpu.PrefetchScal...  13.4 us
    pallas_call x1, Pallas kernels, body(): pl.pallas_call(functools.partial(row_kernel, z), grid_spec=pltpu.Prefetch...  8.91 us
    pallas_call x1, Pallas kernels, body(): pl.pallas_call(functools.partial(down_kernel, z), grid_spec=pltpu.Prefetc...  6.4 us
    ppermute x3, starting transfers between devices, chain_step(): go = lax.ppermute(go, axis, [(i, i + 1) for i in range(d - 1, size - 1)])  6.05 us
    ppermute x3, starting transfers between devices, chain_step(): lax.ppermute(back, axis, [(i, i - 1) for i in range(size - d, 0, -1)])  3.86 us
  transfers between devices with their start and end apart: 25, of which 11 were waited for; matrix products, arithmetic and copies ran while one was open for 1% of the time, Pallas kernels for 11%

profile of v7, /device:TPU:0, one launch (start us, length us, event | category | flops | bytes accessed | tf_op | source)
XLA Modules:
  0.0 172.5 jit_solution(10876506061816854869)
XLA Ops:
  1.4 2.0 %route.1.refs_1_.refs_0_ = bf16[144,512]{1,0:T(8,128)(2,1)} custom-call(s32[1]{0:T(128)S(6)} %copy.32.count_ref, bf16[128,512]{1,0:T(8,128)(2,1)} %grad_ref.1, bf16[8,128]{1,0:T(8,128)(2,1)} %bitcast.22, s32[8,128]{1,0:T(8,128)} %bitcast.18, s32[8,128]{1,0:T(8,128)} %bitcast.20, s32[4,16]{1,0:T(4,128)} %bitcast.14), custom_call_target="tpu_custom_call" | custom-call | tf_op jit(solution)/shard_map/route/pallas_call | solution.py:483
  3.5 3.0 %collective-permute-start = (bf16[144,512]{1,0:T(8,128)(2,1)}, bf16[144,512]{1,0:T(8,128)(2,1)S(1)}, u32[]{:S(2)}, u32[]{:S(2)}) collective-permute-start(bf16[144,512]{1,0:T(8,128)(2,1)} %route.1.refs_1_.refs_0_), channel_id=1, source_target_pairs={{0,4},{4,0},{8,12},{12,8},{1,5},{5,1},{9,13},{13,9},{2,6},{6,2},{1... | collective-permute-start | bytes 442376 | tf_op jit(solution)/shard_map/ppermute | solution.py:424
  6.5 2.5 %collective-permute-start.2 = (bf16[144,512]{1,0:T(8,128)(2,1)}, bf16[144,512]{1,0:T(8,128)(2,1)S(1)}, u32[]{:S(2)}, u32[]{:S(2)}) collective-permute-start(bf16[144,512]{1,0:T(8,128)(2,1)} %route.1.refs_1_.refs_0_), channel_id=1, source_target_pairs={{0,12},{4,8},{8,4},{12,0},{1,13},{5,9},{9,5},{13,1},{2,14},{6,10},... | collective-permute-start | bytes 442376 | tf_op jit(solution)/shard_map/ppermute | solution.py:424
  9.0 0.1 collective-permute-start.1
  9.1 0.1 pad_add_fusion.ids_ref
  9.2 1.2 copy.23.refs_0_
  10.4 0.9 copy-done.2
  11.3 1.1 hidden_columns.1
  12.4 2.0 %collective-permute-start.3 = (bf16[192,256]{1,0:T(8,128)(2,1)S(1)}, bf16[192,256]{1,0:T(8,128)(2,1)S(1)}, u32[]{:S(2)}, u32[]{:S(2)}) collective-permute-start(bf16[192,256]{1,0:T(8,128)(2,1)S(1)} %get-tuple-element.29), channel_id=1, source_target_pairs={{0,4},{4,0},{8,12},{12,8},{1,5},{5,1},{9,13},{13,9},{2,6},{6,2},{1... | collective-permute-start | bytes 294920 | tf_op jit(solution)/shard_map/ppermute | solution.py:424
  14.4 4.0 %collective-permute-start.4 = (bf16[192,256]{1,0:T(8,128)(2,1)S(1)}, bf16[192,256]{1,0:T(8,128)(2,1)S(1)}, u32[]{:S(2)}, u32[]{:S(2)}) collective-permute-start(bf16[192,256]{1,0:T(8,128)(2,1)S(1)} %get-tuple-element.30), channel_id=1, source_target_pairs={{0,8},{4,12},{8,0},{12,4},{1,9},{5,13},{9,1},{13,5},{2,10},{6,14},... | collective-permute-start | bytes 294920 | tf_op jit(solution)/shard_map/ppermute | solution.py:424
  18.4 9.4 %collective-permute-done.1.refs_2_ = bf16[144,512]{1,0:T(8,128)(2,1)} collective-permute-done((bf16[144,512]{1,0:T(8,128)(2,1)}, bf16[144,512]{1,0:T(8,128)(2,1)}, u32[]{:S(2)}, u32[]{:S(2)}) %collective-permute-start.1) | collective-permute-done | bytes 147488 | tf_op jit(solution)/shard_map/ppermute | solution.py:424
  27.8 1.9 %collective-permute-done.4.refs_6_.refs_2_ = bf16[192,256]{1,0:T(8,128)(2,1)S(1)} collective-permute-done((bf16[192,256]{1,0:T(8,128)(2,1)S(1)}, bf16[192,256]{1,0:T(8,128)(2,1)S(1)}, u32[]{:S(2)}, u32[]{:S(2)}) %collective-permute-start.4) | collective-permute-done | bytes 98336 | tf_op jit(solution)/shard_map/ppermute | solution.py:424
  29.8 6.4 %hidden_partials.1 = (bf16[2,256,768]{2,1,0:T(8,128)(2,1)S(1)}, bf16[2,256,768]{2,1,0:T(8,128)(2,1)S(1)}, bf16[4,128,512]{2,1,0:T(8,128)(2,1)S(1)}, f32[4,64,128]{2,1,0:T(8,128)S(1)}) custom-call(s32[2]{0:T(128)S(1)} %pad_add_fusion.ids_ref, bf16[144,512]{1,0:T(8,128)(2,1)S(1)} %copy-done.3, bf16[144,512]{1,0:T(8,128)(2,1)S(1)} %collective-permute-done.after_ref.refs_1_, ...), custom_call_target="tpu_custom_call" | custom-call | tf_op jit(solution)/shard_map/hidden_partials/pallas_call | solution.py:543
  36.2 0.1 collective-permute-start.6
  36.2 2.3 %collective-permute-done.6.got_ref = bf16[2,256,768]{2,1,0:T(8,128)(2,1)S(1)} collective-permute-done((bf16[2,256,768]{2,1,0:T(8,128)(2,1)S(1)}, bf16[2,256,768]{2,1,0:T(8,128)(2,1)S(1)}, u32[]{:S(2)}, u32[]{:S(2)}) %collective-permute-start.6) | collective-permute-done | bytes 786464 | tf_op jit(solution)/shard_map/ppermute | solution.py:424
  38.5 0.2 halve.2
  38.7 2.5 %collective-permute-start.7 = (bf16[1,256,768]{2,1,0:T(8,128)(2,1)S(1)}, bf16[1,256,768]{2,1,0:T(8,128)(2,1)S(1)}, u32[]{:S(2)}, u32[]{:S(2)}) collective-permute-start(bf16[1,256,768]{2,1,0:T(8,128)(2,1)S(1)} %get-tuple-element.35), channel_id=1, source_target_pairs={{0,2},{1,3},{2,0},{3,1},{4,6},{5,7},{6,4},{7,5},{8,10},{9,11},{10,... | collective-permute-start | bytes 1179656 | tf_op jit(solution)/shard_map/ppermute | solution.py:424
  41.2 1.3 collective-permute-start.20
  42.5 4.6 %collective-permute-start.19 = (bf16[1024,512]{1,0:T(8,128)(2,1)S(1)}, bf16[1024,512]{1,0:T(8,128)(2,1)S(1)}, u32[]{:S(2)}, u32[]{:S(2)}) collective-permute-start(bf16[1024,512]{1,0:T(8,128)(2,1)S(1)} %gate.11), channel_id=1, source_target_pairs={{0,4},{4,8},{8,12},{1,5},{5,9},{9,13},{2,6},{6,10},{10,14},{3,7},{... | collective-permute-start | bytes 3145736 | tf_op jit(solution)/shard_map/ppermute | solution.py:455
  47.1 3.5 %collective-permute-done.7.got_ref = bf16[1,256,768]{2,1,0:T(8,128)(2,1)S(1)} collective-permute-done((bf16[1,256,768]{2,1,0:T(8,128)(2,1)S(1)}, bf16[1,256,768]{2,1,0:T(8,128)(2,1)S(1)}, u32[]{:S(2)}, u32[]{:S(2)}) %collective-permute-start.7) | collective-permute-done | bytes 393248 | tf_op jit(solution)/shard_map/ppermute | solution.py:424
  50.6 1.7 pre_grads.1
  52.3 1.7 collective-permute-start.8
  54.0 19.4 %collective-permute-done.8.refs_1_.refs_2_ = bf16[384,256]{1,0:T(8,128)(2,1)S(1)} collective-permute-done((bf16[384,256]{1,0:T(8,128)(2,1)S(1)}, bf16[384,256]{1,0:T(8,128)(2,1)S(1)}, u32[]{:S(2)}, u32[]{:S(2)}) %collective-permute-start.8) | collective-permute-done | bytes 196640 | tf_op jit(solution)/shard_map/ppermute | solution.py:424
  73.4 0.3 collective-permute-start.10
  73.7 2.8 %collective-permute-start.14 = (bf16[384,256]{1,0:T(8,128)(2,1)S(1)}, bf16[384,256]{1,0:T(8,128)(2,1)S(1)}, u32[]{:S(2)}, u32[]{:S(2)}) collective-permute-start(bf16[384,256]{1,0:T(8,128)(2,1)S(1)} %get-tuple-element.47), channel_id=1, source_target_pairs={{0,8},{4,12},{8,0},{12,4},{1,9},{5,13},{9,1},{13,5},{2,10},{6,14},... | collective-permute-start | bytes 589832 | tf_op jit(solution)/shard_map/ppermute | solution.py:424
  76.5 2.0 %collective-permute-start.15 = (bf16[384,256]{1,0:T(8,128)(2,1)S(1)}, bf16[384,256]{1,0:T(8,128)(2,1)S(1)}, u32[]{:S(2)}, u32[]{:S(2)}) collective-permute-start(bf16[384,256]{1,0:T(8,128)(2,1)S(1)} %get-tuple-element.48), channel_id=1, source_target_pairs={{0,12},{4,8},{8,4},{12,0},{1,13},{5,9},{9,5},{13,1},{2,14},{6,10},... | collective-permute-start | bytes 589832 | tf_op jit(solution)/shard_map/ppermute | solution.py:424
  78.6 12.2 %collective-permute-done.14.refs_2_.refs_3_ = bf16[384,256]{1,0:T(8,128)(2,1)S(1)} collective-permute-done((bf16[384,256]{1,0:T(8,128)(2,1)S(1)}, bf16[384,256]{1,0:T(8,128)(2,1)S(1)}, u32[]{:S(2)}, u32[]{:S(2)}) %collective-permute-start.14) | collective-permute-done | bytes 196640 | tf_op jit(solution)/shard_map/ppermute | solution.py:424
  90.8 0.7 collective-permute-start.21
  91.5 1.3 collective-permute-start.22
  92.8 0.1 collective-permute-start.9
  92.9 0.5 collective-permute-start.11
  93.5 1.5 collective-permute-start.17
  94.9 0.2 collective-permute-done.9.refs_1_
  95.2 1.1 collective-permute-done.11.refs_3_
  96.3 8.9 %row_grads.1 = (bf16[2,160,512]{2,1,0:T(8,128)(2,1)S(1)}, bf16[2,160,512]{2,1,0:T(8,128)(2,1)S(1)}) custom-call(s32[2]{0:T(128)S(1)} %pad_add_fusion.ids_ref, bf16[8,192,256]{2,1,0:T(8,128)(2,1)S(1)} %gate.8.refs_0_, bf16[8,192,256]{2,1,0:T(8,128)(2,1)S(1)} %collective-permute-done.9.refs_1_, ...), custom_call_target="tpu_custom_call" | custom-call | tf_op jit(solution)/shard_map/row_grads/pallas_call | solution.py:606
  105.3 17.8 %collective-permute-done.22.refs_1_ = bf16[1024,512]{1,0:T(8,128)(2,1)S(1)} collective-permute-done((bf16[1024,512]{1,0:T(8,128)(2,1)S(1)}, bf16[1024,512]{1,0:T(8,128)(2,1)S(1)}, u32[]{:S(2)}, u32[]{:S(2)}) %collective-permute-start.22) | collective-permute-done | bytes 1048608 | tf_op jit(solution)/shard_map/ppermute | solution.py:456
  123.1 0.7 collective-permute-start.23
  123.8 1.3 collective-permute-start.24
  125.1 0.1 collective-permute-start.16
  125.2 0.5 collective-permute-start.18
  125.7 2.7 %collective-permute-start.12 = (bf16[2,160,512]{2,1,0:T(8,128)(2,1)S(1)}, bf16[2,160,512]{2,1,0:T(8,128)(2,1)S(1)}, u32[]{:S(2)}, u32[]{:S(2)}) collective-permute-start(bf16[2,160,512]{2,1,0:T(8,128)(2,1)S(1)} %get-tuple-element.41), channel_id=1, source_target_pairs={{0,4},{4,0},{8,12},{12,8},{1,5},{5,1},{9,13},{13,9},{2,6},{6,2},{1... | collective-permute-start | bytes 983048 | tf_op jit(solution)/shard_map/ppermute | solution.py:424
  128.4 28.6 %collective-permute-done.12.got_ref = bf16[2,160,512]{2,1,0:T(8,128)(2,1)S(1)} collective-permute-done((bf16[2,160,512]{2,1,0:T(8,128)(2,1)S(1)}, bf16[2,160,512]{2,1,0:T(8,128)(2,1)S(1)}, u32[]{:S(2)}, u32[]{:S(2)}) %collective-permute-start.12) | collective-permute-done | bytes 327712 | tf_op jit(solution)/shard_map/ppermute | solution.py:424
  157.0 0.1 halve.3
  157.0 0.1 collective-permute-start.13
  157.1 6.5 %down_grads.1 = bf16[16,192,512]{2,1,0:T(8,128)(2,1)} custom-call(s32[2]{0:T(128)S(1)} %pad_add_fusion.ids_ref, s32[4,16]{1,0:T(4,128)S(1)} %bitcast.15, bf16[8,192,256]{2,1,0:T(8,128)(2,1)S(1)} %gate.8.refs_0_, bf16[8,192,256]{2,1,0:T(8,128)(2,1)S(1)} %collective-permute-done.9.refs_1_, bf16[8,192,256]{2,1,0:T(8,128)(2,1)S(1)} %collective-permute-done.10.refs_2_.refs_1_, ...), custom_call_target="tpu_custom_call" | custom-call | tf_op jit(solution)/shard_map/down_grads/pallas_call | solution.py:657
  163.7 1.2 collective-permute-done.13.refs_1_
  164.8 0.8 token_grads.1
  165.7 6.9 %in_grads.1 = bf16[16,384,512]{2,1,0:T(8,128)(2,1)} custom-call(s32[2]{0:T(128)S(1)} %pad_add_fusion.ids_ref, s32[4,16]{1,0:T(4,128)S(1)} %bitcast.17, bf16[4,384,256]{2,1,0:T(8,128)(2,1)S(1)} %gate.9.refs_0_, bf16[4,384,256]{2,1,0:T(8,128)(2,1)S(1)} %collective-permute-done.16.refs_1_, bf16[4,384,256]{2,1,0:T(8,128)(2,1)S(1)} %gate.10.refs_2_, ...), custom_call_target="tpu_custom_call" | custom-call | tf_op jit(solution)/shard_map/in_grads/pallas_call | solution.py:657
  (36 shorter events, 0.1 us)
Async XLA Ops:
  0.6 10.7 %copy-start = (bf16[8,128,1536]{2,1,0:T(8,128)(2,1)S(1)}, bf16[8,128,1536]{2,1,0:T(8,128)(2,1)}, u32[]{:S(2)}) copy-start(bf16[8,128,1536]{2,1,0:T(8,128)(2,1)} %param.17) | copy-start | bytes 9437188
  3.5 7.8 %collective-permute-start = (bf16[144,512]{1,0:T(8,128)(2,1)}, bf16[144,512]{1,0:T(8,128)(2,1)S(1)}, u32[]{:S(2)}, u32[]{:S(2)}) collective-permute-start(bf16[144,512]{1,0:T(8,128)(2,1)} %route.1.refs_1_.refs_0_), channel_id=1, source_target_pairs={{0,4},{4,0},{8,12},{12,8},{1,5},{5,1},{9,13},{13,9},{2,6},{6,2},{1... | collective-permute-start | bytes 442376 | tf_op jit(solution)/shard_map/ppermute | solution.py:424
  6.5 11.9 %collective-permute-start.2 = (bf16[144,512]{1,0:T(8,128)(2,1)}, bf16[144,512]{1,0:T(8,128)(2,1)S(1)}, u32[]{:S(2)}, u32[]{:S(2)}) collective-permute-start(bf16[144,512]{1,0:T(8,128)(2,1)} %route.1.refs_1_.refs_0_), channel_id=1, source_target_pairs={{0,12},{4,8},{8,4},{12,0},{1,13},{5,9},{9,5},{13,1},{2,14},{6,10},... | collective-permute-start | bytes 442376 | tf_op jit(solution)/shard_map/ppermute | solution.py:424
  9.0 18.8 %collective-permute-start.1 = (bf16[144,512]{1,0:T(8,128)(2,1)}, bf16[144,512]{1,0:T(8,128)(2,1)}, u32[]{:S(2)}, u32[]{:S(2)}) collective-permute-start(bf16[144,512]{1,0:T(8,128)(2,1)} %route.1.refs_1_.refs_0_), channel_id=1, source_target_pairs={{0,8},{4,12},{8,0},{12,4},{1,9},{5,13},{9,1},{13,5},{2,10},{6,14},... | collective-permute-start | bytes 442376 | tf_op jit(solution)/shard_map/ppermute | solution.py:424
  10.4 0.9 copy-start.2
  11.3 18.5 %copy-start.3 = (bf16[144,512]{1,0:T(8,128)(2,1)S(1)}, bf16[144,512]{1,0:T(8,128)(2,1)}, u32[]{:S(2)}) copy-start(bf16[144,512]{1,0:T(8,128)(2,1)} %route.1.refs_1_.refs_0_) | copy-start | bytes 442372
  12.4 15.4 %collective-permute-start.3 = (bf16[192,256]{1,0:T(8,128)(2,1)S(1)}, bf16[192,256]{1,0:T(8,128)(2,1)S(1)}, u32[]{:S(2)}, u32[]{:S(2)}) collective-permute-start(bf16[192,256]{1,0:T(8,128)(2,1)S(1)} %get-tuple-element.29), channel_id=1, source_target_pairs={{0,4},{4,0},{8,12},{12,8},{1,5},{5,1},{9,13},{13,9},{2,6},{6,2},{1... | collective-permute-start | bytes 294920 | tf_op jit(solution)/shard_map/ppermute | solution.py:424
  14.4 15.4 %collective-permute-start.4 = (bf16[192,256]{1,0:T(8,128)(2,1)S(1)}, bf16[192,256]{1,0:T(8,128)(2,1)S(1)}, u32[]{:S(2)}, u32[]{:S(2)}) collective-permute-start(bf16[192,256]{1,0:T(8,128)(2,1)S(1)} %get-tuple-element.30), channel_id=1, source_target_pairs={{0,8},{4,12},{8,0},{12,4},{1,9},{5,13},{9,1},{13,5},{2,10},{6,14},... | collective-permute-start | bytes 294920 | tf_op jit(solution)/shard_map/ppermute | solution.py:424
  18.4 11.4 %collective-permute-start.5 = (bf16[192,256]{1,0:T(8,128)(2,1)S(1)}, bf16[192,256]{1,0:T(8,128)(2,1)S(1)}, u32[]{:S(2)}, u32[]{:S(2)}) collective-permute-start(bf16[192,256]{1,0:T(8,128)(2,1)S(1)} %get-tuple-element.31), channel_id=1, source_target_pairs={{0,12},{4,8},{8,4},{12,0},{1,13},{5,9},{9,5},{13,1},{2,14},{6,10},... | collective-permute-start | bytes 294920 | tf_op jit(solution)/shard_map/ppermute | solution.py:424
  36.2 2.4 %collective-permute-start.6 = (bf16[2,256,768]{2,1,0:T(8,128)(2,1)S(1)}, bf16[2,256,768]{2,1,0:T(8,128)(2,1)S(1)}, u32[]{:S(2)}, u32[]{:S(2)}) collective-permute-start(bf16[2,256,768]{2,1,0:T(8,128)(2,1)S(1)} %get-tuple-element.33), channel_id=1, source_target_pairs={{0,1},{1,0},{2,3},{3,2},{4,5},{5,4},{6,7},{7,6},{8,9},{9,8},{10,11... | collective-permute-start | bytes 2359304 | tf_op jit(solution)/shard_map/ppermute | solution.py:424
  38.7 11.9 %collective-permute-start.7 = (bf16[1,256,768]{2,1,0:T(8,128)(2,1)S(1)}, bf16[1,256,768]{2,1,0:T(8,128)(2,1)S(1)}, u32[]{:S(2)}, u32[]{:S(2)}) collective-permute-start(bf16[1,256,768]{2,1,0:T(8,128)(2,1)S(1)} %get-tuple-element.35), channel_id=1, source_target_pairs={{0,2},{1,3},{2,0},{3,1},{4,6},{5,7},{6,4},{7,5},{8,10},{9,11},{10,... | collective-permute-start | bytes 1179656 | tf_op jit(solution)/shard_map/ppermute | solution.py:424
  41.2 37.4 %collective-permute-start.20 = (bf16[1024,512]{1,0:T(8,128)(2,1)S(1)}, bf16[1024,512]{1,0:T(8,128)(2,1)S(1)}, u32[]{:S(2)}, u32[]{:S(2)}) collective-permute-start(bf16[1024,512]{1,0:T(8,128)(2,1)S(1)} %gate.11), channel_id=1, source_target_pairs={{12,8},{8,4},{4,0},{13,9},{9,5},{5,1},{14,10},{10,6},{6,2},{15,11}... | collective-permute-start | bytes 3145736 | tf_op jit(solution)/shard_map/ppermute | solution.py:456
  42.5 36.1 %collective-permute-start.19 = (bf16[1024,512]{1,0:T(8,128)(2,1)S(1)}, bf16[1024,512]{1,0:T(8,128)(2,1)S(1)}, u32[]{:S(2)}, u32[]{:S(2)}) collective-permute-start(bf16[1024,512]{1,0:T(8,128)(2,1)S(1)} %gate.11), channel_id=1, source_target_pairs={{0,4},{4,8},{8,12},{1,5},{5,9},{9,13},{2,6},{6,10},{10,14},{3,7},{... | collective-permute-start | bytes 3145736 | tf_op jit(solution)/shard_map/ppermute | solution.py:455
  52.3 21.1 %collective-permute-start.8 = (bf16[384,256]{1,0:T(8,128)(2,1)S(1)}, bf16[384,256]{1,0:T(8,128)(2,1)S(1)}, u32[]{:S(2)}, u32[]{:S(2)}) collective-permute-start(bf16[384,256]{1,0:T(8,128)(2,1)S(1)} %get-tuple-element.39), channel_id=1, source_target_pairs={{0,4},{4,0},{8,12},{12,8},{1,5},{5,1},{9,13},{13,9},{2,6},{6,2},{1... | collective-permute-start | bytes 589832 | tf_op jit(solution)/shard_map/ppermute | solution.py:424
  73.4 19.5 %collective-permute-start.10 = (bf16[8,192,256]{2,1,0:T(8,128)(2,1)S(1)}, bf16[8,192,256]{2,1,0:T(8,128)(2,1)S(1)}, u32[]{:S(2)}, u32[]{:S(2)}) collective-permute-start(bf16[8,192,256]{2,1,0:T(8,128)(2,1)S(1)} %gate.8.refs_0_), channel_id=1, source_target_pairs={{0,2},{1,3},{2,0},{3,1},{4,6},{5,7},{6,4},{7,5},{8,10},{9,11},{10,... | collective-permute-start | bytes 2359304 | tf_op jit(solution)/shard_map/ppermute | solution.py:424
  73.7 17.1 %collective-permute-start.14 = (bf16[384,256]{1,0:T(8,128)(2,1)S(1)}, bf16[384,256]{1,0:T(8,128)(2,1)S(1)}, u32[]{:S(2)}, u32[]{:S(2)}) collective-permute-start(bf16[384,256]{1,0:T(8,128)(2,1)S(1)} %get-tuple-element.47), channel_id=1, source_target_pairs={{0,8},{4,12},{8,0},{12,4},{1,9},{5,13},{9,1},{13,5},{2,10},{6,14},... | collective-permute-start | bytes 589832 | tf_op jit(solution)/shard_map/ppermute | solution.py:424
  76.5 14.3 %collective-permute-start.15 = (bf16[384,256]{1,0:T(8,128)(2,1)S(1)}, bf16[384,256]{1,0:T(8,128)(2,1)S(1)}, u32[]{:S(2)}, u32[]{:S(2)}) collective-permute-start(bf16[384,256]{1,0:T(8,128)(2,1)S(1)} %get-tuple-element.48), channel_id=1, source_target_pairs={{0,12},{4,8},{8,4},{12,0},{1,13},{5,9},{9,5},{13,1},{2,14},{6,10},... | collective-permute-start | bytes 589832 | tf_op jit(solution)/shard_map/ppermute | solution.py:424
  90.8 14.5 %collective-permute-start.21 = (bf16[1024,512]{1,0:T(8,128)(2,1)S(1)}, bf16[1024,512]{1,0:T(8,128)(2,1)S(1)}, u32[]{:S(2)}, u32[]{:S(2)}) collective-permute-start(bf16[1024,512]{1,0:T(8,128)(2,1)S(1)} %get-tuple-element.49.refs_5_), channel_id=1, source_target_pairs={{4,8},{8,12},{5,9},{9,13},{6,10},{10,14},{7,11},{11,15},{20,24},{2... | collective-permute-start | bytes 3145736 | tf_op jit(solution)/shard_map/ppermute | solution.py:455
  91.5 31.5 %collective-permute-start.22 = (bf16[1024,512]{1,0:T(8,128)(2,1)S(1)}, bf16[1024,512]{1,0:T(8,128)(2,1)S(1)}, u32[]{:S(2)}, u32[]{:S(2)}) collective-permute-start(bf16[1024,512]{1,0:T(8,128)(2,1)S(1)} %get-tuple-element.50.refs_8_), channel_id=1, source_target_pairs={{8,4},{4,0},{9,5},{5,1},{10,6},{6,2},{11,7},{7,3},{24,20},{20,16},... | collective-permute-start | bytes 3145736 | tf_op jit(solution)/shard_map/ppermute | solution.py:456
  92.8 2.4 %collective-permute-start.9 = (bf16[8,192,256]{2,1,0:T(8,128)(2,1)S(1)}, bf16[8,192,256]{2,1,0:T(8,128)(2,1)S(1)}, u32[]{:S(2)}, u32[]{:S(2)}) collective-permute-start(bf16[8,192,256]{2,1,0:T(8,128)(2,1)S(1)} %gate.8.refs_0_), channel_id=1, source_target_pairs={{0,1},{1,0},{2,3},{3,2},{4,5},{5,4},{6,7},{7,6},{8,9},{9,8},{10,11... | collective-permute-start | bytes 2359304 | tf_op jit(solution)/shard_map/ppermute | solution.py:424
  92.9 3.4 %collective-permute-start.11 = (bf16[8,192,256]{2,1,0:T(8,128)(2,1)S(1)}, bf16[8,192,256]{2,1,0:T(8,128)(2,1)S(1)}, u32[]{:S(2)}, u32[]{:S(2)}) collective-permute-start(bf16[8,192,256]{2,1,0:T(8,128)(2,1)S(1)} %collective-permute-done.10.refs_2_.refs_1_), channel_id=1, source_target_pairs={{0,1},{1,0},{2,3},{3,2},{4,5},{5,4},{6,7},{7,6},{8,9},{9,8},{10,11... | collective-permute-start | bytes 2359304 | tf_op jit(solution)/shard_map/ppermute | solution.py:424
  93.5 63.6 %copy-start.4 = (s32[16,4]{0,1:T(4,128)S(1)}, s32[16,4]{0,1:T(4,128)}, u32[]{:S(2)}) copy-start(s32[16,4]{0,1:T(4,128)} %param.14) | copy-start | bytes 772
  93.5 31.7 %collective-permute-start.17 = (bf16[4,384,256]{2,1,0:T(8,128)(2,1)S(1)}, bf16[4,384,256]{2,1,0:T(8,128)(2,1)S(1)}, u32[]{:S(2)}, u32[]{:S(2)}) collective-permute-start(bf16[4,384,256]{2,1,0:T(8,128)(2,1)S(1)} %gate.9.refs_0_), channel_id=1, source_target_pairs={{0,2},{1,3},{2,0},{3,1},{4,6},{5,7},{6,4},{7,5},{8,10},{9,11},{10,... | collective-permute-start | bytes 2359304 | tf_op jit(solution)/shard_map/ppermute | solution.py:424
  105.2 59.6 %copy-start.5 = (s32[128,8]{0,1:T(8,128)S(1)}, s32[128,8]{0,1:T(8,128)}, u32[]{:S(2)}) copy-start(s32[128,8]{0,1:T(8,128)} %param.12) | copy-start | bytes 12292
  105.2 59.6 %copy-start.6 = (s32[128,8]{0,1:T(8,128)S(1)}, s32[128,8]{0,1:T(8,128)}, u32[]{:S(2)}) copy-start(s32[128,8]{0,1:T(8,128)} %param.13) | copy-start | bytes 12292
  105.3 60.4 %copy-start.1 = (bf16[8,4,32,512]{3,2,1,0:T(8,128)(2,1)S(1)}, bf16[8,4,32,512]{3,2,1,0:T(8,128)(2,1)}, u32[]{:S(2)}) copy-start(bf16[8,4,32,512]{3,2,1,0:T(8,128)(2,1)} %param.16) | copy-start | bytes 3145732
  123.1 42.6 %collective-permute-start.23 = (bf16[1024,512]{1,0:T(8,128)(2,1)S(1)}, bf16[1024,512]{1,0:T(8,128)(2,1)S(1)}, u32[]{:S(2)}, u32[]{:S(2)}) collective-permute-start(bf16[1024,512]{1,0:T(8,128)(2,1)S(1)} %get-tuple-element.51.refs_6_), channel_id=1, source_target_pairs={{8,12},{9,13},{10,14},{11,15},{24,28},{25,29},{26,30},{27,31}} | collective-permute-start | bytes 3145736 | tf_op jit(solution)/shard_map/ppermute | solution.py:455
  123.8 41.9 %collective-permute-start.24 = (bf16[1024,512]{1,0:T(8,128)(2,1)S(1)}, bf16[1024,512]{1,0:T(8,128)(2,1)S(1)}, u32[]{:S(2)}, u32[]{:S(2)}) collective-permute-start(bf16[1024,512]{1,0:T(8,128)(2,1)S(1)} %get-tuple-element.52.refs_9_), channel_id=1, source_target_pairs={{4,0},{5,1},{6,2},{7,3},{20,16},{21,17},{22,18},{23,19}} | collective-permute-start | bytes 3145736 | tf_op jit(solution)/shard_map/ppermute | solution.py:456
  125.1 40.6 %collective-permute-start.16 = (bf16[4,384,256]{2,1,0:T(8,128)(2,1)S(1)}, bf16[4,384,256]{2,1,0:T(8,128)(2,1)S(1)}, u32[]{:S(2)}, u32[]{:S(2)}) collective-permute-start(bf16[4,384,256]{2,1,0:T(8,128)(2,1)S(1)} %gate.9.refs_0_), channel_id=1, source_target_pairs={{0,1},{1,0},{2,3},{3,2},{4,5},{5,4},{6,7},{7,6},{8,9},{9,8},{10,11... | collective-permute-start | bytes 2359304 | tf_op jit(solution)/shard_map/ppermute | solution.py:424
  125.2 40.5 %collective-permute-start.18 = (bf16[4,384,256]{2,1,0:T(8,128)(2,1)S(1)}, bf16[4,384,256]{2,1,0:T(8,128)(2,1)S(1)}, u32[]{:S(2)}, u32[]{:S(2)}) collective-permute-start(bf16[4,384,256]{2,1,0:T(8,128)(2,1)S(1)} %gate.10.refs_2_), channel_id=1, source_target_pairs={{0,1},{1,0},{2,3},{3,2},{4,5},{5,4},{6,7},{7,6},{8,9},{9,8},{10,11... | collective-permute-start | bytes 2359304 | tf_op jit(solution)/shard_map/ppermute | solution.py:424
  125.7 31.3 %collective-permute-start.12 = (bf16[2,160,512]{2,1,0:T(8,128)(2,1)S(1)}, bf16[2,160,512]{2,1,0:T(8,128)(2,1)S(1)}, u32[]{:S(2)}, u32[]{:S(2)}) collective-permute-start(bf16[2,160,512]{2,1,0:T(8,128)(2,1)S(1)} %get-tuple-element.41), channel_id=1, source_target_pairs={{0,4},{4,0},{8,12},{12,8},{1,5},{5,1},{9,13},{13,9},{2,6},{6,2},{1... | collective-permute-start | bytes 983048 | tf_op jit(solution)/shard_map/ppermute | solution.py:424
  157.0 7.8 %collective-permute-start.13 = (bf16[1,160,512]{2,1,0:T(8,128)(2,1)S(1)}, bf16[1,160,512]{2,1,0:T(8,128)(2,1)S(1)}, u32[]{:S(2)}, u32[]{:S(2)}) collective-permute-start(bf16[1,160,512]{2,1,0:T(8,128)(2,1)S(1)} %get-tuple-element.43), channel_id=1, source_target_pairs={{0,8},{4,12},{8,0},{12,4},{1,9},{5,13},{9,1},{13,5},{2,10},{6,14},... | collective-permute-start | bytes 491528 | tf_op jit(solution)/shard_map/ppermute | solution.py:424

commit v8 on v6

--- a/solution.py
+++ b/solution.py
@@ -105,18 +105,6 @@
         ]
 
 
-def hidden_kernel(z, ids_ref, pair_ref, after_ref, *refs):
-    outs, sides = refs[:-1], refs[-1]
-    pair = pair_ref[...]
-    gate_pre = pair[:, : z.hidden].astype(F32)
-    up = pair[:, z.hidden :].astype(F32)
-    hidden = (gate_pre * (1.0 / (1.0 + jnp.exp(-gate_pre))) * up).astype(BF).T
-    for q in range(z.ep):
-        sides[q] = hidden[q * z.down_cols : (q + 1) * z.down_cols, :]
-    for k in range(z.ep):
-        outs[k][...] = sides[ids_ref[0] ^ k]
-
-
 def block_place(z, block):
     slot = block // z.slot_blocks
     first = (block % z.slot_blocks) * z.sources
@@ -157,8 +145,8 @@
 def down_kernel(z, ids_ref, *refs):
     bufs = refs[: z.ep]
     weight_ref = refs[z.ep]
-    parts = refs[z.ep + 2 : z.ep + 4]
-    grads_ref, codes_ref, rows_ref, held, sems = refs[z.ep + 4 :]
+    parts = refs[z.ep + 1 : z.ep + 3]
+    grads_ref, codes_ref, rows_ref, held, sems = refs[z.ep + 3 :]
     me, mine = ids_ref[0], ids_ref[1]
     step = pl.program_id(0)
 
@@ -208,29 +196,28 @@
 
 
 def pre_kernel(z, ids_ref, keep_ref, got_ref, pair_ref, codes_ref, *refs):
-    downs = refs[: z.ep]
-    out_ref, bundle_ref = refs[-2:]
-
-    @pl.when(pl.program_id(0) == 0)
-    def _():
-        for k in range(z.ep):
-            bundle_ref[k] = downs[k][...]
-
+    outs, (grad_ref, sides) = refs[: z.ep], refs[z.ep :]
     me = ids_ref[0]
     block = ids_ref[1] * z.part_blocks + pl.program_id(0)
     slot, first = block_place(z, block)
     scale = block_scale(z, codes_ref, me * z.local + slot, first)
     grad = keep_ref[0].astype(F32) + got_ref[0].astype(F32)
-    turned = grad.astype(BF).T
-    spot = pl.multiple_of(pl.program_id(0) * z.block, z.block)
-    for q in range(z.ep):
-        bundle_ref[z.ep + q, :, pl.ds(spot, z.block)] = turned[
-            q * z.down_cols : (q + 1) * z.down_cols, :
-        ]
-    _, grad_gate, grad_up = gate_terms(z, pair_ref[...], grad, scale)
+    grad_ref[...] = grad.astype(BF)
+    hidden, grad_gate, grad_up = gate_terms(z, pair_ref[...], grad, scale)
+    hidden = hidden.astype(BF).T
     pre = jnp.concatenate([grad_gate.T, grad_up.T], axis=0)
     for q in range(z.ep):
-        out_ref[q] = pre[q * z.in_cols : (q + 1) * z.in_cols, :]
+        sides[q, : z.in_cols, :] = pre[q * z.in_cols : (q + 1) * z.in_cols, :]
+        sides[q, z.in_cols :, :] = hidden[q * z.down_cols : (q + 1) * z.down_cols, :]
+    for k in range(z.ep):
+        outs[k][...] = sides[me ^ k]
+
+
+def stack_kernel(z, *refs):
+    refs = refs[: z.ep] + refs[-2:]
+    for k in range(z.ep):
+        refs[-2][k] = refs[k][: z.in_cols, :]
+        refs[-1][k] = refs[k][z.in_cols :, :]
 
 
 def row_kernel(z, ids_ref, *refs):
@@ -254,8 +241,7 @@
 
         @pl.when(place == k)
         def _():
-            turned = [grads[k][z.ep + q, :, pl.ds(spot, z.block)] for q in range(z.ep)]
-            held[...] = jnp.concatenate(turned, axis=0).T
+            held[...] = grads[k][pl.ds(spot, z.block), :]
 
     grad = held[...].astype(F32)
     scale = block_scale(z, codes_ref, me * z.local + slot, first)
@@ -365,13 +351,14 @@
 
 def total_down_kernel(z, ids_ref, table_ref, *refs):
     sides = refs[: z.sub]
-    grads_ref, codes_ref, out_ref, held, made, out_sems, scaled, sems = refs[z.sub :]
+    grads_ref, codes_ref, out_ref, token_ref, held, made, out_sems, scaled, sems = refs[z.sub :]
+    token_ref[...] = jnp.zeros_like(token_ref)
 
     def moves(act):
         for k in range(z.sub):
             act(
                 pltpu.make_async_copy(
-                    sides[k].at[pl.ds(0, z.ep)], held.at[k, pl.ds(0, z.ep)], sems.at[k]
+                    sides[k], held.at[k, pl.ds(0, z.ep)], sems.at[k]
                 )
             )
 
@@ -395,7 +382,8 @@
 def total_in_kernel(z, ids_ref, table_ref, *refs):
     sides, refs = refs[: z.sub], refs[z.sub :]
     own_ref, rights, lefts = refs[0], refs[1 : z.ep], refs[z.ep : 2 * z.ep - 1]
-    out_ref, held, made, out_sems, inputs_ref, sems, *other_sems = refs[2 * z.ep - 1 :]
+    out_ref, token_ref, held, made, out_sems, inputs_ref, sems, *other_sems = refs[2 * z.ep - 1 :]
+    token_ref[...] = jnp.zeros_like(token_ref)
 
     def moves(act):
         for k in range(z.sub):
@@ -410,7 +398,7 @@
         start = pl.multiple_of(block * z.block, z.block)
         return inputs_ref[slot_id // z.local, pl.ds(start, z.block), :]
 
-    expert_products(z, ids_ref, table_ref, 0, held, right_rows, out_ref, made, out_sems)
+    expert_products(z, ids_ref, table_ref, ids_ref[0], held, right_rows, out_ref, made, out_sems)
 
 
 def swap(x, axis, size, bit):
@@ -484,23 +472,21 @@
     )(token_count, *routing)
     bufs = [buf] + [swap(buf, "ep", n, k) for k in range(1, n)]
 
-    downs = pl.pallas_call(
-        functools.partial(hidden_kernel, z),
-        grid_spec=pltpu.PrefetchScalarGridSpec(
-            num_scalar_prefetch=1,
-            grid=(z.part_blocks,),
-            in_specs=[
-                pl.BlockSpec((z.block, z.pair), lambda i, r: (r[1] * z.part_blocks + i, 0)),
-                pl.BlockSpec(memory_space=pl.ANY),
-            ],
-            out_specs=[pl.BlockSpec((z.down_cols, z.block), lambda i, r: (0, i))] * n,
-            scratch_shapes=[pltpu.VMEM((n, z.down_cols, z.block), BF)],
-        ),
-        out_shape=[jax.ShapeDtypeStruct((z.down_cols, z.part), BF)] * n,
-        compiler_params=params(16),
-        name="hidden_columns",
-    )(ids, pair_rows, bufs[1])
-    downs = [downs[0]] + [swap(downs[k], "ep", n, k) for k in range(1, n)]
+    chain = gate([inputs], bufs[1:])
+    steps = [chain_step(chain[0], chain[0], "ep", n, 1)]
+    steps.append(chain_step(*steps[0], "ep", n, 2))
+
+    def stack(pieces, after):
+        shapes = [(n, z.in_cols, z.part), (n, z.down_cols, z.part)]
+        return pl.pallas_call(
+            functools.partial(stack_kernel, z),
+            in_specs=[whole((z.cols, z.part))] * n + [pl.BlockSpec(memory_space=pl.ANY)],
+            out_specs=[whole(shape) for shape in shapes],
+            out_shape=[jax.ShapeDtypeStruct(shape, BF) for shape in shapes],
+            grid=(1,),
+            compiler_params=params(12),
+            name="stack_columns",
+        )(*pieces, after)
 
     def halve(keep, got):
         half = (keep.shape[0] // 2,) + keep.shape[1:]
@@ -518,17 +504,13 @@
         place = i // z.part_blocks
         return (place ^ ids_ref[1]) * z.part_blocks + i % z.part_blocks
 
-    chain = gate([inputs], bufs[1:] + downs[1:])
-    steps = [chain_step(chain[0], chain[0], "ep", n, 1)]
-
     part_shape = (m // 2, z.part, z.hidden)
     outs = pl.pallas_call(
         functools.partial(down_kernel, z),
         grid_spec=pltpu.PrefetchScalarGridSpec(
             num_scalar_prefetch=1,
             grid=(z.blocks,),
-            in_specs=[whole(grad_shape)] * n
-            + [pl.BlockSpec(memory_space=pltpu.HBM), pl.BlockSpec(memory_space=pl.ANY)],
+            in_specs=[whole(grad_shape)] * n + [pl.BlockSpec(memory_space=pltpu.HBM)],
             out_specs=[whole(part_shape)] * 2
             + [whole((n, z.tokens, z.width)), whole(code_shape)],
             scratch_shapes=[
@@ -544,15 +526,16 @@
         ],
         compiler_params=params(48),
         name="hidden_partials",
-    )(ids, *bufs, weight_down, chain[0])
+    )(ids, *bufs, weight_down)
     keep, send, grads_all, codes = outs
+    send = gate([send], steps[0])[0]
     got = swap(send, "sub", m, 1)
     bit = 2
     while bit < m:
         keep, send = halve(keep, got)
         got = swap(send, "sub", m, bit)
         bit *= 2
-    pre, bundle = pl.pallas_call(
+    *pieces, grad_part = pl.pallas_call(
         functools.partial(pre_kernel, z),
         grid_spec=pltpu.PrefetchScalarGridSpec(
             num_scalar_prefetch=1,
@@ -561,29 +544,19 @@
             + [
                 pl.BlockSpec((z.block, z.pair), lambda i, r: (r[1] * z.part_blocks + i, 0)),
                 whole(code_shape),
-            ]
-            + [whole((z.down_cols, z.part))] * n
-            + [pl.BlockSpec(memory_space=pl.ANY)] * 2,
-            out_specs=[
-                pl.BlockSpec((n, z.in_cols, z.block), lambda i, r: (0, 0, i)),
-                whole((2 * n, z.down_cols, z.part)),
             ],
+            out_specs=[pl.BlockSpec((z.cols, z.block), lambda i, r: (0, i))] * n
+            + [pl.BlockSpec((z.block, z.hidden), lambda i, r: (i, 0))],
+            scratch_shapes=[pltpu.VMEM((n, z.cols, z.block), BF)],
         ),
-        out_shape=[
-            jax.ShapeDtypeStruct((n, z.in_cols, z.part), BF),
-            jax.ShapeDtypeStruct((2 * n, z.down_cols, z.part), BF),
-        ],
+        out_shape=[jax.ShapeDtypeStruct((z.cols, z.part), BF)] * n
+        + [jax.ShapeDtypeStruct((z.part, z.hidden), BF)],
         compiler_params=params(16),
         name="pre_grads",
-    )(ids, keep, got, pair_rows, codes, *downs, *steps[0])
-    columns = lax.all_to_all(pre, "ep", split_axis=0, concat_axis=0, tiled=True)
-    steps[0] = gate(steps[0], [columns])
-    for d in range(2, n):
-        steps.append(chain_step(*steps[-1], "ep", n, d))
-    bundles = spread_over({0: bundle}, "sub", m, m // 2)
-    sides = {0: gate([columns], [bundles[m // 2]])[0]}
-    sides[m // 2] = swap(sides[0], "sub", m, m // 2)
-    gathered = [inputs] + [go for go, _ in steps] + [back for _, back in steps]
+    )(ids, keep, got, pair_rows, codes)
+    late = gate(pieces[1:], steps[1])
+    pieces = pieces[:1] + [swap(a, "ep", n, k) for k, a in enumerate(late, 1)]
+    grad_parts = spread_over({0: grad_part}, "sub", m, m // 2)
 
     back_shape = (n // 2, z.tokens + z.slots, z.width)
     keep, send = pl.pallas_call(
@@ -591,7 +564,7 @@
         grid_spec=pltpu.PrefetchScalarGridSpec(
             num_scalar_prefetch=1,
             grid=(z.blocks,),
-            in_specs=[whole(bundle.shape)] * m
+            in_specs=[whole((z.part, z.hidden))] * m
             + [
                 pl.BlockSpec((z.block, z.pair), lambda i, r: (row_block(i, r), 0)),
                 pl.BlockSpec(memory_space=pltpu.HBM),
@@ -609,13 +582,54 @@
         out_shape=[jax.ShapeDtypeStruct(back_shape, BF)] * 2,
         compiler_params=params(46),
         name="row_grads",
-    )(ids, *bundles, pair_rows, weight_in, codes)
-    sides[m // 2] = gate([sides[m // 2]], [keep])[0]
+    )(ids, *grad_parts, pair_rows, weight_in, codes)
+    columns, down_columns = stack(pieces, keep)
+    down_sides = spread_over({0: down_columns}, "sub", m, m // 2)
+    got = swap(send, "ep", n, 1)
+    sides = {0: gate([columns], [down_sides[m // 2], got])[0]}
+    sides[m // 2] = swap(sides[0], "sub", m, m // 2)
+    steps[1] = gate(steps[1], [got])
+    for d in range(3, n):
+        steps.append(chain_step(*steps[-1], "ep", n, d))
+    gathered = [inputs] + [go for go, _ in steps] + [back for _, back in steps]
+    def total_call(kernel, operands, specs, cols, scratch, name):
+        return pl.pallas_call(
+            functools.partial(kernel, z),
+            grid_spec=pltpu.PrefetchScalarGridSpec(
+                num_scalar_prefetch=2,
+                grid=(1,),
+                in_specs=specs,
+                out_specs=[pl.BlockSpec(memory_space=pl.ANY), whole((8, 128))],
+                scratch_shapes=[
+                    pltpu.VMEM((m, n + 1, cols, z.part), BF),
+                    pltpu.VMEM((z.experts, cols, z.width), BF),
+                    pltpu.SemaphoreType.DMA((z.experts,)),
+                ]
+                + scratch,
+            ),
+            out_shape=[
+                jax.ShapeDtypeStruct((z.experts, cols, z.width), BF),
+                jax.ShapeDtypeStruct((8, 128), F32),
+            ],
+            compiler_params=params(32),
+            name=name,
+        )(ids, table, *operands)
+
+    anywhere = pl.BlockSpec(memory_space=pl.ANY)
+    grad_down, down_made = total_call(
+        total_down_kernel,
+        [*down_sides, grads_all, codes],
+        [anywhere] * m + [whole((n, z.tokens, z.width)), whole(code_shape)],
+        z.down_cols,
+        [pltpu.VMEM((z.slots, z.rows, z.width), BF), pltpu.SemaphoreType.DMA((m,))],
+        "down_grads",
+    )
+    sides[0], sides[m // 2] = gate([sides[0], sides[m // 2]], [down_made])
     sides = spread_over(sides, "sub", m, m // 4)
-    got = swap(send, "ep", n, 1)
     bit = 2
     while bit < n:
         keep, send = halve(keep, got)
+        send = gate([send], [down_made])[0]
         got = swap(send, "ep", n, bit)
         bit *= 2
 
@@ -632,36 +646,7 @@
         name="token_grads",
     )(token_count, keep, got, routes, replica, table)
 
-    def total_call(kernel, operands, specs, cols, scratch, name):
-        return pl.pallas_call(
-            functools.partial(kernel, z),
-            grid_spec=pltpu.PrefetchScalarGridSpec(
-                num_scalar_prefetch=2,
-                grid=(1,),
-                in_specs=specs,
-                out_specs=pl.BlockSpec(memory_space=pl.ANY),
-                scratch_shapes=[
-                    pltpu.VMEM((m, n + 1, cols, z.part), BF),
-                    pltpu.VMEM((z.experts, cols, z.width), BF),
-                    pltpu.SemaphoreType.DMA((z.experts,)),
-                ]
-                + scratch,
-            ),
-            out_shape=jax.ShapeDtypeStruct((z.experts, cols, z.width), BF),
-            compiler_params=params(32),
-            name=name,
-        )(ids, table, *operands)
-
-    anywhere = pl.BlockSpec(memory_space=pl.ANY)
-    grad_down = total_call(
-        total_down_kernel,
-        [*bundles, grads_all, codes],
-        [anywhere] * m + [whole((n, z.tokens, z.width)), whole(code_shape)],
-        z.down_cols,
-        [pltpu.VMEM((z.slots, z.rows, z.width), BF), pltpu.SemaphoreType.DMA((m,))],
-        "down_grads",
-    )
-    grad_in = total_call(
+    grad_in, _ = total_call(
         total_in_kernel,
         [*sides, *gathered],
         [anywhere] * (m + 2 * n - 1),

time: 171 us -> 161 us (0.942)
  starting transfers between devices: 42.2 us -> 35.9 us
  Pallas kernels: 36.3 us -> 33.4 us
  local copies, waits for them, and re-layouts: 6.82 us -> 4.76 us
    ppermute x16 -> x19, waiting for transfers between devices: 25.8 us -> 66.3 us  [swap(): return lax.ppermute(x, axis, [(i, i ^ bit) for i in range(size)])]
    ppermute x3, waiting for transfers between devices: 39.2 us -> 17.3 us  [chain_step(): lax.ppermute(back, axis, [(i, i - 1) for i in range(size - d, 0, -1)])]
    all_to_all x1 -> x0, waiting for transfers between devices: 17.4 us -> none  [body(): columns = lax.all_to_all(pre, 'ep', split_axis=0, concat_axis=0, tiled=True)]
    all_to_all x1 -> x0, starting transfers between devices: 7.01 us -> none  [body(): columns = lax.all_to_all(pre, 'ep', split_axis=0, concat_axis=0, tiled=True)]
    unnamed x25 -> x17, local copies, waits for them, and re-layouts: 6.82 us -> 4.76 us
    pallas_call x1, Pallas kernels: 10 us -> 8.29 us  [body(): pl.pallas_call(functools.partial(row_kernel, z), grid_spec=pltpu.Prefetch...]
    ppermute x16 -> x19, starting transfers between devices: 24.3 us -> 24.8 us  [swap(): return lax.ppermute(x, axis, [(i, i ^ bit) for i in range(size)])]
  transfers between devices with their start and end apart: 23 -> 25, of which waited for: 9 -> 14; matrix products, arithmetic and copies ran while one was open for 1% -> 1% of each run, Pallas kernels for 11% -> 14%
where the time goes in v8:
time: 161 us; the launch traced here: 160 us
  waiting for transfers between devices  84.8 us (53%)
  starting transfers between devices  35.9 us (22%)
  Pallas kernels  33.4 us (21%)
  local copies, waits for them, and re-layouts  4.76 us (3%)
    ppermute x19, waiting for transfers between devices, swap(): return lax.ppermute(x, axis, [(i, i ^ bit) for i in range(size)])  66.3 us
    ppermute x19, starting transfers between devices, swap(): return lax.ppermute(x, axis, [(i, i ^ bit) for i in range(size)])  24.8 us
    ppermute x3, waiting for transfers between devices, chain_step(): lax.ppermute(back, axis, [(i, i - 1) for i in range(size - d, 0, -1)])  17.3 us
    pallas_call x2, Pallas kernels, total_call(): pl.pallas_call(functools.partial(kernel, z), grid_spec=pltpu.PrefetchScal...  14.9 us
    pallas_call x1, Pallas kernels, body(): pl.pallas_call(functools.partial(row_kernel, z), grid_spec=pltpu.Prefetch...  8.29 us
    ppermute x3, starting transfers between devices, chain_step(): go = lax.ppermute(go, axis, [(i, i + 1) for i in range(d - 1, size - 1)])  6.99 us
    pallas_call x1, Pallas kernels, body(): pl.pallas_call(functools.partial(down_kernel, z), grid_spec=pltpu.Prefetc...  5.48 us
    unnamed x17, local copies, waits for them, and re-layouts  4.76 us
  transfers between devices with their start and end apart: 25, of which 14 were waited for; matrix products, arithmetic and copies ran while one was open for 1% of the time, Pallas kernels for 14%

profile of v8, /device:TPU:0, one launch (start us, length us, event | category | flops | bytes accessed | tf_op | source)
XLA Modules:
  0.0 160.4 jit_solution(1434758648196854175)
XLA Ops:
  1.3 1.9 %route.1.refs_0_ = bf16[144,512]{1,0:T(8,128)(2,1)} custom-call(s32[1]{0:T(128)S(6)} %copy.36.count_ref, bf16[128,512]{1,0:T(8,128)(2,1)} %grad_ref.1, bf16[8,128]{1,0:T(8,128)(2,1)} %bitcast.21, s32[8,128]{1,0:T(8,128)} %bitcast.17, s32[8,128]{1,0:T(8,128)} %bitcast.19, s32[4,16]{1,0:T(4,128)} %bitcast.13), custom_call_target="tpu_custom_call" | custom-call | tf_op jit(solution)/shard_map/route/pallas_call | solution.py:464
  3.2 5.0 %collective-permute-start.2 = (bf16[144,512]{1,0:T(8,128)(2,1)}, bf16[144,512]{1,0:T(8,128)(2,1)S(1)}, u32[]{:S(2)}, u32[]{:S(2)}) collective-permute-start(bf16[144,512]{1,0:T(8,128)(2,1)} %route.1.refs_0_), channel_id=1, source_target_pairs={{0,12},{4,8},{8,4},{12,0},{1,13},{5,9},{9,5},{13,1},{2,14},{6,10},... | collective-permute-start | bytes 442376 | tf_op jit(solution)/shard_map/ppermute | solution.py:405
  8.2 0.6 collective-permute-start
  8.8 2.3 %copy.25.refs_0_ = bf16[1024,512]{1,0:T(8,128)(2,1)} copy(bf16[1024,512]{1,0:T(8,128)(2,1)} %bitcast.11) | data formatting | bytes 2097152
  11.0 2.2 %collective-permute-done.2.refs_3_ = bf16[144,512]{1,0:T(8,128)(2,1)S(1)} collective-permute-done((bf16[144,512]{1,0:T(8,128)(2,1)}, bf16[144,512]{1,0:T(8,128)(2,1)S(1)}, u32[]{:S(2)}, u32[]{:S(2)}) %collective-permute-start.2) | collective-permute-done | bytes 147488 | tf_op jit(solution)/shard_map/ppermute | solution.py:405
  13.2 7.7 %collective-permute-done.1.refs_2_ = bf16[144,512]{1,0:T(8,128)(2,1)S(1)} collective-permute-done((bf16[144,512]{1,0:T(8,128)(2,1)}, bf16[144,512]{1,0:T(8,128)(2,1)S(1)}, u32[]{:S(2)}, u32[]{:S(2)}) %collective-permute-start.1) | collective-permute-done | bytes 147488 | tf_op jit(solution)/shard_map/ppermute | solution.py:405
  20.9 0.7 copy-done.2
  21.6 1.5 collective-permute-start.4
  23.1 5.5 %collective-permute-start.3 = (bf16[1024,512]{1,0:T(8,128)(2,1)}, bf16[1024,512]{1,0:T(8,128)(2,1)}, u32[]{:S(2)}, u32[]{:S(2)}) collective-permute-start(bf16[1024,512]{1,0:T(8,128)(2,1)} %gate.7), channel_id=1, source_target_pairs={{0,4},{4,8},{8,12},{1,5},{5,9},{9,13},{2,6},{6,10},{10,14},{3,7},{... | collective-permute-start | bytes 3145736 | tf_op jit(solution)/shard_map/ppermute | solution.py:436
  28.7 0.1 pad_add_fusion.ids_ref
  28.7 0.9 copy-done.3
  29.7 0.9 copy-done.4
  30.6 5.5 %hidden_partials.1 = (bf16[2,256,768]{2,1,0:T(8,128)(2,1)S(1)}, bf16[2,256,768]{2,1,0:T(8,128)(2,1)S(1)}, bf16[4,128,512]{2,1,0:T(8,128)(2,1)S(1)}, f32[4,64,128]{2,1,0:T(8,128)S(1)}) custom-call(s32[2]{0:T(128)S(1)} %pad_add_fusion.ids_ref, bf16[144,512]{1,0:T(8,128)(2,1)S(1)} %copy-done.4, bf16[144,512]{1,0:T(8,128)(2,1)S(1)} %copy-done.3, ...), custom_call_target="tpu_custom_call" | custom-call | tf_op jit(solution)/shard_map/hidden_partials/pallas_call | solution.py:508
  36.0 12.2 %collective-permute-done.4.refs_2_.refs_8_ = bf16[1024,512]{1,0:T(8,128)(2,1)} collective-permute-done((bf16[1024,512]{1,0:T(8,128)(2,1)}, bf16[1024,512]{1,0:T(8,128)(2,1)}, u32[]{:S(2)}, u32[]{:S(2)}) %collective-permute-start.4) | collective-permute-done | bytes 1048608 | tf_op jit(solution)/shard_map/ppermute | solution.py:437
  48.2 1.2 collective-permute-done.3.refs_1_.refs_5_
  49.4 1.3 collective-permute-start.12
  50.7 0.7 collective-permute-start.11
  51.5 0.3 collective-permute-done.5.got_ref
  51.7 0.2 halve.2
  51.9 1.6 collective-permute-start.6
  53.5 9.8 %collective-permute-done.6.got_ref = bf16[1,256,768]{2,1,0:T(8,128)(2,1)S(1)} collective-permute-done((bf16[1,256,768]{2,1,0:T(8,128)(2,1)S(1)}, bf16[1,256,768]{2,1,0:T(8,128)(2,1)S(1)}, u32[]{:S(2)}, u32[]{:S(2)}) %collective-permute-start.6) | collective-permute-done | bytes 393248 | tf_op jit(solution)/shard_map/ppermute | solution.py:405
  63.3 1.7 %pre_grads.1 = (bf16[576,256]{1,0:T(8,128)(2,1)S(1)}, bf16[576,256]{1,0:T(8,128)(2,1)S(1)}, bf16[576,256]{1,0:T(8,128)(2,1)S(1)}, bf16[576,256]{1,0:T(8,128)(2,1)S(1)}, bf16[256,768]{1,0:T(8,128)(2,1)S(1)}) custom-call(s32[2]{0:T(128)S(1)} %pad_add_fusion.ids_ref, bf16[1,256,768]{2,1,0:T(8,128)(2,1)S(1)} %get-tuple-element.35.keep_ref, ...), custom_call_target="tpu_custom_call" | custom-call | tf_op jit(solution)/shard_map/pre_grads/pallas_call | solution.py:538
  65.0 1.6 collective-permute-start.8
  66.6 9.0 %collective-permute-done.8.refs_2_ = bf16[256,768]{1,0:T(8,128)(2,1)S(1)} collective-permute-done((bf16[256,768]{1,0:T(8,128)(2,1)S(1)}, bf16[256,768]{1,0:T(8,128)(2,1)S(1)}, u32[]{:S(2)}, u32[]{:S(2)}) %collective-permute-start.8) | collective-permute-done | bytes 393248 | tf_op jit(solution)/shard_map/ppermute | solution.py:405
  75.5 2.3 %collective-permute-done.12.refs_4_.refs_1_ = bf16[1024,512]{1,0:T(8,128)(2,1)S(1)} collective-permute-done((bf16[1024,512]{1,0:T(8,128)(2,1)}, bf16[1024,512]{1,0:T(8,128)(2,1)S(1)}, u32[]{:S(2)}, u32[]{:S(2)}) %collective-permute-start.12) | collective-permute-done | bytes 1048608 | tf_op jit(solution)/shard_map/ppermute | solution.py:437
  77.8 3.3 %collective-permute-start.13 = (bf16[576,256]{1,0:T(8,128)(2,1)S(1)}, bf16[576,256]{1,0:T(8,128)(2,1)S(1)}, u32[]{:S(2)}, u32[]{:S(2)}) collective-permute-start(bf16[576,256]{1,0:T(8,128)(2,1)S(1)} %get-tuple-element.47), channel_id=1, source_target_pairs={{0,4},{4,0},{8,12},{12,8},{1,5},{5,1},{9,13},{13,9},{2,6},{6,2},{1... | collective-permute-start | bytes 884744 | tf_op jit(solution)/shard_map/ppermute | solution.py:405
  81.1 1.9 %collective-permute-start.14 = (bf16[576,256]{1,0:T(8,128)(2,1)S(1)}, bf16[576,256]{1,0:T(8,128)(2,1)S(1)}, u32[]{:S(2)}, u32[]{:S(2)}) collective-permute-start(bf16[576,256]{1,0:T(8,128)(2,1)S(1)} %get-tuple-element.48), channel_id=1, source_target_pairs={{0,8},{4,12},{8,0},{12,4},{1,9},{5,13},{9,1},{13,5},{2,10},{6,14},... | collective-permute-start | bytes 884744 | tf_op jit(solution)/shard_map/ppermute | solution.py:405
  83.0 1.2 collective-permute-start.15
  84.2 8.3 %row_grads.1 = (bf16[2,160,512]{2,1,0:T(8,128)(2,1)S(1)}, bf16[2,160,512]{2,1,0:T(8,128)(2,1)S(1)}) custom-call(s32[2]{0:T(128)S(1)} %pad_add_fusion.ids_ref, bf16[256,768]{1,0:T(8,128)(2,1)S(1)} %get-tuple-element.38.refs_0_, bf16[256,768]{1,0:T(8,128)(2,1)S(1)} %collective-permute-done.7.refs_1_, bf16[256,768]{1,0:T(8,128)(2,1)S(1)} %collective-permute-done.8.refs_2_, ...), custom_call_target="tpu_custom_call" | custom-call | tf_op jit(solution)/shard_map/row_grads/pallas_call | solution.py:562
  92.6 1.8 %collective-permute-done.13.refs_1_ = bf16[576,256]{1,0:T(8,128)(2,1)S(1)} collective-permute-done((bf16[576,256]{1,0:T(8,128)(2,1)S(1)}, bf16[576,256]{1,0:T(8,128)(2,1)S(1)}, u32[]{:S(2)}, u32[]{:S(2)}) %collective-permute-start.13) | collective-permute-done | bytes 294944 | tf_op jit(solution)/shard_map/ppermute | solution.py:405
  94.4 10.2 %collective-permute-done.14.refs_2_ = bf16[576,256]{1,0:T(8,128)(2,1)S(1)} collective-permute-done((bf16[576,256]{1,0:T(8,128)(2,1)S(1)}, bf16[576,256]{1,0:T(8,128)(2,1)S(1)}, u32[]{:S(2)}, u32[]{:S(2)}) %collective-permute-start.14) | collective-permute-done | bytes 294944 | tf_op jit(solution)/shard_map/ppermute | solution.py:405
  104.6 0.1 stack_columns.1
  104.6 1.6 collective-permute-start.17
  106.2 6.1 %collective-permute-start.10 = (bf16[2,160,512]{2,1,0:T(8,128)(2,1)S(1)}, bf16[2,160,512]{2,1,0:T(8,128)(2,1)S(1)}, u32[]{:S(2)}, u32[]{:S(2)}) collective-permute-start(bf16[2,160,512]{2,1,0:T(8,128)(2,1)S(1)} %get-tuple-element.40), channel_id=1, source_target_pairs={{0,4},{4,0},{8,12},{12,8},{1,5},{5,1},{9,13},{13,9},{2,6},{6,2},{1... | collective-permute-start | bytes 983048 | tf_op jit(solution)/shard_map/ppermute | solution.py:405
  112.3 6.9 %collective-permute-done.10.got_ref.refs_2_ = bf16[2,160,512]{2,1,0:T(8,128)(2,1)S(1)} collective-permute-done((bf16[2,160,512]{2,1,0:T(8,128)(2,1)S(1)}, bf16[2,160,512]{2,1,0:T(8,128)(2,1)S(1)}, u32[]{:S(2)}, u32[]{:S(2)}) %collective-permute-start.10) | collective-permute-done | bytes 327712 | tf_op jit(solution)/shard_map/ppermute | solution.py:405
  119.2 0.5 collective-permute-start.20
  119.8 0.5 collective-permute-start.18
  120.3 0.7 collective-permute-start.23
  121.0 1.3 collective-permute-start.24
  122.3 6.5 %down_grads.1 = (bf16[16,192,512]{2,1,0:T(8,128)(2,1)}, f32[8,128]{1,0:T(8,128)S(1)}) custom-call(s32[2]{0:T(128)S(1)} %pad_add_fusion.ids_ref, s32[4,16]{1,0:T(4,128)S(1)} %bitcast.14, bf16[4,192,256]{2,1,0:T(8,128)(2,1)S(1)} %get-tuple-element.50.refs_0_, bf16[4,192,256]{2,1,0:T(8,128)(2,1)S(1)} %collective-permute-done.16.refs_1_, ...), custom_call_target="tpu_custom_call" | custom-call | tf_op jit(solution)/shard_map/down_grads/pallas_call | solution.py:596
  128.9 8.2 %collective-permute-done.20.refs_1_ = bf16[4,384,256]{2,1,0:T(8,128)(2,1)S(1)} collective-permute-done((bf16[4,384,256]{2,1,0:T(8,128)(2,1)S(1)}, bf16[4,384,256]{2,1,0:T(8,128)(2,1)S(1)}, u32[]{:S(2)}, u32[]{:S(2)}) %collective-permute-start.20) | collective-permute-done | bytes 786464 | tf_op jit(solution)/shard_map/ppermute | solution.py:405
  137.1 0.5 collective-permute-start.22
  137.6 0.1 halve.3
  137.7 0.5 collective-permute-start.19
  138.2 10.3 %collective-permute-done.19.refs_1_ = bf16[1,160,512]{2,1,0:T(8,128)(2,1)S(1)} collective-permute-done((bf16[1,160,512]{2,1,0:T(8,128)(2,1)S(1)}, bf16[1,160,512]{2,1,0:T(8,128)(2,1)S(1)}, u32[]{:S(2)}, u32[]{:S(2)}) %collective-permute-start.19) | collective-permute-done | bytes 163872 | tf_op jit(solution)/shard_map/ppermute | solution.py:405
  148.4 0.8 token_grads.1
  149.3 2.8 %collective-permute-done.24.refs_10_ = bf16[1024,512]{1,0:T(8,128)(2,1)S(1)} collective-permute-done((bf16[1024,512]{1,0:T(8,128)(2,1)S(1)}, bf16[1024,512]{1,0:T(8,128)(2,1)S(1)}, u32[]{:S(2)}, u32[]{:S(2)}) %collective-permute-start.24) | collective-permute-done | bytes 1048608 | tf_op jit(solution)/shard_map/ppermute | solution.py:437
  152.0 8.3 %in_grads.1 = (bf16[16,384,512]{2,1,0:T(8,128)(2,1)}, f32[8,128]{1,0:T(8,128)}) custom-call(s32[2]{0:T(128)S(1)} %pad_add_fusion.ids_ref, s32[4,16]{1,0:T(4,128)S(1)} %bitcast.16, bf16[4,384,256]{2,1,0:T(8,128)(2,1)S(1)} %get-tuple-element.56.refs_0_, bf16[4,384,256]{2,1,0:T(8,128)(2,1)S(1)} %collective-permute-done.21.refs_1_, ...), custom_call_target="tpu_custom_call" | custom-call | tf_op jit(solution)/shard_map/in_grads/pallas_call | solution.py:596
  (37 shorter events, 0.1 us)
Async XLA Ops:
  3.2 10.0 %collective-permute-start.2 = (bf16[144,512]{1,0:T(8,128)(2,1)}, bf16[144,512]{1,0:T(8,128)(2,1)S(1)}, u32[]{:S(2)}, u32[]{:S(2)}) collective-permute-start(bf16[144,512]{1,0:T(8,128)(2,1)} %route.1.refs_0_), channel_id=1, source_target_pairs={{0,12},{4,8},{8,4},{12,0},{1,13},{5,9},{9,5},{13,1},{2,14},{6,10},... | collective-permute-start | bytes 442376 | tf_op jit(solution)/shard_map/ppermute | solution.py:405
  8.2 12.7 %collective-permute-start.1 = (bf16[144,512]{1,0:T(8,128)(2,1)}, bf16[144,512]{1,0:T(8,128)(2,1)S(1)}, u32[]{:S(2)}, u32[]{:S(2)}) collective-permute-start(bf16[144,512]{1,0:T(8,128)(2,1)} %route.1.refs_0_), channel_id=1, source_target_pairs={{0,8},{4,12},{8,0},{12,4},{1,9},{5,13},{9,1},{13,5},{2,10},{6,14},... | collective-permute-start | bytes 442376 | tf_op jit(solution)/shard_map/ppermute | solution.py:405
  8.2 12.7 %collective-permute-start = (bf16[144,512]{1,0:T(8,128)(2,1)}, bf16[144,512]{1,0:T(8,128)(2,1)S(1)}, u32[]{:S(2)}, u32[]{:S(2)}) collective-permute-start(bf16[144,512]{1,0:T(8,128)(2,1)} %route.1.refs_0_), channel_id=1, source_target_pairs={{0,4},{4,0},{8,12},{12,8},{1,5},{5,1},{9,13},{13,9},{2,6},{6,2},{1... | collective-permute-start | bytes 442376 | tf_op jit(solution)/shard_map/ppermute | solution.py:405
  20.9 0.7 copy-start.2
  21.6 41.7 %copy-start = (bf16[8,128,1536]{2,1,0:T(8,128)(2,1)S(1)}, bf16[8,128,1536]{2,1,0:T(8,128)(2,1)}, u32[]{:S(2)}) copy-start(bf16[8,128,1536]{2,1,0:T(8,128)(2,1)} %param.17) | copy-start | bytes 9437188
  21.6 26.7 %collective-permute-start.4 = (bf16[1024,512]{1,0:T(8,128)(2,1)}, bf16[1024,512]{1,0:T(8,128)(2,1)}, u32[]{:S(2)}, u32[]{:S(2)}) collective-permute-start(bf16[1024,512]{1,0:T(8,128)(2,1)} %gate.7), channel_id=1, source_target_pairs={{12,8},{8,4},{4,0},{13,9},{9,5},{5,1},{14,10},{10,6},{6,2},{15,11}... | collective-permute-start | bytes 3145736 | tf_op jit(solution)/shard_map/ppermute | solution.py:437
  23.1 26.3 %collective-permute-start.3 = (bf16[1024,512]{1,0:T(8,128)(2,1)}, bf16[1024,512]{1,0:T(8,128)(2,1)}, u32[]{:S(2)}, u32[]{:S(2)}) collective-permute-start(bf16[1024,512]{1,0:T(8,128)(2,1)} %gate.7), channel_id=1, source_target_pairs={{0,4},{4,8},{8,12},{1,5},{5,9},{9,13},{2,6},{6,10},{10,14},{3,7},{... | collective-permute-start | bytes 3145736 | tf_op jit(solution)/shard_map/ppermute | solution.py:436
  28.7 0.9 copy-start.3
  29.7 0.9 copy-start.4
  49.4 2.3 %collective-permute-start.5 = (bf16[2,256,768]{2,1,0:T(8,128)(2,1)S(1)}, bf16[2,256,768]{2,1,0:T(8,128)(2,1)S(1)}, u32[]{:S(2)}, u32[]{:S(2)}) collective-permute-start(bf16[2,256,768]{2,1,0:T(8,128)(2,1)S(1)} %gate.8), channel_id=1, source_target_pairs={{0,1},{1,0},{2,3},{3,2},{4,5},{5,4},{6,7},{7,6},{8,9},{9,8},{10,11... | collective-permute-start | bytes 2359304 | tf_op jit(solution)/shard_map/ppermute | solution.py:405
  49.4 28.4 %collective-permute-start.12 = (bf16[1024,512]{1,0:T(8,128)(2,1)}, bf16[1024,512]{1,0:T(8,128)(2,1)S(1)}, u32[]{:S(2)}, u32[]{:S(2)}) collective-permute-start(bf16[1024,512]{1,0:T(8,128)(2,1)} %collective-permute-done.4.refs_2_.refs_8_), channel_id=1, source_target_pairs={{8,4},{4,0},{9,5},{5,1},{10,6},{6,2},{11,7},{7,3},{24,20},{20,16},... | collective-permute-start | bytes 3145736 | tf_op jit(solution)/shard_map/ppermute | solution.py:437
  50.7 27.1 %collective-permute-start.11 = (bf16[1024,512]{1,0:T(8,128)(2,1)}, bf16[1024,512]{1,0:T(8,128)(2,1)S(1)}, u32[]{:S(2)}, u32[]{:S(2)}) collective-permute-start(bf16[1024,512]{1,0:T(8,128)(2,1)} %collective-permute-done.3.refs_1_.refs_5_), channel_id=1, source_target_pairs={{4,8},{8,12},{5,9},{9,13},{6,10},{10,14},{7,11},{11,15},{20,24},{2... | collective-permute-start | bytes 3145736 | tf_op jit(solution)/shard_map/ppermute | solution.py:436
  51.9 11.3 %collective-permute-start.6 = (bf16[1,256,768]{2,1,0:T(8,128)(2,1)S(1)}, bf16[1,256,768]{2,1,0:T(8,128)(2,1)S(1)}, u32[]{:S(2)}, u32[]{:S(2)}) collective-permute-start(bf16[1,256,768]{2,1,0:T(8,128)(2,1)S(1)} %get-tuple-element.36), channel_id=1, source_target_pairs={{0,2},{1,3},{2,0},{3,1},{4,6},{5,7},{6,4},{7,5},{8,10},{9,11},{10,... | collective-permute-start | bytes 1179656 | tf_op jit(solution)/shard_map/ppermute | solution.py:405
  65.0 10.5 %collective-permute-start.8 = (bf16[256,768]{1,0:T(8,128)(2,1)S(1)}, bf16[256,768]{1,0:T(8,128)(2,1)S(1)}, u32[]{:S(2)}, u32[]{:S(2)}) collective-permute-start(bf16[256,768]{1,0:T(8,128)(2,1)S(1)} %get-tuple-element.38.refs_0_), channel_id=1, source_target_pairs={{0,2},{1,3},{2,0},{3,1},{4,6},{5,7},{6,4},{7,5},{8,10},{9,11},{10,... | collective-permute-start | bytes 1179656 | tf_op jit(solution)/shard_map/ppermute | solution.py:405
  66.5 17.7 %collective-permute-start.7 = (bf16[256,768]{1,0:T(8,128)(2,1)S(1)}, bf16[256,768]{1,0:T(8,128)(2,1)S(1)}, u32[]{:S(2)}, u32[]{:S(2)}) collective-permute-start(bf16[256,768]{1,0:T(8,128)(2,1)S(1)} %get-tuple-element.38.refs_0_), channel_id=1, source_target_pairs={{0,1},{1,0},{2,3},{3,2},{4,5},{5,4},{6,7},{7,6},{8,9},{9,8},{10,11... | collective-permute-start | bytes 1179656 | tf_op jit(solution)/shard_map/ppermute | solution.py:405
  75.5 8.7 %collective-permute-start.9 = (bf16[256,768]{1,0:T(8,128)(2,1)S(1)}, bf16[256,768]{1,0:T(8,128)(2,1)S(1)}, u32[]{:S(2)}, u32[]{:S(2)}) collective-permute-start(bf16[256,768]{1,0:T(8,128)(2,1)S(1)} %collective-permute-done.8.refs_2_), channel_id=1, source_target_pairs={{0,1},{1,0},{2,3},{3,2},{4,5},{5,4},{6,7},{7,6},{8,9},{9,8},{10,11... | collective-permute-start | bytes 1179656 | tf_op jit(solution)/shard_map/ppermute | solution.py:405
  77.8 16.5 %collective-permute-start.13 = (bf16[576,256]{1,0:T(8,128)(2,1)S(1)}, bf16[576,256]{1,0:T(8,128)(2,1)S(1)}, u32[]{:S(2)}, u32[]{:S(2)}) collective-permute-start(bf16[576,256]{1,0:T(8,128)(2,1)S(1)} %get-tuple-element.47), channel_id=1, source_target_pairs={{0,4},{4,0},{8,12},{12,8},{1,5},{5,1},{9,13},{13,9},{2,6},{6,2},{1... | collective-permute-start | bytes 884744 | tf_op jit(solution)/shard_map/ppermute | solution.py:405
  81.1 23.4 %collective-permute-start.14 = (bf16[576,256]{1,0:T(8,128)(2,1)S(1)}, bf16[576,256]{1,0:T(8,128)(2,1)S(1)}, u32[]{:S(2)}, u32[]{:S(2)}) collective-permute-start(bf16[576,256]{1,0:T(8,128)(2,1)S(1)} %get-tuple-element.48), channel_id=1, source_target_pairs={{0,8},{4,12},{8,0},{12,4},{1,9},{5,13},{9,1},{13,5},{2,10},{6,14},... | collective-permute-start | bytes 884744 | tf_op jit(solution)/shard_map/ppermute | solution.py:405
  83.0 39.3 %copy-start.5 = (s32[16,4]{0,1:T(4,128)S(1)}, s32[16,4]{0,1:T(4,128)}, u32[]{:S(2)}) copy-start(s32[16,4]{0,1:T(4,128)} %param.14) | copy-start | bytes 772
  83.0 21.5 %collective-permute-start.15 = (bf16[576,256]{1,0:T(8,128)(2,1)S(1)}, bf16[576,256]{1,0:T(8,128)(2,1)S(1)}, u32[]{:S(2)}, u32[]{:S(2)}) collective-permute-start(bf16[576,256]{1,0:T(8,128)(2,1)S(1)} %get-tuple-element.49), channel_id=1, source_target_pairs={{0,12},{4,8},{8,4},{12,0},{1,13},{5,9},{9,5},{13,1},{2,14},{6,10},... | collective-permute-start | bytes 884744 | tf_op jit(solution)/shard_map/ppermute | solution.py:405
  92.5 55.9 %copy-start.6 = (s32[128,8]{0,1:T(8,128)S(1)}, s32[128,8]{0,1:T(8,128)}, u32[]{:S(2)}) copy-start(s32[128,8]{0,1:T(8,128)} %param.12) | copy-start | bytes 12292
  92.5 55.9 %copy-start.7 = (s32[128,8]{0,1:T(8,128)S(1)}, s32[128,8]{0,1:T(8,128)}, u32[]{:S(2)}) copy-start(s32[128,8]{0,1:T(8,128)} %param.13) | copy-start | bytes 12292
  92.5 59.5 %copy-start.1 = (bf16[8,4,32,512]{3,2,1,0:T(8,128)(2,1)S(1)}, bf16[8,4,32,512]{3,2,1,0:T(8,128)(2,1)}, u32[]{:S(2)}) copy-start(bf16[8,4,32,512]{3,2,1,0:T(8,128)(2,1)} %param.16) | copy-start | bytes 3145732
  104.6 14.6 %collective-permute-start.17 = (bf16[4,192,256]{2,1,0:T(8,128)(2,1)S(1)}, bf16[4,192,256]{2,1,0:T(8,128)(2,1)S(1)}, u32[]{:S(2)}, u32[]{:S(2)}) collective-permute-start(bf16[4,192,256]{2,1,0:T(8,128)(2,1)S(1)} %get-tuple-element.50.refs_0_), channel_id=1, source_target_pairs={{0,2},{1,3},{2,0},{3,1},{4,6},{5,7},{6,4},{7,5},{8,10},{9,11},{10,... | collective-permute-start | bytes 1179656 | tf_op jit(solution)/shard_map/ppermute | solution.py:405
  106.2 13.0 %collective-permute-start.10 = (bf16[2,160,512]{2,1,0:T(8,128)(2,1)S(1)}, bf16[2,160,512]{2,1,0:T(8,128)(2,1)S(1)}, u32[]{:S(2)}, u32[]{:S(2)}) collective-permute-start(bf16[2,160,512]{2,1,0:T(8,128)(2,1)S(1)} %get-tuple-element.40), channel_id=1, source_target_pairs={{0,4},{4,0},{8,12},{12,8},{1,5},{5,1},{9,13},{13,9},{2,6},{6,2},{1... | collective-permute-start | bytes 983048 | tf_op jit(solution)/shard_map/ppermute | solution.py:405
  119.2 17.9 %collective-permute-start.20 = (bf16[4,384,256]{2,1,0:T(8,128)(2,1)S(1)}, bf16[4,384,256]{2,1,0:T(8,128)(2,1)S(1)}, u32[]{:S(2)}, u32[]{:S(2)}) collective-permute-start(bf16[4,384,256]{2,1,0:T(8,128)(2,1)S(1)} %gate.11.refs_0_), channel_id=1, source_target_pairs={{0,2},{1,3},{2,0},{3,1},{4,6},{5,7},{6,4},{7,5},{8,10},{9,11},{10,... | collective-permute-start | bytes 2359304 | tf_op jit(solution)/shard_map/ppermute | solution.py:405
  119.8 2.5 %collective-permute-start.16 = (bf16[4,192,256]{2,1,0:T(8,128)(2,1)S(1)}, bf16[4,192,256]{2,1,0:T(8,128)(2,1)S(1)}, u32[]{:S(2)}, u32[]{:S(2)}) collective-permute-start(bf16[4,192,256]{2,1,0:T(8,128)(2,1)S(1)} %get-tuple-element.50.refs_0_), channel_id=1, source_target_pairs={{0,1},{1,0},{2,3},{3,2},{4,5},{5,4},{6,7},{7,6},{8,9},{9,8},{10,11... | collective-permute-start | bytes 1179656 | tf_op jit(solution)/shard_map/ppermute | solution.py:405
  119.8 2.5 %collective-permute-start.18 = (bf16[4,192,256]{2,1,0:T(8,128)(2,1)S(1)}, bf16[4,192,256]{2,1,0:T(8,128)(2,1)S(1)}, u32[]{:S(2)}, u32[]{:S(2)}) collective-permute-start(bf16[4,192,256]{2,1,0:T(8,128)(2,1)S(1)} %collective-permute-done.17.refs_2_.refs_1_), channel_id=1, source_target_pairs={{0,1},{1,0},{2,3},{3,2},{4,5},{5,4},{6,7},{7,6},{8,9},{9,8},{10,11... | collective-permute-start | bytes 1179656 | tf_op jit(solution)/shard_map/ppermute | solution.py:405
  120.3 29.0 %collective-permute-start.23 = (bf16[1024,512]{1,0:T(8,128)(2,1)S(1)}, bf16[1024,512]{1,0:T(8,128)(2,1)S(1)}, u32[]{:S(2)}, u32[]{:S(2)}) collective-permute-start(bf16[1024,512]{1,0:T(8,128)(2,1)S(1)} %get-tuple-element.58.refs_6_), channel_id=1, source_target_pairs={{8,12},{9,13},{10,14},{11,15},{24,28},{25,29},{26,30},{27,31}} | collective-permute-start | bytes 3145736 | tf_op jit(solution)/shard_map/ppermute | solution.py:436
  121.0 31.0 %collective-permute-start.24 = (bf16[1024,512]{1,0:T(8,128)(2,1)S(1)}, bf16[1024,512]{1,0:T(8,128)(2,1)S(1)}, u32[]{:S(2)}, u32[]{:S(2)}) collective-permute-start(bf16[1024,512]{1,0:T(8,128)(2,1)S(1)} %get-tuple-element.59.refs_9_), channel_id=1, source_target_pairs={{4,0},{5,1},{6,2},{7,3},{20,16},{21,17},{22,18},{23,19}} | collective-permute-start | bytes 3145736 | tf_op jit(solution)/shard_map/ppermute | solution.py:437
  137.1 14.9 %collective-permute-start.21 = (bf16[4,384,256]{2,1,0:T(8,128)(2,1)S(1)}, bf16[4,384,256]{2,1,0:T(8,128)(2,1)S(1)}, u32[]{:S(2)}, u32[]{:S(2)}) collective-permute-start(bf16[4,384,256]{2,1,0:T(8,128)(2,1)S(1)} %get-tuple-element.56.refs_0_), channel_id=1, source_target_pairs={{0,1},{1,0},{2,3},{3,2},{4,5},{5,4},{6,7},{7,6},{8,9},{9,8},{10,11... | collective-permute-start | bytes 2359304 | tf_op jit(solution)/shard_map/ppermute | solution.py:405
  137.1 14.9 %collective-permute-start.22 = (bf16[4,384,256]{2,1,0:T(8,128)(2,1)S(1)}, bf16[4,384,256]{2,1,0:T(8,128)(2,1)S(1)}, u32[]{:S(2)}, u32[]{:S(2)}) collective-permute-start(bf16[4,384,256]{2,1,0:T(8,128)(2,1)S(1)} %get-tuple-element.57.refs_2_), channel_id=1, source_target_pairs={{0,1},{1,0},{2,3},{3,2},{4,5},{5,4},{6,7},{7,6},{8,9},{9,8},{10,11... | collective-permute-start | bytes 2359304 | tf_op jit(solution)/shard_map/ppermute | solution.py:405
  137.7 10.7 %collective-permute-start.19 = (bf16[1,160,512]{2,1,0:T(8,128)(2,1)S(1)}, bf16[1,160,512]{2,1,0:T(8,128)(2,1)S(1)}, u32[]{:S(2)}, u32[]{:S(2)}) collective-permute-start(bf16[1,160,512]{2,1,0:T(8,128)(2,1)S(1)} %gate.10), channel_id=1, source_target_pairs={{0,8},{4,12},{8,0},{12,4},{1,9},{5,13},{9,1},{13,5},{2,10},{6,14},... | collective-permute-start | bytes 491528 | tf_op jit(solution)/shard_map/ppermute | solution.py:405

commit v9 on v8

--- a/solution.py
+++ b/solution.py
@@ -145,8 +145,8 @@
 def down_kernel(z, ids_ref, *refs):
     bufs = refs[: z.ep]
     weight_ref = refs[z.ep]
-    parts = refs[z.ep + 1 : z.ep + 3]
-    grads_ref, codes_ref, rows_ref, held, sems = refs[z.ep + 3 :]
+    parts = refs[z.ep + 2 : z.ep + 4]
+    grads_ref, codes_ref, rows_ref, held, sems = refs[z.ep + 4 :]
     me, mine = ids_ref[0], ids_ref[1]
     step = pl.program_id(0)
 
@@ -203,21 +203,29 @@
     scale = block_scale(z, codes_ref, me * z.local + slot, first)
     grad = keep_ref[0].astype(F32) + got_ref[0].astype(F32)
     grad_ref[...] = grad.astype(BF)
-    hidden, grad_gate, grad_up = gate_terms(z, pair_ref[...], grad, scale)
-    hidden = hidden.astype(BF).T
-    pre = jnp.concatenate([grad_gate.T, grad_up.T], axis=0)
+    _, grad_gate, grad_up = gate_terms(z, pair_ref[...], grad, scale)
+    send_columns(z, me, jnp.concatenate([grad_gate.T, grad_up.T], axis=0), sides, outs)
+
+
+def send_columns(z, me, columns, sides, outs):
+    size = columns.shape[0] // z.ep
     for q in range(z.ep):
-        sides[q, : z.in_cols, :] = pre[q * z.in_cols : (q + 1) * z.in_cols, :]
-        sides[q, z.in_cols :, :] = hidden[q * z.down_cols : (q + 1) * z.down_cols, :]
+        sides[q] = columns[q * size : (q + 1) * size, :]
     for k in range(z.ep):
         outs[k][...] = sides[me ^ k]
 
 
+def hidden_kernel(z, ids_ref, pair_ref, after_ref, other_ref, *refs):
+    pair = pair_ref[...]
+    gate_pre = pair[:, : z.hidden].astype(F32)
+    up = pair[:, z.hidden :].astype(F32)
+    hidden = gate_pre * (1.0 / (1.0 + jnp.exp(-gate_pre))) * up
+    send_columns(z, ids_ref[0], hidden.astype(BF).T, refs[-1], refs[:-1])
+
+
 def stack_kernel(z, *refs):
-    refs = refs[: z.ep] + refs[-2:]
     for k in range(z.ep):
-        refs[-2][k] = refs[k][: z.in_cols, :]
-        refs[-1][k] = refs[k][z.in_cols :, :]
+        refs[-1][k] = refs[k][...]
 
 
 def row_kernel(z, ids_ref, *refs):
@@ -314,6 +322,10 @@
                     lefts[d - 1], inputs_ref.at[me + d], left_sems.at[d - 1]
                 )
             )
+
+
+def left_rows(held, part, side, spot, size):
+    return held[part, side, :, pl.ds(spot, size)]
 
 
 def expert_products(z, ids_ref, table_ref, turn, held, right_rows, out_ref, made, out_sems):
@@ -337,10 +349,26 @@
                     side = source ^ turn
                     if r:
                         side = jnp.where(slot_id == first, z.ep, side)
-                    left.append(held[part, side, :, pl.ds(spot, z.block)])
-                    right.append(right_rows(slot_id, block, b))
-            left = jnp.concatenate(left, axis=1)
-            made[expert] = nn(left, jnp.concatenate(right, axis=0)).astype(BF)
+                    left.append(functools.partial(left_rows, held, part, side, spot, z.block))
+                    right.append(functools.partial(right_rows, slot_id, block, b))
+            half = len(left) // 2
+
+            def product(lo, hi):
+                return nn(
+                    jnp.concatenate([f() for f in left[lo:hi]], axis=1),
+                    jnp.concatenate([f() for f in right[lo:hi]], axis=0),
+                )
+
+            few = table_ref[z.reps // 2, expert] == first
+
+            @pl.when(few)
+            def _():
+                made[expert] = product(0, half).astype(BF)
+
+            @pl.when(jnp.logical_not(few))
+            def _():
+                made[expert] = product(0, 2 * half).astype(BF)
+
             out_copy(expert).start()
         return carry
 
@@ -472,21 +500,39 @@
     )(token_count, *routing)
     bufs = [buf] + [swap(buf, "ep", n, k) for k in range(1, n)]
 
-    chain = gate([inputs], bufs[1:])
+    chain = gate([inputs], [buf])
+    downs = pl.pallas_call(
+        functools.partial(hidden_kernel, z),
+        grid_spec=pltpu.PrefetchScalarGridSpec(
+            num_scalar_prefetch=1,
+            grid=(z.part_blocks,),
+            in_specs=[
+                pl.BlockSpec((z.block, z.pair), lambda i, r: (r[1] * z.part_blocks + i, 0)),
+                pl.BlockSpec(memory_space=pl.ANY),
+                pl.BlockSpec(memory_space=pl.ANY),
+            ],
+            out_specs=[pl.BlockSpec((z.down_cols, z.block), lambda i, r: (0, i))] * n,
+            scratch_shapes=[pltpu.VMEM((n, z.down_cols, z.block), BF)],
+        ),
+        out_shape=[jax.ShapeDtypeStruct((z.down_cols, z.part), BF)] * n,
+        compiler_params=params(16),
+        name="hidden_columns",
+    )(ids, pair_rows, bufs[1], chain[0])
+    downs = [downs[0]] + [swap(downs[k], "ep", n, k) for k in range(1, n)]
+    chain = gate(chain, bufs[1:] + downs[1:])
     steps = [chain_step(chain[0], chain[0], "ep", n, 1)]
-    steps.append(chain_step(*steps[0], "ep", n, 2))
-
-    def stack(pieces, after):
-        shapes = [(n, z.in_cols, z.part), (n, z.down_cols, z.part)]
+
+    def stack(pieces):
+        shape = pieces[0].shape
         return pl.pallas_call(
             functools.partial(stack_kernel, z),
-            in_specs=[whole((z.cols, z.part))] * n + [pl.BlockSpec(memory_space=pl.ANY)],
-            out_specs=[whole(shape) for shape in shapes],
-            out_shape=[jax.ShapeDtypeStruct(shape, BF) for shape in shapes],
+            in_specs=[whole(shape)] * n,
+            out_specs=whole((n,) + shape),
+            out_shape=jax.ShapeDtypeStruct((n,) + shape, BF),
             grid=(1,),
             compiler_params=params(12),
             name="stack_columns",
-        )(*pieces, after)
+        )(*pieces)
 
     def halve(keep, got):
         half = (keep.shape[0] // 2,) + keep.shape[1:]
@@ -510,7 +556,8 @@
         grid_spec=pltpu.PrefetchScalarGridSpec(
             num_scalar_prefetch=1,
             grid=(z.blocks,),
-            in_specs=[whole(grad_shape)] * n + [pl.BlockSpec(memory_space=pltpu.HBM)],
+            in_specs=[whole(grad_shape)] * n
+            + [pl.BlockSpec(memory_space=pltpu.HBM), pl.BlockSpec(memory_space=pl.ANY)],
             out_specs=[whole(part_shape)] * 2
             + [whole((n, z.tokens, z.width)), whole(code_shape)],
             scratch_shapes=[
@@ -526,9 +573,43 @@
         ],
         compiler_params=params(48),
         name="hidden_partials",
-    )(ids, *bufs, weight_down)
+    )(ids, *bufs, weight_down, *downs[:1])
     keep, send, grads_all, codes = outs
-    send = gate([send], steps[0])[0]
+    down_sides = spread_over({0: stack(downs)}, "sub", m, m // 2)
+    def total_call(kernel, operands, specs, cols, scratch, name):
+        return pl.pallas_call(
+            functools.partial(kernel, z),
+            grid_spec=pltpu.PrefetchScalarGridSpec(
+                num_scalar_prefetch=2,
+                grid=(1,),
+                in_specs=specs,
+                out_specs=[pl.BlockSpec(memory_space=pl.ANY), whole((8, 128))],
+                scratch_shapes=[
+                    pltpu.VMEM((m, n + 1, cols, z.part), BF),
+                    pltpu.VMEM((z.experts, cols, z.width), BF),
+                    pltpu.SemaphoreType.DMA((z.experts,)),
+                ]
+                + scratch,
+            ),
+            out_shape=[
+                jax.ShapeDtypeStruct((z.experts, cols, z.width), BF),
+                jax.ShapeDtypeStruct((8, 128), F32),
+            ],
+            compiler_params=params(32),
+            name=name,
+        )(ids, table, *operands)
+
+    anywhere = pl.BlockSpec(memory_space=pl.ANY)
+    grad_down, down_made = total_call(
+        total_down_kernel,
+        [*down_sides, grads_all, codes],
+        [anywhere] * m + [whole((n, z.tokens, z.width)), whole(code_shape)],
+        z.down_cols,
+        [pltpu.VMEM((z.slots, z.rows, z.width), BF), pltpu.SemaphoreType.DMA((m,))],
+        "down_grads",
+    )
+    steps[0] = gate(steps[0], [down_made])
+    steps.append(chain_step(*steps[0], "ep", n, 2))
     got = swap(send, "sub", m, 1)
     bit = 2
     while bit < m:
@@ -545,11 +626,11 @@
                 pl.BlockSpec((z.block, z.pair), lambda i, r: (r[1] * z.part_blocks + i, 0)),
                 whole(code_shape),
             ],
-            out_specs=[pl.BlockSpec((z.cols, z.block), lambda i, r: (0, i))] * n
+            out_specs=[pl.BlockSpec((z.in_cols, z.block), lambda i, r: (0, i))] * n
             + [pl.BlockSpec((z.block, z.hidden), lambda i, r: (i, 0))],
-            scratch_shapes=[pltpu.VMEM((n, z.cols, z.block), BF)],
+            scratch_shapes=[pltpu.VMEM((n, z.in_cols, z.block), BF)],
         ),
-        out_shape=[jax.ShapeDtypeStruct((z.cols, z.part), BF)] * n
+        out_shape=[jax.ShapeDtypeStruct((z.in_cols, z.part), BF)] * n
         + [jax.ShapeDtypeStruct((z.part, z.hidden), BF)],
         compiler_params=params(16),
         name="pre_grads",
@@ -583,70 +664,19 @@
         compiler_params=params(46),
         name="row_grads",
     )(ids, *grad_parts, pair_rows, weight_in, codes)
-    columns, down_columns = stack(pieces, keep)
-    down_sides = spread_over({0: down_columns}, "sub", m, m // 2)
-    got = swap(send, "ep", n, 1)
-    sides = {0: gate([columns], [down_sides[m // 2], got])[0]}
-    sides[m // 2] = swap(sides[0], "sub", m, m // 2)
-    steps[1] = gate(steps[1], [got])
     for d in range(3, n):
         steps.append(chain_step(*steps[-1], "ep", n, d))
     gathered = [inputs] + [go for go, _ in steps] + [back for _, back in steps]
-    def total_call(kernel, operands, specs, cols, scratch, name):
-        return pl.pallas_call(
-            functools.partial(kernel, z),
-            grid_spec=pltpu.PrefetchScalarGridSpec(
-                num_scalar_prefetch=2,
-                grid=(1,),
-                in_specs=specs,
-                out_specs=[pl.BlockSpec(memory_space=pl.ANY), whole((8, 128))],
-                scratch_shapes=[
-                    pltpu.VMEM((m, n + 1, cols, z.part), BF),
-                    pltpu.VMEM((z.experts, cols, z.width), BF),
-                    pltpu.SemaphoreType.DMA((z.experts,)),
-                ]
-                + scratch,
-            ),
-            out_shape=[
-                jax.ShapeDtypeStruct((z.experts, cols, z.width), BF),
-                jax.ShapeDtypeStruct((8, 128), F32),
-            ],
-            compiler_params=params(32),
-            name=name,
-        )(ids, table, *operands)
-
-    anywhere = pl.BlockSpec(memory_space=pl.ANY)
-    grad_down, down_made = total_call(
-        total_down_kernel,
-        [*down_sides, grads_all, codes],
-        [anywhere] * m + [whole((n, z.tokens, z.width)), whole(code_shape)],
-        z.down_cols,
-        [pltpu.VMEM((z.slots, z.rows, z.width), BF), pltpu.SemaphoreType.DMA((m,))],
-        "down_grads",
-    )
-    sides[0], sides[m // 2] = gate([sides[0], sides[m // 2]], [down_made])
-    sides = spread_over(sides, "sub", m, m // 4)
+    got = swap(send, "ep", n, 1)
+    pieces[:1] = gate(pieces[:1], [got])
+    sides = spread_over({0: stack(pieces)}, "sub", m, m // 2)
     bit = 2
     while bit < n:
         keep, send = halve(keep, got)
-        send = gate([send], [down_made])[0]
         got = swap(send, "ep", n, bit)
         bit *= 2
 
-    grad_tokens, grad_routes = pl.pallas_call(
-        functools.partial(token_kernel, z),
-        out_shape=[
-            jax.ShapeDtypeStruct((z.tokens, z.width), BF),
-            jax.ShapeDtypeStruct((z.top, z.tokens), BF),
-        ],
-        in_specs=[smem()] + [whole(a.shape) for a in (keep, got, routes, replica, table)],
-        out_specs=[whole((z.tokens, z.width)), whole((z.top, z.tokens))],
-        grid=(1,),
-        compiler_params=params(16),
-        name="token_grads",
-    )(token_count, keep, got, routes, replica, table)
-
-    grad_in, _ = total_call(
+    grad_in, in_made = total_call(
         total_in_kernel,
         [*sides, *gathered],
         [anywhere] * (m + 2 * n - 1),
@@ -660,6 +690,20 @@
         ],
         "in_grads",
     )
+    got = gate([got], [in_made])[0]
+    grad_tokens, grad_routes = pl.pallas_call(
+        functools.partial(token_kernel, z),
+        out_shape=[
+            jax.ShapeDtypeStruct((z.tokens, z.width), BF),
+            jax.ShapeDtypeStruct((z.top, z.tokens), BF),
+        ],
+        in_specs=[smem()] + [whole(a.shape) for a in (keep, got, routes, replica, table)],
+        out_specs=[whole((z.tokens, z.width)), whole((z.top, z.tokens))],
+        grid=(1,),
+        compiler_params=params(16),
+        name="token_grads",
+    )(token_count, keep, got, routes, replica, table)
+
     return grad_tokens, grad_routes.T, grad_in, grad_down
 
 

time: 161 us -> 160 us (level)
  waiting for transfers between devices: 84.8 us -> 78.3 us
  starting transfers between devices: 35.9 us -> 41.4 us
  Pallas kernels: 33.4 us -> 36.1 us
  local copies, waits for them, and re-layouts: 4.76 us -> 2.16 us
    ppermute x19 -> x22, starting transfers between devices: 24.8 us -> 31.5 us  [swap(): return lax.ppermute(x, axis, [(i, i ^ bit) for i in range(size)])]
    ppermute x3, waiting for transfers between devices: 17.3 us -> 13 us  [chain_step(): lax.ppermute(back, axis, [(i, i - 1) for i in range(size - d, 0, -1)])]
    unnamed x17 -> x15, local copies, waits for them, and re-layouts: 4.76 us -> 2.16 us
    ppermute x19 -> x22, waiting for transfers between devices: 66.3 us -> 64.1 us  [swap(): return lax.ppermute(x, axis, [(i, i ^ bit) for i in range(size)])]
  transfers between devices with their start and end apart: 25 -> 28, of which waited for: 14 -> 10; matrix products, arithmetic and copies ran while one was open for 1% -> 1% of each run, Pallas kernels for 14% -> 21%
where the time goes in v9:
time: 160 us
  waiting for transfers between devices  78.3 us (49%)
  starting transfers between devices  41.4 us (26%)
  Pallas kernels  36.1 us (23%)
  local copies, waits for them, and re-layouts  2.16 us (1%)
  between operations  1.72 us (1%)
    ppermute x22, waiting for transfers between devices, swap(): return lax.ppermute(x, axis, [(i, i ^ bit) for i in range(size)])  64.1 us
    ppermute x22, starting transfers between devices, swap(): return lax.ppermute(x, axis, [(i, i ^ bit) for i in range(size)])  31.5 us
    pallas_call x2, Pallas kernels, total_call(): pl.pallas_call(functools.partial(kernel, z), grid_spec=pltpu.PrefetchScal...  15.5 us
    ppermute x3, waiting for transfers between devices, chain_step(): lax.ppermute(back, axis, [(i, i - 1) for i in range(size - d, 0, -1)])  13 us
    pallas_call x1, Pallas kernels, body(): pl.pallas_call(functools.partial(row_kernel, z), grid_spec=pltpu.Prefetch...  8.32 us
    pallas_call x1, Pallas kernels, body(): pl.pallas_call(functools.partial(down_kernel, z), grid_spec=pltpu.Prefetc...  6.39 us
    ppermute x3, starting transfers between devices, chain_step(): go = lax.ppermute(go, axis, [(i, i + 1) for i in range(d - 1, size - 1)])  6.04 us
    ppermute x3, starting transfers between devices, chain_step(): lax.ppermute(back, axis, [(i, i - 1) for i in range(size - d, 0, -1)])  3.88 us
  transfers between devices with their start and end apart: 28, of which 10 were waited for; matrix products, arithmetic and copies ran while one was open for 1% of the time, Pallas kernels for 21%

profile of v9, /device:TPU:0, one launch (start us, length us, event | category | flops | bytes accessed | tf_op | source)
XLA Modules:
  0.0 159.7 jit_solution(24615570827565710)
XLA Ops:
  1.4 2.0 %route.1.refs_1_.refs_0_ = bf16[144,512]{1,0:T(8,128)(2,1)} custom-call(s32[1]{0:T(128)S(6)} %copy.32.count_ref, bf16[128,512]{1,0:T(8,128)(2,1)} %grad_ref.1, bf16[8,128]{1,0:T(8,128)(2,1)} %bitcast.22, s32[8,128]{1,0:T(8,128)} %bitcast.18, s32[8,128]{1,0:T(8,128)} %bitcast.20, s32[4,16]{1,0:T(4,128)} %bitcast.14), custom_call_target="tpu_custom_call" | custom-call | tf_op jit(solution)/shard_map/route/pallas_call | solution.py:492
  3.5 3.0 %collective-permute-start = (bf16[144,512]{1,0:T(8,128)(2,1)}, bf16[144,512]{1,0:T(8,128)(2,1)S(1)}, u32[]{:S(2)}, u32[]{:S(2)}) collective-permute-start(bf16[144,512]{1,0:T(8,128)(2,1)} %route.1.refs_1_.refs_0_), channel_id=1, source_target_pairs={{0,4},{4,0},{8,12},{12,8},{1,5},{5,1},{9,13},{13,9},{2,6},{6,2},{1... | collective-permute-start | bytes 442376 | tf_op jit(solution)/shard_map/ppermute | solution.py:433
  6.5 2.5 %collective-permute-start.2 = (bf16[144,512]{1,0:T(8,128)(2,1)}, bf16[144,512]{1,0:T(8,128)(2,1)S(1)}, u32[]{:S(2)}, u32[]{:S(2)}) collective-permute-start(bf16[144,512]{1,0:T(8,128)(2,1)} %route.1.refs_1_.refs_0_), channel_id=1, source_target_pairs={{0,12},{4,8},{8,4},{12,0},{1,13},{5,9},{9,5},{13,1},{2,14},{6,10},... | collective-permute-start | bytes 442376 | tf_op jit(solution)/shard_map/ppermute | solution.py:433
  9.0 0.1 collective-permute-start.1
  9.1 0.1 pad_add_fusion.ids_ref
  9.2 1.2 copy.23.refs_0_
  10.4 0.9 copy-done.2
  11.3 1.1 hidden_columns.1
  12.4 0.0 copy-start.4
  12.4 2.0 %collective-permute-start.10 = (bf16[192,256]{1,0:T(8,128)(2,1)S(1)}, bf16[192,256]{1,0:T(8,128)(2,1)S(1)}, u32[]{:S(2)}, u32[]{:S(2)}) collective-permute-start(bf16[192,256]{1,0:T(8,128)(2,1)S(1)} %get-tuple-element.49), channel_id=1, source_target_pairs={{0,4},{4,0},{8,12},{12,8},{1,5},{5,1},{9,13},{13,9},{2,6},{6,2},{1... | collective-permute-start | bytes 294920 | tf_op jit(solution)/shard_map/ppermute | solution.py:433
  14.4 4.0 %collective-permute-start.11 = (bf16[192,256]{1,0:T(8,128)(2,1)S(1)}, bf16[192,256]{1,0:T(8,128)(2,1)S(1)}, u32[]{:S(2)}, u32[]{:S(2)}) collective-permute-start(bf16[192,256]{1,0:T(8,128)(2,1)S(1)} %get-tuple-element.50), channel_id=1, source_target_pairs={{0,8},{4,12},{8,0},{12,4},{1,9},{5,13},{9,1},{13,5},{2,10},{6,14},... | collective-permute-start | bytes 294920 | tf_op jit(solution)/shard_map/ppermute | solution.py:433
  18.4 9.4 %collective-permute-done.1.refs_2_ = bf16[144,512]{1,0:T(8,128)(2,1)} collective-permute-done((bf16[144,512]{1,0:T(8,128)(2,1)}, bf16[144,512]{1,0:T(8,128)(2,1)}, u32[]{:S(2)}, u32[]{:S(2)}) %collective-permute-start.1) | collective-permute-done | bytes 147488 | tf_op jit(solution)/shard_map/ppermute | solution.py:433
  27.8 6.4 %hidden_partials.1 = (bf16[2,256,768]{2,1,0:T(8,128)(2,1)S(1)}, bf16[2,256,768]{2,1,0:T(8,128)(2,1)S(1)}, bf16[4,128,512]{2,1,0:T(8,128)(2,1)S(1)}, f32[4,64,128]{2,1,0:T(8,128)S(1)}) custom-call(s32[2]{0:T(128)S(1)} %pad_add_fusion.ids_ref, bf16[144,512]{1,0:T(8,128)(2,1)S(1)} %copy-done.3, bf16[144,512]{1,0:T(8,128)(2,1)S(1)} %collective-permute-done.after_ref.refs_1_, ...), custom_call_target="tpu_custom_call" | custom-call | tf_op jit(solution)/shard_map/hidden_partials/pallas_call | solution.py:554
  34.2 0.1 collective-permute-start.3
  34.3 1.3 collective-permute-start.14
  35.6 4.6 %collective-permute-start.13 = (bf16[1024,512]{1,0:T(8,128)(2,1)S(1)}, bf16[1024,512]{1,0:T(8,128)(2,1)S(1)}, u32[]{:S(2)}, u32[]{:S(2)}) collective-permute-start(bf16[1024,512]{1,0:T(8,128)(2,1)S(1)} %gate.8), channel_id=1, source_target_pairs={{0,4},{4,8},{8,12},{1,5},{5,9},{9,13},{2,6},{6,10},{10,14},{3,7},{... | collective-permute-start | bytes 3145736 | tf_op jit(solution)/shard_map/ppermute | solution.py:464
  40.3 2.5 %collective-permute-start.16 = (bf16[4,192,256]{2,1,0:T(8,128)(2,1)S(1)}, bf16[4,192,256]{2,1,0:T(8,128)(2,1)S(1)}, u32[]{:S(2)}, u32[]{:S(2)}) collective-permute-start(bf16[4,192,256]{2,1,0:T(8,128)(2,1)S(1)} %stack_columns.2.refs_0_), channel_id=1, source_target_pairs={{0,2},{1,3},{2,0},{3,1},{4,6},{5,7},{6,4},{7,5},{8,10},{9,11},{10,... | collective-permute-start | bytes 1179656 | tf_op jit(solution)/shard_map/ppermute | solution.py:433
  42.8 9.2 %collective-permute-done.16.refs_2_ = bf16[4,192,256]{2,1,0:T(8,128)(2,1)S(1)} collective-permute-done((bf16[4,192,256]{2,1,0:T(8,128)(2,1)S(1)}, bf16[4,192,256]{2,1,0:T(8,128)(2,1)S(1)}, u32[]{:S(2)}, u32[]{:S(2)}) %collective-permute-start.16) | collective-permute-done | bytes 393248 | tf_op jit(solution)/shard_map/ppermute | solution.py:433
  52.0 0.2 halve.2
  52.2 1.8 %collective-permute-start.4 = (bf16[1,256,768]{2,1,0:T(8,128)(2,1)S(1)}, bf16[1,256,768]{2,1,0:T(8,128)(2,1)S(1)}, u32[]{:S(2)}, u32[]{:S(2)}) collective-permute-start(bf16[1,256,768]{2,1,0:T(8,128)(2,1)S(1)} %get-tuple-element.38), channel_id=1, source_target_pairs={{0,2},{1,3},{2,0},{3,1},{4,6},{5,7},{6,4},{7,5},{8,10},{9,11},{10,... | collective-permute-start | bytes 1179656 | tf_op jit(solution)/shard_map/ppermute | solution.py:433
  54.0 7.8 %down_grads.1 = (bf16[16,192,512]{2,1,0:T(8,128)(2,1)}, f32[8,128]{1,0:T(8,128)S(1)}) custom-call(s32[2]{0:T(128)S(1)} %pad_add_fusion.ids_ref, s32[4,16]{1,0:T(4,128)S(1)} %bitcast.15, bf16[4,192,256]{2,1,0:T(8,128)(2,1)S(1)} %stack_columns.2.refs_0_, bf16[4,192,256]{2,1,0:T(8,128)(2,1)S(1)} %collective-permute-done.15.refs_1_, ...), custom_call_target="tpu_custom_call" | custom-call | tf_op jit(solution)/shard_map/down_grads/pallas_call | solution.py:580
  61.8 1.1 collective-permute-done.13.refs_0_
  63.0 0.7 collective-permute-start.18
  63.7 1.3 collective-permute-start.19
  65.0 1.6 %pre_grads.1 = (bf16[384,256]{1,0:T(8,128)(2,1)S(1)}, bf16[384,256]{1,0:T(8,128)(2,1)S(1)}, bf16[384,256]{1,0:T(8,128)(2,1)S(1)}, bf16[384,256]{1,0:T(8,128)(2,1)S(1)}, bf16[256,768]{1,0:T(8,128)(2,1)S(1)}) custom-call(s32[2]{0:T(128)S(1)} %pad_add_fusion.ids_ref, bf16[1,256,768]{2,1,0:T(8,128)(2,1)S(1)} %get-tuple-element.37.keep_ref, ...), custom_call_target="tpu_custom_call" | custom-call | tf_op jit(solution)/shard_map/pre_grads/pallas_call | solution.py:619
  66.6 2.5 %collective-permute-start.6 = (bf16[256,768]{1,0:T(8,128)(2,1)S(1)}, bf16[256,768]{1,0:T(8,128)(2,1)S(1)}, u32[]{:S(2)}, u32[]{:S(2)}) collective-permute-start(bf16[256,768]{1,0:T(8,128)(2,1)S(1)} %get-tuple-element.40.refs_0_), channel_id=1, source_target_pairs={{0,2},{1,3},{2,0},{3,1},{4,6},{5,7},{6,4},{7,5},{8,10},{9,11},{10,... | collective-permute-start | bytes 1179656 | tf_op jit(solution)/shard_map/ppermute | solution.py:433
  69.1 8.7 %collective-permute-done.6.refs_2_ = bf16[256,768]{1,0:T(8,128)(2,1)S(1)} collective-permute-done((bf16[256,768]{1,0:T(8,128)(2,1)S(1)}, bf16[256,768]{1,0:T(8,128)(2,1)S(1)}, u32[]{:S(2)}, u32[]{:S(2)}) %collective-permute-start.6) | collective-permute-done | bytes 393248 | tf_op jit(solution)/shard_map/ppermute | solution.py:433
  77.8 1.7 %collective-permute-done.7.refs_3_ = bf16[256,768]{1,0:T(8,128)(2,1)S(1)} collective-permute-done((bf16[256,768]{1,0:T(8,128)(2,1)S(1)}, bf16[256,768]{1,0:T(8,128)(2,1)S(1)}, u32[]{:S(2)}, u32[]{:S(2)}) %collective-permute-start.7) | collective-permute-done | bytes 393248 | tf_op jit(solution)/shard_map/ppermute | solution.py:433
  79.5 8.3 %row_grads.1 = (bf16[2,160,512]{2,1,0:T(8,128)(2,1)S(1)}, bf16[2,160,512]{2,1,0:T(8,128)(2,1)S(1)}) custom-call(s32[2]{0:T(128)S(1)} %pad_add_fusion.ids_ref, bf16[256,768]{1,0:T(8,128)(2,1)S(1)} %get-tuple-element.40.refs_0_, bf16[256,768]{1,0:T(8,128)(2,1)S(1)} %collective-permute-done.5.refs_1_, bf16[256,768]{1,0:T(8,128)(2,1)S(1)} %collective-permute-done.6.refs_2_, ...), custom_call_target="tpu_custom_call" | custom-call | tf_op jit(solution)/shard_map/row_grads/pallas_call | solution.py:643
  87.8 0.0 copy-start.1
  87.8 4.7 %collective-permute-start.8 = (bf16[2,160,512]{2,1,0:T(8,128)(2,1)S(1)}, bf16[2,160,512]{2,1,0:T(8,128)(2,1)S(1)}, u32[]{:S(2)}, u32[]{:S(2)}) collective-permute-start(bf16[2,160,512]{2,1,0:T(8,128)(2,1)S(1)} %get-tuple-element.42), channel_id=1, source_target_pairs={{0,4},{4,0},{8,12},{12,8},{1,5},{5,1},{9,13},{13,9},{2,6},{6,2},{1... | collective-permute-start | bytes 983048 | tf_op jit(solution)/shard_map/ppermute | solution.py:433
  92.6 1.5 collective-permute-start.20
  94.1 1.8 %collective-permute-start.21 = (bf16[384,256]{1,0:T(8,128)(2,1)S(1)}, bf16[384,256]{1,0:T(8,128)(2,1)S(1)}, u32[]{:S(2)}, u32[]{:S(2)}) collective-permute-start(bf16[384,256]{1,0:T(8,128)(2,1)S(1)} %get-tuple-element.57), channel_id=1, source_target_pairs={{0,8},{4,12},{8,0},{12,4},{1,9},{5,13},{9,1},{13,5},{2,10},{6,14},... | collective-permute-start | bytes 589832 | tf_op jit(solution)/shard_map/ppermute | solution.py:433
  95.9 1.1 collective-permute-start.22
  97.0 8.1 %collective-permute-done.8.got_ref.refs_1_ = bf16[2,160,512]{2,1,0:T(8,128)(2,1)S(1)} collective-permute-done((bf16[2,160,512]{2,1,0:T(8,128)(2,1)S(1)}, bf16[2,160,512]{2,1,0:T(8,128)(2,1)S(1)}, u32[]{:S(2)}, u32[]{:S(2)}) %collective-permute-start.8) | collective-permute-done | bytes 327712 | tf_op jit(solution)/shard_map/ppermute | solution.py:433
  105.1 4.2 %collective-permute-done.20.refs_1_ = bf16[384,256]{1,0:T(8,128)(2,1)S(1)} collective-permute-done((bf16[384,256]{1,0:T(8,128)(2,1)S(1)}, bf16[384,256]{1,0:T(8,128)(2,1)S(1)}, u32[]{:S(2)}, u32[]{:S(2)}) %collective-permute-start.20) | collective-permute-done | bytes 196640 | tf_op jit(solution)/shard_map/ppermute | solution.py:433
  109.3 7.1 %collective-permute-done.22.refs_3_ = bf16[384,256]{1,0:T(8,128)(2,1)S(1)} collective-permute-done((bf16[384,256]{1,0:T(8,128)(2,1)S(1)}, bf16[384,256]{1,0:T(8,128)(2,1)S(1)}, u32[]{:S(2)}, u32[]{:S(2)}) %collective-permute-start.22) | collective-permute-done | bytes 196640 | tf_op jit(solution)/shard_map/ppermute | solution.py:433
  116.4 0.1 stack_columns.3.refs_0_
  116.4 3.7 %collective-permute-start.24 = (bf16[4,384,256]{2,1,0:T(8,128)(2,1)S(1)}, bf16[4,384,256]{2,1,0:T(8,128)(2,1)S(1)}, u32[]{:S(2)}, u32[]{:S(2)}) collective-permute-start(bf16[4,384,256]{2,1,0:T(8,128)(2,1)S(1)} %stack_columns.3.refs_0_), channel_id=1, source_target_pairs={{0,2},{1,3},{2,0},{3,1},{4,6},{5,7},{6,4},{7,5},{8,10},{9,11},{10,... | collective-permute-start | bytes 2359304 | tf_op jit(solution)/shard_map/ppermute | solution.py:433
  120.2 0.7 collective-permute-start.26
  120.9 1.3 collective-permute-start.27
  122.2 0.1 collective-permute-start.23
  122.3 15.7 %collective-permute-done.24.refs_2_ = bf16[4,384,256]{2,1,0:T(8,128)(2,1)S(1)} collective-permute-done((bf16[4,384,256]{2,1,0:T(8,128)(2,1)S(1)}, bf16[4,384,256]{2,1,0:T(8,128)(2,1)S(1)}, u32[]{:S(2)}, u32[]{:S(2)}) %collective-permute-start.24) | collective-permute-done | bytes 786464 | tf_op jit(solution)/shard_map/ppermute | solution.py:433
  138.0 0.1 halve.3
  138.1 0.1 collective-permute-start.9
  138.2 13.0 %collective-permute-done.27.refs_10_ = bf16[1024,512]{1,0:T(8,128)(2,1)S(1)} collective-permute-done((bf16[1024,512]{1,0:T(8,128)(2,1)S(1)}, bf16[1024,512]{1,0:T(8,128)(2,1)S(1)}, u32[]{:S(2)}, u32[]{:S(2)}) %collective-permute-start.27) | collective-permute-done | bytes 1048608 | tf_op jit(solution)/shard_map/ppermute | solution.py:465
  151.2 7.7 %in_grads.1 = (bf16[16,384,512]{2,1,0:T(8,128)(2,1)}, f32[8,128]{1,0:T(8,128)S(1)}) custom-call(s32[2]{0:T(128)S(1)} %pad_add_fusion.ids_ref, s32[4,16]{1,0:T(4,128)S(1)} %bitcast.16, bf16[4,384,256]{2,1,0:T(8,128)(2,1)S(1)} %stack_columns.3.refs_0_, bf16[4,384,256]{2,1,0:T(8,128)(2,1)S(1)} %collective-permute-done.23.refs_1_, ...), custom_call_target="tpu_custom_call" | custom-call | tf_op jit(solution)/shard_map/in_grads/pallas_call | solution.py:580
  158.9 0.8 token_grads.1
  (42 shorter events, 0.1 us)
Async XLA Ops:
  0.6 10.7 %copy-start = (bf16[8,128,1536]{2,1,0:T(8,128)(2,1)S(1)}, bf16[8,128,1536]{2,1,0:T(8,128)(2,1)}, u32[]{:S(2)}) copy-start(bf16[8,128,1536]{2,1,0:T(8,128)(2,1)} %param.17) | copy-start | bytes 9437188
  3.5 7.8 %collective-permute-start = (bf16[144,512]{1,0:T(8,128)(2,1)}, bf16[144,512]{1,0:T(8,128)(2,1)S(1)}, u32[]{:S(2)}, u32[]{:S(2)}) collective-permute-start(bf16[144,512]{1,0:T(8,128)(2,1)} %route.1.refs_1_.refs_0_), channel_id=1, source_target_pairs={{0,4},{4,0},{8,12},{12,8},{1,5},{5,1},{9,13},{13,9},{2,6},{6,2},{1... | collective-permute-start | bytes 442376 | tf_op jit(solution)/shard_map/ppermute | solution.py:433
  6.5 11.9 %collective-permute-start.2 = (bf16[144,512]{1,0:T(8,128)(2,1)}, bf16[144,512]{1,0:T(8,128)(2,1)S(1)}, u32[]{:S(2)}, u32[]{:S(2)}) collective-permute-start(bf16[144,512]{1,0:T(8,128)(2,1)} %route.1.refs_1_.refs_0_), channel_id=1, source_target_pairs={{0,12},{4,8},{8,4},{12,0},{1,13},{5,9},{9,5},{13,1},{2,14},{6,10},... | collective-permute-start | bytes 442376 | tf_op jit(solution)/shard_map/ppermute | solution.py:433
  9.0 18.8 %collective-permute-start.1 = (bf16[144,512]{1,0:T(8,128)(2,1)}, bf16[144,512]{1,0:T(8,128)(2,1)}, u32[]{:S(2)}, u32[]{:S(2)}) collective-permute-start(bf16[144,512]{1,0:T(8,128)(2,1)} %route.1.refs_1_.refs_0_), channel_id=1, source_target_pairs={{0,8},{4,12},{8,0},{12,4},{1,9},{5,13},{9,1},{13,5},{2,10},{6,14},... | collective-permute-start | bytes 442376 | tf_op jit(solution)/shard_map/ppermute | solution.py:433
  10.4 0.9 copy-start.2
  11.3 16.5 %copy-start.3 = (bf16[144,512]{1,0:T(8,128)(2,1)S(1)}, bf16[144,512]{1,0:T(8,128)(2,1)}, u32[]{:S(2)}) copy-start(bf16[144,512]{1,0:T(8,128)(2,1)} %route.1.refs_1_.refs_0_) | copy-start | bytes 442372
  12.4 41.6 %copy-start.4 = (s32[16,4]{0,1:T(4,128)S(1)}, s32[16,4]{0,1:T(4,128)}, u32[]{:S(2)}) copy-start(s32[16,4]{0,1:T(4,128)} %param.14) | copy-start | bytes 772
  12.4 21.9 %collective-permute-start.10 = (bf16[192,256]{1,0:T(8,128)(2,1)S(1)}, bf16[192,256]{1,0:T(8,128)(2,1)S(1)}, u32[]{:S(2)}, u32[]{:S(2)}) collective-permute-start(bf16[192,256]{1,0:T(8,128)(2,1)S(1)} %get-tuple-element.49), channel_id=1, source_target_pairs={{0,4},{4,0},{8,12},{12,8},{1,5},{5,1},{9,13},{13,9},{2,6},{6,2},{1... | collective-permute-start | bytes 294920 | tf_op jit(solution)/shard_map/ppermute | solution.py:433
  14.4 19.9 %collective-permute-start.11 = (bf16[192,256]{1,0:T(8,128)(2,1)S(1)}, bf16[192,256]{1,0:T(8,128)(2,1)S(1)}, u32[]{:S(2)}, u32[]{:S(2)}) collective-permute-start(bf16[192,256]{1,0:T(8,128)(2,1)S(1)} %get-tuple-element.50), channel_id=1, source_target_pairs={{0,8},{4,12},{8,0},{12,4},{1,9},{5,13},{9,1},{13,5},{2,10},{6,14},... | collective-permute-start | bytes 294920 | tf_op jit(solution)/shard_map/ppermute | solution.py:433
  18.4 15.9 %collective-permute-start.12 = (bf16[192,256]{1,0:T(8,128)(2,1)S(1)}, bf16[192,256]{1,0:T(8,128)(2,1)S(1)}, u32[]{:S(2)}, u32[]{:S(2)}) collective-permute-start(bf16[192,256]{1,0:T(8,128)(2,1)S(1)} %get-tuple-element.51), channel_id=1, source_target_pairs={{0,12},{4,8},{8,4},{12,0},{1,13},{5,9},{9,5},{13,1},{2,14},{6,10},... | collective-permute-start | bytes 294920 | tf_op jit(solution)/shard_map/ppermute | solution.py:433
  34.2 17.8 %collective-permute-start.3 = (bf16[2,256,768]{2,1,0:T(8,128)(2,1)S(1)}, bf16[2,256,768]{2,1,0:T(8,128)(2,1)S(1)}, u32[]{:S(2)}, u32[]{:S(2)}) collective-permute-start(bf16[2,256,768]{2,1,0:T(8,128)(2,1)S(1)} %get-tuple-element.36), channel_id=1, source_target_pairs={{0,1},{1,0},{2,3},{3,2},{4,5},{5,4},{6,7},{7,6},{8,9},{9,8},{10,11... | collective-permute-start | bytes 2359304 | tf_op jit(solution)/shard_map/ppermute | solution.py:433
  34.3 27.5 %collective-permute-start.14 = (bf16[1024,512]{1,0:T(8,128)(2,1)S(1)}, bf16[1024,512]{1,0:T(8,128)(2,1)S(1)}, u32[]{:S(2)}, u32[]{:S(2)}) collective-permute-start(bf16[1024,512]{1,0:T(8,128)(2,1)S(1)} %gate.8), channel_id=1, source_target_pairs={{12,8},{8,4},{4,0},{13,9},{9,5},{5,1},{14,10},{10,6},{6,2},{15,11}... | collective-permute-start | bytes 3145736 | tf_op jit(solution)/shard_map/ppermute | solution.py:465
  35.6 27.3 %collective-permute-start.13 = (bf16[1024,512]{1,0:T(8,128)(2,1)S(1)}, bf16[1024,512]{1,0:T(8,128)(2,1)S(1)}, u32[]{:S(2)}, u32[]{:S(2)}) collective-permute-start(bf16[1024,512]{1,0:T(8,128)(2,1)S(1)} %gate.8), channel_id=1, source_target_pairs={{0,4},{4,8},{8,12},{1,5},{5,9},{9,13},{2,6},{6,10},{10,14},{3,7},{... | collective-permute-start | bytes 3145736 | tf_op jit(solution)/shard_map/ppermute | solution.py:464
  40.3 11.7 %collective-permute-start.16 = (bf16[4,192,256]{2,1,0:T(8,128)(2,1)S(1)}, bf16[4,192,256]{2,1,0:T(8,128)(2,1)S(1)}, u32[]{:S(2)}, u32[]{:S(2)}) collective-permute-start(bf16[4,192,256]{2,1,0:T(8,128)(2,1)S(1)} %stack_columns.2.refs_0_), channel_id=1, source_target_pairs={{0,2},{1,3},{2,0},{3,1},{4,6},{5,7},{6,4},{7,5},{8,10},{9,11},{10,... | collective-permute-start | bytes 1179656 | tf_op jit(solution)/shard_map/ppermute | solution.py:433
  42.8 11.2 %collective-permute-start.15 = (bf16[4,192,256]{2,1,0:T(8,128)(2,1)S(1)}, bf16[4,192,256]{2,1,0:T(8,128)(2,1)S(1)}, u32[]{:S(2)}, u32[]{:S(2)}) collective-permute-start(bf16[4,192,256]{2,1,0:T(8,128)(2,1)S(1)} %stack_columns.2.refs_0_), channel_id=1, source_target_pairs={{0,1},{1,0},{2,3},{3,2},{4,5},{5,4},{6,7},{7,6},{8,9},{9,8},{10,11... | collective-permute-start | bytes 1179656 | tf_op jit(solution)/shard_map/ppermute | solution.py:433
  52.0 2.0 %collective-permute-start.17 = (bf16[4,192,256]{2,1,0:T(8,128)(2,1)S(1)}, bf16[4,192,256]{2,1,0:T(8,128)(2,1)S(1)}, u32[]{:S(2)}, u32[]{:S(2)}) collective-permute-start(bf16[4,192,256]{2,1,0:T(8,128)(2,1)S(1)} %collective-permute-done.16.refs_2_), channel_id=1, source_target_pairs={{0,1},{1,0},{2,3},{3,2},{4,5},{5,4},{6,7},{7,6},{8,9},{9,8},{10,11... | collective-permute-start | bytes 1179656 | tf_op jit(solution)/shard_map/ppermute | solution.py:433
  52.2 12.8 %collective-permute-start.4 = (bf16[1,256,768]{2,1,0:T(8,128)(2,1)S(1)}, bf16[1,256,768]{2,1,0:T(8,128)(2,1)S(1)}, u32[]{:S(2)}, u32[]{:S(2)}) collective-permute-start(bf16[1,256,768]{2,1,0:T(8,128)(2,1)S(1)} %get-tuple-element.38), channel_id=1, source_target_pairs={{0,2},{1,3},{2,0},{3,1},{4,6},{5,7},{6,4},{7,5},{8,10},{9,11},{10,... | collective-permute-start | bytes 1179656 | tf_op jit(solution)/shard_map/ppermute | solution.py:433
  63.0 29.6 %collective-permute-start.18 = (bf16[1024,512]{1,0:T(8,128)(2,1)S(1)}, bf16[1024,512]{1,0:T(8,128)(2,1)S(1)}, u32[]{:S(2)}, u32[]{:S(2)}) collective-permute-start(bf16[1024,512]{1,0:T(8,128)(2,1)S(1)} %get-tuple-element.54.refs_5_), channel_id=1, source_target_pairs={{4,8},{8,12},{5,9},{9,13},{6,10},{10,14},{7,11},{11,15},{20,24},{2... | collective-permute-start | bytes 3145736 | tf_op jit(solution)/shard_map/ppermute | solution.py:464
  63.7 28.9 %collective-permute-start.19 = (bf16[1024,512]{1,0:T(8,128)(2,1)S(1)}, bf16[1024,512]{1,0:T(8,128)(2,1)S(1)}, u32[]{:S(2)}, u32[]{:S(2)}) collective-permute-start(bf16[1024,512]{1,0:T(8,128)(2,1)S(1)} %get-tuple-element.55.refs_8_), channel_id=1, source_target_pairs={{8,4},{4,0},{9,5},{5,1},{10,6},{6,2},{11,7},{7,3},{24,20},{20,16},... | collective-permute-start | bytes 3145736 | tf_op jit(solution)/shard_map/ppermute | solution.py:465
  66.6 11.1 %collective-permute-start.6 = (bf16[256,768]{1,0:T(8,128)(2,1)S(1)}, bf16[256,768]{1,0:T(8,128)(2,1)S(1)}, u32[]{:S(2)}, u32[]{:S(2)}) collective-permute-start(bf16[256,768]{1,0:T(8,128)(2,1)S(1)} %get-tuple-element.40.refs_0_), channel_id=1, source_target_pairs={{0,2},{1,3},{2,0},{3,1},{4,6},{5,7},{6,4},{7,5},{8,10},{9,11},{10,... | collective-permute-start | bytes 1179656 | tf_op jit(solution)/shard_map/ppermute | solution.py:433
  69.1 8.7 %collective-permute-start.5 = (bf16[256,768]{1,0:T(8,128)(2,1)S(1)}, bf16[256,768]{1,0:T(8,128)(2,1)S(1)}, u32[]{:S(2)}, u32[]{:S(2)}) collective-permute-start(bf16[256,768]{1,0:T(8,128)(2,1)S(1)} %get-tuple-element.40.refs_0_), channel_id=1, source_target_pairs={{0,1},{1,0},{2,3},{3,2},{4,5},{5,4},{6,7},{7,6},{8,9},{9,8},{10,11... | collective-permute-start | bytes 1179656 | tf_op jit(solution)/shard_map/ppermute | solution.py:433
  77.8 1.7 %collective-permute-start.7 = (bf16[256,768]{1,0:T(8,128)(2,1)S(1)}, bf16[256,768]{1,0:T(8,128)(2,1)S(1)}, u32[]{:S(2)}, u32[]{:S(2)}) collective-permute-start(bf16[256,768]{1,0:T(8,128)(2,1)S(1)} %collective-permute-done.6.refs_2_), channel_id=1, source_target_pairs={{0,1},{1,0},{2,3},{3,2},{4,5},{5,4},{6,7},{7,6},{8,9},{9,8},{10,11... | collective-permute-start | bytes 1179656 | tf_op jit(solution)/shard_map/ppermute | solution.py:433
  87.8 63.4 %copy-start.1 = (bf16[8,4,32,512]{3,2,1,0:T(8,128)(2,1)S(1)}, bf16[8,4,32,512]{3,2,1,0:T(8,128)(2,1)}, u32[]{:S(2)}) copy-start(bf16[8,4,32,512]{3,2,1,0:T(8,128)(2,1)} %param.16) | copy-start | bytes 3145732
  87.8 17.2 %collective-permute-start.8 = (bf16[2,160,512]{2,1,0:T(8,128)(2,1)S(1)}, bf16[2,160,512]{2,1,0:T(8,128)(2,1)S(1)}, u32[]{:S(2)}, u32[]{:S(2)}) collective-permute-start(bf16[2,160,512]{2,1,0:T(8,128)(2,1)S(1)} %get-tuple-element.42), channel_id=1, source_target_pairs={{0,4},{4,0},{8,12},{12,8},{1,5},{5,1},{9,13},{13,9},{2,6},{6,2},{1... | collective-permute-start | bytes 983048 | tf_op jit(solution)/shard_map/ppermute | solution.py:433
  92.6 16.7 %collective-permute-start.20 = (bf16[384,256]{1,0:T(8,128)(2,1)S(1)}, bf16[384,256]{1,0:T(8,128)(2,1)S(1)}, u32[]{:S(2)}, u32[]{:S(2)}) collective-permute-start(bf16[384,256]{1,0:T(8,128)(2,1)S(1)} %get-tuple-element.56), channel_id=1, source_target_pairs={{0,4},{4,0},{8,12},{12,8},{1,5},{5,1},{9,13},{13,9},{2,6},{6,2},{1... | collective-permute-start | bytes 589832 | tf_op jit(solution)/shard_map/ppermute | solution.py:433
  94.1 15.2 %collective-permute-start.21 = (bf16[384,256]{1,0:T(8,128)(2,1)S(1)}, bf16[384,256]{1,0:T(8,128)(2,1)S(1)}, u32[]{:S(2)}, u32[]{:S(2)}) collective-permute-start(bf16[384,256]{1,0:T(8,128)(2,1)S(1)} %get-tuple-element.57), channel_id=1, source_target_pairs={{0,8},{4,12},{8,0},{12,4},{1,9},{5,13},{9,1},{13,5},{2,10},{6,14},... | collective-permute-start | bytes 589832 | tf_op jit(solution)/shard_map/ppermute | solution.py:433
  95.9 20.5 %collective-permute-start.22 = (bf16[384,256]{1,0:T(8,128)(2,1)S(1)}, bf16[384,256]{1,0:T(8,128)(2,1)S(1)}, u32[]{:S(2)}, u32[]{:S(2)}) collective-permute-start(bf16[384,256]{1,0:T(8,128)(2,1)S(1)} %get-tuple-element.58), channel_id=1, source_target_pairs={{0,12},{4,8},{8,4},{12,0},{1,13},{5,9},{9,5},{13,1},{2,14},{6,10},... | collective-permute-start | bytes 589832 | tf_op jit(solution)/shard_map/ppermute | solution.py:433
  105.1 53.8 %copy-start.5 = (s32[128,8]{0,1:T(8,128)S(1)}, s32[128,8]{0,1:T(8,128)}, u32[]{:S(2)}) copy-start(s32[128,8]{0,1:T(8,128)} %param.12) | copy-start | bytes 12292
  105.1 53.8 %copy-start.6 = (s32[128,8]{0,1:T(8,128)S(1)}, s32[128,8]{0,1:T(8,128)}, u32[]{:S(2)}) copy-start(s32[128,8]{0,1:T(8,128)} %param.13) | copy-start | bytes 12292
  116.4 21.6 %collective-permute-start.24 = (bf16[4,384,256]{2,1,0:T(8,128)(2,1)S(1)}, bf16[4,384,256]{2,1,0:T(8,128)(2,1)S(1)}, u32[]{:S(2)}, u32[]{:S(2)}) collective-permute-start(bf16[4,384,256]{2,1,0:T(8,128)(2,1)S(1)} %stack_columns.3.refs_0_), channel_id=1, source_target_pairs={{0,2},{1,3},{2,0},{3,1},{4,6},{5,7},{6,4},{7,5},{8,10},{9,11},{10,... | collective-permute-start | bytes 2359304 | tf_op jit(solution)/shard_map/ppermute | solution.py:433
  120.2 18.0 %collective-permute-start.26 = (bf16[1024,512]{1,0:T(8,128)(2,1)S(1)}, bf16[1024,512]{1,0:T(8,128)(2,1)S(1)}, u32[]{:S(2)}, u32[]{:S(2)}) collective-permute-start(bf16[1024,512]{1,0:T(8,128)(2,1)S(1)} %collective-permute-done.18.refs_3_.refs_6_), channel_id=1, source_target_pairs={{8,12},{9,13},{10,14},{11,15},{24,28},{25,29},{26,30},{27,31}} | collective-permute-start | bytes 3145736 | tf_op jit(solution)/shard_map/ppermute | solution.py:464
  120.9 30.3 %collective-permute-start.27 = (bf16[1024,512]{1,0:T(8,128)(2,1)S(1)}, bf16[1024,512]{1,0:T(8,128)(2,1)S(1)}, u32[]{:S(2)}, u32[]{:S(2)}) collective-permute-start(bf16[1024,512]{1,0:T(8,128)(2,1)S(1)} %collective-permute-done.19.refs_4_.refs_9_), channel_id=1, source_target_pairs={{4,0},{5,1},{6,2},{7,3},{20,16},{21,17},{22,18},{23,19}} | collective-permute-start | bytes 3145736 | tf_op jit(solution)/shard_map/ppermute | solution.py:465
  122.2 16.0 %collective-permute-start.23 = (bf16[4,384,256]{2,1,0:T(8,128)(2,1)S(1)}, bf16[4,384,256]{2,1,0:T(8,128)(2,1)S(1)}, u32[]{:S(2)}, u32[]{:S(2)}) collective-permute-start(bf16[4,384,256]{2,1,0:T(8,128)(2,1)S(1)} %stack_columns.3.refs_0_), channel_id=1, source_target_pairs={{0,1},{1,0},{2,3},{3,2},{4,5},{5,4},{6,7},{7,6},{8,9},{9,8},{10,11... | collective-permute-start | bytes 2359304 | tf_op jit(solution)/shard_map/ppermute | solution.py:433
  138.0 13.2 %collective-permute-start.25 = (bf16[4,384,256]{2,1,0:T(8,128)(2,1)S(1)}, bf16[4,384,256]{2,1,0:T(8,128)(2,1)S(1)}, u32[]{:S(2)}, u32[]{:S(2)}) collective-permute-start(bf16[4,384,256]{2,1,0:T(8,128)(2,1)S(1)} %collective-permute-done.24.refs_2_), channel_id=1, source_target_pairs={{0,1},{1,0},{2,3},{3,2},{4,5},{5,4},{6,7},{7,6},{8,9},{9,8},{10,11... | collective-permute-start | bytes 2359304 | tf_op jit(solution)/shard_map/ppermute | solution.py:433
  138.1 20.8 %collective-permute-start.9 = (bf16[1,160,512]{2,1,0:T(8,128)(2,1)S(1)}, bf16[1,160,512]{2,1,0:T(8,128)(2,1)S(1)}, u32[]{:S(2)}, u32[]{:S(2)}) collective-permute-start(bf16[1,160,512]{2,1,0:T(8,128)(2,1)S(1)} %get-tuple-element.44), channel_id=1, source_target_pairs={{0,8},{4,12},{8,0},{12,4},{1,9},{5,13},{9,1},{13,5},{2,10},{6,14},... | collective-permute-start | bytes 491528 | tf_op jit(solution)/shard_map/ppermute | solution.py:433

commit v10 on v9

--- a/solution.py
+++ b/solution.py
@@ -215,7 +215,8 @@
         outs[k][...] = sides[me ^ k]
 
 
-def hidden_kernel(z, ids_ref, pair_ref, after_ref, other_ref, *refs):
+def hidden_kernel(z, ids_ref, pair_ref, *refs):
+    refs = refs[z.ep :]
     pair = pair_ref[...]
     gate_pre = pair[:, : z.hidden].astype(F32)
     up = pair[:, z.hidden :].astype(F32)
@@ -379,7 +380,7 @@
 
 def total_down_kernel(z, ids_ref, table_ref, *refs):
     sides = refs[: z.sub]
-    grads_ref, codes_ref, out_ref, token_ref, held, made, out_sems, scaled, sems = refs[z.sub :]
+    grads_ref, codes_ref, _, out_ref, token_ref, held, made, out_sems, scaled, sems = refs[z.sub :]
     token_ref[...] = jnp.zeros_like(token_ref)
 
     def moves(act):
@@ -507,19 +508,18 @@
             num_scalar_prefetch=1,
             grid=(z.part_blocks,),
             in_specs=[
-                pl.BlockSpec((z.block, z.pair), lambda i, r: (r[1] * z.part_blocks + i, 0)),
-                pl.BlockSpec(memory_space=pl.ANY),
-                pl.BlockSpec(memory_space=pl.ANY),
-            ],
+                pl.BlockSpec((z.block, z.pair), lambda i, r: (r[1] * z.part_blocks + i, 0))
+            ]
+            + [pl.BlockSpec(memory_space=pl.ANY)] * n,
             out_specs=[pl.BlockSpec((z.down_cols, z.block), lambda i, r: (0, i))] * n,
             scratch_shapes=[pltpu.VMEM((n, z.down_cols, z.block), BF)],
         ),
         out_shape=[jax.ShapeDtypeStruct((z.down_cols, z.part), BF)] * n,
         compiler_params=params(16),
         name="hidden_columns",
-    )(ids, pair_rows, bufs[1], chain[0])
+    )(ids, pair_rows, *bufs[1:], chain[0])
+    chain = gate(chain, [*bufs[1:], downs[0]])
     downs = [downs[0]] + [swap(downs[k], "ep", n, k) for k in range(1, n)]
-    chain = gate(chain, bufs[1:] + downs[1:])
     steps = [chain_step(chain[0], chain[0], "ep", n, 1)]
 
     def stack(pieces):
@@ -573,8 +573,14 @@
         ],
         compiler_params=params(48),
         name="hidden_partials",
-    )(ids, *bufs, weight_down, *downs[:1])
+    )(ids, *bufs, weight_down, chain[0])
     keep, send, grads_all, codes = outs
+    got = swap(send, "sub", m, 1)
+    bit = 2
+    while bit < m:
+        keep, send = halve(keep, got)
+        got = swap(send, "sub", m, bit)
+        bit *= 2
     down_sides = spread_over({0: stack(downs)}, "sub", m, m // 2)
     def total_call(kernel, operands, specs, cols, scratch, name):
         return pl.pallas_call(
@@ -602,20 +608,14 @@
     anywhere = pl.BlockSpec(memory_space=pl.ANY)
     grad_down, down_made = total_call(
         total_down_kernel,
-        [*down_sides, grads_all, codes],
-        [anywhere] * m + [whole((n, z.tokens, z.width)), whole(code_shape)],
+        [*down_sides, grads_all, codes, send],
+        [anywhere] * m + [whole((n, z.tokens, z.width)), whole(code_shape), anywhere],
         z.down_cols,
         [pltpu.VMEM((z.slots, z.rows, z.width), BF), pltpu.SemaphoreType.DMA((m,))],
         "down_grads",
     )
     steps[0] = gate(steps[0], [down_made])
     steps.append(chain_step(*steps[0], "ep", n, 2))
-    got = swap(send, "sub", m, 1)
-    bit = 2
-    while bit < m:
-        keep, send = halve(keep, got)
-        got = swap(send, "sub", m, bit)
-        bit *= 2
     *pieces, grad_part = pl.pallas_call(
         functools.partial(pre_kernel, z),
         grid_spec=pltpu.PrefetchScalarGridSpec(
@@ -664,12 +664,14 @@
         compiler_params=params(46),
         name="row_grads",
     )(ids, *grad_parts, pair_rows, weight_in, codes)
+    steps[1] = gate(steps[1], pieces[1:])
     for d in range(3, n):
         steps.append(chain_step(*steps[-1], "ep", n, d))
     gathered = [inputs] + [go for go, _ in steps] + [back for _, back in steps]
     got = swap(send, "ep", n, 1)
     pieces[:1] = gate(pieces[:1], [got])
-    sides = spread_over({0: stack(pieces)}, "sub", m, m // 2)
+    columns = stack(pieces)
+    sides = spread_over({0: columns}, "sub", m, m // 2)
     bit = 2
     while bit < n:
         keep, send = halve(keep, got)

time: 160 us -> 184 us (1.15)
  waiting for transfers between devices: 78.3 us -> 106 us
  starting transfers between devices: 41.4 us -> 37.4 us
    ppermute x22, waiting for transfers between devices: 64.1 us -> 92.3 us  [swap(): return lax.ppermute(x, axis, [(i, i ^ bit) for i in range(size)])]
    ppermute x22, starting transfers between devices: 31.5 us -> 27.3 us  [swap(): return lax.ppermute(x, axis, [(i, i ^ bit) for i in range(size)])]
  transfers between devices with their start and end apart: 28 -> 28, of which waited for: 10 -> 13; matrix products, arithmetic and copies ran while one was open for 1% -> 1% of each run, Pallas kernels for 21% -> 14%
where the time goes in v10:
time: 184 us; the launch traced here: 183 us
  waiting for transfers between devices  106 us (58%)
  starting transfers between devices  37.4 us (20%)
  Pallas kernels  36.1 us (20%)
  local copies, waits for them, and re-layouts  2.16 us (1%)
    ppermute x22, waiting for transfers between devices, swap(): return lax.ppermute(x, axis, [(i, i ^ bit) for i in range(size)])  92.3 us
    ppermute x22, starting transfers between devices, swap(): return lax.ppermute(x, axis, [(i, i ^ bit) for i in range(size)])  27.3 us
    pallas_call x2, Pallas kernels, total_call(): pl.pallas_call(functools.partial(kernel, z), grid_spec=pltpu.PrefetchScal...  15.5 us
    ppermute x3, waiting for transfers between devices, chain_step(): lax.ppermute(back, axis, [(i, i - 1) for i in range(size - d, 0, -1)])  13.6 us
    pallas_call x1, Pallas kernels, body(): pl.pallas_call(functools.partial(row_kernel, z), grid_spec=pltpu.Prefetch...  8.32 us
    pallas_call x1, Pallas kernels, body(): pl.pallas_call(functools.partial(down_kernel, z), grid_spec=pltpu.Prefetc...  6.4 us
    ppermute x3, starting transfers between devices, chain_step(): go = lax.ppermute(go, axis, [(i, i + 1) for i in range(d - 1, size - 1)])  6.19 us
    ppermute x3, starting transfers between devices, chain_step(): lax.ppermute(back, axis, [(i, i - 1) for i in range(size - d, 0, -1)])  3.88 us
  transfers between devices with their start and end apart: 28, of which 13 were waited for; matrix products, arithmetic and copies ran while one was open for 1% of the time, Pallas kernels for 14%

profile of v10, /device:TPU:0, one launch (start us, length us, event | category | flops | bytes accessed | tf_op | source)
XLA Modules:
  0.0 183.3 jit_solution(10670547912834263525)
XLA Ops:
  1.4 2.0 %route.1.refs_1_.refs_0_ = bf16[144,512]{1,0:T(8,128)(2,1)} custom-call(s32[1]{0:T(128)S(6)} %copy.36.count_ref, bf16[128,512]{1,0:T(8,128)(2,1)} %grad_ref.1, bf16[8,128]{1,0:T(8,128)(2,1)} %bitcast.22, s32[8,128]{1,0:T(8,128)} %bitcast.18, s32[8,128]{1,0:T(8,128)} %bitcast.20, s32[4,16]{1,0:T(4,128)} %bitcast.14), custom_call_target="tpu_custom_call" | custom-call | tf_op jit(solution)/shard_map/route/pallas_call | solution.py:493
  3.5 5.0 %collective-permute-start.2 = (bf16[144,512]{1,0:T(8,128)(2,1)}, bf16[144,512]{1,0:T(8,128)(2,1)S(1)}, u32[]{:S(2)}, u32[]{:S(2)}) collective-permute-start(bf16[144,512]{1,0:T(8,128)(2,1)} %route.1.refs_1_.refs_0_), channel_id=1, source_target_pairs={{0,12},{4,8},{8,4},{12,0},{1,13},{5,9},{9,5},{13,1},{2,14},{6,10},... | collective-permute-start | bytes 442376 | tf_op jit(solution)/shard_map/ppermute | solution.py:434
  8.5 0.6 collective-permute-start
  9.1 1.2 copy.25.refs_0_
  10.3 0.9 copy-done.2
  11.2 0.1 pad_add_fusion.ids_ref
  11.3 2.2 %collective-permute-done.2.refs_2_.refs_3_ = bf16[144,512]{1,0:T(8,128)(2,1)S(1)} collective-permute-done((bf16[144,512]{1,0:T(8,128)(2,1)}, bf16[144,512]{1,0:T(8,128)(2,1)S(1)}, u32[]{:S(2)}, u32[]{:S(2)}) %collective-permute-start.2) | collective-permute-done | bytes 147488 | tf_op jit(solution)/shard_map/ppermute | solution.py:434
  13.5 7.7 %collective-permute-done.1.refs_1_.refs_2_ = bf16[144,512]{1,0:T(8,128)(2,1)S(1)} collective-permute-done((bf16[144,512]{1,0:T(8,128)(2,1)}, bf16[144,512]{1,0:T(8,128)(2,1)S(1)}, u32[]{:S(2)}, u32[]{:S(2)}) %collective-permute-start.1) | collective-permute-done | bytes 147488 | tf_op jit(solution)/shard_map/ppermute | solution.py:434
  21.2 1.1 hidden_columns.1
  22.3 6.4 %hidden_partials.1 = (bf16[2,256,768]{2,1,0:T(8,128)(2,1)S(1)}, bf16[2,256,768]{2,1,0:T(8,128)(2,1)S(1)}, bf16[4,128,512]{2,1,0:T(8,128)(2,1)S(1)}, f32[4,64,128]{2,1,0:T(8,128)S(1)}) custom-call(s32[2]{0:T(128)S(1)} %pad_add_fusion.ids_ref, bf16[144,512]{1,0:T(8,128)(2,1)S(1)} %copy-done.3, bf16[144,512]{1,0:T(8,128)(2,1)} %collective-permute-done.refs_0_.refs_1_, ...), custom_call_target="tpu_custom_call" | custom-call | tf_op jit(solution)/shard_map/hidden_partials/pallas_call | solution.py:554
  28.7 0.1 collective-permute-start.3
  28.8 1.3 collective-permute-start.11
  30.1 4.6 %collective-permute-start.10 = (bf16[1024,512]{1,0:T(8,128)(2,1)S(1)}, bf16[1024,512]{1,0:T(8,128)(2,1)S(1)}, u32[]{:S(2)}, u32[]{:S(2)}) collective-permute-start(bf16[1024,512]{1,0:T(8,128)(2,1)S(1)} %gate.8.refs_5_), channel_id=1, source_target_pairs={{0,4},{4,8},{8,12},{1,5},{5,9},{9,13},{2,6},{6,10},{10,14},{3,7},{... | collective-permute-start | bytes 3145736 | tf_op jit(solution)/shard_map/ppermute | solution.py:465
  34.7 0.1 collective-permute-start.12
  34.8 0.5 collective-permute-start.13
  35.3 25.1 %collective-permute-done.12.refs_1_ = bf16[192,256]{1,0:T(8,128)(2,1)S(1)} collective-permute-done((bf16[192,256]{1,0:T(8,128)(2,1)S(1)}, bf16[192,256]{1,0:T(8,128)(2,1)S(1)}, u32[]{:S(2)}, u32[]{:S(2)}) %collective-permute-start.12) | collective-permute-done | bytes 98336 | tf_op jit(solution)/shard_map/ppermute | solution.py:434
  60.5 3.9 %collective-permute-start.14 = (bf16[192,256]{1,0:T(8,128)(2,1)S(1)}, bf16[192,256]{1,0:T(8,128)(2,1)S(1)}, u32[]{:S(2)}, u32[]{:S(2)}) collective-permute-start(bf16[192,256]{1,0:T(8,128)(2,1)S(1)} %get-tuple-element.53), channel_id=1, source_target_pairs={{0,12},{4,8},{8,4},{12,0},{1,13},{5,9},{9,5},{13,1},{2,14},{6,10},... | collective-permute-start | bytes 294920 | tf_op jit(solution)/shard_map/ppermute | solution.py:434
  64.4 2.8 %collective-permute-done.14.refs_3_ = bf16[192,256]{1,0:T(8,128)(2,1)S(1)} collective-permute-done((bf16[192,256]{1,0:T(8,128)(2,1)S(1)}, bf16[192,256]{1,0:T(8,128)(2,1)S(1)}, u32[]{:S(2)}, u32[]{:S(2)}) %collective-permute-start.14) | collective-permute-done | bytes 98336 | tf_op jit(solution)/shard_map/ppermute | solution.py:434
  67.2 2.5 %collective-permute-start.16 = (bf16[4,192,256]{2,1,0:T(8,128)(2,1)S(1)}, bf16[4,192,256]{2,1,0:T(8,128)(2,1)S(1)}, u32[]{:S(2)}, u32[]{:S(2)}) collective-permute-start(bf16[4,192,256]{2,1,0:T(8,128)(2,1)S(1)} %stack_columns.2.refs_0_), channel_id=1, source_target_pairs={{0,2},{1,3},{2,0},{3,1},{4,6},{5,7},{6,4},{7,5},{8,10},{9,11},{10,... | collective-permute-start | bytes 1179656 | tf_op jit(solution)/shard_map/ppermute | solution.py:434
  69.7 8.3 %collective-permute-done.16.refs_2_ = bf16[4,192,256]{2,1,0:T(8,128)(2,1)S(1)} collective-permute-done((bf16[4,192,256]{2,1,0:T(8,128)(2,1)S(1)}, bf16[4,192,256]{2,1,0:T(8,128)(2,1)S(1)}, u32[]{:S(2)}, u32[]{:S(2)}) %collective-permute-start.16) | collective-permute-done | bytes 393248 | tf_op jit(solution)/shard_map/ppermute | solution.py:434
  78.0 0.2 halve.2
  78.2 1.8 collective-permute-start.4
  80.0 7.8 %down_grads.1 = (bf16[16,192,512]{2,1,0:T(8,128)(2,1)}, f32[8,128]{1,0:T(8,128)S(1)}) custom-call(s32[2]{0:T(128)S(1)} %pad_add_fusion.ids_ref, s32[4,16]{1,0:T(4,128)S(1)} %bitcast.15, bf16[4,192,256]{2,1,0:T(8,128)(2,1)S(1)} %stack_columns.2.refs_0_, bf16[4,192,256]{2,1,0:T(8,128)(2,1)S(1)} %collective-permute-done.15.refs_1_, ...), custom_call_target="tpu_custom_call" | custom-call | tf_op jit(solution)/shard_map/down_grads/pallas_call | solution.py:586
  87.8 0.7 collective-permute-start.18
  88.6 1.3 collective-permute-start.19
  89.9 1.6 pre_grads.1
  91.5 1.7 collective-permute-start.6
  93.2 9.6 %collective-permute-done.6.refs_2_ = bf16[256,768]{1,0:T(8,128)(2,1)S(1)} collective-permute-done((bf16[256,768]{1,0:T(8,128)(2,1)S(1)}, bf16[256,768]{1,0:T(8,128)(2,1)S(1)}, u32[]{:S(2)}, u32[]{:S(2)}) %collective-permute-start.6) | collective-permute-done | bytes 393248 | tf_op jit(solution)/shard_map/ppermute | solution.py:434
  102.8 1.7 collective-permute-done.7.refs_3_
  104.5 8.3 %row_grads.1 = (bf16[2,160,512]{2,1,0:T(8,128)(2,1)S(1)}, bf16[2,160,512]{2,1,0:T(8,128)(2,1)S(1)}) custom-call(s32[2]{0:T(128)S(1)} %pad_add_fusion.ids_ref, bf16[256,768]{1,0:T(8,128)(2,1)S(1)} %get-tuple-element.42.refs_0_, bf16[256,768]{1,0:T(8,128)(2,1)S(1)} %collective-permute-done.5.refs_1_, bf16[256,768]{1,0:T(8,128)(2,1)S(1)} %collective-permute-done.6.refs_2_, ...), custom_call_target="tpu_custom_call" | custom-call | tf_op jit(solution)/shard_map/row_grads/pallas_call | solution.py:643
  112.9 2.4 %collective-permute-start.8 = (bf16[2,160,512]{2,1,0:T(8,128)(2,1)S(1)}, bf16[2,160,512]{2,1,0:T(8,128)(2,1)S(1)}, u32[]{:S(2)}, u32[]{:S(2)}) collective-permute-start(bf16[2,160,512]{2,1,0:T(8,128)(2,1)S(1)} %get-tuple-element.44), channel_id=1, source_target_pairs={{0,4},{4,0},{8,12},{12,8},{1,5},{5,1},{9,13},{13,9},{2,6},{6,2},{1... | collective-permute-start | bytes 983048 | tf_op jit(solution)/shard_map/ppermute | solution.py:434
  115.3 0.4 collective-permute-done.19.refs_4_.refs_1_
  115.7 2.8 %collective-permute-start.20 = (bf16[384,256]{1,0:T(8,128)(2,1)S(1)}, bf16[384,256]{1,0:T(8,128)(2,1)S(1)}, u32[]{:S(2)}, u32[]{:S(2)}) collective-permute-start(bf16[384,256]{1,0:T(8,128)(2,1)S(1)} %get-tuple-element.58), channel_id=1, source_target_pairs={{0,4},{4,0},{8,12},{12,8},{1,5},{5,1},{9,13},{13,9},{2,6},{6,2},{1... | collective-permute-start | bytes 589832 | tf_op jit(solution)/shard_map/ppermute | solution.py:434
  118.6 1.1 collective-permute-start.21
  119.7 1.3 collective-permute-start.22
  120.9 6.8 %collective-permute-done.8.got_ref.refs_1_ = bf16[2,160,512]{2,1,0:T(8,128)(2,1)S(1)} collective-permute-done((bf16[2,160,512]{2,1,0:T(8,128)(2,1)S(1)}, bf16[2,160,512]{2,1,0:T(8,128)(2,1)S(1)}, u32[]{:S(2)}, u32[]{:S(2)}) %collective-permute-start.8) | collective-permute-done | bytes 327712 | tf_op jit(solution)/shard_map/ppermute | solution.py:434
  127.8 4.2 %collective-permute-done.20.refs_1_.refs_2_ = bf16[384,256]{1,0:T(8,128)(2,1)S(1)} collective-permute-done((bf16[384,256]{1,0:T(8,128)(2,1)S(1)}, bf16[384,256]{1,0:T(8,128)(2,1)S(1)}, u32[]{:S(2)}, u32[]{:S(2)}) %collective-permute-start.20) | collective-permute-done | bytes 196640 | tf_op jit(solution)/shard_map/ppermute | solution.py:434
  132.0 8.2 %collective-permute-done.22.refs_3_.refs_4_ = bf16[384,256]{1,0:T(8,128)(2,1)S(1)} collective-permute-done((bf16[384,256]{1,0:T(8,128)(2,1)S(1)}, bf16[384,256]{1,0:T(8,128)(2,1)S(1)}, u32[]{:S(2)}, u32[]{:S(2)}) %collective-permute-start.22) | collective-permute-done | bytes 196640 | tf_op jit(solution)/shard_map/ppermute | solution.py:434
  140.3 3.4 %collective-permute-start.24 = (bf16[4,384,256]{2,1,0:T(8,128)(2,1)S(1)}, bf16[4,384,256]{2,1,0:T(8,128)(2,1)S(1)}, u32[]{:S(2)}, u32[]{:S(2)}) collective-permute-start(bf16[4,384,256]{2,1,0:T(8,128)(2,1)S(1)} %stack_columns.3.refs_0_), channel_id=1, source_target_pairs={{0,2},{1,3},{2,0},{3,1},{4,6},{5,7},{6,4},{7,5},{8,10},{9,11},{10,... | collective-permute-start | bytes 2359304 | tf_op jit(solution)/shard_map/ppermute | solution.py:434
  143.6 0.8 collective-permute-start.26
  144.5 1.3 collective-permute-start.27
  145.8 0.1 collective-permute-start.23
  145.9 15.6 %collective-permute-done.24.refs_2_ = bf16[4,384,256]{2,1,0:T(8,128)(2,1)S(1)} collective-permute-done((bf16[4,384,256]{2,1,0:T(8,128)(2,1)S(1)}, bf16[4,384,256]{2,1,0:T(8,128)(2,1)S(1)}, u32[]{:S(2)}, u32[]{:S(2)}) %collective-permute-start.24) | collective-permute-done | bytes 786464 | tf_op jit(solution)/shard_map/ppermute | solution.py:434
  161.4 0.1 halve.3
  161.5 0.1 collective-permute-start.9
  161.6 13.2 %collective-permute-done.27.refs_10_ = bf16[1024,512]{1,0:T(8,128)(2,1)S(1)} collective-permute-done((bf16[1024,512]{1,0:T(8,128)(2,1)S(1)}, bf16[1024,512]{1,0:T(8,128)(2,1)S(1)}, u32[]{:S(2)}, u32[]{:S(2)}) %collective-permute-start.27) | collective-permute-done | bytes 1048608 | tf_op jit(solution)/shard_map/ppermute | solution.py:466
  174.8 7.7 %in_grads.1 = (bf16[16,384,512]{2,1,0:T(8,128)(2,1)}, f32[8,128]{1,0:T(8,128)S(1)}) custom-call(s32[2]{0:T(128)S(1)} %pad_add_fusion.ids_ref, s32[4,16]{1,0:T(4,128)S(1)} %bitcast.16, bf16[4,384,256]{2,1,0:T(8,128)(2,1)S(1)} %stack_columns.3.refs_0_, bf16[4,384,256]{2,1,0:T(8,128)(2,1)S(1)} %collective-permute-done.23.refs_1_, ...), custom_call_target="tpu_custom_call" | custom-call | tf_op jit(solution)/shard_map/in_grads/pallas_call | solution.py:586
  182.5 0.8 token_grads.1
  (43 shorter events, 0.2 us)
Async XLA Ops:
  0.6 20.6 %copy-start = (bf16[8,128,1536]{2,1,0:T(8,128)(2,1)S(1)}, bf16[8,128,1536]{2,1,0:T(8,128)(2,1)}, u32[]{:S(2)}) copy-start(bf16[8,128,1536]{2,1,0:T(8,128)(2,1)} %param.17) | copy-start | bytes 9437188
  3.5 10.0 %collective-permute-start.2 = (bf16[144,512]{1,0:T(8,128)(2,1)}, bf16[144,512]{1,0:T(8,128)(2,1)S(1)}, u32[]{:S(2)}, u32[]{:S(2)}) collective-permute-start(bf16[144,512]{1,0:T(8,128)(2,1)} %route.1.refs_1_.refs_0_), channel_id=1, source_target_pairs={{0,12},{4,8},{8,4},{12,0},{1,13},{5,9},{9,5},{13,1},{2,14},{6,10},... | collective-permute-start | bytes 442376 | tf_op jit(solution)/shard_map/ppermute | solution.py:434
  8.5 12.7 %collective-permute-start.1 = (bf16[144,512]{1,0:T(8,128)(2,1)}, bf16[144,512]{1,0:T(8,128)(2,1)S(1)}, u32[]{:S(2)}, u32[]{:S(2)}) collective-permute-start(bf16[144,512]{1,0:T(8,128)(2,1)} %route.1.refs_1_.refs_0_), channel_id=1, source_target_pairs={{0,8},{4,12},{8,0},{12,4},{1,9},{5,13},{9,1},{13,5},{2,10},{6,14},... | collective-permute-start | bytes 442376 | tf_op jit(solution)/shard_map/ppermute | solution.py:434
  8.5 12.7 %collective-permute-start = (bf16[144,512]{1,0:T(8,128)(2,1)}, bf16[144,512]{1,0:T(8,128)(2,1)}, u32[]{:S(2)}, u32[]{:S(2)}) collective-permute-start(bf16[144,512]{1,0:T(8,128)(2,1)} %route.1.refs_1_.refs_0_), channel_id=1, source_target_pairs={{0,4},{4,0},{8,12},{12,8},{1,5},{5,1},{9,13},{13,9},{2,6},{6,2},{1... | collective-permute-start | bytes 442376 | tf_op jit(solution)/shard_map/ppermute | solution.py:434
  10.3 0.9 copy-start.2
  11.2 11.1 %copy-start.3 = (bf16[144,512]{1,0:T(8,128)(2,1)S(1)}, bf16[144,512]{1,0:T(8,128)(2,1)}, u32[]{:S(2)}) copy-start(bf16[144,512]{1,0:T(8,128)(2,1)} %route.1.refs_1_.refs_0_) | copy-start | bytes 442372
  22.3 57.7 %copy-start.4 = (s32[16,4]{0,1:T(4,128)S(1)}, s32[16,4]{0,1:T(4,128)}, u32[]{:S(2)}) copy-start(s32[16,4]{0,1:T(4,128)} %param.14) | copy-start | bytes 772
  28.7 49.2 %collective-permute-start.3 = (bf16[2,256,768]{2,1,0:T(8,128)(2,1)S(1)}, bf16[2,256,768]{2,1,0:T(8,128)(2,1)S(1)}, u32[]{:S(2)}, u32[]{:S(2)}) collective-permute-start(bf16[2,256,768]{2,1,0:T(8,128)(2,1)S(1)} %get-tuple-element.38), channel_id=1, source_target_pairs={{0,1},{1,0},{2,3},{3,2},{4,5},{5,4},{6,7},{7,6},{8,9},{9,8},{10,11... | collective-permute-start | bytes 2359304 | tf_op jit(solution)/shard_map/ppermute | solution.py:434
  28.8 59.0 %collective-permute-start.11 = (bf16[1024,512]{1,0:T(8,128)(2,1)S(1)}, bf16[1024,512]{1,0:T(8,128)(2,1)S(1)}, u32[]{:S(2)}, u32[]{:S(2)}) collective-permute-start(bf16[1024,512]{1,0:T(8,128)(2,1)S(1)} %gate.8.refs_5_), channel_id=1, source_target_pairs={{12,8},{8,4},{4,0},{13,9},{9,5},{5,1},{14,10},{10,6},{6,2},{15,11}... | collective-permute-start | bytes 3145736 | tf_op jit(solution)/shard_map/ppermute | solution.py:466
  30.1 57.7 %collective-permute-start.10 = (bf16[1024,512]{1,0:T(8,128)(2,1)S(1)}, bf16[1024,512]{1,0:T(8,128)(2,1)S(1)}, u32[]{:S(2)}, u32[]{:S(2)}) collective-permute-start(bf16[1024,512]{1,0:T(8,128)(2,1)S(1)} %gate.8.refs_5_), channel_id=1, source_target_pairs={{0,4},{4,8},{8,12},{1,5},{5,9},{9,13},{2,6},{6,10},{10,14},{3,7},{... | collective-permute-start | bytes 3145736 | tf_op jit(solution)/shard_map/ppermute | solution.py:465
  34.7 25.7 %collective-permute-start.12 = (bf16[192,256]{1,0:T(8,128)(2,1)S(1)}, bf16[192,256]{1,0:T(8,128)(2,1)S(1)}, u32[]{:S(2)}, u32[]{:S(2)}) collective-permute-start(bf16[192,256]{1,0:T(8,128)(2,1)S(1)} %get-tuple-element.51), channel_id=1, source_target_pairs={{0,4},{4,0},{8,12},{12,8},{1,5},{5,1},{9,13},{13,9},{2,6},{6,2},{1... | collective-permute-start | bytes 294920 | tf_op jit(solution)/shard_map/ppermute | solution.py:434
  34.8 29.6 %collective-permute-start.13 = (bf16[192,256]{1,0:T(8,128)(2,1)S(1)}, bf16[192,256]{1,0:T(8,128)(2,1)S(1)}, u32[]{:S(2)}, u32[]{:S(2)}) collective-permute-start(bf16[192,256]{1,0:T(8,128)(2,1)S(1)} %get-tuple-element.52), channel_id=1, source_target_pairs={{0,8},{4,12},{8,0},{12,4},{1,9},{5,13},{9,1},{13,5},{2,10},{6,14},... | collective-permute-start | bytes 294920 | tf_op jit(solution)/shard_map/ppermute | solution.py:434
  60.5 6.7 %collective-permute-start.14 = (bf16[192,256]{1,0:T(8,128)(2,1)S(1)}, bf16[192,256]{1,0:T(8,128)(2,1)S(1)}, u32[]{:S(2)}, u32[]{:S(2)}) collective-permute-start(bf16[192,256]{1,0:T(8,128)(2,1)S(1)} %get-tuple-element.53), channel_id=1, source_target_pairs={{0,12},{4,8},{8,4},{12,0},{1,13},{5,9},{9,5},{13,1},{2,14},{6,10},... | collective-permute-start | bytes 294920 | tf_op jit(solution)/shard_map/ppermute | solution.py:434
  67.2 10.8 %collective-permute-start.16 = (bf16[4,192,256]{2,1,0:T(8,128)(2,1)S(1)}, bf16[4,192,256]{2,1,0:T(8,128)(2,1)S(1)}, u32[]{:S(2)}, u32[]{:S(2)}) collective-permute-start(bf16[4,192,256]{2,1,0:T(8,128)(2,1)S(1)} %stack_columns.2.refs_0_), channel_id=1, source_target_pairs={{0,2},{1,3},{2,0},{3,1},{4,6},{5,7},{6,4},{7,5},{8,10},{9,11},{10,... | collective-permute-start | bytes 1179656 | tf_op jit(solution)/shard_map/ppermute | solution.py:434
  69.7 10.3 %collective-permute-start.15 = (bf16[4,192,256]{2,1,0:T(8,128)(2,1)S(1)}, bf16[4,192,256]{2,1,0:T(8,128)(2,1)S(1)}, u32[]{:S(2)}, u32[]{:S(2)}) collective-permute-start(bf16[4,192,256]{2,1,0:T(8,128)(2,1)S(1)} %stack_columns.2.refs_0_), channel_id=1, source_target_pairs={{0,1},{1,0},{2,3},{3,2},{4,5},{5,4},{6,7},{7,6},{8,9},{9,8},{10,11... | collective-permute-start | bytes 1179656 | tf_op jit(solution)/shard_map/ppermute | solution.py:434
  78.0 2.0 %collective-permute-start.17 = (bf16[4,192,256]{2,1,0:T(8,128)(2,1)S(1)}, bf16[4,192,256]{2,1,0:T(8,128)(2,1)S(1)}, u32[]{:S(2)}, u32[]{:S(2)}) collective-permute-start(bf16[4,192,256]{2,1,0:T(8,128)(2,1)S(1)} %collective-permute-done.16.refs_2_), channel_id=1, source_target_pairs={{0,1},{1,0},{2,3},{3,2},{4,5},{5,4},{6,7},{7,6},{8,9},{9,8},{10,11... | collective-permute-start | bytes 1179656 | tf_op jit(solution)/shard_map/ppermute | solution.py:434
  78.2 11.7 %collective-permute-start.4 = (bf16[1,256,768]{2,1,0:T(8,128)(2,1)S(1)}, bf16[1,256,768]{2,1,0:T(8,128)(2,1)S(1)}, u32[]{:S(2)}, u32[]{:S(2)}) collective-permute-start(bf16[1,256,768]{2,1,0:T(8,128)(2,1)S(1)} %get-tuple-element.40.refs_6_), channel_id=1, source_target_pairs={{0,2},{1,3},{2,0},{3,1},{4,6},{5,7},{6,4},{7,5},{8,10},{9,11},{10,... | collective-permute-start | bytes 1179656 | tf_op jit(solution)/shard_map/ppermute | solution.py:434
  87.8 27.5 %collective-permute-start.18 = (bf16[1024,512]{1,0:T(8,128)(2,1)S(1)}, bf16[1024,512]{1,0:T(8,128)(2,1)S(1)}, u32[]{:S(2)}, u32[]{:S(2)}) collective-permute-start(bf16[1024,512]{1,0:T(8,128)(2,1)S(1)} %get-tuple-element.56.refs_5_), channel_id=1, source_target_pairs={{4,8},{8,12},{5,9},{9,13},{6,10},{10,14},{7,11},{11,15},{20,24},{2... | collective-permute-start | bytes 3145736 | tf_op jit(solution)/shard_map/ppermute | solution.py:465
  88.6 27.2 %collective-permute-start.19 = (bf16[1024,512]{1,0:T(8,128)(2,1)S(1)}, bf16[1024,512]{1,0:T(8,128)(2,1)S(1)}, u32[]{:S(2)}, u32[]{:S(2)}) collective-permute-start(bf16[1024,512]{1,0:T(8,128)(2,1)S(1)} %get-tuple-element.57.refs_8_), channel_id=1, source_target_pairs={{8,4},{4,0},{9,5},{5,1},{10,6},{6,2},{11,7},{7,3},{24,20},{20,16},... | collective-permute-start | bytes 3145736 | tf_op jit(solution)/shard_map/ppermute | solution.py:466
  91.5 11.3 %collective-permute-start.6 = (bf16[256,768]{1,0:T(8,128)(2,1)S(1)}, bf16[256,768]{1,0:T(8,128)(2,1)S(1)}, u32[]{:S(2)}, u32[]{:S(2)}) collective-permute-start(bf16[256,768]{1,0:T(8,128)(2,1)S(1)} %get-tuple-element.42.refs_0_), channel_id=1, source_target_pairs={{0,2},{1,3},{2,0},{3,1},{4,6},{5,7},{6,4},{7,5},{8,10},{9,11},{10,... | collective-permute-start | bytes 1179656 | tf_op jit(solution)/shard_map/ppermute | solution.py:434
  93.2 9.6 %collective-permute-start.5 = (bf16[256,768]{1,0:T(8,128)(2,1)S(1)}, bf16[256,768]{1,0:T(8,128)(2,1)S(1)}, u32[]{:S(2)}, u32[]{:S(2)}) collective-permute-start(bf16[256,768]{1,0:T(8,128)(2,1)S(1)} %get-tuple-element.42.refs_0_), channel_id=1, source_target_pairs={{0,1},{1,0},{2,3},{3,2},{4,5},{5,4},{6,7},{7,6},{8,9},{9,8},{10,11... | collective-permute-start | bytes 1179656 | tf_op jit(solution)/shard_map/ppermute | solution.py:434
  102.8 1.7 collective-permute-start.7
  112.9 61.9 %copy-start.1 = (bf16[8,4,32,512]{3,2,1,0:T(8,128)(2,1)S(1)}, bf16[8,4,32,512]{3,2,1,0:T(8,128)(2,1)}, u32[]{:S(2)}) copy-start(bf16[8,4,32,512]{3,2,1,0:T(8,128)(2,1)} %param.16) | copy-start | bytes 3145732
  112.9 14.9 %collective-permute-start.8 = (bf16[2,160,512]{2,1,0:T(8,128)(2,1)S(1)}, bf16[2,160,512]{2,1,0:T(8,128)(2,1)S(1)}, u32[]{:S(2)}, u32[]{:S(2)}) collective-permute-start(bf16[2,160,512]{2,1,0:T(8,128)(2,1)S(1)} %get-tuple-element.44), channel_id=1, source_target_pairs={{0,4},{4,0},{8,12},{12,8},{1,5},{5,1},{9,13},{13,9},{2,6},{6,2},{1... | collective-permute-start | bytes 983048 | tf_op jit(solution)/shard_map/ppermute | solution.py:434
  115.7 16.3 %collective-permute-start.20 = (bf16[384,256]{1,0:T(8,128)(2,1)S(1)}, bf16[384,256]{1,0:T(8,128)(2,1)S(1)}, u32[]{:S(2)}, u32[]{:S(2)}) collective-permute-start(bf16[384,256]{1,0:T(8,128)(2,1)S(1)} %get-tuple-element.58), channel_id=1, source_target_pairs={{0,4},{4,0},{8,12},{12,8},{1,5},{5,1},{9,13},{13,9},{2,6},{6,2},{1... | collective-permute-start | bytes 589832 | tf_op jit(solution)/shard_map/ppermute | solution.py:434
  118.6 13.4 %collective-permute-start.21 = (bf16[384,256]{1,0:T(8,128)(2,1)S(1)}, bf16[384,256]{1,0:T(8,128)(2,1)S(1)}, u32[]{:S(2)}, u32[]{:S(2)}) collective-permute-start(bf16[384,256]{1,0:T(8,128)(2,1)S(1)} %get-tuple-element.59), channel_id=1, source_target_pairs={{0,8},{4,12},{8,0},{12,4},{1,9},{5,13},{9,1},{13,5},{2,10},{6,14},... | collective-permute-start | bytes 589832 | tf_op jit(solution)/shard_map/ppermute | solution.py:434
  119.7 20.5 %collective-permute-start.22 = (bf16[384,256]{1,0:T(8,128)(2,1)S(1)}, bf16[384,256]{1,0:T(8,128)(2,1)S(1)}, u32[]{:S(2)}, u32[]{:S(2)}) collective-permute-start(bf16[384,256]{1,0:T(8,128)(2,1)S(1)} %get-tuple-element.60), channel_id=1, source_target_pairs={{0,12},{4,8},{8,4},{12,0},{1,13},{5,9},{9,5},{13,1},{2,14},{6,10},... | collective-permute-start | bytes 589832 | tf_op jit(solution)/shard_map/ppermute | solution.py:434
  140.3 21.2 %collective-permute-start.24 = (bf16[4,384,256]{2,1,0:T(8,128)(2,1)S(1)}, bf16[4,384,256]{2,1,0:T(8,128)(2,1)S(1)}, u32[]{:S(2)}, u32[]{:S(2)}) collective-permute-start(bf16[4,384,256]{2,1,0:T(8,128)(2,1)S(1)} %stack_columns.3.refs_0_), channel_id=1, source_target_pairs={{0,2},{1,3},{2,0},{3,1},{4,6},{5,7},{6,4},{7,5},{8,10},{9,11},{10,... | collective-permute-start | bytes 2359304 | tf_op jit(solution)/shard_map/ppermute | solution.py:434
  143.6 38.9 %copy-start.5 = (s32[128,8]{0,1:T(8,128)S(1)}, s32[128,8]{0,1:T(8,128)}, u32[]{:S(2)}) copy-start(s32[128,8]{0,1:T(8,128)} %param.12) | copy-start | bytes 12292
  143.6 38.9 %copy-start.6 = (s32[128,8]{0,1:T(8,128)S(1)}, s32[128,8]{0,1:T(8,128)}, u32[]{:S(2)}) copy-start(s32[128,8]{0,1:T(8,128)} %param.13) | copy-start | bytes 12292
  143.6 18.0 %collective-permute-start.26 = (bf16[1024,512]{1,0:T(8,128)(2,1)S(1)}, bf16[1024,512]{1,0:T(8,128)(2,1)S(1)}, u32[]{:S(2)}, u32[]{:S(2)}) collective-permute-start(bf16[1024,512]{1,0:T(8,128)(2,1)S(1)} %get-tuple-element.61.refs_6_), channel_id=1, source_target_pairs={{8,12},{9,13},{10,14},{11,15},{24,28},{25,29},{26,30},{27,31}} | collective-permute-start | bytes 3145736 | tf_op jit(solution)/shard_map/ppermute | solution.py:465
  144.5 30.3 %collective-permute-start.27 = (bf16[1024,512]{1,0:T(8,128)(2,1)S(1)}, bf16[1024,512]{1,0:T(8,128)(2,1)S(1)}, u32[]{:S(2)}, u32[]{:S(2)}) collective-permute-start(bf16[1024,512]{1,0:T(8,128)(2,1)S(1)} %get-tuple-element.62.refs_9_), channel_id=1, source_target_pairs={{4,0},{5,1},{6,2},{7,3},{20,16},{21,17},{22,18},{23,19}} | collective-permute-start | bytes 3145736 | tf_op jit(solution)/shard_map/ppermute | solution.py:466
  145.8 15.8 %collective-permute-start.23 = (bf16[4,384,256]{2,1,0:T(8,128)(2,1)S(1)}, bf16[4,384,256]{2,1,0:T(8,128)(2,1)S(1)}, u32[]{:S(2)}, u32[]{:S(2)}) collective-permute-start(bf16[4,384,256]{2,1,0:T(8,128)(2,1)S(1)} %stack_columns.3.refs_0_), channel_id=1, source_target_pairs={{0,1},{1,0},{2,3},{3,2},{4,5},{5,4},{6,7},{7,6},{8,9},{9,8},{10,11... | collective-permute-start | bytes 2359304 | tf_op jit(solution)/shard_map/ppermute | solution.py:434
  161.4 13.3 %collective-permute-start.25 = (bf16[4,384,256]{2,1,0:T(8,128)(2,1)S(1)}, bf16[4,384,256]{2,1,0:T(8,128)(2,1)S(1)}, u32[]{:S(2)}, u32[]{:S(2)}) collective-permute-start(bf16[4,384,256]{2,1,0:T(8,128)(2,1)S(1)} %collective-permute-done.24.refs_2_), channel_id=1, source_target_pairs={{0,1},{1,0},{2,3},{3,2},{4,5},{5,4},{6,7},{7,6},{8,9},{9,8},{10,11... | collective-permute-start | bytes 2359304 | tf_op jit(solution)/shard_map/ppermute | solution.py:434
  161.5 21.0 %collective-permute-start.9 = (bf16[1,160,512]{2,1,0:T(8,128)(2,1)S(1)}, bf16[1,160,512]{2,1,0:T(8,128)(2,1)S(1)}, u32[]{:S(2)}, u32[]{:S(2)}) collective-permute-start(bf16[1,160,512]{2,1,0:T(8,128)(2,1)S(1)} %get-tuple-element.46), channel_id=1, source_target_pairs={{0,8},{4,12},{8,0},{12,4},{1,9},{5,13},{9,1},{13,5},{2,10},{6,14},... | collective-permute-start | bytes 491528 | tf_op jit(solution)/shard_map/ppermute | solution.py:434

commit v11 on v10

--- a/solution.py
+++ b/solution.py
@@ -11,6 +11,7 @@
 BF = jnp.bfloat16
 F32 = jnp.float32
 PER = 2
+GROUPS = 2
 
 
 def nt(a, b):
@@ -196,6 +197,7 @@
 
 
 def pre_kernel(z, ids_ref, keep_ref, got_ref, pair_ref, codes_ref, *refs):
+    refs = refs[z.ep - 1 :]
     outs, (grad_ref, sides) = refs[: z.ep], refs[z.ep :]
     me = ids_ref[0]
     block = ids_ref[1] * z.part_blocks + pl.program_id(0)
@@ -216,7 +218,7 @@
 
 
 def hidden_kernel(z, ids_ref, pair_ref, *refs):
-    refs = refs[z.ep :]
+    refs = refs[z.ep - 1 :]
     pair = pair_ref[...]
     gate_pre = pair[:, : z.hidden].astype(F32)
     up = pair[:, z.hidden :].astype(F32)
@@ -224,9 +226,9 @@
     send_columns(z, ids_ref[0], hidden.astype(BF).T, refs[-1], refs[:-1])
 
 
-def stack_kernel(z, *refs):
-    for k in range(z.ep):
-        refs[-1][k] = refs[k][...]
+def stack_kernel(*refs):
+    for k, ref in enumerate(refs[:-1]):
+        refs[-1][k] = ref[...]
 
 
 def row_kernel(z, ids_ref, *refs):
@@ -302,27 +304,6 @@
             same = key_hits(z, count_ref, routes_ref, replica_ref, r, k)
             totals[k] += jnp.sum(jnp.where(same, spread, 0.0), axis=0, keepdims=True)
     route_ref[...] = jnp.concatenate(totals, axis=0).astype(BF)
-
-
-def input_moves(z, me, own_ref, rights, lefts, inputs_ref, own_sem, right_sems, left_sems, act):
-    act(pltpu.make_async_copy(own_ref, inputs_ref.at[me], own_sem))
-    for d in range(1, z.ep):
-
-        @pl.when(me >= d)
-        def _():
-            act(
-                pltpu.make_async_copy(
-                    rights[d - 1], inputs_ref.at[me - d], right_sems.at[d - 1]
-                )
-            )
-
-        @pl.when(me + d < z.ep)
-        def _():
-            act(
-                pltpu.make_async_copy(
-                    lefts[d - 1], inputs_ref.at[me + d], left_sems.at[d - 1]
-                )
-            )
 
 
 def left_rows(held, part, side, spot, size):
@@ -409,15 +390,18 @@
 
 
 def total_in_kernel(z, ids_ref, table_ref, *refs):
-    sides, refs = refs[: z.sub], refs[z.sub :]
-    own_ref, rights, lefts = refs[0], refs[1 : z.ep], refs[z.ep : 2 * z.ep - 1]
-    out_ref, token_ref, held, made, out_sems, inputs_ref, sems, *other_sems = refs[2 * z.ep - 1 :]
+    sides, refs = refs[: GROUPS * z.sub], refs[GROUPS * z.sub :]
+    size = z.ep // GROUPS
+    gathered_ref, out_ref, token_ref, held, made, out_sems, inputs_ref, sems, in_sems = refs
     token_ref[...] = jnp.zeros_like(token_ref)
 
     def moves(act):
-        for k in range(z.sub):
-            act(pltpu.make_async_copy(sides[k], held.at[k, pl.ds(0, z.ep)], sems.at[k]))
-        input_moves(z, ids_ref[0], own_ref, rights, lefts, inputs_ref, *other_sems, act)
+        for i in range(GROUPS * z.sub):
+            g, k = divmod(i, z.sub)
+            spots = held.at[k, pl.ds(g * size, size)]
+            act(pltpu.make_async_copy(sides[i], spots, sems.at[i]))
+        for p in range(z.ep):
+            act(pltpu.make_async_copy(gathered_ref.at[p], inputs_ref.at[p], in_sems.at[p]))
 
     moves(lambda copy: copy.start())
     held[:, z.ep] = jnp.zeros_like(held[:, z.ep])
@@ -459,12 +443,6 @@
         compiler_params=pltpu.CompilerParams(vmem_limit_bytes=1024 * 1024),
         name="gate",
     )(*values, *after)
-
-
-def chain_step(go, back, axis, size, d):
-    go = lax.ppermute(go, axis, [(i, i + 1) for i in range(d - 1, size - 1)])
-    back = lax.ppermute(back, axis, [(i, i - 1) for i in range(size - d, 0, -1)])
-    return go, back
 
 
 def body(
@@ -501,7 +479,7 @@
     )(token_count, *routing)
     bufs = [buf] + [swap(buf, "ep", n, k) for k in range(1, n)]
 
-    chain = gate([inputs], [buf])
+    gathered = lax.all_gather(inputs, "ep")
     downs = pl.pallas_call(
         functools.partial(hidden_kernel, z),
         grid_spec=pltpu.PrefetchScalarGridSpec(
@@ -510,25 +488,23 @@
             in_specs=[
                 pl.BlockSpec((z.block, z.pair), lambda i, r: (r[1] * z.part_blocks + i, 0))
             ]
-            + [pl.BlockSpec(memory_space=pl.ANY)] * n,
+            + [pl.BlockSpec(memory_space=pl.ANY)] * (n - 1),
             out_specs=[pl.BlockSpec((z.down_cols, z.block), lambda i, r: (0, i))] * n,
             scratch_shapes=[pltpu.VMEM((n, z.down_cols, z.block), BF)],
         ),
         out_shape=[jax.ShapeDtypeStruct((z.down_cols, z.part), BF)] * n,
         compiler_params=params(16),
         name="hidden_columns",
-    )(ids, pair_rows, *bufs[1:], chain[0])
-    chain = gate(chain, [*bufs[1:], downs[0]])
+    )(ids, pair_rows, *bufs[1:])
     downs = [downs[0]] + [swap(downs[k], "ep", n, k) for k in range(1, n)]
-    steps = [chain_step(chain[0], chain[0], "ep", n, 1)]
 
     def stack(pieces):
-        shape = pieces[0].shape
+        shape, count = pieces[0].shape, len(pieces)
         return pl.pallas_call(
-            functools.partial(stack_kernel, z),
-            in_specs=[whole(shape)] * n,
-            out_specs=whole((n,) + shape),
-            out_shape=jax.ShapeDtypeStruct((n,) + shape, BF),
+            stack_kernel,
+            in_specs=[whole(shape)] * count,
+            out_specs=whole((count,) + shape),
+            out_shape=jax.ShapeDtypeStruct((count,) + shape, BF),
             grid=(1,),
             compiler_params=params(12),
             name="stack_columns",
@@ -573,7 +549,7 @@
         ],
         compiler_params=params(48),
         name="hidden_partials",
-    )(ids, *bufs, weight_down, chain[0])
+    )(ids, *bufs, weight_down, downs[0])
     keep, send, grads_all, codes = outs
     got = swap(send, "sub", m, 1)
     bit = 2
@@ -614,8 +590,6 @@
         [pltpu.VMEM((z.slots, z.rows, z.width), BF), pltpu.SemaphoreType.DMA((m,))],
         "down_grads",
     )
-    steps[0] = gate(steps[0], [down_made])
-    steps.append(chain_step(*steps[0], "ep", n, 2))
     *pieces, grad_part = pl.pallas_call(
         functools.partial(pre_kernel, z),
         grid_spec=pltpu.PrefetchScalarGridSpec(
@@ -625,7 +599,8 @@
             + [
                 pl.BlockSpec((z.block, z.pair), lambda i, r: (r[1] * z.part_blocks + i, 0)),
                 whole(code_shape),
-            ],
+            ]
+            + [pl.BlockSpec(memory_space=pl.ANY)] * (n - 1),
             out_specs=[pl.BlockSpec((z.in_cols, z.block), lambda i, r: (0, i))] * n
             + [pl.BlockSpec((z.block, z.hidden), lambda i, r: (i, 0))],
             scratch_shapes=[pltpu.VMEM((n, z.in_cols, z.block), BF)],
@@ -634,9 +609,8 @@
         + [jax.ShapeDtypeStruct((z.part, z.hidden), BF)],
         compiler_params=params(16),
         name="pre_grads",
-    )(ids, keep, got, pair_rows, codes)
-    late = gate(pieces[1:], steps[1])
-    pieces = pieces[:1] + [swap(a, "ep", n, k) for k, a in enumerate(late, 1)]
+    )(ids, keep, got, pair_rows, codes, *downs[1:])
+    pieces = [pieces[0]] + [swap(pieces[k], "ep", n, k) for k in range(1, n)]
     grad_parts = spread_over({0: grad_part}, "sub", m, m // 2)
 
     back_shape = (n // 2, z.tokens + z.slots, z.width)
@@ -664,14 +638,11 @@
         compiler_params=params(46),
         name="row_grads",
     )(ids, *grad_parts, pair_rows, weight_in, codes)
-    steps[1] = gate(steps[1], pieces[1:])
-    for d in range(3, n):
-        steps.append(chain_step(*steps[-1], "ep", n, d))
-    gathered = [inputs] + [go for go, _ in steps] + [back for _, back in steps]
     got = swap(send, "ep", n, 1)
-    pieces[:1] = gate(pieces[:1], [got])
-    columns = stack(pieces)
-    sides = spread_over({0: columns}, "sub", m, m // 2)
+    sides = []
+    for g in range(0, n, n // GROUPS):
+        stacked = stack(pieces[g : g + n // GROUPS])
+        sides += spread_over({0: stacked}, "sub", m, m // 2)
     bit = 2
     while bit < n:
         keep, send = halve(keep, got)
@@ -680,15 +651,13 @@
 
     grad_in, in_made = total_call(
         total_in_kernel,
-        [*sides, *gathered],
-        [anywhere] * (m + 2 * n - 1),
+        [*sides, gathered],
+        [anywhere] * (GROUPS * m + 1),
         z.in_cols,
         [
             pltpu.VMEM((n, z.all_rows, z.width), BF),
-            pltpu.SemaphoreType.DMA((m,)),
-            pltpu.SemaphoreType.DMA,
-            pltpu.SemaphoreType.DMA((n - 1,)),
-            pltpu.SemaphoreType.DMA((n - 1,)),
+            pltpu.SemaphoreType.DMA((GROUPS * m,)),
+            pltpu.SemaphoreType.DMA((n,)),
         ],
         "in_grads",
     )

time: 184 us -> 174 us (0.946)
  waiting for transfers between devices: 106 us -> 62.6 us
  starting transfers between devices: 37.4 us -> 52.5 us
  between operations: 1.72 us -> 14.9 us
  local copies, waits for them, and re-layouts: 2.16 us -> 5.66 us
    ppermute x22 -> x25, waiting for transfers between devices: 92.3 us -> 61.9 us  [swap(): return lax.ppermute(x, axis, [(i, i ^ bit) for i in range(size)])]
    ppermute x22 -> x25, starting transfers between devices: 27.3 us -> 52.4 us  [swap(): return lax.ppermute(x, axis, [(i, i ^ bit) for i in range(size)])]
    ppermute x6 -> x0, waiting for transfers between devices: 13.6 us -> none  [the longest x3 13.6 us: chain_step(): lax.ppermute(back, axis, [(i, i - 1) for i in range(size - d, 0, -1)])]
    ppermute x6 -> x0, starting transfers between devices: 10.1 us -> none  [the longest x3 6.19 us: chain_step(): go = lax.ppermute(go, axis, [(i, i + 1) for i in range(d - 1, size - 1)])]
    unnamed x15 -> x18, local copies, waits for them, and re-layouts: 2.16 us -> 5.66 us
    pallas_call x2, Pallas kernels: 15.5 us -> 17.4 us  [total_call(): pl.pallas_call(functools.partial(kernel, z), grid_spec=pltpu.PrefetchScal...]
  transfers between devices with their start and end apart: 28 -> 26, of which waited for: 13 -> 11; matrix products, arithmetic and copies ran while one was open for 1% -> 0% of each run, Pallas kernels for 14% -> 21%
where the time goes in v11:
time: 174 us; the launch traced here: 173 us
  waiting for transfers between devices  62.6 us (36%)
  starting transfers between devices  52.5 us (30%)
  Pallas kernels  37.6 us (22%)
  between operations  14.9 us (9%)
  local copies, waits for them, and re-layouts  5.66 us (3%)
    ppermute x25, waiting for transfers between devices, swap(): return lax.ppermute(x, axis, [(i, i ^ bit) for i in range(size)])  61.9 us
    ppermute x25, starting transfers between devices, swap(): return lax.ppermute(x, axis, [(i, i ^ bit) for i in range(size)])  52.4 us
    pallas_call x2, Pallas kernels, total_call(): pl.pallas_call(functools.partial(kernel, z), grid_spec=pltpu.PrefetchScal...  17.4 us
    pallas_call x1, Pallas kernels, body(): pl.pallas_call(functools.partial(row_kernel, z), grid_spec=pltpu.Prefetch...  8.32 us
    unnamed x18, local copies, waits for them, and re-layouts  5.66 us
    pallas_call x1, Pallas kernels, body(): pl.pallas_call(functools.partial(down_kernel, z), grid_spec=pltpu.Prefetc...  5.48 us
  transfers between devices with their start and end apart: 26, of which 11 were waited for; matrix products, arithmetic and copies ran while one was open for 0% of the time, Pallas kernels for 21%

profile of v11, /device:TPU:0, one launch (start us, length us, event | category | flops | bytes accessed | tf_op | source)
XLA Modules:
  0.0 173.2 jit_solution(3024329295147322373)
XLA Ops:
  7.2 0.0 all-gather.2.cloned.1.call-start
  7.2 0.7 all-gather.2.cloned.1.call-update
  8.5 1.9 %route.1.refs_0_ = bf16[144,512]{1,0:T(8,128)(2,1)} custom-call(s32[1]{0:T(128)S(6)} %copy.16.count_ref, bf16[128,512]{1,0:T(8,128)(2,1)} %grad_ref.1, bf16[8,128]{1,0:T(8,128)(2,1)} %bitcast.21, s32[8,128]{1,0:T(8,128)} %bitcast.16, s32[8,128]{1,0:T(8,128)} %bitcast.18, s32[4,16]{1,0:T(4,128)} %bitcast.12), custom_call_target="tpu_custom_call" | custom-call | tf_op jit(solution)/shard_map/route/pallas_call | solution.py:471
  10.4 3.0 %collective-permute-start = (bf16[144,512]{1,0:T(8,128)(2,1)}, bf16[144,512]{1,0:T(8,128)(2,1)S(1)}, u32[]{:S(2)}, u32[]{:S(2)}) collective-permute-start(bf16[144,512]{1,0:T(8,128)(2,1)} %route.1.refs_0_), channel_id=1, source_target_pairs={{0,4},{4,0},{8,12},{12,8},{1,5},{5,1},{9,13},{13,9},{2,6},{6,2},{1... | collective-permute-start | bytes 442376 | tf_op jit(solution)/shard_map/ppermute | solution.py:418
  13.5 2.6 %collective-permute-start.1 = (bf16[144,512]{1,0:T(8,128)(2,1)}, bf16[144,512]{1,0:T(8,128)(2,1)S(1)}, u32[]{:S(2)}, u32[]{:S(2)}) collective-permute-start(bf16[144,512]{1,0:T(8,128)(2,1)} %route.1.refs_0_), channel_id=1, source_target_pairs={{0,8},{4,12},{8,0},{12,4},{1,9},{5,13},{9,1},{13,5},{2,10},{6,14},... | collective-permute-start | bytes 442376 | tf_op jit(solution)/shard_map/ppermute | solution.py:418
  16.1 0.1 pad_add_fusion.ids_ref
  16.1 3.4 %collective-permute-done.refs_0_.refs_1_ = bf16[144,512]{1,0:T(8,128)(2,1)S(1)} collective-permute-done((bf16[144,512]{1,0:T(8,128)(2,1)}, bf16[144,512]{1,0:T(8,128)(2,1)S(1)}, u32[]{:S(2)}, u32[]{:S(2)}) %collective-permute-start) | collective-permute-done | bytes 147488 | tf_op jit(solution)/shard_map/ppermute | solution.py:418
  19.5 15.3 %collective-permute-done.1.refs_1_.refs_2_ = bf16[144,512]{1,0:T(8,128)(2,1)S(1)} collective-permute-done((bf16[144,512]{1,0:T(8,128)(2,1)}, bf16[144,512]{1,0:T(8,128)(2,1)S(1)}, u32[]{:S(2)}, u32[]{:S(2)}) %collective-permute-start.1) | collective-permute-done | bytes 147488 | tf_op jit(solution)/shard_map/ppermute | solution.py:418
  34.8 1.9 %copy-done = bf16[8,128,1536]{2,1,0:T(8,128)(2,1)S(1)} copy-done((bf16[8,128,1536]{2,1,0:T(8,128)(2,1)S(1)}, bf16[8,128,1536]{2,1,0:T(8,128)(2,1)}, u32[]{:S(2)}) %copy-start) | copy-done | bytes 3145752
  36.7 1.1 hidden_columns.1
  37.8 0.9 copy-done.3
  38.7 5.5 %hidden_partials.1 = (bf16[2,256,768]{2,1,0:T(8,128)(2,1)S(1)}, bf16[2,256,768]{2,1,0:T(8,128)(2,1)S(1)}, bf16[4,128,512]{2,1,0:T(8,128)(2,1)S(1)}, f32[4,64,128]{2,1,0:T(8,128)S(1)}) custom-call(s32[2]{0:T(128)S(1)} %pad_add_fusion.ids_ref, bf16[144,512]{1,0:T(8,128)(2,1)S(1)} %copy-done.3, bf16[144,512]{1,0:T(8,128)(2,1)S(1)} %collective-permute-done.refs_0_.refs_1_, ...), custom_call_target="tpu_custom_call" | custom-call | tf_op jit(solution)/shard_map/hidden_partials/pallas_call | solution.py:530
  44.2 0.1 collective-permute-start.3
  44.3 2.3 %collective-permute-done.3.got_ref = bf16[2,256,768]{2,1,0:T(8,128)(2,1)S(1)} collective-permute-done((bf16[2,256,768]{2,1,0:T(8,128)(2,1)S(1)}, bf16[2,256,768]{2,1,0:T(8,128)(2,1)S(1)}, u32[]{:S(2)}, u32[]{:S(2)}) %collective-permute-start.3) | collective-permute-done | bytes 786464 | tf_op jit(solution)/shard_map/ppermute | solution.py:418
  46.5 0.2 halve.2
  46.7 2.5 %collective-permute-start.4 = (bf16[1,256,768]{2,1,0:T(8,128)(2,1)S(1)}, bf16[1,256,768]{2,1,0:T(8,128)(2,1)S(1)}, u32[]{:S(2)}, u32[]{:S(2)}) collective-permute-start(bf16[1,256,768]{2,1,0:T(8,128)(2,1)S(1)} %get-tuple-element.32.refs_6_), channel_id=1, source_target_pairs={{0,2},{1,3},{2,0},{3,1},{4,6},{5,7},{6,4},{7,5},{8,10},{9,11},{10,... | collective-permute-start | bytes 1179656 | tf_op jit(solution)/shard_map/ppermute | solution.py:418
  49.2 11.2 %collective-permute-start.5 = (bf16[192,256]{1,0:T(8,128)(2,1)S(1)}, bf16[192,256]{1,0:T(8,128)(2,1)S(1)}, u32[]{:S(2)}, u32[]{:S(2)}) collective-permute-start(bf16[192,256]{1,0:T(8,128)(2,1)S(1)} %get-tuple-element.34), channel_id=1, source_target_pairs={{0,4},{4,0},{8,12},{12,8},{1,5},{5,1},{9,13},{13,9},{2,6},{6,2},{1... | collective-permute-start | bytes 294920 | tf_op jit(solution)/shard_map/ppermute | solution.py:418
  60.4 1.9 %collective-permute-start.6 = (bf16[192,256]{1,0:T(8,128)(2,1)S(1)}, bf16[192,256]{1,0:T(8,128)(2,1)S(1)}, u32[]{:S(2)}, u32[]{:S(2)}) collective-permute-start(bf16[192,256]{1,0:T(8,128)(2,1)S(1)} %get-tuple-element.35), channel_id=1, source_target_pairs={{0,8},{4,12},{8,0},{12,4},{1,9},{5,13},{9,1},{13,5},{2,10},{6,14},... | collective-permute-start | bytes 294920 | tf_op jit(solution)/shard_map/ppermute | solution.py:418
  62.3 1.5 collective-permute-start.7
  63.8 6.8 %collective-permute-done.5.refs_0_.refs_1_ = bf16[192,256]{1,0:T(8,128)(2,1)S(1)} collective-permute-done((bf16[192,256]{1,0:T(8,128)(2,1)S(1)}, bf16[192,256]{1,0:T(8,128)(2,1)S(1)}, u32[]{:S(2)}, u32[]{:S(2)}) %collective-permute-start.5) | collective-permute-done | bytes 98336 | tf_op jit(solution)/shard_map/ppermute | solution.py:418
  70.6 4.5 %collective-permute-done.6.refs_1_.refs_2_ = bf16[192,256]{1,0:T(8,128)(2,1)S(1)} collective-permute-done((bf16[192,256]{1,0:T(8,128)(2,1)S(1)}, bf16[192,256]{1,0:T(8,128)(2,1)S(1)}, u32[]{:S(2)}, u32[]{:S(2)}) %collective-permute-start.6) | collective-permute-done | bytes 98336 | tf_op jit(solution)/shard_map/ppermute | solution.py:418
  75.0 2.5 %collective-permute-done.7.refs_2_.refs_3_ = bf16[192,256]{1,0:T(8,128)(2,1)S(1)} collective-permute-done((bf16[192,256]{1,0:T(8,128)(2,1)S(1)}, bf16[192,256]{1,0:T(8,128)(2,1)S(1)}, u32[]{:S(2)}, u32[]{:S(2)}) %collective-permute-start.7) | collective-permute-done | bytes 98336 | tf_op jit(solution)/shard_map/ppermute | solution.py:418
  77.5 1.6 pre_grads.1
  79.2 0.3 collective-permute-start.9
  79.4 8.4 %collective-permute-start.13 = (bf16[384,256]{1,0:T(8,128)(2,1)S(1)}, bf16[384,256]{1,0:T(8,128)(2,1)S(1)}, u32[]{:S(2)}, u32[]{:S(2)}) collective-permute-start(bf16[384,256]{1,0:T(8,128)(2,1)S(1)} %get-tuple-element.43), channel_id=1, source_target_pairs={{0,4},{4,0},{8,12},{12,8},{1,5},{5,1},{9,13},{13,9},{2,6},{6,2},{1... | collective-permute-start | bytes 589832 | tf_op jit(solution)/shard_map/ppermute | solution.py:418
  87.8 1.4 collective-permute-done.9.refs_2_
  89.2 8.1 %collective-permute-start.17 = (bf16[384,256]{1,0:T(8,128)(2,1)S(1)}, bf16[384,256]{1,0:T(8,128)(2,1)S(1)}, u32[]{:S(2)}, u32[]{:S(2)}) collective-permute-start(bf16[384,256]{1,0:T(8,128)(2,1)S(1)} %get-tuple-element.44), channel_id=1, source_target_pairs={{0,8},{4,12},{8,0},{12,4},{1,9},{5,13},{9,1},{13,5},{2,10},{6,14},... | collective-permute-start | bytes 589832 | tf_op jit(solution)/shard_map/ppermute | solution.py:418
  97.4 0.4 collective-permute-start.18
  97.8 2.3 %collective-permute-done.13.refs_1_ = bf16[384,256]{1,0:T(8,128)(2,1)S(1)} collective-permute-done((bf16[384,256]{1,0:T(8,128)(2,1)S(1)}, bf16[384,256]{1,0:T(8,128)(2,1)S(1)}, u32[]{:S(2)}, u32[]{:S(2)}) %collective-permute-start.13) | collective-permute-done | bytes 196640 | tf_op jit(solution)/shard_map/ppermute | solution.py:418
  100.1 1.5 collective-permute-start.23
  101.7 15.8 %collective-permute-done.17.refs_0_ = bf16[384,256]{1,0:T(8,128)(2,1)S(1)} collective-permute-done((bf16[384,256]{1,0:T(8,128)(2,1)S(1)}, bf16[384,256]{1,0:T(8,128)(2,1)S(1)}, u32[]{:S(2)}, u32[]{:S(2)}) %collective-permute-start.17) | collective-permute-done | bytes 196640 | tf_op jit(solution)/shard_map/ppermute | solution.py:418
  117.5 0.1 collective-permute-start.22
  117.6 0.6 collective-permute-start.15
  118.2 1.5 collective-permute-start.20
  119.7 8.3 %row_grads.1 = (bf16[2,160,512]{2,1,0:T(8,128)(2,1)S(1)}, bf16[2,160,512]{2,1,0:T(8,128)(2,1)S(1)}) custom-call(s32[2]{0:T(128)S(1)} %pad_add_fusion.ids_ref, bf16[256,768]{1,0:T(8,128)(2,1)S(1)} %get-tuple-element.37.refs_0_, bf16[256,768]{1,0:T(8,128)(2,1)S(1)} %collective-permute-done.8.refs_1_, bf16[256,768]{1,0:T(8,128)(2,1)S(1)} %collective-permute-done.9.refs_2_, ...), custom_call_target="tpu_custom_call" | custom-call | tf_op jit(solution)/shard_map/row_grads/pallas_call | solution.py:617
  128.1 5.5 %collective-permute-start.11 = (bf16[2,160,512]{2,1,0:T(8,128)(2,1)S(1)}, bf16[2,160,512]{2,1,0:T(8,128)(2,1)S(1)}, u32[]{:S(2)}, u32[]{:S(2)}) collective-permute-start(bf16[2,160,512]{2,1,0:T(8,128)(2,1)S(1)} %get-tuple-element.39), channel_id=1, source_target_pairs={{0,4},{4,0},{8,12},{12,8},{1,5},{5,1},{9,13},{13,9},{2,6},{6,2},{1... | collective-permute-start | bytes 983048 | tf_op jit(solution)/shard_map/ppermute | solution.py:418
  133.5 0.2 collective-permute-start.24
  133.7 0.3 collective-permute-start.14
  134.1 0.2 collective-permute-start.19
  134.2 3.2 %collective-permute-done.20.refs_6_ = bf16[2,384,256]{2,1,0:T(8,128)(2,1)S(1)} collective-permute-done((bf16[2,384,256]{2,1,0:T(8,128)(2,1)S(1)}, bf16[2,384,256]{2,1,0:T(8,128)(2,1)S(1)}, u32[]{:S(2)}, u32[]{:S(2)}) %collective-permute-start.20) | collective-permute-done | bytes 393248 | tf_op jit(solution)/shard_map/ppermute | solution.py:418
  137.5 4.4 %collective-permute-done.11.got_ref = bf16[2,160,512]{2,1,0:T(8,128)(2,1)S(1)} collective-permute-done((bf16[2,160,512]{2,1,0:T(8,128)(2,1)S(1)}, bf16[2,160,512]{2,1,0:T(8,128)(2,1)S(1)}, u32[]{:S(2)}, u32[]{:S(2)}) %collective-permute-start.11) | collective-permute-done | bytes 327712 | tf_op jit(solution)/shard_map/ppermute | solution.py:418
  141.9 0.7 halve.3
  142.6 0.7 copy-done.4
  143.2 2.6 %collective-permute-start.12 = (bf16[1,160,512]{2,1,0:T(8,128)(2,1)}, bf16[1,160,512]{2,1,0:T(8,128)(2,1)S(1)}, u32[]{:S(2)}, u32[]{:S(2)}) collective-permute-start(bf16[1,160,512]{2,1,0:T(8,128)(2,1)} %get-tuple-element.41), channel_id=1, source_target_pairs={{0,8},{4,12},{8,0},{12,4},{1,9},{5,13},{9,1},{13,5},{2,10},{6,14},... | collective-permute-start | bytes 491528 | tf_op jit(solution)/shard_map/ppermute | solution.py:418
  145.8 8.4 %down_grads.1 = (bf16[16,192,512]{2,1,0:T(8,128)(2,1)}, f32[8,128]{1,0:T(8,128)}) custom-call(s32[2]{0:T(128)S(1)} %pad_add_fusion.ids_ref, s32[4,16]{1,0:T(4,128)S(1)} %bitcast.13, bf16[4,192,256]{2,1,0:T(8,128)(2,1)S(1)} %stack_columns.5.refs_0_, bf16[4,192,256]{2,1,0:T(8,128)(2,1)S(1)} %collective-permute-done.22.refs_1_, ...), custom_call_target="tpu_custom_call" | custom-call | tf_op jit(solution)/shard_map/down_grads/pallas_call | solution.py:562
  154.4 2.2 %copy-done.2 = bf16[4,1024,512]{2,1,0:T(8,128)(2,1)S(1)} copy-done((bf16[4,1024,512]{2,1,0:T(8,128)(2,1)S(1)}, bf16[4,1024,512]{2,1,0:T(8,128)(2,1)}, u32[]{:S(2)}) %copy-start.2) | copy-done | bytes 4194328
  156.5 9.0 %in_grads.1 = (bf16[16,384,512]{2,1,0:T(8,128)(2,1)}, f32[8,128]{1,0:T(8,128)S(1)}) custom-call(s32[2]{0:T(128)S(1)} %pad_add_fusion.ids_ref, s32[4,16]{1,0:T(4,128)S(1)} %bitcast.14, bf16[2,384,256]{2,1,0:T(8,128)(2,1)S(1)} %stack_columns.3.refs_0_, bf16[2,384,256]{2,1,0:T(8,128)(2,1)S(1)} %collective-permute-done.14.refs_1_, ...), custom_call_target="tpu_custom_call" | custom-call | tf_op jit(solution)/shard_map/in_grads/pallas_call | solution.py:562
  165.6 0.8 token_grads.1
  (38 shorter events, 0.2 us)
Async XLA Ops:
  7.2 147.2 %all-gather.2.cloned.1.call-start = ((), (), s32[]{:S(2)}) async-start(), calls=%async_computation | async-start | bytes 5242880 | tf_op jit(solution)/shard_map/all_gather | solution.py:482
  10.4 9.1 %collective-permute-start = (bf16[144,512]{1,0:T(8,128)(2,1)}, bf16[144,512]{1,0:T(8,128)(2,1)S(1)}, u32[]{:S(2)}, u32[]{:S(2)}) collective-permute-start(bf16[144,512]{1,0:T(8,128)(2,1)} %route.1.refs_0_), channel_id=1, source_target_pairs={{0,4},{4,0},{8,12},{12,8},{1,5},{5,1},{9,13},{13,9},{2,6},{6,2},{1... | collective-permute-start | bytes 442376 | tf_op jit(solution)/shard_map/ppermute | solution.py:418
  13.5 21.3 %collective-permute-start.1 = (bf16[144,512]{1,0:T(8,128)(2,1)}, bf16[144,512]{1,0:T(8,128)(2,1)S(1)}, u32[]{:S(2)}, u32[]{:S(2)}) collective-permute-start(bf16[144,512]{1,0:T(8,128)(2,1)} %route.1.refs_0_), channel_id=1, source_target_pairs={{0,8},{4,12},{8,0},{12,4},{1,9},{5,13},{9,1},{13,5},{2,10},{6,14},... | collective-permute-start | bytes 442376 | tf_op jit(solution)/shard_map/ppermute | solution.py:418
  16.0 18.8 %collective-permute-start.2 = (bf16[144,512]{1,0:T(8,128)(2,1)}, bf16[144,512]{1,0:T(8,128)(2,1)S(1)}, u32[]{:S(2)}, u32[]{:S(2)}) collective-permute-start(bf16[144,512]{1,0:T(8,128)(2,1)} %route.1.refs_0_), channel_id=1, source_target_pairs={{0,12},{4,8},{8,4},{12,0},{1,13},{5,9},{9,5},{13,1},{2,14},{6,10},... | collective-permute-start | bytes 442376 | tf_op jit(solution)/shard_map/ppermute | solution.py:418
  34.8 1.9 %copy-start = (bf16[8,128,1536]{2,1,0:T(8,128)(2,1)S(1)}, bf16[8,128,1536]{2,1,0:T(8,128)(2,1)}, u32[]{:S(2)}) copy-start(bf16[8,128,1536]{2,1,0:T(8,128)(2,1)} %param.17) | copy-start | bytes 9437188
  36.7 40.8 %copy-start.1 = (bf16[8,128,1536]{2,1,0:T(8,128)(2,1)S(1)}, bf16[8,128,1536]{2,1,0:T(8,128)(2,1)}, u32[]{:S(2)}) copy-start(bf16[8,128,1536]{2,1,0:T(8,128)(2,1)} %param.17) | copy-start | bytes 9437188
  37.8 0.9 copy-start.3
  44.2 2.4 %collective-permute-start.3 = (bf16[2,256,768]{2,1,0:T(8,128)(2,1)S(1)}, bf16[2,256,768]{2,1,0:T(8,128)(2,1)S(1)}, u32[]{:S(2)}, u32[]{:S(2)}) collective-permute-start(bf16[2,256,768]{2,1,0:T(8,128)(2,1)S(1)} %get-tuple-element.30), channel_id=1, source_target_pairs={{0,1},{1,0},{2,3},{3,2},{4,5},{5,4},{6,7},{7,6},{8,9},{9,8},{10,11... | collective-permute-start | bytes 2359304 | tf_op jit(solution)/shard_map/ppermute | solution.py:418
  46.7 30.8 %collective-permute-start.4 = (bf16[1,256,768]{2,1,0:T(8,128)(2,1)S(1)}, bf16[1,256,768]{2,1,0:T(8,128)(2,1)S(1)}, u32[]{:S(2)}, u32[]{:S(2)}) collective-permute-start(bf16[1,256,768]{2,1,0:T(8,128)(2,1)S(1)} %get-tuple-element.32.refs_6_), channel_id=1, source_target_pairs={{0,2},{1,3},{2,0},{3,1},{4,6},{5,7},{6,4},{7,5},{8,10},{9,11},{10,... | collective-permute-start | bytes 1179656 | tf_op jit(solution)/shard_map/ppermute | solution.py:418
  49.2 21.3 %collective-permute-start.5 = (bf16[192,256]{1,0:T(8,128)(2,1)S(1)}, bf16[192,256]{1,0:T(8,128)(2,1)S(1)}, u32[]{:S(2)}, u32[]{:S(2)}) collective-permute-start(bf16[192,256]{1,0:T(8,128)(2,1)S(1)} %get-tuple-element.34), channel_id=1, source_target_pairs={{0,4},{4,0},{8,12},{12,8},{1,5},{5,1},{9,13},{13,9},{2,6},{6,2},{1... | collective-permute-start | bytes 294920 | tf_op jit(solution)/shard_map/ppermute | solution.py:418
  60.4 14.6 %collective-permute-start.6 = (bf16[192,256]{1,0:T(8,128)(2,1)S(1)}, bf16[192,256]{1,0:T(8,128)(2,1)S(1)}, u32[]{:S(2)}, u32[]{:S(2)}) collective-permute-start(bf16[192,256]{1,0:T(8,128)(2,1)S(1)} %get-tuple-element.35), channel_id=1, source_target_pairs={{0,8},{4,12},{8,0},{12,4},{1,9},{5,13},{9,1},{13,5},{2,10},{6,14},... | collective-permute-start | bytes 294920 | tf_op jit(solution)/shard_map/ppermute | solution.py:418
  62.3 15.2 %collective-permute-start.7 = (bf16[192,256]{1,0:T(8,128)(2,1)S(1)}, bf16[192,256]{1,0:T(8,128)(2,1)S(1)}, u32[]{:S(2)}, u32[]{:S(2)}) collective-permute-start(bf16[192,256]{1,0:T(8,128)(2,1)S(1)} %get-tuple-element.36), channel_id=1, source_target_pairs={{0,12},{4,8},{8,4},{12,0},{1,13},{5,9},{9,5},{13,1},{2,14},{6,10},... | collective-permute-start | bytes 294920 | tf_op jit(solution)/shard_map/ppermute | solution.py:418
  79.2 10.1 %collective-permute-start.9 = (bf16[256,768]{1,0:T(8,128)(2,1)S(1)}, bf16[256,768]{1,0:T(8,128)(2,1)S(1)}, u32[]{:S(2)}, u32[]{:S(2)}) collective-permute-start(bf16[256,768]{1,0:T(8,128)(2,1)S(1)} %get-tuple-element.37.refs_0_), channel_id=1, source_target_pairs={{0,2},{1,3},{2,0},{3,1},{4,6},{5,7},{6,4},{7,5},{8,10},{9,11},{10,... | collective-permute-start | bytes 1179656 | tf_op jit(solution)/shard_map/ppermute | solution.py:418
  79.4 38.8 %collective-permute-start.8 = (bf16[256,768]{1,0:T(8,128)(2,1)S(1)}, bf16[256,768]{1,0:T(8,128)(2,1)S(1)}, u32[]{:S(2)}, u32[]{:S(2)}) collective-permute-start(bf16[256,768]{1,0:T(8,128)(2,1)S(1)} %get-tuple-element.37.refs_0_), channel_id=1, source_target_pairs={{0,1},{1,0},{2,3},{3,2},{4,5},{5,4},{6,7},{7,6},{8,9},{9,8},{10,11... | collective-permute-start | bytes 1179656 | tf_op jit(solution)/shard_map/ppermute | solution.py:418
  79.4 20.7 %collective-permute-start.13 = (bf16[384,256]{1,0:T(8,128)(2,1)S(1)}, bf16[384,256]{1,0:T(8,128)(2,1)S(1)}, u32[]{:S(2)}, u32[]{:S(2)}) collective-permute-start(bf16[384,256]{1,0:T(8,128)(2,1)S(1)} %get-tuple-element.43), channel_id=1, source_target_pairs={{0,4},{4,0},{8,12},{12,8},{1,5},{5,1},{9,13},{13,9},{2,6},{6,2},{1... | collective-permute-start | bytes 589832 | tf_op jit(solution)/shard_map/ppermute | solution.py:418
  89.2 30.5 %collective-permute-start.10 = (bf16[256,768]{1,0:T(8,128)(2,1)S(1)}, bf16[256,768]{1,0:T(8,128)(2,1)S(1)}, u32[]{:S(2)}, u32[]{:S(2)}) collective-permute-start(bf16[256,768]{1,0:T(8,128)(2,1)S(1)} %collective-permute-done.9.refs_2_), channel_id=1, source_target_pairs={{0,1},{1,0},{2,3},{3,2},{4,5},{5,4},{6,7},{7,6},{8,9},{9,8},{10,11... | collective-permute-start | bytes 1179656 | tf_op jit(solution)/shard_map/ppermute | solution.py:418
  89.2 28.2 %collective-permute-start.17 = (bf16[384,256]{1,0:T(8,128)(2,1)S(1)}, bf16[384,256]{1,0:T(8,128)(2,1)S(1)}, u32[]{:S(2)}, u32[]{:S(2)}) collective-permute-start(bf16[384,256]{1,0:T(8,128)(2,1)S(1)} %get-tuple-element.44), channel_id=1, source_target_pairs={{0,8},{4,12},{8,0},{12,4},{1,9},{5,13},{9,1},{13,5},{2,10},{6,14},... | collective-permute-start | bytes 589832 | tf_op jit(solution)/shard_map/ppermute | solution.py:418
  97.4 20.2 %collective-permute-start.18 = (bf16[384,256]{1,0:T(8,128)(2,1)S(1)}, bf16[384,256]{1,0:T(8,128)(2,1)S(1)}, u32[]{:S(2)}, u32[]{:S(2)}) collective-permute-start(bf16[384,256]{1,0:T(8,128)(2,1)S(1)} %get-tuple-element.45), channel_id=1, source_target_pairs={{0,12},{4,8},{8,4},{12,0},{1,13},{5,9},{9,5},{13,1},{2,14},{6,10},... | collective-permute-start | bytes 589832 | tf_op jit(solution)/shard_map/ppermute | solution.py:418
  100.1 33.4 %collective-permute-start.23 = (bf16[4,192,256]{2,1,0:T(8,128)(2,1)S(1)}, bf16[4,192,256]{2,1,0:T(8,128)(2,1)S(1)}, u32[]{:S(2)}, u32[]{:S(2)}) collective-permute-start(bf16[4,192,256]{2,1,0:T(8,128)(2,1)S(1)} %stack_columns.5.refs_0_), channel_id=1, source_target_pairs={{0,2},{1,3},{2,0},{3,1},{4,6},{5,7},{6,4},{7,5},{8,10},{9,11},{10,... | collective-permute-start | bytes 1179656 | tf_op jit(solution)/shard_map/ppermute | solution.py:418
  117.5 16.3 %collective-permute-start.22 = (bf16[4,192,256]{2,1,0:T(8,128)(2,1)S(1)}, bf16[4,192,256]{2,1,0:T(8,128)(2,1)S(1)}, u32[]{:S(2)}, u32[]{:S(2)}) collective-permute-start(bf16[4,192,256]{2,1,0:T(8,128)(2,1)S(1)} %stack_columns.5.refs_0_), channel_id=1, source_target_pairs={{0,1},{1,0},{2,3},{3,2},{4,5},{5,4},{6,7},{7,6},{8,9},{9,8},{10,11... | collective-permute-start | bytes 1179656 | tf_op jit(solution)/shard_map/ppermute | solution.py:418
  117.6 16.5 %collective-permute-start.15 = (bf16[2,384,256]{2,1,0:T(8,128)(2,1)S(1)}, bf16[2,384,256]{2,1,0:T(8,128)(2,1)S(1)}, u32[]{:S(2)}, u32[]{:S(2)}) collective-permute-start(bf16[2,384,256]{2,1,0:T(8,128)(2,1)S(1)} %stack_columns.3.refs_0_), channel_id=1, source_target_pairs={{0,2},{1,3},{2,0},{3,1},{4,6},{5,7},{6,4},{7,5},{8,10},{9,11},{10,... | collective-permute-start | bytes 1179656 | tf_op jit(solution)/shard_map/ppermute | solution.py:418
  118.2 27.6 %copy-start.6 = (s32[16,4]{0,1:T(4,128)S(1)}, s32[16,4]{0,1:T(4,128)}, u32[]{:S(2)}) copy-start(s32[16,4]{0,1:T(4,128)} %param.14) | copy-start | bytes 772
  118.2 19.2 %collective-permute-start.20 = (bf16[2,384,256]{2,1,0:T(8,128)(2,1)S(1)}, bf16[2,384,256]{2,1,0:T(8,128)(2,1)S(1)}, u32[]{:S(2)}, u32[]{:S(2)}) collective-permute-start(bf16[2,384,256]{2,1,0:T(8,128)(2,1)S(1)} %stack_columns.4.refs_4_), channel_id=1, source_target_pairs={{0,2},{1,3},{2,0},{3,1},{4,6},{5,7},{6,4},{7,5},{8,10},{9,11},{10,... | collective-permute-start | bytes 1179656 | tf_op jit(solution)/shard_map/ppermute | solution.py:418
  128.1 37.5 %copy-start.7 = (s32[128,8]{0,1:T(8,128)S(1)}, s32[128,8]{0,1:T(8,128)}, u32[]{:S(2)}) copy-start(s32[128,8]{0,1:T(8,128)} %param.12) | copy-start | bytes 12292
  128.1 37.5 %copy-start.8 = (s32[128,8]{0,1:T(8,128)S(1)}, s32[128,8]{0,1:T(8,128)}, u32[]{:S(2)}) copy-start(s32[128,8]{0,1:T(8,128)} %param.13) | copy-start | bytes 12292
  128.1 13.8 %collective-permute-start.11 = (bf16[2,160,512]{2,1,0:T(8,128)(2,1)S(1)}, bf16[2,160,512]{2,1,0:T(8,128)(2,1)S(1)}, u32[]{:S(2)}, u32[]{:S(2)}) collective-permute-start(bf16[2,160,512]{2,1,0:T(8,128)(2,1)S(1)} %get-tuple-element.39), channel_id=1, source_target_pairs={{0,4},{4,0},{8,12},{12,8},{1,5},{5,1},{9,13},{13,9},{2,6},{6,2},{1... | collective-permute-start | bytes 983048 | tf_op jit(solution)/shard_map/ppermute | solution.py:418
  133.5 9.7 %collective-permute-start.24 = (bf16[4,192,256]{2,1,0:T(8,128)(2,1)S(1)}, bf16[4,192,256]{2,1,0:T(8,128)(2,1)S(1)}, u32[]{:S(2)}, u32[]{:S(2)}) collective-permute-start(bf16[4,192,256]{2,1,0:T(8,128)(2,1)S(1)} %collective-permute-done.23.refs_2_), channel_id=1, source_target_pairs={{0,1},{1,0},{2,3},{3,2},{4,5},{5,4},{6,7},{7,6},{8,9},{9,8},{10,11... | collective-permute-start | bytes 1179656 | tf_op jit(solution)/shard_map/ppermute | solution.py:418
  133.7 20.5 %collective-permute-start.14 = (bf16[2,384,256]{2,1,0:T(8,128)(2,1)S(1)}, bf16[2,384,256]{2,1,0:T(8,128)(2,1)S(1)}, u32[]{:S(2)}, u32[]{:S(2)}) collective-permute-start(bf16[2,384,256]{2,1,0:T(8,128)(2,1)S(1)} %stack_columns.3.refs_0_), channel_id=1, source_target_pairs={{0,1},{1,0},{2,3},{3,2},{4,5},{5,4},{6,7},{7,6},{8,9},{9,8},{10,11... | collective-permute-start | bytes 1179656 | tf_op jit(solution)/shard_map/ppermute | solution.py:418
  134.1 20.2 %collective-permute-start.19 = (bf16[2,384,256]{2,1,0:T(8,128)(2,1)S(1)}, bf16[2,384,256]{2,1,0:T(8,128)(2,1)S(1)}, u32[]{:S(2)}, u32[]{:S(2)}) collective-permute-start(bf16[2,384,256]{2,1,0:T(8,128)(2,1)S(1)} %stack_columns.4.refs_4_), channel_id=1, source_target_pairs={{0,1},{1,0},{2,3},{3,2},{4,5},{5,4},{6,7},{7,6},{8,9},{9,8},{10,11... | collective-permute-start | bytes 1179656 | tf_op jit(solution)/shard_map/ppermute | solution.py:418
  137.5 16.8 %collective-permute-start.16 = (bf16[2,384,256]{2,1,0:T(8,128)(2,1)S(1)}, bf16[2,384,256]{2,1,0:T(8,128)(2,1)S(1)}, u32[]{:S(2)}, u32[]{:S(2)}) collective-permute-start(bf16[2,384,256]{2,1,0:T(8,128)(2,1)S(1)} %collective-permute-done.15.refs_2_), channel_id=1, source_target_pairs={{0,1},{1,0},{2,3},{3,2},{4,5},{5,4},{6,7},{7,6},{8,9},{9,8},{10,11... | collective-permute-start | bytes 1179656 | tf_op jit(solution)/shard_map/ppermute | solution.py:418
  141.9 12.4 %collective-permute-start.21 = (bf16[2,384,256]{2,1,0:T(8,128)(2,1)S(1)}, bf16[2,384,256]{2,1,0:T(8,128)(2,1)S(1)}, u32[]{:S(2)}, u32[]{:S(2)}) collective-permute-start(bf16[2,384,256]{2,1,0:T(8,128)(2,1)S(1)} %collective-permute-done.20.refs_6_), channel_id=1, source_target_pairs={{0,1},{1,0},{2,3},{3,2},{4,5},{5,4},{6,7},{7,6},{8,9},{9,8},{10,11... | collective-permute-start | bytes 1179656 | tf_op jit(solution)/shard_map/ppermute | solution.py:418
  142.6 0.7 copy-start.4
  143.2 22.3 %collective-permute-start.12 = (bf16[1,160,512]{2,1,0:T(8,128)(2,1)}, bf16[1,160,512]{2,1,0:T(8,128)(2,1)S(1)}, u32[]{:S(2)}, u32[]{:S(2)}) collective-permute-start(bf16[1,160,512]{2,1,0:T(8,128)(2,1)} %get-tuple-element.41), channel_id=1, source_target_pairs={{0,8},{4,12},{8,0},{12,4},{1,9},{5,13},{9,1},{13,5},{2,10},{6,14},... | collective-permute-start | bytes 491528 | tf_op jit(solution)/shard_map/ppermute | solution.py:418
  154.3 2.2 %copy-start.2 = (bf16[4,1024,512]{2,1,0:T(8,128)(2,1)S(1)}, bf16[4,1024,512]{2,1,0:T(8,128)(2,1)}, u32[]{:S(2)}) copy-start(bf16[4,1024,512]{2,1,0:T(8,128)(2,1)} %all-gather.2.cloned.1.call-done.refs_8_) | copy-start | bytes 12582916
  156.5 9.0 %copy-start.5 = (bf16[1,160,512]{2,1,0:T(8,128)(2,1)S(1)}, bf16[1,160,512]{2,1,0:T(8,128)(2,1)}, u32[]{:S(2)}) copy-start(bf16[1,160,512]{2,1,0:T(8,128)(2,1)} %copy-done.4) | copy-start | bytes 491524
Sparse Core Ops, SparseCore 0:
  9.6 109.6 all-gather.1

commit v12 on v11

--- a/solution.py
+++ b/solution.py
@@ -11,7 +11,7 @@
 BF = jnp.bfloat16
 F32 = jnp.float32
 PER = 2
-GROUPS = 2
+GROUPS = 1
 
 
 def nt(a, b):
@@ -66,6 +66,9 @@
         self.cols = self.in_cols + self.down_cols
         self.folds = self.width // self.tokens
         self.tail = 2 * self.slots // self.folds
+        self.side_folds = self.width // self.part
+        self.side_rows = self.down_cols // self.side_folds
+        self.side_start = self.tokens + self.tail
 
 
 def slot_table(z, table_ref, r):
@@ -80,7 +83,9 @@
     return key == ids
 
 
-def route_kernel(z, count_ref, grad_ref, weight_ref, routes_ref, replica_ref, table_ref, out_ref):
+def route_kernel(z, ids_ref, count_ref, *refs):
+    grad_ref, weight_ref, routes_ref, replica_ref, table_ref, pair_ref = refs[:6]
+    outs, sides = refs[6:-1], refs[-1]
     weights = weight_ref[...].astype(F32)
     hits = jnp.zeros((z.slots, z.tokens), F32)
     loads = jnp.zeros((z.slots, z.tokens), F32)
@@ -99,11 +104,21 @@
     earlier = nn(hits.astype(BF), (before < after).astype(F32).astype(BF))
     code = jnp.where(hits > 0.5, earlier, -1.0)
     both = jnp.concatenate([code, loads], axis=0).astype(BF)
-    out_ref[: z.tokens, :] = grad_ref[...]
-    for b in range(z.folds):
-        out_ref[z.tokens :, b * z.tokens : (b + 1) * z.tokens] = both[
-            b * z.tail : (b + 1) * z.tail, :
-        ]
+    pair = pair_ref[...]
+    gate_pre = pair[:, : z.hidden].astype(F32)
+    up = pair[:, z.hidden :].astype(F32)
+    hidden = (gate_pre * (1.0 / (1.0 + jnp.exp(-gate_pre))) * up).astype(BF).T
+    for q in range(z.ep):
+        for f in range(z.side_folds):
+            lo = q * z.down_cols + f * z.side_rows
+            sides[q, :, f * z.part : (f + 1) * z.part] = hidden[lo : lo + z.side_rows, :]
+    for k in range(z.ep):
+        outs[k][: z.tokens, :] = grad_ref[...]
+        for b in range(z.folds):
+            outs[k][z.tokens : z.side_start, b * z.tokens : (b + 1) * z.tokens] = both[
+                b * z.tail : (b + 1) * z.tail, :
+            ]
+        outs[k][z.side_start :, :] = sides[ids_ref[0] ^ k]
 
 
 def block_place(z, block):
@@ -146,8 +161,8 @@
 def down_kernel(z, ids_ref, *refs):
     bufs = refs[: z.ep]
     weight_ref = refs[z.ep]
-    parts = refs[z.ep + 2 : z.ep + 4]
-    grads_ref, codes_ref, rows_ref, held, sems = refs[z.ep + 4 :]
+    parts = refs[z.ep + 1 : z.ep + 1 + z.sub]
+    grads_ref, codes_ref, rows_ref, held, sems = refs[z.ep + 1 + z.sub :]
     me, mine = ids_ref[0], ids_ref[1]
     step = pl.program_id(0)
 
@@ -160,7 +175,7 @@
             grads_ref[source] = bufs[k][: z.tokens, :]
             for b in range(z.folds):
                 codes_ref[source, b * z.tail : (b + 1) * z.tail, :] = bufs[k][
-                    z.tokens :, b * z.tokens : (b + 1) * z.tokens
+                    z.tokens : z.side_start, b * z.tokens : (b + 1) * z.tokens
                 ].astype(F32)
         for p in range(z.ep):
             rows = nn(local_picks(z, codes_ref, p, me), grads_ref[p]).astype(BF)
@@ -181,7 +196,7 @@
 
         @pl.when(place == k)
         def _():
-            parts[k % 2][k // 2, pl.ds(spot, z.block), :] = partial
+            parts[k][pl.ds(spot, z.block), :] = partial
 
 
 def gate_terms(z, pair, grad, scale):
@@ -197,38 +212,27 @@
 
 
 def pre_kernel(z, ids_ref, keep_ref, got_ref, pair_ref, codes_ref, *refs):
-    refs = refs[z.ep - 1 :]
-    outs, (grad_ref, sides) = refs[: z.ep], refs[z.ep :]
+    bufs = refs[: z.ep]
+    out_ref, grad_ref, down_ref = refs[z.ep :]
+
+    @pl.when(pl.program_id(0) == 0)
+    def _():
+        for k in range(z.ep):
+            for f in range(z.side_folds):
+                down_ref[k, f * z.side_rows : (f + 1) * z.side_rows, :] = bufs[k][
+                    z.side_start :, f * z.part : (f + 1) * z.part
+                ]
+
     me = ids_ref[0]
     block = ids_ref[1] * z.part_blocks + pl.program_id(0)
     slot, first = block_place(z, block)
     scale = block_scale(z, codes_ref, me * z.local + slot, first)
-    grad = keep_ref[0].astype(F32) + got_ref[0].astype(F32)
+    grad = keep_ref[...].astype(F32) + got_ref[...].astype(F32)
     grad_ref[...] = grad.astype(BF)
     _, grad_gate, grad_up = gate_terms(z, pair_ref[...], grad, scale)
-    send_columns(z, me, jnp.concatenate([grad_gate.T, grad_up.T], axis=0), sides, outs)
-
-
-def send_columns(z, me, columns, sides, outs):
-    size = columns.shape[0] // z.ep
+    pre = jnp.concatenate([grad_gate.T, grad_up.T], axis=0)
     for q in range(z.ep):
-        sides[q] = columns[q * size : (q + 1) * size, :]
-    for k in range(z.ep):
-        outs[k][...] = sides[me ^ k]
-
-
-def hidden_kernel(z, ids_ref, pair_ref, *refs):
-    refs = refs[z.ep - 1 :]
-    pair = pair_ref[...]
-    gate_pre = pair[:, : z.hidden].astype(F32)
-    up = pair[:, z.hidden :].astype(F32)
-    hidden = gate_pre * (1.0 / (1.0 + jnp.exp(-gate_pre))) * up
-    send_columns(z, ids_ref[0], hidden.astype(BF).T, refs[-1], refs[:-1])
-
-
-def stack_kernel(*refs):
-    for k, ref in enumerate(refs[:-1]):
-        refs[-1][k] = ref[...]
+        out_ref[q] = pre[q * z.in_cols : (q + 1) * z.in_cols, :]
 
 
 def row_kernel(z, ids_ref, *refs):
@@ -283,6 +287,13 @@
             out_ref[k // 2, : z.tokens, :] = tn(picks, rows).astype(BF)
             out_ref[k // 2, z.tokens :, : z.tokens] = marks[source].astype(BF)
             out_ref[k // 2, z.tokens :, z.tokens :] = blank
+
+
+def sum_kernel(*refs):
+    count = len(refs) // 3
+    for i in range(count):
+        total = refs[i][...].astype(F32) + refs[count + i][...].astype(F32)
+        refs[2 * count + i][...] = total.astype(BF)
 
 
 def halve_kernel(keep_ref, got_ref, out_keep, out_send):
@@ -361,7 +372,7 @@
 
 def total_down_kernel(z, ids_ref, table_ref, *refs):
     sides = refs[: z.sub]
-    grads_ref, codes_ref, _, out_ref, token_ref, held, made, out_sems, scaled, sems = refs[z.sub :]
+    grads_ref, codes_ref, out_ref, token_ref, held, made, out_sems, scaled, sems = refs[z.sub :]
     token_ref[...] = jnp.zeros_like(token_ref)
 
     def moves(act):
@@ -411,7 +422,7 @@
         start = pl.multiple_of(block * z.block, z.block)
         return inputs_ref[slot_id // z.local, pl.ds(start, z.block), :]
 
-    expert_products(z, ids_ref, table_ref, ids_ref[0], held, right_rows, out_ref, made, out_sems)
+    expert_products(z, ids_ref, table_ref, 0, held, right_rows, out_ref, made, out_sems)
 
 
 def swap(x, axis, size, bit):
@@ -463,52 +474,28 @@
     routes, replica, table = routes.T, replica.T, replica_slot.T
     route_weight = route_weight.T
     pair_rows = saved_gate_up.reshape(z.all_rows, z.pair)
-    grad_shape = (z.tokens + z.tail, z.width)
+    grad_shape = (z.side_start + z.side_rows, z.width)
     code_shape = (n, 2 * z.slots, z.tokens)
     inputs = saved_input.reshape(z.all_rows, z.width)
 
     routing = (grad_out, route_weight, routes, replica, table)
-    buf = pl.pallas_call(
+    gathered = lax.all_gather(inputs, "ep")
+    bufs = pl.pallas_call(
         functools.partial(route_kernel, z),
-        out_shape=jax.ShapeDtypeStruct(grad_shape, BF),
-        in_specs=[smem()] + [whole(a.shape) for a in routing],
-        out_specs=whole(grad_shape),
-        grid=(1,),
+        grid_spec=pltpu.PrefetchScalarGridSpec(
+            num_scalar_prefetch=1,
+            grid=(1,),
+            in_specs=[smem()]
+            + [whole(a.shape) for a in routing]
+            + [pl.BlockSpec((z.part, z.pair), lambda i, r: (r[1], 0))],
+            out_specs=[whole(grad_shape)] * n,
+            scratch_shapes=[pltpu.VMEM((n, z.side_rows, z.width), BF)],
+        ),
+        out_shape=[jax.ShapeDtypeStruct(grad_shape, BF)] * n,
         compiler_params=params(60),
         name="route",
-    )(token_count, *routing)
-    bufs = [buf] + [swap(buf, "ep", n, k) for k in range(1, n)]
-
-    gathered = lax.all_gather(inputs, "ep")
-    downs = pl.pallas_call(
-        functools.partial(hidden_kernel, z),
-        grid_spec=pltpu.PrefetchScalarGridSpec(
-            num_scalar_prefetch=1,
-            grid=(z.part_blocks,),
-            in_specs=[
-                pl.BlockSpec((z.block, z.pair), lambda i, r: (r[1] * z.part_blocks + i, 0))
-            ]
-            + [pl.BlockSpec(memory_space=pl.ANY)] * (n - 1),
-            out_specs=[pl.BlockSpec((z.down_cols, z.block), lambda i, r: (0, i))] * n,
-            scratch_shapes=[pltpu.VMEM((n, z.down_cols, z.block), BF)],
-        ),
-        out_shape=[jax.ShapeDtypeStruct((z.down_cols, z.part), BF)] * n,
-        compiler_params=params(16),
-        name="hidden_columns",
-    )(ids, pair_rows, *bufs[1:])
-    downs = [downs[0]] + [swap(downs[k], "ep", n, k) for k in range(1, n)]
-
-    def stack(pieces):
-        shape, count = pieces[0].shape, len(pieces)
-        return pl.pallas_call(
-            stack_kernel,
-            in_specs=[whole(shape)] * count,
-            out_specs=whole((count,) + shape),
-            out_shape=jax.ShapeDtypeStruct((count,) + shape, BF),
-            grid=(1,),
-            compiler_params=params(12),
-            name="stack_columns",
-        )(*pieces)
+    )(ids, token_count, *routing, pair_rows)
+    bufs = [bufs[0]] + [swap(bufs[k], "ep", n, k) for k in range(1, n)]
 
     def halve(keep, got):
         half = (keep.shape[0] // 2,) + keep.shape[1:]
@@ -526,15 +513,14 @@
         place = i // z.part_blocks
         return (place ^ ids_ref[1]) * z.part_blocks + i % z.part_blocks
 
-    part_shape = (m // 2, z.part, z.hidden)
+    part_shape = (z.part, z.hidden)
     outs = pl.pallas_call(
         functools.partial(down_kernel, z),
         grid_spec=pltpu.PrefetchScalarGridSpec(
             num_scalar_prefetch=1,
             grid=(z.blocks,),
-            in_specs=[whole(grad_shape)] * n
-            + [pl.BlockSpec(memory_space=pltpu.HBM), pl.BlockSpec(memory_space=pl.ANY)],
-            out_specs=[whole(part_shape)] * 2
+            in_specs=[whole(grad_shape)] * n + [pl.BlockSpec(memory_space=pltpu.HBM)],
+            out_specs=[whole(part_shape)] * m
             + [whole((n, z.tokens, z.width)), whole(code_shape)],
             scratch_shapes=[
                 pltpu.VMEM((z.local, z.rows, z.width), BF),
@@ -542,23 +528,60 @@
                 pltpu.SemaphoreType.DMA((z.local,)),
             ],
         ),
-        out_shape=[jax.ShapeDtypeStruct(part_shape, BF)] * 2
+        out_shape=[jax.ShapeDtypeStruct(part_shape, BF)] * m
         + [
             jax.ShapeDtypeStruct((n, z.tokens, z.width), BF),
             jax.ShapeDtypeStruct(code_shape, F32),
         ],
         compiler_params=params(48),
         name="hidden_partials",
-    )(ids, *bufs, weight_down, downs[0])
-    keep, send, grads_all, codes = outs
-    got = swap(send, "sub", m, 1)
-    bit = 2
-    while bit < m:
-        keep, send = halve(keep, got)
-        got = swap(send, "sub", m, bit)
+    )(ids, *bufs, weight_down)
+    parts, (grads_all, codes) = outs[:m], outs[m:]
+    bit = 1
+    while True:
+        keep = parts[::2]
+        got = [swap(part, "sub", m, bit) for part in parts[1::2]]
         bit *= 2
-    down_sides = spread_over({0: stack(downs)}, "sub", m, m // 2)
-    def total_call(kernel, operands, specs, cols, scratch, name):
+        if bit == m:
+            break
+        count = len(keep)
+        parts = pl.pallas_call(
+            sum_kernel,
+            in_specs=[whole(part_shape)] * 2 * count,
+            out_specs=[whole(part_shape)] * count,
+            out_shape=[jax.ShapeDtypeStruct(part_shape, BF)] * count,
+            grid=(1,),
+            compiler_params=params(16),
+            name="sum_parts",
+        )(*keep, *got)
+    pre, grad_part, down_columns = pl.pallas_call(
+        functools.partial(pre_kernel, z),
+        grid_spec=pltpu.PrefetchScalarGridSpec(
+            num_scalar_prefetch=1,
+            grid=(z.part_blocks,),
+            in_specs=[pl.BlockSpec((z.block, z.hidden), lambda i, r: (i, 0))] * 2
+            + [
+                pl.BlockSpec((z.block, z.pair), lambda i, r: (r[1] * z.part_blocks + i, 0)),
+                whole(code_shape),
+            ]
+            + [whole(grad_shape)] * n,
+            out_specs=[
+                pl.BlockSpec((n, z.in_cols, z.block), lambda i, r: (0, 0, i)),
+                pl.BlockSpec((z.block, z.hidden), lambda i, r: (i, 0)),
+                whole((n, z.down_cols, z.part)),
+            ],
+        ),
+        out_shape=[
+            jax.ShapeDtypeStruct((n, z.in_cols, z.part), BF),
+            jax.ShapeDtypeStruct((z.part, z.hidden), BF),
+            jax.ShapeDtypeStruct((n, z.down_cols, z.part), BF),
+        ],
+        compiler_params=params(16),
+        name="pre_grads",
+    )(ids, keep[0], got[0], pair_rows, codes, *bufs)
+    columns = lax.all_to_all(pre, "ep", split_axis=0, concat_axis=0, tiled=True)
+    down_sides = spread_over({0: down_columns}, "sub", m, m // 2)
+    def total_call(kernel, operands, specs, cols, scratch, mib, name):
         return pl.pallas_call(
             functools.partial(kernel, z),
             grid_spec=pltpu.PrefetchScalarGridSpec(
@@ -577,40 +600,20 @@
                 jax.ShapeDtypeStruct((z.experts, cols, z.width), BF),
                 jax.ShapeDtypeStruct((8, 128), F32),
             ],
-            compiler_params=params(32),
+            compiler_params=params(mib),
             name=name,
         )(ids, table, *operands)
 
     anywhere = pl.BlockSpec(memory_space=pl.ANY)
     grad_down, down_made = total_call(
         total_down_kernel,
-        [*down_sides, grads_all, codes, send],
-        [anywhere] * m + [whole((n, z.tokens, z.width)), whole(code_shape), anywhere],
+        [*down_sides, grads_all, codes],
+        [anywhere] * m + [whole((n, z.tokens, z.width)), whole(code_shape)],
         z.down_cols,
         [pltpu.VMEM((z.slots, z.rows, z.width), BF), pltpu.SemaphoreType.DMA((m,))],
+        32,
         "down_grads",
     )
-    *pieces, grad_part = pl.pallas_call(
-        functools.partial(pre_kernel, z),
-        grid_spec=pltpu.PrefetchScalarGridSpec(
-            num_scalar_prefetch=1,
-            grid=(z.part_blocks,),
-            in_specs=[pl.BlockSpec((1, z.block, z.hidden), lambda i, r: (0, i, 0))] * 2
-            + [
-                pl.BlockSpec((z.block, z.pair), lambda i, r: (r[1] * z.part_blocks + i, 0)),
-                whole(code_shape),
-            ]
-            + [pl.BlockSpec(memory_space=pl.ANY)] * (n - 1),
-            out_specs=[pl.BlockSpec((z.in_cols, z.block), lambda i, r: (0, i))] * n
-            + [pl.BlockSpec((z.block, z.hidden), lambda i, r: (i, 0))],
-            scratch_shapes=[pltpu.VMEM((n, z.in_cols, z.block), BF)],
-        ),
-        out_shape=[jax.ShapeDtypeStruct((z.in_cols, z.part), BF)] * n
-        + [jax.ShapeDtypeStruct((z.part, z.hidden), BF)],
-        compiler_params=params(16),
-        name="pre_grads",
-    )(ids, keep, got, pair_rows, codes, *downs[1:])
-    pieces = [pieces[0]] + [swap(pieces[k], "ep", n, k) for k in range(1, n)]
     grad_parts = spread_over({0: grad_part}, "sub", m, m // 2)
 
     back_shape = (n // 2, z.tokens + z.slots, z.width)
@@ -639,10 +642,9 @@
         name="row_grads",
     )(ids, *grad_parts, pair_rows, weight_in, codes)
     got = swap(send, "ep", n, 1)
-    sides = []
-    for g in range(0, n, n // GROUPS):
-        stacked = stack(pieces[g : g + n // GROUPS])
-        sides += spread_over({0: stacked}, "sub", m, m // 2)
+    sides = [columns, swap(columns, "sub", m, m // 2)]
+    sides = gate(sides, [gathered, keep, down_made])
+    sides = spread_over({0: sides[0], m // 2: sides[1]}, "sub", m, m // 4)
     bit = 2
     while bit < n:
         keep, send = halve(keep, got)
@@ -652,13 +654,14 @@
     grad_in, in_made = total_call(
         total_in_kernel,
         [*sides, gathered],
-        [anywhere] * (GROUPS * m + 1),
+        [anywhere] * (GROUPS * m) + [pl.BlockSpec(memory_space=pltpu.HBM)],
         z.in_cols,
         [
             pltpu.VMEM((n, z.all_rows, z.width), BF),
             pltpu.SemaphoreType.DMA((GROUPS * m,)),
             pltpu.SemaphoreType.DMA((n,)),
         ],
+        44,
         "in_grads",
     )
     got = gate([got], [in_made])[0]

time: 174 us -> 179 us (1.029)
  waiting for transfers between devices: 62.6 us -> 81.3 us
  starting transfers between devices: 52.5 us -> 38.1 us
    ppermute x25 -> x17, starting transfers between devices: 52.4 us -> 15.2 us  [swap(): return lax.ppermute(x, axis, [(i, i ^ bit) for i in range(size)])]
    all_to_all x0 -> x1, waiting for transfers between devices: none -> 29.9 us  [body(): columns = lax.all_to_all(pre, 'ep', split_axis=0, concat_axis=0, tiled=True)]
    all_to_all x0 -> x1, starting transfers between devices: none -> 22.9 us  [body(): columns = lax.all_to_all(pre, 'ep', split_axis=0, concat_axis=0, tiled=True)]
    ppermute x25 -> x17, waiting for transfers between devices: 61.9 us -> 50.6 us  [swap(): return lax.ppermute(x, axis, [(i, i ^ bit) for i in range(size)])]
    unnamed x18 -> x34, local copies, waits for them, and re-layouts: 5.66 us -> 6.55 us
  transfers between devices with their start and end apart: 26 -> 19, of which waited for: 11 -> 11; matrix products, arithmetic and copies ran while one was open for 0% -> 0% of each run, Pallas kernels for 21% -> 20%
where the time goes in v12:
time: 179 us
  waiting for transfers between devices  81.3 us (45%)
  starting transfers between devices  38.1 us (21%)
  Pallas kernels  37.3 us (21%)
  between operations  15 us (8%)
  local copies, waits for them, and re-layouts  6.55 us (4%)
    ppermute x17, waiting for transfers between devices, swap(): return lax.ppermute(x, axis, [(i, i ^ bit) for i in range(size)])  50.6 us
    all_to_all x1, waiting for transfers between devices, body(): columns = lax.all_to_all(pre, 'ep', split_axis=0, concat_axis=0, tiled=True)  29.9 us
    all_to_all x1, starting transfers between devices, body(): columns = lax.all_to_all(pre, 'ep', split_axis=0, concat_axis=0, tiled=True)  22.9 us
    pallas_call x2, Pallas kernels, total_call(): pl.pallas_call(functools.partial(kernel, z), grid_spec=pltpu.PrefetchScal...  15.8 us
    ppermute x17, starting transfers between devices, swap(): return lax.ppermute(x, axis, [(i, i ^ bit) for i in range(size)])  15.2 us
    pallas_call x1, Pallas kernels, body(): pl.pallas_call(functools.partial(row_kernel, z), grid_spec=pltpu.Prefetch...  9.27 us
    unnamed x34, local copies, waits for them, and re-layouts  6.55 us
    pallas_call x1, Pallas kernels, body(): pl.pallas_call(functools.partial(down_kernel, z), grid_spec=pltpu.Prefetc...  5.48 us
  transfers between devices with their start and end apart: 19, of which 11 were waited for; matrix products, arithmetic and copies ran while one was open for 0% of the time, Pallas kernels for 20%

profile of v12, /device:TPU:0, one launch (start us, length us, event | category | flops | bytes accessed | tf_op | source)
XLA Modules:
  0.0 178.8 jit_solution(13066916441504168282)
XLA Ops:
  7.2 0.0 all-gather.2.cloned.1.call-start
  7.2 0.7 all-gather.2.cloned.1.call-update
  7.9 0.0 copy-start
  8.7 0.6 pad_add_fusion.ids_ref
  9.3 3.3 %route.1 = (bf16[240,512]{1,0:T(8,128)(2,1)}, bf16[240,512]{1,0:T(8,128)(2,1)}, bf16[240,512]{1,0:T(8,128)(2,1)}, bf16[240,512]{1,0:T(8,128)(2,1)}) custom-call(s32[2]{0:T(128)} %pad_add_fusion.ids_ref, s32[1]{0:T(128)S(6)} %copy.20.count_ref, bf16[128,512]{1,0:T(8,128)(2,1)} %refs_0_.1, bf16[8,128]{1,0:T(8,128)(2,1)} %bitcast.21, s32[8,128]{1,0:T(8,128)} %bitcast.16, ...), custom_call_target="tpu_custom_call" | custom-call | tf_op jit(solution)/shard_map/route/pallas_call | solution.py:483
  12.6 3.0 %collective-permute-start = (bf16[240,512]{1,0:T(8,128)(2,1)}, bf16[240,512]{1,0:T(8,128)(2,1)S(1)}, u32[]{:S(2)}, u32[]{:S(2)}) collective-permute-start(bf16[240,512]{1,0:T(8,128)(2,1)} %get-tuple-element.32), channel_id=1, source_target_pairs={{0,4},{4,0},{8,12},{12,8},{1,5},{5,1},{9,13},{13,9},{2,6},{6,2},{1... | collective-permute-start | bytes 737288 | tf_op jit(solution)/shard_map/ppermute | solution.py:429
  15.6 2.6 %collective-permute-start.1 = (bf16[240,512]{1,0:T(8,128)(2,1)}, bf16[240,512]{1,0:T(8,128)(2,1)S(1)}, u32[]{:S(2)}, u32[]{:S(2)}) collective-permute-start(bf16[240,512]{1,0:T(8,128)(2,1)} %get-tuple-element.33), channel_id=1, source_target_pairs={{0,8},{4,12},{8,0},{12,4},{1,9},{5,13},{9,1},{13,5},{2,10},{6,14},... | collective-permute-start | bytes 737288 | tf_op jit(solution)/shard_map/ppermute | solution.py:429
  18.2 11.3 %collective-permute-done.refs_1_ = bf16[240,512]{1,0:T(8,128)(2,1)S(1)} collective-permute-done((bf16[240,512]{1,0:T(8,128)(2,1)}, bf16[240,512]{1,0:T(8,128)(2,1)S(1)}, u32[]{:S(2)}, u32[]{:S(2)}) %collective-permute-start) | collective-permute-done | bytes 245792 | tf_op jit(solution)/shard_map/ppermute | solution.py:429
  29.5 13.2 %collective-permute-done.1.refs_2_ = bf16[240,512]{1,0:T(8,128)(2,1)S(1)} collective-permute-done((bf16[240,512]{1,0:T(8,128)(2,1)}, bf16[240,512]{1,0:T(8,128)(2,1)S(1)}, u32[]{:S(2)}, u32[]{:S(2)}) %collective-permute-start.1) | collective-permute-done | bytes 245792 | tf_op jit(solution)/shard_map/ppermute | solution.py:429
  42.7 2.3 %collective-permute-done.2.refs_3_ = bf16[240,512]{1,0:T(8,128)(2,1)S(1)} collective-permute-done((bf16[240,512]{1,0:T(8,128)(2,1)}, bf16[240,512]{1,0:T(8,128)(2,1)S(1)}, u32[]{:S(2)}, u32[]{:S(2)}) %collective-permute-start.2) | collective-permute-done | bytes 245792 | tf_op jit(solution)/shard_map/ppermute | solution.py:429
  45.0 0.9 copy-done.5
  45.9 0.6 copy-done.12
  46.5 5.5 %hidden_partials.1 = (bf16[256,768]{1,0:T(8,128)(2,1)S(1)}, bf16[256,768]{1,0:T(8,128)(2,1)S(1)}, bf16[256,768]{1,0:T(8,128)(2,1)S(1)}, bf16[256,768]{1,0:T(8,12...) custom-call(s32[2]{0:T(128)S(1)} %copy-done.12, bf16[240,512]{1,0:T(8,128)(2,1)S(1)} %copy-done.5, ...), custom_call_target="tpu_custom_call" | custom-call | tf_op jit(solution)/shard_map/hidden_partials/pallas_call | solution.py:517
  52.0 0.0 copy-start.3
  52.0 0.0 copy-start.7
  52.0 0.1 collective-permute-start.3
  52.1 0.5 collective-permute-start.4
  52.6 1.2 collective-permute-done.3.refs_2_
  53.8 0.6 collective-permute-done.4.refs_3_
  54.4 0.2 sum_parts.1
  54.6 2.5 %collective-permute-start.5 = (bf16[256,768]{1,0:T(8,128)(2,1)S(1)}, bf16[256,768]{1,0:T(8,128)(2,1)S(1)}, u32[]{:S(2)}, u32[]{:S(2)}) collective-permute-start(bf16[256,768]{1,0:T(8,128)(2,1)S(1)} %get-tuple-element.40), channel_id=1, source_target_pairs={{0,2},{1,3},{2,0},{3,1},{4,6},{5,7},{6,4},{7,5},{8,10},{9,11},{10,... | collective-permute-start | bytes 1179656 | tf_op jit(solution)/shard_map/ppermute | solution.py:429
  57.1 9.4 %collective-permute-done.5.got_ref = bf16[256,768]{1,0:T(8,128)(2,1)S(1)} collective-permute-done((bf16[256,768]{1,0:T(8,128)(2,1)S(1)}, bf16[256,768]{1,0:T(8,128)(2,1)S(1)}, u32[]{:S(2)}, u32[]{:S(2)}) %collective-permute-start.5) | collective-permute-done | bytes 393248 | tf_op jit(solution)/shard_map/ppermute | solution.py:429
  66.5 2.3 %pre_grads.1 = (bf16[4,384,256]{2,1,0:T(8,128)(2,1)S(1)}, bf16[256,768]{1,0:T(8,128)(2,1)S(1)}, bf16[4,192,256]{2,1,0:T(8,128)(2,1)}) custom-call(s32[2]{0:T(128)S(1)} %copy-done.12, bf16[256,768]{1,0:T(8,128)(2,1)S(1)} %get-tuple-element.39.keep_ref, bf16[256,768]{1,0:T(8,128)(2,1)S(1)} %collective-permute-done.5.got_ref, bf16[1024,1536]{1,0:T(8,128)(2,1)S(1)} %bitcast.10, ...), custom_call_target="tpu_custom_call" | custom-call | tf_op jit(solution)/shard_map/pre_grads/pallas_call | solution.py:557
  68.8 0.9 copy-done.6
  69.7 22.9 %all-to-all-start = ((bf16[4,384,256]{2,1,0:T(8,128)(2,1)}), bf16[4,384,256]{2,1,0:T(8,128)(2,1)}, u32[]{:S(2)}, u32[]{:S(2)}) async-start(bf16[4,384,256]{2,1,0:T(8,128)(2,1)} %copy-done.6), calls=%async_computation | async-start | bytes 1572864 | tf_op jit(solution)/shard_map/all_to_all | solution.py:582
  92.6 1.7 collective-permute-start.7
  94.3 0.3 collective-permute-start.13
  94.6 29.9 %all-to-all-done.refs_0_ = bf16[4,384,256]{2,1,0:T(8,128)(2,1)} async-done(((bf16[4,384,256]{2,1,0:T(8,128)(2,1)}), bf16[4,384,256]{2,1,0:T(8,128)(2,1)}, u32[]{:S(2)}, u32[]{:S(2)}) %all-to-all-start) | async-done | bytes 786464 | tf_op jit(solution)/shard_map/all_to_all | solution.py:582
  124.6 1.5 collective-permute-start.11
  126.1 0.5 collective-permute-start.8
  126.6 0.0 collective-permute-start.12
  126.6 0.5 collective-permute-start.14
  127.1 1.2 collective-permute-done.6.refs_1_
  128.3 0.3 collective-permute-done.8.refs_3_
  128.5 0.9 copy-done.4
  129.5 1.0 copy-done.10
  130.4 9.3 %row_grads.1 = (bf16[2,160,512]{2,1,0:T(8,128)(2,1)S(1)}, bf16[2,160,512]{2,1,0:T(8,128)(2,1)S(1)}) custom-call(s32[2]{0:T(128)S(1)} %copy-done.13, bf16[256,768]{1,0:T(8,128)(2,1)S(1)} %copy-done.10, bf16[256,768]{1,0:T(8,128)(2,1)S(1)} %collective-permute-done.6.refs_1_, bf16[256,768]{1,0:T(8,128)(2,1)} %collective-permute-done.7.refs_2_, ...), custom_call_target="tpu_custom_call" | custom-call | tf_op jit(solution)/shard_map/row_grads/pallas_call | solution.py:620
  139.8 7.4 %down_grads.1 = (bf16[16,192,512]{2,1,0:T(8,128)(2,1)}, f32[8,128]{1,0:T(8,128)S(1)}) custom-call(s32[2]{0:T(128)S(1)} %copy-done.13, s32[4,16]{1,0:T(4,128)S(1)} %bitcast.13, bf16[4,192,256]{2,1,0:T(8,128)(2,1)} %get-tuple-element.48.refs_0_, bf16[4,192,256]{2,1,0:T(8,128)(2,1)S(1)} %collective-permute-done.12.refs_1_, ...), custom_call_target="tpu_custom_call" | custom-call | tf_op jit(solution)/shard_map/down_grads/pallas_call | solution.py:585
  147.3 0.0 all-gather.2.cloned.1.call-done.refs_2_.refs_4_
  147.3 2.2 %copy-done.1 = bf16[4,1024,512]{2,1,0:T(8,128)(2,1)S(1)} copy-done((bf16[4,1024,512]{2,1,0:T(8,128)(2,1)S(1)}, bf16[4,1024,512]{2,1,0:T(8,128)(2,1)}, u32[]{:S(2)}) %copy-start.1) | copy-done | bytes 4194328
  149.5 1.1 collective-permute-start.15
  150.6 0.1 collective-permute-start.16
  150.6 10.3 %collective-permute-done.9.got_ref = bf16[2,160,512]{2,1,0:T(8,128)(2,1)S(1)} collective-permute-done((bf16[2,160,512]{2,1,0:T(8,128)(2,1)}, bf16[2,160,512]{2,1,0:T(8,128)(2,1)S(1)}, u32[]{:S(2)}, u32[]{:S(2)}) %collective-permute-start.9) | collective-permute-done | bytes 327712 | tf_op jit(solution)/shard_map/ppermute | solution.py:429
  160.9 0.1 halve.1
  161.0 0.8 collective-permute-start.10
  161.8 8.4 %in_grads.1 = (bf16[16,384,512]{2,1,0:T(8,128)(2,1)}, f32[8,128]{1,0:T(8,128)S(1)}) custom-call(s32[2]{0:T(128)S(1)} %copy-done.13, s32[4,16]{1,0:T(4,128)S(1)} %bitcast.14, bf16[4,384,256]{2,1,0:T(8,128)(2,1)} %get-tuple-element.51.refs_0_, bf16[4,384,256]{2,1,0:T(8,128)(2,1)S(1)} %collective-permute-done.15.refs_1_, ...), custom_call_target="tpu_custom_call" | custom-call | tf_op jit(solution)/shard_map/in_grads/pallas_call | solution.py:585
  170.2 1.0 collective-permute-done.10.refs_0_
  171.1 0.8 token_grads.1
  (37 shorter events, 0.1 us)
Async XLA Ops:
  7.2 140.1 %all-gather.2.cloned.1.call-start = ((), (), s32[]{:S(2)}) async-start(), calls=%async_computation.1 | async-start | bytes 5242880 | tf_op jit(solution)/shard_map/all_gather | solution.py:482
  7.9 58.6 %copy-start = (bf16[8,128,1536]{2,1,0:T(8,128)(2,1)S(1)}, bf16[8,128,1536]{2,1,0:T(8,128)(2,1)}, u32[]{:S(2)}) copy-start(bf16[8,128,1536]{2,1,0:T(8,128)(2,1)} %param.17) | copy-start | bytes 9437188
  12.6 16.9 %collective-permute-start = (bf16[240,512]{1,0:T(8,128)(2,1)}, bf16[240,512]{1,0:T(8,128)(2,1)S(1)}, u32[]{:S(2)}, u32[]{:S(2)}) collective-permute-start(bf16[240,512]{1,0:T(8,128)(2,1)} %get-tuple-element.32), channel_id=1, source_target_pairs={{0,4},{4,0},{8,12},{12,8},{1,5},{5,1},{9,13},{13,9},{2,6},{6,2},{1... | collective-permute-start | bytes 737288 | tf_op jit(solution)/shard_map/ppermute | solution.py:429
  15.6 27.0 %collective-permute-start.1 = (bf16[240,512]{1,0:T(8,128)(2,1)}, bf16[240,512]{1,0:T(8,128)(2,1)S(1)}, u32[]{:S(2)}, u32[]{:S(2)}) collective-permute-start(bf16[240,512]{1,0:T(8,128)(2,1)} %get-tuple-element.33), channel_id=1, source_target_pairs={{0,8},{4,12},{8,0},{12,4},{1,9},{5,13},{9,1},{13,5},{2,10},{6,14},... | collective-permute-start | bytes 737288 | tf_op jit(solution)/shard_map/ppermute | solution.py:429
  18.2 26.8 %collective-permute-start.2 = (bf16[240,512]{1,0:T(8,128)(2,1)}, bf16[240,512]{1,0:T(8,128)(2,1)S(1)}, u32[]{:S(2)}, u32[]{:S(2)}) collective-permute-start(bf16[240,512]{1,0:T(8,128)(2,1)} %get-tuple-element.34), channel_id=1, source_target_pairs={{0,12},{4,8},{8,4},{12,0},{1,13},{5,9},{9,5},{13,1},{2,14},{6,10},... | collective-permute-start | bytes 737288 | tf_op jit(solution)/shard_map/ppermute | solution.py:429
  45.0 0.9 copy-start.5
  45.9 0.6 copy-start.12
  46.5 82.0 %copy-start.13 = (s32[2]{0:T(128)S(1)}, s32[2]{0:T(128)}, u32[]{:S(2)}) copy-start(s32[2]{0:T(128)} %pad_add_fusion.ids_ref) | copy-start | bytes 28
  52.0 14.5 %copy-start.3 = (f32[4,64,128]{2,1,0:T(8,128)}, f32[4,64,128]{2,1,0:T(8,128)S(1)}, u32[]{:S(2)}) copy-start(f32[4,64,128]{2,1,0:T(8,128)S(1)} %get-tuple-element.41.codes_ref.refs_6_.refs_5_) | copy-start | bytes 393220
  52.0 16.8 %copy-start.7 = (bf16[4,128,512]{2,1,0:T(8,128)(2,1)}, bf16[4,128,512]{2,1,0:T(8,128)(2,1)S(1)}, u32[]{:S(2)}) copy-start(bf16[4,128,512]{2,1,0:T(8,128)(2,1)S(1)} %get-tuple-element.49.refs_4_) | copy-start | bytes 1572868
  52.0 1.8 %collective-permute-start.3 = (bf16[256,768]{1,0:T(8,128)(2,1)S(1)}, bf16[256,768]{1,0:T(8,128)(2,1)S(1)}, u32[]{:S(2)}, u32[]{:S(2)}) collective-permute-start(bf16[256,768]{1,0:T(8,128)(2,1)S(1)} %get-tuple-element.37), channel_id=1, source_target_pairs={{0,1},{1,0},{2,3},{3,2},{4,5},{5,4},{6,7},{7,6},{8,9},{9,8},{10,11... | collective-permute-start | bytes 1179656 | tf_op jit(solution)/shard_map/ppermute | solution.py:429
  52.1 2.3 %collective-permute-start.4 = (bf16[256,768]{1,0:T(8,128)(2,1)S(1)}, bf16[256,768]{1,0:T(8,128)(2,1)S(1)}, u32[]{:S(2)}, u32[]{:S(2)}) collective-permute-start(bf16[256,768]{1,0:T(8,128)(2,1)S(1)} %get-tuple-element.38), channel_id=1, source_target_pairs={{0,1},{1,0},{2,3},{3,2},{4,5},{5,4},{6,7},{7,6},{8,9},{9,8},{10,11... | collective-permute-start | bytes 1179656 | tf_op jit(solution)/shard_map/ppermute | solution.py:429
  54.6 11.9 %collective-permute-start.5 = (bf16[256,768]{1,0:T(8,128)(2,1)S(1)}, bf16[256,768]{1,0:T(8,128)(2,1)S(1)}, u32[]{:S(2)}, u32[]{:S(2)}) collective-permute-start(bf16[256,768]{1,0:T(8,128)(2,1)S(1)} %get-tuple-element.40), channel_id=1, source_target_pairs={{0,2},{1,3},{2,0},{3,1},{4,6},{5,7},{6,4},{7,5},{8,10},{9,11},{10,... | collective-permute-start | bytes 1179656 | tf_op jit(solution)/shard_map/ppermute | solution.py:429
  68.8 0.9 copy-start.6
  69.7 58.5 %copy-start.9 = (bf16[256,768]{1,0:T(8,128)(2,1)}, bf16[256,768]{1,0:T(8,128)(2,1)S(1)}, u32[]{:S(2)}) copy-start(bf16[256,768]{1,0:T(8,128)(2,1)S(1)} %get-tuple-element.42.refs_0_) | copy-start | bytes 1179652
  69.7 54.8 %all-to-all-start = ((bf16[4,384,256]{2,1,0:T(8,128)(2,1)}), bf16[4,384,256]{2,1,0:T(8,128)(2,1)}, u32[]{:S(2)}, u32[]{:S(2)}) async-start(bf16[4,384,256]{2,1,0:T(8,128)(2,1)} %copy-done.6), calls=%async_computation | async-start | bytes 1572864 | tf_op jit(solution)/shard_map/all_to_all | solution.py:582
  92.6 47.2 %copy-start.11 = (s32[16,4]{0,1:T(4,128)S(1)}, s32[16,4]{0,1:T(4,128)}, u32[]{:S(2)}) copy-start(s32[16,4]{0,1:T(4,128)} %param.14) | copy-start | bytes 772
  92.6 33.5 %collective-permute-start.7 = (bf16[256,768]{1,0:T(8,128)(2,1)S(1)}, bf16[256,768]{1,0:T(8,128)(2,1)}, u32[]{:S(2)}, u32[]{:S(2)}) collective-permute-start(bf16[256,768]{1,0:T(8,128)(2,1)S(1)} %get-tuple-element.42.refs_0_), channel_id=1, source_target_pairs={{0,2},{1,3},{2,0},{3,1},{4,6},{5,7},{6,4},{7,5},{8,10},{9,11},{10,... | collective-permute-start | bytes 1179656 | tf_op jit(solution)/shard_map/ppermute | solution.py:429
  94.3 32.2 %collective-permute-start.13 = (bf16[4,192,256]{2,1,0:T(8,128)(2,1)}, bf16[4,192,256]{2,1,0:T(8,128)(2,1)}, u32[]{:S(2)}, u32[]{:S(2)}) collective-permute-start(bf16[4,192,256]{2,1,0:T(8,128)(2,1)} %get-tuple-element.48.refs_0_), channel_id=1, source_target_pairs={{0,2},{1,3},{2,0},{3,1},{4,6},{5,7},{6,4},{7,5},{8,10},{9,11},{10,... | collective-permute-start | bytes 1179656 | tf_op jit(solution)/shard_map/ppermute | solution.py:429
  124.6 22.7 %collective-permute-start.11 = (bf16[4,384,256]{2,1,0:T(8,128)(2,1)}, bf16[4,384,256]{2,1,0:T(8,128)(2,1)}, u32[]{:S(2)}, u32[]{:S(2)}) collective-permute-start(bf16[4,384,256]{2,1,0:T(8,128)(2,1)} %all-to-all-done.refs_0_), channel_id=1, source_target_pairs={{0,2},{1,3},{2,0},{3,1},{4,6},{5,7},{6,4},{7,5},{8,10},{9,11},{10,... | collective-permute-start | bytes 2359304 | tf_op jit(solution)/shard_map/ppermute | solution.py:429
  126.0 2.2 %collective-permute-start.6 = (bf16[256,768]{1,0:T(8,128)(2,1)S(1)}, bf16[256,768]{1,0:T(8,128)(2,1)S(1)}, u32[]{:S(2)}, u32[]{:S(2)}) collective-permute-start(bf16[256,768]{1,0:T(8,128)(2,1)S(1)} %get-tuple-element.42.refs_0_), channel_id=1, source_target_pairs={{0,1},{1,0},{2,3},{3,2},{4,5},{5,4},{6,7},{7,6},{8,9},{9,8},{10,11... | collective-permute-start | bytes 1179656 | tf_op jit(solution)/shard_map/ppermute | solution.py:429
  126.1 2.5 %collective-permute-start.8 = (bf16[256,768]{1,0:T(8,128)(2,1)}, bf16[256,768]{1,0:T(8,128)(2,1)S(1)}, u32[]{:S(2)}, u32[]{:S(2)}) collective-permute-start(bf16[256,768]{1,0:T(8,128)(2,1)} %collective-permute-done.7.refs_2_), channel_id=1, source_target_pairs={{0,1},{1,0},{2,3},{3,2},{4,5},{5,4},{6,7},{7,6},{8,9},{9,8},{10,11... | collective-permute-start | bytes 1179656 | tf_op jit(solution)/shard_map/ppermute | solution.py:429
  126.6 13.2 %collective-permute-start.12 = (bf16[4,192,256]{2,1,0:T(8,128)(2,1)}, bf16[4,192,256]{2,1,0:T(8,128)(2,1)S(1)}, u32[]{:S(2)}, u32[]{:S(2)}) collective-permute-start(bf16[4,192,256]{2,1,0:T(8,128)(2,1)} %get-tuple-element.48.refs_0_), channel_id=1, source_target_pairs={{0,1},{1,0},{2,3},{3,2},{4,5},{5,4},{6,7},{7,6},{8,9},{9,8},{10,11... | collective-permute-start | bytes 1179656 | tf_op jit(solution)/shard_map/ppermute | solution.py:429
  126.6 13.2 %collective-permute-start.14 = (bf16[4,192,256]{2,1,0:T(8,128)(2,1)}, bf16[4,192,256]{2,1,0:T(8,128)(2,1)S(1)}, u32[]{:S(2)}, u32[]{:S(2)}) collective-permute-start(bf16[4,192,256]{2,1,0:T(8,128)(2,1)} %collective-permute-done.13.refs_2_), channel_id=1, source_target_pairs={{0,1},{1,0},{2,3},{3,2},{4,5},{5,4},{6,7},{7,6},{8,9},{9,8},{10,11... | collective-permute-start | bytes 1179656 | tf_op jit(solution)/shard_map/ppermute | solution.py:429
  128.5 0.9 copy-start.4
  129.5 1.0 copy-start.10
  130.4 9.3 %copy-start.8 = (bf16[4,128,512]{2,1,0:T(8,128)(2,1)S(1)}, bf16[4,128,512]{2,1,0:T(8,128)(2,1)}, u32[]{:S(2)}) copy-start(bf16[4,128,512]{2,1,0:T(8,128)(2,1)} %copy-done.7) | copy-start | bytes 1572868
  139.7 7.5 %copy-start.16 = (bf16[2,160,512]{2,1,0:T(8,128)(2,1)}, bf16[2,160,512]{2,1,0:T(8,128)(2,1)S(1)}, u32[]{:S(2)}) copy-start(bf16[2,160,512]{2,1,0:T(8,128)(2,1)S(1)} %get-tuple-element.44) | copy-start | bytes 983044
  147.3 2.2 %copy-start.1 = (bf16[4,1024,512]{2,1,0:T(8,128)(2,1)S(1)}, bf16[4,1024,512]{2,1,0:T(8,128)(2,1)}, u32[]{:S(2)}) copy-start(bf16[4,1024,512]{2,1,0:T(8,128)(2,1)} %all-gather.2.cloned.1.call-done.refs_2_.refs_4_) | copy-start | bytes 12582916
  149.5 12.3 %copy-start.2 = (bf16[4,1024,512]{2,1,0:T(8,128)(2,1)S(1)}, bf16[4,1024,512]{2,1,0:T(8,128)(2,1)}, u32[]{:S(2)}) copy-start(bf16[4,1024,512]{2,1,0:T(8,128)(2,1)} %all-gather.2.cloned.1.call-done.refs_2_.refs_4_) | copy-start | bytes 12582916
  149.5 21.7 %copy-start.14 = (s32[128,8]{0,1:T(8,128)S(1)}, s32[128,8]{0,1:T(8,128)}, u32[]{:S(2)}) copy-start(s32[128,8]{0,1:T(8,128)} %param.12) | copy-start | bytes 12292
  149.5 21.7 %copy-start.15 = (s32[128,8]{0,1:T(8,128)S(1)}, s32[128,8]{0,1:T(8,128)}, u32[]{:S(2)}) copy-start(s32[128,8]{0,1:T(8,128)} %param.13) | copy-start | bytes 12292
  149.5 12.3 %collective-permute-start.15 = (bf16[4,384,256]{2,1,0:T(8,128)(2,1)}, bf16[4,384,256]{2,1,0:T(8,128)(2,1)S(1)}, u32[]{:S(2)}, u32[]{:S(2)}) collective-permute-start(bf16[4,384,256]{2,1,0:T(8,128)(2,1)} %get-tuple-element.51.refs_0_), channel_id=1, source_target_pairs={{0,1},{1,0},{2,3},{3,2},{4,5},{5,4},{6,7},{7,6},{8,9},{9,8},{10,11... | collective-permute-start | bytes 2359304 | tf_op jit(solution)/shard_map/ppermute | solution.py:429
  150.6 11.2 %collective-permute-start.16 = (bf16[4,384,256]{2,1,0:T(8,128)(2,1)}, bf16[4,384,256]{2,1,0:T(8,128)(2,1)S(1)}, u32[]{:S(2)}, u32[]{:S(2)}) collective-permute-start(bf16[4,384,256]{2,1,0:T(8,128)(2,1)} %get-tuple-element.52.refs_2_), channel_id=1, source_target_pairs={{0,1},{1,0},{2,3},{3,2},{4,5},{5,4},{6,7},{7,6},{8,9},{9,8},{10,11... | collective-permute-start | bytes 2359304 | tf_op jit(solution)/shard_map/ppermute | solution.py:429
  150.6 10.3 %collective-permute-start.9 = (bf16[2,160,512]{2,1,0:T(8,128)(2,1)}, bf16[2,160,512]{2,1,0:T(8,128)(2,1)S(1)}, u32[]{:S(2)}, u32[]{:S(2)}) collective-permute-start(bf16[2,160,512]{2,1,0:T(8,128)(2,1)} %copy-done.16), channel_id=1, source_target_pairs={{0,4},{4,0},{8,12},{12,8},{1,5},{5,1},{9,13},{13,9},{2,6},{6,2},{1... | collective-permute-start | bytes 983048 | tf_op jit(solution)/shard_map/ppermute | solution.py:429
  161.0 10.2 %collective-permute-start.10 = (bf16[1,160,512]{2,1,0:T(8,128)(2,1)S(1)}, bf16[1,160,512]{2,1,0:T(8,128)(2,1)S(1)}, u32[]{:S(2)}, u32[]{:S(2)}) collective-permute-start(bf16[1,160,512]{2,1,0:T(8,128)(2,1)S(1)} %get-tuple-element.46), channel_id=1, source_target_pairs={{0,8},{4,12},{8,0},{12,4},{1,9},{5,13},{9,1},{13,5},{2,10},{6,14},... | collective-permute-start | bytes 491528 | tf_op jit(solution)/shard_map/ppermute | solution.py:429
Sparse Core Ops, SparseCore 0:
  9.6 115.1 all-gather.1

commit v13 on v9

--- a/solution.py
+++ b/solution.py
@@ -230,8 +230,9 @@
 
 def row_kernel(z, ids_ref, *refs):
     grads = refs[: z.sub]
-    pair_ref, weight_ref, codes_ref, keep_ref, send_ref = refs[z.sub : z.sub + 5]
-    rows_ref, marks, held, weights, sems = refs[z.sub + 5 :]
+    pair_ref, weight_ref, codes_ref = refs[z.sub : z.sub + 3]
+    outs = refs[z.sub + 3 : z.sub + 3 + z.ep]
+    rows_ref, marks, held, weights, sems = refs[z.sub + 3 + z.ep :]
     me, mine = ids_ref[0], ids_ref[1]
     step = pl.program_id(0)
     place = step // z.part_blocks
@@ -275,11 +276,17 @@
             source = me ^ k
             start = pl.multiple_of(source * z.cap, z.cap)
             rows = rows_ref[:, pl.ds(start, z.cap), :].reshape(z.local * z.cap, z.width)
-            out_ref = send_ref if k % 2 else keep_ref
             picks = local_picks(z, codes_ref, source, me)
-            out_ref[k // 2, : z.tokens, :] = tn(picks, rows).astype(BF)
-            out_ref[k // 2, z.tokens :, : z.tokens] = marks[source].astype(BF)
-            out_ref[k // 2, z.tokens :, z.tokens :] = blank
+            outs[k][: z.tokens, :] = tn(picks, rows).astype(BF)
+            outs[k][z.tokens :, : z.tokens] = marks[source].astype(BF)
+            outs[k][z.tokens :, z.tokens :] = blank
+
+
+def sum_kernel(*refs):
+    count = len(refs) // 3
+    for i in range(count):
+        total = refs[i][...].astype(F32) + refs[count + i][...].astype(F32)
+        refs[2 * count + i][...] = total.astype(BF)
 
 
 def halve_kernel(keep_ref, got_ref, out_keep, out_send):
@@ -291,7 +298,7 @@
 
 def token_kernel(z, count_ref, *refs):
     keep_ref, got_ref, routes_ref, replica_ref, table_ref, tokens_ref, route_ref = refs
-    total = keep_ref[0].astype(F32) + got_ref[0].astype(F32)
+    total = keep_ref[...].astype(F32) + got_ref[...].astype(F32)
     tokens_ref[...] = total[: z.tokens, :].astype(BF)
     rows = total[z.tokens :, : z.tokens].astype(BF)
     totals = [jnp.zeros((1, z.tokens), F32)] * z.top
@@ -460,10 +467,36 @@
     )(*values, *after)
 
 
+def pick_kernel(first, ids_ref, go_ref, back_ref, out_ref, sem):
+    for condition, ref in ((ids_ref[0] >= first, go_ref), (ids_ref[0] < first, back_ref)):
+
+        @pl.when(condition)
+        def _():
+            copy = pltpu.make_async_copy(ref, out_ref, sem)
+            copy.start()
+            copy.wait()
+
+
+def pick(ids, go, back, first):
+    anywhere = pl.BlockSpec(memory_space=pl.ANY)
+    return pl.pallas_call(
+        functools.partial(pick_kernel, first),
+        in_specs=[smem(), anywhere, anywhere],
+        out_specs=anywhere,
+        out_shape=jax.ShapeDtypeStruct(go.shape, go.dtype),
+        scratch_shapes=[pltpu.SemaphoreType.DMA],
+        compiler_params=pltpu.CompilerParams(vmem_limit_bytes=1024 * 1024),
+        name="pick",
+    )(ids, go, back)
+
+
 def chain_step(go, back, axis, size, d):
-    go = lax.ppermute(go, axis, [(i, i + 1) for i in range(d - 1, size - 1)])
-    back = lax.ppermute(back, axis, [(i, i - 1) for i in range(size - d, 0, -1)])
-    return go, back
+    rights = [(i, i + 1) for i in range(d - 1, size - 1)]
+    lefts = [(i, i - 1) for i in range(size - d, 0, -1)]
+    if d > 1 and go is back:
+        got = lax.ppermute(go, axis, rights + lefts)
+        return got, got
+    return lax.ppermute(go, axis, rights), lax.ppermute(back, axis, lefts)
 
 
 def body(
@@ -520,7 +553,7 @@
     )(ids, pair_rows, bufs[1], chain[0])
     downs = [downs[0]] + [swap(downs[k], "ep", n, k) for k in range(1, n)]
     chain = gate(chain, bufs[1:] + downs[1:])
-    steps = [chain_step(chain[0], chain[0], "ep", n, 1)]
+    steps = [list(chain_step(chain[0], chain[0], "ep", n, 1))]
 
     def stack(pieces):
         shape = pieces[0].shape
@@ -608,14 +641,16 @@
         [pltpu.VMEM((z.slots, z.rows, z.width), BF), pltpu.SemaphoreType.DMA((m,))],
         "down_grads",
     )
-    steps[0] = gate(steps[0], [down_made])
     steps.append(chain_step(*steps[0], "ep", n, 2))
     got = swap(send, "sub", m, 1)
+    after = [*steps[0], down_made]
     bit = 2
     while bit < m:
         keep, send = halve(keep, got)
+        send = gate([send], after)[0]
         got = swap(send, "sub", m, bit)
         bit *= 2
+
     *pieces, grad_part = pl.pallas_call(
         functools.partial(pre_kernel, z),
         grid_spec=pltpu.PrefetchScalarGridSpec(
@@ -639,8 +674,8 @@
     pieces = pieces[:1] + [swap(a, "ep", n, k) for k, a in enumerate(late, 1)]
     grad_parts = spread_over({0: grad_part}, "sub", m, m // 2)
 
-    back_shape = (n // 2, z.tokens + z.slots, z.width)
-    keep, send = pl.pallas_call(
+    back_shape = (z.tokens + z.slots, z.width)
+    parts = pl.pallas_call(
         functools.partial(row_kernel, z),
         grid_spec=pltpu.PrefetchScalarGridSpec(
             num_scalar_prefetch=1,
@@ -651,7 +686,7 @@
                 pl.BlockSpec(memory_space=pltpu.HBM),
                 whole(code_shape),
             ],
-            out_specs=[whole(back_shape)] * 2,
+            out_specs=[whole(back_shape)] * n,
             scratch_shapes=[
                 pltpu.VMEM((z.local, z.rows, z.width), BF),
                 pltpu.VMEM((n, z.slots, z.tokens), F32),
@@ -660,20 +695,36 @@
                 pltpu.SemaphoreType.DMA((z.local,)),
             ],
         ),
-        out_shape=[jax.ShapeDtypeStruct(back_shape, BF)] * 2,
+        out_shape=[jax.ShapeDtypeStruct(back_shape, BF)] * n,
         compiler_params=params(46),
         name="row_grads",
     )(ids, *grad_parts, pair_rows, weight_in, codes)
+    steps[1] = go, back = gate(steps[1], pieces[1:])
+    picked = []
     for d in range(3, n):
-        steps.append(chain_step(*steps[-1], "ep", n, d))
+        if 2 * d > n + 1 and go is not back:
+            go = back = pick(ids, go, back, d - 1)
+            picked.append(go)
+        go, back = chain_step(go, back, "ep", n, d)
+        steps.append((go, back))
     gathered = [inputs] + [go for go, _ in steps] + [back for _, back in steps]
-    got = swap(send, "ep", n, 1)
-    pieces[:1] = gate(pieces[:1], [got])
+    got = [swap(part, "ep", n, 1) for part in parts[1::2]]
+    pieces[:1] = gate(pieces[:1], [*got, *picked])
     sides = spread_over({0: stack(pieces)}, "sub", m, m // 2)
-    bit = 2
+    keep, bit = parts[::2], 2
     while bit < n:
-        keep, send = halve(keep, got)
-        got = swap(send, "ep", n, bit)
+        count = len(keep)
+        parts = pl.pallas_call(
+            sum_kernel,
+            in_specs=[whole(back_shape)] * 2 * count,
+            out_specs=[whole(back_shape)] * count,
+            out_shape=[jax.ShapeDtypeStruct(back_shape, BF)] * count,
+            grid=(1,),
+            compiler_params=params(16),
+            name="sum_parts",
+        )(*keep, *got)
+        keep = parts[::2]
+        got = [swap(part, "ep", n, bit) for part in parts[1::2]]
         bit *= 2
 
     grad_in, in_made = total_call(
@@ -690,7 +741,7 @@
         ],
         "in_grads",
     )
-    got = gate([got], [in_made])[0]
+    keep, got = keep[0], gate(got, [in_made])[0]
     grad_tokens, grad_routes = pl.pallas_call(
         functools.partial(token_kernel, z),
         out_shape=[

time: 160 us -> 158 us (0.988)
  starting transfers between devices: 41.4 us -> 36 us
  waiting for transfers between devices: 78.3 us -> 81.1 us
    ppermute x22 -> x23, starting transfers between devices: 31.5 us -> 26.8 us  [swap(): return lax.ppermute(x, axis, [(i, i ^ bit) for i in range(size)])]
    ppermute x6 -> x5, waiting for transfers between devices: 14.2 us -> 16.2 us  [the longest x1 10.9 us: chain_step(): got = lax.ppermute(go, axis, rights + lefts)]
    ppermute x22 -> x23, waiting for transfers between devices: 64.1 us -> 64.9 us  [swap(): return lax.ppermute(x, axis, [(i, i ^ bit) for i in range(size)])]
    ppermute x6 -> x5, starting transfers between devices: 9.92 us -> 9.18 us  [the longest x4 7.9 us: chain_step(): return (lax.ppermute(go, axis, rights), lax.ppermute(back, axis, lefts))]
  transfers between devices with their start and end apart: 28 -> 28, of which waited for: 10 -> 12; matrix products, arithmetic and copies ran while one was open for 1% -> 1% of each run, Pallas kernels for 21% -> 21%
where the time goes in v13:
time: 158 us
  waiting for transfers between devices  81.1 us (51%)
  Pallas kernels  36.7 us (23%)
  starting transfers between devices  36 us (23%)
  local copies, waits for them, and re-layouts  2.16 us (1%)
  between operations  1.7 us (1%)
    ppermute x23, waiting for transfers between devices, swap(): return lax.ppermute(x, axis, [(i, i ^ bit) for i in range(size)])  64.9 us
    ppermute x23, starting transfers between devices, swap(): return lax.ppermute(x, axis, [(i, i ^ bit) for i in range(size)])  26.8 us
    pallas_call x2, Pallas kernels, total_call(): pl.pallas_call(functools.partial(kernel, z), grid_spec=pltpu.PrefetchScal...  15.5 us
    ppermute x1, waiting for transfers between devices, chain_step(): got = lax.ppermute(go, axis, rights + lefts)  10.9 us
    pallas_call x1, Pallas kernels, body(): pl.pallas_call(functools.partial(row_kernel, z), grid_spec=pltpu.Prefetch...  8.31 us
    ppermute x4, starting transfers between devices, chain_step(): return (lax.ppermute(go, axis, rights), lax.ppermute(back, axis, lefts))  7.9 us
    pallas_call x1, Pallas kernels, body(): pl.pallas_call(functools.partial(down_kernel, z), grid_spec=pltpu.Prefetc...  6.4 us
    ppermute x4, waiting for transfers between devices, chain_step(): return (lax.ppermute(go, axis, rights), lax.ppermute(back, axis, lefts))  5.35 us
  transfers between devices with their start and end apart: 28, of which 12 were waited for; matrix products, arithmetic and copies ran while one was open for 1% of the time, Pallas kernels for 21%

profile of v13, /device:TPU:0, one launch (start us, length us, event | category | flops | bytes accessed | tf_op | source)
XLA Modules:
  0.0 157.7 jit_solution(8139675989097518499)
XLA Ops:
  1.4 2.0 %route.1.refs_1_.refs_0_ = bf16[144,512]{1,0:T(8,128)(2,1)} custom-call(s32[1]{0:T(128)S(6)} %copy.34.count_ref, bf16[128,512]{1,0:T(8,128)(2,1)} %grad_ref.1, bf16[8,128]{1,0:T(8,128)(2,1)} %bitcast.22, s32[8,128]{1,0:T(8,128)} %bitcast.18, s32[8,128]{1,0:T(8,128)} %bitcast.20, s32[4,16]{1,0:T(4,128)} %bitcast.14), custom_call_target="tpu_custom_call" | custom-call | tf_op jit(solution)/shard_map/route/pallas_call | solution.py:525
  3.5 3.0 %collective-permute-start = (bf16[144,512]{1,0:T(8,128)(2,1)}, bf16[144,512]{1,0:T(8,128)(2,1)S(1)}, u32[]{:S(2)}, u32[]{:S(2)}) collective-permute-start(bf16[144,512]{1,0:T(8,128)(2,1)} %route.1.refs_1_.refs_0_), channel_id=1, source_target_pairs={{0,4},{4,0},{8,12},{12,8},{1,5},{5,1},{9,13},{13,9},{2,6},{6,2},{1... | collective-permute-start | bytes 442376 | tf_op jit(solution)/shard_map/ppermute | solution.py:440
  6.5 2.5 %collective-permute-start.2 = (bf16[144,512]{1,0:T(8,128)(2,1)}, bf16[144,512]{1,0:T(8,128)(2,1)S(1)}, u32[]{:S(2)}, u32[]{:S(2)}) collective-permute-start(bf16[144,512]{1,0:T(8,128)(2,1)} %route.1.refs_1_.refs_0_), channel_id=1, source_target_pairs={{0,12},{4,8},{8,4},{12,0},{1,13},{5,9},{9,5},{13,1},{2,14},{6,10},... | collective-permute-start | bytes 442376 | tf_op jit(solution)/shard_map/ppermute | solution.py:440
  9.0 0.1 collective-permute-start.1
  9.1 0.1 pad_add_fusion.ids_ref
  9.2 1.2 copy.24.refs_0_
  10.4 0.9 copy-done.2
  11.3 1.1 hidden_columns.1
  12.4 2.0 %collective-permute-start.4 = (bf16[192,256]{1,0:T(8,128)(2,1)S(1)}, bf16[192,256]{1,0:T(8,128)(2,1)S(1)}, u32[]{:S(2)}, u32[]{:S(2)}) collective-permute-start(bf16[192,256]{1,0:T(8,128)(2,1)S(1)} %get-tuple-element.41), channel_id=1, source_target_pairs={{0,4},{4,0},{8,12},{12,8},{1,5},{5,1},{9,13},{13,9},{2,6},{6,2},{1... | collective-permute-start | bytes 294920 | tf_op jit(solution)/shard_map/ppermute | solution.py:440
  14.4 4.0 %collective-permute-start.5 = (bf16[192,256]{1,0:T(8,128)(2,1)S(1)}, bf16[192,256]{1,0:T(8,128)(2,1)S(1)}, u32[]{:S(2)}, u32[]{:S(2)}) collective-permute-start(bf16[192,256]{1,0:T(8,128)(2,1)S(1)} %get-tuple-element.42), channel_id=1, source_target_pairs={{0,8},{4,12},{8,0},{12,4},{1,9},{5,13},{9,1},{13,5},{2,10},{6,14},... | collective-permute-start | bytes 294920 | tf_op jit(solution)/shard_map/ppermute | solution.py:440
  18.4 9.4 %collective-permute-done.1.refs_2_ = bf16[144,512]{1,0:T(8,128)(2,1)} collective-permute-done((bf16[144,512]{1,0:T(8,128)(2,1)}, bf16[144,512]{1,0:T(8,128)(2,1)}, u32[]{:S(2)}, u32[]{:S(2)}) %collective-permute-start.1) | collective-permute-done | bytes 147488 | tf_op jit(solution)/shard_map/ppermute | solution.py:440
  27.8 1.9 %collective-permute-done.5.refs_5_.refs_2_ = bf16[192,256]{1,0:T(8,128)(2,1)S(1)} collective-permute-done((bf16[192,256]{1,0:T(8,128)(2,1)S(1)}, bf16[192,256]{1,0:T(8,128)(2,1)S(1)}, u32[]{:S(2)}, u32[]{:S(2)}) %collective-permute-start.5) | collective-permute-done | bytes 98336 | tf_op jit(solution)/shard_map/ppermute | solution.py:440
  29.8 1.3 collective-permute-start.8
  31.0 4.6 %collective-permute-start.7 = (bf16[1024,512]{1,0:T(8,128)(2,1)S(1)}, bf16[1024,512]{1,0:T(8,128)(2,1)S(1)}, u32[]{:S(2)}, u32[]{:S(2)}) collective-permute-start(bf16[1024,512]{1,0:T(8,128)(2,1)S(1)} %gate.8), channel_id=1, source_target_pairs={{0,4},{4,8},{8,12},{1,5},{5,9},{9,13},{2,6},{6,10},{10,14},{3,7},{... | collective-permute-start | bytes 3145736 | tf_op jit(solution)/shard_map/ppermute | solution.py:499
  35.7 6.4 %hidden_partials.1 = (bf16[2,256,768]{2,1,0:T(8,128)(2,1)S(1)}, bf16[2,256,768]{2,1,0:T(8,128)(2,1)S(1)}, bf16[4,128,512]{2,1,0:T(8,128)(2,1)S(1)}, f32[4,64,128]{2,1,0:T(8,128)S(1)}) custom-call(s32[2]{0:T(128)S(1)} %pad_add_fusion.ids_ref, bf16[144,512]{1,0:T(8,128)(2,1)S(1)} %copy-done.3, bf16[144,512]{1,0:T(8,128)(2,1)S(1)} %collective-permute-done.after_ref.refs_1_, ...), custom_call_target="tpu_custom_call" | custom-call | tf_op jit(solution)/shard_map/hidden_partials/pallas_call | solution.py:587
  42.1 0.1 collective-permute-start.3
  42.2 2.5 %collective-permute-start.10 = (bf16[4,192,256]{2,1,0:T(8,128)(2,1)S(1)}, bf16[4,192,256]{2,1,0:T(8,128)(2,1)S(1)}, u32[]{:S(2)}, u32[]{:S(2)}) collective-permute-start(bf16[4,192,256]{2,1,0:T(8,128)(2,1)S(1)} %stack_columns.2.refs_0_), channel_id=1, source_target_pairs={{0,2},{1,3},{2,0},{3,1},{4,6},{5,7},{6,4},{7,5},{8,10},{9,11},{10,... | collective-permute-start | bytes 1179656 | tf_op jit(solution)/shard_map/ppermute | solution.py:440
  44.7 0.2 collective-permute-start.9
  44.9 9.6 %collective-permute-done.10.refs_2_ = bf16[4,192,256]{2,1,0:T(8,128)(2,1)S(1)} collective-permute-done((bf16[4,192,256]{2,1,0:T(8,128)(2,1)S(1)}, bf16[4,192,256]{2,1,0:T(8,128)(2,1)S(1)}, u32[]{:S(2)}, u32[]{:S(2)}) %collective-permute-start.10) | collective-permute-done | bytes 393248 | tf_op jit(solution)/shard_map/ppermute | solution.py:440
  54.5 0.2 halve.1
  54.7 1.5 collective-permute-done.11.refs_3_
  56.2 7.8 %down_grads.1 = (bf16[16,192,512]{2,1,0:T(8,128)(2,1)}, f32[8,128]{1,0:T(8,128)S(1)}) custom-call(s32[2]{0:T(128)S(1)} %pad_add_fusion.ids_ref, s32[4,16]{1,0:T(4,128)S(1)} %bitcast.15, bf16[4,192,256]{2,1,0:T(8,128)(2,1)S(1)} %stack_columns.2.refs_0_, bf16[4,192,256]{2,1,0:T(8,128)(2,1)S(1)} %collective-permute-done.9.refs_1_, ...), custom_call_target="tpu_custom_call" | custom-call | tf_op jit(solution)/shard_map/down_grads/pallas_call | solution.py:613
  64.0 1.8 %collective-permute-start.12 = (bf16[1,256,768]{2,1,0:T(8,128)(2,1)S(1)}, bf16[1,256,768]{2,1,0:T(8,128)(2,1)S(1)}, u32[]{:S(2)}, u32[]{:S(2)}) collective-permute-start(bf16[1,256,768]{2,1,0:T(8,128)(2,1)S(1)} %gate.9), channel_id=1, source_target_pairs={{0,2},{1,3},{2,0},{3,1},{4,6},{5,7},{6,4},{7,5},{8,10},{9,11},{10,... | collective-permute-start | bytes 1179656 | tf_op jit(solution)/shard_map/ppermute | solution.py:440
  65.9 1.3 collective-permute-start.20
  67.1 0.7 collective-permute-start.19
  67.9 7.4 %collective-permute-done.12.got_ref = bf16[1,256,768]{2,1,0:T(8,128)(2,1)S(1)} collective-permute-done((bf16[1,256,768]{2,1,0:T(8,128)(2,1)S(1)}, bf16[1,256,768]{2,1,0:T(8,128)(2,1)S(1)}, u32[]{:S(2)}, u32[]{:S(2)}) %collective-permute-start.12) | collective-permute-done | bytes 393248 | tf_op jit(solution)/shard_map/ppermute | solution.py:440
  75.3 1.6 %pre_grads.1 = (bf16[384,256]{1,0:T(8,128)(2,1)S(1)}, bf16[384,256]{1,0:T(8,128)(2,1)S(1)}, bf16[384,256]{1,0:T(8,128)(2,1)S(1)}, bf16[384,256]{1,0:T(8,128)(2,1)S(1)}, bf16[256,768]{1,0:T(8,128)(2,1)S(1)}) custom-call(s32[2]{0:T(128)S(1)} %pad_add_fusion.ids_ref, bf16[1,256,768]{2,1,0:T(8,128)(2,1)S(1)} %get-tuple-element.39.keep_ref, ...), custom_call_target="tpu_custom_call" | custom-call | tf_op jit(solution)/shard_map/pre_grads/pallas_call | solution.py:654
  76.9 1.8 %collective-permute-start.14 = (bf16[256,768]{1,0:T(8,128)(2,1)S(1)}, bf16[256,768]{1,0:T(8,128)(2,1)S(1)}, u32[]{:S(2)}, u32[]{:S(2)}) collective-permute-start(bf16[256,768]{1,0:T(8,128)(2,1)S(1)} %get-tuple-element.47.refs_0_), channel_id=1, source_target_pairs={{0,2},{1,3},{2,0},{3,1},{4,6},{5,7},{6,4},{7,5},{8,10},{9,11},{10,... | collective-permute-start | bytes 1179656 | tf_op jit(solution)/shard_map/ppermute | solution.py:440
  78.7 8.6 %collective-permute-done.14.refs_2_ = bf16[256,768]{1,0:T(8,128)(2,1)S(1)} collective-permute-done((bf16[256,768]{1,0:T(8,128)(2,1)S(1)}, bf16[256,768]{1,0:T(8,128)(2,1)S(1)}, u32[]{:S(2)}, u32[]{:S(2)}) %collective-permute-start.14) | collective-permute-done | bytes 393248 | tf_op jit(solution)/shard_map/ppermute | solution.py:440
  87.3 5.3 %collective-permute-done.20.refs_4_.refs_1_ = bf16[1024,512]{1,0:T(8,128)(2,1)S(1)} collective-permute-done((bf16[1024,512]{1,0:T(8,128)(2,1)S(1)}, bf16[1024,512]{1,0:T(8,128)(2,1)S(1)}, u32[]{:S(2)}, u32[]{:S(2)}) %collective-permute-start.20) | collective-permute-done | bytes 1048608 | tf_op jit(solution)/shard_map/ppermute | solution.py:499
  92.7 2.8 %collective-permute-start.21 = (bf16[384,256]{1,0:T(8,128)(2,1)S(1)}, bf16[384,256]{1,0:T(8,128)(2,1)S(1)}, u32[]{:S(2)}, u32[]{:S(2)}) collective-permute-start(bf16[384,256]{1,0:T(8,128)(2,1)S(1)} %get-tuple-element.58), channel_id=1, source_target_pairs={{0,4},{4,0},{8,12},{12,8},{1,5},{5,1},{9,13},{13,9},{2,6},{6,2},{1... | collective-permute-start | bytes 589832 | tf_op jit(solution)/shard_map/ppermute | solution.py:440
  95.5 2.2 %collective-permute-start.22 = (bf16[384,256]{1,0:T(8,128)(2,1)S(1)}, bf16[384,256]{1,0:T(8,128)(2,1)S(1)}, u32[]{:S(2)}, u32[]{:S(2)}) collective-permute-start(bf16[384,256]{1,0:T(8,128)(2,1)S(1)} %get-tuple-element.59), channel_id=1, source_target_pairs={{0,8},{4,12},{8,0},{12,4},{1,9},{5,13},{9,1},{13,5},{2,10},{6,14},... | collective-permute-start | bytes 589832 | tf_op jit(solution)/shard_map/ppermute | solution.py:440
  97.7 1.2 collective-permute-start.23
  98.8 8.3 %row_grads.1 = (bf16[160,512]{1,0:T(8,128)(2,1)S(1)}, bf16[160,512]{1,0:T(8,128)(2,1)S(1)}, bf16[160,512]{1,0:T(8,128)(2,1)S(1)}, bf16[160,512]{1,0:T(8,128)(2,1)S(1)}) custom-call(s32[2]{0:T(128)S(1)} %pad_add_fusion.ids_ref, bf16[256,768]{1,0:T(8,128)(2,1)S(1)} %get-tuple-element.47.refs_0_, bf16[256,768]{1,0:T(8,128)(2,1)S(1)} %collective-permute-done.13.refs_1_, ...), custom_call_target="tpu_custom_call" | custom-call | tf_op jit(solution)/shard_map/row_grads/pallas_call | solution.py:678
  107.2 0.6 collective-permute-start.16
  107.8 1.4 collective-permute-start.17
  109.3 2.9 %collective-permute-done.22.refs_3_.refs_2_ = bf16[384,256]{1,0:T(8,128)(2,1)S(1)} collective-permute-done((bf16[384,256]{1,0:T(8,128)(2,1)S(1)}, bf16[384,256]{1,0:T(8,128)(2,1)S(1)}, u32[]{:S(2)}, u32[]{:S(2)}) %collective-permute-start.22) | collective-permute-done | bytes 196640 | tf_op jit(solution)/shard_map/ppermute | solution.py:440
  112.2 0.6 pick.1.refs_3_
  112.8 2.4 %collective-permute-done.16.refs_2_.refs_1_ = bf16[160,512]{1,0:T(8,128)(2,1)S(1)} collective-permute-done((bf16[160,512]{1,0:T(8,128)(2,1)S(1)}, bf16[160,512]{1,0:T(8,128)(2,1)S(1)}, u32[]{:S(2)}, u32[]{:S(2)}) %collective-permute-start.16) | collective-permute-done | bytes 163872 | tf_op jit(solution)/shard_map/ppermute | solution.py:440
  115.3 3.3 %collective-permute-done.17.refs_3_.refs_2_ = bf16[160,512]{1,0:T(8,128)(2,1)S(1)} collective-permute-done((bf16[160,512]{1,0:T(8,128)(2,1)S(1)}, bf16[160,512]{1,0:T(8,128)(2,1)S(1)}, u32[]{:S(2)}, u32[]{:S(2)}) %collective-permute-start.17) | collective-permute-done | bytes 163872 | tf_op jit(solution)/shard_map/ppermute | solution.py:440
  118.7 0.4 collective-permute-start.25
  119.1 1.3 collective-permute-start.27
  120.4 17.7 %collective-permute-done.25.refs_2_ = bf16[4,384,256]{2,1,0:T(8,128)(2,1)S(1)} collective-permute-done((bf16[4,384,256]{2,1,0:T(8,128)(2,1)S(1)}, bf16[4,384,256]{2,1,0:T(8,128)(2,1)S(1)}, u32[]{:S(2)}, u32[]{:S(2)}) %collective-permute-start.25) | collective-permute-done | bytes 786464 | tf_op jit(solution)/shard_map/ppermute | solution.py:440
  138.1 0.1 sum_parts.1
  138.2 0.1 collective-permute-start.18
  138.3 10.9 %collective-permute-done.27.refs_7_.refs_10_ = bf16[1024,512]{1,0:T(8,128)(2,1)S(1)} collective-permute-done((bf16[1024,512]{1,0:T(8,128)(2,1)S(1)}, bf16[1024,512]{1,0:T(8,128)(2,1)S(1)}, u32[]{:S(2)}, u32[]{:S(2)}) %collective-permute-start.27) | collective-permute-done | bytes 1048608 | tf_op jit(solution)/shard_map/ppermute | solution.py:497
  149.2 7.7 %in_grads.1 = (bf16[16,384,512]{2,1,0:T(8,128)(2,1)}, f32[8,128]{1,0:T(8,128)S(1)}) custom-call(s32[2]{0:T(128)S(1)} %pad_add_fusion.ids_ref, s32[4,16]{1,0:T(4,128)S(1)} %bitcast.16, bf16[4,384,256]{2,1,0:T(8,128)(2,1)S(1)} %stack_columns.3.refs_0_, bf16[4,384,256]{2,1,0:T(8,128)(2,1)S(1)} %collective-permute-done.24.refs_1_, ...), custom_call_target="tpu_custom_call" | custom-call | tf_op jit(solution)/shard_map/in_grads/pallas_call | solution.py:613
  156.9 0.8 token_grads.1
  (44 shorter events, 0.2 us)
Async XLA Ops:
  0.6 10.7 %copy-start = (bf16[8,128,1536]{2,1,0:T(8,128)(2,1)S(1)}, bf16[8,128,1536]{2,1,0:T(8,128)(2,1)}, u32[]{:S(2)}) copy-start(bf16[8,128,1536]{2,1,0:T(8,128)(2,1)} %param.17) | copy-start | bytes 9437188
  3.5 7.8 %collective-permute-start = (bf16[144,512]{1,0:T(8,128)(2,1)}, bf16[144,512]{1,0:T(8,128)(2,1)S(1)}, u32[]{:S(2)}, u32[]{:S(2)}) collective-permute-start(bf16[144,512]{1,0:T(8,128)(2,1)} %route.1.refs_1_.refs_0_), channel_id=1, source_target_pairs={{0,4},{4,0},{8,12},{12,8},{1,5},{5,1},{9,13},{13,9},{2,6},{6,2},{1... | collective-permute-start | bytes 442376 | tf_op jit(solution)/shard_map/ppermute | solution.py:440
  6.5 11.9 %collective-permute-start.2 = (bf16[144,512]{1,0:T(8,128)(2,1)}, bf16[144,512]{1,0:T(8,128)(2,1)S(1)}, u32[]{:S(2)}, u32[]{:S(2)}) collective-permute-start(bf16[144,512]{1,0:T(8,128)(2,1)} %route.1.refs_1_.refs_0_), channel_id=1, source_target_pairs={{0,12},{4,8},{8,4},{12,0},{1,13},{5,9},{9,5},{13,1},{2,14},{6,10},... | collective-permute-start | bytes 442376 | tf_op jit(solution)/shard_map/ppermute | solution.py:440
  9.0 18.8 %collective-permute-start.1 = (bf16[144,512]{1,0:T(8,128)(2,1)}, bf16[144,512]{1,0:T(8,128)(2,1)}, u32[]{:S(2)}, u32[]{:S(2)}) collective-permute-start(bf16[144,512]{1,0:T(8,128)(2,1)} %route.1.refs_1_.refs_0_), channel_id=1, source_target_pairs={{0,8},{4,12},{8,0},{12,4},{1,9},{5,13},{9,1},{13,5},{2,10},{6,14},... | collective-permute-start | bytes 442376 | tf_op jit(solution)/shard_map/ppermute | solution.py:440
  10.4 0.9 copy-start.2
  11.3 24.4 %copy-start.3 = (bf16[144,512]{1,0:T(8,128)(2,1)S(1)}, bf16[144,512]{1,0:T(8,128)(2,1)}, u32[]{:S(2)}) copy-start(bf16[144,512]{1,0:T(8,128)(2,1)} %route.1.refs_1_.refs_0_) | copy-start | bytes 442372
  12.4 43.8 %copy-start.4 = (s32[16,4]{0,1:T(4,128)S(1)}, s32[16,4]{0,1:T(4,128)}, u32[]{:S(2)}) copy-start(s32[16,4]{0,1:T(4,128)} %param.14) | copy-start | bytes 772
  12.4 15.4 %collective-permute-start.4 = (bf16[192,256]{1,0:T(8,128)(2,1)S(1)}, bf16[192,256]{1,0:T(8,128)(2,1)S(1)}, u32[]{:S(2)}, u32[]{:S(2)}) collective-permute-start(bf16[192,256]{1,0:T(8,128)(2,1)S(1)} %get-tuple-element.41), channel_id=1, source_target_pairs={{0,4},{4,0},{8,12},{12,8},{1,5},{5,1},{9,13},{13,9},{2,6},{6,2},{1... | collective-permute-start | bytes 294920 | tf_op jit(solution)/shard_map/ppermute | solution.py:440
  14.4 15.3 %collective-permute-start.5 = (bf16[192,256]{1,0:T(8,128)(2,1)S(1)}, bf16[192,256]{1,0:T(8,128)(2,1)S(1)}, u32[]{:S(2)}, u32[]{:S(2)}) collective-permute-start(bf16[192,256]{1,0:T(8,128)(2,1)S(1)} %get-tuple-element.42), channel_id=1, source_target_pairs={{0,8},{4,12},{8,0},{12,4},{1,9},{5,13},{9,1},{13,5},{2,10},{6,14},... | collective-permute-start | bytes 294920 | tf_op jit(solution)/shard_map/ppermute | solution.py:440
  18.4 11.4 %collective-permute-start.6 = (bf16[192,256]{1,0:T(8,128)(2,1)S(1)}, bf16[192,256]{1,0:T(8,128)(2,1)S(1)}, u32[]{:S(2)}, u32[]{:S(2)}) collective-permute-start(bf16[192,256]{1,0:T(8,128)(2,1)S(1)} %get-tuple-element.43), channel_id=1, source_target_pairs={{0,12},{4,8},{8,4},{12,0},{1,13},{5,9},{9,5},{13,1},{2,14},{6,10},... | collective-permute-start | bytes 294920 | tf_op jit(solution)/shard_map/ppermute | solution.py:440
  29.8 34.3 %collective-permute-start.8 = (bf16[1024,512]{1,0:T(8,128)(2,1)S(1)}, bf16[1024,512]{1,0:T(8,128)(2,1)S(1)}, u32[]{:S(2)}, u32[]{:S(2)}) collective-permute-start(bf16[1024,512]{1,0:T(8,128)(2,1)S(1)} %gate.8), channel_id=1, source_target_pairs={{12,8},{8,4},{4,0},{13,9},{9,5},{5,1},{14,10},{10,6},{6,2},{15,11}... | collective-permute-start | bytes 3145736 | tf_op jit(solution)/shard_map/ppermute | solution.py:499
  31.0 33.0 %collective-permute-start.7 = (bf16[1024,512]{1,0:T(8,128)(2,1)S(1)}, bf16[1024,512]{1,0:T(8,128)(2,1)S(1)}, u32[]{:S(2)}, u32[]{:S(2)}) collective-permute-start(bf16[1024,512]{1,0:T(8,128)(2,1)S(1)} %gate.8), channel_id=1, source_target_pairs={{0,4},{4,8},{8,12},{1,5},{5,9},{9,13},{2,6},{6,10},{10,14},{3,7},{... | collective-permute-start | bytes 3145736 | tf_op jit(solution)/shard_map/ppermute | solution.py:499
  42.1 12.4 %collective-permute-start.3 = (bf16[2,256,768]{2,1,0:T(8,128)(2,1)S(1)}, bf16[2,256,768]{2,1,0:T(8,128)(2,1)S(1)}, u32[]{:S(2)}, u32[]{:S(2)}) collective-permute-start(bf16[2,256,768]{2,1,0:T(8,128)(2,1)S(1)} %get-tuple-element.38), channel_id=1, source_target_pairs={{0,1},{1,0},{2,3},{3,2},{4,5},{5,4},{6,7},{7,6},{8,9},{9,8},{10,11... | collective-permute-start | bytes 2359304 | tf_op jit(solution)/shard_map/ppermute | solution.py:440
  42.2 12.3 %collective-permute-start.10 = (bf16[4,192,256]{2,1,0:T(8,128)(2,1)S(1)}, bf16[4,192,256]{2,1,0:T(8,128)(2,1)S(1)}, u32[]{:S(2)}, u32[]{:S(2)}) collective-permute-start(bf16[4,192,256]{2,1,0:T(8,128)(2,1)S(1)} %stack_columns.2.refs_0_), channel_id=1, source_target_pairs={{0,2},{1,3},{2,0},{3,1},{4,6},{5,7},{6,4},{7,5},{8,10},{9,11},{10,... | collective-permute-start | bytes 1179656 | tf_op jit(solution)/shard_map/ppermute | solution.py:440
  44.7 10.0 %collective-permute-start.9 = (bf16[4,192,256]{2,1,0:T(8,128)(2,1)S(1)}, bf16[4,192,256]{2,1,0:T(8,128)(2,1)S(1)}, u32[]{:S(2)}, u32[]{:S(2)}) collective-permute-start(bf16[4,192,256]{2,1,0:T(8,128)(2,1)S(1)} %stack_columns.2.refs_0_), channel_id=1, source_target_pairs={{0,1},{1,0},{2,3},{3,2},{4,5},{5,4},{6,7},{7,6},{8,9},{9,8},{10,11... | collective-permute-start | bytes 1179656 | tf_op jit(solution)/shard_map/ppermute | solution.py:440
  54.5 1.7 %collective-permute-start.11 = (bf16[4,192,256]{2,1,0:T(8,128)(2,1)S(1)}, bf16[4,192,256]{2,1,0:T(8,128)(2,1)S(1)}, u32[]{:S(2)}, u32[]{:S(2)}) collective-permute-start(bf16[4,192,256]{2,1,0:T(8,128)(2,1)S(1)} %collective-permute-done.10.refs_2_), channel_id=1, source_target_pairs={{0,1},{1,0},{2,3},{3,2},{4,5},{5,4},{6,7},{7,6},{8,9},{9,8},{10,11... | collective-permute-start | bytes 1179656 | tf_op jit(solution)/shard_map/ppermute | solution.py:440
  64.0 11.2 %collective-permute-start.12 = (bf16[1,256,768]{2,1,0:T(8,128)(2,1)S(1)}, bf16[1,256,768]{2,1,0:T(8,128)(2,1)S(1)}, u32[]{:S(2)}, u32[]{:S(2)}) collective-permute-start(bf16[1,256,768]{2,1,0:T(8,128)(2,1)S(1)} %gate.9), channel_id=1, source_target_pairs={{0,2},{1,3},{2,0},{3,1},{4,6},{5,7},{6,4},{7,5},{8,10},{9,11},{10,... | collective-permute-start | bytes 1179656 | tf_op jit(solution)/shard_map/ppermute | solution.py:440
  65.9 26.8 %collective-permute-start.20 = (bf16[1024,512]{1,0:T(8,128)(2,1)S(1)}, bf16[1024,512]{1,0:T(8,128)(2,1)S(1)}, u32[]{:S(2)}, u32[]{:S(2)}) collective-permute-start(bf16[1024,512]{1,0:T(8,128)(2,1)S(1)} %collective-permute-done.8.refs_2_.refs_8_), channel_id=1, source_target_pairs={{8,4},{4,0},{9,5},{5,1},{10,6},{6,2},{11,7},{7,3},{24,20},{20,16},... | collective-permute-start | bytes 3145736 | tf_op jit(solution)/shard_map/ppermute | solution.py:499
  67.1 25.5 %collective-permute-start.19 = (bf16[1024,512]{1,0:T(8,128)(2,1)S(1)}, bf16[1024,512]{1,0:T(8,128)(2,1)S(1)}, u32[]{:S(2)}, u32[]{:S(2)}) collective-permute-start(bf16[1024,512]{1,0:T(8,128)(2,1)S(1)} %collective-permute-done.7.refs_1_.refs_5_), channel_id=1, source_target_pairs={{4,8},{8,12},{5,9},{9,13},{6,10},{10,14},{7,11},{11,15},{20,24},{2... | collective-permute-start | bytes 3145736 | tf_op jit(solution)/shard_map/ppermute | solution.py:499
  76.9 10.4 %collective-permute-start.14 = (bf16[256,768]{1,0:T(8,128)(2,1)S(1)}, bf16[256,768]{1,0:T(8,128)(2,1)S(1)}, u32[]{:S(2)}, u32[]{:S(2)}) collective-permute-start(bf16[256,768]{1,0:T(8,128)(2,1)S(1)} %get-tuple-element.47.refs_0_), channel_id=1, source_target_pairs={{0,2},{1,3},{2,0},{3,1},{4,6},{5,7},{6,4},{7,5},{8,10},{9,11},{10,... | collective-permute-start | bytes 1179656 | tf_op jit(solution)/shard_map/ppermute | solution.py:440
  78.7 20.1 %collective-permute-start.13 = (bf16[256,768]{1,0:T(8,128)(2,1)S(1)}, bf16[256,768]{1,0:T(8,128)(2,1)S(1)}, u32[]{:S(2)}, u32[]{:S(2)}) collective-permute-start(bf16[256,768]{1,0:T(8,128)(2,1)S(1)} %get-tuple-element.47.refs_0_), channel_id=1, source_target_pairs={{0,1},{1,0},{2,3},{3,2},{4,5},{5,4},{6,7},{7,6},{8,9},{9,8},{10,11... | collective-permute-start | bytes 1179656 | tf_op jit(solution)/shard_map/ppermute | solution.py:440
  87.3 11.5 %collective-permute-start.15 = (bf16[256,768]{1,0:T(8,128)(2,1)S(1)}, bf16[256,768]{1,0:T(8,128)(2,1)S(1)}, u32[]{:S(2)}, u32[]{:S(2)}) collective-permute-start(bf16[256,768]{1,0:T(8,128)(2,1)S(1)} %collective-permute-done.14.refs_2_), channel_id=1, source_target_pairs={{0,1},{1,0},{2,3},{3,2},{4,5},{5,4},{6,7},{7,6},{8,9},{9,8},{10,11... | collective-permute-start | bytes 1179656 | tf_op jit(solution)/shard_map/ppermute | solution.py:440
  92.7 16.6 %collective-permute-start.21 = (bf16[384,256]{1,0:T(8,128)(2,1)S(1)}, bf16[384,256]{1,0:T(8,128)(2,1)S(1)}, u32[]{:S(2)}, u32[]{:S(2)}) collective-permute-start(bf16[384,256]{1,0:T(8,128)(2,1)S(1)} %get-tuple-element.58), channel_id=1, source_target_pairs={{0,4},{4,0},{8,12},{12,8},{1,5},{5,1},{9,13},{13,9},{2,6},{6,2},{1... | collective-permute-start | bytes 589832 | tf_op jit(solution)/shard_map/ppermute | solution.py:440
  95.5 16.7 %collective-permute-start.22 = (bf16[384,256]{1,0:T(8,128)(2,1)S(1)}, bf16[384,256]{1,0:T(8,128)(2,1)S(1)}, u32[]{:S(2)}, u32[]{:S(2)}) collective-permute-start(bf16[384,256]{1,0:T(8,128)(2,1)S(1)} %get-tuple-element.59), channel_id=1, source_target_pairs={{0,8},{4,12},{8,0},{12,4},{1,9},{5,13},{9,1},{13,5},{2,10},{6,14},... | collective-permute-start | bytes 589832 | tf_op jit(solution)/shard_map/ppermute | solution.py:440
  97.7 14.5 %collective-permute-start.23 = (bf16[384,256]{1,0:T(8,128)(2,1)S(1)}, bf16[384,256]{1,0:T(8,128)(2,1)S(1)}, u32[]{:S(2)}, u32[]{:S(2)}) collective-permute-start(bf16[384,256]{1,0:T(8,128)(2,1)S(1)} %get-tuple-element.60), channel_id=1, source_target_pairs={{0,12},{4,8},{8,4},{12,0},{1,13},{5,9},{9,5},{13,1},{2,14},{6,10},... | collective-permute-start | bytes 589832 | tf_op jit(solution)/shard_map/ppermute | solution.py:440
  107.2 42.0 %copy-start.1 = (bf16[8,4,32,512]{3,2,1,0:T(8,128)(2,1)S(1)}, bf16[8,4,32,512]{3,2,1,0:T(8,128)(2,1)}, u32[]{:S(2)}) copy-start(bf16[8,4,32,512]{3,2,1,0:T(8,128)(2,1)} %param.16) | copy-start | bytes 3145732
  107.2 8.1 %collective-permute-start.16 = (bf16[160,512]{1,0:T(8,128)(2,1)S(1)}, bf16[160,512]{1,0:T(8,128)(2,1)S(1)}, u32[]{:S(2)}, u32[]{:S(2)}) collective-permute-start(bf16[160,512]{1,0:T(8,128)(2,1)S(1)} %get-tuple-element.50), channel_id=1, source_target_pairs={{0,4},{4,0},{8,12},{12,8},{1,5},{5,1},{9,13},{13,9},{2,6},{6,2},{1... | collective-permute-start | bytes 491528 | tf_op jit(solution)/shard_map/ppermute | solution.py:440
  107.8 10.8 %collective-permute-start.17 = (bf16[160,512]{1,0:T(8,128)(2,1)S(1)}, bf16[160,512]{1,0:T(8,128)(2,1)S(1)}, u32[]{:S(2)}, u32[]{:S(2)}) collective-permute-start(bf16[160,512]{1,0:T(8,128)(2,1)S(1)} %get-tuple-element.51), channel_id=1, source_target_pairs={{0,4},{4,0},{8,12},{12,8},{1,5},{5,1},{9,13},{13,9},{2,6},{6,2},{1... | collective-permute-start | bytes 491528 | tf_op jit(solution)/shard_map/ppermute | solution.py:440
  118.6 38.3 %copy-start.5 = (s32[128,8]{0,1:T(8,128)S(1)}, s32[128,8]{0,1:T(8,128)}, u32[]{:S(2)}) copy-start(s32[128,8]{0,1:T(8,128)} %param.12) | copy-start | bytes 12292
  118.6 38.3 %copy-start.6 = (s32[128,8]{0,1:T(8,128)S(1)}, s32[128,8]{0,1:T(8,128)}, u32[]{:S(2)}) copy-start(s32[128,8]{0,1:T(8,128)} %param.13) | copy-start | bytes 12292
  118.7 19.5 %collective-permute-start.25 = (bf16[4,384,256]{2,1,0:T(8,128)(2,1)S(1)}, bf16[4,384,256]{2,1,0:T(8,128)(2,1)S(1)}, u32[]{:S(2)}, u32[]{:S(2)}) collective-permute-start(bf16[4,384,256]{2,1,0:T(8,128)(2,1)S(1)} %stack_columns.3.refs_0_), channel_id=1, source_target_pairs={{0,2},{1,3},{2,0},{3,1},{4,6},{5,7},{6,4},{7,5},{8,10},{9,11},{10,... | collective-permute-start | bytes 2359304 | tf_op jit(solution)/shard_map/ppermute | solution.py:440
  119.1 30.1 %collective-permute-start.27 = (bf16[1024,512]{1,0:T(8,128)(2,1)S(1)}, bf16[1024,512]{1,0:T(8,128)(2,1)S(1)}, u32[]{:S(2)}, u32[]{:S(2)}) collective-permute-start(bf16[1024,512]{1,0:T(8,128)(2,1)S(1)} %pick.1.refs_3_), channel_id=1, source_target_pairs={{8,12},{4,0},{9,13},{5,1},{10,14},{6,2},{11,15},{7,3},{24,28},{20,... | collective-permute-start | bytes 3145736 | tf_op jit(solution)/shard_map/ppermute | solution.py:497
  120.3 18.0 %collective-permute-start.24 = (bf16[4,384,256]{2,1,0:T(8,128)(2,1)S(1)}, bf16[4,384,256]{2,1,0:T(8,128)(2,1)S(1)}, u32[]{:S(2)}, u32[]{:S(2)}) collective-permute-start(bf16[4,384,256]{2,1,0:T(8,128)(2,1)S(1)} %stack_columns.3.refs_0_), channel_id=1, source_target_pairs={{0,1},{1,0},{2,3},{3,2},{4,5},{5,4},{6,7},{7,6},{8,9},{9,8},{10,11... | collective-permute-start | bytes 2359304 | tf_op jit(solution)/shard_map/ppermute | solution.py:440
  138.1 11.0 %collective-permute-start.26 = (bf16[4,384,256]{2,1,0:T(8,128)(2,1)S(1)}, bf16[4,384,256]{2,1,0:T(8,128)(2,1)S(1)}, u32[]{:S(2)}, u32[]{:S(2)}) collective-permute-start(bf16[4,384,256]{2,1,0:T(8,128)(2,1)S(1)} %collective-permute-done.25.refs_2_), channel_id=1, source_target_pairs={{0,1},{1,0},{2,3},{3,2},{4,5},{5,4},{6,7},{7,6},{8,9},{9,8},{10,11... | collective-permute-start | bytes 2359304 | tf_op jit(solution)/shard_map/ppermute | solution.py:440
  138.2 18.6 %collective-permute-start.18 = (bf16[160,512]{1,0:T(8,128)(2,1)S(1)}, bf16[160,512]{1,0:T(8,128)(2,1)S(1)}, u32[]{:S(2)}, u32[]{:S(2)}) collective-permute-start(bf16[160,512]{1,0:T(8,128)(2,1)S(1)} %get-tuple-element.53), channel_id=1, source_target_pairs={{0,8},{4,12},{8,0},{12,4},{1,9},{5,13},{9,1},{13,5},{2,10},{6,14},... | collective-permute-start | bytes 491528 | tf_op jit(solution)/shard_map/ppermute | solution.py:440

commit v14 on v13

--- a/solution.py
+++ b/solution.py
@@ -643,7 +643,7 @@
     )
     steps.append(chain_step(*steps[0], "ep", n, 2))
     got = swap(send, "sub", m, 1)
-    after = [*steps[0], down_made]
+    after = list(steps[0])
     bit = 2
     while bit < m:
         keep, send = halve(keep, got)
@@ -651,6 +651,7 @@
         got = swap(send, "sub", m, bit)
         bit *= 2
 
+    got = gate([got], [down_made])[0]
     *pieces, grad_part = pl.pallas_call(
         functools.partial(pre_kernel, z),
         grid_spec=pltpu.PrefetchScalarGridSpec(
@@ -724,7 +725,8 @@
             name="sum_parts",
         )(*keep, *got)
         keep = parts[::2]
-        got = [swap(part, "ep", n, bit) for part in parts[1::2]]
+        send = gate(parts[1::2], gathered[1:])
+        got = [swap(part, "ep", n, bit) for part in send]
         bit *= 2
 
     grad_in, in_made = total_call(

time: 158 us -> 143 us (0.905)
  waiting for transfers between devices: 81.1 us -> 67.3 us
    ppermute x23, waiting for transfers between devices: 64.9 us -> 53.7 us  [swap(): return lax.ppermute(x, axis, [(i, i ^ bit) for i in range(size)])]
    ppermute x1, waiting for transfers between devices: 10.9 us -> 7.44 us  [chain_step(): got = lax.ppermute(go, axis, rights + lefts)]
  transfers between devices with their start and end apart: 28 -> 28, of which waited for: 12 -> 12; matrix products, arithmetic and copies ran while one was open for 1% -> 1% of each run, Pallas kernels for 21% -> 24%
where the time goes in v14:
time: 143 us
  waiting for transfers between devices  67.3 us (47%)
  Pallas kernels  36.8 us (26%)
  starting transfers between devices  35 us (24%)
  local copies, waits for them, and re-layouts  2.16 us (2%)
  between operations  1.68 us (1%)
    ppermute x23, waiting for transfers between devices, swap(): return lax.ppermute(x, axis, [(i, i ^ bit) for i in range(size)])  53.7 us
    ppermute x23, starting transfers between devices, swap(): return lax.ppermute(x, axis, [(i, i ^ bit) for i in range(size)])  25.7 us
    pallas_call x2, Pallas kernels, total_call(): pl.pallas_call(functools.partial(kernel, z), grid_spec=pltpu.PrefetchScal...  15.5 us
    pallas_call x1, Pallas kernels, body(): pl.pallas_call(functools.partial(row_kernel, z), grid_spec=pltpu.Prefetch...  8.31 us
    ppermute x4, starting transfers between devices, chain_step(): return (lax.ppermute(go, axis, rights), lax.ppermute(back, axis, lefts))  8.03 us
    ppermute x1, waiting for transfers between devices, chain_step(): got = lax.ppermute(go, axis, rights + lefts)  7.44 us
    pallas_call x1, Pallas kernels, body(): pl.pallas_call(functools.partial(down_kernel, z), grid_spec=pltpu.Prefetc...  6.4 us
    ppermute x4, waiting for transfers between devices, chain_step(): return (lax.ppermute(go, axis, rights), lax.ppermute(back, axis, lefts))  6.14 us
  transfers between devices with their start and end apart: 28, of which 12 were waited for; matrix products, arithmetic and copies ran while one was open for 1% of the time, Pallas kernels for 24%

profile of v14, /device:TPU:0, one launch (start us, length us, event | category | flops | bytes accessed | tf_op | source)
XLA Modules:
  0.0 143.0 jit_solution(11730998936177379482)
XLA Ops:
  1.4 2.0 %route.1.refs_1_.refs_0_ = bf16[144,512]{1,0:T(8,128)(2,1)} custom-call(s32[1]{0:T(128)S(6)} %copy.38.count_ref, bf16[128,512]{1,0:T(8,128)(2,1)} %grad_ref.1, bf16[8,128]{1,0:T(8,128)(2,1)} %bitcast.22, s32[8,128]{1,0:T(8,128)} %bitcast.18, s32[8,128]{1,0:T(8,128)} %bitcast.20, s32[4,16]{1,0:T(4,128)} %bitcast.14), custom_call_target="tpu_custom_call" | custom-call | tf_op jit(solution)/shard_map/route/pallas_call | solution.py:525
  3.5 3.0 %collective-permute-start = (bf16[144,512]{1,0:T(8,128)(2,1)}, bf16[144,512]{1,0:T(8,128)(2,1)S(1)}, u32[]{:S(2)}, u32[]{:S(2)}) collective-permute-start(bf16[144,512]{1,0:T(8,128)(2,1)} %route.1.refs_1_.refs_0_), channel_id=1, source_target_pairs={{0,4},{4,0},{8,12},{12,8},{1,5},{5,1},{9,13},{13,9},{2,6},{6,2},{1... | collective-permute-start | bytes 442376 | tf_op jit(solution)/shard_map/ppermute | solution.py:440
  6.5 2.5 %collective-permute-start.2 = (bf16[144,512]{1,0:T(8,128)(2,1)}, bf16[144,512]{1,0:T(8,128)(2,1)S(1)}, u32[]{:S(2)}, u32[]{:S(2)}) collective-permute-start(bf16[144,512]{1,0:T(8,128)(2,1)} %route.1.refs_1_.refs_0_), channel_id=1, source_target_pairs={{0,12},{4,8},{8,4},{12,0},{1,13},{5,9},{9,5},{13,1},{2,14},{6,10},... | collective-permute-start | bytes 442376 | tf_op jit(solution)/shard_map/ppermute | solution.py:440
  9.0 0.1 collective-permute-start.1
  9.1 0.1 pad_add_fusion.ids_ref
  9.2 1.2 copy.26.refs_0_
  10.4 0.9 copy-done.2
  11.3 1.1 hidden_columns.1
  12.4 2.0 %collective-permute-start.4 = (bf16[192,256]{1,0:T(8,128)(2,1)S(1)}, bf16[192,256]{1,0:T(8,128)(2,1)S(1)}, u32[]{:S(2)}, u32[]{:S(2)}) collective-permute-start(bf16[192,256]{1,0:T(8,128)(2,1)S(1)} %get-tuple-element.41), channel_id=1, source_target_pairs={{0,4},{4,0},{8,12},{12,8},{1,5},{5,1},{9,13},{13,9},{2,6},{6,2},{1... | collective-permute-start | bytes 294920 | tf_op jit(solution)/shard_map/ppermute | solution.py:440
  14.4 4.0 %collective-permute-start.5 = (bf16[192,256]{1,0:T(8,128)(2,1)S(1)}, bf16[192,256]{1,0:T(8,128)(2,1)S(1)}, u32[]{:S(2)}, u32[]{:S(2)}) collective-permute-start(bf16[192,256]{1,0:T(8,128)(2,1)S(1)} %get-tuple-element.42), channel_id=1, source_target_pairs={{0,8},{4,12},{8,0},{12,4},{1,9},{5,13},{9,1},{13,5},{2,10},{6,14},... | collective-permute-start | bytes 294920 | tf_op jit(solution)/shard_map/ppermute | solution.py:440
  18.4 9.4 %collective-permute-done.1.refs_2_ = bf16[144,512]{1,0:T(8,128)(2,1)} collective-permute-done((bf16[144,512]{1,0:T(8,128)(2,1)}, bf16[144,512]{1,0:T(8,128)(2,1)}, u32[]{:S(2)}, u32[]{:S(2)}) %collective-permute-start.1) | collective-permute-done | bytes 147488 | tf_op jit(solution)/shard_map/ppermute | solution.py:440
  27.8 1.9 %collective-permute-done.5.refs_5_.refs_2_ = bf16[192,256]{1,0:T(8,128)(2,1)S(1)} collective-permute-done((bf16[192,256]{1,0:T(8,128)(2,1)S(1)}, bf16[192,256]{1,0:T(8,128)(2,1)S(1)}, u32[]{:S(2)}, u32[]{:S(2)}) %collective-permute-start.5) | collective-permute-done | bytes 98336 | tf_op jit(solution)/shard_map/ppermute | solution.py:440
  29.8 1.4 collective-permute-start.8
  31.2 4.6 %collective-permute-start.7 = (bf16[1024,512]{1,0:T(8,128)(2,1)S(1)}, bf16[1024,512]{1,0:T(8,128)(2,1)S(1)}, u32[]{:S(2)}, u32[]{:S(2)}) collective-permute-start(bf16[1024,512]{1,0:T(8,128)(2,1)S(1)} %gate.10), channel_id=1, source_target_pairs={{0,4},{4,8},{8,12},{1,5},{5,9},{9,13},{2,6},{6,10},{10,14},{3,7},{... | collective-permute-start | bytes 3145736 | tf_op jit(solution)/shard_map/ppermute | solution.py:499
  35.8 6.4 %hidden_partials.1 = (bf16[2,256,768]{2,1,0:T(8,128)(2,1)S(1)}, bf16[2,256,768]{2,1,0:T(8,128)(2,1)S(1)}, bf16[4,128,512]{2,1,0:T(8,128)(2,1)S(1)}, f32[4,64,128]{2,1,0:T(8,128)S(1)}) custom-call(s32[2]{0:T(128)S(1)} %pad_add_fusion.ids_ref, bf16[144,512]{1,0:T(8,128)(2,1)S(1)} %copy-done.3, bf16[144,512]{1,0:T(8,128)(2,1)S(1)} %collective-permute-done.after_ref.refs_1_, ...), custom_call_target="tpu_custom_call" | custom-call | tf_op jit(solution)/shard_map/hidden_partials/pallas_call | solution.py:587
  42.2 0.1 collective-permute-start.3
  42.3 2.5 %collective-permute-start.11 = (bf16[4,192,256]{2,1,0:T(8,128)(2,1)S(1)}, bf16[4,192,256]{2,1,0:T(8,128)(2,1)S(1)}, u32[]{:S(2)}, u32[]{:S(2)}) collective-permute-start(bf16[4,192,256]{2,1,0:T(8,128)(2,1)S(1)} %stack_columns.2.refs_0_), channel_id=1, source_target_pairs={{0,2},{1,3},{2,0},{3,1},{4,6},{5,7},{6,4},{7,5},{8,10},{9,11},{10,... | collective-permute-start | bytes 1179656 | tf_op jit(solution)/shard_map/ppermute | solution.py:440
  44.8 0.2 collective-permute-start.10
  45.0 9.6 %collective-permute-done.11.refs_2_ = bf16[4,192,256]{2,1,0:T(8,128)(2,1)S(1)} collective-permute-done((bf16[4,192,256]{2,1,0:T(8,128)(2,1)S(1)}, bf16[4,192,256]{2,1,0:T(8,128)(2,1)S(1)}, u32[]{:S(2)}, u32[]{:S(2)}) %collective-permute-start.11) | collective-permute-done | bytes 393248 | tf_op jit(solution)/shard_map/ppermute | solution.py:440
  54.6 0.2 halve.1
  54.8 0.6 collective-permute-done.8.refs_2_.refs_4_.refs_8_
  55.4 1.2 collective-permute-done.7.refs_1_.refs_5_
  56.6 1.5 %collective-permute-start.9 = (bf16[1,256,768]{2,1,0:T(8,128)(2,1)S(1)}, bf16[1,256,768]{2,1,0:T(8,128)(2,1)S(1)}, u32[]{:S(2)}, u32[]{:S(2)}) collective-permute-start(bf16[1,256,768]{2,1,0:T(8,128)(2,1)S(1)} %gate.11), channel_id=1, source_target_pairs={{0,2},{1,3},{2,0},{3,1},{4,6},{5,7},{6,4},{7,5},{8,10},{9,11},{10,... | collective-permute-start | bytes 1179656 | tf_op jit(solution)/shard_map/ppermute | solution.py:440
  58.1 1.3 collective-permute-start.19
  59.4 0.7 collective-permute-start.18
  60.2 7.8 %down_grads.1 = (bf16[16,192,512]{2,1,0:T(8,128)(2,1)}, f32[8,128]{1,0:T(8,128)S(1)}) custom-call(s32[2]{0:T(128)S(1)} %pad_add_fusion.ids_ref, s32[4,16]{1,0:T(4,128)S(1)} %bitcast.15, bf16[4,192,256]{2,1,0:T(8,128)(2,1)S(1)} %stack_columns.2.refs_0_, bf16[4,192,256]{2,1,0:T(8,128)(2,1)S(1)} %collective-permute-done.10.refs_1_, ...), custom_call_target="tpu_custom_call" | custom-call | tf_op jit(solution)/shard_map/down_grads/pallas_call | solution.py:613
  68.0 1.6 %pre_grads.1 = (bf16[384,256]{1,0:T(8,128)(2,1)S(1)}, bf16[384,256]{1,0:T(8,128)(2,1)S(1)}, bf16[384,256]{1,0:T(8,128)(2,1)S(1)}, bf16[384,256]{1,0:T(8,128)(2,1)S(1)}, bf16[256,768]{1,0:T(8,128)(2,1)S(1)}) custom-call(s32[2]{0:T(128)S(1)} %pad_add_fusion.ids_ref, bf16[1,256,768]{2,1,0:T(8,128)(2,1)S(1)} %get-tuple-element.39.keep_ref, ...), custom_call_target="tpu_custom_call" | custom-call | tf_op jit(solution)/shard_map/pre_grads/pallas_call | solution.py:655
  69.6 0.6 collective-permute-start.14
  70.2 9.2 %collective-permute-done.14.refs_2_ = bf16[256,768]{1,0:T(8,128)(2,1)S(1)} collective-permute-done((bf16[256,768]{1,0:T(8,128)(2,1)S(1)}, bf16[256,768]{1,0:T(8,128)(2,1)S(1)}, u32[]{:S(2)}, u32[]{:S(2)}) %collective-permute-start.14) | collective-permute-done | bytes 393248 | tf_op jit(solution)/shard_map/ppermute | solution.py:440
  79.5 4.3 %collective-permute-done.19.refs_4_.refs_1_ = bf16[1024,512]{1,0:T(8,128)(2,1)S(1)} collective-permute-done((bf16[1024,512]{1,0:T(8,128)(2,1)S(1)}, bf16[1024,512]{1,0:T(8,128)(2,1)S(1)}, u32[]{:S(2)}, u32[]{:S(2)}) %collective-permute-start.19) | collective-permute-done | bytes 1048608 | tf_op jit(solution)/shard_map/ppermute | solution.py:499
  83.8 2.8 %collective-permute-start.20 = (bf16[384,256]{1,0:T(8,128)(2,1)S(1)}, bf16[384,256]{1,0:T(8,128)(2,1)S(1)}, u32[]{:S(2)}, u32[]{:S(2)}) collective-permute-start(bf16[384,256]{1,0:T(8,128)(2,1)S(1)} %get-tuple-element.57), channel_id=1, source_target_pairs={{0,4},{4,0},{8,12},{12,8},{1,5},{5,1},{9,13},{13,9},{2,6},{6,2},{1... | collective-permute-start | bytes 589832 | tf_op jit(solution)/shard_map/ppermute | solution.py:440
  86.6 2.8 %collective-permute-start.21 = (bf16[384,256]{1,0:T(8,128)(2,1)S(1)}, bf16[384,256]{1,0:T(8,128)(2,1)S(1)}, u32[]{:S(2)}, u32[]{:S(2)}) collective-permute-start(bf16[384,256]{1,0:T(8,128)(2,1)S(1)} %get-tuple-element.58), channel_id=1, source_target_pairs={{0,8},{4,12},{8,0},{12,4},{1,9},{5,13},{9,1},{13,5},{2,10},{6,14},... | collective-permute-start | bytes 589832 | tf_op jit(solution)/shard_map/ppermute | solution.py:440
  89.4 0.6 collective-permute-start.22
  90.0 8.3 %row_grads.1 = (bf16[160,512]{1,0:T(8,128)(2,1)S(1)}, bf16[160,512]{1,0:T(8,128)(2,1)S(1)}, bf16[160,512]{1,0:T(8,128)(2,1)S(1)}, bf16[160,512]{1,0:T(8,128)(2,1)S(1)}) custom-call(s32[2]{0:T(128)S(1)} %pad_add_fusion.ids_ref, bf16[256,768]{1,0:T(8,128)(2,1)S(1)} %get-tuple-element.47.refs_0_, bf16[256,768]{1,0:T(8,128)(2,1)S(1)} %collective-permute-done.13.refs_1_, ...), custom_call_target="tpu_custom_call" | custom-call | tf_op jit(solution)/shard_map/row_grads/pallas_call | solution.py:679
  98.3 0.6 collective-permute-start.16
  99.0 1.4 %collective-permute-start.17 = (bf16[160,512]{1,0:T(8,128)(2,1)S(1)}, bf16[160,512]{1,0:T(8,128)(2,1)S(1)}, u32[]{:S(2)}, u32[]{:S(2)}) collective-permute-start(bf16[160,512]{1,0:T(8,128)(2,1)S(1)} %get-tuple-element.51), channel_id=1, source_target_pairs={{0,4},{4,0},{8,12},{12,8},{1,5},{5,1},{9,13},{13,9},{2,6},{6,2},{1... | collective-permute-start | bytes 491528 | tf_op jit(solution)/shard_map/ppermute | solution.py:440
  100.4 1.7 %collective-permute-done.21.refs_3_.refs_2_ = bf16[384,256]{1,0:T(8,128)(2,1)S(1)} collective-permute-done((bf16[384,256]{1,0:T(8,128)(2,1)S(1)}, bf16[384,256]{1,0:T(8,128)(2,1)S(1)}, u32[]{:S(2)}, u32[]{:S(2)}) %collective-permute-start.21) | collective-permute-done | bytes 196640 | tf_op jit(solution)/shard_map/ppermute | solution.py:440
  102.1 0.6 pick.1.refs_3_
  102.7 2.9 %collective-permute-done.16.refs_2_.refs_1_ = bf16[160,512]{1,0:T(8,128)(2,1)S(1)} collective-permute-done((bf16[160,512]{1,0:T(8,128)(2,1)S(1)}, bf16[160,512]{1,0:T(8,128)(2,1)S(1)}, u32[]{:S(2)}, u32[]{:S(2)}) %collective-permute-start.16) | collective-permute-done | bytes 163872 | tf_op jit(solution)/shard_map/ppermute | solution.py:440
  105.6 2.4 %collective-permute-done.17.refs_3_.refs_2_ = bf16[160,512]{1,0:T(8,128)(2,1)S(1)} collective-permute-done((bf16[160,512]{1,0:T(8,128)(2,1)S(1)}, bf16[160,512]{1,0:T(8,128)(2,1)S(1)}, u32[]{:S(2)}, u32[]{:S(2)}) %collective-permute-start.17) | collective-permute-done | bytes 163872 | tf_op jit(solution)/shard_map/ppermute | solution.py:440
  108.0 0.6 collective-permute-start.26
  108.7 1.3 collective-permute-start.23
  110.0 16.5 %collective-permute-done.26.refs_2_ = bf16[4,384,256]{2,1,0:T(8,128)(2,1)S(1)} collective-permute-done((bf16[4,384,256]{2,1,0:T(8,128)(2,1)S(1)}, bf16[4,384,256]{2,1,0:T(8,128)(2,1)S(1)}, u32[]{:S(2)}, u32[]{:S(2)}) %collective-permute-start.26) | collective-permute-done | bytes 786464 | tf_op jit(solution)/shard_map/ppermute | solution.py:440
  126.6 0.1 sum_parts.1
  126.6 7.4 %collective-permute-done.23.refs_3_.refs_6_.refs_7_.refs_10_ = bf16[1024,512]{1,0:T(8,128)(2,1)S(1)} collective-permute-done((bf16[1024,512]{1,0:T(8,128)(2,1)S(1)}, bf16[1024,512]{1,0:T(8,128)(2,1)S(1)}, u32[]{:S(2)}, u32[]{:S(2)}) %collective-permute-start.23) | collective-permute-done | bytes 1048608 | tf_op jit(solution)/shard_map/ppermute | solution.py:497
  134.1 0.3 collective-permute-start.24
  134.4 7.7 %in_grads.1 = (bf16[16,384,512]{2,1,0:T(8,128)(2,1)}, f32[8,128]{1,0:T(8,128)S(1)}) custom-call(s32[2]{0:T(128)S(1)} %pad_add_fusion.ids_ref, s32[4,16]{1,0:T(4,128)S(1)} %bitcast.16, bf16[4,384,256]{2,1,0:T(8,128)(2,1)S(1)} %stack_columns.3.refs_0_, bf16[4,384,256]{2,1,0:T(8,128)(2,1)S(1)} %collective-permute-done.25.refs_1_, ...), custom_call_target="tpu_custom_call" | custom-call | tf_op jit(solution)/shard_map/in_grads/pallas_call | solution.py:613
  142.2 0.8 token_grads.1
  (46 shorter events, 0.2 us)
Async XLA Ops:
  0.6 10.7 %copy-start = (bf16[8,128,1536]{2,1,0:T(8,128)(2,1)S(1)}, bf16[8,128,1536]{2,1,0:T(8,128)(2,1)}, u32[]{:S(2)}) copy-start(bf16[8,128,1536]{2,1,0:T(8,128)(2,1)} %param.17) | copy-start | bytes 9437188
  3.5 7.8 %collective-permute-start = (bf16[144,512]{1,0:T(8,128)(2,1)}, bf16[144,512]{1,0:T(8,128)(2,1)S(1)}, u32[]{:S(2)}, u32[]{:S(2)}) collective-permute-start(bf16[144,512]{1,0:T(8,128)(2,1)} %route.1.refs_1_.refs_0_), channel_id=1, source_target_pairs={{0,4},{4,0},{8,12},{12,8},{1,5},{5,1},{9,13},{13,9},{2,6},{6,2},{1... | collective-permute-start | bytes 442376 | tf_op jit(solution)/shard_map/ppermute | solution.py:440
  6.5 11.9 %collective-permute-start.2 = (bf16[144,512]{1,0:T(8,128)(2,1)}, bf16[144,512]{1,0:T(8,128)(2,1)S(1)}, u32[]{:S(2)}, u32[]{:S(2)}) collective-permute-start(bf16[144,512]{1,0:T(8,128)(2,1)} %route.1.refs_1_.refs_0_), channel_id=1, source_target_pairs={{0,12},{4,8},{8,4},{12,0},{1,13},{5,9},{9,5},{13,1},{2,14},{6,10},... | collective-permute-start | bytes 442376 | tf_op jit(solution)/shard_map/ppermute | solution.py:440
  9.0 18.8 %collective-permute-start.1 = (bf16[144,512]{1,0:T(8,128)(2,1)}, bf16[144,512]{1,0:T(8,128)(2,1)}, u32[]{:S(2)}, u32[]{:S(2)}) collective-permute-start(bf16[144,512]{1,0:T(8,128)(2,1)} %route.1.refs_1_.refs_0_), channel_id=1, source_target_pairs={{0,8},{4,12},{8,0},{12,4},{1,9},{5,13},{9,1},{13,5},{2,10},{6,14},... | collective-permute-start | bytes 442376 | tf_op jit(solution)/shard_map/ppermute | solution.py:440
  10.4 0.9 copy-start.2
  11.3 24.5 %copy-start.3 = (bf16[144,512]{1,0:T(8,128)(2,1)S(1)}, bf16[144,512]{1,0:T(8,128)(2,1)}, u32[]{:S(2)}) copy-start(bf16[144,512]{1,0:T(8,128)(2,1)} %route.1.refs_1_.refs_0_) | copy-start | bytes 442372
  12.4 15.4 %collective-permute-start.4 = (bf16[192,256]{1,0:T(8,128)(2,1)S(1)}, bf16[192,256]{1,0:T(8,128)(2,1)S(1)}, u32[]{:S(2)}, u32[]{:S(2)}) collective-permute-start(bf16[192,256]{1,0:T(8,128)(2,1)S(1)} %get-tuple-element.41), channel_id=1, source_target_pairs={{0,4},{4,0},{8,12},{12,8},{1,5},{5,1},{9,13},{13,9},{2,6},{6,2},{1... | collective-permute-start | bytes 294920 | tf_op jit(solution)/shard_map/ppermute | solution.py:440
  14.4 15.4 %collective-permute-start.5 = (bf16[192,256]{1,0:T(8,128)(2,1)S(1)}, bf16[192,256]{1,0:T(8,128)(2,1)S(1)}, u32[]{:S(2)}, u32[]{:S(2)}) collective-permute-start(bf16[192,256]{1,0:T(8,128)(2,1)S(1)} %get-tuple-element.42), channel_id=1, source_target_pairs={{0,8},{4,12},{8,0},{12,4},{1,9},{5,13},{9,1},{13,5},{2,10},{6,14},... | collective-permute-start | bytes 294920 | tf_op jit(solution)/shard_map/ppermute | solution.py:440
  18.4 11.4 %collective-permute-start.6 = (bf16[192,256]{1,0:T(8,128)(2,1)S(1)}, bf16[192,256]{1,0:T(8,128)(2,1)S(1)}, u32[]{:S(2)}, u32[]{:S(2)}) collective-permute-start(bf16[192,256]{1,0:T(8,128)(2,1)S(1)} %get-tuple-element.43), channel_id=1, source_target_pairs={{0,12},{4,8},{8,4},{12,0},{1,13},{5,9},{9,5},{13,1},{2,14},{6,10},... | collective-permute-start | bytes 294920 | tf_op jit(solution)/shard_map/ppermute | solution.py:440
  29.8 30.4 %copy-start.4 = (s32[16,4]{0,1:T(4,128)S(1)}, s32[16,4]{0,1:T(4,128)}, u32[]{:S(2)}) copy-start(s32[16,4]{0,1:T(4,128)} %param.14) | copy-start | bytes 772
  29.8 25.7 %collective-permute-start.8 = (bf16[1024,512]{1,0:T(8,128)(2,1)S(1)}, bf16[1024,512]{1,0:T(8,128)(2,1)S(1)}, u32[]{:S(2)}, u32[]{:S(2)}) collective-permute-start(bf16[1024,512]{1,0:T(8,128)(2,1)S(1)} %gate.10), channel_id=1, source_target_pairs={{12,8},{8,4},{4,0},{13,9},{9,5},{5,1},{14,10},{10,6},{6,2},{15,11}... | collective-permute-start | bytes 3145736 | tf_op jit(solution)/shard_map/ppermute | solution.py:499
  31.2 25.4 %collective-permute-start.7 = (bf16[1024,512]{1,0:T(8,128)(2,1)S(1)}, bf16[1024,512]{1,0:T(8,128)(2,1)S(1)}, u32[]{:S(2)}, u32[]{:S(2)}) collective-permute-start(bf16[1024,512]{1,0:T(8,128)(2,1)S(1)} %gate.10), channel_id=1, source_target_pairs={{0,4},{4,8},{8,12},{1,5},{5,9},{9,13},{2,6},{6,10},{10,14},{3,7},{... | collective-permute-start | bytes 3145736 | tf_op jit(solution)/shard_map/ppermute | solution.py:499
  42.2 12.4 %collective-permute-start.3 = (bf16[2,256,768]{2,1,0:T(8,128)(2,1)S(1)}, bf16[2,256,768]{2,1,0:T(8,128)(2,1)S(1)}, u32[]{:S(2)}, u32[]{:S(2)}) collective-permute-start(bf16[2,256,768]{2,1,0:T(8,128)(2,1)S(1)} %get-tuple-element.38), channel_id=1, source_target_pairs={{0,1},{1,0},{2,3},{3,2},{4,5},{5,4},{6,7},{7,6},{8,9},{9,8},{10,11... | collective-permute-start | bytes 2359304 | tf_op jit(solution)/shard_map/ppermute | solution.py:440
  42.3 12.3 %collective-permute-start.11 = (bf16[4,192,256]{2,1,0:T(8,128)(2,1)S(1)}, bf16[4,192,256]{2,1,0:T(8,128)(2,1)S(1)}, u32[]{:S(2)}, u32[]{:S(2)}) collective-permute-start(bf16[4,192,256]{2,1,0:T(8,128)(2,1)S(1)} %stack_columns.2.refs_0_), channel_id=1, source_target_pairs={{0,2},{1,3},{2,0},{3,1},{4,6},{5,7},{6,4},{7,5},{8,10},{9,11},{10,... | collective-permute-start | bytes 1179656 | tf_op jit(solution)/shard_map/ppermute | solution.py:440
  44.8 15.3 %collective-permute-start.10 = (bf16[4,192,256]{2,1,0:T(8,128)(2,1)S(1)}, bf16[4,192,256]{2,1,0:T(8,128)(2,1)S(1)}, u32[]{:S(2)}, u32[]{:S(2)}) collective-permute-start(bf16[4,192,256]{2,1,0:T(8,128)(2,1)S(1)} %stack_columns.2.refs_0_), channel_id=1, source_target_pairs={{0,1},{1,0},{2,3},{3,2},{4,5},{5,4},{6,7},{7,6},{8,9},{9,8},{10,11... | collective-permute-start | bytes 1179656 | tf_op jit(solution)/shard_map/ppermute | solution.py:440
  54.6 5.5 %collective-permute-start.12 = (bf16[4,192,256]{2,1,0:T(8,128)(2,1)S(1)}, bf16[4,192,256]{2,1,0:T(8,128)(2,1)S(1)}, u32[]{:S(2)}, u32[]{:S(2)}) collective-permute-start(bf16[4,192,256]{2,1,0:T(8,128)(2,1)S(1)} %collective-permute-done.11.refs_2_), channel_id=1, source_target_pairs={{0,1},{1,0},{2,3},{3,2},{4,5},{5,4},{6,7},{7,6},{8,9},{9,8},{10,11... | collective-permute-start | bytes 1179656 | tf_op jit(solution)/shard_map/ppermute | solution.py:440
  56.6 11.4 %collective-permute-start.9 = (bf16[1,256,768]{2,1,0:T(8,128)(2,1)S(1)}, bf16[1,256,768]{2,1,0:T(8,128)(2,1)S(1)}, u32[]{:S(2)}, u32[]{:S(2)}) collective-permute-start(bf16[1,256,768]{2,1,0:T(8,128)(2,1)S(1)} %gate.11), channel_id=1, source_target_pairs={{0,2},{1,3},{2,0},{3,1},{4,6},{5,7},{6,4},{7,5},{8,10},{9,11},{10,... | collective-permute-start | bytes 1179656 | tf_op jit(solution)/shard_map/ppermute | solution.py:440
  58.1 25.7 %collective-permute-start.19 = (bf16[1024,512]{1,0:T(8,128)(2,1)S(1)}, bf16[1024,512]{1,0:T(8,128)(2,1)S(1)}, u32[]{:S(2)}, u32[]{:S(2)}) collective-permute-start(bf16[1024,512]{1,0:T(8,128)(2,1)S(1)} %collective-permute-done.8.refs_2_.refs_4_.refs_8_), channel_id=1, source_target_pairs={{8,4},{4,0},{9,5},{5,1},{10,6},{6,2},{11,7},{7,3},{24,20},{20,16},... | collective-permute-start | bytes 3145736 | tf_op jit(solution)/shard_map/ppermute | solution.py:499
  59.4 24.4 %collective-permute-start.18 = (bf16[1024,512]{1,0:T(8,128)(2,1)S(1)}, bf16[1024,512]{1,0:T(8,128)(2,1)S(1)}, u32[]{:S(2)}, u32[]{:S(2)}) collective-permute-start(bf16[1024,512]{1,0:T(8,128)(2,1)S(1)} %collective-permute-done.7.refs_1_.refs_5_), channel_id=1, source_target_pairs={{4,8},{8,12},{5,9},{9,13},{6,10},{10,14},{7,11},{11,15},{20,24},{2... | collective-permute-start | bytes 3145736 | tf_op jit(solution)/shard_map/ppermute | solution.py:499
  69.6 9.8 %collective-permute-start.14 = (bf16[256,768]{1,0:T(8,128)(2,1)S(1)}, bf16[256,768]{1,0:T(8,128)(2,1)S(1)}, u32[]{:S(2)}, u32[]{:S(2)}) collective-permute-start(bf16[256,768]{1,0:T(8,128)(2,1)S(1)} %get-tuple-element.47.refs_0_), channel_id=1, source_target_pairs={{0,2},{1,3},{2,0},{3,1},{4,6},{5,7},{6,4},{7,5},{8,10},{9,11},{10,... | collective-permute-start | bytes 1179656 | tf_op jit(solution)/shard_map/ppermute | solution.py:440
  70.2 19.7 %collective-permute-start.13 = (bf16[256,768]{1,0:T(8,128)(2,1)S(1)}, bf16[256,768]{1,0:T(8,128)(2,1)S(1)}, u32[]{:S(2)}, u32[]{:S(2)}) collective-permute-start(bf16[256,768]{1,0:T(8,128)(2,1)S(1)} %get-tuple-element.47.refs_0_), channel_id=1, source_target_pairs={{0,1},{1,0},{2,3},{3,2},{4,5},{5,4},{6,7},{7,6},{8,9},{9,8},{10,11... | collective-permute-start | bytes 1179656 | tf_op jit(solution)/shard_map/ppermute | solution.py:440
  79.5 10.5 %collective-permute-start.15 = (bf16[256,768]{1,0:T(8,128)(2,1)S(1)}, bf16[256,768]{1,0:T(8,128)(2,1)S(1)}, u32[]{:S(2)}, u32[]{:S(2)}) collective-permute-start(bf16[256,768]{1,0:T(8,128)(2,1)S(1)} %collective-permute-done.14.refs_2_), channel_id=1, source_target_pairs={{0,1},{1,0},{2,3},{3,2},{4,5},{5,4},{6,7},{7,6},{8,9},{9,8},{10,11... | collective-permute-start | bytes 1179656 | tf_op jit(solution)/shard_map/ppermute | solution.py:440
  83.8 16.6 %collective-permute-start.20 = (bf16[384,256]{1,0:T(8,128)(2,1)S(1)}, bf16[384,256]{1,0:T(8,128)(2,1)S(1)}, u32[]{:S(2)}, u32[]{:S(2)}) collective-permute-start(bf16[384,256]{1,0:T(8,128)(2,1)S(1)} %get-tuple-element.57), channel_id=1, source_target_pairs={{0,4},{4,0},{8,12},{12,8},{1,5},{5,1},{9,13},{13,9},{2,6},{6,2},{1... | collective-permute-start | bytes 589832 | tf_op jit(solution)/shard_map/ppermute | solution.py:440
  86.6 15.5 %collective-permute-start.21 = (bf16[384,256]{1,0:T(8,128)(2,1)S(1)}, bf16[384,256]{1,0:T(8,128)(2,1)S(1)}, u32[]{:S(2)}, u32[]{:S(2)}) collective-permute-start(bf16[384,256]{1,0:T(8,128)(2,1)S(1)} %get-tuple-element.58), channel_id=1, source_target_pairs={{0,8},{4,12},{8,0},{12,4},{1,9},{5,13},{9,1},{13,5},{2,10},{6,14},... | collective-permute-start | bytes 589832 | tf_op jit(solution)/shard_map/ppermute | solution.py:440
  89.4 12.7 %collective-permute-start.22 = (bf16[384,256]{1,0:T(8,128)(2,1)S(1)}, bf16[384,256]{1,0:T(8,128)(2,1)S(1)}, u32[]{:S(2)}, u32[]{:S(2)}) collective-permute-start(bf16[384,256]{1,0:T(8,128)(2,1)S(1)} %get-tuple-element.59), channel_id=1, source_target_pairs={{0,12},{4,8},{8,4},{12,0},{1,13},{5,9},{9,5},{13,1},{2,14},{6,10},... | collective-permute-start | bytes 589832 | tf_op jit(solution)/shard_map/ppermute | solution.py:440
  98.3 7.3 %collective-permute-start.16 = (bf16[160,512]{1,0:T(8,128)(2,1)S(1)}, bf16[160,512]{1,0:T(8,128)(2,1)S(1)}, u32[]{:S(2)}, u32[]{:S(2)}) collective-permute-start(bf16[160,512]{1,0:T(8,128)(2,1)S(1)} %get-tuple-element.50), channel_id=1, source_target_pairs={{0,4},{4,0},{8,12},{12,8},{1,5},{5,1},{9,13},{13,9},{2,6},{6,2},{1... | collective-permute-start | bytes 491528 | tf_op jit(solution)/shard_map/ppermute | solution.py:440
  99.0 9.0 %collective-permute-start.17 = (bf16[160,512]{1,0:T(8,128)(2,1)S(1)}, bf16[160,512]{1,0:T(8,128)(2,1)S(1)}, u32[]{:S(2)}, u32[]{:S(2)}) collective-permute-start(bf16[160,512]{1,0:T(8,128)(2,1)S(1)} %get-tuple-element.51), channel_id=1, source_target_pairs={{0,4},{4,0},{8,12},{12,8},{1,5},{5,1},{9,13},{13,9},{2,6},{6,2},{1... | collective-permute-start | bytes 491528 | tf_op jit(solution)/shard_map/ppermute | solution.py:440
  102.1 32.3 %copy-start.1 = (bf16[8,4,32,512]{3,2,1,0:T(8,128)(2,1)S(1)}, bf16[8,4,32,512]{3,2,1,0:T(8,128)(2,1)}, u32[]{:S(2)}) copy-start(bf16[8,4,32,512]{3,2,1,0:T(8,128)(2,1)} %param.16) | copy-start | bytes 3145732
  108.0 18.5 %collective-permute-start.26 = (bf16[4,384,256]{2,1,0:T(8,128)(2,1)S(1)}, bf16[4,384,256]{2,1,0:T(8,128)(2,1)S(1)}, u32[]{:S(2)}, u32[]{:S(2)}) collective-permute-start(bf16[4,384,256]{2,1,0:T(8,128)(2,1)S(1)} %stack_columns.3.refs_0_), channel_id=1, source_target_pairs={{0,2},{1,3},{2,0},{3,1},{4,6},{5,7},{6,4},{7,5},{8,10},{9,11},{10,... | collective-permute-start | bytes 2359304 | tf_op jit(solution)/shard_map/ppermute | solution.py:440
  108.7 25.4 %collective-permute-start.23 = (bf16[1024,512]{1,0:T(8,128)(2,1)S(1)}, bf16[1024,512]{1,0:T(8,128)(2,1)S(1)}, u32[]{:S(2)}, u32[]{:S(2)}) collective-permute-start(bf16[1024,512]{1,0:T(8,128)(2,1)S(1)} %pick.1.refs_3_), channel_id=1, source_target_pairs={{8,12},{4,0},{9,13},{5,1},{10,14},{6,2},{11,15},{7,3},{24,28},{20,... | collective-permute-start | bytes 3145736 | tf_op jit(solution)/shard_map/ppermute | solution.py:497
  109.9 24.4 %collective-permute-start.25 = (bf16[4,384,256]{2,1,0:T(8,128)(2,1)S(1)}, bf16[4,384,256]{2,1,0:T(8,128)(2,1)S(1)}, u32[]{:S(2)}, u32[]{:S(2)}) collective-permute-start(bf16[4,384,256]{2,1,0:T(8,128)(2,1)S(1)} %stack_columns.3.refs_0_), channel_id=1, source_target_pairs={{0,1},{1,0},{2,3},{3,2},{4,5},{5,4},{6,7},{7,6},{8,9},{9,8},{10,11... | collective-permute-start | bytes 2359304 | tf_op jit(solution)/shard_map/ppermute | solution.py:440
  126.6 7.8 %collective-permute-start.27 = (bf16[4,384,256]{2,1,0:T(8,128)(2,1)S(1)}, bf16[4,384,256]{2,1,0:T(8,128)(2,1)S(1)}, u32[]{:S(2)}, u32[]{:S(2)}) collective-permute-start(bf16[4,384,256]{2,1,0:T(8,128)(2,1)S(1)} %collective-permute-done.26.refs_2_), channel_id=1, source_target_pairs={{0,1},{1,0},{2,3},{3,2},{4,5},{5,4},{6,7},{7,6},{8,9},{9,8},{10,11... | collective-permute-start | bytes 2359304 | tf_op jit(solution)/shard_map/ppermute | solution.py:440
  134.1 8.1 %copy-start.5 = (s32[128,8]{0,1:T(8,128)S(1)}, s32[128,8]{0,1:T(8,128)}, u32[]{:S(2)}) copy-start(s32[128,8]{0,1:T(8,128)} %param.12) | copy-start | bytes 12292
  134.1 8.1 %copy-start.6 = (s32[128,8]{0,1:T(8,128)S(1)}, s32[128,8]{0,1:T(8,128)}, u32[]{:S(2)}) copy-start(s32[128,8]{0,1:T(8,128)} %param.13) | copy-start | bytes 12292
  134.1 8.0 %collective-permute-start.24 = (bf16[160,512]{1,0:T(8,128)(2,1)S(1)}, bf16[160,512]{1,0:T(8,128)(2,1)S(1)}, u32[]{:S(2)}, u32[]{:S(2)}) collective-permute-start(bf16[160,512]{1,0:T(8,128)(2,1)S(1)} %gate.15), channel_id=1, source_target_pairs={{0,8},{4,12},{8,0},{12,4},{1,9},{5,13},{9,1},{13,5},{2,10},{6,14},... | collective-permute-start | bytes 491528 | tf_op jit(solution)/shard_map/ppermute | solution.py:440

commit v15 on v14

--- a/solution.py
+++ b/solution.py
@@ -671,8 +671,8 @@
         compiler_params=params(16),
         name="pre_grads",
     )(ids, keep, got, pair_rows, codes)
-    late = gate(pieces[1:], steps[1])
-    pieces = pieces[:1] + [swap(a, "ep", n, k) for k, a in enumerate(late, 1)]
+    late = gate(pieces[2:], steps[1])
+    pieces = pieces[:1] + [swap(a, "ep", n, k) for k, a in enumerate([pieces[1], *late], 1)]
     grad_parts = spread_over({0: grad_part}, "sub", m, m // 2)
 
     back_shape = (z.tokens + z.slots, z.width)

time: 143 us -> 145 us (1.014)
  starting transfers between devices: 35 us -> 41.1 us
  waiting for transfers between devices: 67.3 us -> 63.2 us
    ppermute x23, starting transfers between devices: 25.7 us -> 31.8 us  [swap(): return lax.ppermute(x, axis, [(i, i ^ bit) for i in range(size)])]
    ppermute x4, waiting for transfers between devices: 6.14 us -> 1.82 us  [chain_step(): return (lax.ppermute(go, axis, rights), lax.ppermute(back, axis, lefts))]
  transfers between devices with their start and end apart: 28 -> 28, of which waited for: 12 -> 11; matrix products, arithmetic and copies ran while one was open for 1% -> 1% of each run, Pallas kernels for 24% -> 23%
where the time goes in v15:
time: 145 us
  waiting for transfers between devices  63.2 us (44%)
  starting transfers between devices  41.1 us (28%)
  Pallas kernels  36.7 us (25%)
  local copies, waits for them, and re-layouts  2.16 us (1%)
  between operations  1.68 us (1%)
    ppermute x23, waiting for transfers between devices, swap(): return lax.ppermute(x, axis, [(i, i ^ bit) for i in range(size)])  54 us
    ppermute x23, starting transfers between devices, swap(): return lax.ppermute(x, axis, [(i, i ^ bit) for i in range(size)])  31.8 us
    pallas_call x2, Pallas kernels, total_call(): pl.pallas_call(functools.partial(kernel, z), grid_spec=pltpu.PrefetchScal...  15.5 us
    pallas_call x1, Pallas kernels, body(): pl.pallas_call(functools.partial(row_kernel, z), grid_spec=pltpu.Prefetch...  8.25 us
    ppermute x4, starting transfers between devices, chain_step(): return (lax.ppermute(go, axis, rights), lax.ppermute(back, axis, lefts))  8.03 us
    ppermute x1, waiting for transfers between devices, chain_step(): got = lax.ppermute(go, axis, rights + lefts)  7.44 us
    pallas_call x1, Pallas kernels, body(): pl.pallas_call(functools.partial(down_kernel, z), grid_spec=pltpu.Prefetc...  6.4 us
  transfers between devices with their start and end apart: 28, of which 11 were waited for; matrix products, arithmetic and copies ran while one was open for 1% of the time, Pallas kernels for 23%

profile of v15, /device:TPU:0, one launch (start us, length us, event | category | flops | bytes accessed | tf_op | source)
XLA Modules:
  0.0 145.0 jit_solution(7780351815473289379)
XLA Ops:
  1.4 2.0 %route.1.refs_1_.refs_0_ = bf16[144,512]{1,0:T(8,128)(2,1)} custom-call(s32[1]{0:T(128)S(6)} %copy.36.count_ref, bf16[128,512]{1,0:T(8,128)(2,1)} %grad_ref.1, bf16[8,128]{1,0:T(8,128)(2,1)} %bitcast.22, s32[8,128]{1,0:T(8,128)} %bitcast.18, s32[8,128]{1,0:T(8,128)} %bitcast.20, s32[4,16]{1,0:T(4,128)} %bitcast.14), custom_call_target="tpu_custom_call" | custom-call | tf_op jit(solution)/shard_map/route/pallas_call | solution.py:525
  3.5 3.0 %collective-permute-start = (bf16[144,512]{1,0:T(8,128)(2,1)}, bf16[144,512]{1,0:T(8,128)(2,1)S(1)}, u32[]{:S(2)}, u32[]{:S(2)}) collective-permute-start(bf16[144,512]{1,0:T(8,128)(2,1)} %route.1.refs_1_.refs_0_), channel_id=1, source_target_pairs={{0,4},{4,0},{8,12},{12,8},{1,5},{5,1},{9,13},{13,9},{2,6},{6,2},{1... | collective-permute-start | bytes 442376 | tf_op jit(solution)/shard_map/ppermute | solution.py:440
  6.5 2.5 %collective-permute-start.2 = (bf16[144,512]{1,0:T(8,128)(2,1)}, bf16[144,512]{1,0:T(8,128)(2,1)S(1)}, u32[]{:S(2)}, u32[]{:S(2)}) collective-permute-start(bf16[144,512]{1,0:T(8,128)(2,1)} %route.1.refs_1_.refs_0_), channel_id=1, source_target_pairs={{0,12},{4,8},{8,4},{12,0},{1,13},{5,9},{9,5},{13,1},{2,14},{6,10},... | collective-permute-start | bytes 442376 | tf_op jit(solution)/shard_map/ppermute | solution.py:440
  9.0 0.1 collective-permute-start.1
  9.1 0.1 pad_add_fusion.ids_ref
  9.2 1.2 copy.25.refs_0_
  10.4 0.9 copy-done.2
  11.3 1.1 hidden_columns.1
  12.4 2.0 %collective-permute-start.4 = (bf16[192,256]{1,0:T(8,128)(2,1)S(1)}, bf16[192,256]{1,0:T(8,128)(2,1)S(1)}, u32[]{:S(2)}, u32[]{:S(2)}) collective-permute-start(bf16[192,256]{1,0:T(8,128)(2,1)S(1)} %get-tuple-element.40), channel_id=1, source_target_pairs={{0,4},{4,0},{8,12},{12,8},{1,5},{5,1},{9,13},{13,9},{2,6},{6,2},{1... | collective-permute-start | bytes 294920 | tf_op jit(solution)/shard_map/ppermute | solution.py:440
  14.4 4.0 %collective-permute-start.5 = (bf16[192,256]{1,0:T(8,128)(2,1)S(1)}, bf16[192,256]{1,0:T(8,128)(2,1)S(1)}, u32[]{:S(2)}, u32[]{:S(2)}) collective-permute-start(bf16[192,256]{1,0:T(8,128)(2,1)S(1)} %get-tuple-element.41), channel_id=1, source_target_pairs={{0,8},{4,12},{8,0},{12,4},{1,9},{5,13},{9,1},{13,5},{2,10},{6,14},... | collective-permute-start | bytes 294920 | tf_op jit(solution)/shard_map/ppermute | solution.py:440
  18.4 9.4 %collective-permute-done.1.refs_2_ = bf16[144,512]{1,0:T(8,128)(2,1)} collective-permute-done((bf16[144,512]{1,0:T(8,128)(2,1)}, bf16[144,512]{1,0:T(8,128)(2,1)}, u32[]{:S(2)}, u32[]{:S(2)}) %collective-permute-start.1) | collective-permute-done | bytes 147488 | tf_op jit(solution)/shard_map/ppermute | solution.py:440
  27.8 1.9 %collective-permute-done.5.refs_5_.refs_2_ = bf16[192,256]{1,0:T(8,128)(2,1)S(1)} collective-permute-done((bf16[192,256]{1,0:T(8,128)(2,1)S(1)}, bf16[192,256]{1,0:T(8,128)(2,1)S(1)}, u32[]{:S(2)}, u32[]{:S(2)}) %collective-permute-start.5) | collective-permute-done | bytes 98336 | tf_op jit(solution)/shard_map/ppermute | solution.py:440
  29.8 1.4 collective-permute-start.8
  31.2 4.6 %collective-permute-start.7 = (bf16[1024,512]{1,0:T(8,128)(2,1)S(1)}, bf16[1024,512]{1,0:T(8,128)(2,1)S(1)}, u32[]{:S(2)}, u32[]{:S(2)}) collective-permute-start(bf16[1024,512]{1,0:T(8,128)(2,1)S(1)} %gate.10), channel_id=1, source_target_pairs={{0,4},{4,8},{8,12},{1,5},{5,9},{9,13},{2,6},{6,10},{10,14},{3,7},{... | collective-permute-start | bytes 3145736 | tf_op jit(solution)/shard_map/ppermute | solution.py:499
  35.8 6.4 %hidden_partials.1 = (bf16[2,256,768]{2,1,0:T(8,128)(2,1)S(1)}, bf16[2,256,768]{2,1,0:T(8,128)(2,1)S(1)}, bf16[4,128,512]{2,1,0:T(8,128)(2,1)S(1)}, f32[4,64,128]{2,1,0:T(8,128)S(1)}) custom-call(s32[2]{0:T(128)S(1)} %pad_add_fusion.ids_ref, bf16[144,512]{1,0:T(8,128)(2,1)S(1)} %copy-done.3, bf16[144,512]{1,0:T(8,128)(2,1)S(1)} %collective-permute-done.after_ref.refs_1_, ...), custom_call_target="tpu_custom_call" | custom-call | tf_op jit(solution)/shard_map/hidden_partials/pallas_call | solution.py:587
  42.2 0.1 collective-permute-start.3
  42.3 2.5 %collective-permute-start.11 = (bf16[4,192,256]{2,1,0:T(8,128)(2,1)S(1)}, bf16[4,192,256]{2,1,0:T(8,128)(2,1)S(1)}, u32[]{:S(2)}, u32[]{:S(2)}) collective-permute-start(bf16[4,192,256]{2,1,0:T(8,128)(2,1)S(1)} %stack_columns.2.refs_0_), channel_id=1, source_target_pairs={{0,2},{1,3},{2,0},{3,1},{4,6},{5,7},{6,4},{7,5},{8,10},{9,11},{10,... | collective-permute-start | bytes 1179656 | tf_op jit(solution)/shard_map/ppermute | solution.py:440
  44.8 0.2 collective-permute-start.10
  45.0 9.6 %collective-permute-done.11.refs_2_ = bf16[4,192,256]{2,1,0:T(8,128)(2,1)S(1)} collective-permute-done((bf16[4,192,256]{2,1,0:T(8,128)(2,1)S(1)}, bf16[4,192,256]{2,1,0:T(8,128)(2,1)S(1)}, u32[]{:S(2)}, u32[]{:S(2)}) %collective-permute-start.11) | collective-permute-done | bytes 393248 | tf_op jit(solution)/shard_map/ppermute | solution.py:440
  54.6 0.2 halve.1
  54.8 0.6 collective-permute-done.8.refs_2_.refs_4_.refs_8_
  55.4 1.2 collective-permute-done.7.refs_1_.refs_5_
  56.6 1.5 %collective-permute-start.9 = (bf16[1,256,768]{2,1,0:T(8,128)(2,1)S(1)}, bf16[1,256,768]{2,1,0:T(8,128)(2,1)S(1)}, u32[]{:S(2)}, u32[]{:S(2)}) collective-permute-start(bf16[1,256,768]{2,1,0:T(8,128)(2,1)S(1)} %gate.11), channel_id=1, source_target_pairs={{0,2},{1,3},{2,0},{3,1},{4,6},{5,7},{6,4},{7,5},{8,10},{9,11},{10,... | collective-permute-start | bytes 1179656 | tf_op jit(solution)/shard_map/ppermute | solution.py:440
  58.1 1.3 collective-permute-start.19
  59.4 0.7 collective-permute-start.18
  60.2 7.8 %down_grads.1 = (bf16[16,192,512]{2,1,0:T(8,128)(2,1)}, f32[8,128]{1,0:T(8,128)S(1)}) custom-call(s32[2]{0:T(128)S(1)} %pad_add_fusion.ids_ref, s32[4,16]{1,0:T(4,128)S(1)} %bitcast.15, bf16[4,192,256]{2,1,0:T(8,128)(2,1)S(1)} %stack_columns.2.refs_0_, bf16[4,192,256]{2,1,0:T(8,128)(2,1)S(1)} %collective-permute-done.10.refs_1_, ...), custom_call_target="tpu_custom_call" | custom-call | tf_op jit(solution)/shard_map/down_grads/pallas_call | solution.py:613
  68.0 1.6 %pre_grads.1 = (bf16[384,256]{1,0:T(8,128)(2,1)S(1)}, bf16[384,256]{1,0:T(8,128)(2,1)S(1)}, bf16[384,256]{1,0:T(8,128)(2,1)S(1)}, bf16[384,256]{1,0:T(8,128)(2,1)S(1)}, bf16[256,768]{1,0:T(8,128)(2,1)S(1)}) custom-call(s32[2]{0:T(128)S(1)} %pad_add_fusion.ids_ref, bf16[1,256,768]{2,1,0:T(8,128)(2,1)S(1)} %get-tuple-element.38.keep_ref, ...), custom_call_target="tpu_custom_call" | custom-call | tf_op jit(solution)/shard_map/pre_grads/pallas_call | solution.py:655
  69.7 0.6 collective-permute-start.14
  70.3 9.2 %collective-permute-done.14.refs_2_ = bf16[256,768]{1,0:T(8,128)(2,1)S(1)} collective-permute-done((bf16[256,768]{1,0:T(8,128)(2,1)S(1)}, bf16[256,768]{1,0:T(8,128)(2,1)S(1)}, u32[]{:S(2)}, u32[]{:S(2)}) %collective-permute-start.14) | collective-permute-done | bytes 393248 | tf_op jit(solution)/shard_map/ppermute | solution.py:440
  79.5 4.9 %collective-permute-start.20 = (bf16[384,256]{1,0:T(8,128)(2,1)S(1)}, bf16[384,256]{1,0:T(8,128)(2,1)S(1)}, u32[]{:S(2)}, u32[]{:S(2)}) collective-permute-start(bf16[384,256]{1,0:T(8,128)(2,1)S(1)} %get-tuple-element.53), channel_id=1, source_target_pairs={{0,4},{4,0},{8,12},{12,8},{1,5},{5,1},{9,13},{13,9},{2,6},{6,2},{1... | collective-permute-start | bytes 589832 | tf_op jit(solution)/shard_map/ppermute | solution.py:440
  84.4 4.1 %collective-permute-start.21 = (bf16[384,256]{1,0:T(8,128)(2,1)S(1)}, bf16[384,256]{1,0:T(8,128)(2,1)S(1)}, u32[]{:S(2)}, u32[]{:S(2)}) collective-permute-start(bf16[384,256]{1,0:T(8,128)(2,1)S(1)} %get-tuple-element.56), channel_id=1, source_target_pairs={{0,8},{4,12},{8,0},{12,4},{1,9},{5,13},{9,1},{13,5},{2,10},{6,14},... | collective-permute-start | bytes 589832 | tf_op jit(solution)/shard_map/ppermute | solution.py:440
  88.6 1.0 collective-permute-start.22
  89.6 8.2 %row_grads.1 = (bf16[160,512]{1,0:T(8,128)(2,1)S(1)}, bf16[160,512]{1,0:T(8,128)(2,1)S(1)}, bf16[160,512]{1,0:T(8,128)(2,1)S(1)}, bf16[160,512]{1,0:T(8,128)(2,1)S(1)}) custom-call(s32[2]{0:T(128)S(1)} %pad_add_fusion.ids_ref, bf16[256,768]{1,0:T(8,128)(2,1)S(1)} %get-tuple-element.46.refs_0_, bf16[256,768]{1,0:T(8,128)(2,1)S(1)} %collective-permute-done.13.refs_1_, ...), custom_call_target="tpu_custom_call" | custom-call | tf_op jit(solution)/shard_map/row_grads/pallas_call | solution.py:679
  97.8 0.7 collective-permute-start.16
  98.5 1.4 collective-permute-start.17
  99.9 2.9 %collective-permute-done.21.refs_3_.refs_2_ = bf16[384,256]{1,0:T(8,128)(2,1)S(1)} collective-permute-done((bf16[384,256]{1,0:T(8,128)(2,1)S(1)}, bf16[384,256]{1,0:T(8,128)(2,1)S(1)}, u32[]{:S(2)}, u32[]{:S(2)}) %collective-permute-start.21) | collective-permute-done | bytes 196640 | tf_op jit(solution)/shard_map/ppermute | solution.py:440
  102.8 0.6 pick.1.refs_3_
  103.5 2.2 %collective-permute-done.16.refs_2_.refs_1_ = bf16[160,512]{1,0:T(8,128)(2,1)S(1)} collective-permute-done((bf16[160,512]{1,0:T(8,128)(2,1)S(1)}, bf16[160,512]{1,0:T(8,128)(2,1)S(1)}, u32[]{:S(2)}, u32[]{:S(2)}) %collective-permute-start.16) | collective-permute-done | bytes 163872 | tf_op jit(solution)/shard_map/ppermute | solution.py:440
  105.7 2.4 %collective-permute-done.17.refs_3_.refs_2_ = bf16[160,512]{1,0:T(8,128)(2,1)S(1)} collective-permute-done((bf16[160,512]{1,0:T(8,128)(2,1)S(1)}, bf16[160,512]{1,0:T(8,128)(2,1)S(1)}, u32[]{:S(2)}, u32[]{:S(2)}) %collective-permute-start.17) | collective-permute-done | bytes 163872 | tf_op jit(solution)/shard_map/ppermute | solution.py:440
  108.2 0.9 collective-permute-start.26
  109.1 1.3 collective-permute-start.23
  110.4 0.1 collective-permute-start.25
  110.5 16.2 %collective-permute-done.26.refs_2_ = bf16[4,384,256]{2,1,0:T(8,128)(2,1)S(1)} collective-permute-done((bf16[4,384,256]{2,1,0:T(8,128)(2,1)S(1)}, bf16[4,384,256]{2,1,0:T(8,128)(2,1)S(1)}, u32[]{:S(2)}, u32[]{:S(2)}) %collective-permute-start.26) | collective-permute-done | bytes 786464 | tf_op jit(solution)/shard_map/ppermute | solution.py:440
  126.7 0.1 sum_parts.1
  126.8 7.4 %collective-permute-done.23.refs_3_.refs_6_.refs_7_.refs_10_ = bf16[1024,512]{1,0:T(8,128)(2,1)S(1)} collective-permute-done((bf16[1024,512]{1,0:T(8,128)(2,1)S(1)}, bf16[1024,512]{1,0:T(8,128)(2,1)S(1)}, u32[]{:S(2)}, u32[]{:S(2)}) %collective-permute-start.23) | collective-permute-done | bytes 1048608 | tf_op jit(solution)/shard_map/ppermute | solution.py:497
  134.2 2.2 %collective-permute-start.24 = (bf16[160,512]{1,0:T(8,128)(2,1)S(1)}, bf16[160,512]{1,0:T(8,128)(2,1)S(1)}, u32[]{:S(2)}, u32[]{:S(2)}) collective-permute-start(bf16[160,512]{1,0:T(8,128)(2,1)S(1)} %gate.15), channel_id=1, source_target_pairs={{0,8},{4,12},{8,0},{12,4},{1,9},{5,13},{9,1},{13,5},{2,10},{6,14},... | collective-permute-start | bytes 491528 | tf_op jit(solution)/shard_map/ppermute | solution.py:440
  136.4 7.7 %in_grads.1 = (bf16[16,384,512]{2,1,0:T(8,128)(2,1)}, f32[8,128]{1,0:T(8,128)S(1)}) custom-call(s32[2]{0:T(128)S(1)} %pad_add_fusion.ids_ref, s32[4,16]{1,0:T(4,128)S(1)} %bitcast.16, bf16[4,384,256]{2,1,0:T(8,128)(2,1)S(1)} %stack_columns.3.refs_0_, bf16[4,384,256]{2,1,0:T(8,128)(2,1)S(1)} %collective-permute-done.25.refs_1_, ...), custom_call_target="tpu_custom_call" | custom-call | tf_op jit(solution)/shard_map/in_grads/pallas_call | solution.py:613
  144.2 0.8 token_grads.1
  (46 shorter events, 0.2 us)
Async XLA Ops:
  0.6 10.7 %copy-start = (bf16[8,128,1536]{2,1,0:T(8,128)(2,1)S(1)}, bf16[8,128,1536]{2,1,0:T(8,128)(2,1)}, u32[]{:S(2)}) copy-start(bf16[8,128,1536]{2,1,0:T(8,128)(2,1)} %param.17) | copy-start | bytes 9437188
  3.5 7.8 %collective-permute-start = (bf16[144,512]{1,0:T(8,128)(2,1)}, bf16[144,512]{1,0:T(8,128)(2,1)S(1)}, u32[]{:S(2)}, u32[]{:S(2)}) collective-permute-start(bf16[144,512]{1,0:T(8,128)(2,1)} %route.1.refs_1_.refs_0_), channel_id=1, source_target_pairs={{0,4},{4,0},{8,12},{12,8},{1,5},{5,1},{9,13},{13,9},{2,6},{6,2},{1... | collective-permute-start | bytes 442376 | tf_op jit(solution)/shard_map/ppermute | solution.py:440
  6.5 11.9 %collective-permute-start.2 = (bf16[144,512]{1,0:T(8,128)(2,1)}, bf16[144,512]{1,0:T(8,128)(2,1)S(1)}, u32[]{:S(2)}, u32[]{:S(2)}) collective-permute-start(bf16[144,512]{1,0:T(8,128)(2,1)} %route.1.refs_1_.refs_0_), channel_id=1, source_target_pairs={{0,12},{4,8},{8,4},{12,0},{1,13},{5,9},{9,5},{13,1},{2,14},{6,10},... | collective-permute-start | bytes 442376 | tf_op jit(solution)/shard_map/ppermute | solution.py:440
  9.0 18.8 %collective-permute-start.1 = (bf16[144,512]{1,0:T(8,128)(2,1)}, bf16[144,512]{1,0:T(8,128)(2,1)}, u32[]{:S(2)}, u32[]{:S(2)}) collective-permute-start(bf16[144,512]{1,0:T(8,128)(2,1)} %route.1.refs_1_.refs_0_), channel_id=1, source_target_pairs={{0,8},{4,12},{8,0},{12,4},{1,9},{5,13},{9,1},{13,5},{2,10},{6,14},... | collective-permute-start | bytes 442376 | tf_op jit(solution)/shard_map/ppermute | solution.py:440
  10.4 0.9 copy-start.2
  11.3 24.5 %copy-start.3 = (bf16[144,512]{1,0:T(8,128)(2,1)S(1)}, bf16[144,512]{1,0:T(8,128)(2,1)}, u32[]{:S(2)}) copy-start(bf16[144,512]{1,0:T(8,128)(2,1)} %route.1.refs_1_.refs_0_) | copy-start | bytes 442372
  12.4 15.4 %collective-permute-start.4 = (bf16[192,256]{1,0:T(8,128)(2,1)S(1)}, bf16[192,256]{1,0:T(8,128)(2,1)S(1)}, u32[]{:S(2)}, u32[]{:S(2)}) collective-permute-start(bf16[192,256]{1,0:T(8,128)(2,1)S(1)} %get-tuple-element.40), channel_id=1, source_target_pairs={{0,4},{4,0},{8,12},{12,8},{1,5},{5,1},{9,13},{13,9},{2,6},{6,2},{1... | collective-permute-start | bytes 294920 | tf_op jit(solution)/shard_map/ppermute | solution.py:440
  14.4 15.4 %collective-permute-start.5 = (bf16[192,256]{1,0:T(8,128)(2,1)S(1)}, bf16[192,256]{1,0:T(8,128)(2,1)S(1)}, u32[]{:S(2)}, u32[]{:S(2)}) collective-permute-start(bf16[192,256]{1,0:T(8,128)(2,1)S(1)} %get-tuple-element.41), channel_id=1, source_target_pairs={{0,8},{4,12},{8,0},{12,4},{1,9},{5,13},{9,1},{13,5},{2,10},{6,14},... | collective-permute-start | bytes 294920 | tf_op jit(solution)/shard_map/ppermute | solution.py:440
  18.4 11.4 %collective-permute-start.6 = (bf16[192,256]{1,0:T(8,128)(2,1)S(1)}, bf16[192,256]{1,0:T(8,128)(2,1)S(1)}, u32[]{:S(2)}, u32[]{:S(2)}) collective-permute-start(bf16[192,256]{1,0:T(8,128)(2,1)S(1)} %get-tuple-element.42), channel_id=1, source_target_pairs={{0,12},{4,8},{8,4},{12,0},{1,13},{5,9},{9,5},{13,1},{2,14},{6,10},... | collective-permute-start | bytes 294920 | tf_op jit(solution)/shard_map/ppermute | solution.py:440
  29.8 30.4 %copy-start.4 = (s32[16,4]{0,1:T(4,128)S(1)}, s32[16,4]{0,1:T(4,128)}, u32[]{:S(2)}) copy-start(s32[16,4]{0,1:T(4,128)} %param.14) | copy-start | bytes 772
  29.8 25.7 %collective-permute-start.8 = (bf16[1024,512]{1,0:T(8,128)(2,1)S(1)}, bf16[1024,512]{1,0:T(8,128)(2,1)S(1)}, u32[]{:S(2)}, u32[]{:S(2)}) collective-permute-start(bf16[1024,512]{1,0:T(8,128)(2,1)S(1)} %gate.10), channel_id=1, source_target_pairs={{12,8},{8,4},{4,0},{13,9},{9,5},{5,1},{14,10},{10,6},{6,2},{15,11}... | collective-permute-start | bytes 3145736 | tf_op jit(solution)/shard_map/ppermute | solution.py:499
  31.2 25.4 %collective-permute-start.7 = (bf16[1024,512]{1,0:T(8,128)(2,1)S(1)}, bf16[1024,512]{1,0:T(8,128)(2,1)S(1)}, u32[]{:S(2)}, u32[]{:S(2)}) collective-permute-start(bf16[1024,512]{1,0:T(8,128)(2,1)S(1)} %gate.10), channel_id=1, source_target_pairs={{0,4},{4,8},{8,12},{1,5},{5,9},{9,13},{2,6},{6,10},{10,14},{3,7},{... | collective-permute-start | bytes 3145736 | tf_op jit(solution)/shard_map/ppermute | solution.py:499
  42.2 12.4 %collective-permute-start.3 = (bf16[2,256,768]{2,1,0:T(8,128)(2,1)S(1)}, bf16[2,256,768]{2,1,0:T(8,128)(2,1)S(1)}, u32[]{:S(2)}, u32[]{:S(2)}) collective-permute-start(bf16[2,256,768]{2,1,0:T(8,128)(2,1)S(1)} %get-tuple-element.37), channel_id=1, source_target_pairs={{0,1},{1,0},{2,3},{3,2},{4,5},{5,4},{6,7},{7,6},{8,9},{9,8},{10,11... | collective-permute-start | bytes 2359304 | tf_op jit(solution)/shard_map/ppermute | solution.py:440
  42.3 12.3 %collective-permute-start.11 = (bf16[4,192,256]{2,1,0:T(8,128)(2,1)S(1)}, bf16[4,192,256]{2,1,0:T(8,128)(2,1)S(1)}, u32[]{:S(2)}, u32[]{:S(2)}) collective-permute-start(bf16[4,192,256]{2,1,0:T(8,128)(2,1)S(1)} %stack_columns.2.refs_0_), channel_id=1, source_target_pairs={{0,2},{1,3},{2,0},{3,1},{4,6},{5,7},{6,4},{7,5},{8,10},{9,11},{10,... | collective-permute-start | bytes 1179656 | tf_op jit(solution)/shard_map/ppermute | solution.py:440
  44.8 15.3 %collective-permute-start.10 = (bf16[4,192,256]{2,1,0:T(8,128)(2,1)S(1)}, bf16[4,192,256]{2,1,0:T(8,128)(2,1)S(1)}, u32[]{:S(2)}, u32[]{:S(2)}) collective-permute-start(bf16[4,192,256]{2,1,0:T(8,128)(2,1)S(1)} %stack_columns.2.refs_0_), channel_id=1, source_target_pairs={{0,1},{1,0},{2,3},{3,2},{4,5},{5,4},{6,7},{7,6},{8,9},{9,8},{10,11... | collective-permute-start | bytes 1179656 | tf_op jit(solution)/shard_map/ppermute | solution.py:440
  54.6 5.5 %collective-permute-start.12 = (bf16[4,192,256]{2,1,0:T(8,128)(2,1)S(1)}, bf16[4,192,256]{2,1,0:T(8,128)(2,1)S(1)}, u32[]{:S(2)}, u32[]{:S(2)}) collective-permute-start(bf16[4,192,256]{2,1,0:T(8,128)(2,1)S(1)} %collective-permute-done.11.refs_2_), channel_id=1, source_target_pairs={{0,1},{1,0},{2,3},{3,2},{4,5},{5,4},{6,7},{7,6},{8,9},{9,8},{10,11... | collective-permute-start | bytes 1179656 | tf_op jit(solution)/shard_map/ppermute | solution.py:440
  56.6 11.4 %collective-permute-start.9 = (bf16[1,256,768]{2,1,0:T(8,128)(2,1)S(1)}, bf16[1,256,768]{2,1,0:T(8,128)(2,1)S(1)}, u32[]{:S(2)}, u32[]{:S(2)}) collective-permute-start(bf16[1,256,768]{2,1,0:T(8,128)(2,1)S(1)} %gate.11), channel_id=1, source_target_pairs={{0,2},{1,3},{2,0},{3,1},{4,6},{5,7},{6,4},{7,5},{8,10},{9,11},{10,... | collective-permute-start | bytes 1179656 | tf_op jit(solution)/shard_map/ppermute | solution.py:440
  58.1 26.3 %collective-permute-start.19 = (bf16[1024,512]{1,0:T(8,128)(2,1)S(1)}, bf16[1024,512]{1,0:T(8,128)(2,1)S(1)}, u32[]{:S(2)}, u32[]{:S(2)}) collective-permute-start(bf16[1024,512]{1,0:T(8,128)(2,1)S(1)} %collective-permute-done.8.refs_2_.refs_4_.refs_8_), channel_id=1, source_target_pairs={{8,4},{4,0},{9,5},{5,1},{10,6},{6,2},{11,7},{7,3},{24,20},{20,16},... | collective-permute-start | bytes 3145736 | tf_op jit(solution)/shard_map/ppermute | solution.py:499
  59.4 25.1 %collective-permute-start.18 = (bf16[1024,512]{1,0:T(8,128)(2,1)S(1)}, bf16[1024,512]{1,0:T(8,128)(2,1)S(1)}, u32[]{:S(2)}, u32[]{:S(2)}) collective-permute-start(bf16[1024,512]{1,0:T(8,128)(2,1)S(1)} %collective-permute-done.7.refs_1_.refs_5_), channel_id=1, source_target_pairs={{4,8},{8,12},{5,9},{9,13},{6,10},{10,14},{7,11},{11,15},{20,24},{2... | collective-permute-start | bytes 3145736 | tf_op jit(solution)/shard_map/ppermute | solution.py:499
  69.7 9.8 %collective-permute-start.14 = (bf16[256,768]{1,0:T(8,128)(2,1)S(1)}, bf16[256,768]{1,0:T(8,128)(2,1)S(1)}, u32[]{:S(2)}, u32[]{:S(2)}) collective-permute-start(bf16[256,768]{1,0:T(8,128)(2,1)S(1)} %get-tuple-element.46.refs_0_), channel_id=1, source_target_pairs={{0,2},{1,3},{2,0},{3,1},{4,6},{5,7},{6,4},{7,5},{8,10},{9,11},{10,... | collective-permute-start | bytes 1179656 | tf_op jit(solution)/shard_map/ppermute | solution.py:440
  70.3 19.3 %collective-permute-start.13 = (bf16[256,768]{1,0:T(8,128)(2,1)S(1)}, bf16[256,768]{1,0:T(8,128)(2,1)S(1)}, u32[]{:S(2)}, u32[]{:S(2)}) collective-permute-start(bf16[256,768]{1,0:T(8,128)(2,1)S(1)} %get-tuple-element.46.refs_0_), channel_id=1, source_target_pairs={{0,1},{1,0},{2,3},{3,2},{4,5},{5,4},{6,7},{7,6},{8,9},{9,8},{10,11... | collective-permute-start | bytes 1179656 | tf_op jit(solution)/shard_map/ppermute | solution.py:440
  79.5 10.1 %collective-permute-start.15 = (bf16[256,768]{1,0:T(8,128)(2,1)S(1)}, bf16[256,768]{1,0:T(8,128)(2,1)S(1)}, u32[]{:S(2)}, u32[]{:S(2)}) collective-permute-start(bf16[256,768]{1,0:T(8,128)(2,1)S(1)} %collective-permute-done.14.refs_2_), channel_id=1, source_target_pairs={{0,1},{1,0},{2,3},{3,2},{4,5},{5,4},{6,7},{7,6},{8,9},{9,8},{10,11... | collective-permute-start | bytes 1179656 | tf_op jit(solution)/shard_map/ppermute | solution.py:440
  79.5 20.4 %collective-permute-start.20 = (bf16[384,256]{1,0:T(8,128)(2,1)S(1)}, bf16[384,256]{1,0:T(8,128)(2,1)S(1)}, u32[]{:S(2)}, u32[]{:S(2)}) collective-permute-start(bf16[384,256]{1,0:T(8,128)(2,1)S(1)} %get-tuple-element.53), channel_id=1, source_target_pairs={{0,4},{4,0},{8,12},{12,8},{1,5},{5,1},{9,13},{13,9},{2,6},{6,2},{1... | collective-permute-start | bytes 589832 | tf_op jit(solution)/shard_map/ppermute | solution.py:440
  84.4 18.4 %collective-permute-start.21 = (bf16[384,256]{1,0:T(8,128)(2,1)S(1)}, bf16[384,256]{1,0:T(8,128)(2,1)S(1)}, u32[]{:S(2)}, u32[]{:S(2)}) collective-permute-start(bf16[384,256]{1,0:T(8,128)(2,1)S(1)} %get-tuple-element.56), channel_id=1, source_target_pairs={{0,8},{4,12},{8,0},{12,4},{1,9},{5,13},{9,1},{13,5},{2,10},{6,14},... | collective-permute-start | bytes 589832 | tf_op jit(solution)/shard_map/ppermute | solution.py:440
  88.6 14.2 %collective-permute-start.22 = (bf16[384,256]{1,0:T(8,128)(2,1)S(1)}, bf16[384,256]{1,0:T(8,128)(2,1)S(1)}, u32[]{:S(2)}, u32[]{:S(2)}) collective-permute-start(bf16[384,256]{1,0:T(8,128)(2,1)S(1)} %get-tuple-element.57), channel_id=1, source_target_pairs={{0,12},{4,8},{8,4},{12,0},{1,13},{5,9},{9,5},{13,1},{2,14},{6,10},... | collective-permute-start | bytes 589832 | tf_op jit(solution)/shard_map/ppermute | solution.py:440
  97.8 7.9 %collective-permute-start.16 = (bf16[160,512]{1,0:T(8,128)(2,1)S(1)}, bf16[160,512]{1,0:T(8,128)(2,1)S(1)}, u32[]{:S(2)}, u32[]{:S(2)}) collective-permute-start(bf16[160,512]{1,0:T(8,128)(2,1)S(1)} %get-tuple-element.49), channel_id=1, source_target_pairs={{0,4},{4,0},{8,12},{12,8},{1,5},{5,1},{9,13},{13,9},{2,6},{6,2},{1... | collective-permute-start | bytes 491528 | tf_op jit(solution)/shard_map/ppermute | solution.py:440
  98.5 9.6 %collective-permute-start.17 = (bf16[160,512]{1,0:T(8,128)(2,1)S(1)}, bf16[160,512]{1,0:T(8,128)(2,1)S(1)}, u32[]{:S(2)}, u32[]{:S(2)}) collective-permute-start(bf16[160,512]{1,0:T(8,128)(2,1)S(1)} %get-tuple-element.50), channel_id=1, source_target_pairs={{0,4},{4,0},{8,12},{12,8},{1,5},{5,1},{9,13},{13,9},{2,6},{6,2},{1... | collective-permute-start | bytes 491528 | tf_op jit(solution)/shard_map/ppermute | solution.py:440
  102.8 33.6 %copy-start.1 = (bf16[8,4,32,512]{3,2,1,0:T(8,128)(2,1)S(1)}, bf16[8,4,32,512]{3,2,1,0:T(8,128)(2,1)}, u32[]{:S(2)}) copy-start(bf16[8,4,32,512]{3,2,1,0:T(8,128)(2,1)} %param.16) | copy-start | bytes 3145732
  108.2 18.5 %collective-permute-start.26 = (bf16[4,384,256]{2,1,0:T(8,128)(2,1)S(1)}, bf16[4,384,256]{2,1,0:T(8,128)(2,1)S(1)}, u32[]{:S(2)}, u32[]{:S(2)}) collective-permute-start(bf16[4,384,256]{2,1,0:T(8,128)(2,1)S(1)} %stack_columns.3.refs_0_), channel_id=1, source_target_pairs={{0,2},{1,3},{2,0},{3,1},{4,6},{5,7},{6,4},{7,5},{8,10},{9,11},{10,... | collective-permute-start | bytes 2359304 | tf_op jit(solution)/shard_map/ppermute | solution.py:440
  109.1 25.1 %collective-permute-start.23 = (bf16[1024,512]{1,0:T(8,128)(2,1)S(1)}, bf16[1024,512]{1,0:T(8,128)(2,1)S(1)}, u32[]{:S(2)}, u32[]{:S(2)}) collective-permute-start(bf16[1024,512]{1,0:T(8,128)(2,1)S(1)} %pick.1.refs_3_), channel_id=1, source_target_pairs={{8,12},{4,0},{9,13},{5,1},{10,14},{6,2},{11,15},{7,3},{24,28},{20,... | collective-permute-start | bytes 3145736 | tf_op jit(solution)/shard_map/ppermute | solution.py:497
  110.4 26.0 %collective-permute-start.25 = (bf16[4,384,256]{2,1,0:T(8,128)(2,1)S(1)}, bf16[4,384,256]{2,1,0:T(8,128)(2,1)S(1)}, u32[]{:S(2)}, u32[]{:S(2)}) collective-permute-start(bf16[4,384,256]{2,1,0:T(8,128)(2,1)S(1)} %stack_columns.3.refs_0_), channel_id=1, source_target_pairs={{0,1},{1,0},{2,3},{3,2},{4,5},{5,4},{6,7},{7,6},{8,9},{9,8},{10,11... | collective-permute-start | bytes 2359304 | tf_op jit(solution)/shard_map/ppermute | solution.py:440
  126.7 9.7 %collective-permute-start.27 = (bf16[4,384,256]{2,1,0:T(8,128)(2,1)S(1)}, bf16[4,384,256]{2,1,0:T(8,128)(2,1)S(1)}, u32[]{:S(2)}, u32[]{:S(2)}) collective-permute-start(bf16[4,384,256]{2,1,0:T(8,128)(2,1)S(1)} %collective-permute-done.26.refs_2_), channel_id=1, source_target_pairs={{0,1},{1,0},{2,3},{3,2},{4,5},{5,4},{6,7},{7,6},{8,9},{9,8},{10,11... | collective-permute-start | bytes 2359304 | tf_op jit(solution)/shard_map/ppermute | solution.py:440
  134.2 9.9 %copy-start.5 = (s32[128,8]{0,1:T(8,128)S(1)}, s32[128,8]{0,1:T(8,128)}, u32[]{:S(2)}) copy-start(s32[128,8]{0,1:T(8,128)} %param.12) | copy-start | bytes 12292
  134.2 9.9 %copy-start.6 = (s32[128,8]{0,1:T(8,128)S(1)}, s32[128,8]{0,1:T(8,128)}, u32[]{:S(2)}) copy-start(s32[128,8]{0,1:T(8,128)} %param.13) | copy-start | bytes 12292
  134.2 9.9 %collective-permute-start.24 = (bf16[160,512]{1,0:T(8,128)(2,1)S(1)}, bf16[160,512]{1,0:T(8,128)(2,1)S(1)}, u32[]{:S(2)}, u32[]{:S(2)}) collective-permute-start(bf16[160,512]{1,0:T(8,128)(2,1)S(1)} %gate.15), channel_id=1, source_target_pairs={{0,8},{4,12},{8,0},{12,4},{1,9},{5,13},{9,1},{13,5},{2,10},{6,14},... | collective-permute-start | bytes 491528 | tf_op jit(solution)/shard_map/ppermute | solution.py:440

commit v16 on v14

--- a/solution.py
+++ b/solution.py
@@ -725,7 +725,7 @@
             name="sum_parts",
         )(*keep, *got)
         keep = parts[::2]
-        send = gate(parts[1::2], gathered[1:])
+        send = gate(parts[1::2], sides[1:])
         got = [swap(part, "ep", n, bit) for part in send]
         bit *= 2
 

time: 143 us -> 144 us (level)
    ppermute x1, waiting for transfers between devices: 7.44 us -> 5.02 us  [chain_step(): got = lax.ppermute(go, axis, rights + lefts)]
    ppermute x23, waiting for transfers between devices: 53.7 us -> 55.9 us  [swap(): return lax.ppermute(x, axis, [(i, i ^ bit) for i in range(size)])]
  transfers between devices with their start and end apart: 28 -> 28, of which waited for: 12 -> 13; matrix products, arithmetic and copies ran while one was open for 1% -> 1% of each run, Pallas kernels for 24% -> 24%
where the time goes in v16:
time: 144 us; the launch traced here: 143 us
  waiting for transfers between devices  67 us (47%)
  Pallas kernels  36.8 us (26%)
  starting transfers between devices  35 us (24%)
  local copies, waits for them, and re-layouts  2.16 us (2%)
  between operations  1.69 us (1%)
    ppermute x23, waiting for transfers between devices, swap(): return lax.ppermute(x, axis, [(i, i ^ bit) for i in range(size)])  55.9 us
    ppermute x23, starting transfers between devices, swap(): return lax.ppermute(x, axis, [(i, i ^ bit) for i in range(size)])  25.7 us
    pallas_call x2, Pallas kernels, total_call(): pl.pallas_call(functools.partial(kernel, z), grid_spec=pltpu.PrefetchScal...  15.5 us
    pallas_call x1, Pallas kernels, body(): pl.pallas_call(functools.partial(row_kernel, z), grid_spec=pltpu.Prefetch...  8.29 us
    ppermute x4, starting transfers between devices, chain_step(): return (lax.ppermute(go, axis, rights), lax.ppermute(back, axis, lefts))  8.03 us
    pallas_call x1, Pallas kernels, body(): pl.pallas_call(functools.partial(down_kernel, z), grid_spec=pltpu.Prefetc...  6.4 us
    ppermute x4, waiting for transfers between devices, chain_step(): return (lax.ppermute(go, axis, rights), lax.ppermute(back, axis, lefts))  6.11 us
    ppermute x1, waiting for transfers between devices, chain_step(): got = lax.ppermute(go, axis, rights + lefts)  5.02 us
  transfers between devices with their start and end apart: 28, of which 13 were waited for; matrix products, arithmetic and copies ran while one was open for 1% of the time, Pallas kernels for 24%

profile of v16, /device:TPU:0, one launch (start us, length us, event | category | flops | bytes accessed | tf_op | source)
XLA Modules:
  0.0 142.7 jit_solution(3285487910765325238)
XLA Ops:
  1.4 2.0 %route.1.refs_1_.refs_0_ = bf16[144,512]{1,0:T(8,128)(2,1)} custom-call(s32[1]{0:T(128)S(6)} %copy.38.count_ref, bf16[128,512]{1,0:T(8,128)(2,1)} %grad_ref.1, bf16[8,128]{1,0:T(8,128)(2,1)} %bitcast.22, s32[8,128]{1,0:T(8,128)} %bitcast.18, s32[8,128]{1,0:T(8,128)} %bitcast.20, s32[4,16]{1,0:T(4,128)} %bitcast.14), custom_call_target="tpu_custom_call" | custom-call | tf_op jit(solution)/shard_map/route/pallas_call | solution.py:525
  3.5 3.0 %collective-permute-start = (bf16[144,512]{1,0:T(8,128)(2,1)}, bf16[144,512]{1,0:T(8,128)(2,1)S(1)}, u32[]{:S(2)}, u32[]{:S(2)}) collective-permute-start(bf16[144,512]{1,0:T(8,128)(2,1)} %route.1.refs_1_.refs_0_), channel_id=1, source_target_pairs={{0,4},{4,0},{8,12},{12,8},{1,5},{5,1},{9,13},{13,9},{2,6},{6,2},{1... | collective-permute-start | bytes 442376 | tf_op jit(solution)/shard_map/ppermute | solution.py:440
  6.5 2.5 %collective-permute-start.2 = (bf16[144,512]{1,0:T(8,128)(2,1)}, bf16[144,512]{1,0:T(8,128)(2,1)S(1)}, u32[]{:S(2)}, u32[]{:S(2)}) collective-permute-start(bf16[144,512]{1,0:T(8,128)(2,1)} %route.1.refs_1_.refs_0_), channel_id=1, source_target_pairs={{0,12},{4,8},{8,4},{12,0},{1,13},{5,9},{9,5},{13,1},{2,14},{6,10},... | collective-permute-start | bytes 442376 | tf_op jit(solution)/shard_map/ppermute | solution.py:440
  9.0 0.1 collective-permute-start.1
  9.1 0.1 pad_add_fusion.ids_ref
  9.2 1.2 copy.26.refs_0_
  10.4 0.9 copy-done.2
  11.3 1.1 hidden_columns.1
  12.4 2.0 %collective-permute-start.4 = (bf16[192,256]{1,0:T(8,128)(2,1)S(1)}, bf16[192,256]{1,0:T(8,128)(2,1)S(1)}, u32[]{:S(2)}, u32[]{:S(2)}) collective-permute-start(bf16[192,256]{1,0:T(8,128)(2,1)S(1)} %get-tuple-element.41), channel_id=1, source_target_pairs={{0,4},{4,0},{8,12},{12,8},{1,5},{5,1},{9,13},{13,9},{2,6},{6,2},{1... | collective-permute-start | bytes 294920 | tf_op jit(solution)/shard_map/ppermute | solution.py:440
  14.4 4.0 %collective-permute-start.5 = (bf16[192,256]{1,0:T(8,128)(2,1)S(1)}, bf16[192,256]{1,0:T(8,128)(2,1)S(1)}, u32[]{:S(2)}, u32[]{:S(2)}) collective-permute-start(bf16[192,256]{1,0:T(8,128)(2,1)S(1)} %get-tuple-element.42), channel_id=1, source_target_pairs={{0,8},{4,12},{8,0},{12,4},{1,9},{5,13},{9,1},{13,5},{2,10},{6,14},... | collective-permute-start | bytes 294920 | tf_op jit(solution)/shard_map/ppermute | solution.py:440
  18.4 9.4 %collective-permute-done.1.refs_2_ = bf16[144,512]{1,0:T(8,128)(2,1)} collective-permute-done((bf16[144,512]{1,0:T(8,128)(2,1)}, bf16[144,512]{1,0:T(8,128)(2,1)}, u32[]{:S(2)}, u32[]{:S(2)}) %collective-permute-start.1) | collective-permute-done | bytes 147488 | tf_op jit(solution)/shard_map/ppermute | solution.py:440
  27.8 1.9 %collective-permute-done.5.refs_5_.refs_2_ = bf16[192,256]{1,0:T(8,128)(2,1)S(1)} collective-permute-done((bf16[192,256]{1,0:T(8,128)(2,1)S(1)}, bf16[192,256]{1,0:T(8,128)(2,1)S(1)}, u32[]{:S(2)}, u32[]{:S(2)}) %collective-permute-start.5) | collective-permute-done | bytes 98336 | tf_op jit(solution)/shard_map/ppermute | solution.py:440
  29.8 1.4 collective-permute-start.8
  31.2 4.6 %collective-permute-start.7 = (bf16[1024,512]{1,0:T(8,128)(2,1)S(1)}, bf16[1024,512]{1,0:T(8,128)(2,1)S(1)}, u32[]{:S(2)}, u32[]{:S(2)}) collective-permute-start(bf16[1024,512]{1,0:T(8,128)(2,1)S(1)} %gate.10), channel_id=1, source_target_pairs={{0,4},{4,8},{8,12},{1,5},{5,9},{9,13},{2,6},{6,10},{10,14},{3,7},{... | collective-permute-start | bytes 3145736 | tf_op jit(solution)/shard_map/ppermute | solution.py:499
  35.8 6.4 %hidden_partials.1 = (bf16[2,256,768]{2,1,0:T(8,128)(2,1)S(1)}, bf16[2,256,768]{2,1,0:T(8,128)(2,1)S(1)}, bf16[4,128,512]{2,1,0:T(8,128)(2,1)S(1)}, f32[4,64,128]{2,1,0:T(8,128)S(1)}) custom-call(s32[2]{0:T(128)S(1)} %pad_add_fusion.ids_ref, bf16[144,512]{1,0:T(8,128)(2,1)S(1)} %copy-done.3, bf16[144,512]{1,0:T(8,128)(2,1)S(1)} %collective-permute-done.after_ref.refs_1_, ...), custom_call_target="tpu_custom_call" | custom-call | tf_op jit(solution)/shard_map/hidden_partials/pallas_call | solution.py:587
  42.3 2.5 %collective-permute-start.11 = (bf16[4,192,256]{2,1,0:T(8,128)(2,1)S(1)}, bf16[4,192,256]{2,1,0:T(8,128)(2,1)S(1)}, u32[]{:S(2)}, u32[]{:S(2)}) collective-permute-start(bf16[4,192,256]{2,1,0:T(8,128)(2,1)S(1)} %stack_columns.2.refs_0_), channel_id=1, source_target_pairs={{0,2},{1,3},{2,0},{3,1},{4,6},{5,7},{6,4},{7,5},{8,10},{9,11},{10,... | collective-permute-start | bytes 1179656 | tf_op jit(solution)/shard_map/ppermute | solution.py:440
  44.8 0.2 collective-permute-start.10
  45.0 9.6 %collective-permute-done.11.refs_2_ = bf16[4,192,256]{2,1,0:T(8,128)(2,1)S(1)} collective-permute-done((bf16[4,192,256]{2,1,0:T(8,128)(2,1)S(1)}, bf16[4,192,256]{2,1,0:T(8,128)(2,1)S(1)}, u32[]{:S(2)}, u32[]{:S(2)}) %collective-permute-start.11) | collective-permute-done | bytes 393248 | tf_op jit(solution)/shard_map/ppermute | solution.py:440
  54.6 0.2 halve.1
  54.8 0.6 collective-permute-done.8.refs_2_.refs_8_
  55.4 1.2 collective-permute-done.7.refs_1_.refs_5_
  56.6 1.5 %collective-permute-start.9 = (bf16[1,256,768]{2,1,0:T(8,128)(2,1)S(1)}, bf16[1,256,768]{2,1,0:T(8,128)(2,1)S(1)}, u32[]{:S(2)}, u32[]{:S(2)}) collective-permute-start(bf16[1,256,768]{2,1,0:T(8,128)(2,1)S(1)} %gate.11), channel_id=1, source_target_pairs={{0,2},{1,3},{2,0},{3,1},{4,6},{5,7},{6,4},{7,5},{8,10},{9,11},{10,... | collective-permute-start | bytes 1179656 | tf_op jit(solution)/shard_map/ppermute | solution.py:440
  58.1 1.3 collective-permute-start.19
  59.4 0.7 collective-permute-start.18
  60.2 7.8 %down_grads.1 = (bf16[16,192,512]{2,1,0:T(8,128)(2,1)}, f32[8,128]{1,0:T(8,128)S(1)}) custom-call(s32[2]{0:T(128)S(1)} %pad_add_fusion.ids_ref, s32[4,16]{1,0:T(4,128)S(1)} %bitcast.15, bf16[4,192,256]{2,1,0:T(8,128)(2,1)S(1)} %stack_columns.2.refs_0_, bf16[4,192,256]{2,1,0:T(8,128)(2,1)S(1)} %collective-permute-done.10.refs_1_, ...), custom_call_target="tpu_custom_call" | custom-call | tf_op jit(solution)/shard_map/down_grads/pallas_call | solution.py:613
  68.0 1.6 %pre_grads.1 = (bf16[384,256]{1,0:T(8,128)(2,1)S(1)}, bf16[384,256]{1,0:T(8,128)(2,1)S(1)}, bf16[384,256]{1,0:T(8,128)(2,1)S(1)}, bf16[384,256]{1,0:T(8,128)(2,1)S(1)}, bf16[256,768]{1,0:T(8,128)(2,1)S(1)}) custom-call(s32[2]{0:T(128)S(1)} %pad_add_fusion.ids_ref, bf16[1,256,768]{2,1,0:T(8,128)(2,1)S(1)} %get-tuple-element.39.keep_ref, ...), custom_call_target="tpu_custom_call" | custom-call | tf_op jit(solution)/shard_map/pre_grads/pallas_call | solution.py:655
  69.7 0.6 collective-permute-start.14
  70.3 9.2 %collective-permute-done.14.refs_2_ = bf16[256,768]{1,0:T(8,128)(2,1)S(1)} collective-permute-done((bf16[256,768]{1,0:T(8,128)(2,1)S(1)}, bf16[256,768]{1,0:T(8,128)(2,1)S(1)}, u32[]{:S(2)}, u32[]{:S(2)}) %collective-permute-start.14) | collective-permute-done | bytes 393248 | tf_op jit(solution)/shard_map/ppermute | solution.py:440
  79.5 4.3 %collective-permute-done.19.refs_4_.refs_1_ = bf16[1024,512]{1,0:T(8,128)(2,1)S(1)} collective-permute-done((bf16[1024,512]{1,0:T(8,128)(2,1)S(1)}, bf16[1024,512]{1,0:T(8,128)(2,1)S(1)}, u32[]{:S(2)}, u32[]{:S(2)}) %collective-permute-start.19) | collective-permute-done | bytes 1048608 | tf_op jit(solution)/shard_map/ppermute | solution.py:499
  83.8 2.8 %collective-permute-start.20 = (bf16[384,256]{1,0:T(8,128)(2,1)S(1)}, bf16[384,256]{1,0:T(8,128)(2,1)S(1)}, u32[]{:S(2)}, u32[]{:S(2)}) collective-permute-start(bf16[384,256]{1,0:T(8,128)(2,1)S(1)} %get-tuple-element.58), channel_id=1, source_target_pairs={{0,4},{4,0},{8,12},{12,8},{1,5},{5,1},{9,13},{13,9},{2,6},{6,2},{1... | collective-permute-start | bytes 589832 | tf_op jit(solution)/shard_map/ppermute | solution.py:440
  86.6 2.8 %collective-permute-start.21 = (bf16[384,256]{1,0:T(8,128)(2,1)S(1)}, bf16[384,256]{1,0:T(8,128)(2,1)S(1)}, u32[]{:S(2)}, u32[]{:S(2)}) collective-permute-start(bf16[384,256]{1,0:T(8,128)(2,1)S(1)} %get-tuple-element.59), channel_id=1, source_target_pairs={{0,8},{4,12},{8,0},{12,4},{1,9},{5,13},{9,1},{13,5},{2,10},{6,14},... | collective-permute-start | bytes 589832 | tf_op jit(solution)/shard_map/ppermute | solution.py:440
  89.4 0.6 collective-permute-start.22
  90.0 8.3 %row_grads.1 = (bf16[160,512]{1,0:T(8,128)(2,1)S(1)}, bf16[160,512]{1,0:T(8,128)(2,1)S(1)}, bf16[160,512]{1,0:T(8,128)(2,1)S(1)}, bf16[160,512]{1,0:T(8,128)(2,1)S(1)}) custom-call(s32[2]{0:T(128)S(1)} %pad_add_fusion.ids_ref, bf16[256,768]{1,0:T(8,128)(2,1)S(1)} %get-tuple-element.47.refs_0_, bf16[256,768]{1,0:T(8,128)(2,1)S(1)} %collective-permute-done.13.refs_1_, ...), custom_call_target="tpu_custom_call" | custom-call | tf_op jit(solution)/shard_map/row_grads/pallas_call | solution.py:679
  98.3 0.7 collective-permute-start.16
  99.0 1.4 %collective-permute-start.17 = (bf16[160,512]{1,0:T(8,128)(2,1)S(1)}, bf16[160,512]{1,0:T(8,128)(2,1)S(1)}, u32[]{:S(2)}, u32[]{:S(2)}) collective-permute-start(bf16[160,512]{1,0:T(8,128)(2,1)S(1)} %get-tuple-element.51), channel_id=1, source_target_pairs={{0,4},{4,0},{8,12},{12,8},{1,5},{5,1},{9,13},{13,9},{2,6},{6,2},{1... | collective-permute-start | bytes 491528 | tf_op jit(solution)/shard_map/ppermute | solution.py:440
  100.4 1.7 %collective-permute-done.21.refs_3_.refs_2_ = bf16[384,256]{1,0:T(8,128)(2,1)S(1)} collective-permute-done((bf16[384,256]{1,0:T(8,128)(2,1)S(1)}, bf16[384,256]{1,0:T(8,128)(2,1)S(1)}, u32[]{:S(2)}, u32[]{:S(2)}) %collective-permute-start.21) | collective-permute-done | bytes 196640 | tf_op jit(solution)/shard_map/ppermute | solution.py:440
  102.1 0.6 pick.1.refs_3_
  102.7 2.9 %collective-permute-done.16.refs_2_.refs_1_ = bf16[160,512]{1,0:T(8,128)(2,1)S(1)} collective-permute-done((bf16[160,512]{1,0:T(8,128)(2,1)S(1)}, bf16[160,512]{1,0:T(8,128)(2,1)S(1)}, u32[]{:S(2)}, u32[]{:S(2)}) %collective-permute-start.16) | collective-permute-done | bytes 163872 | tf_op jit(solution)/shard_map/ppermute | solution.py:440
  105.6 2.4 %collective-permute-done.17.refs_3_.refs_2_ = bf16[160,512]{1,0:T(8,128)(2,1)S(1)} collective-permute-done((bf16[160,512]{1,0:T(8,128)(2,1)S(1)}, bf16[160,512]{1,0:T(8,128)(2,1)S(1)}, u32[]{:S(2)}, u32[]{:S(2)}) %collective-permute-start.17) | collective-permute-done | bytes 163872 | tf_op jit(solution)/shard_map/ppermute | solution.py:440
  108.0 0.6 collective-permute-start.24
  108.7 1.3 collective-permute-start.27
  110.0 16.5 %collective-permute-done.24.refs_2_ = bf16[4,384,256]{2,1,0:T(8,128)(2,1)S(1)} collective-permute-done((bf16[4,384,256]{2,1,0:T(8,128)(2,1)S(1)}, bf16[4,384,256]{2,1,0:T(8,128)(2,1)S(1)}, u32[]{:S(2)}, u32[]{:S(2)}) %collective-permute-start.24) | collective-permute-done | bytes 786464 | tf_op jit(solution)/shard_map/ppermute | solution.py:440
  126.6 0.1 sum_parts.1
  126.7 2.2 %collective-permute-done.25.refs_3_ = bf16[4,384,256]{2,1,0:T(8,128)(2,1)S(1)} collective-permute-done((bf16[4,384,256]{2,1,0:T(8,128)(2,1)S(1)}, bf16[4,384,256]{2,1,0:T(8,128)(2,1)S(1)}, u32[]{:S(2)}, u32[]{:S(2)}) %collective-permute-start.25) | collective-permute-done | bytes 786464 | tf_op jit(solution)/shard_map/ppermute | solution.py:440
  128.9 0.3 collective-permute-start.26
  129.2 5.0 %collective-permute-done.27.refs_7_.refs_10_ = bf16[1024,512]{1,0:T(8,128)(2,1)S(1)} collective-permute-done((bf16[1024,512]{1,0:T(8,128)(2,1)S(1)}, bf16[1024,512]{1,0:T(8,128)(2,1)S(1)}, u32[]{:S(2)}, u32[]{:S(2)}) %collective-permute-start.27) | collective-permute-done | bytes 1048608 | tf_op jit(solution)/shard_map/ppermute | solution.py:497
  134.2 7.7 %in_grads.1 = (bf16[16,384,512]{2,1,0:T(8,128)(2,1)}, f32[8,128]{1,0:T(8,128)S(1)}) custom-call(s32[2]{0:T(128)S(1)} %pad_add_fusion.ids_ref, s32[4,16]{1,0:T(4,128)S(1)} %bitcast.16, bf16[4,384,256]{2,1,0:T(8,128)(2,1)S(1)} %stack_columns.3.refs_0_, bf16[4,384,256]{2,1,0:T(8,128)(2,1)S(1)} %collective-permute-done.23.refs_1_, ...), custom_call_target="tpu_custom_call" | custom-call | tf_op jit(solution)/shard_map/in_grads/pallas_call | solution.py:613
  141.9 0.8 token_grads.1
  (46 shorter events, 0.3 us)
Async XLA Ops:
  0.6 10.7 %copy-start = (bf16[8,128,1536]{2,1,0:T(8,128)(2,1)S(1)}, bf16[8,128,1536]{2,1,0:T(8,128)(2,1)}, u32[]{:S(2)}) copy-start(bf16[8,128,1536]{2,1,0:T(8,128)(2,1)} %param.17) | copy-start | bytes 9437188
  3.5 7.8 %collective-permute-start = (bf16[144,512]{1,0:T(8,128)(2,1)}, bf16[144,512]{1,0:T(8,128)(2,1)S(1)}, u32[]{:S(2)}, u32[]{:S(2)}) collective-permute-start(bf16[144,512]{1,0:T(8,128)(2,1)} %route.1.refs_1_.refs_0_), channel_id=1, source_target_pairs={{0,4},{4,0},{8,12},{12,8},{1,5},{5,1},{9,13},{13,9},{2,6},{6,2},{1... | collective-permute-start | bytes 442376 | tf_op jit(solution)/shard_map/ppermute | solution.py:440
  6.5 11.9 %collective-permute-start.2 = (bf16[144,512]{1,0:T(8,128)(2,1)}, bf16[144,512]{1,0:T(8,128)(2,1)S(1)}, u32[]{:S(2)}, u32[]{:S(2)}) collective-permute-start(bf16[144,512]{1,0:T(8,128)(2,1)} %route.1.refs_1_.refs_0_), channel_id=1, source_target_pairs={{0,12},{4,8},{8,4},{12,0},{1,13},{5,9},{9,5},{13,1},{2,14},{6,10},... | collective-permute-start | bytes 442376 | tf_op jit(solution)/shard_map/ppermute | solution.py:440
  9.0 18.8 %collective-permute-start.1 = (bf16[144,512]{1,0:T(8,128)(2,1)}, bf16[144,512]{1,0:T(8,128)(2,1)}, u32[]{:S(2)}, u32[]{:S(2)}) collective-permute-start(bf16[144,512]{1,0:T(8,128)(2,1)} %route.1.refs_1_.refs_0_), channel_id=1, source_target_pairs={{0,8},{4,12},{8,0},{12,4},{1,9},{5,13},{9,1},{13,5},{2,10},{6,14},... | collective-permute-start | bytes 442376 | tf_op jit(solution)/shard_map/ppermute | solution.py:440
  10.4 0.9 copy-start.2
  11.3 24.5 %copy-start.3 = (bf16[144,512]{1,0:T(8,128)(2,1)S(1)}, bf16[144,512]{1,0:T(8,128)(2,1)}, u32[]{:S(2)}) copy-start(bf16[144,512]{1,0:T(8,128)(2,1)} %route.1.refs_1_.refs_0_) | copy-start | bytes 442372
  12.4 15.4 %collective-permute-start.4 = (bf16[192,256]{1,0:T(8,128)(2,1)S(1)}, bf16[192,256]{1,0:T(8,128)(2,1)S(1)}, u32[]{:S(2)}, u32[]{:S(2)}) collective-permute-start(bf16[192,256]{1,0:T(8,128)(2,1)S(1)} %get-tuple-element.41), channel_id=1, source_target_pairs={{0,4},{4,0},{8,12},{12,8},{1,5},{5,1},{9,13},{13,9},{2,6},{6,2},{1... | collective-permute-start | bytes 294920 | tf_op jit(solution)/shard_map/ppermute | solution.py:440
  14.4 15.4 %collective-permute-start.5 = (bf16[192,256]{1,0:T(8,128)(2,1)S(1)}, bf16[192,256]{1,0:T(8,128)(2,1)S(1)}, u32[]{:S(2)}, u32[]{:S(2)}) collective-permute-start(bf16[192,256]{1,0:T(8,128)(2,1)S(1)} %get-tuple-element.42), channel_id=1, source_target_pairs={{0,8},{4,12},{8,0},{12,4},{1,9},{5,13},{9,1},{13,5},{2,10},{6,14},... | collective-permute-start | bytes 294920 | tf_op jit(solution)/shard_map/ppermute | solution.py:440
  18.4 11.4 %collective-permute-start.6 = (bf16[192,256]{1,0:T(8,128)(2,1)S(1)}, bf16[192,256]{1,0:T(8,128)(2,1)S(1)}, u32[]{:S(2)}, u32[]{:S(2)}) collective-permute-start(bf16[192,256]{1,0:T(8,128)(2,1)S(1)} %get-tuple-element.43), channel_id=1, source_target_pairs={{0,12},{4,8},{8,4},{12,0},{1,13},{5,9},{9,5},{13,1},{2,14},{6,10},... | collective-permute-start | bytes 294920 | tf_op jit(solution)/shard_map/ppermute | solution.py:440
  29.8 30.4 %copy-start.4 = (s32[16,4]{0,1:T(4,128)S(1)}, s32[16,4]{0,1:T(4,128)}, u32[]{:S(2)}) copy-start(s32[16,4]{0,1:T(4,128)} %param.14) | copy-start | bytes 772
  29.8 25.7 %collective-permute-start.8 = (bf16[1024,512]{1,0:T(8,128)(2,1)S(1)}, bf16[1024,512]{1,0:T(8,128)(2,1)S(1)}, u32[]{:S(2)}, u32[]{:S(2)}) collective-permute-start(bf16[1024,512]{1,0:T(8,128)(2,1)S(1)} %gate.10), channel_id=1, source_target_pairs={{12,8},{8,4},{4,0},{13,9},{9,5},{5,1},{14,10},{10,6},{6,2},{15,11}... | collective-permute-start | bytes 3145736 | tf_op jit(solution)/shard_map/ppermute | solution.py:499
  31.2 25.4 %collective-permute-start.7 = (bf16[1024,512]{1,0:T(8,128)(2,1)S(1)}, bf16[1024,512]{1,0:T(8,128)(2,1)S(1)}, u32[]{:S(2)}, u32[]{:S(2)}) collective-permute-start(bf16[1024,512]{1,0:T(8,128)(2,1)S(1)} %gate.10), channel_id=1, source_target_pairs={{0,4},{4,8},{8,12},{1,5},{5,9},{9,13},{2,6},{6,10},{10,14},{3,7},{... | collective-permute-start | bytes 3145736 | tf_op jit(solution)/shard_map/ppermute | solution.py:499
  42.2 12.4 %collective-permute-start.3 = (bf16[2,256,768]{2,1,0:T(8,128)(2,1)S(1)}, bf16[2,256,768]{2,1,0:T(8,128)(2,1)S(1)}, u32[]{:S(2)}, u32[]{:S(2)}) collective-permute-start(bf16[2,256,768]{2,1,0:T(8,128)(2,1)S(1)} %get-tuple-element.38), channel_id=1, source_target_pairs={{0,1},{1,0},{2,3},{3,2},{4,5},{5,4},{6,7},{7,6},{8,9},{9,8},{10,11... | collective-permute-start | bytes 2359304 | tf_op jit(solution)/shard_map/ppermute | solution.py:440
  42.3 12.3 %collective-permute-start.11 = (bf16[4,192,256]{2,1,0:T(8,128)(2,1)S(1)}, bf16[4,192,256]{2,1,0:T(8,128)(2,1)S(1)}, u32[]{:S(2)}, u32[]{:S(2)}) collective-permute-start(bf16[4,192,256]{2,1,0:T(8,128)(2,1)S(1)} %stack_columns.2.refs_0_), channel_id=1, source_target_pairs={{0,2},{1,3},{2,0},{3,1},{4,6},{5,7},{6,4},{7,5},{8,10},{9,11},{10,... | collective-permute-start | bytes 1179656 | tf_op jit(solution)/shard_map/ppermute | solution.py:440
  44.8 15.3 %collective-permute-start.10 = (bf16[4,192,256]{2,1,0:T(8,128)(2,1)S(1)}, bf16[4,192,256]{2,1,0:T(8,128)(2,1)S(1)}, u32[]{:S(2)}, u32[]{:S(2)}) collective-permute-start(bf16[4,192,256]{2,1,0:T(8,128)(2,1)S(1)} %stack_columns.2.refs_0_), channel_id=1, source_target_pairs={{0,1},{1,0},{2,3},{3,2},{4,5},{5,4},{6,7},{7,6},{8,9},{9,8},{10,11... | collective-permute-start | bytes 1179656 | tf_op jit(solution)/shard_map/ppermute | solution.py:440
  54.6 5.5 %collective-permute-start.12 = (bf16[4,192,256]{2,1,0:T(8,128)(2,1)S(1)}, bf16[4,192,256]{2,1,0:T(8,128)(2,1)S(1)}, u32[]{:S(2)}, u32[]{:S(2)}) collective-permute-start(bf16[4,192,256]{2,1,0:T(8,128)(2,1)S(1)} %collective-permute-done.11.refs_2_), channel_id=1, source_target_pairs={{0,1},{1,0},{2,3},{3,2},{4,5},{5,4},{6,7},{7,6},{8,9},{9,8},{10,11... | collective-permute-start | bytes 1179656 | tf_op jit(solution)/shard_map/ppermute | solution.py:440
  56.6 11.4 %collective-permute-start.9 = (bf16[1,256,768]{2,1,0:T(8,128)(2,1)S(1)}, bf16[1,256,768]{2,1,0:T(8,128)(2,1)S(1)}, u32[]{:S(2)}, u32[]{:S(2)}) collective-permute-start(bf16[1,256,768]{2,1,0:T(8,128)(2,1)S(1)} %gate.11), channel_id=1, source_target_pairs={{0,2},{1,3},{2,0},{3,1},{4,6},{5,7},{6,4},{7,5},{8,10},{9,11},{10,... | collective-permute-start | bytes 1179656 | tf_op jit(solution)/shard_map/ppermute | solution.py:440
  58.1 25.7 %collective-permute-start.19 = (bf16[1024,512]{1,0:T(8,128)(2,1)S(1)}, bf16[1024,512]{1,0:T(8,128)(2,1)S(1)}, u32[]{:S(2)}, u32[]{:S(2)}) collective-permute-start(bf16[1024,512]{1,0:T(8,128)(2,1)S(1)} %collective-permute-done.8.refs_2_.refs_8_), channel_id=1, source_target_pairs={{8,4},{4,0},{9,5},{5,1},{10,6},{6,2},{11,7},{7,3},{24,20},{20,16},... | collective-permute-start | bytes 3145736 | tf_op jit(solution)/shard_map/ppermute | solution.py:499
  59.4 24.4 %collective-permute-start.18 = (bf16[1024,512]{1,0:T(8,128)(2,1)S(1)}, bf16[1024,512]{1,0:T(8,128)(2,1)S(1)}, u32[]{:S(2)}, u32[]{:S(2)}) collective-permute-start(bf16[1024,512]{1,0:T(8,128)(2,1)S(1)} %collective-permute-done.7.refs_1_.refs_5_), channel_id=1, source_target_pairs={{4,8},{8,12},{5,9},{9,13},{6,10},{10,14},{7,11},{11,15},{20,24},{2... | collective-permute-start | bytes 3145736 | tf_op jit(solution)/shard_map/ppermute | solution.py:499
  69.7 9.8 %collective-permute-start.14 = (bf16[256,768]{1,0:T(8,128)(2,1)S(1)}, bf16[256,768]{1,0:T(8,128)(2,1)S(1)}, u32[]{:S(2)}, u32[]{:S(2)}) collective-permute-start(bf16[256,768]{1,0:T(8,128)(2,1)S(1)} %get-tuple-element.47.refs_0_), channel_id=1, source_target_pairs={{0,2},{1,3},{2,0},{3,1},{4,6},{5,7},{6,4},{7,5},{8,10},{9,11},{10,... | collective-permute-start | bytes 1179656 | tf_op jit(solution)/shard_map/ppermute | solution.py:440
  70.3 19.7 %collective-permute-start.13 = (bf16[256,768]{1,0:T(8,128)(2,1)S(1)}, bf16[256,768]{1,0:T(8,128)(2,1)S(1)}, u32[]{:S(2)}, u32[]{:S(2)}) collective-permute-start(bf16[256,768]{1,0:T(8,128)(2,1)S(1)} %get-tuple-element.47.refs_0_), channel_id=1, source_target_pairs={{0,1},{1,0},{2,3},{3,2},{4,5},{5,4},{6,7},{7,6},{8,9},{9,8},{10,11... | collective-permute-start | bytes 1179656 | tf_op jit(solution)/shard_map/ppermute | solution.py:440
  79.5 10.5 %collective-permute-start.15 = (bf16[256,768]{1,0:T(8,128)(2,1)S(1)}, bf16[256,768]{1,0:T(8,128)(2,1)S(1)}, u32[]{:S(2)}, u32[]{:S(2)}) collective-permute-start(bf16[256,768]{1,0:T(8,128)(2,1)S(1)} %collective-permute-done.14.refs_2_), channel_id=1, source_target_pairs={{0,1},{1,0},{2,3},{3,2},{4,5},{5,4},{6,7},{7,6},{8,9},{9,8},{10,11... | collective-permute-start | bytes 1179656 | tf_op jit(solution)/shard_map/ppermute | solution.py:440
  83.8 16.6 %collective-permute-start.20 = (bf16[384,256]{1,0:T(8,128)(2,1)S(1)}, bf16[384,256]{1,0:T(8,128)(2,1)S(1)}, u32[]{:S(2)}, u32[]{:S(2)}) collective-permute-start(bf16[384,256]{1,0:T(8,128)(2,1)S(1)} %get-tuple-element.58), channel_id=1, source_target_pairs={{0,4},{4,0},{8,12},{12,8},{1,5},{5,1},{9,13},{13,9},{2,6},{6,2},{1... | collective-permute-start | bytes 589832 | tf_op jit(solution)/shard_map/ppermute | solution.py:440
  86.6 15.5 %collective-permute-start.21 = (bf16[384,256]{1,0:T(8,128)(2,1)S(1)}, bf16[384,256]{1,0:T(8,128)(2,1)S(1)}, u32[]{:S(2)}, u32[]{:S(2)}) collective-permute-start(bf16[384,256]{1,0:T(8,128)(2,1)S(1)} %get-tuple-element.59), channel_id=1, source_target_pairs={{0,8},{4,12},{8,0},{12,4},{1,9},{5,13},{9,1},{13,5},{2,10},{6,14},... | collective-permute-start | bytes 589832 | tf_op jit(solution)/shard_map/ppermute | solution.py:440
  89.4 12.7 %collective-permute-start.22 = (bf16[384,256]{1,0:T(8,128)(2,1)S(1)}, bf16[384,256]{1,0:T(8,128)(2,1)S(1)}, u32[]{:S(2)}, u32[]{:S(2)}) collective-permute-start(bf16[384,256]{1,0:T(8,128)(2,1)S(1)} %get-tuple-element.60), channel_id=1, source_target_pairs={{0,12},{4,8},{8,4},{12,0},{1,13},{5,9},{9,5},{13,1},{2,14},{6,10},... | collective-permute-start | bytes 589832 | tf_op jit(solution)/shard_map/ppermute | solution.py:440
  98.3 35.9 %copy-start.1 = (bf16[8,4,32,512]{3,2,1,0:T(8,128)(2,1)S(1)}, bf16[8,4,32,512]{3,2,1,0:T(8,128)(2,1)}, u32[]{:S(2)}) copy-start(bf16[8,4,32,512]{3,2,1,0:T(8,128)(2,1)} %param.16) | copy-start | bytes 3145732
  98.3 7.3 %collective-permute-start.16 = (bf16[160,512]{1,0:T(8,128)(2,1)S(1)}, bf16[160,512]{1,0:T(8,128)(2,1)S(1)}, u32[]{:S(2)}, u32[]{:S(2)}) collective-permute-start(bf16[160,512]{1,0:T(8,128)(2,1)S(1)} %get-tuple-element.50), channel_id=1, source_target_pairs={{0,4},{4,0},{8,12},{12,8},{1,5},{5,1},{9,13},{13,9},{2,6},{6,2},{1... | collective-permute-start | bytes 491528 | tf_op jit(solution)/shard_map/ppermute | solution.py:440
  99.0 9.0 %collective-permute-start.17 = (bf16[160,512]{1,0:T(8,128)(2,1)S(1)}, bf16[160,512]{1,0:T(8,128)(2,1)S(1)}, u32[]{:S(2)}, u32[]{:S(2)}) collective-permute-start(bf16[160,512]{1,0:T(8,128)(2,1)S(1)} %get-tuple-element.51), channel_id=1, source_target_pairs={{0,4},{4,0},{8,12},{12,8},{1,5},{5,1},{9,13},{13,9},{2,6},{6,2},{1... | collective-permute-start | bytes 491528 | tf_op jit(solution)/shard_map/ppermute | solution.py:440
  108.0 18.5 %collective-permute-start.24 = (bf16[4,384,256]{2,1,0:T(8,128)(2,1)S(1)}, bf16[4,384,256]{2,1,0:T(8,128)(2,1)S(1)}, u32[]{:S(2)}, u32[]{:S(2)}) collective-permute-start(bf16[4,384,256]{2,1,0:T(8,128)(2,1)S(1)} %stack_columns.3.refs_0_), channel_id=1, source_target_pairs={{0,2},{1,3},{2,0},{3,1},{4,6},{5,7},{6,4},{7,5},{8,10},{9,11},{10,... | collective-permute-start | bytes 2359304 | tf_op jit(solution)/shard_map/ppermute | solution.py:440
  108.7 25.5 %collective-permute-start.27 = (bf16[1024,512]{1,0:T(8,128)(2,1)S(1)}, bf16[1024,512]{1,0:T(8,128)(2,1)S(1)}, u32[]{:S(2)}, u32[]{:S(2)}) collective-permute-start(bf16[1024,512]{1,0:T(8,128)(2,1)S(1)} %pick.1.refs_3_), channel_id=1, source_target_pairs={{8,12},{4,0},{9,13},{5,1},{10,14},{6,2},{11,15},{7,3},{24,28},{20,... | collective-permute-start | bytes 3145736 | tf_op jit(solution)/shard_map/ppermute | solution.py:497
  110.0 16.7 %collective-permute-start.23 = (bf16[4,384,256]{2,1,0:T(8,128)(2,1)S(1)}, bf16[4,384,256]{2,1,0:T(8,128)(2,1)S(1)}, u32[]{:S(2)}, u32[]{:S(2)}) collective-permute-start(bf16[4,384,256]{2,1,0:T(8,128)(2,1)S(1)} %stack_columns.3.refs_0_), channel_id=1, source_target_pairs={{0,1},{1,0},{2,3},{3,2},{4,5},{5,4},{6,7},{7,6},{8,9},{9,8},{10,11... | collective-permute-start | bytes 2359304 | tf_op jit(solution)/shard_map/ppermute | solution.py:440
  126.6 2.3 %collective-permute-start.25 = (bf16[4,384,256]{2,1,0:T(8,128)(2,1)S(1)}, bf16[4,384,256]{2,1,0:T(8,128)(2,1)S(1)}, u32[]{:S(2)}, u32[]{:S(2)}) collective-permute-start(bf16[4,384,256]{2,1,0:T(8,128)(2,1)S(1)} %collective-permute-done.24.refs_2_), channel_id=1, source_target_pairs={{0,1},{1,0},{2,3},{3,2},{4,5},{5,4},{6,7},{7,6},{8,9},{9,8},{10,11... | collective-permute-start | bytes 2359304 | tf_op jit(solution)/shard_map/ppermute | solution.py:440
  128.8 13.0 %copy-start.5 = (s32[128,8]{0,1:T(8,128)S(1)}, s32[128,8]{0,1:T(8,128)}, u32[]{:S(2)}) copy-start(s32[128,8]{0,1:T(8,128)} %param.12) | copy-start | bytes 12292
  128.8 13.1 %copy-start.6 = (s32[128,8]{0,1:T(8,128)S(1)}, s32[128,8]{0,1:T(8,128)}, u32[]{:S(2)}) copy-start(s32[128,8]{0,1:T(8,128)} %param.13) | copy-start | bytes 12292
  128.9 13.0 %collective-permute-start.26 = (bf16[160,512]{1,0:T(8,128)(2,1)S(1)}, bf16[160,512]{1,0:T(8,128)(2,1)S(1)}, u32[]{:S(2)}, u32[]{:S(2)}) collective-permute-start(bf16[160,512]{1,0:T(8,128)(2,1)S(1)} %gate.16), channel_id=1, source_target_pairs={{0,8},{4,12},{8,0},{12,4},{1,9},{5,13},{9,1},{13,5},{2,10},{6,14},... | collective-permute-start | bytes 491528 | tf_op jit(solution)/shard_map/ppermute | solution.py:440

commit v17 on v16

--- a/solution.py
+++ b/solution.py
@@ -10,7 +10,7 @@
 
 BF = jnp.bfloat16
 F32 = jnp.float32
-PER = 2
+PER = 4
 
 
 def nt(a, b):
@@ -65,6 +65,8 @@
         self.cols = self.in_cols + self.down_cols
         self.folds = self.width // self.tokens
         self.tail = 2 * self.slots // self.folds
+        self.mark_rows = self.slots // self.folds
+        self.mark_tail = -(-self.mark_rows // 16) * 16
 
 
 def slot_table(z, table_ref, r):
@@ -271,15 +273,18 @@
 
     @pl.when(step == z.blocks - 1)
     def _():
-        blank = jnp.zeros((z.slots, z.width - z.tokens), BF)
+        spare = z.mark_tail - z.mark_rows
+        blank = jnp.zeros((spare, z.tokens), F32) if spare else None
         for k in range(z.ep):
             source = me ^ k
             start = pl.multiple_of(source * z.cap, z.cap)
             rows = rows_ref[:, pl.ds(start, z.cap), :].reshape(z.local * z.cap, z.width)
             picks = local_picks(z, codes_ref, source, me)
             outs[k][: z.tokens, :] = tn(picks, rows).astype(BF)
-            outs[k][z.tokens :, : z.tokens] = marks[source].astype(BF)
-            outs[k][z.tokens :, z.tokens :] = blank
+            for f in range(z.folds):
+                part = marks[source, f * z.mark_rows : (f + 1) * z.mark_rows, :]
+                part = jnp.concatenate([part, blank], axis=0) if spare else part
+                outs[k][z.tokens :, f * z.tokens : (f + 1) * z.tokens] = part.astype(BF)
 
 
 def sum_kernel(*refs):
@@ -300,7 +305,11 @@
     keep_ref, got_ref, routes_ref, replica_ref, table_ref, tokens_ref, route_ref = refs
     total = keep_ref[...].astype(F32) + got_ref[...].astype(F32)
     tokens_ref[...] = total[: z.tokens, :].astype(BF)
-    rows = total[z.tokens :, : z.tokens].astype(BF)
+    rows = [
+        total[z.tokens : z.tokens + z.mark_rows, f * z.tokens : (f + 1) * z.tokens]
+        for f in range(z.folds)
+    ]
+    rows = jnp.concatenate(rows, axis=0).astype(BF)
     totals = [jnp.zeros((1, z.tokens), F32)] * z.top
     for r in range(z.reps):
         spread = tn(slot_table(z, table_ref, r), rows)
@@ -675,7 +684,7 @@
     pieces = pieces[:1] + [swap(a, "ep", n, k) for k, a in enumerate(late, 1)]
     grad_parts = spread_over({0: grad_part}, "sub", m, m // 2)
 
-    back_shape = (z.tokens + z.slots, z.width)
+    back_shape = (z.tokens + z.mark_tail, z.width)
     parts = pl.pallas_call(
         functools.partial(row_kernel, z),
         grid_spec=pltpu.PrefetchScalarGridSpec(

time: 144 us -> 144 us (level)
  no operation moved by 1% of the time
where the time goes in v17:
time: 144 us; the launch traced here: 142 us
  waiting for transfers between devices  66.4 us (46%)
  Pallas kernels  36.7 us (25%)
  starting transfers between devices  35 us (24%)
  local copies, waits for them, and re-layouts  2.16 us (2%)
  between operations  1.69 us (1%)
    ppermute x23, waiting for transfers between devices, swap(): return lax.ppermute(x, axis, [(i, i ^ bit) for i in range(size)])  55.2 us
    ppermute x23, starting transfers between devices, swap(): return lax.ppermute(x, axis, [(i, i ^ bit) for i in range(size)])  25.6 us
    pallas_call x2, Pallas kernels, total_call(): pl.pallas_call(functools.partial(kernel, z), grid_spec=pltpu.PrefetchScal...  15.5 us
    pallas_call x1, Pallas kernels, body(): pl.pallas_call(functools.partial(row_kernel, z), grid_spec=pltpu.Prefetch...  8.3 us
    ppermute x4, starting transfers between devices, chain_step(): return (lax.ppermute(go, axis, rights), lax.ppermute(back, axis, lefts))  8.03 us
    pallas_call x1, Pallas kernels, body(): pl.pallas_call(functools.partial(down_kernel, z), grid_spec=pltpu.Prefetc...  6.4 us
    ppermute x4, waiting for transfers between devices, chain_step(): return (lax.ppermute(go, axis, rights), lax.ppermute(back, axis, lefts))  6.15 us
    ppermute x1, waiting for transfers between devices, chain_step(): got = lax.ppermute(go, axis, rights + lefts)  5.1 us
  transfers between devices with their start and end apart: 28, of which 13 were waited for; matrix products, arithmetic and copies ran while one was open for 1% of the time, Pallas kernels for 24%

profile of v17, /device:TPU:0, one launch (start us, length us, event | category | flops | bytes accessed | tf_op | source)
XLA Modules:
  0.0 142.0 jit_solution(12026912573025932147)
XLA Ops:
  1.4 2.0 %route.1.refs_1_.refs_0_ = bf16[144,512]{1,0:T(8,128)(2,1)} custom-call(s32[1]{0:T(128)S(6)} %copy.38.count_ref, bf16[128,512]{1,0:T(8,128)(2,1)} %grad_ref.1, bf16[8,128]{1,0:T(8,128)(2,1)} %bitcast.22, s32[8,128]{1,0:T(8,128)} %bitcast.18, s32[8,128]{1,0:T(8,128)} %bitcast.20, s32[4,16]{1,0:T(4,128)} %bitcast.14), custom_call_target="tpu_custom_call" | custom-call | tf_op jit(solution)/shard_map/route/pallas_call | solution.py:534
  3.5 3.0 %collective-permute-start = (bf16[144,512]{1,0:T(8,128)(2,1)}, bf16[144,512]{1,0:T(8,128)(2,1)S(1)}, u32[]{:S(2)}, u32[]{:S(2)}) collective-permute-start(bf16[144,512]{1,0:T(8,128)(2,1)} %route.1.refs_1_.refs_0_), channel_id=1, source_target_pairs={{0,4},{4,0},{8,12},{12,8},{1,5},{5,1},{9,13},{13,9},{2,6},{6,2},{1... | collective-permute-start | bytes 442376 | tf_op jit(solution)/shard_map/ppermute | solution.py:449
  6.5 2.5 %collective-permute-start.2 = (bf16[144,512]{1,0:T(8,128)(2,1)}, bf16[144,512]{1,0:T(8,128)(2,1)S(1)}, u32[]{:S(2)}, u32[]{:S(2)}) collective-permute-start(bf16[144,512]{1,0:T(8,128)(2,1)} %route.1.refs_1_.refs_0_), channel_id=1, source_target_pairs={{0,12},{4,8},{8,4},{12,0},{1,13},{5,9},{9,5},{13,1},{2,14},{6,10},... | collective-permute-start | bytes 442376 | tf_op jit(solution)/shard_map/ppermute | solution.py:449
  9.0 0.1 collective-permute-start.1
  9.1 0.1 pad_add_fusion.ids_ref
  9.2 1.2 copy.26.refs_0_
  10.4 0.9 copy-done.2
  11.3 1.1 hidden_columns.1
  12.4 2.0 %collective-permute-start.4 = (bf16[192,256]{1,0:T(8,128)(2,1)S(1)}, bf16[192,256]{1,0:T(8,128)(2,1)S(1)}, u32[]{:S(2)}, u32[]{:S(2)}) collective-permute-start(bf16[192,256]{1,0:T(8,128)(2,1)S(1)} %get-tuple-element.41), channel_id=1, source_target_pairs={{0,4},{4,0},{8,12},{12,8},{1,5},{5,1},{9,13},{13,9},{2,6},{6,2},{1... | collective-permute-start | bytes 294920 | tf_op jit(solution)/shard_map/ppermute | solution.py:449
  14.4 4.0 %collective-permute-start.5 = (bf16[192,256]{1,0:T(8,128)(2,1)S(1)}, bf16[192,256]{1,0:T(8,128)(2,1)S(1)}, u32[]{:S(2)}, u32[]{:S(2)}) collective-permute-start(bf16[192,256]{1,0:T(8,128)(2,1)S(1)} %get-tuple-element.42), channel_id=1, source_target_pairs={{0,8},{4,12},{8,0},{12,4},{1,9},{5,13},{9,1},{13,5},{2,10},{6,14},... | collective-permute-start | bytes 294920 | tf_op jit(solution)/shard_map/ppermute | solution.py:449
  18.4 9.4 %collective-permute-done.1.refs_2_ = bf16[144,512]{1,0:T(8,128)(2,1)} collective-permute-done((bf16[144,512]{1,0:T(8,128)(2,1)}, bf16[144,512]{1,0:T(8,128)(2,1)}, u32[]{:S(2)}, u32[]{:S(2)}) %collective-permute-start.1) | collective-permute-done | bytes 147488 | tf_op jit(solution)/shard_map/ppermute | solution.py:449
  27.8 1.9 %collective-permute-done.5.refs_5_.refs_2_ = bf16[192,256]{1,0:T(8,128)(2,1)S(1)} collective-permute-done((bf16[192,256]{1,0:T(8,128)(2,1)S(1)}, bf16[192,256]{1,0:T(8,128)(2,1)S(1)}, u32[]{:S(2)}, u32[]{:S(2)}) %collective-permute-start.5) | collective-permute-done | bytes 98336 | tf_op jit(solution)/shard_map/ppermute | solution.py:449
  29.8 1.4 collective-permute-start.8
  31.2 4.6 %collective-permute-start.7 = (bf16[1024,512]{1,0:T(8,128)(2,1)S(1)}, bf16[1024,512]{1,0:T(8,128)(2,1)S(1)}, u32[]{:S(2)}, u32[]{:S(2)}) collective-permute-start(bf16[1024,512]{1,0:T(8,128)(2,1)S(1)} %gate.10), channel_id=1, source_target_pairs={{0,4},{4,8},{8,12},{1,5},{5,9},{9,13},{2,6},{6,10},{10,14},{3,7},{... | collective-permute-start | bytes 3145736 | tf_op jit(solution)/shard_map/ppermute | solution.py:508
  35.8 6.4 %hidden_partials.1 = (bf16[2,256,768]{2,1,0:T(8,128)(2,1)S(1)}, bf16[2,256,768]{2,1,0:T(8,128)(2,1)S(1)}, bf16[4,128,512]{2,1,0:T(8,128)(2,1)S(1)}, f32[4,64,128]{2,1,0:T(8,128)S(1)}) custom-call(s32[2]{0:T(128)S(1)} %pad_add_fusion.ids_ref, bf16[144,512]{1,0:T(8,128)(2,1)S(1)} %copy-done.3, bf16[144,512]{1,0:T(8,128)(2,1)S(1)} %collective-permute-done.after_ref.refs_1_, ...), custom_call_target="tpu_custom_call" | custom-call | tf_op jit(solution)/shard_map/hidden_partials/pallas_call | solution.py:596
  42.3 2.5 %collective-permute-start.11 = (bf16[4,192,256]{2,1,0:T(8,128)(2,1)S(1)}, bf16[4,192,256]{2,1,0:T(8,128)(2,1)S(1)}, u32[]{:S(2)}, u32[]{:S(2)}) collective-permute-start(bf16[4,192,256]{2,1,0:T(8,128)(2,1)S(1)} %stack_columns.2.refs_0_), channel_id=1, source_target_pairs={{0,2},{1,3},{2,0},{3,1},{4,6},{5,7},{6,4},{7,5},{8,10},{9,11},{10,... | collective-permute-start | bytes 1179656 | tf_op jit(solution)/shard_map/ppermute | solution.py:449
  44.8 0.2 collective-permute-start.10
  45.0 9.6 %collective-permute-done.11.refs_2_ = bf16[4,192,256]{2,1,0:T(8,128)(2,1)S(1)} collective-permute-done((bf16[4,192,256]{2,1,0:T(8,128)(2,1)S(1)}, bf16[4,192,256]{2,1,0:T(8,128)(2,1)S(1)}, u32[]{:S(2)}, u32[]{:S(2)}) %collective-permute-start.11) | collective-permute-done | bytes 393248 | tf_op jit(solution)/shard_map/ppermute | solution.py:449
  54.6 0.2 halve.1
  54.8 0.6 collective-permute-done.8.refs_2_.refs_8_
  55.4 1.2 collective-permute-done.7.refs_1_.refs_5_
  56.6 1.5 %collective-permute-start.9 = (bf16[1,256,768]{2,1,0:T(8,128)(2,1)S(1)}, bf16[1,256,768]{2,1,0:T(8,128)(2,1)S(1)}, u32[]{:S(2)}, u32[]{:S(2)}) collective-permute-start(bf16[1,256,768]{2,1,0:T(8,128)(2,1)S(1)} %gate.11), channel_id=1, source_target_pairs={{0,2},{1,3},{2,0},{3,1},{4,6},{5,7},{6,4},{7,5},{8,10},{9,11},{10,... | collective-permute-start | bytes 1179656 | tf_op jit(solution)/shard_map/ppermute | solution.py:449
  58.1 1.3 collective-permute-start.19
  59.4 0.7 collective-permute-start.18
  60.2 7.8 %down_grads.1 = (bf16[16,192,512]{2,1,0:T(8,128)(2,1)}, f32[8,128]{1,0:T(8,128)S(1)}) custom-call(s32[2]{0:T(128)S(1)} %pad_add_fusion.ids_ref, s32[4,16]{1,0:T(4,128)S(1)} %bitcast.15, bf16[4,192,256]{2,1,0:T(8,128)(2,1)S(1)} %stack_columns.2.refs_0_, bf16[4,192,256]{2,1,0:T(8,128)(2,1)S(1)} %collective-permute-done.10.refs_1_, ...), custom_call_target="tpu_custom_call" | custom-call | tf_op jit(solution)/shard_map/down_grads/pallas_call | solution.py:622
  68.0 1.6 %pre_grads.1 = (bf16[384,256]{1,0:T(8,128)(2,1)S(1)}, bf16[384,256]{1,0:T(8,128)(2,1)S(1)}, bf16[384,256]{1,0:T(8,128)(2,1)S(1)}, bf16[384,256]{1,0:T(8,128)(2,1)S(1)}, bf16[256,768]{1,0:T(8,128)(2,1)S(1)}) custom-call(s32[2]{0:T(128)S(1)} %pad_add_fusion.ids_ref, bf16[1,256,768]{2,1,0:T(8,128)(2,1)S(1)} %get-tuple-element.39.keep_ref, ...), custom_call_target="tpu_custom_call" | custom-call | tf_op jit(solution)/shard_map/pre_grads/pallas_call | solution.py:664
  69.6 0.6 collective-permute-start.14
  70.2 9.2 %collective-permute-done.14.refs_2_ = bf16[256,768]{1,0:T(8,128)(2,1)S(1)} collective-permute-done((bf16[256,768]{1,0:T(8,128)(2,1)S(1)}, bf16[256,768]{1,0:T(8,128)(2,1)S(1)}, u32[]{:S(2)}, u32[]{:S(2)}) %collective-permute-start.14) | collective-permute-done | bytes 393248 | tf_op jit(solution)/shard_map/ppermute | solution.py:449
  79.5 4.3 %collective-permute-done.19.refs_4_.refs_1_ = bf16[1024,512]{1,0:T(8,128)(2,1)S(1)} collective-permute-done((bf16[1024,512]{1,0:T(8,128)(2,1)S(1)}, bf16[1024,512]{1,0:T(8,128)(2,1)S(1)}, u32[]{:S(2)}, u32[]{:S(2)}) %collective-permute-start.19) | collective-permute-done | bytes 1048608 | tf_op jit(solution)/shard_map/ppermute | solution.py:508
  83.8 2.8 %collective-permute-start.20 = (bf16[384,256]{1,0:T(8,128)(2,1)S(1)}, bf16[384,256]{1,0:T(8,128)(2,1)S(1)}, u32[]{:S(2)}, u32[]{:S(2)}) collective-permute-start(bf16[384,256]{1,0:T(8,128)(2,1)S(1)} %get-tuple-element.58), channel_id=1, source_target_pairs={{0,4},{4,0},{8,12},{12,8},{1,5},{5,1},{9,13},{13,9},{2,6},{6,2},{1... | collective-permute-start | bytes 589832 | tf_op jit(solution)/shard_map/ppermute | solution.py:449
  86.6 2.8 %collective-permute-start.21 = (bf16[384,256]{1,0:T(8,128)(2,1)S(1)}, bf16[384,256]{1,0:T(8,128)(2,1)S(1)}, u32[]{:S(2)}, u32[]{:S(2)}) collective-permute-start(bf16[384,256]{1,0:T(8,128)(2,1)S(1)} %get-tuple-element.59), channel_id=1, source_target_pairs={{0,8},{4,12},{8,0},{12,4},{1,9},{5,13},{9,1},{13,5},{2,10},{6,14},... | collective-permute-start | bytes 589832 | tf_op jit(solution)/shard_map/ppermute | solution.py:449
  89.4 0.6 collective-permute-start.22
  90.0 8.3 %row_grads.1 = (bf16[144,512]{1,0:T(8,128)(2,1)S(1)}, bf16[144,512]{1,0:T(8,128)(2,1)S(1)}, bf16[144,512]{1,0:T(8,128)(2,1)S(1)}, bf16[144,512]{1,0:T(8,128)(2,1)S(1)}) custom-call(s32[2]{0:T(128)S(1)} %pad_add_fusion.ids_ref, bf16[256,768]{1,0:T(8,128)(2,1)S(1)} %get-tuple-element.47.refs_0_, bf16[256,768]{1,0:T(8,128)(2,1)S(1)} %collective-permute-done.13.refs_1_, ...), custom_call_target="tpu_custom_call" | custom-call | tf_op jit(solution)/shard_map/row_grads/pallas_call | solution.py:688
  98.3 0.7 collective-permute-start.16
  99.0 1.4 %collective-permute-start.17 = (bf16[144,512]{1,0:T(8,128)(2,1)S(1)}, bf16[144,512]{1,0:T(8,128)(2,1)S(1)}, u32[]{:S(2)}, u32[]{:S(2)}) collective-permute-start(bf16[144,512]{1,0:T(8,128)(2,1)S(1)} %get-tuple-element.51), channel_id=1, source_target_pairs={{0,4},{4,0},{8,12},{12,8},{1,5},{5,1},{9,13},{13,9},{2,6},{6,2},{1... | collective-permute-start | bytes 442376 | tf_op jit(solution)/shard_map/ppermute | solution.py:449
  100.4 1.7 %collective-permute-done.21.refs_3_.refs_2_ = bf16[384,256]{1,0:T(8,128)(2,1)S(1)} collective-permute-done((bf16[384,256]{1,0:T(8,128)(2,1)S(1)}, bf16[384,256]{1,0:T(8,128)(2,1)S(1)}, u32[]{:S(2)}, u32[]{:S(2)}) %collective-permute-start.21) | collective-permute-done | bytes 196640 | tf_op jit(solution)/shard_map/ppermute | solution.py:449
  102.1 0.6 pick.1.refs_3_
  102.7 2.5 %collective-permute-done.16.refs_2_.refs_1_ = bf16[144,512]{1,0:T(8,128)(2,1)S(1)} collective-permute-done((bf16[144,512]{1,0:T(8,128)(2,1)S(1)}, bf16[144,512]{1,0:T(8,128)(2,1)S(1)}, u32[]{:S(2)}, u32[]{:S(2)}) %collective-permute-start.16) | collective-permute-done | bytes 147488 | tf_op jit(solution)/shard_map/ppermute | solution.py:449
  105.2 2.1 %collective-permute-done.17.refs_3_.refs_2_ = bf16[144,512]{1,0:T(8,128)(2,1)S(1)} collective-permute-done((bf16[144,512]{1,0:T(8,128)(2,1)S(1)}, bf16[144,512]{1,0:T(8,128)(2,1)S(1)}, u32[]{:S(2)}, u32[]{:S(2)}) %collective-permute-start.17) | collective-permute-done | bytes 147488 | tf_op jit(solution)/shard_map/ppermute | solution.py:449
  107.3 0.6 collective-permute-start.24
  108.0 1.3 collective-permute-start.27
  109.2 0.1 collective-permute-start.23
  109.3 16.5 %collective-permute-done.24.refs_2_ = bf16[4,384,256]{2,1,0:T(8,128)(2,1)S(1)} collective-permute-done((bf16[4,384,256]{2,1,0:T(8,128)(2,1)S(1)}, bf16[4,384,256]{2,1,0:T(8,128)(2,1)S(1)}, u32[]{:S(2)}, u32[]{:S(2)}) %collective-permute-start.24) | collective-permute-done | bytes 786464 | tf_op jit(solution)/shard_map/ppermute | solution.py:449
  125.9 2.2 %collective-permute-done.25.refs_3_ = bf16[4,384,256]{2,1,0:T(8,128)(2,1)S(1)} collective-permute-done((bf16[4,384,256]{2,1,0:T(8,128)(2,1)S(1)}, bf16[4,384,256]{2,1,0:T(8,128)(2,1)S(1)}, u32[]{:S(2)}, u32[]{:S(2)}) %collective-permute-start.25) | collective-permute-done | bytes 786464 | tf_op jit(solution)/shard_map/ppermute | solution.py:449
  128.2 0.2 collective-permute-start.26
  128.4 5.1 %collective-permute-done.27.refs_7_.refs_10_ = bf16[1024,512]{1,0:T(8,128)(2,1)S(1)} collective-permute-done((bf16[1024,512]{1,0:T(8,128)(2,1)S(1)}, bf16[1024,512]{1,0:T(8,128)(2,1)S(1)}, u32[]{:S(2)}, u32[]{:S(2)}) %collective-permute-start.27) | collective-permute-done | bytes 1048608 | tf_op jit(solution)/shard_map/ppermute | solution.py:506
  133.5 7.7 %in_grads.1 = (bf16[16,384,512]{2,1,0:T(8,128)(2,1)}, f32[8,128]{1,0:T(8,128)S(1)}) custom-call(s32[2]{0:T(128)S(1)} %pad_add_fusion.ids_ref, s32[4,16]{1,0:T(4,128)S(1)} %bitcast.16, bf16[4,384,256]{2,1,0:T(8,128)(2,1)S(1)} %stack_columns.3.refs_0_, bf16[4,384,256]{2,1,0:T(8,128)(2,1)S(1)} %collective-permute-done.23.refs_1_, ...), custom_call_target="tpu_custom_call" | custom-call | tf_op jit(solution)/shard_map/in_grads/pallas_call | solution.py:622
  141.2 0.8 token_grads.1
  (46 shorter events, 0.3 us)
Async XLA Ops:
  0.6 10.7 %copy-start = (bf16[8,128,1536]{2,1,0:T(8,128)(2,1)S(1)}, bf16[8,128,1536]{2,1,0:T(8,128)(2,1)}, u32[]{:S(2)}) copy-start(bf16[8,128,1536]{2,1,0:T(8,128)(2,1)} %param.17) | copy-start | bytes 9437188
  3.5 7.8 %collective-permute-start = (bf16[144,512]{1,0:T(8,128)(2,1)}, bf16[144,512]{1,0:T(8,128)(2,1)S(1)}, u32[]{:S(2)}, u32[]{:S(2)}) collective-permute-start(bf16[144,512]{1,0:T(8,128)(2,1)} %route.1.refs_1_.refs_0_), channel_id=1, source_target_pairs={{0,4},{4,0},{8,12},{12,8},{1,5},{5,1},{9,13},{13,9},{2,6},{6,2},{1... | collective-permute-start | bytes 442376 | tf_op jit(solution)/shard_map/ppermute | solution.py:449
  6.5 11.9 %collective-permute-start.2 = (bf16[144,512]{1,0:T(8,128)(2,1)}, bf16[144,512]{1,0:T(8,128)(2,1)S(1)}, u32[]{:S(2)}, u32[]{:S(2)}) collective-permute-start(bf16[144,512]{1,0:T(8,128)(2,1)} %route.1.refs_1_.refs_0_), channel_id=1, source_target_pairs={{0,12},{4,8},{8,4},{12,0},{1,13},{5,9},{9,5},{13,1},{2,14},{6,10},... | collective-permute-start | bytes 442376 | tf_op jit(solution)/shard_map/ppermute | solution.py:449
  9.0 18.8 %collective-permute-start.1 = (bf16[144,512]{1,0:T(8,128)(2,1)}, bf16[144,512]{1,0:T(8,128)(2,1)}, u32[]{:S(2)}, u32[]{:S(2)}) collective-permute-start(bf16[144,512]{1,0:T(8,128)(2,1)} %route.1.refs_1_.refs_0_), channel_id=1, source_target_pairs={{0,8},{4,12},{8,0},{12,4},{1,9},{5,13},{9,1},{13,5},{2,10},{6,14},... | collective-permute-start | bytes 442376 | tf_op jit(solution)/shard_map/ppermute | solution.py:449
  10.4 0.9 copy-start.2
  11.3 24.5 %copy-start.3 = (bf16[144,512]{1,0:T(8,128)(2,1)S(1)}, bf16[144,512]{1,0:T(8,128)(2,1)}, u32[]{:S(2)}) copy-start(bf16[144,512]{1,0:T(8,128)(2,1)} %route.1.refs_1_.refs_0_) | copy-start | bytes 442372
  12.4 15.4 %collective-permute-start.4 = (bf16[192,256]{1,0:T(8,128)(2,1)S(1)}, bf16[192,256]{1,0:T(8,128)(2,1)S(1)}, u32[]{:S(2)}, u32[]{:S(2)}) collective-permute-start(bf16[192,256]{1,0:T(8,128)(2,1)S(1)} %get-tuple-element.41), channel_id=1, source_target_pairs={{0,4},{4,0},{8,12},{12,8},{1,5},{5,1},{9,13},{13,9},{2,6},{6,2},{1... | collective-permute-start | bytes 294920 | tf_op jit(solution)/shard_map/ppermute | solution.py:449
  14.4 15.4 %collective-permute-start.5 = (bf16[192,256]{1,0:T(8,128)(2,1)S(1)}, bf16[192,256]{1,0:T(8,128)(2,1)S(1)}, u32[]{:S(2)}, u32[]{:S(2)}) collective-permute-start(bf16[192,256]{1,0:T(8,128)(2,1)S(1)} %get-tuple-element.42), channel_id=1, source_target_pairs={{0,8},{4,12},{8,0},{12,4},{1,9},{5,13},{9,1},{13,5},{2,10},{6,14},... | collective-permute-start | bytes 294920 | tf_op jit(solution)/shard_map/ppermute | solution.py:449
  18.4 11.4 %collective-permute-start.6 = (bf16[192,256]{1,0:T(8,128)(2,1)S(1)}, bf16[192,256]{1,0:T(8,128)(2,1)S(1)}, u32[]{:S(2)}, u32[]{:S(2)}) collective-permute-start(bf16[192,256]{1,0:T(8,128)(2,1)S(1)} %get-tuple-element.43), channel_id=1, source_target_pairs={{0,12},{4,8},{8,4},{12,0},{1,13},{5,9},{9,5},{13,1},{2,14},{6,10},... | collective-permute-start | bytes 294920 | tf_op jit(solution)/shard_map/ppermute | solution.py:449
  29.8 30.4 %copy-start.4 = (s32[16,4]{0,1:T(4,128)S(1)}, s32[16,4]{0,1:T(4,128)}, u32[]{:S(2)}) copy-start(s32[16,4]{0,1:T(4,128)} %param.14) | copy-start | bytes 772
  29.8 25.7 %collective-permute-start.8 = (bf16[1024,512]{1,0:T(8,128)(2,1)S(1)}, bf16[1024,512]{1,0:T(8,128)(2,1)S(1)}, u32[]{:S(2)}, u32[]{:S(2)}) collective-permute-start(bf16[1024,512]{1,0:T(8,128)(2,1)S(1)} %gate.10), channel_id=1, source_target_pairs={{12,8},{8,4},{4,0},{13,9},{9,5},{5,1},{14,10},{10,6},{6,2},{15,11}... | collective-permute-start | bytes 3145736 | tf_op jit(solution)/shard_map/ppermute | solution.py:508
  31.2 25.4 %collective-permute-start.7 = (bf16[1024,512]{1,0:T(8,128)(2,1)S(1)}, bf16[1024,512]{1,0:T(8,128)(2,1)S(1)}, u32[]{:S(2)}, u32[]{:S(2)}) collective-permute-start(bf16[1024,512]{1,0:T(8,128)(2,1)S(1)} %gate.10), channel_id=1, source_target_pairs={{0,4},{4,8},{8,12},{1,5},{5,9},{9,13},{2,6},{6,10},{10,14},{3,7},{... | collective-permute-start | bytes 3145736 | tf_op jit(solution)/shard_map/ppermute | solution.py:508
  42.2 12.4 %collective-permute-start.3 = (bf16[2,256,768]{2,1,0:T(8,128)(2,1)S(1)}, bf16[2,256,768]{2,1,0:T(8,128)(2,1)S(1)}, u32[]{:S(2)}, u32[]{:S(2)}) collective-permute-start(bf16[2,256,768]{2,1,0:T(8,128)(2,1)S(1)} %get-tuple-element.38), channel_id=1, source_target_pairs={{0,1},{1,0},{2,3},{3,2},{4,5},{5,4},{6,7},{7,6},{8,9},{9,8},{10,11... | collective-permute-start | bytes 2359304 | tf_op jit(solution)/shard_map/ppermute | solution.py:449
  42.3 12.3 %collective-permute-start.11 = (bf16[4,192,256]{2,1,0:T(8,128)(2,1)S(1)}, bf16[4,192,256]{2,1,0:T(8,128)(2,1)S(1)}, u32[]{:S(2)}, u32[]{:S(2)}) collective-permute-start(bf16[4,192,256]{2,1,0:T(8,128)(2,1)S(1)} %stack_columns.2.refs_0_), channel_id=1, source_target_pairs={{0,2},{1,3},{2,0},{3,1},{4,6},{5,7},{6,4},{7,5},{8,10},{9,11},{10,... | collective-permute-start | bytes 1179656 | tf_op jit(solution)/shard_map/ppermute | solution.py:449
  44.8 15.3 %collective-permute-start.10 = (bf16[4,192,256]{2,1,0:T(8,128)(2,1)S(1)}, bf16[4,192,256]{2,1,0:T(8,128)(2,1)S(1)}, u32[]{:S(2)}, u32[]{:S(2)}) collective-permute-start(bf16[4,192,256]{2,1,0:T(8,128)(2,1)S(1)} %stack_columns.2.refs_0_), channel_id=1, source_target_pairs={{0,1},{1,0},{2,3},{3,2},{4,5},{5,4},{6,7},{7,6},{8,9},{9,8},{10,11... | collective-permute-start | bytes 1179656 | tf_op jit(solution)/shard_map/ppermute | solution.py:449
  54.6 5.5 %collective-permute-start.12 = (bf16[4,192,256]{2,1,0:T(8,128)(2,1)S(1)}, bf16[4,192,256]{2,1,0:T(8,128)(2,1)S(1)}, u32[]{:S(2)}, u32[]{:S(2)}) collective-permute-start(bf16[4,192,256]{2,1,0:T(8,128)(2,1)S(1)} %collective-permute-done.11.refs_2_), channel_id=1, source_target_pairs={{0,1},{1,0},{2,3},{3,2},{4,5},{5,4},{6,7},{7,6},{8,9},{9,8},{10,11... | collective-permute-start | bytes 1179656 | tf_op jit(solution)/shard_map/ppermute | solution.py:449
  56.6 11.4 %collective-permute-start.9 = (bf16[1,256,768]{2,1,0:T(8,128)(2,1)S(1)}, bf16[1,256,768]{2,1,0:T(8,128)(2,1)S(1)}, u32[]{:S(2)}, u32[]{:S(2)}) collective-permute-start(bf16[1,256,768]{2,1,0:T(8,128)(2,1)S(1)} %gate.11), channel_id=1, source_target_pairs={{0,2},{1,3},{2,0},{3,1},{4,6},{5,7},{6,4},{7,5},{8,10},{9,11},{10,... | collective-permute-start | bytes 1179656 | tf_op jit(solution)/shard_map/ppermute | solution.py:449
  58.1 25.7 %collective-permute-start.19 = (bf16[1024,512]{1,0:T(8,128)(2,1)S(1)}, bf16[1024,512]{1,0:T(8,128)(2,1)S(1)}, u32[]{:S(2)}, u32[]{:S(2)}) collective-permute-start(bf16[1024,512]{1,0:T(8,128)(2,1)S(1)} %collective-permute-done.8.refs_2_.refs_8_), channel_id=1, source_target_pairs={{8,4},{4,0},{9,5},{5,1},{10,6},{6,2},{11,7},{7,3},{24,20},{20,16},... | collective-permute-start | bytes 3145736 | tf_op jit(solution)/shard_map/ppermute | solution.py:508
  59.4 24.4 %collective-permute-start.18 = (bf16[1024,512]{1,0:T(8,128)(2,1)S(1)}, bf16[1024,512]{1,0:T(8,128)(2,1)S(1)}, u32[]{:S(2)}, u32[]{:S(2)}) collective-permute-start(bf16[1024,512]{1,0:T(8,128)(2,1)S(1)} %collective-permute-done.7.refs_1_.refs_5_), channel_id=1, source_target_pairs={{4,8},{8,12},{5,9},{9,13},{6,10},{10,14},{7,11},{11,15},{20,24},{2... | collective-permute-start | bytes 3145736 | tf_op jit(solution)/shard_map/ppermute | solution.py:508
  69.6 9.8 %collective-permute-start.14 = (bf16[256,768]{1,0:T(8,128)(2,1)S(1)}, bf16[256,768]{1,0:T(8,128)(2,1)S(1)}, u32[]{:S(2)}, u32[]{:S(2)}) collective-permute-start(bf16[256,768]{1,0:T(8,128)(2,1)S(1)} %get-tuple-element.47.refs_0_), channel_id=1, source_target_pairs={{0,2},{1,3},{2,0},{3,1},{4,6},{5,7},{6,4},{7,5},{8,10},{9,11},{10,... | collective-permute-start | bytes 1179656 | tf_op jit(solution)/shard_map/ppermute | solution.py:449
  70.2 19.8 %collective-permute-start.13 = (bf16[256,768]{1,0:T(8,128)(2,1)S(1)}, bf16[256,768]{1,0:T(8,128)(2,1)S(1)}, u32[]{:S(2)}, u32[]{:S(2)}) collective-permute-start(bf16[256,768]{1,0:T(8,128)(2,1)S(1)} %get-tuple-element.47.refs_0_), channel_id=1, source_target_pairs={{0,1},{1,0},{2,3},{3,2},{4,5},{5,4},{6,7},{7,6},{8,9},{9,8},{10,11... | collective-permute-start | bytes 1179656 | tf_op jit(solution)/shard_map/ppermute | solution.py:449
  79.5 10.5 %collective-permute-start.15 = (bf16[256,768]{1,0:T(8,128)(2,1)S(1)}, bf16[256,768]{1,0:T(8,128)(2,1)S(1)}, u32[]{:S(2)}, u32[]{:S(2)}) collective-permute-start(bf16[256,768]{1,0:T(8,128)(2,1)S(1)} %collective-permute-done.14.refs_2_), channel_id=1, source_target_pairs={{0,1},{1,0},{2,3},{3,2},{4,5},{5,4},{6,7},{7,6},{8,9},{9,8},{10,11... | collective-permute-start | bytes 1179656 | tf_op jit(solution)/shard_map/ppermute | solution.py:449
  83.8 16.6 %collective-permute-start.20 = (bf16[384,256]{1,0:T(8,128)(2,1)S(1)}, bf16[384,256]{1,0:T(8,128)(2,1)S(1)}, u32[]{:S(2)}, u32[]{:S(2)}) collective-permute-start(bf16[384,256]{1,0:T(8,128)(2,1)S(1)} %get-tuple-element.58), channel_id=1, source_target_pairs={{0,4},{4,0},{8,12},{12,8},{1,5},{5,1},{9,13},{13,9},{2,6},{6,2},{1... | collective-permute-start | bytes 589832 | tf_op jit(solution)/shard_map/ppermute | solution.py:449
  86.6 15.5 %collective-permute-start.21 = (bf16[384,256]{1,0:T(8,128)(2,1)S(1)}, bf16[384,256]{1,0:T(8,128)(2,1)S(1)}, u32[]{:S(2)}, u32[]{:S(2)}) collective-permute-start(bf16[384,256]{1,0:T(8,128)(2,1)S(1)} %get-tuple-element.59), channel_id=1, source_target_pairs={{0,8},{4,12},{8,0},{12,4},{1,9},{5,13},{9,1},{13,5},{2,10},{6,14},... | collective-permute-start | bytes 589832 | tf_op jit(solution)/shard_map/ppermute | solution.py:449
  89.4 12.7 %collective-permute-start.22 = (bf16[384,256]{1,0:T(8,128)(2,1)S(1)}, bf16[384,256]{1,0:T(8,128)(2,1)S(1)}, u32[]{:S(2)}, u32[]{:S(2)}) collective-permute-start(bf16[384,256]{1,0:T(8,128)(2,1)S(1)} %get-tuple-element.60), channel_id=1, source_target_pairs={{0,12},{4,8},{8,4},{12,0},{1,13},{5,9},{9,5},{13,1},{2,14},{6,10},... | collective-permute-start | bytes 589832 | tf_op jit(solution)/shard_map/ppermute | solution.py:449
  98.3 35.2 %copy-start.1 = (bf16[8,4,32,512]{3,2,1,0:T(8,128)(2,1)S(1)}, bf16[8,4,32,512]{3,2,1,0:T(8,128)(2,1)}, u32[]{:S(2)}) copy-start(bf16[8,4,32,512]{3,2,1,0:T(8,128)(2,1)} %param.16) | copy-start | bytes 3145732
  98.3 6.9 %collective-permute-start.16 = (bf16[144,512]{1,0:T(8,128)(2,1)S(1)}, bf16[144,512]{1,0:T(8,128)(2,1)S(1)}, u32[]{:S(2)}, u32[]{:S(2)}) collective-permute-start(bf16[144,512]{1,0:T(8,128)(2,1)S(1)} %get-tuple-element.50), channel_id=1, source_target_pairs={{0,4},{4,0},{8,12},{12,8},{1,5},{5,1},{9,13},{13,9},{2,6},{6,2},{1... | collective-permute-start | bytes 442376 | tf_op jit(solution)/shard_map/ppermute | solution.py:449
  99.0 8.3 %collective-permute-start.17 = (bf16[144,512]{1,0:T(8,128)(2,1)S(1)}, bf16[144,512]{1,0:T(8,128)(2,1)S(1)}, u32[]{:S(2)}, u32[]{:S(2)}) collective-permute-start(bf16[144,512]{1,0:T(8,128)(2,1)S(1)} %get-tuple-element.51), channel_id=1, source_target_pairs={{0,4},{4,0},{8,12},{12,8},{1,5},{5,1},{9,13},{13,9},{2,6},{6,2},{1... | collective-permute-start | bytes 442376 | tf_op jit(solution)/shard_map/ppermute | solution.py:449
  107.3 18.5 %collective-permute-start.24 = (bf16[4,384,256]{2,1,0:T(8,128)(2,1)S(1)}, bf16[4,384,256]{2,1,0:T(8,128)(2,1)S(1)}, u32[]{:S(2)}, u32[]{:S(2)}) collective-permute-start(bf16[4,384,256]{2,1,0:T(8,128)(2,1)S(1)} %stack_columns.3.refs_0_), channel_id=1, source_target_pairs={{0,2},{1,3},{2,0},{3,1},{4,6},{5,7},{6,4},{7,5},{8,10},{9,11},{10,... | collective-permute-start | bytes 2359304 | tf_op jit(solution)/shard_map/ppermute | solution.py:449
  108.0 25.5 %collective-permute-start.27 = (bf16[1024,512]{1,0:T(8,128)(2,1)S(1)}, bf16[1024,512]{1,0:T(8,128)(2,1)S(1)}, u32[]{:S(2)}, u32[]{:S(2)}) collective-permute-start(bf16[1024,512]{1,0:T(8,128)(2,1)S(1)} %pick.1.refs_3_), channel_id=1, source_target_pairs={{8,12},{4,0},{9,13},{5,1},{10,14},{6,2},{11,15},{7,3},{24,28},{20,... | collective-permute-start | bytes 3145736 | tf_op jit(solution)/shard_map/ppermute | solution.py:506
  109.2 16.7 %collective-permute-start.23 = (bf16[4,384,256]{2,1,0:T(8,128)(2,1)S(1)}, bf16[4,384,256]{2,1,0:T(8,128)(2,1)S(1)}, u32[]{:S(2)}, u32[]{:S(2)}) collective-permute-start(bf16[4,384,256]{2,1,0:T(8,128)(2,1)S(1)} %stack_columns.3.refs_0_), channel_id=1, source_target_pairs={{0,1},{1,0},{2,3},{3,2},{4,5},{5,4},{6,7},{7,6},{8,9},{9,8},{10,11... | collective-permute-start | bytes 2359304 | tf_op jit(solution)/shard_map/ppermute | solution.py:449
  125.9 2.3 %collective-permute-start.25 = (bf16[4,384,256]{2,1,0:T(8,128)(2,1)S(1)}, bf16[4,384,256]{2,1,0:T(8,128)(2,1)S(1)}, u32[]{:S(2)}, u32[]{:S(2)}) collective-permute-start(bf16[4,384,256]{2,1,0:T(8,128)(2,1)S(1)} %collective-permute-done.24.refs_2_), channel_id=1, source_target_pairs={{0,1},{1,0},{2,3},{3,2},{4,5},{5,4},{6,7},{7,6},{8,9},{9,8},{10,11... | collective-permute-start | bytes 2359304 | tf_op jit(solution)/shard_map/ppermute | solution.py:449
  128.1 13.0 %copy-start.5 = (s32[128,8]{0,1:T(8,128)S(1)}, s32[128,8]{0,1:T(8,128)}, u32[]{:S(2)}) copy-start(s32[128,8]{0,1:T(8,128)} %param.12) | copy-start | bytes 12292
  128.1 13.0 %copy-start.6 = (s32[128,8]{0,1:T(8,128)S(1)}, s32[128,8]{0,1:T(8,128)}, u32[]{:S(2)}) copy-start(s32[128,8]{0,1:T(8,128)} %param.13) | copy-start | bytes 12292
  128.2 13.0 %collective-permute-start.26 = (bf16[144,512]{1,0:T(8,128)(2,1)S(1)}, bf16[144,512]{1,0:T(8,128)(2,1)S(1)}, u32[]{:S(2)}, u32[]{:S(2)}) collective-permute-start(bf16[144,512]{1,0:T(8,128)(2,1)S(1)} %gate.16), channel_id=1, source_target_pairs={{0,8},{4,12},{8,0},{12,4},{1,9},{5,13},{9,1},{13,5},{2,10},{6,14},... | collective-permute-start | bytes 442376 | tf_op jit(solution)/shard_map/ppermute | solution.py:449

commit v18 on v14

--- a/solution.py
+++ b/solution.py
@@ -552,7 +552,7 @@
         name="hidden_columns",
     )(ids, pair_rows, bufs[1], chain[0])
     downs = [downs[0]] + [swap(downs[k], "ep", n, k) for k in range(1, n)]
-    chain = gate(chain, bufs[1:] + downs[1:])
+    chain = gate(chain, bufs[1:] + downs[1:-1])
     steps = [list(chain_step(chain[0], chain[0], "ep", n, 1))]
 
     def stack(pieces):

time: 143 us -> 157 us (1.098)
  waiting for transfers between devices: 67.3 us -> 81.2 us
    ppermute x23, waiting for transfers between devices: 53.7 us -> 69.4 us  [swap(): return lax.ppermute(x, axis, [(i, i ^ bit) for i in range(size)])]
    ppermute x4, waiting for transfers between devices: 6.14 us -> 4.31 us  [chain_step(): return (lax.ppermute(go, axis, rights), lax.ppermute(back, axis, lefts))]
  transfers between devices with their start and end apart: 28 -> 28, of which waited for: 12 -> 13; matrix products, arithmetic and copies ran while one was open for 1% -> 1% of each run, Pallas kernels for 24% -> 22%
where the time goes in v18:
time: 157 us
  waiting for transfers between devices  81.2 us (52%)
  Pallas kernels  36.8 us (23%)
  starting transfers between devices  34.9 us (22%)
  local copies, waits for them, and re-layouts  2.16 us (1%)
  between operations  1.68 us (1%)
    ppermute x23, waiting for transfers between devices, swap(): return lax.ppermute(x, axis, [(i, i ^ bit) for i in range(size)])  69.4 us
    ppermute x23, starting transfers between devices, swap(): return lax.ppermute(x, axis, [(i, i ^ bit) for i in range(size)])  25.5 us
    pallas_call x2, Pallas kernels, total_call(): pl.pallas_call(functools.partial(kernel, z), grid_spec=pltpu.PrefetchScal...  15.5 us
    pallas_call x1, Pallas kernels, body(): pl.pallas_call(functools.partial(row_kernel, z), grid_spec=pltpu.Prefetch...  8.31 us
    ppermute x4, starting transfers between devices, chain_step(): return (lax.ppermute(go, axis, rights), lax.ppermute(back, axis, lefts))  8.03 us
    ppermute x1, waiting for transfers between devices, chain_step(): got = lax.ppermute(go, axis, rights + lefts)  7.44 us
    pallas_call x1, Pallas kernels, body(): pl.pallas_call(functools.partial(down_kernel, z), grid_spec=pltpu.Prefetc...  6.4 us
    ppermute x4, waiting for transfers between devices, chain_step(): return (lax.ppermute(go, axis, rights), lax.ppermute(back, axis, lefts))  4.31 us
  transfers between devices with their start and end apart: 28, of which 13 were waited for; matrix products, arithmetic and copies ran while one was open for 1% of the time, Pallas kernels for 22%

profile of v18, /device:TPU:0, one launch (start us, length us, event | category | flops | bytes accessed | tf_op | source)
XLA Modules:
  0.0 156.7 jit_solution(11206654150880937089)
XLA Ops:
  1.4 2.0 %route.1.refs_1_.refs_0_ = bf16[144,512]{1,0:T(8,128)(2,1)} custom-call(s32[1]{0:T(128)S(6)} %copy.38.count_ref, bf16[128,512]{1,0:T(8,128)(2,1)} %grad_ref.1, bf16[8,128]{1,0:T(8,128)(2,1)} %bitcast.22, s32[8,128]{1,0:T(8,128)} %bitcast.18, s32[8,128]{1,0:T(8,128)} %bitcast.20, s32[4,16]{1,0:T(4,128)} %bitcast.14), custom_call_target="tpu_custom_call" | custom-call | tf_op jit(solution)/shard_map/route/pallas_call | solution.py:525
  3.5 3.0 %collective-permute-start = (bf16[144,512]{1,0:T(8,128)(2,1)}, bf16[144,512]{1,0:T(8,128)(2,1)S(1)}, u32[]{:S(2)}, u32[]{:S(2)}) collective-permute-start(bf16[144,512]{1,0:T(8,128)(2,1)} %route.1.refs_1_.refs_0_), channel_id=1, source_target_pairs={{0,4},{4,0},{8,12},{12,8},{1,5},{5,1},{9,13},{13,9},{2,6},{6,2},{1... | collective-permute-start | bytes 442376 | tf_op jit(solution)/shard_map/ppermute | solution.py:440
  6.5 2.5 %collective-permute-start.2 = (bf16[144,512]{1,0:T(8,128)(2,1)}, bf16[144,512]{1,0:T(8,128)(2,1)S(1)}, u32[]{:S(2)}, u32[]{:S(2)}) collective-permute-start(bf16[144,512]{1,0:T(8,128)(2,1)} %route.1.refs_1_.refs_0_), channel_id=1, source_target_pairs={{0,12},{4,8},{8,4},{12,0},{1,13},{5,9},{9,5},{13,1},{2,14},{6,10},... | collective-permute-start | bytes 442376 | tf_op jit(solution)/shard_map/ppermute | solution.py:440
  9.0 0.1 collective-permute-start.1
  9.1 0.1 pad_add_fusion.ids_ref
  9.2 1.2 copy.26.refs_0_
  10.4 0.9 copy-done.2
  11.3 1.1 hidden_columns.1
  12.4 2.0 %collective-permute-start.4 = (bf16[192,256]{1,0:T(8,128)(2,1)S(1)}, bf16[192,256]{1,0:T(8,128)(2,1)S(1)}, u32[]{:S(2)}, u32[]{:S(2)}) collective-permute-start(bf16[192,256]{1,0:T(8,128)(2,1)S(1)} %get-tuple-element.41), channel_id=1, source_target_pairs={{0,4},{4,0},{8,12},{12,8},{1,5},{5,1},{9,13},{13,9},{2,6},{6,2},{1... | collective-permute-start | bytes 294920 | tf_op jit(solution)/shard_map/ppermute | solution.py:440
  14.4 4.0 %collective-permute-start.5 = (bf16[192,256]{1,0:T(8,128)(2,1)S(1)}, bf16[192,256]{1,0:T(8,128)(2,1)S(1)}, u32[]{:S(2)}, u32[]{:S(2)}) collective-permute-start(bf16[192,256]{1,0:T(8,128)(2,1)S(1)} %get-tuple-element.42), channel_id=1, source_target_pairs={{0,8},{4,12},{8,0},{12,4},{1,9},{5,13},{9,1},{13,5},{2,10},{6,14},... | collective-permute-start | bytes 294920 | tf_op jit(solution)/shard_map/ppermute | solution.py:440
  18.4 7.3 %collective-permute-done.1.refs_2_ = bf16[144,512]{1,0:T(8,128)(2,1)} collective-permute-done((bf16[144,512]{1,0:T(8,128)(2,1)}, bf16[144,512]{1,0:T(8,128)(2,1)}, u32[]{:S(2)}, u32[]{:S(2)}) %collective-permute-start.1) | collective-permute-done | bytes 147488 | tf_op jit(solution)/shard_map/ppermute | solution.py:440
  25.7 0.9 collective-permute-done.5.refs_5_.refs_2_
  26.6 1.4 collective-permute-start.7
  28.0 4.6 %collective-permute-start.6 = (bf16[1024,512]{1,0:T(8,128)(2,1)S(1)}, bf16[1024,512]{1,0:T(8,128)(2,1)S(1)}, u32[]{:S(2)}, u32[]{:S(2)}) collective-permute-start(bf16[1024,512]{1,0:T(8,128)(2,1)S(1)} %gate.10), channel_id=1, source_target_pairs={{0,4},{4,8},{8,12},{1,5},{5,9},{9,13},{2,6},{6,10},{10,14},{3,7},{... | collective-permute-start | bytes 3145736 | tf_op jit(solution)/shard_map/ppermute | solution.py:499
  32.6 6.4 %hidden_partials.1 = (bf16[2,256,768]{2,1,0:T(8,128)(2,1)S(1)}, bf16[2,256,768]{2,1,0:T(8,128)(2,1)S(1)}, bf16[4,128,512]{2,1,0:T(8,128)(2,1)S(1)}, f32[4,64,128]{2,1,0:T(8,128)S(1)}) custom-call(s32[2]{0:T(128)S(1)} %pad_add_fusion.ids_ref, bf16[144,512]{1,0:T(8,128)(2,1)S(1)} %copy-done.3, bf16[144,512]{1,0:T(8,128)(2,1)S(1)} %collective-permute-done.after_ref.refs_1_, ...), custom_call_target="tpu_custom_call" | custom-call | tf_op jit(solution)/shard_map/hidden_partials/pallas_call | solution.py:587
  39.1 0.1 collective-permute-start.3
  39.1 0.1 collective-permute-start.9
  39.2 16.9 %collective-permute-done.9.refs_3_ = bf16[192,256]{1,0:T(8,128)(2,1)S(1)} collective-permute-done((bf16[192,256]{1,0:T(8,128)(2,1)S(1)}, bf16[192,256]{1,0:T(8,128)(2,1)S(1)}, u32[]{:S(2)}, u32[]{:S(2)}) %collective-permute-start.9) | collective-permute-done | bytes 98336 | tf_op jit(solution)/shard_map/ppermute | solution.py:440
  56.1 1.6 collective-permute-start.11
  57.7 7.4 %collective-permute-done.11.refs_2_ = bf16[4,192,256]{2,1,0:T(8,128)(2,1)S(1)} collective-permute-done((bf16[4,192,256]{2,1,0:T(8,128)(2,1)S(1)}, bf16[4,192,256]{2,1,0:T(8,128)(2,1)S(1)}, u32[]{:S(2)}, u32[]{:S(2)}) %collective-permute-start.11) | collective-permute-done | bytes 393248 | tf_op jit(solution)/shard_map/ppermute | solution.py:440
  65.1 0.2 halve.1
  65.3 1.6 collective-permute-start.8
  66.9 1.3 collective-permute-start.19
  68.2 0.7 collective-permute-start.18
  68.9 7.8 %down_grads.1 = (bf16[16,192,512]{2,1,0:T(8,128)(2,1)}, f32[8,128]{1,0:T(8,128)S(1)}) custom-call(s32[2]{0:T(128)S(1)} %pad_add_fusion.ids_ref, s32[4,16]{1,0:T(4,128)S(1)} %bitcast.15, bf16[4,192,256]{2,1,0:T(8,128)(2,1)S(1)} %stack_columns.2.refs_0_, bf16[4,192,256]{2,1,0:T(8,128)(2,1)S(1)} %collective-permute-done.10.refs_1_, ...), custom_call_target="tpu_custom_call" | custom-call | tf_op jit(solution)/shard_map/down_grads/pallas_call | solution.py:613
  76.8 0.2 collective-permute-done.8.refs_0_
  76.9 1.6 %pre_grads.1 = (bf16[384,256]{1,0:T(8,128)(2,1)S(1)}, bf16[384,256]{1,0:T(8,128)(2,1)S(1)}, bf16[384,256]{1,0:T(8,128)(2,1)S(1)}, bf16[384,256]{1,0:T(8,128)(2,1)S(1)}, bf16[256,768]{1,0:T(8,128)(2,1)S(1)}) custom-call(s32[2]{0:T(128)S(1)} %pad_add_fusion.ids_ref, bf16[1,256,768]{2,1,0:T(8,128)(2,1)S(1)} %get-tuple-element.39.keep_ref, ...), custom_call_target="tpu_custom_call" | custom-call | tf_op jit(solution)/shard_map/pre_grads/pallas_call | solution.py:655
  78.6 1.6 collective-permute-start.14
  80.1 9.6 %collective-permute-done.14.refs_2_ = bf16[256,768]{1,0:T(8,128)(2,1)S(1)} collective-permute-done((bf16[256,768]{1,0:T(8,128)(2,1)S(1)}, bf16[256,768]{1,0:T(8,128)(2,1)S(1)}, u32[]{:S(2)}, u32[]{:S(2)}) %collective-permute-start.14) | collective-permute-done | bytes 393248 | tf_op jit(solution)/shard_map/ppermute | solution.py:440
  89.7 4.3 %collective-permute-done.19.refs_4_.refs_1_ = bf16[1024,512]{1,0:T(8,128)(2,1)S(1)} collective-permute-done((bf16[1024,512]{1,0:T(8,128)(2,1)S(1)}, bf16[1024,512]{1,0:T(8,128)(2,1)S(1)}, u32[]{:S(2)}, u32[]{:S(2)}) %collective-permute-start.19) | collective-permute-done | bytes 1048608 | tf_op jit(solution)/shard_map/ppermute | solution.py:499
  94.0 3.0 %collective-permute-start.20 = (bf16[384,256]{1,0:T(8,128)(2,1)S(1)}, bf16[384,256]{1,0:T(8,128)(2,1)S(1)}, u32[]{:S(2)}, u32[]{:S(2)}) collective-permute-start(bf16[384,256]{1,0:T(8,128)(2,1)S(1)} %get-tuple-element.57), channel_id=1, source_target_pairs={{0,4},{4,0},{8,12},{12,8},{1,5},{5,1},{9,13},{13,9},{2,6},{6,2},{1... | collective-permute-start | bytes 589832 | tf_op jit(solution)/shard_map/ppermute | solution.py:440
  97.0 2.3 %collective-permute-start.21 = (bf16[384,256]{1,0:T(8,128)(2,1)S(1)}, bf16[384,256]{1,0:T(8,128)(2,1)S(1)}, u32[]{:S(2)}, u32[]{:S(2)}) collective-permute-start(bf16[384,256]{1,0:T(8,128)(2,1)S(1)} %get-tuple-element.58), channel_id=1, source_target_pairs={{0,8},{4,12},{8,0},{12,4},{1,9},{5,13},{9,1},{13,5},{2,10},{6,14},... | collective-permute-start | bytes 589832 | tf_op jit(solution)/shard_map/ppermute | solution.py:440
  99.3 1.1 collective-permute-start.22
  100.4 8.3 %row_grads.1 = (bf16[160,512]{1,0:T(8,128)(2,1)S(1)}, bf16[160,512]{1,0:T(8,128)(2,1)S(1)}, bf16[160,512]{1,0:T(8,128)(2,1)S(1)}, bf16[160,512]{1,0:T(8,128)(2,1)S(1)}) custom-call(s32[2]{0:T(128)S(1)} %pad_add_fusion.ids_ref, bf16[256,768]{1,0:T(8,128)(2,1)S(1)} %get-tuple-element.47.refs_0_, bf16[256,768]{1,0:T(8,128)(2,1)S(1)} %collective-permute-done.13.refs_1_, ...), custom_call_target="tpu_custom_call" | custom-call | tf_op jit(solution)/shard_map/row_grads/pallas_call | solution.py:679
  108.7 0.6 collective-permute-start.16
  109.3 1.5 collective-permute-start.17
  110.8 3.4 %collective-permute-done.21.refs_3_.refs_2_ = bf16[384,256]{1,0:T(8,128)(2,1)S(1)} collective-permute-done((bf16[384,256]{1,0:T(8,128)(2,1)S(1)}, bf16[384,256]{1,0:T(8,128)(2,1)S(1)}, u32[]{:S(2)}, u32[]{:S(2)}) %collective-permute-start.21) | collective-permute-done | bytes 196640 | tf_op jit(solution)/shard_map/ppermute | solution.py:440
  114.2 0.6 pick.1.refs_3_
  114.8 2.4 %collective-permute-done.16.refs_2_.refs_1_ = bf16[160,512]{1,0:T(8,128)(2,1)S(1)} collective-permute-done((bf16[160,512]{1,0:T(8,128)(2,1)S(1)}, bf16[160,512]{1,0:T(8,128)(2,1)S(1)}, u32[]{:S(2)}, u32[]{:S(2)}) %collective-permute-start.16) | collective-permute-done | bytes 163872 | tf_op jit(solution)/shard_map/ppermute | solution.py:440
  117.3 3.4 %collective-permute-done.17.refs_3_.refs_2_ = bf16[160,512]{1,0:T(8,128)(2,1)S(1)} collective-permute-done((bf16[160,512]{1,0:T(8,128)(2,1)S(1)}, bf16[160,512]{1,0:T(8,128)(2,1)S(1)}, u32[]{:S(2)}, u32[]{:S(2)}) %collective-permute-start.17) | collective-permute-done | bytes 163872 | tf_op jit(solution)/shard_map/ppermute | solution.py:440
  120.7 0.6 collective-permute-start.26
  121.3 1.3 collective-permute-start.23
  122.7 17.6 %collective-permute-done.26.refs_2_ = bf16[4,384,256]{2,1,0:T(8,128)(2,1)S(1)} collective-permute-done((bf16[4,384,256]{2,1,0:T(8,128)(2,1)S(1)}, bf16[4,384,256]{2,1,0:T(8,128)(2,1)S(1)}, u32[]{:S(2)}, u32[]{:S(2)}) %collective-permute-start.26) | collective-permute-done | bytes 786464 | tf_op jit(solution)/shard_map/ppermute | solution.py:440
  140.3 0.1 sum_parts.1
  140.4 7.4 %collective-permute-done.23.refs_3_.refs_6_.refs_7_.refs_10_ = bf16[1024,512]{1,0:T(8,128)(2,1)S(1)} collective-permute-done((bf16[1024,512]{1,0:T(8,128)(2,1)S(1)}, bf16[1024,512]{1,0:T(8,128)(2,1)S(1)}, u32[]{:S(2)}, u32[]{:S(2)}) %collective-permute-start.23) | collective-permute-done | bytes 1048608 | tf_op jit(solution)/shard_map/ppermute | solution.py:497
  147.8 7.7 %in_grads.1 = (bf16[16,384,512]{2,1,0:T(8,128)(2,1)}, f32[8,128]{1,0:T(8,128)S(1)}) custom-call(s32[2]{0:T(128)S(1)} %pad_add_fusion.ids_ref, s32[4,16]{1,0:T(4,128)S(1)} %bitcast.16, bf16[4,384,256]{2,1,0:T(8,128)(2,1)S(1)} %stack_columns.3.refs_0_, bf16[4,384,256]{2,1,0:T(8,128)(2,1)S(1)} %collective-permute-done.25.refs_1_, ...), custom_call_target="tpu_custom_call" | custom-call | tf_op jit(solution)/shard_map/in_grads/pallas_call | solution.py:613
  155.5 0.3 collective-permute-done.24.refs_0_
  155.9 0.8 token_grads.1
  (46 shorter events, 0.2 us)
Async XLA Ops:
  0.6 10.7 %copy-start = (bf16[8,128,1536]{2,1,0:T(8,128)(2,1)S(1)}, bf16[8,128,1536]{2,1,0:T(8,128)(2,1)}, u32[]{:S(2)}) copy-start(bf16[8,128,1536]{2,1,0:T(8,128)(2,1)} %param.17) | copy-start | bytes 9437188
  3.5 7.8 %collective-permute-start = (bf16[144,512]{1,0:T(8,128)(2,1)}, bf16[144,512]{1,0:T(8,128)(2,1)S(1)}, u32[]{:S(2)}, u32[]{:S(2)}) collective-permute-start(bf16[144,512]{1,0:T(8,128)(2,1)} %route.1.refs_1_.refs_0_), channel_id=1, source_target_pairs={{0,4},{4,0},{8,12},{12,8},{1,5},{5,1},{9,13},{13,9},{2,6},{6,2},{1... | collective-permute-start | bytes 442376 | tf_op jit(solution)/shard_map/ppermute | solution.py:440
  6.5 11.9 %collective-permute-start.2 = (bf16[144,512]{1,0:T(8,128)(2,1)}, bf16[144,512]{1,0:T(8,128)(2,1)S(1)}, u32[]{:S(2)}, u32[]{:S(2)}) collective-permute-start(bf16[144,512]{1,0:T(8,128)(2,1)} %route.1.refs_1_.refs_0_), channel_id=1, source_target_pairs={{0,12},{4,8},{8,4},{12,0},{1,13},{5,9},{9,5},{13,1},{2,14},{6,10},... | collective-permute-start | bytes 442376 | tf_op jit(solution)/shard_map/ppermute | solution.py:440
  9.0 16.7 %collective-permute-start.1 = (bf16[144,512]{1,0:T(8,128)(2,1)}, bf16[144,512]{1,0:T(8,128)(2,1)}, u32[]{:S(2)}, u32[]{:S(2)}) collective-permute-start(bf16[144,512]{1,0:T(8,128)(2,1)} %route.1.refs_1_.refs_0_), channel_id=1, source_target_pairs={{0,8},{4,12},{8,0},{12,4},{1,9},{5,13},{9,1},{13,5},{2,10},{6,14},... | collective-permute-start | bytes 442376 | tf_op jit(solution)/shard_map/ppermute | solution.py:440
  10.4 0.9 copy-start.2
  11.3 21.3 %copy-start.3 = (bf16[144,512]{1,0:T(8,128)(2,1)S(1)}, bf16[144,512]{1,0:T(8,128)(2,1)}, u32[]{:S(2)}) copy-start(bf16[144,512]{1,0:T(8,128)(2,1)} %route.1.refs_1_.refs_0_) | copy-start | bytes 442372
  12.4 13.3 %collective-permute-start.4 = (bf16[192,256]{1,0:T(8,128)(2,1)S(1)}, bf16[192,256]{1,0:T(8,128)(2,1)S(1)}, u32[]{:S(2)}, u32[]{:S(2)}) collective-permute-start(bf16[192,256]{1,0:T(8,128)(2,1)S(1)} %get-tuple-element.41), channel_id=1, source_target_pairs={{0,4},{4,0},{8,12},{12,8},{1,5},{5,1},{9,13},{13,9},{2,6},{6,2},{1... | collective-permute-start | bytes 294920 | tf_op jit(solution)/shard_map/ppermute | solution.py:440
  14.4 12.2 %collective-permute-start.5 = (bf16[192,256]{1,0:T(8,128)(2,1)S(1)}, bf16[192,256]{1,0:T(8,128)(2,1)S(1)}, u32[]{:S(2)}, u32[]{:S(2)}) collective-permute-start(bf16[192,256]{1,0:T(8,128)(2,1)S(1)} %get-tuple-element.42), channel_id=1, source_target_pairs={{0,8},{4,12},{8,0},{12,4},{1,9},{5,13},{9,1},{13,5},{2,10},{6,14},... | collective-permute-start | bytes 294920 | tf_op jit(solution)/shard_map/ppermute | solution.py:440
  26.6 42.3 %copy-start.4 = (s32[16,4]{0,1:T(4,128)S(1)}, s32[16,4]{0,1:T(4,128)}, u32[]{:S(2)}) copy-start(s32[16,4]{0,1:T(4,128)} %param.14) | copy-start | bytes 772
  26.6 38.7 %collective-permute-start.7 = (bf16[1024,512]{1,0:T(8,128)(2,1)S(1)}, bf16[1024,512]{1,0:T(8,128)(2,1)S(1)}, u32[]{:S(2)}, u32[]{:S(2)}) collective-permute-start(bf16[1024,512]{1,0:T(8,128)(2,1)S(1)} %gate.10), channel_id=1, source_target_pairs={{12,8},{8,4},{4,0},{13,9},{9,5},{5,1},{14,10},{10,6},{6,2},{15,11}... | collective-permute-start | bytes 3145736 | tf_op jit(solution)/shard_map/ppermute | solution.py:499
  28.0 37.3 %collective-permute-start.6 = (bf16[1024,512]{1,0:T(8,128)(2,1)S(1)}, bf16[1024,512]{1,0:T(8,128)(2,1)S(1)}, u32[]{:S(2)}, u32[]{:S(2)}) collective-permute-start(bf16[1024,512]{1,0:T(8,128)(2,1)S(1)} %gate.10), channel_id=1, source_target_pairs={{0,4},{4,8},{8,12},{1,5},{5,9},{9,13},{2,6},{6,10},{10,14},{3,7},{... | collective-permute-start | bytes 3145736 | tf_op jit(solution)/shard_map/ppermute | solution.py:499
  39.1 26.0 %collective-permute-start.3 = (bf16[2,256,768]{2,1,0:T(8,128)(2,1)S(1)}, bf16[2,256,768]{2,1,0:T(8,128)(2,1)S(1)}, u32[]{:S(2)}, u32[]{:S(2)}) collective-permute-start(bf16[2,256,768]{2,1,0:T(8,128)(2,1)S(1)} %get-tuple-element.38), channel_id=1, source_target_pairs={{0,1},{1,0},{2,3},{3,2},{4,5},{5,4},{6,7},{7,6},{8,9},{9,8},{10,11... | collective-permute-start | bytes 2359304 | tf_op jit(solution)/shard_map/ppermute | solution.py:440
  39.1 17.0 %collective-permute-start.9 = (bf16[192,256]{1,0:T(8,128)(2,1)S(1)}, bf16[192,256]{1,0:T(8,128)(2,1)S(1)}, u32[]{:S(2)}, u32[]{:S(2)}) collective-permute-start(bf16[192,256]{1,0:T(8,128)(2,1)S(1)} %get-tuple-element.43), channel_id=1, source_target_pairs={{0,12},{4,8},{8,4},{12,0},{1,13},{5,9},{9,5},{13,1},{2,14},{6,10},... | collective-permute-start | bytes 294920 | tf_op jit(solution)/shard_map/ppermute | solution.py:440
  56.1 8.9 %collective-permute-start.11 = (bf16[4,192,256]{2,1,0:T(8,128)(2,1)S(1)}, bf16[4,192,256]{2,1,0:T(8,128)(2,1)S(1)}, u32[]{:S(2)}, u32[]{:S(2)}) collective-permute-start(bf16[4,192,256]{2,1,0:T(8,128)(2,1)S(1)} %stack_columns.2.refs_0_), channel_id=1, source_target_pairs={{0,2},{1,3},{2,0},{3,1},{4,6},{5,7},{6,4},{7,5},{8,10},{9,11},{10,... | collective-permute-start | bytes 1179656 | tf_op jit(solution)/shard_map/ppermute | solution.py:440
  57.7 11.2 %collective-permute-start.10 = (bf16[4,192,256]{2,1,0:T(8,128)(2,1)S(1)}, bf16[4,192,256]{2,1,0:T(8,128)(2,1)S(1)}, u32[]{:S(2)}, u32[]{:S(2)}) collective-permute-start(bf16[4,192,256]{2,1,0:T(8,128)(2,1)S(1)} %stack_columns.2.refs_0_), channel_id=1, source_target_pairs={{0,1},{1,0},{2,3},{3,2},{4,5},{5,4},{6,7},{7,6},{8,9},{9,8},{10,11... | collective-permute-start | bytes 1179656 | tf_op jit(solution)/shard_map/ppermute | solution.py:440
  65.1 3.8 %collective-permute-start.12 = (bf16[4,192,256]{2,1,0:T(8,128)(2,1)S(1)}, bf16[4,192,256]{2,1,0:T(8,128)(2,1)S(1)}, u32[]{:S(2)}, u32[]{:S(2)}) collective-permute-start(bf16[4,192,256]{2,1,0:T(8,128)(2,1)S(1)} %collective-permute-done.11.refs_2_), channel_id=1, source_target_pairs={{0,1},{1,0},{2,3},{3,2},{4,5},{5,4},{6,7},{7,6},{8,9},{9,8},{10,11... | collective-permute-start | bytes 1179656 | tf_op jit(solution)/shard_map/ppermute | solution.py:440
  65.3 11.6 %collective-permute-start.8 = (bf16[1,256,768]{2,1,0:T(8,128)(2,1)S(1)}, bf16[1,256,768]{2,1,0:T(8,128)(2,1)S(1)}, u32[]{:S(2)}, u32[]{:S(2)}) collective-permute-start(bf16[1,256,768]{2,1,0:T(8,128)(2,1)S(1)} %gate.11), channel_id=1, source_target_pairs={{0,2},{1,3},{2,0},{3,1},{4,6},{5,7},{6,4},{7,5},{8,10},{9,11},{10,... | collective-permute-start | bytes 1179656 | tf_op jit(solution)/shard_map/ppermute | solution.py:440
  66.9 27.2 %collective-permute-start.19 = (bf16[1024,512]{1,0:T(8,128)(2,1)S(1)}, bf16[1024,512]{1,0:T(8,128)(2,1)S(1)}, u32[]{:S(2)}, u32[]{:S(2)}) collective-permute-start(bf16[1024,512]{1,0:T(8,128)(2,1)S(1)} %collective-permute-done.7.refs_2_.refs_4_.refs_8_), channel_id=1, source_target_pairs={{8,4},{4,0},{9,5},{5,1},{10,6},{6,2},{11,7},{7,3},{24,20},{20,16},... | collective-permute-start | bytes 3145736 | tf_op jit(solution)/shard_map/ppermute | solution.py:499
  68.2 25.9 %collective-permute-start.18 = (bf16[1024,512]{1,0:T(8,128)(2,1)S(1)}, bf16[1024,512]{1,0:T(8,128)(2,1)S(1)}, u32[]{:S(2)}, u32[]{:S(2)}) collective-permute-start(bf16[1024,512]{1,0:T(8,128)(2,1)S(1)} %collective-permute-done.6.refs_1_.refs_5_), channel_id=1, source_target_pairs={{4,8},{8,12},{5,9},{9,13},{6,10},{10,14},{7,11},{11,15},{20,24},{2... | collective-permute-start | bytes 3145736 | tf_op jit(solution)/shard_map/ppermute | solution.py:499
  78.6 11.2 %collective-permute-start.14 = (bf16[256,768]{1,0:T(8,128)(2,1)S(1)}, bf16[256,768]{1,0:T(8,128)(2,1)S(1)}, u32[]{:S(2)}, u32[]{:S(2)}) collective-permute-start(bf16[256,768]{1,0:T(8,128)(2,1)S(1)} %get-tuple-element.47.refs_0_), channel_id=1, source_target_pairs={{0,2},{1,3},{2,0},{3,1},{4,6},{5,7},{6,4},{7,5},{8,10},{9,11},{10,... | collective-permute-start | bytes 1179656 | tf_op jit(solution)/shard_map/ppermute | solution.py:440
  80.1 20.3 %collective-permute-start.13 = (bf16[256,768]{1,0:T(8,128)(2,1)S(1)}, bf16[256,768]{1,0:T(8,128)(2,1)S(1)}, u32[]{:S(2)}, u32[]{:S(2)}) collective-permute-start(bf16[256,768]{1,0:T(8,128)(2,1)S(1)} %get-tuple-element.47.refs_0_), channel_id=1, source_target_pairs={{0,1},{1,0},{2,3},{3,2},{4,5},{5,4},{6,7},{7,6},{8,9},{9,8},{10,11... | collective-permute-start | bytes 1179656 | tf_op jit(solution)/shard_map/ppermute | solution.py:440
  89.7 10.7 %collective-permute-start.15 = (bf16[256,768]{1,0:T(8,128)(2,1)S(1)}, bf16[256,768]{1,0:T(8,128)(2,1)S(1)}, u32[]{:S(2)}, u32[]{:S(2)}) collective-permute-start(bf16[256,768]{1,0:T(8,128)(2,1)S(1)} %collective-permute-done.14.refs_2_), channel_id=1, source_target_pairs={{0,1},{1,0},{2,3},{3,2},{4,5},{5,4},{6,7},{7,6},{8,9},{9,8},{10,11... | collective-permute-start | bytes 1179656 | tf_op jit(solution)/shard_map/ppermute | solution.py:440
  94.0 16.8 %collective-permute-start.20 = (bf16[384,256]{1,0:T(8,128)(2,1)S(1)}, bf16[384,256]{1,0:T(8,128)(2,1)S(1)}, u32[]{:S(2)}, u32[]{:S(2)}) collective-permute-start(bf16[384,256]{1,0:T(8,128)(2,1)S(1)} %get-tuple-element.57), channel_id=1, source_target_pairs={{0,4},{4,0},{8,12},{12,8},{1,5},{5,1},{9,13},{13,9},{2,6},{6,2},{1... | collective-permute-start | bytes 589832 | tf_op jit(solution)/shard_map/ppermute | solution.py:440
  97.0 17.2 %collective-permute-start.21 = (bf16[384,256]{1,0:T(8,128)(2,1)S(1)}, bf16[384,256]{1,0:T(8,128)(2,1)S(1)}, u32[]{:S(2)}, u32[]{:S(2)}) collective-permute-start(bf16[384,256]{1,0:T(8,128)(2,1)S(1)} %get-tuple-element.58), channel_id=1, source_target_pairs={{0,8},{4,12},{8,0},{12,4},{1,9},{5,13},{9,1},{13,5},{2,10},{6,14},... | collective-permute-start | bytes 589832 | tf_op jit(solution)/shard_map/ppermute | solution.py:440
  99.3 14.9 %collective-permute-start.22 = (bf16[384,256]{1,0:T(8,128)(2,1)S(1)}, bf16[384,256]{1,0:T(8,128)(2,1)S(1)}, u32[]{:S(2)}, u32[]{:S(2)}) collective-permute-start(bf16[384,256]{1,0:T(8,128)(2,1)S(1)} %get-tuple-element.59), channel_id=1, source_target_pairs={{0,12},{4,8},{8,4},{12,0},{1,13},{5,9},{9,5},{13,1},{2,14},{6,10},... | collective-permute-start | bytes 589832 | tf_op jit(solution)/shard_map/ppermute | solution.py:440
  108.7 8.5 %collective-permute-start.16 = (bf16[160,512]{1,0:T(8,128)(2,1)S(1)}, bf16[160,512]{1,0:T(8,128)(2,1)S(1)}, u32[]{:S(2)}, u32[]{:S(2)}) collective-permute-start(bf16[160,512]{1,0:T(8,128)(2,1)S(1)} %get-tuple-element.50), channel_id=1, source_target_pairs={{0,4},{4,0},{8,12},{12,8},{1,5},{5,1},{9,13},{13,9},{2,6},{6,2},{1... | collective-permute-start | bytes 491528 | tf_op jit(solution)/shard_map/ppermute | solution.py:440
  109.3 11.4 %collective-permute-start.17 = (bf16[160,512]{1,0:T(8,128)(2,1)S(1)}, bf16[160,512]{1,0:T(8,128)(2,1)S(1)}, u32[]{:S(2)}, u32[]{:S(2)}) collective-permute-start(bf16[160,512]{1,0:T(8,128)(2,1)S(1)} %get-tuple-element.51), channel_id=1, source_target_pairs={{0,4},{4,0},{8,12},{12,8},{1,5},{5,1},{9,13},{13,9},{2,6},{6,2},{1... | collective-permute-start | bytes 491528 | tf_op jit(solution)/shard_map/ppermute | solution.py:440
  114.2 33.6 %copy-start.1 = (bf16[8,4,32,512]{3,2,1,0:T(8,128)(2,1)S(1)}, bf16[8,4,32,512]{3,2,1,0:T(8,128)(2,1)}, u32[]{:S(2)}) copy-start(bf16[8,4,32,512]{3,2,1,0:T(8,128)(2,1)} %param.16) | copy-start | bytes 3145732
  120.7 19.5 %collective-permute-start.26 = (bf16[4,384,256]{2,1,0:T(8,128)(2,1)S(1)}, bf16[4,384,256]{2,1,0:T(8,128)(2,1)S(1)}, u32[]{:S(2)}, u32[]{:S(2)}) collective-permute-start(bf16[4,384,256]{2,1,0:T(8,128)(2,1)S(1)} %stack_columns.3.refs_0_), channel_id=1, source_target_pairs={{0,2},{1,3},{2,0},{3,1},{4,6},{5,7},{6,4},{7,5},{8,10},{9,11},{10,... | collective-permute-start | bytes 2359304 | tf_op jit(solution)/shard_map/ppermute | solution.py:440
  121.3 26.5 %collective-permute-start.23 = (bf16[1024,512]{1,0:T(8,128)(2,1)S(1)}, bf16[1024,512]{1,0:T(8,128)(2,1)S(1)}, u32[]{:S(2)}, u32[]{:S(2)}) collective-permute-start(bf16[1024,512]{1,0:T(8,128)(2,1)S(1)} %pick.1.refs_3_), channel_id=1, source_target_pairs={{8,12},{4,0},{9,13},{5,1},{10,14},{6,2},{11,15},{7,3},{24,28},{20,... | collective-permute-start | bytes 3145736 | tf_op jit(solution)/shard_map/ppermute | solution.py:497
  122.6 25.2 %collective-permute-start.25 = (bf16[4,384,256]{2,1,0:T(8,128)(2,1)S(1)}, bf16[4,384,256]{2,1,0:T(8,128)(2,1)S(1)}, u32[]{:S(2)}, u32[]{:S(2)}) collective-permute-start(bf16[4,384,256]{2,1,0:T(8,128)(2,1)S(1)} %stack_columns.3.refs_0_), channel_id=1, source_target_pairs={{0,1},{1,0},{2,3},{3,2},{4,5},{5,4},{6,7},{7,6},{8,9},{9,8},{10,11... | collective-permute-start | bytes 2359304 | tf_op jit(solution)/shard_map/ppermute | solution.py:440
  140.3 7.5 %collective-permute-start.27 = (bf16[4,384,256]{2,1,0:T(8,128)(2,1)S(1)}, bf16[4,384,256]{2,1,0:T(8,128)(2,1)S(1)}, u32[]{:S(2)}, u32[]{:S(2)}) collective-permute-start(bf16[4,384,256]{2,1,0:T(8,128)(2,1)S(1)} %collective-permute-done.26.refs_2_), channel_id=1, source_target_pairs={{0,1},{1,0},{2,3},{3,2},{4,5},{5,4},{6,7},{7,6},{8,9},{9,8},{10,11... | collective-permute-start | bytes 2359304 | tf_op jit(solution)/shard_map/ppermute | solution.py:440
  147.8 8.1 %copy-start.5 = (s32[128,8]{0,1:T(8,128)S(1)}, s32[128,8]{0,1:T(8,128)}, u32[]{:S(2)}) copy-start(s32[128,8]{0,1:T(8,128)} %param.12) | copy-start | bytes 12292
  147.8 8.1 %copy-start.6 = (s32[128,8]{0,1:T(8,128)S(1)}, s32[128,8]{0,1:T(8,128)}, u32[]{:S(2)}) copy-start(s32[128,8]{0,1:T(8,128)} %param.13) | copy-start | bytes 12292
  147.8 8.1 %collective-permute-start.24 = (bf16[160,512]{1,0:T(8,128)(2,1)S(1)}, bf16[160,512]{1,0:T(8,128)(2,1)S(1)}, u32[]{:S(2)}, u32[]{:S(2)}) collective-permute-start(bf16[160,512]{1,0:T(8,128)(2,1)S(1)} %gate.15), channel_id=1, source_target_pairs={{0,8},{4,12},{8,0},{12,4},{1,9},{5,13},{9,1},{13,5},{2,10},{6,14},... | collective-permute-start | bytes 491528 | tf_op jit(solution)/shard_map/ppermute | solution.py:440
